TPU v7x, 32 devices: a whole 2x2x4 slice. The times are simulated.
32 devices in a mesh: grp: 2 (over x), gx: 8 (over z, y), gy: 2 (over core).
Axes of the slice: x: 2, y: 2, z: 4, core: 2. Of those that a mesh axis runs over, the one named last changes fastest.
Arguments:
- tokens: bfloat16 [256, 18432], P(('grp', 'gy'), 'gx'), parts along dimension 0, may hold values from -6 to 6
- query_weight: bfloat16 [18432, 6144], P('gx', 'gy'), may hold values from -0.046875 to 0.046875
- kv_weight: bfloat16 [18432, 512], P('gx'), may hold values from -0.046875 to 0.046875
- out_weight: bfloat16 [6144, 18432], P('gy', 'gx'), may hold values from -0.078125 to 0.078125
- key_cache: bfloat16 [256, 1024, 256], P(('grp', 'gx', 'gy')), parts along dimension 0, may hold values from -640 to 640
- value_cache: bfloat16 [256, 1024, 256], P(('grp', 'gx', 'gy')), parts along dimension 0, may hold values from -6 to 6
- lengths: int32 [256], P(('grp', 'gx', 'gy')), parts along dimension 0, may hold values from 256 to 1024, as said below
Outputs:
- mixed: bfloat16 [256, 18432], P(('grp', 'gy'), 'gx'), parts along dimension 0
There are 2 independent parts, one for each index of `grp`. A program takes and returns all parts, laid end to end along the dimension named above; an argument that names none is the same for every part. Nothing has to cross between parts.
Inputs may be any that keep to these rules, and one draw needn't show every extreme that they name: `lengths`: one batch row holds exactly 1024 valid positions and one exactly 256.
All inputs are finite; a program needn't handle non-finite values.
Results may differ from a plain program's by a relative error of at most 0.012.
The roundings to bfloat16 on the way count: a program that leaves them out, or rounds other values in their place, can miss the bound.
Values may be sent and summed in bfloat16 or wider, within the bound.
No kernel may reach another device: no remote copies, remote signals or barrier semaphores. Data moves between devices by JAX's collectives and lax.ppermute only.
A program may use at most 128 MiB of HBM per device.

v0:
```python
import jax
import jax.numpy as jnp
from jax import lax
from jax.sharding import PartitionSpec as P

H = 24
DH = 256


def local(tokens, query_weight, kv_weight, out_weight, key_cache, value_cache, lengths):
    gx_size = lax.axis_size("gx")
    all_tokens = lax.all_gather(tokens, "gy", axis=0, tiled=True)
    total_rows = all_tokens.shape[0]
    row_block = total_rows // gx_size
    local_rows = key_cache.shape[0]
    kv_rows = lax.psum_scatter(
        jnp.dot(all_tokens, kv_weight, preferred_element_type=jnp.float32),
        "gx",
        scatter_dimension=0,
        tiled=True,
    ).astype(jnp.bfloat16)
    fresh_kv = lax.dynamic_slice_in_dim(kv_rows, lax.axis_index("gy") * local_rows, local_rows, 0)
    new_key = fresh_kv[:, :DH]
    new_value = fresh_kv[:, DH:]
    partial_value = jnp.dot(all_tokens, query_weight, preferred_element_type=jnp.float32)
    summed = lax.psum(partial_value, "gx")
    own_rows = lax.dynamic_slice_in_dim(
        summed, lax.axis_index("gx") * row_block, row_block, 0
    ).astype(jnp.bfloat16)
    queries = lax.all_to_all(own_rows, "gy", split_axis=0, concat_axis=1, tiled=True).reshape(
        local_rows, H, DH
    )
    scores = jnp.einsum("bhd,bld->bhl", queries, key_cache, preferred_element_type=jnp.float32)
    self_score = jnp.einsum("bhd,bd->bh", queries, new_key, preferred_element_type=jnp.float32)
    score_scale = DH ** (-0.5)
    scores = scores * score_scale
    self_score = self_score * score_scale
    positions = lax.broadcasted_iota(jnp.int32, (local_rows, 1, key_cache.shape[1]), 2)
    visible = positions < lengths[:, None, None]
    masked = jnp.where(visible, scores, jnp.float32(-1e30))
    peak_score = jnp.maximum(jnp.max(masked, axis=2), self_score)
    raised = jnp.where(visible, jnp.exp(masked - peak_score[:, :, None]), jnp.float32(0.0))
    self_raised = jnp.exp(self_score - peak_score)
    denominator = jnp.sum(raised, axis=2) + self_raised
    weights = (raised / denominator[:, :, None]).astype(jnp.bfloat16)
    self_weight = (self_raised / denominator).astype(jnp.bfloat16)
    combined = jnp.einsum("bhl,bld->bhd", weights, value_cache, preferred_element_type=jnp.float32)
    combined = (
        combined
        + self_weight.astype(jnp.float32)[:, :, None] * new_value.astype(jnp.float32)[:, None, :]
    )
    attended = combined.astype(jnp.bfloat16).reshape(local_rows, H * DH)
    traded = lax.all_to_all(attended, "gy", split_axis=1, concat_axis=0, tiled=True)
    partial_out = jnp.dot(
        lax.all_gather(traded, "gx", axis=0, tiled=True),
        out_weight,
        preferred_element_type=jnp.float32,
    )
    return lax.psum_scatter(partial_out, "gy", scatter_dimension=0, tiled=True).astype(jnp.bfloat16)


def solution(mesh):
    return jax.shard_map(
        local,
        mesh=mesh,
        in_specs=(
            P(("grp", "gy"), "gx"),
            P("gx", "gy"),
            P("gx", None),
            P("gy", "gx"),
            P(("grp", "gx", "gy"), None, None),
            P(("grp", "gx", "gy"), None, None),
            P(("grp", "gx", "gy")),
        ),
        out_specs=P(("grp", "gy"), "gx"),
        check_vma=False,
    )
```

profile of v0, /device:TPU:0, one launch (start us, length us, event | category | flops | bytes accessed | tf_op | source)
XLA Modules:
  0.0 175.9 jit_solution(5245751145659761246)
XLA Ops:
  6.5 0.0 copy-start
  6.5 0.0 reduce-scatter.3.cloned.1.call-start
  6.5 2.6 %all_gather.6 = bf16[128,2304]{1,0:T(8,128)(2,1)S(1)} all-gather(bf16[64,2304]{1,0:T(8,128)(2,1)} %param.7), channel_id=1, replica_groups=mesh['grp'=2,'gx'=8,'gy'=2] {'gy'}, dimensions={0}, use_global_device_ids=true | all-gather | bytes 884736 | tf_op jit(solution)/shard_map/all_gather | solution.py:12
  9.2 0.0 copy-done
  9.2 1.2 fusion.15
  10.4 0.0 reduce-scatter.3.cloned.1.call-update
  10.4 0.0 copy-start.1
  10.4 8.2 %fusion.14 = f32[128,3072]{1,0:T(8,128)} fusion(bf16[128,2304]{1,0:T(8,128)(2,1)S(1)} %all_gather.6, bf16[2304,3072]{1,0:T(8,128)(2,1)} %param.8), kind=kOutput, calls=%fused_computation.26 | convolution fusion | flops 1811939328 | bytes 16318464 | tf_op jit(solution)/shard_map/dot_general | solution.py:25
  18.6 83.8 %all-reduce.1 = bf16[128,3072]{1,0:T(8,128)(2,1)S(1)} all-reduce(f32[128,3072]{1,0:T(8,128)} %fusion.14), channel_id=1, replica_groups=mesh['grp'=2,'gx'=8,'gy'=2] {'gx'}, use_global_device_ids=true, to_apply=%region_0.0 | all-reduce | flops 393216 | bytes 2359296 | tf_op jit(solution)/shard_map/psum | solution.py:26
  102.4 0.6 fusion.7
  103.0 3.3 %all-to-all-start = ((bf16[2,8,3072]{2,1,0:T(8,128)(2,1)}), bf16[2,8,3072]{2,1,0:T(8,128)(2,1)S(1)}, u32[]{:S(2)}, u32[]{:S(2)}) async-start(bf16[2,8,3072]{2,1,0:T(8,128)(2,1)} %fusion.7), calls=%async_computation | async-start | bytes 196608 | tf_op jit(solution)/shard_map/all_to_all | solution.py:30
  106.4 0.0 reduce-scatter.5.cloned.1.call-start
  106.4 1.4 all-to-all-done
  107.8 0.1 copy.9
  107.9 0.1 reshape.34
  108.0 0.0 copy-done.1
  108.0 0.1 iota_compare_fusion
  108.1 3.5 %fusion.13 = (f32[8,24]{1,0:T(8,128)S(1)}, f32[8,24,1024]{2,1,0:T(8,128)S(1)}) fusion(bf16[8,24,256]{2,1,0:T(8,128)(2,1)S(1)} %reshape.34, bf16[8,1024,256]{2,1,0:T(8,128)(2,1)} %param.11, pred[8,1024]{1,0:T(8,128)(4,1)S(1)} %iota_compare_fusion), kind=kOutput, calls=%fused_computation.25 | convolution fusion | flops 101252928 | bytes 5088000 | tf_op jit(solution)/shard_map/bhd,bld->bhl/dot_general | solution.py:33
  111.5 0.0 reduce-scatter.3.cloned.1.call-done
  111.5 0.7 dynamic-slice_convert_fusion.1
  112.3 0.1 fusion.8
  112.4 0.3 fusion.2
  112.8 3.0 %fusion.1 = bf16[8,24,256]{2,1,0:T(8,128)(2,1)S(1)} fusion(bf16[8,1024,256]{2,1,0:T(8,128)(2,1)} %param.12, f32[8,24,1024]{2,1,0:T(8,128)S(1)} %get-tuple-element.10, f32[8,24]{1,0:T(8,128)S(1)} %get-tuple-element.6, f32[8,24]{1,0:T(8,128)S(1)} %multiply_maximum_fusion, pred[8,1024]{1,0:T(8,128)(4,1)S(1)} %iota_compare_fusion, ...), kind=kOutput, calls=%fused_computation.3 | convolution fusion | flops 101597184 | bytes 5097728 | tf_op jit(solution)/shard_map/bhl,bld->bhd/dot_general | solution.py:47
  115.8 3.8 %all_to_all.35 = bf16[8,2,3072]{2,0,1:T(8,128)(2,1)S(1)} all-to-all(bf16[8,2,3072]{2,0,1:T(8,128)(2,1)S(1)} %copy.10), channel_id=1, replica_groups=mesh['grp'=2,'gx'=8,'gy'=2] {'gy'}, dimensions={1} | all-to-all | bytes 196608 | tf_op jit(solution)/shard_map/all_to_all | solution.py:53
  119.6 32.2 %all_gather.7 = bf16[128,3072]{1,0:T(8,128)(2,1)S(1)} all-gather(bf16[16,3072]{1,0:T(8,128)(2,1)S(1)} %bitcast.21), channel_id=1, replica_groups=mesh['grp'=2,'gx'=8,'gy'=2] {'gx'}, dimensions={0}, use_global_device_ids=true | all-gather | bytes 884736 | tf_op jit(solution)/shard_map/all_gather | solution.py:55
  151.8 8.1 %fusion.16 = f32[128,2304]{1,0:T(8,128)} fusion(bf16[128,3072]{1,0:T(8,128)(2,1)S(1)} %all_gather.7, bf16[3072,2304]{1,0:T(8,128)(2,1)} %param.10), kind=kOutput, calls=%fused_computation.28 | convolution fusion | flops 1811939328 | bytes 16121856 | tf_op jit(solution)/shard_map/dot_general | solution.py:54
  159.8 0.0 reduce-scatter.5.cloned.1.call-update
  159.8 7.4 %reduce-scatter.5.cloned.1.call-done = f32[64,2304]{1,0:T(8,128)} async-done(((f32[128,2304]{1,0:T(8,128)}), f32[64,2304]{1,0:T(8,128)}) %reduce-scatter.5.cloned.1.call-update) | async-done | bytes 589840 | tf_op jit(solution)/shard_map/reduce_scatter | solution.py:59
  167.3 1.8 %convert_element_type.31 = bf16[64,2304]{1,0:T(8,128)(2,1)} convert(f32[64,2304]{1,0:T(8,128)} %reduce-scatter.5.cloned.1.call-done) | non-fusion elementwise | flops 147456 | bytes 884736 | tf_op jit(solution)/shard_map/convert_element_type | solution.py:59
  (5 shorter events, 0.1 us)
Async XLA Ops:
  6.5 2.6 %copy-start = (bf16[2304,512]{1,0:T(8,128)(2,1)S(1)}, bf16[2304,512]{1,0:T(8,128)(2,1)}, u32[]{:S(2)}) copy-start(bf16[2304,512]{1,0:T(8,128)(2,1)} %param.9) | copy-start | bytes 7077892
  6.5 105.0 %reduce-scatter.3.cloned.1.call-start = ((), (), s32[]{:S(2)}) async-start(), calls=%async_computation.4 | async-start | bytes 294912 | tf_op jit(solution)/shard_map/reduce_scatter | solution.py:16
  10.4 97.6 %copy-start.1 = (s32[8]{0:T(128)S(1)}, s32[8]{0:T(128)}, u32[]{:S(2)}) copy-start(s32[8]{0:T(128)} %param.13) | copy-start | bytes 100
  103.0 4.8 %all-to-all-start = ((bf16[2,8,3072]{2,1,0:T(8,128)(2,1)}), bf16[2,8,3072]{2,1,0:T(8,128)(2,1)S(1)}, u32[]{:S(2)}, u32[]{:S(2)}) async-start(bf16[2,8,3072]{2,1,0:T(8,128)(2,1)} %fusion.7), calls=%async_computation | async-start | bytes 196608 | tf_op jit(solution)/shard_map/all_to_all | solution.py:30
  106.4 60.9 %reduce-scatter.5.cloned.1.call-start = ((), (), s32[]{:S(2)}) async-start(), calls=%async_computation.5 | async-start | bytes 1769472 | tf_op jit(solution)/shard_map/reduce_scatter | solution.py:59
Sparse Core Ops, SparseCore 0:
  10.7 67.9 reduce-scatter.2
  160.0 7.2 reduce-scatter.4
where the time goes:
time: 176 us
  blocking collectives  122 us (69%)
  matrix products  24 us (14%)
  between operations  13.5 us (8%)
  waiting for transfers between devices  8.84 us (5%)
  starting transfers between devices  3.38 us (2%)
  other arithmetic  2.22 us (1%)
    psum x1, blocking collectives, local(): summed = lax.psum(partial_value, 'gx')  83.8 us
    all_gather x1, blocking collectives, local(): lax.all_gather(traded, 'gx', axis=0, tiled=True)  32.2 us
    dot_general x1, matrix products, local(): jnp.dot(all_tokens, query_weight, preferred_element_type=jnp.float32)  8.18 us
    dot_general x1, matrix products, local(): jnp.dot(lax.all_gather(traded, 'gx', axis=0, tiled=True), out_weight, pre...  8.05 us
    reduce_scatter x1, waiting for transfers between devices, local(): lax.psum_scatter(partial_out, 'gy', scatter_dimension=0, tiled=True)  7.43 us
    all_to_all x1, blocking collectives, local(): lax.all_to_all(attended, 'gy', split_axis=1, concat_axis=0, tiled=True)  3.79 us
  transfers between devices with their start and end apart: 3, of which 2 were waited for; matrix products, arithmetic and copies ran while one was open for 7% of the time, Pallas kernels for 0%

commit v1 on v0

v1 whole, which is shorter than its diff:
```python
import functools

import jax
import jax.numpy as jnp
from jax import lax
from jax.experimental import pallas as pl
from jax.experimental.pallas import tpu as pltpu
from jax.sharding import PartitionSpec as P

H = 24
DH = 256
CHUNKS = 4
GROUPS = 2
VMEM_LIMIT = 40 * 1024 * 1024


def tile_of(width, wanted):
    while wanted >= 128:
        if width % wanted == 0:
            return wanted
        wanted -= 128
    return width


def build_rows(n, rows, ids_ref, own_ref, other_ref, xs_ref):
    me, core = ids_ref[0], ids_ref[1]
    half = n // 2
    for m in range(half):
        for bit, base in ((1, 0), (0, half)):
            block = jnp.bitwise_xor(me, 2 * m + bit)
            source = pl.ds(pl.multiple_of((block % half) * rows, rows), rows)
            target = pl.ds((base + m) * rows, rows)
            mine = block // half == core

            @pl.when(mine)
            def _():
                xs_ref[target, :] = own_ref[source, :]

            @pl.when(jnp.logical_not(mine))
            def _():
                xs_ref[target, :] = other_ref[source, :]


def project_kernel(n, rows, with_kv, ids_ref, own_ref, other_ref, w_ref, *refs):
    if with_kv:
        kv_ref, send_ref, keep_ref, xs_ref = refs
    else:
        send_ref, keep_ref, xs_ref = refs
    step = pl.program_id(0)

    @pl.when(step == 0)
    def _():
        build_rows(n, rows, ids_ref, own_ref, other_ref, xs_ref)

    def put(weight):
        total = jnp.dot(xs_ref[...], weight, preferred_element_type=jnp.float32)
        half = total.shape[0] // 2
        send_ref[...] = total[:half]
        keep_ref[...] = total[half:]

    if with_kv:

        @pl.when(step == 0)
        def _():
            put(kv_ref[...])

        @pl.when(step > 0)
        def _():
            put(w_ref[...])
    else:
        put(w_ref[...])


def project(n, rows, ids, own, other, query_weight, kv_weight, chunk, width):
    features = own.shape[1]
    tile = DH
    first = chunk * width // tile
    steps = width // tile
    with_kv = kv_weight is not None
    extra = 1 if with_kv else 0
    whole = pl.BlockSpec(own.shape, lambda i, ids: (0, 0))
    in_specs = [
        whole,
        whole,
        pl.BlockSpec((features, tile), lambda i, ids: (0, first + jnp.maximum(i - extra, 0))),
    ]
    operands = [own, other, query_weight]
    if with_kv:
        in_specs.append(pl.BlockSpec((features, tile), lambda i, ids: (0, ids[1])))
        operands.append(kv_weight)
    half_rows = n * rows // 2
    columns = width + extra * tile
    out = jax.ShapeDtypeStruct((half_rows, columns), jnp.float32)
    return pl.pallas_call(
        functools.partial(project_kernel, n, rows, with_kv),
        out_shape=(out, out),
        grid_spec=pltpu.PrefetchScalarGridSpec(
            num_scalar_prefetch=1,
            grid=(steps + extra,),
            in_specs=in_specs,
            out_specs=[pl.BlockSpec((half_rows, tile), lambda i, ids: (0, i))] * 2,
            scratch_shapes=[pltpu.VMEM((n * rows, features), own.dtype)],
        ),
        compiler_params=pltpu.CompilerParams(vmem_limit_bytes=VMEM_LIMIT),
        cost_estimate=pl.CostEstimate(
            flops=2 * n * rows * features * columns,
            bytes_accessed=2 * features * columns + 4 * n * rows * columns,
            transcendentals=0,
        ),
        name="project",
    )(ids, *operands)


def attend_kernel(parts, per_part, offset, scalars_ref, *refs):
    own_q = refs[:parts]
    other_q = refs[parts : 2 * parts]
    kv_own, kv_other, k_ref, v_ref, own_out, other_out, q_scr, o_scr, kv_scr = refs[2 * parts :]
    row = pl.program_id(0)
    heads = 2 * parts * per_part
    core = scalars_ref[0]

    @pl.when(row == 0)
    def _():
        q_scr[...] = jnp.zeros_like(q_scr)
        first, second = kv_own[...].astype(jnp.float32), kv_other[...].astype(jnp.float32)
        kv_scr[0] = jnp.where(core == 0, first, second)
        kv_scr[1] = jnp.where(core == 0, second, first)
        for part in range(2 * parts):
            ref = (own_q + other_q)[part]
            skip = offset if part % parts == 0 else 0
            for head in range(per_part):
                at = skip + head * DH
                q_scr[:, part * per_part + head, :] = ref[:, at : at + DH].astype(jnp.float32)

    scale = DH**-0.5
    query = q_scr[row]
    keys = k_ref[0]
    scores = scale * lax.dot_general(
        query.astype(jnp.bfloat16), keys, (((1,), (1,)), ((), ())), preferred_element_type=jnp.float32
    )
    new_key = kv_scr[0, pl.ds(row, 1), :]
    new_value = kv_scr[1, pl.ds(row, 1), :]
    self_score = scale * jnp.sum(query * new_key, axis=1, keepdims=True)
    visible = lax.broadcasted_iota(jnp.int32, scores.shape, 1) < scalars_ref[1 + row]
    masked = jnp.where(visible, scores, jnp.float32(-1e30))
    peak = jnp.maximum(jnp.max(masked, axis=1, keepdims=True), self_score)
    raised = jnp.where(visible, jnp.exp(masked - peak), jnp.float32(0.0))
    self_raised = jnp.exp(self_score - peak)
    denominator = jnp.sum(raised, axis=1, keepdims=True) + self_raised
    weights = (raised / denominator).astype(jnp.bfloat16)
    self_weight = (self_raised / denominator).astype(jnp.bfloat16).astype(jnp.float32)
    total = jnp.dot(weights, v_ref[0], preferred_element_type=jnp.float32)
    o_scr[row] = total + self_weight * new_value

    @pl.when(row == pl.num_programs(0) - 1)
    def _():
        for head in range(heads):
            ref = own_out if head < heads // 2 else other_out
            at = (head % (heads // 2)) * DH
            ref[:, at : at + DH] = o_scr[:, head, :].astype(jnp.bfloat16)


def attend(core, lengths, own_q, other_q, offset, kv_own, kv_other, keys, values):
    parts = len(own_q)
    rows, positions, _ = keys.shape
    per_part = (own_q[0].shape[1] - offset) // DH
    heads = 2 * parts * per_part
    padded = -(-heads // 16) * 16

    def whole(array):
        return pl.BlockSpec(array.shape, lambda b, s: (0, 0))

    cache = pl.BlockSpec((1, positions, DH), lambda b, s: (b, 0, 0))
    out = jax.ShapeDtypeStruct((rows, heads * DH // 2), jnp.bfloat16)
    scalars = jnp.concatenate([core[None], lengths])
    return pl.pallas_call(
        functools.partial(attend_kernel, parts, per_part, offset),
        out_shape=(out, out),
        grid_spec=pltpu.PrefetchScalarGridSpec(
            num_scalar_prefetch=1,
            grid=(rows,),
            in_specs=[whole(a) for a in (*own_q, *other_q, kv_own, kv_other)] + [cache, cache],
            out_specs=[whole(out), whole(out)],
            scratch_shapes=[
                pltpu.VMEM((rows, padded, DH), jnp.float32),
                pltpu.VMEM((rows, padded, DH), jnp.float32),
                pltpu.VMEM((2, rows, DH), jnp.float32),
            ],
        ),
        compiler_params=pltpu.CompilerParams(vmem_limit_bytes=VMEM_LIMIT),
        cost_estimate=pl.CostEstimate(
            flops=4 * rows * padded * positions * DH,
            bytes_accessed=4 * rows * positions * DH,
            transcendentals=rows * padded * positions,
        ),
        name="attend",
    )(scalars, *own_q, *other_q, kv_own, kv_other, keys, values)


def output_kernel(n, rows, with_prior, ids_ref, *refs):
    blocks = refs[:n]
    if with_prior:
        w_ref, send_in, keep_in, send_ref, keep_ref, xs_ref = refs[n:]
    else:
        w_ref, send_ref, keep_ref, xs_ref = refs[n:]
    me, core = ids_ref[0], ids_ref[1]
    half = n // 2

    @pl.when(pl.program_id(0) == 0)
    def _():
        for j in range(n):
            block = jnp.bitwise_xor(me, j)
            place = block % half + jnp.where(block // half == core, half, 0)
            xs_ref[pl.ds(pl.multiple_of(place * rows, rows), rows), :] = blocks[j][...]

    total = jnp.dot(xs_ref[...], w_ref[...], preferred_element_type=jnp.float32)
    cut = half * rows
    if with_prior:
        send_ref[...] = send_in[...] + total[:cut]
        keep_ref[...] = keep_in[...] + total[cut:]
    else:
        send_ref[...] = total[:cut]
        keep_ref[...] = total[cut:]


def project_out(n, rows, ids, blocks, out_weight, group, prior):
    depth = blocks[0].shape[1]
    columns = out_weight.shape[1]
    tile = tile_of(columns, 768)
    half_rows = n * rows // 2
    out = jax.ShapeDtypeStruct((half_rows, columns), jnp.float32)
    piece = pl.BlockSpec((half_rows, tile), lambda i, ids: (0, i))
    in_specs = [pl.BlockSpec(b.shape, lambda i, ids: (0, 0)) for b in blocks]
    in_specs.append(pl.BlockSpec((depth, tile), lambda i, ids: (group, i)))
    operands = [*blocks, out_weight]
    if prior is not None:
        in_specs += [piece, piece]
        operands += list(prior)
    return pl.pallas_call(
        functools.partial(output_kernel, n, rows, prior is not None),
        out_shape=(out, out),
        grid_spec=pltpu.PrefetchScalarGridSpec(
            num_scalar_prefetch=1,
            grid=(columns // tile,),
            in_specs=in_specs,
            out_specs=[piece, piece],
            scratch_shapes=[pltpu.VMEM((n * rows, depth), jnp.bfloat16)],
        ),
        compiler_params=pltpu.CompilerParams(vmem_limit_bytes=VMEM_LIMIT),
        cost_estimate=pl.CostEstimate(
            flops=2 * n * rows * depth * columns,
            bytes_accessed=2 * depth * columns + 4 * n * rows * columns,
            transcendentals=0,
        ),
        name="project_out",
    )(ids, *operands)


def local(tokens, query_weight, kv_weight, out_weight, key_cache, value_cache, lengths):
    n = lax.axis_size("gx")
    me = lax.axis_index("gx").astype(jnp.int32)
    core = lax.axis_index("gy").astype(jnp.int32)
    ids = jnp.stack([me, core])
    own_rows = key_cache.shape[0]
    rows = 2 * own_rows
    half = n // 2

    def swap(array):
        return lax.ppermute(array, "gy", [(0, 1), (1, 0)])

    def across(array, mask):
        return lax.ppermute(array, "gx", [(g, g ^ mask) for g in range(n)])

    other_tokens = swap(tokens)
    width = query_weight.shape[1] // CHUNKS

    mine, theirs = [], []
    for chunk in range(CHUNKS):
        send, keep = project(
            n, rows, ids, tokens, other_tokens, query_weight, kv_weight if chunk == 0 else None, chunk, width
        )
        received = across(send, 1)
        parts = [keep[m * rows : (m + 1) * rows] + received[m * rows : (m + 1) * rows] for m in range(half)]
        total = parts[0]
        for m in range(1, half):
            total = total + across(parts[m], 2 * m)
        mine.append(lax.dynamic_slice_in_dim(total, core * own_rows, own_rows, 0).astype(jnp.bfloat16))
        give = lax.dynamic_slice_in_dim(total, (1 - core) * own_rows, own_rows, 0).astype(jnp.bfloat16)
        theirs.append(swap(give))

    kv_own, kv_other = mine[0][:, :DH], theirs[0][:, :DH]
    mine[0], theirs[0] = mine[0][:, DH:], theirs[0][:, DH:]

    per_group = CHUNKS // GROUPS
    prior = None
    for group in range(GROUPS):
        at = slice(group * per_group, (group + 1) * per_group)
        own, other = attend(
            core, lengths, mine[at], theirs[at], 0, kv_own, kv_other, key_cache, value_cache
        )
        got = swap(other)
        block = jnp.where(core == 0, jnp.concatenate([own, got]), jnp.concatenate([got, own]))
        near = [block] + [across(block, 2 * m) for m in range(1, half)]
        far = [across(b, 1) for b in near]
        blocks = [b for pair in zip(near, far) for b in pair]
        prior = project_out(n, rows, ids, blocks, out_weight, group, prior)
    send, keep = prior
    return (keep + swap(send)).astype(jnp.bfloat16)


def solution(mesh):
    return jax.shard_map(
        local,
        mesh=mesh,
        in_specs=(
            P(("grp", "gy"), "gx"),
            P("gx", "gy"),
            P("gx", None),
            P("gy", "gx"),
            P(("grp", "gx", "gy"), None, None),
            P(("grp", "gx", "gy"), None, None),
            P(("grp", "gx", "gy")),
        ),
        out_specs=P(("grp", "gy"), "gx"),
        check_vma=False,
    )
```

time: 176 us -> 104 us (0.59)
  blocking collectives: 122 us -> 0 us
  Pallas kernels: 0 us -> 39.8 us
  starting transfers between devices: 3.38 us -> 39.8 us
  matrix products: 24 us -> 0 us
  between operations: 13.5 us -> 0.27 us
  waiting for transfers between devices: 8.84 us -> 17 us
  local copies, waits for them, and re-layouts: 1.6 us -> 5.41 us
    psum x1 -> x0, blocking collectives: 83.8 us -> none  [local(): summed = lax.psum(partial_value, 'gx')]
    pallas_call x0 -> x8, Pallas kernels: none -> 39.8 us  [the longest x4 16.8 us: project(): pl.pallas_call(functools.partial(project_kernel, n, rows, with_kv), out_s...]
    ppermute x0 -> x38, starting transfers between devices: none -> 39.8 us  [the longest x30 37.5 us: across(): return lax.ppermute(array, 'gx', [(g, g ^ mask) for g in range(n)])]
    all_gather x2 -> x0, blocking collectives: 34.8 us -> none  [the longest x1 32.2 us: local(): lax.all_gather(traded, 'gx', axis=0, tiled=True)]
    dot_general x6 -> x0, matrix products: 24 us -> none  [the longest x1 8.18 us: local(): jnp.dot(all_tokens, query_weight, preferred_element_type=jnp.float32)]
    ppermute x0 -> x38, waiting for transfers between devices: none -> 17 us  [the longest x30 13 us: across(): return lax.ppermute(array, 'gx', [(g, g ^ mask) for g in range(n)])]
    reduce_scatter x2 -> x0, waiting for transfers between devices: 7.43 us -> none  [the longest x1 7.43 us: local(): lax.psum_scatter(partial_out, 'gy', scatter_dimension=0, tiled=True)]
    unnamed x4 -> x16, local copies, waits for them, and re-layouts: 0.01 us -> 5.35 us
  transfers between devices with their start and end apart: 3 -> 38, of which waited for: 2 -> 14; matrix products, arithmetic and copies ran while one was open for 7% -> 0% of each run, Pallas kernels for 0% -> 30%
where the time goes in v1:
time: 104 us; the launch traced here: 103 us
  starting transfers between devices  39.8 us (38%)
  Pallas kernels  39.8 us (38%)
  waiting for transfers between devices  17 us (16%)
  local copies, waits for them, and re-layouts  5.41 us (5%)
  other arithmetic  1.14 us (1%)
    ppermute x30, starting transfers between devices, across(): return lax.ppermute(array, 'gx', [(g, g ^ mask) for g in range(n)])  37.5 us
    pallas_call x4, Pallas kernels, project(): pl.pallas_call(functools.partial(project_kernel, n, rows, with_kv), out_s...  16.8 us
    ppermute x30, waiting for transfers between devices, across(): return lax.ppermute(array, 'gx', [(g, g ^ mask) for g in range(n)])  13 us
    pallas_call x2, Pallas kernels, attend(): pl.pallas_call(functools.partial(attend_kernel, parts, per_part, offset),...  13 us
    pallas_call x2, Pallas kernels, project_out(): pl.pallas_call(functools.partial(output_kernel, n, rows, prior is not Non...  10.1 us
    unnamed x16, local copies, waits for them, and re-layouts  5.35 us
    ppermute x8, waiting for transfers between devices, swap(): return lax.ppermute(array, 'gy', [(0, 1), (1, 0)])  4.02 us
    ppermute x8, starting transfers between devices, swap(): return lax.ppermute(array, 'gy', [(0, 1), (1, 0)])  2.29 us
  transfers between devices with their start and end apart: 38, of which 14 were waited for; matrix products, arithmetic and copies ran while one was open for 0% of the time, Pallas kernels for 30%

profile of v1, /device:TPU:0, one launch (start us, length us, event | category | flops | bytes accessed | tf_op | source)
XLA Modules:
  0.0 103.4 jit_solution(2036749699943692283)
XLA Ops:
  0.5 1.3 %collective-permute-done.other_ref = bf16[64,2304]{1,0:T(8,128)(2,1)S(1)} collective-permute-done((bf16[64,2304]{1,0:T(8,128)(2,1)}, bf16[64,2304]{1,0:T(8,128)(2,1)S(1)}, u32[]{:S(2)}, u32[]{:S(2)}) %collective-permute-start) | collective-permute-done | bytes 294944 | tf_op jit(solution)/shard_map/ppermute | solution.py:269
  2.8 3.9 %project.7 = (f32[64,768]{1,0:T(8,128)S(1)}, f32[64,768]{1,0:T(8,128)S(1)}) custom-call(s32[2]{0:T(128)S(1)} %pad_add_fusion.ids_ref, bf16[64,2304]{1,0:T(8,128)(2,1)S(1)} %copy-done.4, bf16[64,2304]{1,0:T(8,128)(2,1)S(1)} %collective-permute-done.other_ref, bf16[2304,3072]{1,0:T(8,128)(2,1)} %w_ref.7), custom_call_target="tpu_custom_call" | custom-call | flops 452984832 | bytes 3932160 | tf_op jit(solution)/shard_map/project/pallas_call | solution.py:94
  6.8 3.0 %collective-permute-start.24 = (f32[64,768]{1,0:T(8,128)S(1)}, f32[64,768]{1,0:T(8,128)S(1)}, u32[]{:S(2)}, u32[]{:S(2)}) collective-permute-start(f32[64,768]{1,0:T(8,128)S(1)} %get-tuple-element.30), channel_id=1, source_target_pairs={{0,2},{2,0},{4,6},{6,4},{8,10},{10,8},{12,14},{14,12},{1,3},{3,1},... | collective-permute-start | bytes 589832 | tf_op jit(solution)/shard_map/ppermute | solution.py:272
  9.8 4.0 %project.5 = (f32[64,768]{1,0:T(8,128)S(1)}, f32[64,768]{1,0:T(8,128)S(1)}) custom-call(s32[2]{0:T(128)S(1)} %pad_add_fusion.ids_ref, bf16[64,2304]{1,0:T(8,128)(2,1)S(1)} %copy-done.5, bf16[64,2304]{1,0:T(8,128)(2,1)S(1)} %collective-permute-done.other_ref, bf16[2304,3072]{1,0:T(8,128)(2,1)} %w_ref.7), custom_call_target="tpu_custom_call" | custom-call | flops 452984832 | bytes 3932160 | tf_op jit(solution)/shard_map/project/pallas_call | solution.py:94
  13.9 4.0 %project.4 = (f32[64,768]{1,0:T(8,128)S(1)}, f32[64,768]{1,0:T(8,128)S(1)}) custom-call(s32[2]{0:T(128)S(1)} %pad_add_fusion.ids_ref, bf16[64,2304]{1,0:T(8,128)(2,1)S(1)} %copy-done.5, bf16[64,2304]{1,0:T(8,128)(2,1)S(1)} %collective-permute-done.other_ref, bf16[2304,3072]{1,0:T(8,128)(2,1)} %w_ref.7), custom_call_target="tpu_custom_call" | custom-call | flops 452984832 | bytes 3932160 | tf_op jit(solution)/shard_map/project/pallas_call | solution.py:94
  17.9 2.0 %collective-permute-start.1 = (f32[64,768]{1,0:T(8,128)S(1)}, f32[64,768]{1,0:T(8,128)S(1)}, u32[]{:S(2)}, u32[]{:S(2)}) collective-permute-start(f32[64,768]{1,0:T(8,128)S(1)} %get-tuple-element.22), channel_id=1, source_target_pairs={{0,2},{2,0},{4,6},{6,4},{8,10},{10,8},{12,14},{14,12},{1,3},{3,1},... | collective-permute-start | bytes 589832 | tf_op jit(solution)/shard_map/ppermute | solution.py:272
  19.9 4.9 %project.6 = (f32[64,1024]{1,0:T(8,128)S(1)}, f32[64,1024]{1,0:T(8,128)S(1)}) custom-call(s32[2]{0:T(128)S(1)} %pad_add_fusion.ids_ref, bf16[64,2304]{1,0:T(8,128)(2,1)S(1)} %copy-done.5, bf16[64,2304]{1,0:T(8,128)(2,1)S(1)} %collective-permute-done.other_ref, bf16[2304,3072]{1,0:T(8,128)(2,1)} %w_ref.7, bf16[2304,512]{1,0:T(8,128)(2,1)S(1)} %copy-done.6), custom_call_target="tpu_custom_call" | custom-call | flops 603979776 | bytes 5242880 | tf_op jit(solution)/shard_map/project/pallas_call | solution.py:94
  25.0 2.1 %collective-permute-start.25 = (f32[16,768]{1,0:T(8,128)S(1)}, f32[16,768]{1,0:T(8,128)S(1)}, u32[]{:S(2)}, u32[]{:S(2)}) collective-permute-start(f32[16,768]{1,0:T(8,128)S(1)} %get-tuple-element.40), channel_id=1, source_target_pairs={{0,4},{2,6},{4,0},{6,2},{8,12},{10,14},{12,8},{14,10},{1,5},{3,7},... | collective-permute-start | bytes 147464 | tf_op jit(solution)/shard_map/ppermute | solution.py:272
  27.2 4.0 %collective-permute-start.8 = (f32[16,768]{1,0:T(8,128)S(1)}, f32[16,768]{1,0:T(8,128)S(1)}, u32[]{:S(2)}, u32[]{:S(2)}) collective-permute-start(f32[16,768]{1,0:T(8,128)S(1)} %get-tuple-element.44), channel_id=1, source_target_pairs={{0,12},{2,14},{4,8},{6,10},{8,4},{10,6},{12,0},{14,2},{1,13},{3,15... | collective-permute-start | bytes 147464 | tf_op jit(solution)/shard_map/ppermute | solution.py:272
  31.8 2.0 %collective-permute-done.8 = f32[16,768]{1,0:T(8,128)S(1)} collective-permute-done((f32[16,768]{1,0:T(8,128)S(1)}, f32[16,768]{1,0:T(8,128)S(1)}, u32[]{:S(2)}, u32[]{:S(2)}) %collective-permute-start.8) | collective-permute-done | bytes 49184 | tf_op jit(solution)/shard_map/ppermute | solution.py:272
  33.9 3.3 %collective-permute-start.4 = (f32[16,768]{1,0:T(8,128)S(1)}, f32[16,768]{1,0:T(8,128)S(1)}, u32[]{:S(2)}, u32[]{:S(2)}) collective-permute-start(f32[16,768]{1,0:T(8,128)S(1)} %get-tuple-element.47), channel_id=1, source_target_pairs={{0,12},{2,14},{4,8},{6,10},{8,4},{10,6},{12,0},{14,2},{1,13},{3,15... | collective-permute-start | bytes 147464 | tf_op jit(solution)/shard_map/ppermute | solution.py:272
  37.2 1.7 %collective-permute-start.27 = (f32[16,768]{1,0:T(8,128)S(1)}, f32[16,768]{1,0:T(8,128)S(1)}, u32[]{:S(2)}, u32[]{:S(2)}) collective-permute-start(f32[16,768]{1,0:T(8,128)S(1)} %get-tuple-element.41), channel_id=1, source_target_pairs={{0,12},{2,14},{4,8},{6,10},{8,4},{10,6},{12,0},{14,2},{1,13},{3,15... | collective-permute-start | bytes 147464 | tf_op jit(solution)/shard_map/ppermute | solution.py:272
  39.9 1.3 %collective-permute-start.26 = (f32[16,768]{1,0:T(8,128)S(1)}, f32[16,768]{1,0:T(8,128)S(1)}, u32[]{:S(2)}, u32[]{:S(2)}) collective-permute-start(f32[16,768]{1,0:T(8,128)S(1)} %get-tuple-element.42), channel_id=1, source_target_pairs={{0,8},{2,10},{4,12},{6,14},{8,0},{10,2},{12,4},{14,6},{1,9},{3,11}... | collective-permute-start | bytes 147464 | tf_op jit(solution)/shard_map/ppermute | solution.py:272
  42.9 1.5 %collective-permute-start.12 = (f32[16,1024]{1,0:T(8,128)S(1)}, f32[16,1024]{1,0:T(8,128)S(1)}, u32[]{:S(2)}, u32[]{:S(2)}) collective-permute-start(f32[16,1024]{1,0:T(8,128)S(1)} %get-tuple-element.37), channel_id=1, source_target_pairs={{0,4},{2,6},{4,0},{6,2},{8,12},{10,14},{12,8},{14,10},{1,5},{3,7},... | collective-permute-start | bytes 196616 | tf_op jit(solution)/shard_map/ppermute | solution.py:272
  47.3 3.6 %collective-permute-done.14 = f32[16,1024]{1,0:T(8,128)S(1)} collective-permute-done((f32[16,1024]{1,0:T(8,128)S(1)}, f32[16,1024]{1,0:T(8,128)S(1)}, u32[]{:S(2)}, u32[]{:S(2)}) %collective-permute-start.14) | collective-permute-done | bytes 65568 | tf_op jit(solution)/shard_map/ppermute | solution.py:272
  50.8 2.1 %collective-permute-done.13 = f32[16,1024]{1,0:T(8,128)S(1)} collective-permute-done((f32[16,1024]{1,0:T(8,128)S(1)}, f32[16,1024]{1,0:T(8,128)S(1)}, u32[]{:S(2)}, u32[]{:S(2)}) %collective-permute-start.13) | collective-permute-done | bytes 65568 | tf_op jit(solution)/shard_map/ppermute | solution.py:272
  54.3 6.5 %attend.2 = (bf16[8,1536]{1,0:T(8,128)(2,1)S(1)}, bf16[8,1536]{1,0:T(8,128)(2,1)S(1)}) custom-call(s32[9]{0:T(128)S(1)} %pad_add_fusion.1.scalars_ref, bf16[8,768]{1,0:T(8,128)(2,1)S(1)} %get-tuple-element.56.refs_0_, bf16[8,768]{1,0:T(8,128)(2,1)S(1)} %get-tuple-element.54.refs_1_, bf16[8,768]{1,0:T(8,128)(2,1)S(1)} %collective-permute-done.9.refs_2_, ...), custom_call_target="tpu_custom_call" | custom-call | flops 134217728 | bytes 8388608 | tf_op jit(solution)/shard_map/attend/pallas_call | solution.py:176
  61.0 2.2 %copy-done.1 = bf16[8,1024,256]{2,1,0:T(8,128)(2,1)S(1)} copy-done((bf16[8,1024,256]{2,1,0:T(8,128)(2,1)S(1)}, bf16[8,1024,256]{2,1,0:T(8,128)(2,1)}, u32[]{:S(2)}) %copy-start.1) | copy-done | bytes 4194328
  63.2 2.2 %copy-done.3 = bf16[8,1024,256]{2,1,0:T(8,128)(2,1)S(1)} copy-done((bf16[8,1024,256]{2,1,0:T(8,128)(2,1)S(1)}, bf16[8,1024,256]{2,1,0:T(8,128)(2,1)}, u32[]{:S(2)}) %copy-start.3) | copy-done | bytes 4194328
  65.4 6.5 %attend.3 = (bf16[8,1536]{1,0:T(8,128)(2,1)S(1)}, bf16[8,1536]{1,0:T(8,128)(2,1)S(1)}) custom-call(s32[9]{0:T(128)S(1)} %pad_add_fusion.1.scalars_ref, bf16[8,768]{1,0:T(8,128)(2,1)S(1)} %slice.158.refs_0_, bf16[8,768]{1,0:T(8,128)(2,1)S(1)} %get-tuple-element.52.refs_1_, bf16[8,768]{1,0:T(8,128)(2,1)S(1)} %slice.163.refs_2_, ...), custom_call_target="tpu_custom_call" | custom-call | flops 134217728 | bytes 8388608 | tf_op jit(solution)/shard_map/attend/pallas_call | solution.py:176
  72.3 1.8 %collective-permute-start.22 = (bf16[16,1536]{1,0:T(8,128)(2,1)S(1)}, bf16[16,1536]{1,0:T(8,128)(2,1)S(1)}, u32[]{:S(2)}, u32[]{:S(2)}) collective-permute-start(bf16[16,1536]{1,0:T(8,128)(2,1)S(1)} %maximum_select_fusion.refs_0_), channel_id=1, source_target_pairs={{0,12},{2,14},{4,8},{6,10},{8,4},{10,6},{12,0},{14,2},{1,13},{3,15... | collective-permute-start | bytes 147464 | tf_op jit(solution)/shard_map/ppermute | solution.py:272
  74.1 2.2 %collective-permute-start.35 = (bf16[16,1536]{1,0:T(8,128)(2,1)S(1)}, bf16[16,1536]{1,0:T(8,128)(2,1)S(1)}, u32[]{:S(2)}, u32[]{:S(2)}) collective-permute-start(bf16[16,1536]{1,0:T(8,128)(2,1)S(1)} %maximum_select_fusion.1.refs_0_), channel_id=1, source_target_pairs={{0,12},{2,14},{4,8},{6,10},{8,4},{10,6},{12,0},{14,2},{1,13},{3,15... | collective-permute-start | bytes 147464 | tf_op jit(solution)/shard_map/ppermute | solution.py:272
  76.3 2.0 %collective-permute-start.33 = (bf16[16,1536]{1,0:T(8,128)(2,1)S(1)}, bf16[16,1536]{1,0:T(8,128)(2,1)S(1)}, u32[]{:S(2)}, u32[]{:S(2)}) collective-permute-start(bf16[16,1536]{1,0:T(8,128)(2,1)S(1)} %maximum_select_fusion.1.refs_0_), channel_id=1, source_target_pairs={{0,8},{2,10},{4,12},{6,14},{8,0},{10,2},{12,4},{14,6},{1,9},{3,11}... | collective-permute-start | bytes 147464 | tf_op jit(solution)/shard_map/ppermute | solution.py:272
  78.7 1.6 %collective-permute-start.18 = (bf16[16,1536]{1,0:T(8,128)(2,1)S(1)}, bf16[16,1536]{1,0:T(8,128)(2,1)S(1)}, u32[]{:S(2)}, u32[]{:S(2)}) collective-permute-start(bf16[16,1536]{1,0:T(8,128)(2,1)S(1)} %maximum_select_fusion.refs_0_), channel_id=1, source_target_pairs={{0,4},{2,6},{4,0},{6,2},{8,12},{10,14},{12,8},{14,10},{1,5},{3,7},... | collective-permute-start | bytes 147464 | tf_op jit(solution)/shard_map/ppermute | solution.py:272
  80.3 1.6 %collective-permute-done.20.refs_4_ = bf16[16,1536]{1,0:T(8,128)(2,1)S(1)} collective-permute-done((bf16[16,1536]{1,0:T(8,128)(2,1)S(1)}, bf16[16,1536]{1,0:T(8,128)(2,1)S(1)}, u32[]{:S(2)}, u32[]{:S(2)}) %collective-permute-start.20) | collective-permute-done | bytes 49184 | tf_op jit(solution)/shard_map/ppermute | solution.py:272
  81.9 1.3 %collective-permute-start.30 = (bf16[16,1536]{1,0:T(8,128)(2,1)S(1)}, bf16[16,1536]{1,0:T(8,128)(2,1)S(1)}, u32[]{:S(2)}, u32[]{:S(2)}) collective-permute-start(bf16[16,1536]{1,0:T(8,128)(2,1)S(1)} %maximum_select_fusion.1.refs_0_), channel_id=1, source_target_pairs={{0,2},{2,0},{4,6},{6,4},{8,10},{10,8},{12,14},{14,12},{1,3},{3,1},... | collective-permute-start | bytes 147464 | tf_op jit(solution)/shard_map/ppermute | solution.py:272
  84.3 1.6 %collective-permute-start.34 = (bf16[16,1536]{1,0:T(8,128)(2,1)S(1)}, bf16[16,1536]{1,0:T(8,128)(2,1)S(1)}, u32[]{:S(2)}, u32[]{:S(2)}) collective-permute-start(bf16[16,1536]{1,0:T(8,128)(2,1)S(1)} %collective-permute-done.33.refs_4_), channel_id=1, source_target_pairs={{0,2},{2,0},{4,6},{6,4},{8,10},{10,8},{12,14},{14,12},{1,3},{3,1},... | collective-permute-start | bytes 147464 | tf_op jit(solution)/shard_map/ppermute | solution.py:272
  86.3 1.6 %collective-permute-start.17 = (bf16[16,1536]{1,0:T(8,128)(2,1)S(1)}, bf16[16,1536]{1,0:T(8,128)(2,1)S(1)}, u32[]{:S(2)}, u32[]{:S(2)}) collective-permute-start(bf16[16,1536]{1,0:T(8,128)(2,1)S(1)} %maximum_select_fusion.refs_0_), channel_id=1, source_target_pairs={{0,2},{2,0},{4,6},{6,4},{8,10},{10,8},{12,14},{14,12},{1,3},{3,1},... | collective-permute-start | bytes 147464 | tf_op jit(solution)/shard_map/ppermute | solution.py:272
  88.4 1.6 %collective-permute-start.21 = (bf16[16,1536]{1,0:T(8,128)(2,1)S(1)}, bf16[16,1536]{1,0:T(8,128)(2,1)S(1)}, u32[]{:S(2)}, u32[]{:S(2)}) collective-permute-start(bf16[16,1536]{1,0:T(8,128)(2,1)S(1)} %collective-permute-done.20.refs_4_), channel_id=1, source_target_pairs={{0,2},{2,0},{4,6},{6,4},{8,10},{10,8},{12,14},{14,12},{1,3},{3,1},... | collective-permute-start | bytes 147464 | tf_op jit(solution)/shard_map/ppermute | solution.py:272
  90.4 5.0 %project_out.2 = (f32[64,2304]{1,0:T(8,128)S(1)}, f32[64,2304]{1,0:T(8,128)S(1)}) custom-call(s32[2]{0:T(128)S(1)} %pad_add_fusion.ids_ref, bf16[16,1536]{1,0:T(8,128)(2,1)S(1)} %maximum_select_fusion.1.refs_0_, bf16[16,1536]{1,0:T(8,128)(2,1)S(1)} %collective-permute-done.30.refs_1_, bf16[16,1536]{1,0:T(8,128)(2,1)S(1)} %collective-permute-done.31.refs_2_, ...), custom_call_target="tpu_custom_call" | custom-call | flops 905969664 | bytes 8257536 | tf_op jit(solution)/shard_map/project_out/pallas_call | solution.py:239
  95.5 5.0 %project_out.3 = (f32[64,2304]{1,0:T(8,128)S(1)}, f32[64,2304]{1,0:T(8,128)S(1)}) custom-call(s32[2]{0:T(128)S(1)} %pad_add_fusion.ids_ref, bf16[16,1536]{1,0:T(8,128)(2,1)S(1)} %maximum_select_fusion.refs_0_, bf16[16,1536]{1,0:T(8,128)(2,1)S(1)} %collective-permute-done.17.refs_1_, bf16[16,1536]{1,0:T(8,128)(2,1)S(1)} %collective-permute-done.18.refs_2_, ...), custom_call_target="tpu_custom_call" | custom-call | flops 905969664 | bytes 8257536 | tf_op jit(solution)/shard_map/project_out/pallas_call | solution.py:239
  100.6 2.0 %collective-permute-done.37 = f32[64,2304]{1,0:T(8,128)S(1)} collective-permute-done((f32[64,2304]{1,0:T(8,128)S(1)}, f32[64,2304]{1,0:T(8,128)S(1)}, u32[]{:S(2)}, u32[]{:S(2)}) %collective-permute-start.37) | collective-permute-done | bytes 589856 | tf_op jit(solution)/shard_map/ppermute | solution.py:269
  (89 shorter events, 13.6 us)
Async XLA Ops:
  6.8 18.2 %collective-permute-start.24 = (f32[64,768]{1,0:T(8,128)S(1)}, f32[64,768]{1,0:T(8,128)S(1)}, u32[]{:S(2)}, u32[]{:S(2)}) collective-permute-start(f32[64,768]{1,0:T(8,128)S(1)} %get-tuple-element.30), channel_id=1, source_target_pairs={{0,2},{2,0},{4,6},{6,4},{8,10},{10,8},{12,14},{14,12},{1,3},{3,1},... | collective-permute-start | bytes 589832 | tf_op jit(solution)/shard_map/ppermute | solution.py:272
  13.8 13.2 %collective-permute-start.5 = (f32[64,768]{1,0:T(8,128)S(1)}, f32[64,768]{1,0:T(8,128)S(1)}, u32[]{:S(2)}, u32[]{:S(2)}) collective-permute-start(f32[64,768]{1,0:T(8,128)S(1)} %get-tuple-element.24), channel_id=1, source_target_pairs={{0,2},{2,0},{4,6},{6,4},{8,10},{10,8},{12,14},{14,12},{1,3},{3,1},... | collective-permute-start | bytes 589832 | tf_op jit(solution)/shard_map/ppermute | solution.py:272
  17.9 13.3 %collective-permute-start.1 = (f32[64,768]{1,0:T(8,128)S(1)}, f32[64,768]{1,0:T(8,128)S(1)}, u32[]{:S(2)}, u32[]{:S(2)}) collective-permute-start(f32[64,768]{1,0:T(8,128)S(1)} %get-tuple-element.22), channel_id=1, source_target_pairs={{0,2},{2,0},{4,6},{6,4},{8,10},{10,8},{12,14},{14,12},{1,3},{3,1},... | collective-permute-start | bytes 589832 | tf_op jit(solution)/shard_map/ppermute | solution.py:272
  24.8 17.5 %collective-permute-start.11 = (f32[64,1024]{1,0:T(8,128)S(1)}, f32[64,1024]{1,0:T(8,128)S(1)}, u32[]{:S(2)}, u32[]{:S(2)}) collective-permute-start(f32[64,1024]{1,0:T(8,128)S(1)} %get-tuple-element.26), channel_id=1, source_target_pairs={{0,2},{2,0},{4,6},{6,4},{8,10},{10,8},{12,14},{14,12},{1,3},{3,1},... | collective-permute-start | bytes 786440 | tf_op jit(solution)/shard_map/ppermute | solution.py:272
  25.0 17.9 %collective-permute-start.25 = (f32[16,768]{1,0:T(8,128)S(1)}, f32[16,768]{1,0:T(8,128)S(1)}, u32[]{:S(2)}, u32[]{:S(2)}) collective-permute-start(f32[16,768]{1,0:T(8,128)S(1)} %get-tuple-element.40), channel_id=1, source_target_pairs={{0,4},{2,6},{4,0},{6,2},{8,12},{10,14},{12,8},{14,10},{1,5},{3,7},... | collective-permute-start | bytes 147464 | tf_op jit(solution)/shard_map/ppermute | solution.py:272
  27.2 6.7 %collective-permute-start.8 = (f32[16,768]{1,0:T(8,128)S(1)}, f32[16,768]{1,0:T(8,128)S(1)}, u32[]{:S(2)}, u32[]{:S(2)}) collective-permute-start(f32[16,768]{1,0:T(8,128)S(1)} %get-tuple-element.44), channel_id=1, source_target_pairs={{0,12},{2,14},{4,8},{6,10},{8,4},{10,6},{12,0},{14,2},{1,13},{3,15... | collective-permute-start | bytes 147464 | tf_op jit(solution)/shard_map/ppermute | solution.py:272
  31.2 6.0 %collective-permute-start.7 = (f32[16,768]{1,0:T(8,128)S(1)}, f32[16,768]{1,0:T(8,128)S(1)}, u32[]{:S(2)}, u32[]{:S(2)}) collective-permute-start(f32[16,768]{1,0:T(8,128)S(1)} %get-tuple-element.45), channel_id=1, source_target_pairs={{0,8},{2,10},{4,12},{6,14},{8,0},{10,2},{12,4},{14,6},{1,9},{3,11}... | collective-permute-start | bytes 147464 | tf_op jit(solution)/shard_map/ppermute | solution.py:272
  31.4 5.9 %collective-permute-start.2 = (f32[16,768]{1,0:T(8,128)S(1)}, f32[16,768]{1,0:T(8,128)S(1)}, u32[]{:S(2)}, u32[]{:S(2)}) collective-permute-start(f32[16,768]{1,0:T(8,128)S(1)} %get-tuple-element.46), channel_id=1, source_target_pairs={{0,4},{2,6},{4,0},{6,2},{8,12},{10,14},{12,8},{14,10},{1,5},{3,7},... | collective-permute-start | bytes 147464 | tf_op jit(solution)/shard_map/ppermute | solution.py:272
  33.9 6.0 %collective-permute-start.4 = (f32[16,768]{1,0:T(8,128)S(1)}, f32[16,768]{1,0:T(8,128)S(1)}, u32[]{:S(2)}, u32[]{:S(2)}) collective-permute-start(f32[16,768]{1,0:T(8,128)S(1)} %get-tuple-element.47), channel_id=1, source_target_pairs={{0,12},{2,14},{4,8},{6,10},{8,4},{10,6},{12,0},{14,2},{1,13},{3,15... | collective-permute-start | bytes 147464 | tf_op jit(solution)/shard_map/ppermute | solution.py:272
  37.2 5.1 %collective-permute-start.3 = (f32[16,768]{1,0:T(8,128)S(1)}, f32[16,768]{1,0:T(8,128)S(1)}, u32[]{:S(2)}, u32[]{:S(2)}) collective-permute-start(f32[16,768]{1,0:T(8,128)S(1)} %get-tuple-element.48), channel_id=1, source_target_pairs={{0,8},{2,10},{4,12},{6,14},{8,0},{10,2},{12,4},{14,6},{1,9},{3,11}... | collective-permute-start | bytes 147464 | tf_op jit(solution)/shard_map/ppermute | solution.py:272
  37.2 7.2 %collective-permute-start.27 = (f32[16,768]{1,0:T(8,128)S(1)}, f32[16,768]{1,0:T(8,128)S(1)}, u32[]{:S(2)}, u32[]{:S(2)}) collective-permute-start(f32[16,768]{1,0:T(8,128)S(1)} %get-tuple-element.41), channel_id=1, source_target_pairs={{0,12},{2,14},{4,8},{6,10},{8,4},{10,6},{12,0},{14,2},{1,13},{3,15... | collective-permute-start | bytes 147464 | tf_op jit(solution)/shard_map/ppermute | solution.py:272
  39.9 5.5 %collective-permute-start.26 = (f32[16,768]{1,0:T(8,128)S(1)}, f32[16,768]{1,0:T(8,128)S(1)}, u32[]{:S(2)}, u32[]{:S(2)}) collective-permute-start(f32[16,768]{1,0:T(8,128)S(1)} %get-tuple-element.42), channel_id=1, source_target_pairs={{0,8},{2,10},{4,12},{6,14},{8,0},{10,2},{12,4},{14,6},{1,9},{3,11}... | collective-permute-start | bytes 147464 | tf_op jit(solution)/shard_map/ppermute | solution.py:272
  42.3 12.0 %collective-permute-start.10 = (bf16[8,768]{1,0:T(8,128)(2,1)S(1)}, bf16[8,768]{1,0:T(8,128)(2,1)S(1)}, u32[]{:S(2)}, u32[]{:S(2)}) collective-permute-start(bf16[8,768]{1,0:T(8,128)(2,1)S(1)} %get-tuple-element.53), channel_id=1, source_target_pairs={{0,1},{1,0},{2,3},{3,2},{4,5},{5,4},{6,7},{7,6},{8,9},{9,8},{10,11... | collective-permute-start | bytes 36872 | tf_op jit(solution)/shard_map/ppermute | solution.py:269
  42.3 11.9 %collective-permute-start.9 = (bf16[8,768]{1,0:T(8,128)(2,1)S(1)}, bf16[8,768]{1,0:T(8,128)(2,1)S(1)}, u32[]{:S(2)}, u32[]{:S(2)}) collective-permute-start(bf16[8,768]{1,0:T(8,128)(2,1)S(1)} %get-tuple-element.55), channel_id=1, source_target_pairs={{0,1},{1,0},{2,3},{3,2},{4,5},{5,4},{6,7},{7,6},{8,9},{9,8},{10,11... | collective-permute-start | bytes 36872 | tf_op jit(solution)/shard_map/ppermute | solution.py:269
  44.5 6.3 %collective-permute-start.14 = (f32[16,1024]{1,0:T(8,128)S(1)}, f32[16,1024]{1,0:T(8,128)S(1)}, u32[]{:S(2)}, u32[]{:S(2)}) collective-permute-start(f32[16,1024]{1,0:T(8,128)S(1)} %get-tuple-element.38), channel_id=1, source_target_pairs={{0,12},{2,14},{4,8},{6,10},{8,4},{10,6},{12,0},{14,2},{1,13},{3,15... | collective-permute-start | bytes 196616 | tf_op jit(solution)/shard_map/ppermute | solution.py:272
  45.4 7.6 %collective-permute-start.13 = (f32[16,1024]{1,0:T(8,128)S(1)}, f32[16,1024]{1,0:T(8,128)S(1)}, u32[]{:S(2)}, u32[]{:S(2)}) collective-permute-start(f32[16,1024]{1,0:T(8,128)S(1)} %get-tuple-element.39), channel_id=1, source_target_pairs={{0,8},{2,10},{4,12},{6,14},{8,0},{10,2},{12,4},{14,6},{1,9},{3,11}... | collective-permute-start | bytes 196616 | tf_op jit(solution)/shard_map/ppermute | solution.py:272
  53.1 7.9 %collective-permute-start.28 = (bf16[8,768]{1,0:T(8,128)(2,1)S(1)}, bf16[8,768]{1,0:T(8,128)(2,1)S(1)}, u32[]{:S(2)}, u32[]{:S(2)}) collective-permute-start(bf16[8,768]{1,0:T(8,128)(2,1)S(1)} %get-tuple-element.51), channel_id=1, source_target_pairs={{0,1},{1,0},{2,3},{3,2},{4,5},{5,4},{6,7},{7,6},{8,9},{9,8},{10,11... | collective-permute-start | bytes 36872 | tf_op jit(solution)/shard_map/ppermute | solution.py:269
  60.8 11.5 %collective-permute-start.16 = (bf16[8,1536]{1,0:T(8,128)(2,1)S(1)}, bf16[8,1536]{1,0:T(8,128)(2,1)S(1)}, u32[]{:S(2)}, u32[]{:S(2)}) collective-permute-start(bf16[8,1536]{1,0:T(8,128)(2,1)S(1)} %get-tuple-element.28), channel_id=1, source_target_pairs={{0,1},{1,0},{2,3},{3,2},{4,5},{5,4},{6,7},{7,6},{8,9},{9,8},{10,11... | collective-permute-start | bytes 73736 | tf_op jit(solution)/shard_map/ppermute | solution.py:269
  72.3 6.4 %collective-permute-start.22 = (bf16[16,1536]{1,0:T(8,128)(2,1)S(1)}, bf16[16,1536]{1,0:T(8,128)(2,1)S(1)}, u32[]{:S(2)}, u32[]{:S(2)}) collective-permute-start(bf16[16,1536]{1,0:T(8,128)(2,1)S(1)} %maximum_select_fusion.refs_0_), channel_id=1, source_target_pairs={{0,12},{2,14},{4,8},{6,10},{8,4},{10,6},{12,0},{14,2},{1,13},{3,15... | collective-permute-start | bytes 147464 | tf_op jit(solution)/shard_map/ppermute | solution.py:272
  74.1 7.9 %collective-permute-start.20 = (bf16[16,1536]{1,0:T(8,128)(2,1)S(1)}, bf16[16,1536]{1,0:T(8,128)(2,1)S(1)}, u32[]{:S(2)}, u32[]{:S(2)}) collective-permute-start(bf16[16,1536]{1,0:T(8,128)(2,1)S(1)} %maximum_select_fusion.refs_0_), channel_id=1, source_target_pairs={{0,8},{2,10},{4,12},{6,14},{8,0},{10,2},{12,4},{14,6},{1,9},{3,11}... | collective-permute-start | bytes 147464 | tf_op jit(solution)/shard_map/ppermute | solution.py:272
  74.1 9.2 %collective-permute-start.35 = (bf16[16,1536]{1,0:T(8,128)(2,1)S(1)}, bf16[16,1536]{1,0:T(8,128)(2,1)S(1)}, u32[]{:S(2)}, u32[]{:S(2)}) collective-permute-start(bf16[16,1536]{1,0:T(8,128)(2,1)S(1)} %maximum_select_fusion.1.refs_0_), channel_id=1, source_target_pairs={{0,12},{2,14},{4,8},{6,10},{8,4},{10,6},{12,0},{14,2},{1,13},{3,15... | collective-permute-start | bytes 147464 | tf_op jit(solution)/shard_map/ppermute | solution.py:272
  76.3 8.0 %collective-permute-start.33 = (bf16[16,1536]{1,0:T(8,128)(2,1)S(1)}, bf16[16,1536]{1,0:T(8,128)(2,1)S(1)}, u32[]{:S(2)}, u32[]{:S(2)}) collective-permute-start(bf16[16,1536]{1,0:T(8,128)(2,1)S(1)} %maximum_select_fusion.1.refs_0_), channel_id=1, source_target_pairs={{0,8},{2,10},{4,12},{6,14},{8,0},{10,2},{12,4},{14,6},{1,9},{3,11}... | collective-permute-start | bytes 147464 | tf_op jit(solution)/shard_map/ppermute | solution.py:272
  78.3 7.6 %collective-permute-start.31 = (bf16[16,1536]{1,0:T(8,128)(2,1)S(1)}, bf16[16,1536]{1,0:T(8,128)(2,1)S(1)}, u32[]{:S(2)}, u32[]{:S(2)}) collective-permute-start(bf16[16,1536]{1,0:T(8,128)(2,1)S(1)} %maximum_select_fusion.1.refs_0_), channel_id=1, source_target_pairs={{0,4},{2,6},{4,0},{6,2},{8,12},{10,14},{12,8},{14,10},{1,5},{3,7},... | collective-permute-start | bytes 147464 | tf_op jit(solution)/shard_map/ppermute | solution.py:272
  78.7 7.6 %collective-permute-start.18 = (bf16[16,1536]{1,0:T(8,128)(2,1)S(1)}, bf16[16,1536]{1,0:T(8,128)(2,1)S(1)}, u32[]{:S(2)}, u32[]{:S(2)}) collective-permute-start(bf16[16,1536]{1,0:T(8,128)(2,1)S(1)} %maximum_select_fusion.refs_0_), channel_id=1, source_target_pairs={{0,4},{2,6},{4,0},{6,2},{8,12},{10,14},{12,8},{14,10},{1,5},{3,7},... | collective-permute-start | bytes 147464 | tf_op jit(solution)/shard_map/ppermute | solution.py:272
  81.9 6.0 %collective-permute-start.30 = (bf16[16,1536]{1,0:T(8,128)(2,1)S(1)}, bf16[16,1536]{1,0:T(8,128)(2,1)S(1)}, u32[]{:S(2)}, u32[]{:S(2)}) collective-permute-start(bf16[16,1536]{1,0:T(8,128)(2,1)S(1)} %maximum_select_fusion.1.refs_0_), channel_id=1, source_target_pairs={{0,2},{2,0},{4,6},{6,4},{8,10},{10,8},{12,14},{14,12},{1,3},{3,1},... | collective-permute-start | bytes 147464 | tf_op jit(solution)/shard_map/ppermute | solution.py:272
  83.3 5.1 %collective-permute-start.36 = (bf16[16,1536]{1,0:T(8,128)(2,1)S(1)}, bf16[16,1536]{1,0:T(8,128)(2,1)S(1)}, u32[]{:S(2)}, u32[]{:S(2)}) collective-permute-start(bf16[16,1536]{1,0:T(8,128)(2,1)S(1)} %collective-permute-done.35.refs_6_), channel_id=1, source_target_pairs={{0,2},{2,0},{4,6},{6,4},{8,10},{10,8},{12,14},{14,12},{1,3},{3,1},... | collective-permute-start | bytes 147464 | tf_op jit(solution)/shard_map/ppermute | solution.py:272
  84.3 5.7 %collective-permute-start.34 = (bf16[16,1536]{1,0:T(8,128)(2,1)S(1)}, bf16[16,1536]{1,0:T(8,128)(2,1)S(1)}, u32[]{:S(2)}, u32[]{:S(2)}) collective-permute-start(bf16[16,1536]{1,0:T(8,128)(2,1)S(1)} %collective-permute-done.33.refs_4_), channel_id=1, source_target_pairs={{0,2},{2,0},{4,6},{6,4},{8,10},{10,8},{12,14},{14,12},{1,3},{3,1},... | collective-permute-start | bytes 147464 | tf_op jit(solution)/shard_map/ppermute | solution.py:272
  85.9 4.5 %collective-permute-start.32 = (bf16[16,1536]{1,0:T(8,128)(2,1)S(1)}, bf16[16,1536]{1,0:T(8,128)(2,1)S(1)}, u32[]{:S(2)}, u32[]{:S(2)}) collective-permute-start(bf16[16,1536]{1,0:T(8,128)(2,1)S(1)} %collective-permute-done.31.refs_2_), channel_id=1, source_target_pairs={{0,2},{2,0},{4,6},{6,4},{8,10},{10,8},{12,14},{14,12},{1,3},{3,1},... | collective-permute-start | bytes 147464 | tf_op jit(solution)/shard_map/ppermute | solution.py:272
  86.3 9.2 %collective-permute-start.17 = (bf16[16,1536]{1,0:T(8,128)(2,1)S(1)}, bf16[16,1536]{1,0:T(8,128)(2,1)S(1)}, u32[]{:S(2)}, u32[]{:S(2)}) collective-permute-start(bf16[16,1536]{1,0:T(8,128)(2,1)S(1)} %maximum_select_fusion.refs_0_), channel_id=1, source_target_pairs={{0,2},{2,0},{4,6},{6,4},{8,10},{10,8},{12,14},{14,12},{1,3},{3,1},... | collective-permute-start | bytes 147464 | tf_op jit(solution)/shard_map/ppermute | solution.py:272
  87.9 7.5 %collective-permute-start.23 = (bf16[16,1536]{1,0:T(8,128)(2,1)S(1)}, bf16[16,1536]{1,0:T(8,128)(2,1)S(1)}, u32[]{:S(2)}, u32[]{:S(2)}) collective-permute-start(bf16[16,1536]{1,0:T(8,128)(2,1)S(1)} %collective-permute-done.22.refs_6_), channel_id=1, source_target_pairs={{0,2},{2,0},{4,6},{6,4},{8,10},{10,8},{12,14},{14,12},{1,3},{3,1},... | collective-permute-start | bytes 147464 | tf_op jit(solution)/shard_map/ppermute | solution.py:272
  88.4 7.1 %collective-permute-start.21 = (bf16[16,1536]{1,0:T(8,128)(2,1)S(1)}, bf16[16,1536]{1,0:T(8,128)(2,1)S(1)}, u32[]{:S(2)}, u32[]{:S(2)}) collective-permute-start(bf16[16,1536]{1,0:T(8,128)(2,1)S(1)} %collective-permute-done.20.refs_4_), channel_id=1, source_target_pairs={{0,2},{2,0},{4,6},{6,4},{8,10},{10,8},{12,14},{14,12},{1,3},{3,1},... | collective-permute-start | bytes 147464 | tf_op jit(solution)/shard_map/ppermute | solution.py:272
  90.0 5.5 %collective-permute-start.19 = (bf16[16,1536]{1,0:T(8,128)(2,1)S(1)}, bf16[16,1536]{1,0:T(8,128)(2,1)S(1)}, u32[]{:S(2)}, u32[]{:S(2)}) collective-permute-start(bf16[16,1536]{1,0:T(8,128)(2,1)S(1)} %collective-permute-done.18.refs_2_), channel_id=1, source_target_pairs={{0,2},{2,0},{4,6},{6,4},{8,10},{10,8},{12,14},{14,12},{1,3},{3,1},... | collective-permute-start | bytes 147464 | tf_op jit(solution)/shard_map/ppermute | solution.py:272
  (14 other events, 110.0 us)

commit v2 on v0

v2 whole, which is shorter than its diff:
```python
import functools

import jax
import jax.numpy as jnp
from jax import lax
from jax.experimental import pallas as pl
from jax.experimental.pallas import tpu as pltpu
from jax.sharding import PartitionSpec as P

H = 24
DH = 256
MIB = 1024 * 1024
ANY = pl.BlockSpec(memory_space=pl.ANY)
VMEM = pl.BlockSpec(memory_space=pltpu.VMEM)
SMEM = pl.BlockSpec(memory_space=pltpu.SMEM)


def tile_of(width, wanted):
    while wanted >= 128:
        if width % wanted == 0:
            return wanted
        wanted -= 128
    return width


def order_of(bits):
    order = [0]
    for bit in reversed(bits):
        order = order + [j + bit for j in order]
    return order


def project_kernel(order, rows, first, tile, kv_width, ids_ref, own_ref, other_ref, w_ref, *refs):
    if kv_width:
        kv_ref, send_ref, keep_ref, xs_ref, ws_ref, kvs_ref, row_sem, w_sem, kv_sem = refs
    else:
        send_ref, keep_ref, xs_ref, ws_ref, row_sem, w_sem = refs
    n = len(order)
    half = n // 2
    tiles = ws_ref.shape[0]
    me, core = ids_ref[0], ids_ref[1]

    def row_copy(source_ref, p):
        block = jnp.bitwise_xor(me, order[p])
        source = pl.ds(pl.multiple_of((block % half) * rows, rows), rows)
        return pltpu.make_async_copy(
            source_ref.at[source, :], xs_ref.at[pl.ds(p * rows, rows), :], row_sem.at[p]
        )

    def weight_copy(t):
        return pltpu.make_async_copy(
            w_ref.at[:, pl.ds(first + t * tile, tile)], ws_ref.at[t], w_sem.at[t]
        )

    for p in range(n):
        mine = jnp.bitwise_xor(me, order[p]) // half == core

        @pl.when(mine)
        def _():
            row_copy(own_ref, p).start()

        @pl.when(jnp.logical_not(mine))
        def _():
            row_copy(other_ref, p).start()

    if kv_width:
        kv_copy = pltpu.make_async_copy(
            kv_ref.at[:, pl.ds(pl.multiple_of(core * kv_width, kv_width), kv_width)], kvs_ref, kv_sem
        )
        kv_copy.start()
    for t in range(tiles):
        weight_copy(t).start()
    for p in range(n):
        row_copy(own_ref, p).wait()

    cut = half * rows

    def put(weight, at, width):
        total = jnp.dot(xs_ref[...], weight, preferred_element_type=jnp.float32)
        keep_ref[:, at : at + width] = total[:cut]
        send_ref[:, at : at + width] = total[cut:]

    if kv_width:
        kv_copy.wait()
        put(kvs_ref[...], 0, kv_width)
    for t in range(tiles):
        weight_copy(t).wait()
        put(ws_ref[t], kv_width + t * tile, tile)


def project(bits, rows, ids, own, other, query_weight, kv_weight, first, width):
    features = own.shape[1]
    order = order_of(bits)
    n = len(order)
    tile = tile_of(width, 512)
    kv_width = kv_weight.shape[1] // 2 if kv_weight is not None else 0
    columns = width + kv_width
    out = jax.ShapeDtypeStruct((n * rows // 2, columns), jnp.float32)
    scratch = [
        pltpu.VMEM((n * rows, features), own.dtype),
        pltpu.VMEM((width // tile, features, tile), own.dtype),
    ]
    sems = [pltpu.SemaphoreType.DMA((n,)), pltpu.SemaphoreType.DMA((width // tile,))]
    operands = [ids, own, other, query_weight]
    if kv_width:
        scratch.append(pltpu.VMEM((features, kv_width), own.dtype))
        sems.append(pltpu.SemaphoreType.DMA)
        operands.append(kv_weight)
    return pl.pallas_call(
        functools.partial(project_kernel, order, rows, first, tile, kv_width),
        out_shape=(out, out),
        in_specs=[SMEM] + [ANY] * (len(operands) - 1),
        out_specs=(VMEM, VMEM),
        scratch_shapes=scratch + sems,
        compiler_params=pltpu.CompilerParams(vmem_limit_bytes=16 * MIB),
        cost_estimate=pl.CostEstimate(
            flops=2 * n * rows * features * columns,
            bytes_accessed=2 * features * columns + 4 * n * rows * columns,
            transcendentals=0,
        ),
        name="project",
    )(*operands)


def attend_kernel(parts, scalars_ref, *refs):
    own_q, other_q = refs[: len(parts)], refs[len(parts) : 2 * len(parts)]
    k_ref, v_ref, own_out, other_out, q_scr, o_scr = refs[2 * len(parts) :]
    core = scalars_ref[0]
    rows, positions, _ = k_ref.shape
    at = 0
    for side in (own_q, other_q):
        for ref, (heads, skip) in zip(side, parts):
            for head in range(heads):
                column = skip + head * DH
                q_scr[:, at, :] = ref[:, column : column + DH].astype(jnp.float32)
                at += 1
    total_heads = at
    first = own_q[0][:, :DH].astype(jnp.float32)
    second = other_q[0][:, :DH].astype(jnp.float32)
    new_keys = jnp.where(core == 0, first, second)
    new_values = jnp.where(core == 0, second, first)
    scale = DH**-0.5
    for row in range(rows):
        query = q_scr[row]
        scores = scale * lax.dot_general(
            query.astype(jnp.bfloat16),
            k_ref[row],
            (((1,), (1,)), ((), ())),
            preferred_element_type=jnp.float32,
        )
        self_score = scale * jnp.sum(query * new_keys[row : row + 1], axis=1, keepdims=True)
        visible = lax.broadcasted_iota(jnp.int32, scores.shape, 1) < scalars_ref[1 + row]
        masked = jnp.where(visible, scores, jnp.float32(-1e30))
        peak = jnp.maximum(jnp.max(masked, axis=1, keepdims=True), self_score)
        raised = jnp.where(visible, jnp.exp(masked - peak), jnp.float32(0.0))
        self_raised = jnp.exp(self_score - peak)
        denominator = jnp.sum(raised, axis=1, keepdims=True) + self_raised
        weights = (raised / denominator).astype(jnp.bfloat16)
        self_weight = (self_raised / denominator).astype(jnp.bfloat16).astype(jnp.float32)
        total = jnp.dot(weights, v_ref[row], preferred_element_type=jnp.float32)
        o_scr[row] = total + self_weight * new_values[row : row + 1]
    half = total_heads // 2
    for head in range(total_heads):
        ref = own_out if head < half else other_out
        column = (head % half) * DH
        ref[:, column : column + DH] = o_scr[:, head, :].astype(jnp.bfloat16)


def attend(core, lengths, own_q, other_q, parts, keys, values):
    rows, positions, _ = keys.shape
    heads = 2 * sum(part[0] for part in parts)
    out = jax.ShapeDtypeStruct((rows, heads * DH // 2), jnp.bfloat16)
    scalars = jnp.concatenate([core[None], lengths])
    return pl.pallas_call(
        functools.partial(attend_kernel, parts),
        out_shape=(out, out),
        in_specs=[SMEM] + [VMEM] * (2 * len(parts) + 2),
        out_specs=(VMEM, VMEM),
        scratch_shapes=[pltpu.VMEM((rows, heads, DH), jnp.float32)] * 2,
        compiler_params=pltpu.CompilerParams(vmem_limit_bytes=16 * MIB),
        cost_estimate=pl.CostEstimate(
            flops=4 * rows * heads * positions * DH,
            bytes_accessed=4 * rows * positions * DH,
            transcendentals=rows * heads * positions,
        ),
        name="attend",
    )(scalars, *own_q, *other_q, keys, values)


def output_kernel(order, rows, first, tile, with_prior, ids_ref, near_ref, far_ref, w_ref, *refs):
    if with_prior:
        send_in, keep_in, send_ref, keep_ref, xs_ref = refs
    else:
        send_ref, keep_ref, xs_ref = refs
    me, core = ids_ref[0], ids_ref[1]
    n = len(order)
    half = n // 2
    for p, j in enumerate(order):
        block = jnp.bitwise_xor(me, j)
        place = block % half + jnp.where(block // half == core, half, 0)
        source = near_ref if p < half else far_ref
        at = (p % half) * rows
        xs_ref[pl.ds(pl.multiple_of(place * rows, rows), rows), :] = source[at : at + rows, :]
    depth = xs_ref.shape[1]
    cut = half * rows
    for column in range(0, w_ref.shape[1], tile):
        span = slice(column, column + tile)
        total = jnp.dot(
            xs_ref[...], w_ref[first : first + depth, span], preferred_element_type=jnp.float32
        )
        if with_prior:
            send_ref[:, span] = send_in[:, span] + total[:cut]
            keep_ref[:, span] = keep_in[:, span] + total[cut:]
        else:
            send_ref[:, span] = total[:cut]
            keep_ref[:, span] = total[cut:]


def project_out(order, rows, ids, near, far, out_weight, first, prior):
    depth = near.shape[1]
    columns = out_weight.shape[1]
    n = len(order)
    tile = tile_of(columns, 768)
    out = jax.ShapeDtypeStruct((n * rows // 2, columns), jnp.float32)
    operands = [ids, near, far, out_weight] + ([] if prior is None else list(prior))
    return pl.pallas_call(
        functools.partial(output_kernel, order, rows, first, tile, prior is not None),
        out_shape=(out, out),
        in_specs=[SMEM] + [VMEM] * (len(operands) - 1),
        out_specs=(VMEM, VMEM),
        scratch_shapes=[pltpu.VMEM((n * rows, depth), jnp.bfloat16)],
        compiler_params=pltpu.CompilerParams(vmem_limit_bytes=16 * MIB),
        cost_estimate=pl.CostEstimate(
            flops=2 * n * rows * depth * columns,
            bytes_accessed=2 * depth * columns + 4 * n * rows * columns,
            transcendentals=0,
        ),
        name="project_out",
    )(*operands)


def local(tokens, query_weight, kv_weight, out_weight, key_cache, value_cache, lengths):
    n = lax.axis_size("gx")
    me = lax.axis_index("gx").astype(jnp.int32)
    core = lax.axis_index("gy").astype(jnp.int32)
    ids = jnp.stack([me, core])
    own_rows = key_cache.shape[0]
    rows = 2 * own_rows
    bits = [1 << i for i in range(n.bit_length() - 1)]

    def swap(array):
        return lax.ppermute(array, "gy", [(0, 1), (1, 0)])

    def across(array, mask):
        return lax.ppermute(array, "gx", [(g, g ^ mask) for g in range(n)])

    other_tokens = swap(tokens)
    width = query_weight.shape[1] // 2
    heads = width // DH

    orders = [bits, bits[1:] + bits[:1]]
    state = [
        project(orders[0], rows, ids, tokens, other_tokens, query_weight, kv_weight, 0, width),
        project(orders[1], rows, ids, tokens, other_tokens, query_weight, None, width, width),
    ]
    moving = [across(state[i][0], orders[i][0]) for i in range(2)]
    for step in range(len(bits)):
        for i in range(2):
            total = state[i][1] + moving[i]
            if step + 1 < len(bits):
                cut = total.shape[0] // 2
                state[i] = (total[cut:], total[:cut])
                moving[i] = across(state[i][0], orders[i][step + 1])
            else:
                state[i] = total
    mine, theirs = [], []
    for total in state:
        mine.append(lax.dynamic_slice_in_dim(total, core * own_rows, own_rows, 0).astype(jnp.bfloat16))
        give = lax.dynamic_slice_in_dim(total, (1 - core) * own_rows, own_rows, 0).astype(jnp.bfloat16)
        theirs.append(swap(give))

    own, other = attend(
        core, lengths, mine, theirs, ((heads, kv_weight.shape[1] // 2), (heads, 0)), key_cache, value_cache
    )
    got = swap(other)
    block = jnp.where(core == 0, jnp.concatenate([own, got]), jnp.concatenate([got, own]))

    near = [block[:, :width], block[:, width:]]
    far = [None, None]
    paths = [bits[::-1], bits[:1] + bits[:0:-1]]
    for step in range(len(bits)):
        for i in range(2):
            if step:
                near[i] = jnp.concatenate([near[i], far[i]])
            far[i] = across(near[i], paths[i][step])
    prior = None
    for i in range(2):
        prior = project_out(order_of(paths[i][::-1]), rows, ids, near[i], far[i], out_weight, i * width, prior)
    send, keep = prior
    return (keep + swap(send)).astype(jnp.bfloat16)


def solution(mesh):
    return jax.shard_map(
        local,
        mesh=mesh,
        in_specs=(
            P(("grp", "gy"), "gx"),
            P("gx", "gy"),
            P("gx", None),
            P("gy", "gx"),
            P(("grp", "gx", "gy"), None, None),
            P(("grp", "gx", "gy"), None, None),
            P(("grp", "gx", "gy")),
        ),
        out_specs=P(("grp", "gy"), "gx"),
        check_vma=False,
    )
```

time: 176 us -> 91.2 us (0.52)
  blocking collectives: 122 us -> 0 us
  waiting for transfers between devices: 8.84 us -> 39.3 us
  matrix products: 24 us -> 0 us
  Pallas kernels: 0 us -> 16.3 us
  local copies, waits for them, and re-layouts: 1.6 us -> 16.6 us
  starting transfers between devices: 3.38 us -> 17.3 us
  between operations: 13.5 us -> 0.23 us
    psum x1 -> x0, blocking collectives: 83.8 us -> none  [local(): summed = lax.psum(partial_value, 'gx')]
    ppermute x0 -> x17, waiting for transfers between devices: none -> 39.3 us  [the longest x12 33.8 us: across(): return lax.ppermute(array, 'gx', [(g, g ^ mask) for g in range(n)])]
    all_gather x2 -> x0, blocking collectives: 34.8 us -> none  [the longest x1 32.2 us: local(): lax.all_gather(traded, 'gx', axis=0, tiled=True)]
    dot_general x6 -> x0, matrix products: 24 us -> none  [the longest x1 8.18 us: local(): jnp.dot(all_tokens, query_weight, preferred_element_type=jnp.float32)]
    ppermute x0 -> x17, starting transfers between devices: none -> 17.3 us  [the longest x12 16.4 us: across(): return lax.ppermute(array, 'gx', [(g, g ^ mask) for g in range(n)])]
    unnamed x4 -> x16, local copies, waits for them, and re-layouts: 0.01 us -> 16.6 us
    pallas_call x0 -> x5, Pallas kernels: none -> 16.3 us  [the longest x2 8.28 us: project(): pl.pallas_call(functools.partial(project_kernel, order, rows, first, tile...]
    reduce_scatter x2 -> x0, waiting for transfers between devices: 7.43 us -> none  [the longest x1 7.43 us: local(): lax.psum_scatter(partial_out, 'gy', scatter_dimension=0, tiled=True)]
  transfers between devices with their start and end apart: 3 -> 17, of which waited for: 2 -> 13; matrix products, arithmetic and copies ran while one was open for 7% -> 0% of each run, Pallas kernels for 0% -> 7%
where the time goes in v2:
time: 91.2 us; the launch traced here: 90.9 us
  waiting for transfers between devices  39.3 us (43%)
  starting transfers between devices  17.3 us (19%)
  local copies, waits for them, and re-layouts  16.6 us (18%)
  Pallas kernels  16.3 us (18%)
  other arithmetic  1.15 us (1%)
    ppermute x12, waiting for transfers between devices, across(): return lax.ppermute(array, 'gx', [(g, g ^ mask) for g in range(n)])  33.8 us
    unnamed x16, local copies, waits for them, and re-layouts  16.6 us
    ppermute x12, starting transfers between devices, across(): return lax.ppermute(array, 'gx', [(g, g ^ mask) for g in range(n)])  16.4 us
    pallas_call x2, Pallas kernels, project(): pl.pallas_call(functools.partial(project_kernel, order, rows, first, tile...  8.28 us
    ppermute x5, waiting for transfers between devices, swap(): return lax.ppermute(array, 'gy', [(0, 1), (1, 0)])  5.5 us
    pallas_call x1, Pallas kernels, attend(): pl.pallas_call(functools.partial(attend_kernel, parts), out_shape=(out, o...  4.65 us
    pallas_call x2, Pallas kernels, project_out(): pl.pallas_call(functools.partial(output_kernel, order, rows, first, tile,...  3.34 us
  transfers between devices with their start and end apart: 17, of which 13 were waited for; matrix products, arithmetic and copies ran while one was open for 0% of the time, Pallas kernels for 7%

profile of v2, /device:TPU:0, one launch (start us, length us, event | category | flops | bytes accessed | tf_op | source)
XLA Modules:
  0.0 90.9 jit_solution(2950232719234957080)
XLA Ops:
  0.0 0.5 collective-permute-start
  0.5 1.3 %collective-permute-done.other_ref = bf16[64,2304]{1,0:T(8,128)(2,1)S(1)} collective-permute-done((bf16[64,2304]{1,0:T(8,128)(2,1)}, bf16[64,2304]{1,0:T(8,128)(2,1)S(1)}, u32[]{:S(2)}, u32[]{:S(2)}) %collective-permute-start) | collective-permute-done | bytes 294944 | tf_op jit(solution)/shard_map/ppermute | solution.py:252
  1.9 5.0 %copy-done = bf16[2304,3072]{1,0:T(8,128)(2,1)S(1)} copy-done((bf16[2304,3072]{1,0:T(8,128)(2,1)S(1)}, bf16[2304,3072]{1,0:T(8,128)(2,1)}, u32[]{:S(2)}) %copy-start) | copy-done | bytes 14155800
  6.9 1.0 %copy-done.6 = bf16[64,2304]{1,0:T(8,128)(2,1)S(1)} copy-done((bf16[64,2304]{1,0:T(8,128)(2,1)S(1)}, bf16[64,2304]{1,0:T(8,128)(2,1)}, u32[]{:S(2)}) %copy-start.6) | copy-done | bytes 294936
  7.9 3.9 %project.3 = (f32[64,1536]{1,0:T(8,128)S(1)}, f32[64,1536]{1,0:T(8,128)S(1)}) custom-call(s32[2]{0:T(128)S(1)} %pad_add_fusion.ids_ref, bf16[64,2304]{1,0:T(8,128)(2,1)S(1)} %copy-done.6, bf16[64,2304]{1,0:T(8,128)(2,1)S(1)} %collective-permute-done.other_ref, bf16[2304,3072]{1,0:T(8,128)(2,1)S(1)} %copy-done), custom_call_target="tpu_custom_call" | custom-call | flops 905969664 | bytes 7864320 | tf_op jit(solution)/shard_map/project/pallas_call | solution.py:109
  11.8 3.0 %collective-permute-start.4 = (f32[64,1536]{1,0:T(8,128)S(1)}, f32[64,1536]{1,0:T(8,128)S(1)}, u32[]{:S(2)}, u32[]{:S(2)}) collective-permute-start(f32[64,1536]{1,0:T(8,128)S(1)} %get-tuple-element.18), channel_id=1, source_target_pairs={{0,4},{2,6},{4,0},{6,2},{8,12},{10,14},{12,8},{14,10},{1,5},{3,7},... | collective-permute-start | bytes 1179656 | tf_op jit(solution)/shard_map/ppermute | solution.py:255
  14.8 4.4 %project.2 = (f32[64,1792]{1,0:T(8,128)S(1)}, f32[64,1792]{1,0:T(8,128)S(1)}) custom-call(s32[2]{0:T(128)S(1)} %pad_add_fusion.ids_ref, bf16[64,2304]{1,0:T(8,128)(2,1)S(1)} %copy-done.6, bf16[64,2304]{1,0:T(8,128)(2,1)S(1)} %collective-permute-done.other_ref, bf16[2304,3072]{1,0:T(8,128)(2,1)S(1)} %copy-done, bf16[2304,512]{1,0:T(8,128)(2,1)S(1)} %copy-done.5), custom_call_target="tpu_custom_call" | custom-call | flops 1056964608 | bytes 9175040 | tf_op jit(solution)/shard_map/project/pallas_call | solution.py:109
  19.2 1.6 %collective-permute-start.1 = (f32[64,1792]{1,0:T(8,128)S(1)}, f32[64,1792]{1,0:T(8,128)S(1)}, u32[]{:S(2)}, u32[]{:S(2)}) collective-permute-start(f32[64,1792]{1,0:T(8,128)S(1)} %get-tuple-element.16), channel_id=1, source_target_pairs={{0,2},{2,0},{4,6},{6,4},{8,10},{10,8},{12,14},{14,12},{1,3},{3,1},... | collective-permute-start | bytes 1376264 | tf_op jit(solution)/shard_map/ppermute | solution.py:255
  20.8 3.4 %collective-permute-done.4 = f32[64,1536]{1,0:T(8,128)S(1)} collective-permute-done((f32[64,1536]{1,0:T(8,128)S(1)}, f32[64,1536]{1,0:T(8,128)S(1)}, u32[]{:S(2)}, u32[]{:S(2)}) %collective-permute-start.4) | collective-permute-done | bytes 393248 | tf_op jit(solution)/shard_map/ppermute | solution.py:255
  24.3 2.8 %collective-permute-start.5 = (f32[32,1536]{1,0:T(8,128)S(1)}, f32[32,1536]{1,0:T(8,128)S(1)}, u32[]{:S(2)}, u32[]{:S(2)}) collective-permute-start(f32[32,1536]{1,0:T(8,128)S(1)} %slice.45), channel_id=1, source_target_pairs={{0,8},{2,10},{4,12},{6,14},{8,0},{10,2},{12,4},{14,6},{1,9},{3,11}... | collective-permute-start | bytes 589832 | tf_op jit(solution)/shard_map/ppermute | solution.py:255
  27.1 4.4 %collective-permute-done.1 = f32[64,1792]{1,0:T(8,128)S(1)} collective-permute-done((f32[64,1792]{1,0:T(8,128)S(1)}, f32[64,1792]{1,0:T(8,128)S(1)}, u32[]{:S(2)}, u32[]{:S(2)}) %collective-permute-start.1) | collective-permute-done | bytes 458784 | tf_op jit(solution)/shard_map/ppermute | solution.py:255
  32.0 4.0 %collective-permute-done.5 = f32[32,1536]{1,0:T(8,128)S(1)} collective-permute-done((f32[32,1536]{1,0:T(8,128)S(1)}, f32[32,1536]{1,0:T(8,128)S(1)}, u32[]{:S(2)}, u32[]{:S(2)}) %collective-permute-start.5) | collective-permute-done | bytes 196640 | tf_op jit(solution)/shard_map/ppermute | solution.py:255
  36.0 1.4 %collective-permute-start.6 = (f32[16,1536]{1,0:T(8,128)S(1)}, f32[16,1536]{1,0:T(8,128)S(1)}, u32[]{:S(2)}, u32[]{:S(2)}) collective-permute-start(f32[16,1536]{1,0:T(8,128)S(1)} %slice.47), channel_id=1, source_target_pairs={{0,2},{2,0},{4,6},{6,4},{8,10},{10,8},{12,14},{14,12},{1,3},{3,1},... | collective-permute-start | bytes 294920 | tf_op jit(solution)/shard_map/ppermute | solution.py:255
  37.5 3.3 %collective-permute-done.2 = f32[32,1792]{1,0:T(8,128)S(1)} collective-permute-done((f32[32,1792]{1,0:T(8,128)S(1)}, f32[32,1792]{1,0:T(8,128)S(1)}, u32[]{:S(2)}, u32[]{:S(2)}) %collective-permute-start.2) | collective-permute-done | bytes 229408 | tf_op jit(solution)/shard_map/ppermute | solution.py:255
  40.8 1.4 %collective-permute-start.3 = (f32[16,1792]{1,0:T(8,128)S(1)}, f32[16,1792]{1,0:T(8,128)S(1)}, u32[]{:S(2)}, u32[]{:S(2)}) collective-permute-start(f32[16,1792]{1,0:T(8,128)S(1)} %slice.43), channel_id=1, source_target_pairs={{0,8},{2,10},{4,12},{6,14},{8,0},{10,2},{12,4},{14,6},{1,9},{3,11}... | collective-permute-start | bytes 344072 | tf_op jit(solution)/shard_map/ppermute | solution.py:255
  42.4 6.9 %collective-permute-done.3 = f32[16,1792]{1,0:T(8,128)S(1)} collective-permute-done((f32[16,1792]{1,0:T(8,128)S(1)}, f32[16,1792]{1,0:T(8,128)S(1)}, u32[]{:S(2)}, u32[]{:S(2)}) %collective-permute-start.3) | collective-permute-done | bytes 114720 | tf_op jit(solution)/shard_map/ppermute | solution.py:255
  49.5 1.1 %collective-permute-done.7.refs_2_ = bf16[8,1792]{1,0:T(8,128)(2,1)S(1)} collective-permute-done((bf16[8,1792]{1,0:T(8,128)(2,1)S(1)}, bf16[8,1792]{1,0:T(8,128)(2,1)S(1)}, u32[]{:S(2)}, u32[]{:S(2)}) %collective-permute-start.7) | collective-permute-done | bytes 28704 | tf_op jit(solution)/shard_map/ppermute | solution.py:252
  50.7 2.2 %copy-done.4 = bf16[8,1024,256]{2,1,0:T(8,128)(2,1)S(1)} copy-done((bf16[8,1024,256]{2,1,0:T(8,128)(2,1)S(1)}, bf16[8,1024,256]{2,1,0:T(8,128)(2,1)}, u32[]{:S(2)}) %copy-start.4) | copy-done | bytes 4194328
  52.8 4.6 %attend.1 = (bf16[8,3072]{1,0:T(8,128)(2,1)S(1)}, bf16[8,3072]{1,0:T(8,128)(2,1)S(1)}) custom-call(s32[9]{0:T(128)S(1)} %pad_add_fusion.1.scalars_ref, bf16[8,1792]{1,0:T(8,128)(2,1)S(1)} %get-tuple-element.28.refs_0_, bf16[8,1536]{1,0:T(8,128)(2,1)S(1)} %get-tuple-element.30.refs_1_, bf16[8,1792]{1,0:T(8,128)(2,1)S(1)} %collective-permute-done.7.refs_2_, ...), custom_call_target="tpu_custom_call" | custom-call | flops 201326592 | bytes 8388608 | tf_op jit(solution)/shard_map/attend/pallas_call | solution.py:174
  57.7 1.1 %collective-permute-done.9 = bf16[8,3072]{1,0:T(8,128)(2,1)S(1)} collective-permute-done((bf16[8,3072]{1,0:T(8,128)(2,1)S(1)}, bf16[8,3072]{1,0:T(8,128)(2,1)S(1)}, u32[]{:S(2)}, u32[]{:S(2)}) %collective-permute-start.9) | collective-permute-done | bytes 49184 | tf_op jit(solution)/shard_map/ppermute | solution.py:252
  58.9 1.4 %collective-permute-start.10 = (bf16[16,1536]{1,0:T(8,128)(2,1)S(1)}, bf16[16,1536]{1,0:T(8,128)(2,1)S(1)}, u32[]{:S(2)}, u32[]{:S(2)}) collective-permute-start(bf16[16,1536]{1,0:T(8,128)(2,1)S(1)} %get-tuple-element.26), channel_id=1, source_target_pairs={{0,2},{2,0},{4,6},{6,4},{8,10},{10,8},{12,14},{14,12},{1,3},{3,1},... | collective-permute-start | bytes 147464 | tf_op jit(solution)/shard_map/ppermute | solution.py:255
  60.3 4.0 %collective-permute-done.13 = bf16[16,1536]{1,0:T(8,128)(2,1)S(1)} collective-permute-done((bf16[16,1536]{1,0:T(8,128)(2,1)S(1)}, bf16[16,1536]{1,0:T(8,128)(2,1)S(1)}, u32[]{:S(2)}, u32[]{:S(2)}) %collective-permute-start.13) | collective-permute-done | bytes 49184 | tf_op jit(solution)/shard_map/ppermute | solution.py:255
  64.4 2.5 %collective-permute-start.11 = (bf16[32,1536]{1,0:T(8,128)(2,1)S(1)}, bf16[32,1536]{1,0:T(8,128)(2,1)S(1)}, u32[]{:S(2)}, u32[]{:S(2)}) collective-permute-start(bf16[32,1536]{1,0:T(8,128)(2,1)S(1)} %pad_maximum_fusion.2), channel_id=1, source_target_pairs={{0,8},{2,10},{4,12},{6,14},{8,0},{10,2},{12,4},{14,6},{1,9},{3,11}... | collective-permute-start | bytes 294920 | tf_op jit(solution)/shard_map/ppermute | solution.py:255
  66.9 3.4 %collective-permute-done.14 = bf16[32,1536]{1,0:T(8,128)(2,1)S(1)} collective-permute-done((bf16[32,1536]{1,0:T(8,128)(2,1)S(1)}, bf16[32,1536]{1,0:T(8,128)(2,1)S(1)}, u32[]{:S(2)}, u32[]{:S(2)}) %collective-permute-start.14) | collective-permute-done | bytes 98336 | tf_op jit(solution)/shard_map/ppermute | solution.py:255
  70.3 1.6 %collective-permute-start.15 = (bf16[64,1536]{1,0:T(8,128)(2,1)S(1)}, bf16[64,1536]{1,0:T(8,128)(2,1)S(1)}, u32[]{:S(2)}, u32[]{:S(2)}) collective-permute-start(bf16[64,1536]{1,0:T(8,128)(2,1)S(1)} %pad_maximum_fusion.1.near_ref), channel_id=1, source_target_pairs={{0,2},{2,0},{4,6},{6,4},{8,10},{10,8},{12,14},{14,12},{1,3},{3,1},... | collective-permute-start | bytes 589832 | tf_op jit(solution)/shard_map/ppermute | solution.py:255
  72.3 4.0 %collective-permute-done.15.far_ref = bf16[64,1536]{1,0:T(8,128)(2,1)S(1)} collective-permute-done((bf16[64,1536]{1,0:T(8,128)(2,1)S(1)}, bf16[64,1536]{1,0:T(8,128)(2,1)S(1)}, u32[]{:S(2)}, u32[]{:S(2)}) %collective-permute-start.15) | collective-permute-done | bytes 196640 | tf_op jit(solution)/shard_map/ppermute | solution.py:255
  76.3 5.0 %copy-done.1 = bf16[3072,2304]{1,0:T(8,128)(2,1)S(1)} copy-done((bf16[3072,2304]{1,0:T(8,128)(2,1)S(1)}, bf16[3072,2304]{1,0:T(8,128)(2,1)}, u32[]{:S(2)}) %copy-start.1) | copy-done | bytes 14155800
  81.4 1.7 %project_out.2 = (f32[64,2304]{1,0:T(8,128)S(1)}, f32[64,2304]{1,0:T(8,128)S(1)}) custom-call(s32[2]{0:T(128)S(1)} %pad_add_fusion.ids_ref, bf16[64,1536]{1,0:T(8,128)(2,1)S(1)} %pad_maximum_fusion.1.near_ref, bf16[64,1536]{1,0:T(8,128)(2,1)S(1)} %collective-permute-done.15.far_ref, bf16[3072,2304]{1,0:T(8,128)(2,1)S(1)} %copy-done.1), custom_call_target="tpu_custom_call" | custom-call | flops 905969664 | bytes 8257536 | tf_op jit(solution)/shard_map/project_out/pallas_call | solution.py:226
  83.0 3.3 %copy-done.2 = bf16[3072,2304]{1,0:T(8,128)(2,1)S(1)} copy-done((bf16[3072,2304]{1,0:T(8,128)(2,1)S(1)}, bf16[3072,2304]{1,0:T(8,128)(2,1)}, u32[]{:S(2)}) %copy-start.2) | copy-done | bytes 14155800
  86.4 1.7 %project_out.3 = (f32[64,2304]{1,0:T(8,128)S(1)}, f32[64,2304]{1,0:T(8,128)S(1)}) custom-call(s32[2]{0:T(128)S(1)} %pad_add_fusion.ids_ref, bf16[64,1536]{1,0:T(8,128)(2,1)S(1)} %pad_maximum_fusion.near_ref, bf16[64,1536]{1,0:T(8,128)(2,1)S(1)} %collective-permute-done.12.far_ref, bf16[3072,2304]{1,0:T(8,128)(2,1)S(1)} %copy-done.2, ...), custom_call_target="tpu_custom_call" | custom-call | flops 905969664 | bytes 8257536 | tf_op jit(solution)/shard_map/project_out/pallas_call | solution.py:226
  88.2 2.0 %collective-permute-done.16 = f32[64,2304]{1,0:T(8,128)S(1)} collective-permute-done((f32[64,2304]{1,0:T(8,128)S(1)}, f32[64,2304]{1,0:T(8,128)S(1)}, u32[]{:S(2)}, u32[]{:S(2)}) %collective-permute-start.16) | collective-permute-done | bytes 589856 | tf_op jit(solution)/shard_map/ppermute | solution.py:252
  90.1 0.8 add_convert_fusion
  (44 shorter events, 1.8 us)
Async XLA Ops:
  0.0 1.9 %collective-permute-start = (bf16[64,2304]{1,0:T(8,128)(2,1)}, bf16[64,2304]{1,0:T(8,128)(2,1)S(1)}, u32[]{:S(2)}, u32[]{:S(2)}) collective-permute-start(bf16[64,2304]{1,0:T(8,128)(2,1)} %own_ref.3), channel_id=1, source_target_pairs={{0,1},{1,0},{2,3},{3,2},{4,5},{5,4},{6,7},{7,6},{8,9},{9,8},{10,11... | collective-permute-start | bytes 884744 | tf_op jit(solution)/shard_map/ppermute | solution.py:252
  1.9 5.0 %copy-start = (bf16[2304,3072]{1,0:T(8,128)(2,1)S(1)}, bf16[2304,3072]{1,0:T(8,128)(2,1)}, u32[]{:S(2)}) copy-start(bf16[2304,3072]{1,0:T(8,128)(2,1)} %w_ref.5) | copy-start | bytes 42467332
  6.9 1.0 %copy-start.6 = (bf16[64,2304]{1,0:T(8,128)(2,1)S(1)}, bf16[64,2304]{1,0:T(8,128)(2,1)}, u32[]{:S(2)}) copy-start(bf16[64,2304]{1,0:T(8,128)(2,1)} %own_ref.3) | copy-start | bytes 884740
  7.9 6.9 %copy-start.5 = (bf16[2304,512]{1,0:T(8,128)(2,1)S(1)}, bf16[2304,512]{1,0:T(8,128)(2,1)}, u32[]{:S(2)}) copy-start(bf16[2304,512]{1,0:T(8,128)(2,1)} %refs_0_.1) | copy-start | bytes 7077892
  11.8 12.4 %collective-permute-start.4 = (f32[64,1536]{1,0:T(8,128)S(1)}, f32[64,1536]{1,0:T(8,128)S(1)}, u32[]{:S(2)}, u32[]{:S(2)}) collective-permute-start(f32[64,1536]{1,0:T(8,128)S(1)} %get-tuple-element.18), channel_id=1, source_target_pairs={{0,4},{2,6},{4,0},{6,2},{8,12},{10,14},{12,8},{14,10},{1,5},{3,7},... | collective-permute-start | bytes 1179656 | tf_op jit(solution)/shard_map/ppermute | solution.py:255
  19.2 30.3 %copy-start.7 = (s32[8]{0:T(128)S(1)}, s32[8]{0:T(128)}, u32[]{:S(2)}) copy-start(s32[8]{0:T(128)} %param.13) | copy-start | bytes 100
  19.2 12.4 %collective-permute-start.1 = (f32[64,1792]{1,0:T(8,128)S(1)}, f32[64,1792]{1,0:T(8,128)S(1)}, u32[]{:S(2)}, u32[]{:S(2)}) collective-permute-start(f32[64,1792]{1,0:T(8,128)S(1)} %get-tuple-element.16), channel_id=1, source_target_pairs={{0,2},{2,0},{4,6},{6,4},{8,10},{10,8},{12,14},{14,12},{1,3},{3,1},... | collective-permute-start | bytes 1376264 | tf_op jit(solution)/shard_map/ppermute | solution.py:255
  24.3 11.7 %collective-permute-start.5 = (f32[32,1536]{1,0:T(8,128)S(1)}, f32[32,1536]{1,0:T(8,128)S(1)}, u32[]{:S(2)}, u32[]{:S(2)}) collective-permute-start(f32[32,1536]{1,0:T(8,128)S(1)} %slice.45), channel_id=1, source_target_pairs={{0,8},{2,10},{4,12},{6,14},{8,0},{10,2},{12,4},{14,6},{1,9},{3,11}... | collective-permute-start | bytes 589832 | tf_op jit(solution)/shard_map/ppermute | solution.py:255
  27.1 23.6 %copy-start.3 = (bf16[8,1024,256]{2,1,0:T(8,128)(2,1)S(1)}, bf16[8,1024,256]{2,1,0:T(8,128)(2,1)}, u32[]{:S(2)}) copy-start(bf16[8,1024,256]{2,1,0:T(8,128)(2,1)} %refs_4_.1) | copy-start | bytes 12582916
  31.6 9.2 %collective-permute-start.2 = (f32[32,1792]{1,0:T(8,128)S(1)}, f32[32,1792]{1,0:T(8,128)S(1)}, u32[]{:S(2)}, u32[]{:S(2)}) collective-permute-start(f32[32,1792]{1,0:T(8,128)S(1)} %slice.41), channel_id=1, source_target_pairs={{0,4},{2,6},{4,0},{6,2},{8,12},{10,14},{12,8},{14,10},{1,5},{3,7},... | collective-permute-start | bytes 688136 | tf_op jit(solution)/shard_map/ppermute | solution.py:255
  36.0 6.3 %collective-permute-start.6 = (f32[16,1536]{1,0:T(8,128)S(1)}, f32[16,1536]{1,0:T(8,128)S(1)}, u32[]{:S(2)}, u32[]{:S(2)}) collective-permute-start(f32[16,1536]{1,0:T(8,128)S(1)} %slice.47), channel_id=1, source_target_pairs={{0,2},{2,0},{4,6},{6,4},{8,10},{10,8},{12,14},{14,12},{1,3},{3,1},... | collective-permute-start | bytes 294920 | tf_op jit(solution)/shard_map/ppermute | solution.py:255
  40.8 8.5 %collective-permute-start.3 = (f32[16,1792]{1,0:T(8,128)S(1)}, f32[16,1792]{1,0:T(8,128)S(1)}, u32[]{:S(2)}, u32[]{:S(2)}) collective-permute-start(f32[16,1792]{1,0:T(8,128)S(1)} %slice.43), channel_id=1, source_target_pairs={{0,8},{2,10},{4,12},{6,14},{8,0},{10,2},{12,4},{14,6},{1,9},{3,11}... | collective-permute-start | bytes 344072 | tf_op jit(solution)/shard_map/ppermute | solution.py:255
  42.3 7.2 %collective-permute-start.8 = (bf16[8,1536]{1,0:T(8,128)(2,1)S(1)}, bf16[8,1536]{1,0:T(8,128)(2,1)S(1)}, u32[]{:S(2)}, u32[]{:S(2)}) collective-permute-start(bf16[8,1536]{1,0:T(8,128)(2,1)S(1)} %get-tuple-element.29), channel_id=1, source_target_pairs={{0,1},{1,0},{2,3},{3,2},{4,5},{5,4},{6,7},{7,6},{8,9},{9,8},{10,11... | collective-permute-start | bytes 73736 | tf_op jit(solution)/shard_map/ppermute | solution.py:252
  49.4 1.3 %collective-permute-start.7 = (bf16[8,1792]{1,0:T(8,128)(2,1)S(1)}, bf16[8,1792]{1,0:T(8,128)(2,1)S(1)}, u32[]{:S(2)}, u32[]{:S(2)}) collective-permute-start(bf16[8,1792]{1,0:T(8,128)(2,1)S(1)} %get-tuple-element.27), channel_id=1, source_target_pairs={{0,1},{1,0},{2,3},{3,2},{4,5},{5,4},{6,7},{7,6},{8,9},{9,8},{10,11... | collective-permute-start | bytes 86024 | tf_op jit(solution)/shard_map/ppermute | solution.py:252
  50.6 2.2 %copy-start.4 = (bf16[8,1024,256]{2,1,0:T(8,128)(2,1)S(1)}, bf16[8,1024,256]{2,1,0:T(8,128)(2,1)}, u32[]{:S(2)}) copy-start(bf16[8,1024,256]{2,1,0:T(8,128)(2,1)} %refs_5_.1) | copy-start | bytes 12582916
  57.5 1.3 %collective-permute-start.9 = (bf16[8,3072]{1,0:T(8,128)(2,1)S(1)}, bf16[8,3072]{1,0:T(8,128)(2,1)S(1)}, u32[]{:S(2)}, u32[]{:S(2)}) collective-permute-start(bf16[8,3072]{1,0:T(8,128)(2,1)S(1)} %get-tuple-element.20), channel_id=1, source_target_pairs={{0,1},{1,0},{2,3},{3,2},{4,5},{5,4},{6,7},{7,6},{8,9},{9,8},{10,11... | collective-permute-start | bytes 147464 | tf_op jit(solution)/shard_map/ppermute | solution.py:252
  58.8 5.5 %collective-permute-start.13 = (bf16[16,1536]{1,0:T(8,128)(2,1)S(1)}, bf16[16,1536]{1,0:T(8,128)(2,1)S(1)}, u32[]{:S(2)}, u32[]{:S(2)}) collective-permute-start(bf16[16,1536]{1,0:T(8,128)(2,1)S(1)} %get-tuple-element.25), channel_id=1, source_target_pairs={{0,8},{2,10},{4,12},{6,14},{8,0},{10,2},{12,4},{14,6},{1,9},{3,11}... | collective-permute-start | bytes 147464 | tf_op jit(solution)/shard_map/ppermute | solution.py:255
  58.9 5.5 %collective-permute-start.10 = (bf16[16,1536]{1,0:T(8,128)(2,1)S(1)}, bf16[16,1536]{1,0:T(8,128)(2,1)S(1)}, u32[]{:S(2)}, u32[]{:S(2)}) collective-permute-start(bf16[16,1536]{1,0:T(8,128)(2,1)S(1)} %get-tuple-element.26), channel_id=1, source_target_pairs={{0,2},{2,0},{4,6},{6,4},{8,10},{10,8},{12,14},{14,12},{1,3},{3,1},... | collective-permute-start | bytes 147464 | tf_op jit(solution)/shard_map/ppermute | solution.py:255
  64.3 6.0 %collective-permute-start.14 = (bf16[32,1536]{1,0:T(8,128)(2,1)S(1)}, bf16[32,1536]{1,0:T(8,128)(2,1)S(1)}, u32[]{:S(2)}, u32[]{:S(2)}) collective-permute-start(bf16[32,1536]{1,0:T(8,128)(2,1)S(1)} %pad_maximum_fusion.3), channel_id=1, source_target_pairs={{0,4},{2,6},{4,0},{6,2},{8,12},{10,14},{12,8},{14,10},{1,5},{3,7},... | collective-permute-start | bytes 294920 | tf_op jit(solution)/shard_map/ppermute | solution.py:255
  64.4 7.8 %collective-permute-start.11 = (bf16[32,1536]{1,0:T(8,128)(2,1)S(1)}, bf16[32,1536]{1,0:T(8,128)(2,1)S(1)}, u32[]{:S(2)}, u32[]{:S(2)}) collective-permute-start(bf16[32,1536]{1,0:T(8,128)(2,1)S(1)} %pad_maximum_fusion.2), channel_id=1, source_target_pairs={{0,8},{2,10},{4,12},{6,14},{8,0},{10,2},{12,4},{14,6},{1,9},{3,11}... | collective-permute-start | bytes 294920 | tf_op jit(solution)/shard_map/ppermute | solution.py:255
  70.3 6.0 %collective-permute-start.15 = (bf16[64,1536]{1,0:T(8,128)(2,1)S(1)}, bf16[64,1536]{1,0:T(8,128)(2,1)S(1)}, u32[]{:S(2)}, u32[]{:S(2)}) collective-permute-start(bf16[64,1536]{1,0:T(8,128)(2,1)S(1)} %pad_maximum_fusion.1.near_ref), channel_id=1, source_target_pairs={{0,2},{2,0},{4,6},{6,4},{8,10},{10,8},{12,14},{14,12},{1,3},{3,1},... | collective-permute-start | bytes 589832 | tf_op jit(solution)/shard_map/ppermute | solution.py:255
  72.3 10.8 %collective-permute-start.12 = (bf16[64,1536]{1,0:T(8,128)(2,1)S(1)}, bf16[64,1536]{1,0:T(8,128)(2,1)S(1)}, u32[]{:S(2)}, u32[]{:S(2)}) collective-permute-start(bf16[64,1536]{1,0:T(8,128)(2,1)S(1)} %pad_maximum_fusion.near_ref), channel_id=1, source_target_pairs={{0,4},{2,6},{4,0},{6,2},{8,12},{10,14},{12,8},{14,10},{1,5},{3,7},... | collective-permute-start | bytes 589832 | tf_op jit(solution)/shard_map/ppermute | solution.py:255
  76.3 5.0 %copy-start.1 = (bf16[3072,2304]{1,0:T(8,128)(2,1)S(1)}, bf16[3072,2304]{1,0:T(8,128)(2,1)}, u32[]{:S(2)}) copy-start(bf16[3072,2304]{1,0:T(8,128)(2,1)} %w_ref.7) | copy-start | bytes 42467332
  81.4 5.0 %copy-start.2 = (bf16[3072,2304]{1,0:T(8,128)(2,1)S(1)}, bf16[3072,2304]{1,0:T(8,128)(2,1)}, u32[]{:S(2)}) copy-start(bf16[3072,2304]{1,0:T(8,128)(2,1)} %w_ref.7) | copy-start | bytes 42467332
  88.1 2.1 %collective-permute-start.16 = (f32[64,2304]{1,0:T(8,128)S(1)}, f32[64,2304]{1,0:T(8,128)S(1)}, u32[]{:S(2)}, u32[]{:S(2)}) collective-permute-start(f32[64,2304]{1,0:T(8,128)S(1)} %get-tuple-element.24), channel_id=1, source_target_pairs={{0,1},{1,0},{2,3},{3,2},{4,5},{5,4},{6,7},{7,6},{8,9},{9,8},{10,11... | collective-permute-start | bytes 1769480 | tf_op jit(solution)/shard_map/ppermute | solution.py:252

commit v3 on v2

v3 whole, which is shorter than its diff:
```python
import functools

import jax
import jax.numpy as jnp
from jax import lax
from jax.experimental import pallas as pl
from jax.experimental.pallas import tpu as pltpu
from jax.sharding import PartitionSpec as P

H = 24
DH = 256
MIB = 1024 * 1024
TURNS = (0, 1, 2, 3, 2, 1, 0, 3, 2, 1, 0, 3)
VMEM = pl.BlockSpec(memory_space=pltpu.VMEM)
ANY = pl.BlockSpec(memory_space=pl.ANY)
HBM = pl.BlockSpec(memory_space=pltpu.HBM)
SMEM = pl.BlockSpec(memory_space=pltpu.SMEM)


def tile_of(width, wanted):
    while wanted >= 128:
        if width % wanted == 0:
            return wanted
        wanted -= 128
    return width


def order_of(bits):
    order = [0]
    for bit in reversed(bits):
        order = order + [j + bit for j in order]
    return order


def slabs_of(depth):
    return depth // 768 if depth % 768 == 0 else 1


def load_kernel(sources, pieces, *refs):
    count = len(sources)
    ids_ref, in_refs, out_refs, sems = refs[0], refs[1 : 1 + count], refs[-1 - count : -1], refs[-1]
    copies = []
    for at, (source, in_ref, out_ref) in enumerate(zip(sources, in_refs, out_refs)):
        step = out_ref.shape[0] // pieces
        for piece in range(pieces):
            span = pl.ds(piece * step, step)
            if source is None:
                view = in_ref.at[span]
            elif isinstance(source, tuple):
                view = in_ref.at[span, pl.ds(source[0], source[1])]
            else:
                view = in_ref.at[span, pl.ds(pl.multiple_of(ids_ref[1] * source, source), source)]
            copies.append(pltpu.make_async_copy(view, out_ref.at[span], sems.at[at, piece]))
    for copy in copies:
        copy.start()
    for copy in copies:
        copy.wait()


def load(ids, arrays, sources, pieces):
    shapes, total = [], 0
    for array, source in zip(arrays, sources):
        shape = array.shape
        if source is not None:
            shape = (shape[0], source[1] if isinstance(source, tuple) else source)
        shapes.append(jax.ShapeDtypeStruct(shape, array.dtype))
        total += 2 * array.size if source is None else 2 * shape[0] * shape[1]
    return pl.pallas_call(
        functools.partial(load_kernel, sources, pieces),
        out_shape=shapes,
        in_specs=[SMEM] + [HBM] * len(arrays),
        out_specs=[VMEM] * len(arrays),
        scratch_shapes=[pltpu.SemaphoreType.DMA((len(arrays), pieces))],
        compiler_params=pltpu.CompilerParams(vmem_limit_bytes=46 * MIB),
        cost_estimate=pl.CostEstimate(flops=0, bytes_accessed=total, transcendentals=0),
        name="load",
    )(ids, *arrays)


def project_kernel(order, rows, first, held, after, ids_ref, own_ref, other_ref, *refs):
    refs = refs[:1 + held] + refs[1 + held + after :]
    if held:
        w_ref, kv_ref, send_ref, keep_ref, xs_ref, row_sem = refs
    else:
        w_ref, send_ref, keep_ref, xs_ref, ws_ref, row_sem, w_sem = refs
    n = len(order)
    half = n // 2
    me, core = ids_ref[0], ids_ref[1]
    depth = xs_ref.shape[1]
    slabs = slabs_of(depth)
    slab = depth // slabs

    def row_copy(source_ref, p):
        block = jnp.bitwise_xor(me, order[p])
        source = pl.ds(pl.multiple_of((block % half) * rows, rows), rows)
        return pltpu.make_async_copy(
            source_ref.at[source, :], xs_ref.at[pl.ds(p * rows, rows), :], row_sem.at[p]
        )

    def weight_copy(k):
        span = pl.ds(k * slab, slab)
        width = ws_ref.shape[1]
        return pltpu.make_async_copy(w_ref.at[span, pl.ds(first, width)], ws_ref.at[span], w_sem.at[k])

    for p in range(n):
        mine = jnp.bitwise_xor(me, order[p]) // half == core

        @pl.when(mine)
        def _():
            row_copy(own_ref, p).start()

        @pl.when(jnp.logical_not(mine))
        def _():
            row_copy(other_ref, p).start()

    if not held:
        for k in range(slabs):
            weight_copy(k).start()
    for p in range(n):
        row_copy(own_ref, p).wait()

    cut = half * rows

    def put(total, at):
        keep_ref[:, at : at + total.shape[1]] = total[:cut]
        send_ref[:, at : at + total.shape[1]] = total[cut:]

    if held:
        kv_width = kv_ref.shape[1]
        put(jnp.dot(xs_ref[...], kv_ref[...], preferred_element_type=jnp.float32), 0)
        put(jnp.dot(xs_ref[...], w_ref[...], preferred_element_type=jnp.float32), kv_width)
    else:
        total = None
        for k in range(slabs):
            weight_copy(k).wait()
            span = slice(k * slab, (k + 1) * slab)
            part = jnp.dot(xs_ref[:, span], ws_ref[span, :], preferred_element_type=jnp.float32)
            total = part if total is None else total + part
        put(total, 0)


def project(bits, rows, ids, own, other, weights, first, width, after):
    features = own.shape[1]
    order = order_of(bits)
    n = len(order)
    slabs = slabs_of(features)
    held = len(weights) > 1
    columns = sum(w.shape[1] for w in weights) if held else width
    out = jax.ShapeDtypeStruct((n * rows // 2, columns), jnp.float32)
    scratch = [pltpu.VMEM((n * rows, features), own.dtype)]
    sems = [pltpu.SemaphoreType.DMA((n,))]
    if not held:
        scratch.append(pltpu.VMEM((features, width), own.dtype))
        sems.append(pltpu.SemaphoreType.DMA((slabs,)))
    return pl.pallas_call(
        functools.partial(project_kernel, order, rows, first, held, len(after)),
        out_shape=(out, out),
        in_specs=[SMEM, VMEM, VMEM] + [VMEM if held else HBM] * len(weights) + [ANY] * len(after),
        out_specs=(VMEM, VMEM),
        scratch_shapes=scratch + sems,
        compiler_params=pltpu.CompilerParams(vmem_limit_bytes=48 * MIB),
        cost_estimate=pl.CostEstimate(
            flops=2 * n * rows * columns,
            bytes_accessed=4 * n * rows,
            transcendentals=0,
        ),
        name="project",
    )(ids, own, other, *weights, *after)


def combine_kernel(last, ids_ref, keep_ref, got_ref, after_ref, send_ref, left_ref):
    total = keep_ref[...] + got_ref[...]
    cut = total.shape[0] // 2
    if last:
        mine = ids_ref[1] == 0
        send_ref[...] = jnp.where(mine, total[cut:], total[:cut]).astype(jnp.bfloat16)
        left_ref[...] = jnp.where(mine, total[:cut], total[cut:]).astype(jnp.bfloat16)
    else:
        send_ref[...] = total[cut:]
        left_ref[...] = total[:cut]


def combine(ids, keep, got, last, after):
    rows, columns = keep.shape
    out = jax.ShapeDtypeStruct((rows // 2, columns), jnp.bfloat16 if last else jnp.float32)
    return pl.pallas_call(
        functools.partial(combine_kernel, last),
        out_shape=(out, out),
        in_specs=[SMEM, VMEM, VMEM, ANY],
        out_specs=(VMEM, VMEM),
        compiler_params=pltpu.CompilerParams(vmem_limit_bytes=4 * MIB),
        cost_estimate=pl.CostEstimate(
            flops=rows * columns, bytes_accessed=12 * rows * columns, transcendentals=0
        ),
        name="combine",
    )(ids, keep, got, after)


def attend_kernel(parts, scalars_ref, *refs):
    own_q, other_q = refs[: len(parts)], refs[len(parts) : 2 * len(parts)]
    k_hbm, v_hbm, own_out, other_out, k_ref, v_ref, q_scr, o_scr, sems = refs[2 * len(parts) :]
    core = scalars_ref[0]
    rows, positions, _ = k_ref.shape
    copies = []
    for row in range(rows):
        copies.append(pltpu.make_async_copy(k_hbm.at[row], k_ref.at[row], sems.at[0, row]))
        copies.append(pltpu.make_async_copy(v_hbm.at[row], v_ref.at[row], sems.at[1, row]))
    for copy in copies:
        copy.start()
    at = 0
    for side in (own_q, other_q):
        for ref, (heads, skip) in zip(side, parts):
            for head in range(heads):
                column = skip + head * DH
                q_scr[:, at, :] = ref[:, column : column + DH].astype(jnp.float32)
                at += 1
    total_heads = at
    first = own_q[0][:, :DH].astype(jnp.float32)
    second = other_q[0][:, :DH].astype(jnp.float32)
    new_keys = jnp.where(core == 0, first, second)
    new_values = jnp.where(core == 0, second, first)
    scale = DH**-0.5
    for row in range(rows):
        query = q_scr[row]
        copies[2 * row].wait()
        scores = scale * lax.dot_general(
            query.astype(jnp.bfloat16),
            k_ref[row],
            (((1,), (1,)), ((), ())),
            preferred_element_type=jnp.float32,
        )
        self_score = scale * jnp.sum(query * new_keys[row : row + 1], axis=1, keepdims=True)
        visible = lax.broadcasted_iota(jnp.int32, scores.shape, 1) < scalars_ref[1 + row]
        masked = jnp.where(visible, scores, jnp.float32(-1e30))
        peak = jnp.maximum(jnp.max(masked, axis=1, keepdims=True), self_score)
        raised = jnp.where(visible, jnp.exp(masked - peak), jnp.float32(0.0))
        self_raised = jnp.exp(self_score - peak)
        denominator = jnp.sum(raised, axis=1, keepdims=True) + self_raised
        weights = (raised / denominator).astype(jnp.bfloat16)
        self_weight = (self_raised / denominator).astype(jnp.bfloat16).astype(jnp.float32)
        copies[2 * row + 1].wait()
        total = jnp.dot(weights, v_ref[row], preferred_element_type=jnp.float32)
        o_scr[row] = total + self_weight * new_values[row : row + 1]
    half = total_heads // 2
    for head in range(total_heads):
        ref = own_out if head < half else other_out
        column = (head % half) * DH
        ref[:, column : column + DH] = o_scr[:, head, :].astype(jnp.bfloat16)


def attend(core, lengths, own_q, other_q, parts, keys, values):
    rows, positions, _ = keys.shape
    heads = 2 * sum(part[0] for part in parts)
    out = jax.ShapeDtypeStruct((rows, heads * DH // 2), jnp.bfloat16)
    scalars = jnp.concatenate([core[None], lengths])
    return pl.pallas_call(
        functools.partial(attend_kernel, parts),
        out_shape=(out, out),
        in_specs=[SMEM] + [VMEM] * (2 * len(parts)) + [HBM, HBM],
        out_specs=(VMEM, VMEM),
        scratch_shapes=[pltpu.VMEM(keys.shape, keys.dtype)] * 2
        + [pltpu.VMEM((rows, heads, DH), jnp.float32)] * 2
        + [pltpu.SemaphoreType.DMA((2, rows))],
        compiler_params=pltpu.CompilerParams(vmem_limit_bytes=55 * MIB),
        cost_estimate=pl.CostEstimate(
            flops=4 * rows * heads * positions * DH,
            bytes_accessed=4 * rows * positions * DH,
            transcendentals=rows * heads * positions,
        ),
        name="attend",
    )(scalars, *own_q, *other_q, keys, values)


def spans_of(columns):
    if columns % 768:
        return [(0, columns)]
    spans = [(at, 768) for at in range(0, columns - 768, 768)]
    return spans + [(columns - 768, 512), (columns - 256, 256)]


def output_kernel(order, rows, first, spans, with_prior, ids_ref, near_ref, far_ref, w_hbm, *refs):
    if with_prior:
        send_in, keep_in, send_ref, keep_ref, xs_ref, w_ref, sems, row_sems, prior_ref, prior_sems = refs
    else:
        send_ref, keep_ref, xs_ref, w_ref, sems, row_sems = refs
    depth = xs_ref.shape[1]
    me, core = ids_ref[0], ids_ref[1]
    n = len(order)
    half = n // 2
    row_copies = []
    for p, j in enumerate(order):
        block = jnp.bitwise_xor(me, j)
        place = block % half + jnp.where(block // half == core, half, 0)
        source = near_ref if p < half else far_ref
        row_copies.append(
            pltpu.make_async_copy(
                source.at[pl.ds((p % half) * rows, rows), :],
                xs_ref.at[pl.ds(pl.multiple_of(place * rows, rows), rows), :],
                row_sems.at[p],
            )
        )
    for copy in row_copies:
        copy.start()
    copies = []
    for at, (column, width) in enumerate(spans):
        span = pl.ds(column, width)
        copies.append(
            pltpu.make_async_copy(w_hbm.at[pl.ds(first, depth), span], w_ref.at[:, span], sems.at[at])
        )
    for copy in copies:
        copy.start()
    if with_prior:
        prior_copies = [
            pltpu.make_async_copy(ref, prior_ref.at[at], prior_sems.at[at])
            for at, ref in enumerate((send_in, keep_in))
        ]
        for copy in prior_copies:
            copy.start()
    for copy in row_copies:
        copy.wait()
    if with_prior:
        for copy in prior_copies:
            copy.wait()
    cut = half * rows
    for copy, (column, width) in zip(copies, spans):
        copy.wait()
        span = slice(column, column + width)
        total = jnp.dot(xs_ref[...], w_ref[:, span], preferred_element_type=jnp.float32)
        if with_prior:
            send_ref[:, span] = prior_ref[0, :, span] + total[:cut]
            keep_ref[:, span] = prior_ref[1, :, span] + total[cut:]
        else:
            send_ref[:, span] = total[:cut]
            keep_ref[:, span] = total[cut:]


def project_out(order, rows, ids, near, far, out_weight, first, prior):
    depth = near.shape[1]
    columns = out_weight.shape[1]
    n = len(order)
    spans = spans_of(columns)
    out = jax.ShapeDtypeStruct((n * rows // 2, columns), jnp.float32)
    operands = [ids, near, far, out_weight] + ([] if prior is None else list(prior))
    return pl.pallas_call(
        functools.partial(output_kernel, order, rows, first, spans, prior is not None),
        out_shape=(out, out),
        in_specs=[SMEM, ANY, ANY, HBM] + [ANY] * (len(operands) - 4),
        out_specs=(VMEM, VMEM),
        scratch_shapes=[
            pltpu.VMEM((n * rows, depth), jnp.bfloat16),
            pltpu.VMEM((depth, columns), jnp.bfloat16),
            pltpu.SemaphoreType.DMA((len(spans),)),
            pltpu.SemaphoreType.DMA((n,)),
        ]
        + (
            []
            if prior is None
            else [pltpu.VMEM((2, *out.shape), jnp.float32), pltpu.SemaphoreType.DMA((2,))]
        ),
        compiler_params=pltpu.CompilerParams(vmem_limit_bytes=52 * MIB),
        cost_estimate=pl.CostEstimate(
            flops=2 * n * rows * depth * columns,
            bytes_accessed=2 * depth * columns + 4 * n * rows * columns,
            transcendentals=0,
        ),
        name="project_out",
    )(*operands)


def local(tokens, query_weight, kv_weight, out_weight, key_cache, value_cache, lengths):
    n = lax.axis_size("gx")
    me = lax.axis_index("gx").astype(jnp.int32)
    core = lax.axis_index("gy").astype(jnp.int32)
    ids = jnp.stack([me, core])
    own_rows = key_cache.shape[0]
    rows = 2 * own_rows
    bits = [1 << i for i in range(n.bit_length() - 1)]

    def swap(array):
        return lax.ppermute(array, "gy", [(0, 1), (1, 0)])

    def across(array, mask):
        return lax.ppermute(array, "gx", [(g, g ^ mask) for g in range(n)])

    width = query_weight.shape[1] // 2
    kv_width = kv_weight.shape[1] // 2

    y, z = bits[:1], bits[1:]
    unit = query_weight.shape[1] // 12
    plan = [(4 * unit, z + y), (4 * unit, y + z), (2 * unit, z[:1] + y + z[1:]), (2 * unit, y + z)]
    *held, own_tokens = load(ids, [query_weight, kv_weight, tokens], [(0, plan[0][0]), kv_width, None], 4)
    other_tokens = swap(tokens)
    state, moving, first, after = [], [], 0, []
    for i, (columns, order) in enumerate(plan):
        weights = held if i == 0 else [query_weight]
        send, keep = project(order, rows, ids, own_tokens, other_tokens, weights, first, columns, after)
        after = [send]
        state.append((send, keep))
        moving.append(across(send, order[0]))
        first += columns
    mine, theirs = [None] * len(plan), [None] * len(plan)
    turns = [i for _ in bits for i in range(len(plan))]
    if len(bits) == 3:
        turns = TURNS
    steps = [0] * len(plan)
    after = after[0]
    for i in turns:
        steps[i] += 1
        last = steps[i] == len(bits)
        send, keep = combine(ids, state[i][1], moving[i], last, after)
        after = keep
        if last:
            mine[i], theirs[i] = keep, swap(send)
        else:
            state[i] = (send, keep)
            moving[i] = across(send, plan[i][1][steps[i]])

    parts = tuple((columns // DH, 0 if i else kv_width) for i, (columns, _) in enumerate(plan))
    own, other = attend(core, lengths, mine, theirs, parts, key_cache, value_cache)
    got = swap(other)
    block = jnp.where(core == 0, jnp.concatenate([own, got]), jnp.concatenate([got, own]))

    near = [block[:, :width], block[:, width:]]
    far = [None, None]
    paths = [bits[::-1], bits[:1] + bits[:0:-1]]
    for step in range(len(bits)):
        for i in range(2):
            if step:
                near[i] = jnp.concatenate([near[i], far[i]])
            far[i] = across(near[i], paths[i][step])
    prior = None
    for i in range(2):
        prior = project_out(order_of(paths[i][::-1]), rows, ids, near[i], far[i], out_weight, i * width, prior)
    send, keep = prior
    return (keep + swap(send)).astype(jnp.bfloat16)


def solution(mesh):
    return jax.shard_map(
        local,
        mesh=mesh,
        in_specs=(
            P(("grp", "gy"), "gx"),
            P("gx", "gy"),
            P("gx", None),
            P("gy", "gx"),
            P(("grp", "gx", "gy"), None, None),
            P(("grp", "gx", "gy"), None, None),
            P(("grp", "gx", "gy")),
        ),
        out_specs=P(("grp", "gy"), "gx"),
        check_vma=False,
    )
```

time: 91.2 us -> 101 us (1.11)
  Pallas kernels: 16.3 us -> 47.6 us
  waiting for transfers between devices: 39.3 us -> 18.6 us
  local copies, waits for them, and re-layouts: 16.6 us -> 5.48 us
  starting transfers between devices: 17.3 us -> 25.7 us
  other arithmetic: 1.15 us -> 2.45 us
    pallas_call x4 -> x19, Pallas kernels: 11.6 us -> 38.7 us  [the longest x4 15.5 us: project(): pl.pallas_call(functools.partial(project_kernel, order, rows, first, held...]
    ppermute x12 -> x18, waiting for transfers between devices: 33.8 us -> 15.4 us  [across(): return lax.ppermute(array, 'gx', [(g, g ^ mask) for g in range(n)])]
    unnamed x16 -> x26, local copies, waits for them, and re-layouts: 16.6 us -> 5.47 us
    ppermute x12 -> x18, starting transfers between devices: 16.4 us -> 23.6 us  [across(): return lax.ppermute(array, 'gx', [(g, g ^ mask) for g in range(n)])]
    pallas_call x1, Pallas kernels: 4.65 us -> 8.96 us  [attend(): pl.pallas_call(functools.partial(attend_kernel, parts), out_shape=(out, o...]
    ppermute x5 -> x7, waiting for transfers between devices: 5.5 us -> 3.25 us  [swap(): return lax.ppermute(array, 'gy', [(0, 1), (1, 0)])]
    ppermute x5 -> x7, starting transfers between devices: 0.89 us -> 2.07 us  [swap(): return lax.ppermute(array, 'gy', [(0, 1), (1, 0)])]
  transfers between devices with their start and end apart: 17 -> 25, of which waited for: 13 -> 10; matrix products, arithmetic and copies ran while one was open for 0% -> 1% of each run, Pallas kernels for 7% -> 28%
where the time goes in v3:
time: 101 us; the launch traced here: 100 us
  Pallas kernels  47.6 us (47%)
  starting transfers between devices  25.7 us (25%)
  waiting for transfers between devices  18.6 us (18%)
  local copies, waits for them, and re-layouts  5.48 us (5%)
  other arithmetic  2.45 us (2%)
    ppermute x18, starting transfers between devices, across(): return lax.ppermute(array, 'gx', [(g, g ^ mask) for g in range(n)])  23.6 us
    pallas_call x4, Pallas kernels, project(): pl.pallas_call(functools.partial(project_kernel, order, rows, first, held...  15.5 us
    ppermute x18, waiting for transfers between devices, across(): return lax.ppermute(array, 'gx', [(g, g ^ mask) for g in range(n)])  15.4 us
    pallas_call x2, Pallas kernels, project_out(): pl.pallas_call(functools.partial(output_kernel, order, rows, first, spans...  11.3 us
    pallas_call x1, Pallas kernels, attend(): pl.pallas_call(functools.partial(attend_kernel, parts), out_shape=(out, o...  8.96 us
    pallas_call x12, Pallas kernels, combine(): pl.pallas_call(functools.partial(combine_kernel, last), out_shape=(out, o...  6.67 us
    unnamed x26, local copies, waits for them, and re-layouts  5.47 us
    pallas_call x1, Pallas kernels, load(): pl.pallas_call(functools.partial(load_kernel, sources, pieces), out_shape...  5.2 us
  transfers between devices with their start and end apart: 25, of which 10 were waited for; matrix products, arithmetic and copies ran while one was open for 1% of the time, Pallas kernels for 28%

profile of v3, /device:TPU:0, one launch (start us, length us, event | category | flops | bytes accessed | tf_op | source)
XLA Modules:
  0.0 100.2 jit_solution(982737525757774630)
XLA Ops:
  0.5 1.7 %copy-done = bf16[2304,512]{1,0:T(8,128)(2,1)S(1)} copy-done((bf16[2304,512]{1,0:T(8,128)(2,1)S(1)}, bf16[2304,512]{1,0:T(8,128)(2,1)}, u32[]{:S(2)}) %copy-start) | copy-done | bytes 2359320
  2.2 1.0 copy-done.3
  3.2 5.2 %load.1 = (bf16[2304,1024]{1,0:T(8,128)(2,1)}, bf16[2304,256]{1,0:T(8,128)(2,1)S(1)}, bf16[64,2304]{1,0:T(8,128)(2,1)S(1)}) custom-call(s32[2]{0:T(128)S(1)} %pad_add_fusion.refs_0_.ids_ref, bf16[2304,3072]{1,0:T(8,128)(2,1)} %refs_0_.5, bf16[2304,512]{1,0:T(8,128)(2,1)S(1)} %copy-done, bf16[64,2304]{1,0:T(8,128)(2,1)S(1)} %copy-done.3), custom_call_target="tpu_custom_call" | custom-call | bytes 6193152 | tf_op jit(solution)/shard_map/load/pallas_call | solution.py:68
  8.4 4.3 %project.4 = (f32[64,1280]{1,0:T(8,128)S(1)}, f32[64,1280]{1,0:T(8,128)S(1)}) custom-call(s32[2]{0:T(128)S(1)} %pad_add_fusion.refs_0_.ids_ref, bf16[64,2304]{1,0:T(8,128)(2,1)S(1)} %get-tuple-element.46.own_ref, bf16[64,2304]{1,0:T(8,128)(2,1)S(1)} %collective-permute-done.other_ref, bf16[2304,1024]{1,0:T(8,128)(2,1)} %get-tuple-element.47.refs_0_, ...), custom_call_target="tpu_custom_call" | custom-call | flops 327680 | bytes 512 | tf_op jit(solution)/shard_map/project/pallas_call | solution.py:155
  12.7 2.6 %collective-permute-start.1 = (f32[64,1280]{1,0:T(8,128)S(1)}, f32[64,1280]{1,0:T(8,128)S(1)}, u32[]{:S(2)}, u32[]{:S(2)}) collective-permute-start(f32[64,1280]{1,0:T(8,128)S(1)} %get-tuple-element.50.refs_1_), channel_id=1, source_target_pairs={{0,4},{2,6},{4,0},{6,2},{8,12},{10,14},{12,8},{14,10},{1,5},{3,7},... | collective-permute-start | bytes 983048 | tf_op jit(solution)/shard_map/ppermute | solution.py:383
  15.3 4.3 %project.5 = (f32[64,1024]{1,0:T(8,128)S(1)}, f32[64,1024]{1,0:T(8,128)S(1)}) custom-call(s32[2]{0:T(128)S(1)} %pad_add_fusion.refs_0_.ids_ref, bf16[64,2304]{1,0:T(8,128)(2,1)S(1)} %get-tuple-element.46.own_ref, bf16[64,2304]{1,0:T(8,128)(2,1)S(1)} %collective-permute-done.other_ref, bf16[2304,3072]{1,0:T(8,128)(2,1)} %refs_0_.5, ...), custom_call_target="tpu_custom_call" | custom-call | flops 262144 | bytes 512 | tf_op jit(solution)/shard_map/project/pallas_call | solution.py:155
  19.6 1.6 %collective-permute-start.3 = (f32[64,1024]{1,0:T(8,128)S(1)}, f32[64,1024]{1,0:T(8,128)S(1)}, u32[]{:S(2)}, u32[]{:S(2)}) collective-permute-start(f32[64,1024]{1,0:T(8,128)S(1)} %get-tuple-element.51.refs_1_), channel_id=1, source_target_pairs={{0,2},{2,0},{4,6},{6,4},{8,10},{10,8},{12,14},{14,12},{1,3},{3,1},... | collective-permute-start | bytes 786440 | tf_op jit(solution)/shard_map/ppermute | solution.py:383
  21.2 3.4 %project.6 = (f32[64,512]{1,0:T(8,128)S(1)}, f32[64,512]{1,0:T(8,128)S(1)}) custom-call(s32[2]{0:T(128)S(1)} %pad_add_fusion.refs_0_.ids_ref, bf16[64,2304]{1,0:T(8,128)(2,1)S(1)} %get-tuple-element.46.own_ref, bf16[64,2304]{1,0:T(8,128)(2,1)S(1)} %collective-permute-done.other_ref, bf16[2304,3072]{1,0:T(8,128)(2,1)} %refs_0_.5, ...), custom_call_target="tpu_custom_call" | custom-call | flops 131072 | bytes 512 | tf_op jit(solution)/shard_map/project/pallas_call | solution.py:155
  25.2 3.5 %project.7 = (f32[64,512]{1,0:T(8,128)S(1)}, f32[64,512]{1,0:T(8,128)S(1)}) custom-call(s32[2]{0:T(128)S(1)} %pad_add_fusion.refs_0_.ids_ref, bf16[64,2304]{1,0:T(8,128)(2,1)S(1)} %get-tuple-element.46.own_ref, bf16[64,2304]{1,0:T(8,128)(2,1)S(1)} %collective-permute-done.other_ref, bf16[2304,3072]{1,0:T(8,128)(2,1)} %refs_0_.5, ...), custom_call_target="tpu_custom_call" | custom-call | flops 131072 | bytes 512 | tf_op jit(solution)/shard_map/project/pallas_call | solution.py:155
  29.2 2.7 %collective-permute-start.2 = (f32[32,1280]{1,0:T(8,128)S(1)}, f32[32,1280]{1,0:T(8,128)S(1)}, u32[]{:S(2)}, u32[]{:S(2)}) collective-permute-start(f32[32,1280]{1,0:T(8,128)S(1)} %get-tuple-element.55), channel_id=1, source_target_pairs={{0,8},{2,10},{4,12},{6,14},{8,0},{10,2},{12,4},{14,6},{1,9},{3,11}... | collective-permute-start | bytes 491528 | tf_op jit(solution)/shard_map/ppermute | solution.py:383
  33.0 1.6 %collective-permute-start.4 = (f32[32,1024]{1,0:T(8,128)S(1)}, f32[32,1024]{1,0:T(8,128)S(1)}, u32[]{:S(2)}, u32[]{:S(2)}) collective-permute-start(f32[32,1024]{1,0:T(8,128)S(1)} %get-tuple-element.58), channel_id=1, source_target_pairs={{0,4},{2,6},{4,0},{6,2},{8,12},{10,14},{12,8},{14,10},{1,5},{3,7},... | collective-permute-start | bytes 393224 | tf_op jit(solution)/shard_map/ppermute | solution.py:383
  35.2 1.6 %collective-permute-start.6 = (f32[32,512]{1,0:T(8,128)S(1)}, f32[32,512]{1,0:T(8,128)S(1)}, u32[]{:S(2)}, u32[]{:S(2)}) collective-permute-start(f32[32,512]{1,0:T(8,128)S(1)} %get-tuple-element.61), channel_id=1, source_target_pairs={{0,2},{2,0},{4,6},{6,4},{8,10},{10,8},{12,14},{14,12},{1,3},{3,1},... | collective-permute-start | bytes 196616 | tf_op jit(solution)/shard_map/ppermute | solution.py:383
  37.6 2.2 %collective-permute-start.11 = (f32[32,512]{1,0:T(8,128)S(1)}, f32[32,512]{1,0:T(8,128)S(1)}, u32[]{:S(2)}, u32[]{:S(2)}) collective-permute-start(f32[32,512]{1,0:T(8,128)S(1)} %get-tuple-element.70), channel_id=1, source_target_pairs={{0,4},{2,6},{4,0},{6,2},{8,12},{10,14},{12,8},{14,10},{1,5},{3,7},... | collective-permute-start | bytes 196616 | tf_op jit(solution)/shard_map/ppermute | solution.py:383
  41.6 1.8 %collective-permute-start.8 = (f32[16,1280]{1,0:T(8,128)S(1)}, f32[16,1280]{1,0:T(8,128)S(1)}, u32[]{:S(2)}, u32[]{:S(2)}) collective-permute-start(f32[16,1280]{1,0:T(8,128)S(1)} %get-tuple-element.67), channel_id=1, source_target_pairs={{0,2},{2,0},{4,6},{6,4},{8,10},{10,8},{12,14},{14,12},{1,3},{3,1},... | collective-permute-start | bytes 245768 | tf_op jit(solution)/shard_map/ppermute | solution.py:383
  43.3 0.9 collective-permute-start.9
  44.3 2.0 %collective-permute-start.10 = (f32[16,512]{1,0:T(8,128)S(1)}, f32[16,512]{1,0:T(8,128)S(1)}, u32[]{:S(2)}, u32[]{:S(2)}) collective-permute-start(f32[16,512]{1,0:T(8,128)S(1)} %get-tuple-element.69), channel_id=1, source_target_pairs={{0,8},{2,10},{4,12},{6,14},{8,0},{10,2},{12,4},{14,6},{1,9},{3,11}... | collective-permute-start | bytes 98312 | tf_op jit(solution)/shard_map/ppermute | solution.py:383
  46.8 1.0 %collective-permute-start.12 = (f32[16,512]{1,0:T(8,128)S(1)}, f32[16,512]{1,0:T(8,128)S(1)}, u32[]{:S(2)}, u32[]{:S(2)}) collective-permute-start(f32[16,512]{1,0:T(8,128)S(1)} %get-tuple-element.75), channel_id=1, source_target_pairs={{0,8},{2,10},{4,12},{6,14},{8,0},{10,2},{12,4},{14,6},{1,9},{3,11}... | collective-permute-start | bytes 98312 | tf_op jit(solution)/shard_map/ppermute | solution.py:383
  47.8 2.4 %collective-permute-done.10.got_ref = f32[16,512]{1,0:T(8,128)S(1)} collective-permute-done((f32[16,512]{1,0:T(8,128)S(1)}, f32[16,512]{1,0:T(8,128)S(1)}, u32[]{:S(2)}, u32[]{:S(2)}) %collective-permute-start.10) | collective-permute-done | bytes 32800 | tf_op jit(solution)/shard_map/ppermute | solution.py:383
  55.7 9.0 %attend.1 = (bf16[8,3072]{1,0:T(8,128)(2,1)}, bf16[8,3072]{1,0:T(8,128)(2,1)}) custom-call(s32[9]{0:T(128)} %pad_add_fusion.1.scalars_ref, bf16[8,1280]{1,0:T(8,128)(2,1)} %copy-done.4, bf16[8,1024]{1,0:T(8,128)(2,1)} %copy-done.5, bf16[8,512]{1,0:T(8,128)(2,1)} %copy-done.6, bf16[8,512]{1,0:T(8,128)(2,1)} %copy-done.7, bf16[8,1280]{1,0:T(8,128)(2,1)} %copy-done.8, ...), custom_call_target="tpu_custom_call" | custom-call | flops 201326592 | bytes 8388608 | tf_op jit(solution)/shard_map/attend/pallas_call | solution.py:256
  65.0 1.1 %collective-permute-done.17 = bf16[8,3072]{1,0:T(8,128)(2,1)S(1)} collective-permute-done((bf16[8,3072]{1,0:T(8,128)(2,1)}, bf16[8,3072]{1,0:T(8,128)(2,1)S(1)}, u32[]{:S(2)}, u32[]{:S(2)}) %collective-permute-start.17) | collective-permute-done | bytes 49184 | tf_op jit(solution)/shard_map/ppermute | solution.py:380
  66.1 0.9 maximum_select_fusion
  67.1 1.0 %collective-permute-start.21 = (bf16[16,1536]{1,0:T(8,128)(2,1)S(1)}, bf16[16,1536]{1,0:T(8,128)(2,1)S(1)}, u32[]{:S(2)}, u32[]{:S(2)}) collective-permute-start(bf16[16,1536]{1,0:T(8,128)(2,1)S(1)} %get-tuple-element.87), channel_id=1, source_target_pairs={{0,8},{2,10},{4,12},{6,14},{8,0},{10,2},{12,4},{14,6},{1,9},{3,11}... | collective-permute-start | bytes 147464 | tf_op jit(solution)/shard_map/ppermute | solution.py:383
  68.4 4.7 %collective-permute-done.21 = bf16[16,1536]{1,0:T(8,128)(2,1)S(1)} collective-permute-done((bf16[16,1536]{1,0:T(8,128)(2,1)S(1)}, bf16[16,1536]{1,0:T(8,128)(2,1)S(1)}, u32[]{:S(2)}, u32[]{:S(2)}) %collective-permute-start.21) | collective-permute-done | bytes 49184 | tf_op jit(solution)/shard_map/ppermute | solution.py:383
  73.6 2.1 %collective-permute-start.19 = (bf16[32,1536]{1,0:T(8,128)(2,1)S(1)}, bf16[32,1536]{1,0:T(8,128)(2,1)S(1)}, u32[]{:S(2)}, u32[]{:S(2)}) collective-permute-start(bf16[32,1536]{1,0:T(8,128)(2,1)S(1)} %pad_maximum_fusion.2), channel_id=1, source_target_pairs={{0,8},{2,10},{4,12},{6,14},{8,0},{10,2},{12,4},{14,6},{1,9},{3,11}... | collective-permute-start | bytes 294920 | tf_op jit(solution)/shard_map/ppermute | solution.py:383
  75.7 2.9 %collective-permute-done.22 = bf16[32,1536]{1,0:T(8,128)(2,1)S(1)} collective-permute-done((bf16[32,1536]{1,0:T(8,128)(2,1)S(1)}, bf16[32,1536]{1,0:T(8,128)(2,1)S(1)}, u32[]{:S(2)}, u32[]{:S(2)}) %collective-permute-start.22) | collective-permute-done | bytes 98336 | tf_op jit(solution)/shard_map/ppermute | solution.py:383
  79.3 1.6 %collective-permute-done.19 = bf16[32,1536]{1,0:T(8,128)(2,1)S(1)} collective-permute-done((bf16[32,1536]{1,0:T(8,128)(2,1)S(1)}, bf16[32,1536]{1,0:T(8,128)(2,1)S(1)}, u32[]{:S(2)}, u32[]{:S(2)}) %collective-permute-start.19) | collective-permute-done | bytes 98336 | tf_op jit(solution)/shard_map/ppermute | solution.py:383
  81.0 3.3 %collective-permute-done.23.far_ref = bf16[64,1536]{1,0:T(8,128)(2,1)S(1)} collective-permute-done((bf16[64,1536]{1,0:T(8,128)(2,1)S(1)}, bf16[64,1536]{1,0:T(8,128)(2,1)S(1)}, u32[]{:S(2)}, u32[]{:S(2)}) %collective-permute-start.23) | collective-permute-done | bytes 196640 | tf_op jit(solution)/shard_map/ppermute | solution.py:383
  84.4 4.9 %project_out.2 = (f32[64,2304]{1,0:T(8,128)S(1)}, f32[64,2304]{1,0:T(8,128)S(1)}) custom-call(s32[2]{0:T(128)S(1)} %pad_add_fusion.refs_0_.ids_ref, bf16[64,1536]{1,0:T(8,128)(2,1)S(1)} %pad_maximum_fusion.1.near_ref, bf16[64,1536]{1,0:T(8,128)(2,1)S(1)} %collective-permute-done.23.far_ref, bf16[3072,2304]{1,0:T(8,128)(2,1)} %w_hbm.3), custom_call_target="tpu_custom_call" | custom-call | flops 905969664 | bytes 8257536 | tf_op jit(solution)/shard_map/project_out/pallas_call | solution.py:344
  89.3 0.8 copy-done.1
  90.1 0.8 copy-done.2
  90.9 6.4 %project_out.3 = (f32[64,2304]{1,0:T(8,128)S(1)}, f32[64,2304]{1,0:T(8,128)S(1)}) custom-call(s32[2]{0:T(128)S(1)} %pad_add_fusion.refs_0_.ids_ref, bf16[64,1536]{1,0:T(8,128)(2,1)S(1)} %pad_maximum_fusion.near_ref, bf16[64,1536]{1,0:T(8,128)(2,1)S(1)} %collective-permute-done.20.far_ref, bf16[3072,2304]{1,0:T(8,128)(2,1)} %w_hbm.3, f32[64,2304]{1,0:T(8,128)} %copy-done.1, ...), custom_call_target="tpu_custom_call" | custom-call | flops 905969664 | bytes 8257536 | tf_op jit(solution)/shard_map/project_out/pallas_call | solution.py:344
  97.5 2.0 %collective-permute-done.24 = f32[64,2304]{1,0:T(8,128)S(1)} collective-permute-done((f32[64,2304]{1,0:T(8,128)S(1)}, f32[64,2304]{1,0:T(8,128)S(1)}, u32[]{:S(2)}, u32[]{:S(2)}) %collective-permute-start.24) | collective-permute-done | bytes 589856 | tf_op jit(solution)/shard_map/ppermute | solution.py:380
  (73 shorter events, 14.6 us)
Async XLA Ops:
  0.0 8.4 %collective-permute-start = (bf16[64,2304]{1,0:T(8,128)(2,1)}, bf16[64,2304]{1,0:T(8,128)(2,1)S(1)}, u32[]{:S(2)}, u32[]{:S(2)}) collective-permute-start(bf16[64,2304]{1,0:T(8,128)(2,1)} %refs_3_.1), channel_id=1, source_target_pairs={{0,1},{1,0},{2,3},{3,2},{4,5},{5,4},{6,7},{7,6},{8,9},{9,8},{10,11... | collective-permute-start | bytes 884744 | tf_op jit(solution)/shard_map/ppermute | solution.py:380
  0.5 1.7 %copy-start = (bf16[2304,512]{1,0:T(8,128)(2,1)S(1)}, bf16[2304,512]{1,0:T(8,128)(2,1)}, u32[]{:S(2)}) copy-start(bf16[2304,512]{1,0:T(8,128)(2,1)} %refs_2_.1) | copy-start | bytes 7077892
  2.2 1.0 copy-start.3
  12.7 16.0 %collective-permute-start.1 = (f32[64,1280]{1,0:T(8,128)S(1)}, f32[64,1280]{1,0:T(8,128)S(1)}, u32[]{:S(2)}, u32[]{:S(2)}) collective-permute-start(f32[64,1280]{1,0:T(8,128)S(1)} %get-tuple-element.50.refs_1_), channel_id=1, source_target_pairs={{0,4},{2,6},{4,0},{6,2},{8,12},{10,14},{12,8},{14,10},{1,5},{3,7},... | collective-permute-start | bytes 983048 | tf_op jit(solution)/shard_map/ppermute | solution.py:383
  19.6 12.8 %collective-permute-start.3 = (f32[64,1024]{1,0:T(8,128)S(1)}, f32[64,1024]{1,0:T(8,128)S(1)}, u32[]{:S(2)}, u32[]{:S(2)}) collective-permute-start(f32[64,1024]{1,0:T(8,128)S(1)} %get-tuple-element.51.refs_1_), channel_id=1, source_target_pairs={{0,2},{2,0},{4,6},{6,4},{8,10},{10,8},{12,14},{14,12},{1,3},{3,1},... | collective-permute-start | bytes 786440 | tf_op jit(solution)/shard_map/ppermute | solution.py:383
  24.6 29.6 %copy-start.12 = (s32[8]{0:T(128)S(1)}, s32[8]{0:T(128)}, u32[]{:S(2)}) copy-start(s32[8]{0:T(128)} %param.13) | copy-start | bytes 100
  24.7 10.0 %collective-permute-start.5 = (f32[64,512]{1,0:T(8,128)S(1)}, f32[64,512]{1,0:T(8,128)S(1)}, u32[]{:S(2)}, u32[]{:S(2)}) collective-permute-start(f32[64,512]{1,0:T(8,128)S(1)} %get-tuple-element.52.refs_1_), channel_id=1, source_target_pairs={{0,4},{2,6},{4,0},{6,2},{8,12},{10,14},{12,8},{14,10},{1,5},{3,7},... | collective-permute-start | bytes 393224 | tf_op jit(solution)/shard_map/ppermute | solution.py:383
  29.2 11.7 %collective-permute-start.2 = (f32[32,1280]{1,0:T(8,128)S(1)}, f32[32,1280]{1,0:T(8,128)S(1)}, u32[]{:S(2)}, u32[]{:S(2)}) collective-permute-start(f32[32,1280]{1,0:T(8,128)S(1)} %get-tuple-element.55), channel_id=1, source_target_pairs={{0,8},{2,10},{4,12},{6,14},{8,0},{10,2},{12,4},{14,6},{1,9},{3,11}... | collective-permute-start | bytes 491528 | tf_op jit(solution)/shard_map/ppermute | solution.py:383
  31.9 5.1 %collective-permute-start.7 = (f32[64,512]{1,0:T(8,128)S(1)}, f32[64,512]{1,0:T(8,128)S(1)}, u32[]{:S(2)}, u32[]{:S(2)}) collective-permute-start(f32[64,512]{1,0:T(8,128)S(1)} %get-tuple-element.53.after_ref), channel_id=1, source_target_pairs={{0,2},{2,0},{4,6},{6,4},{8,10},{10,8},{12,14},{14,12},{1,3},{3,1},... | collective-permute-start | bytes 393224 | tf_op jit(solution)/shard_map/ppermute | solution.py:383
  33.0 7.4 %collective-permute-start.4 = (f32[32,1024]{1,0:T(8,128)S(1)}, f32[32,1024]{1,0:T(8,128)S(1)}, u32[]{:S(2)}, u32[]{:S(2)}) collective-permute-start(f32[32,1024]{1,0:T(8,128)S(1)} %get-tuple-element.58), channel_id=1, source_target_pairs={{0,4},{2,6},{4,0},{6,2},{8,12},{10,14},{12,8},{14,10},{1,5},{3,7},... | collective-permute-start | bytes 393224 | tf_op jit(solution)/shard_map/ppermute | solution.py:383
  35.2 4.6 %collective-permute-start.6 = (f32[32,512]{1,0:T(8,128)S(1)}, f32[32,512]{1,0:T(8,128)S(1)}, u32[]{:S(2)}, u32[]{:S(2)}) collective-permute-start(f32[32,512]{1,0:T(8,128)S(1)} %get-tuple-element.61), channel_id=1, source_target_pairs={{0,2},{2,0},{4,6},{6,4},{8,10},{10,8},{12,14},{14,12},{1,3},{3,1},... | collective-permute-start | bytes 196616 | tf_op jit(solution)/shard_map/ppermute | solution.py:383
  37.6 8.7 %collective-permute-start.11 = (f32[32,512]{1,0:T(8,128)S(1)}, f32[32,512]{1,0:T(8,128)S(1)}, u32[]{:S(2)}, u32[]{:S(2)}) collective-permute-start(f32[32,512]{1,0:T(8,128)S(1)} %get-tuple-element.70), channel_id=1, source_target_pairs={{0,4},{2,6},{4,0},{6,2},{8,12},{10,14},{12,8},{14,10},{1,5},{3,7},... | collective-permute-start | bytes 196616 | tf_op jit(solution)/shard_map/ppermute | solution.py:383
  41.6 10.4 %collective-permute-start.8 = (f32[16,1280]{1,0:T(8,128)S(1)}, f32[16,1280]{1,0:T(8,128)S(1)}, u32[]{:S(2)}, u32[]{:S(2)}) collective-permute-start(f32[16,1280]{1,0:T(8,128)S(1)} %get-tuple-element.67), channel_id=1, source_target_pairs={{0,2},{2,0},{4,6},{6,4},{8,10},{10,8},{12,14},{14,12},{1,3},{3,1},... | collective-permute-start | bytes 245768 | tf_op jit(solution)/shard_map/ppermute | solution.py:383
  43.3 7.5 %collective-permute-start.9 = (f32[16,1024]{1,0:T(8,128)S(1)}, f32[16,1024]{1,0:T(8,128)S(1)}, u32[]{:S(2)}, u32[]{:S(2)}) collective-permute-start(f32[16,1024]{1,0:T(8,128)S(1)} %get-tuple-element.68), channel_id=1, source_target_pairs={{0,8},{2,10},{4,12},{6,14},{8,0},{10,2},{12,4},{14,6},{1,9},{3,11}... | collective-permute-start | bytes 196616 | tf_op jit(solution)/shard_map/ppermute | solution.py:383
  44.3 5.9 %collective-permute-start.10 = (f32[16,512]{1,0:T(8,128)S(1)}, f32[16,512]{1,0:T(8,128)S(1)}, u32[]{:S(2)}, u32[]{:S(2)}) collective-permute-start(f32[16,512]{1,0:T(8,128)S(1)} %get-tuple-element.69), channel_id=1, source_target_pairs={{0,8},{2,10},{4,12},{6,14},{8,0},{10,2},{12,4},{14,6},{1,9},{3,11}... | collective-permute-start | bytes 98312 | tf_op jit(solution)/shard_map/ppermute | solution.py:383
  46.8 5.7 %collective-permute-start.12 = (f32[16,512]{1,0:T(8,128)S(1)}, f32[16,512]{1,0:T(8,128)S(1)}, u32[]{:S(2)}, u32[]{:S(2)}) collective-permute-start(f32[16,512]{1,0:T(8,128)S(1)} %get-tuple-element.75), channel_id=1, source_target_pairs={{0,8},{2,10},{4,12},{6,14},{8,0},{10,2},{12,4},{14,6},{1,9},{3,11}... | collective-permute-start | bytes 98312 | tf_op jit(solution)/shard_map/ppermute | solution.py:383
  50.7 4.3 %copy-start.6 = (bf16[8,512]{1,0:T(8,128)(2,1)}, bf16[8,512]{1,0:T(8,128)(2,1)S(1)}, u32[]{:S(2)}) copy-start(bf16[8,512]{1,0:T(8,128)(2,1)S(1)} %get-tuple-element.72.after_ref.refs_2_) | copy-start | bytes 24580
  50.8 4.1 %collective-permute-start.15 = (bf16[8,512]{1,0:T(8,128)(2,1)S(1)}, bf16[8,512]{1,0:T(8,128)(2,1)S(1)}, u32[]{:S(2)}, u32[]{:S(2)}) collective-permute-start(bf16[8,512]{1,0:T(8,128)(2,1)S(1)} %get-tuple-element.79), channel_id=1, source_target_pairs={{0,1},{1,0},{2,3},{3,2},{4,5},{5,4},{6,7},{7,6},{8,9},{9,8},{10,11... | collective-permute-start | bytes 24584 | tf_op jit(solution)/shard_map/ppermute | solution.py:380
  51.4 3.7 %copy-start.5 = (bf16[8,1024]{1,0:T(8,128)(2,1)}, bf16[8,1024]{1,0:T(8,128)(2,1)S(1)}, u32[]{:S(2)}) copy-start(bf16[8,1024]{1,0:T(8,128)(2,1)S(1)} %get-tuple-element.73.after_ref.refs_1_) | copy-start | bytes 49156
  51.4 3.5 %collective-permute-start.14 = (bf16[8,1024]{1,0:T(8,128)(2,1)S(1)}, bf16[8,1024]{1,0:T(8,128)(2,1)S(1)}, u32[]{:S(2)}, u32[]{:S(2)}) collective-permute-start(bf16[8,1024]{1,0:T(8,128)(2,1)S(1)} %get-tuple-element.78), channel_id=1, source_target_pairs={{0,1},{1,0},{2,3},{3,2},{4,5},{5,4},{6,7},{7,6},{8,9},{9,8},{10,11... | collective-permute-start | bytes 49160 | tf_op jit(solution)/shard_map/ppermute | solution.py:380
  52.5 2.5 %copy-start.4 = (bf16[8,1280]{1,0:T(8,128)(2,1)}, bf16[8,1280]{1,0:T(8,128)(2,1)S(1)}, u32[]{:S(2)}) copy-start(bf16[8,1280]{1,0:T(8,128)(2,1)S(1)} %get-tuple-element.74.after_ref.refs_0_) | copy-start | bytes 61444
  53.7 1.2 %collective-permute-start.16 = (bf16[8,512]{1,0:T(8,128)(2,1)S(1)}, bf16[8,512]{1,0:T(8,128)(2,1)S(1)}, u32[]{:S(2)}, u32[]{:S(2)}) collective-permute-start(bf16[8,512]{1,0:T(8,128)(2,1)S(1)} %get-tuple-element.80), channel_id=1, source_target_pairs={{0,1},{1,0},{2,3},{3,2},{4,5},{5,4},{6,7},{7,6},{8,9},{9,8},{10,11... | collective-permute-start | bytes 24584 | tf_op jit(solution)/shard_map/ppermute | solution.py:380
  53.7 1.3 %collective-permute-start.13 = (bf16[8,1280]{1,0:T(8,128)(2,1)S(1)}, bf16[8,1280]{1,0:T(8,128)(2,1)S(1)}, u32[]{:S(2)}, u32[]{:S(2)}) collective-permute-start(bf16[8,1280]{1,0:T(8,128)(2,1)S(1)} %get-tuple-element.77), channel_id=1, source_target_pairs={{0,1},{1,0},{2,3},{3,2},{4,5},{5,4},{6,7},{7,6},{8,9},{9,8},{10,11... | collective-permute-start | bytes 61448 | tf_op jit(solution)/shard_map/ppermute | solution.py:380
  64.6 1.5 %collective-permute-start.17 = (bf16[8,3072]{1,0:T(8,128)(2,1)}, bf16[8,3072]{1,0:T(8,128)(2,1)S(1)}, u32[]{:S(2)}, u32[]{:S(2)}) collective-permute-start(bf16[8,3072]{1,0:T(8,128)(2,1)} %get-tuple-element.82), channel_id=1, source_target_pairs={{0,1},{1,0},{2,3},{3,2},{4,5},{5,4},{6,7},{7,6},{8,9},{9,8},{10,11... | collective-permute-start | bytes 147464 | tf_op jit(solution)/shard_map/ppermute | solution.py:380
  67.1 6.1 %collective-permute-start.21 = (bf16[16,1536]{1,0:T(8,128)(2,1)S(1)}, bf16[16,1536]{1,0:T(8,128)(2,1)S(1)}, u32[]{:S(2)}, u32[]{:S(2)}) collective-permute-start(bf16[16,1536]{1,0:T(8,128)(2,1)S(1)} %get-tuple-element.87), channel_id=1, source_target_pairs={{0,8},{2,10},{4,12},{6,14},{8,0},{10,2},{12,4},{14,6},{1,9},{3,11}... | collective-permute-start | bytes 147464 | tf_op jit(solution)/shard_map/ppermute | solution.py:383
  68.1 5.5 %collective-permute-start.18 = (bf16[16,1536]{1,0:T(8,128)(2,1)S(1)}, bf16[16,1536]{1,0:T(8,128)(2,1)S(1)}, u32[]{:S(2)}, u32[]{:S(2)}) collective-permute-start(bf16[16,1536]{1,0:T(8,128)(2,1)S(1)} %get-tuple-element.88), channel_id=1, source_target_pairs={{0,2},{2,0},{4,6},{6,4},{8,10},{10,8},{12,14},{14,12},{1,3},{3,1},... | collective-permute-start | bytes 147464 | tf_op jit(solution)/shard_map/ppermute | solution.py:383
  73.2 5.4 %collective-permute-start.22 = (bf16[32,1536]{1,0:T(8,128)(2,1)S(1)}, bf16[32,1536]{1,0:T(8,128)(2,1)S(1)}, u32[]{:S(2)}, u32[]{:S(2)}) collective-permute-start(bf16[32,1536]{1,0:T(8,128)(2,1)S(1)} %pad_maximum_fusion.3), channel_id=1, source_target_pairs={{0,4},{2,6},{4,0},{6,2},{8,12},{10,14},{12,8},{14,10},{1,5},{3,7},... | collective-permute-start | bytes 294920 | tf_op jit(solution)/shard_map/ppermute | solution.py:383
  73.6 7.4 %collective-permute-start.19 = (bf16[32,1536]{1,0:T(8,128)(2,1)S(1)}, bf16[32,1536]{1,0:T(8,128)(2,1)S(1)}, u32[]{:S(2)}, u32[]{:S(2)}) collective-permute-start(bf16[32,1536]{1,0:T(8,128)(2,1)S(1)} %pad_maximum_fusion.2), channel_id=1, source_target_pairs={{0,8},{2,10},{4,12},{6,14},{8,0},{10,2},{12,4},{14,6},{1,9},{3,11}... | collective-permute-start | bytes 294920 | tf_op jit(solution)/shard_map/ppermute | solution.py:383
  78.6 5.7 %collective-permute-start.23 = (bf16[64,1536]{1,0:T(8,128)(2,1)S(1)}, bf16[64,1536]{1,0:T(8,128)(2,1)S(1)}, u32[]{:S(2)}, u32[]{:S(2)}) collective-permute-start(bf16[64,1536]{1,0:T(8,128)(2,1)S(1)} %pad_maximum_fusion.1.near_ref), channel_id=1, source_target_pairs={{0,2},{2,0},{4,6},{6,4},{8,10},{10,8},{12,14},{14,12},{1,3},{3,1},... | collective-permute-start | bytes 589832 | tf_op jit(solution)/shard_map/ppermute | solution.py:383
  81.0 10.0 %collective-permute-start.20 = (bf16[64,1536]{1,0:T(8,128)(2,1)S(1)}, bf16[64,1536]{1,0:T(8,128)(2,1)S(1)}, u32[]{:S(2)}, u32[]{:S(2)}) collective-permute-start(bf16[64,1536]{1,0:T(8,128)(2,1)S(1)} %pad_maximum_fusion.near_ref), channel_id=1, source_target_pairs={{0,4},{2,6},{4,0},{6,2},{8,12},{10,14},{12,8},{14,10},{1,5},{3,7},... | collective-permute-start | bytes 589832 | tf_op jit(solution)/shard_map/ppermute | solution.py:383
  89.3 0.8 copy-start.1
  97.4 2.1 %collective-permute-start.24 = (f32[64,2304]{1,0:T(8,128)S(1)}, f32[64,2304]{1,0:T(8,128)S(1)}, u32[]{:S(2)}, u32[]{:S(2)}) collective-permute-start(f32[64,2304]{1,0:T(8,128)S(1)} %get-tuple-element.86), channel_id=1, source_target_pairs={{0,1},{1,0},{2,3},{3,2},{4,5},{5,4},{6,7},{7,6},{8,9},{9,8},{10,11... | collective-permute-start | bytes 1769480 | tf_op jit(solution)/shard_map/ppermute | solution.py:380
  (6 other events, 3.8 us)

commit v4 on v2

v4 whole, which is shorter than its diff:
```python
import functools

import jax
import jax.numpy as jnp
from jax import lax
from jax.experimental import pallas as pl
from jax.experimental.pallas import tpu as pltpu
from jax.sharding import PartitionSpec as P

H = 24
DH = 256
MIB = 1024 * 1024
HBM = pl.BlockSpec(memory_space=pltpu.HBM)
ANY = pl.BlockSpec(memory_space=pl.ANY)
VMEM = pl.BlockSpec(memory_space=pltpu.VMEM)
SMEM = pl.BlockSpec(memory_space=pltpu.SMEM)


def slabs_of(depth):
    return depth // 256 if depth % 256 == 0 else 1


class InOrder:
    def __init__(self, copies, ahead):
        self.copies, self.ahead = copies, ahead
        for copy in copies[:ahead]:
            copy.start()

    def wait(self, at):
        self.copies[at].wait()
        if at + self.ahead < len(self.copies):
            self.copies[at + self.ahead].start()


def order_of(bits):
    order = [0]
    for bit in reversed(bits):
        order = order + [j + bit for j in order]
    return order


def project_kernel(order, rows, first, kv_width, after, ids_ref, own_ref, other_ref, w_ref, *refs):
    refs = list(refs)
    kv_ref = refs.pop(0) if kv_width else None
    send_ref, keep_ref, xs_ref, ws_ref, row_sem, w_sem = refs[after:]
    n = len(order)
    slabs, slab, columns = ws_ref.shape
    me, core = ids_ref[0], ids_ref[1]
    half = n // 2

    def row_copy(source_ref, p):
        block = jnp.bitwise_xor(me, order[p])
        source = pl.ds(pl.multiple_of((block % half) * rows, rows), rows)
        return pltpu.make_async_copy(
            source_ref.at[source, :], xs_ref.at[pl.ds(p * rows, rows), :], row_sem.at[p]
        )

    for p in range(n):
        mine = jnp.bitwise_xor(me, order[p]) // half == core

        @pl.when(mine)
        def _():
            row_copy(own_ref, p).start()

        @pl.when(jnp.logical_not(mine))
        def _():
            row_copy(other_ref, p).start()

    copies = []
    per_slab = 1
    for k in range(slabs):
        span = pl.ds(k * slab, slab)
        if kv_width:
            per_slab = 2
            own = pl.ds(pl.multiple_of(core * kv_width, kv_width), kv_width)
            target = ws_ref.at[k, :, pl.ds(0, kv_width)]
            copies.append(pltpu.make_async_copy(kv_ref.at[span, own], target, w_sem.at[1, k]))
        width = columns - kv_width
        target = ws_ref.at[k, :, pl.ds(kv_width, width)]
        copies.append(pltpu.make_async_copy(w_ref.at[span, pl.ds(first, width)], target, w_sem.at[0, k]))
    weights = InOrder(copies, 3 * per_slab)
    for p in range(n):
        row_copy(own_ref, p).wait()
    cut = n * rows // 2
    for k in range(slabs):
        for at in range(per_slab):
            weights.wait(k * per_slab + at)
        part = jnp.dot(
            xs_ref[:, k * slab : (k + 1) * slab], ws_ref[k], preferred_element_type=jnp.float32
        )
        if k == 0:
            keep_ref[...] = part[:cut]
            send_ref[...] = part[cut:]
        else:
            keep_ref[...] += part[:cut]
            send_ref[...] += part[cut:]


def project(bits, rows, ids, tokens, other, query_weight, kv_weight, first, width, after):
    features = tokens.shape[1]
    order = order_of(bits)
    n = len(order)
    slabs = slabs_of(features)
    kv_width = kv_weight.shape[1] // 2 if kv_weight is not None else 0
    columns = width + kv_width
    out = jax.ShapeDtypeStruct((n * rows // 2, columns), jnp.float32)
    weights = [query_weight] + ([kv_weight] if kv_width else [])
    return pl.pallas_call(
        functools.partial(project_kernel, order, rows, first, kv_width, len(after)),
        out_shape=(out, out),
        in_specs=[SMEM, ANY, ANY] + [HBM] * len(weights) + [ANY] * len(after),
        out_specs=(VMEM, VMEM),
        scratch_shapes=[
            pltpu.VMEM((n * rows, features), tokens.dtype),
            pltpu.VMEM((slabs, features // slabs, columns), tokens.dtype),
            pltpu.SemaphoreType.DMA((n,)),
            pltpu.SemaphoreType.DMA((2, slabs)),
        ],
        compiler_params=pltpu.CompilerParams(vmem_limit_bytes=46 * MIB),
        cost_estimate=pl.CostEstimate(
            flops=2 * n * rows * features * columns,
            bytes_accessed=2 * features * columns + 4 * n * rows * columns,
            transcendentals=0,
        ),
        name="project",
    )(ids, tokens, other, *weights, *after)


def attend_kernel(parts, scalars_ref, *refs):
    own_q, other_q = refs[: len(parts)], refs[len(parts) : 2 * len(parts)]
    k_hbm, v_hbm, own_out, other_out, k_ref, v_ref, q_scr, o_scr, sems = refs[2 * len(parts) :]
    core = scalars_ref[0]
    rows, positions, _ = k_ref.shape
    copies = []
    for row in range(rows):
        copies.append(pltpu.make_async_copy(k_hbm.at[row], k_ref.at[row], sems.at[0, row]))
        copies.append(pltpu.make_async_copy(v_hbm.at[row], v_ref.at[row], sems.at[1, row]))
    caches = InOrder(copies, 4)
    at = 0
    for side in (own_q, other_q):
        for ref, (heads, skip) in zip(side, parts):
            for head in range(heads):
                column = skip + head * DH
                q_scr[:, at, :] = ref[:, column : column + DH].astype(jnp.float32)
                at += 1
    total_heads = at
    first = own_q[0][:, :DH].astype(jnp.float32)
    second = other_q[0][:, :DH].astype(jnp.float32)
    new_keys = jnp.where(core == 0, first, second)
    new_values = jnp.where(core == 0, second, first)
    scale = DH**-0.5
    for row in range(rows):
        query = q_scr[row]
        caches.wait(2 * row)
        scores = scale * lax.dot_general(
            query.astype(jnp.bfloat16),
            k_ref[row],
            (((1,), (1,)), ((), ())),
            preferred_element_type=jnp.float32,
        )
        self_score = scale * jnp.sum(query * new_keys[row : row + 1], axis=1, keepdims=True)
        visible = lax.broadcasted_iota(jnp.int32, scores.shape, 1) < scalars_ref[1 + row]
        masked = jnp.where(visible, scores, jnp.float32(-1e30))
        peak = jnp.maximum(jnp.max(masked, axis=1, keepdims=True), self_score)
        raised = jnp.where(visible, jnp.exp(masked - peak), jnp.float32(0.0))
        self_raised = jnp.exp(self_score - peak)
        denominator = jnp.sum(raised, axis=1, keepdims=True) + self_raised
        weights = (raised / denominator).astype(jnp.bfloat16)
        self_weight = (self_raised / denominator).astype(jnp.bfloat16).astype(jnp.float32)
        caches.wait(2 * row + 1)
        total = jnp.dot(weights, v_ref[row], preferred_element_type=jnp.float32)
        o_scr[row] = total + self_weight * new_values[row : row + 1]
    half = total_heads // 2
    for head in range(total_heads):
        ref = own_out if head < half else other_out
        column = (head % half) * DH
        ref[:, column : column + DH] = o_scr[:, head, :].astype(jnp.bfloat16)


def attend(core, lengths, own_q, other_q, parts, keys, values):
    rows, positions, _ = keys.shape
    heads = 2 * sum(part[0] for part in parts)
    out = jax.ShapeDtypeStruct((rows, heads * DH // 2), jnp.bfloat16)
    scalars = jnp.concatenate([core[None], lengths])
    return pl.pallas_call(
        functools.partial(attend_kernel, parts),
        out_shape=(out, out),
        in_specs=[SMEM] + [VMEM] * (2 * len(parts)) + [HBM, HBM],
        out_specs=(VMEM, VMEM),
        scratch_shapes=[pltpu.VMEM(keys.shape, keys.dtype)] * 2
        + [pltpu.VMEM((rows, heads, DH), jnp.float32)] * 2
        + [pltpu.SemaphoreType.DMA((2, rows))],
        compiler_params=pltpu.CompilerParams(vmem_limit_bytes=52 * MIB),
        cost_estimate=pl.CostEstimate(
            flops=4 * rows * heads * positions * DH,
            bytes_accessed=4 * rows * positions * DH,
            transcendentals=rows * heads * positions,
        ),
        name="attend",
    )(scalars, *own_q, *other_q, keys, values)


def output_kernel(order, rows, first, with_prior, ids_ref, near_ref, far_ref, w_hbm, *refs):
    if with_prior:
        send_in, keep_in, send_ref, keep_ref, xs_ref, ws_ref, row_sem, w_sem = refs
    else:
        send_ref, keep_ref, xs_ref, ws_ref, row_sem, w_sem = refs
    me, core = ids_ref[0], ids_ref[1]
    n = len(order)
    half = n // 2
    slabs, slab, _ = ws_ref.shape
    row_copies = []
    for p, j in enumerate(order):
        block = jnp.bitwise_xor(me, j)
        place = block % half + jnp.where(block // half == core, half, 0)
        source = near_ref if p < half else far_ref
        row_copies.append(
            pltpu.make_async_copy(
                source.at[pl.ds((p % half) * rows, rows), :],
                xs_ref.at[pl.ds(pl.multiple_of(place * rows, rows), rows), :],
                row_sem.at[p],
            )
        )
    for copy in row_copies:
        copy.start()
    weights = InOrder(
        [
            pltpu.make_async_copy(w_hbm.at[pl.ds(first + k * slab, slab)], ws_ref.at[k], w_sem.at[k])
            for k in range(slabs)
        ],
        2,
    )
    for copy in row_copies:
        copy.wait()
    cut = half * rows
    for k in range(slabs):
        weights.wait(k)
        part = jnp.dot(
            xs_ref[:, k * slab : (k + 1) * slab], ws_ref[k], preferred_element_type=jnp.float32
        )
        if k:
            send_ref[...] += part[:cut]
            keep_ref[...] += part[cut:]
        elif with_prior:
            send_ref[...] = send_in[...] + part[:cut]
            keep_ref[...] = keep_in[...] + part[cut:]
        else:
            send_ref[...] = part[:cut]
            keep_ref[...] = part[cut:]


def project_out(order, rows, ids, near, far, out_weight, first, prior):
    depth = near.shape[1]
    columns = out_weight.shape[1]
    n = len(order)
    slabs = slabs_of(depth)
    out = jax.ShapeDtypeStruct((n * rows // 2, columns), jnp.float32)
    operands = [ids, near, far, out_weight] + ([] if prior is None else list(prior))
    return pl.pallas_call(
        functools.partial(output_kernel, order, rows, first, prior is not None),
        out_shape=(out, out),
        in_specs=[SMEM, ANY, ANY, HBM] + [VMEM] * (len(operands) - 4),
        out_specs=(VMEM, VMEM),
        scratch_shapes=[
            pltpu.VMEM((n * rows, depth), jnp.bfloat16),
            pltpu.VMEM((slabs, depth // slabs, columns), jnp.bfloat16),
            pltpu.SemaphoreType.DMA((n,)),
            pltpu.SemaphoreType.DMA((slabs,)),
        ],
        compiler_params=pltpu.CompilerParams(vmem_limit_bytes=46 * MIB),
        cost_estimate=pl.CostEstimate(
            flops=2 * n * rows * depth * columns,
            bytes_accessed=2 * depth * columns + 4 * n * rows * columns,
            transcendentals=0,
        ),
        name="project_out",
    )(*operands)


def local(tokens, query_weight, kv_weight, out_weight, key_cache, value_cache, lengths):
    n = lax.axis_size("gx")
    me = lax.axis_index("gx").astype(jnp.int32)
    core = lax.axis_index("gy").astype(jnp.int32)
    ids = jnp.stack([me, core])
    own_rows = key_cache.shape[0]
    rows = 2 * own_rows
    bits = [1 << i for i in range(n.bit_length() - 1)]

    def swap(array):
        return lax.ppermute(array, "gy", [(0, 1), (1, 0)])

    def across(array, mask):
        return lax.ppermute(array, "gx", [(g, g ^ mask) for g in range(n)])

    other_tokens = swap(tokens)
    own_tokens = jnp.where(me < n, tokens, jnp.bfloat16(0))
    width = query_weight.shape[1] // 2

    y, z = bits[:1], bits[1:]
    unit = query_weight.shape[1] // 12
    plan = [(3 * unit, y + z), (5 * unit, y + z), (4 * unit, z + y)]
    state, moving, first, after = [], [], 0, []
    for i, (columns, order) in enumerate(plan):
        send, keep = project(
            order, rows, ids, own_tokens, other_tokens, query_weight, None if i else kv_weight, first, columns, after
        )
        state.append((send, keep))
        moving.append(across(send, order[0]))
        first += columns
        after = []
    for step in range(len(bits)):
        for i, (columns, order) in enumerate(plan):
            total = state[i][1] + moving[i]
            if step + 1 < len(bits):
                cut = total.shape[0] // 2
                state[i] = (total[cut:], total[:cut])
                moving[i] = across(state[i][0], order[step + 1])
            else:
                state[i] = total
    mine, theirs = [], []
    for total in state:
        mine.append(lax.dynamic_slice_in_dim(total, core * own_rows, own_rows, 0).astype(jnp.bfloat16))
        give = lax.dynamic_slice_in_dim(total, (1 - core) * own_rows, own_rows, 0).astype(jnp.bfloat16)
        theirs.append(swap(give))

    kv_width = kv_weight.shape[1] // 2
    parts = tuple((columns // DH, 0 if i else kv_width) for i, (columns, _) in enumerate(plan))
    own, other = attend(core, lengths, mine, theirs, parts, key_cache, value_cache)
    got = swap(other)
    block = jnp.where(core == 0, jnp.concatenate([own, got]), jnp.concatenate([got, own]))

    near = [block[:, :width], block[:, width:]]
    far = [None, None]
    paths = [bits[::-1], bits[:1] + bits[:0:-1]]
    for step in range(len(bits)):
        for i in range(2):
            if step:
                near[i] = jnp.concatenate([near[i], far[i]])
            far[i] = across(near[i], paths[i][step])
    prior = None
    for i in range(2):
        prior = project_out(order_of(paths[i][::-1]), rows, ids, near[i], far[i], out_weight, i * width, prior)
    send, keep = prior
    return (keep + swap(send)).astype(jnp.bfloat16)


def solution(mesh):
    return jax.shard_map(
        local,
        mesh=mesh,
        in_specs=(
            P(("grp", "gy"), "gx"),
            P("gx", "gy"),
            P("gx", None),
            P("gy", "gx"),
            P(("grp", "gx", "gy"), None, None),
            P(("grp", "gx", "gy"), None, None),
            P(("grp", "gx", "gy")),
        ),
        out_specs=P(("grp", "gy"), "gx"),
        check_vma=False,
    )
```

time: 91.2 us -> 92.3 us (1.012)
  Pallas kernels: 16.3 us -> 36.6 us
  local copies, waits for them, and re-layouts: 16.6 us -> 0.1 us
  waiting for transfers between devices: 39.3 us -> 27.2 us
  starting transfers between devices: 17.3 us -> 25.5 us
  other arithmetic: 1.15 us -> 2.19 us
    pallas_call x4 -> x5, Pallas kernels: 11.6 us -> 28.5 us  [the longest x3 16.7 us: project(): pl.pallas_call(functools.partial(project_kernel, order, rows, first, kv_w...]
    unnamed x16 -> x4, local copies, waits for them, and re-layouts: 16.6 us -> 0.01 us
    ppermute x12 -> x15, waiting for transfers between devices: 33.8 us -> 22.7 us  [across(): return lax.ppermute(array, 'gx', [(g, g ^ mask) for g in range(n)])]
    ppermute x12 -> x15, starting transfers between devices: 16.4 us -> 24.6 us  [across(): return lax.ppermute(array, 'gx', [(g, g ^ mask) for g in range(n)])]
    pallas_call x1, Pallas kernels: 4.65 us -> 8.05 us  [attend(): pl.pallas_call(functools.partial(attend_kernel, parts), out_shape=(out, o...]
    ppermute x5 -> x6, waiting for transfers between devices: 5.5 us -> 4.5 us  [swap(): return lax.ppermute(array, 'gy', [(0, 1), (1, 0)])]
    select_n x0 -> x1, other arithmetic: none -> 0.98 us  [local(): own_tokens = jnp.where(me < n, tokens, jnp.bfloat16(0))]
  transfers between devices with their start and end apart: 17 -> 21, of which waited for: 13 -> 13; matrix products, arithmetic and copies ran while one was open for 0% -> 2% of each run, Pallas kernels for 7% -> 19%
where the time goes in v4:
time: 92.3 us; the launch traced here: 91.8 us
  Pallas kernels  36.6 us (40%)
  waiting for transfers between devices  27.2 us (29%)
  starting transfers between devices  25.5 us (28%)
  other arithmetic  2.19 us (2%)
    ppermute x15, starting transfers between devices, across(): return lax.ppermute(array, 'gx', [(g, g ^ mask) for g in range(n)])  24.6 us
    ppermute x15, waiting for transfers between devices, across(): return lax.ppermute(array, 'gx', [(g, g ^ mask) for g in range(n)])  22.7 us
    pallas_call x3, Pallas kernels, project(): pl.pallas_call(functools.partial(project_kernel, order, rows, first, kv_w...  16.7 us
    pallas_call x2, Pallas kernels, project_out(): pl.pallas_call(functools.partial(output_kernel, order, rows, first, prior...  11.8 us
    pallas_call x1, Pallas kernels, attend(): pl.pallas_call(functools.partial(attend_kernel, parts), out_shape=(out, o...  8.05 us
    ppermute x6, waiting for transfers between devices, swap(): return lax.ppermute(array, 'gy', [(0, 1), (1, 0)])  4.5 us
  transfers between devices with their start and end apart: 21, of which 13 were waited for; matrix products, arithmetic and copies ran while one was open for 2% of the time, Pallas kernels for 19%

profile of v4, /device:TPU:0, one launch (start us, length us, event | category | flops | bytes accessed | tf_op | source)
XLA Modules:
  0.0 91.8 jit_solution(9113925099696777177)
XLA Ops:
  0.5 1.0 %broadcast_select_fusion.own_ref = bf16[64,2304]{1,0:T(8,128)(2,1)S(1)} fusion(bf16[64,2304]{1,0:T(8,128)(2,1)} %param.7, pred[]{:T(512)S(6)} %lt.6), kind=kLoop, calls=%fused_computation.1 | loop fusion | flops 147456 | bytes 589825 | tf_op jit(solution)/shard_map/jit(_where)/select_n | solution.py:296
  1.9 5.5 %project.5 = (f32[64,1024]{1,0:T(8,128)S(1)}, f32[64,1024]{1,0:T(8,128)S(1)}) custom-call(s32[2]{0:T(128)S(1)} %pad_add_fusion.ids_ref, bf16[64,2304]{1,0:T(8,128)(2,1)S(1)} %broadcast_select_fusion.own_ref, bf16[64,2304]{1,0:T(8,128)(2,1)S(1)} %collective-permute-done.other_ref, bf16[2304,3072]{1,0:T(8,128)(2,1)} %w_ref.5), custom_call_target="tpu_custom_call" | custom-call | flops 603979776 | bytes 5242880 | tf_op jit(solution)/shard_map/project/pallas_call | solution.py:108
  7.4 3.0 %collective-permute-start.7 = (f32[64,1024]{1,0:T(8,128)S(1)}, f32[64,1024]{1,0:T(8,128)S(1)}, u32[]{:S(2)}, u32[]{:S(2)}) collective-permute-start(f32[64,1024]{1,0:T(8,128)S(1)} %get-tuple-element.22), channel_id=1, source_target_pairs={{0,4},{2,6},{4,0},{6,2},{8,12},{10,14},{12,8},{14,10},{1,5},{3,7},... | collective-permute-start | bytes 786440 | tf_op jit(solution)/shard_map/ppermute | solution.py:293
  10.4 5.9 %project.4 = (f32[64,1280]{1,0:T(8,128)S(1)}, f32[64,1280]{1,0:T(8,128)S(1)}) custom-call(s32[2]{0:T(128)S(1)} %pad_add_fusion.ids_ref, bf16[64,2304]{1,0:T(8,128)(2,1)S(1)} %broadcast_select_fusion.own_ref, bf16[64,2304]{1,0:T(8,128)(2,1)S(1)} %collective-permute-done.other_ref, bf16[2304,3072]{1,0:T(8,128)(2,1)} %w_ref.5), custom_call_target="tpu_custom_call" | custom-call | flops 754974720 | bytes 6553600 | tf_op jit(solution)/shard_map/project/pallas_call | solution.py:108
  16.3 1.6 %collective-permute-start.4 = (f32[64,1280]{1,0:T(8,128)S(1)}, f32[64,1280]{1,0:T(8,128)S(1)}, u32[]{:S(2)}, u32[]{:S(2)}) collective-permute-start(f32[64,1280]{1,0:T(8,128)S(1)} %get-tuple-element.20), channel_id=1, source_target_pairs={{0,2},{2,0},{4,6},{6,4},{8,10},{10,8},{12,14},{14,12},{1,3},{3,1},... | collective-permute-start | bytes 983048 | tf_op jit(solution)/shard_map/ppermute | solution.py:293
  17.9 5.3 %project.3 = (f32[64,1024]{1,0:T(8,128)S(1)}, f32[64,1024]{1,0:T(8,128)S(1)}) custom-call(s32[2]{0:T(128)S(1)} %pad_add_fusion.ids_ref, bf16[64,2304]{1,0:T(8,128)(2,1)S(1)} %broadcast_select_fusion.own_ref, bf16[64,2304]{1,0:T(8,128)(2,1)S(1)} %collective-permute-done.other_ref, bf16[2304,3072]{1,0:T(8,128)(2,1)} %w_ref.5, bf16[2304,512]{1,0:T(8,128)(2,1)S(1)} %copy-done), custom_call_target="tpu_custom_call" | custom-call | flops 603979776 | bytes 5242880 | tf_op jit(solution)/shard_map/project/pallas_call | solution.py:108
  23.3 0.6 collective-permute-start.1
  23.9 2.7 %collective-permute-start.8 = (f32[32,1024]{1,0:T(8,128)S(1)}, f32[32,1024]{1,0:T(8,128)S(1)}, u32[]{:S(2)}, u32[]{:S(2)}) collective-permute-start(f32[32,1024]{1,0:T(8,128)S(1)} %slice.65), channel_id=1, source_target_pairs={{0,8},{2,10},{4,12},{6,14},{8,0},{10,2},{12,4},{14,6},{1,9},{3,11}... | collective-permute-start | bytes 393224 | tf_op jit(solution)/shard_map/ppermute | solution.py:293
  26.5 5.0 %collective-permute-done.1 = f32[64,1024]{1,0:T(8,128)S(1)} collective-permute-done((f32[64,1024]{1,0:T(8,128)S(1)}, f32[64,1024]{1,0:T(8,128)S(1)}, u32[]{:S(2)}, u32[]{:S(2)}) %collective-permute-start.1) | collective-permute-done | bytes 262176 | tf_op jit(solution)/shard_map/ppermute | solution.py:293
  32.0 1.8 %collective-permute-start.5 = (f32[32,1280]{1,0:T(8,128)S(1)}, f32[32,1280]{1,0:T(8,128)S(1)}, u32[]{:S(2)}, u32[]{:S(2)}) collective-permute-start(f32[32,1280]{1,0:T(8,128)S(1)} %slice.61), channel_id=1, source_target_pairs={{0,4},{2,6},{4,0},{6,2},{8,12},{10,14},{12,8},{14,10},{1,5},{3,7},... | collective-permute-start | bytes 491528 | tf_op jit(solution)/shard_map/ppermute | solution.py:293
  33.8 1.6 %collective-permute-start.9 = (f32[16,1024]{1,0:T(8,128)S(1)}, f32[16,1024]{1,0:T(8,128)S(1)}, u32[]{:S(2)}, u32[]{:S(2)}) collective-permute-start(f32[16,1024]{1,0:T(8,128)S(1)} %slice.67), channel_id=1, source_target_pairs={{0,2},{2,0},{4,6},{6,4},{8,10},{10,8},{12,14},{14,12},{1,3},{3,1},... | collective-permute-start | bytes 196616 | tf_op jit(solution)/shard_map/ppermute | solution.py:293
  35.4 2.4 %collective-permute-done.2 = f32[32,1024]{1,0:T(8,128)S(1)} collective-permute-done((f32[32,1024]{1,0:T(8,128)S(1)}, f32[32,1024]{1,0:T(8,128)S(1)}, u32[]{:S(2)}, u32[]{:S(2)}) %collective-permute-start.2) | collective-permute-done | bytes 131104 | tf_op jit(solution)/shard_map/ppermute | solution.py:293
  37.9 2.9 %collective-permute-start.3 = (f32[16,1024]{1,0:T(8,128)S(1)}, f32[16,1024]{1,0:T(8,128)S(1)}, u32[]{:S(2)}, u32[]{:S(2)}) collective-permute-start(f32[16,1024]{1,0:T(8,128)S(1)} %slice.59), channel_id=1, source_target_pairs={{0,8},{2,10},{4,12},{6,14},{8,0},{10,2},{12,4},{14,6},{1,9},{3,11}... | collective-permute-start | bytes 196616 | tf_op jit(solution)/shard_map/ppermute | solution.py:293
  40.9 2.9 %collective-permute-done.3 = f32[16,1024]{1,0:T(8,128)S(1)} collective-permute-done((f32[16,1024]{1,0:T(8,128)S(1)}, f32[16,1024]{1,0:T(8,128)S(1)}, u32[]{:S(2)}, u32[]{:S(2)}) %collective-permute-start.3) | collective-permute-done | bytes 65568 | tf_op jit(solution)/shard_map/ppermute | solution.py:293
  43.8 3.0 %collective-permute-start.6 = (f32[16,1280]{1,0:T(8,128)S(1)}, f32[16,1280]{1,0:T(8,128)S(1)}, u32[]{:S(2)}, u32[]{:S(2)}) collective-permute-start(f32[16,1280]{1,0:T(8,128)S(1)} %slice.63), channel_id=1, source_target_pairs={{0,8},{2,10},{4,12},{6,14},{8,0},{10,2},{12,4},{14,6},{1,9},{3,11}... | collective-permute-start | bytes 245768 | tf_op jit(solution)/shard_map/ppermute | solution.py:293
  46.8 2.9 %collective-permute-done.6 = f32[16,1280]{1,0:T(8,128)S(1)} collective-permute-done((f32[16,1280]{1,0:T(8,128)S(1)}, f32[16,1280]{1,0:T(8,128)S(1)}, u32[]{:S(2)}, u32[]{:S(2)}) %collective-permute-start.6) | collective-permute-done | bytes 81952 | tf_op jit(solution)/shard_map/ppermute | solution.py:293
  49.8 1.1 %collective-permute-done.11.refs_4_ = bf16[8,1280]{1,0:T(8,128)(2,1)S(1)} collective-permute-done((bf16[8,1280]{1,0:T(8,128)(2,1)S(1)}, bf16[8,1280]{1,0:T(8,128)(2,1)S(1)}, u32[]{:S(2)}, u32[]{:S(2)}) %collective-permute-start.11) | collective-permute-done | bytes 20512 | tf_op jit(solution)/shard_map/ppermute | solution.py:290
  50.9 8.0 %attend.1 = (bf16[8,3072]{1,0:T(8,128)(2,1)S(1)}, bf16[8,3072]{1,0:T(8,128)(2,1)S(1)}) custom-call(s32[9]{0:T(128)S(1)} %pad_add_fusion.1.scalars_ref, bf16[8,1024]{1,0:T(8,128)(2,1)S(1)} %get-tuple-element.36.refs_0_, bf16[8,1280]{1,0:T(8,128)(2,1)S(1)} %get-tuple-element.32.refs_1_, bf16[8,1024]{1,0:T(8,128)(2,1)S(1)} %get-tuple-element.34.refs_2_, ...), custom_call_target="tpu_custom_call" | custom-call | flops 201326592 | bytes 8388608 | tf_op jit(solution)/shard_map/attend/pallas_call | solution.py:185
  59.2 1.1 %collective-permute-done.13 = bf16[8,3072]{1,0:T(8,128)(2,1)S(1)} collective-permute-done((bf16[8,3072]{1,0:T(8,128)(2,1)S(1)}, bf16[8,3072]{1,0:T(8,128)(2,1)S(1)}, u32[]{:S(2)}, u32[]{:S(2)}) %collective-permute-start.13) | collective-permute-done | bytes 49184 | tf_op jit(solution)/shard_map/ppermute | solution.py:290
  60.3 2.5 %collective-permute-start.17 = (bf16[16,1536]{1,0:T(8,128)(2,1)S(1)}, bf16[16,1536]{1,0:T(8,128)(2,1)S(1)}, u32[]{:S(2)}, u32[]{:S(2)}) collective-permute-start(bf16[16,1536]{1,0:T(8,128)(2,1)S(1)} %get-tuple-element.29), channel_id=1, source_target_pairs={{0,8},{2,10},{4,12},{6,14},{8,0},{10,2},{12,4},{14,6},{1,9},{3,11}... | collective-permute-start | bytes 147464 | tf_op jit(solution)/shard_map/ppermute | solution.py:293
  62.9 1.5 %collective-permute-start.14 = (bf16[16,1536]{1,0:T(8,128)(2,1)S(1)}, bf16[16,1536]{1,0:T(8,128)(2,1)S(1)}, u32[]{:S(2)}, u32[]{:S(2)}) collective-permute-start(bf16[16,1536]{1,0:T(8,128)(2,1)S(1)} %get-tuple-element.30), channel_id=1, source_target_pairs={{0,2},{2,0},{4,6},{6,4},{8,10},{10,8},{12,14},{14,12},{1,3},{3,1},... | collective-permute-start | bytes 147464 | tf_op jit(solution)/shard_map/ppermute | solution.py:293
  64.4 1.2 %collective-permute-done.17 = bf16[16,1536]{1,0:T(8,128)(2,1)S(1)} collective-permute-done((bf16[16,1536]{1,0:T(8,128)(2,1)S(1)}, bf16[16,1536]{1,0:T(8,128)(2,1)S(1)}, u32[]{:S(2)}, u32[]{:S(2)}) %collective-permute-start.17) | collective-permute-done | bytes 49184 | tf_op jit(solution)/shard_map/ppermute | solution.py:293
  65.7 1.3 %collective-permute-done.14 = bf16[16,1536]{1,0:T(8,128)(2,1)S(1)} collective-permute-done((bf16[16,1536]{1,0:T(8,128)(2,1)S(1)}, bf16[16,1536]{1,0:T(8,128)(2,1)S(1)}, u32[]{:S(2)}, u32[]{:S(2)}) %collective-permute-start.14) | collective-permute-done | bytes 49184 | tf_op jit(solution)/shard_map/ppermute | solution.py:293
  67.0 1.2 %collective-permute-start.15 = (bf16[32,1536]{1,0:T(8,128)(2,1)S(1)}, bf16[32,1536]{1,0:T(8,128)(2,1)S(1)}, u32[]{:S(2)}, u32[]{:S(2)}) collective-permute-start(bf16[32,1536]{1,0:T(8,128)(2,1)S(1)} %pad_maximum_fusion.2), channel_id=1, source_target_pairs={{0,8},{2,10},{4,12},{6,14},{8,0},{10,2},{12,4},{14,6},{1,9},{3,11}... | collective-permute-start | bytes 294920 | tf_op jit(solution)/shard_map/ppermute | solution.py:293
  68.1 3.2 %collective-permute-done.18 = bf16[32,1536]{1,0:T(8,128)(2,1)S(1)} collective-permute-done((bf16[32,1536]{1,0:T(8,128)(2,1)S(1)}, bf16[32,1536]{1,0:T(8,128)(2,1)S(1)}, u32[]{:S(2)}, u32[]{:S(2)}) %collective-permute-start.18) | collective-permute-done | bytes 98336 | tf_op jit(solution)/shard_map/ppermute | solution.py:293
  71.4 1.5 %collective-permute-start.19 = (bf16[64,1536]{1,0:T(8,128)(2,1)S(1)}, bf16[64,1536]{1,0:T(8,128)(2,1)S(1)}, u32[]{:S(2)}, u32[]{:S(2)}) collective-permute-start(bf16[64,1536]{1,0:T(8,128)(2,1)S(1)} %pad_maximum_fusion.1.near_ref), channel_id=1, source_target_pairs={{0,2},{2,0},{4,6},{6,4},{8,10},{10,8},{12,14},{14,12},{1,3},{3,1},... | collective-permute-start | bytes 589832 | tf_op jit(solution)/shard_map/ppermute | solution.py:293
  72.9 0.9 %collective-permute-done.15 = bf16[32,1536]{1,0:T(8,128)(2,1)S(1)} collective-permute-done((bf16[32,1536]{1,0:T(8,128)(2,1)S(1)}, bf16[32,1536]{1,0:T(8,128)(2,1)S(1)}, u32[]{:S(2)}, u32[]{:S(2)}) %collective-permute-start.15) | collective-permute-done | bytes 98336 | tf_op jit(solution)/shard_map/ppermute | solution.py:293
  74.1 3.0 %collective-permute-done.19.far_ref = bf16[64,1536]{1,0:T(8,128)(2,1)S(1)} collective-permute-done((bf16[64,1536]{1,0:T(8,128)(2,1)S(1)}, bf16[64,1536]{1,0:T(8,128)(2,1)S(1)}, u32[]{:S(2)}, u32[]{:S(2)}) %collective-permute-start.19) | collective-permute-done | bytes 196640 | tf_op jit(solution)/shard_map/ppermute | solution.py:293
  77.1 5.9 %project_out.2 = (f32[64,2304]{1,0:T(8,128)S(1)}, f32[64,2304]{1,0:T(8,128)S(1)}) custom-call(s32[2]{0:T(128)S(1)} %pad_add_fusion.ids_ref, bf16[64,1536]{1,0:T(8,128)(2,1)S(1)} %pad_maximum_fusion.1.near_ref, bf16[64,1536]{1,0:T(8,128)(2,1)S(1)} %collective-permute-done.19.far_ref, bf16[3072,2304]{1,0:T(8,128)(2,1)} %w_hbm.3), custom_call_target="tpu_custom_call" | custom-call | flops 905969664 | bytes 8257536 | tf_op jit(solution)/shard_map/project_out/pallas_call | solution.py:259
  83.0 5.9 %project_out.3 = (f32[64,2304]{1,0:T(8,128)S(1)}, f32[64,2304]{1,0:T(8,128)S(1)}) custom-call(s32[2]{0:T(128)S(1)} %pad_add_fusion.ids_ref, bf16[64,1536]{1,0:T(8,128)(2,1)S(1)} %pad_maximum_fusion.near_ref, bf16[64,1536]{1,0:T(8,128)(2,1)S(1)} %collective-permute-done.16.far_ref, bf16[3072,2304]{1,0:T(8,128)(2,1)} %w_hbm.3, ...), custom_call_target="tpu_custom_call" | custom-call | flops 905969664 | bytes 8257536 | tf_op jit(solution)/shard_map/project_out/pallas_call | solution.py:259
  89.0 2.0 %collective-permute-done.20 = f32[64,2304]{1,0:T(8,128)S(1)} collective-permute-done((f32[64,2304]{1,0:T(8,128)S(1)}, f32[64,2304]{1,0:T(8,128)S(1)}, u32[]{:S(2)}, u32[]{:S(2)}) %collective-permute-start.20) | collective-permute-done | bytes 589856 | tf_op jit(solution)/shard_map/ppermute | solution.py:290
  91.0 0.8 add_convert_fusion
  (48 shorter events, 2.6 us)
Async XLA Ops:
  0.0 1.9 %collective-permute-start = (bf16[64,2304]{1,0:T(8,128)(2,1)}, bf16[64,2304]{1,0:T(8,128)(2,1)S(1)}, u32[]{:S(2)}, u32[]{:S(2)}) collective-permute-start(bf16[64,2304]{1,0:T(8,128)(2,1)} %param.7), channel_id=1, source_target_pairs={{0,1},{1,0},{2,3},{3,2},{4,5},{5,4},{6,7},{7,6},{8,9},{9,8},{10,11... | collective-permute-start | bytes 884744 | tf_op jit(solution)/shard_map/ppermute | solution.py:290
  7.4 10.6 %copy-start = (bf16[2304,512]{1,0:T(8,128)(2,1)S(1)}, bf16[2304,512]{1,0:T(8,128)(2,1)}, u32[]{:S(2)}) copy-start(bf16[2304,512]{1,0:T(8,128)(2,1)} %refs_0_.1) | copy-start | bytes 7077892
  7.4 16.4 %collective-permute-start.7 = (f32[64,1024]{1,0:T(8,128)S(1)}, f32[64,1024]{1,0:T(8,128)S(1)}, u32[]{:S(2)}, u32[]{:S(2)}) collective-permute-start(f32[64,1024]{1,0:T(8,128)S(1)} %get-tuple-element.22), channel_id=1, source_target_pairs={{0,4},{2,6},{4,0},{6,2},{8,12},{10,14},{12,8},{14,10},{1,5},{3,7},... | collective-permute-start | bytes 786440 | tf_op jit(solution)/shard_map/ppermute | solution.py:293
  16.3 15.6 %collective-permute-start.4 = (f32[64,1280]{1,0:T(8,128)S(1)}, f32[64,1280]{1,0:T(8,128)S(1)}, u32[]{:S(2)}, u32[]{:S(2)}) collective-permute-start(f32[64,1280]{1,0:T(8,128)S(1)} %get-tuple-element.20), channel_id=1, source_target_pairs={{0,2},{2,0},{4,6},{6,4},{8,10},{10,8},{12,14},{14,12},{1,3},{3,1},... | collective-permute-start | bytes 983048 | tf_op jit(solution)/shard_map/ppermute | solution.py:293
  23.2 26.5 %copy-start.1 = (s32[8]{0:T(128)S(1)}, s32[8]{0:T(128)}, u32[]{:S(2)}) copy-start(s32[8]{0:T(128)} %param.13) | copy-start | bytes 100
  23.3 8.2 %collective-permute-start.1 = (f32[64,1024]{1,0:T(8,128)S(1)}, f32[64,1024]{1,0:T(8,128)S(1)}, u32[]{:S(2)}, u32[]{:S(2)}) collective-permute-start(f32[64,1024]{1,0:T(8,128)S(1)} %get-tuple-element.18), channel_id=1, source_target_pairs={{0,2},{2,0},{4,6},{6,4},{8,10},{10,8},{12,14},{14,12},{1,3},{3,1},... | collective-permute-start | bytes 786440 | tf_op jit(solution)/shard_map/ppermute | solution.py:293
  23.9 9.9 %collective-permute-start.8 = (f32[32,1024]{1,0:T(8,128)S(1)}, f32[32,1024]{1,0:T(8,128)S(1)}, u32[]{:S(2)}, u32[]{:S(2)}) collective-permute-start(f32[32,1024]{1,0:T(8,128)S(1)} %slice.65), channel_id=1, source_target_pairs={{0,8},{2,10},{4,12},{6,14},{8,0},{10,2},{12,4},{14,6},{1,9},{3,11}... | collective-permute-start | bytes 393224 | tf_op jit(solution)/shard_map/ppermute | solution.py:293
  31.6 6.3 %collective-permute-start.2 = (f32[32,1024]{1,0:T(8,128)S(1)}, f32[32,1024]{1,0:T(8,128)S(1)}, u32[]{:S(2)}, u32[]{:S(2)}) collective-permute-start(f32[32,1024]{1,0:T(8,128)S(1)} %slice.57), channel_id=1, source_target_pairs={{0,4},{2,6},{4,0},{6,2},{8,12},{10,14},{12,8},{14,10},{1,5},{3,7},... | collective-permute-start | bytes 393224 | tf_op jit(solution)/shard_map/ppermute | solution.py:293
  32.0 11.8 %collective-permute-start.5 = (f32[32,1280]{1,0:T(8,128)S(1)}, f32[32,1280]{1,0:T(8,128)S(1)}, u32[]{:S(2)}, u32[]{:S(2)}) collective-permute-start(f32[32,1280]{1,0:T(8,128)S(1)} %slice.61), channel_id=1, source_target_pairs={{0,4},{2,6},{4,0},{6,2},{8,12},{10,14},{12,8},{14,10},{1,5},{3,7},... | collective-permute-start | bytes 491528 | tf_op jit(solution)/shard_map/ppermute | solution.py:293
  33.8 6.9 %collective-permute-start.9 = (f32[16,1024]{1,0:T(8,128)S(1)}, f32[16,1024]{1,0:T(8,128)S(1)}, u32[]{:S(2)}, u32[]{:S(2)}) collective-permute-start(f32[16,1024]{1,0:T(8,128)S(1)} %slice.67), channel_id=1, source_target_pairs={{0,2},{2,0},{4,6},{6,4},{8,10},{10,8},{12,14},{14,12},{1,3},{3,1},... | collective-permute-start | bytes 196616 | tf_op jit(solution)/shard_map/ppermute | solution.py:293
  37.9 5.8 %collective-permute-start.3 = (f32[16,1024]{1,0:T(8,128)S(1)}, f32[16,1024]{1,0:T(8,128)S(1)}, u32[]{:S(2)}, u32[]{:S(2)}) collective-permute-start(f32[16,1024]{1,0:T(8,128)S(1)} %slice.59), channel_id=1, source_target_pairs={{0,8},{2,10},{4,12},{6,14},{8,0},{10,2},{12,4},{14,6},{1,9},{3,11}... | collective-permute-start | bytes 196616 | tf_op jit(solution)/shard_map/ppermute | solution.py:293
  40.8 9.1 %collective-permute-start.12 = (bf16[8,1024]{1,0:T(8,128)(2,1)S(1)}, bf16[8,1024]{1,0:T(8,128)(2,1)S(1)}, u32[]{:S(2)}, u32[]{:S(2)}) collective-permute-start(bf16[8,1024]{1,0:T(8,128)(2,1)S(1)} %get-tuple-element.33), channel_id=1, source_target_pairs={{0,1},{1,0},{2,3},{3,2},{4,5},{5,4},{6,7},{7,6},{8,9},{9,8},{10,11... | collective-permute-start | bytes 49160 | tf_op jit(solution)/shard_map/ppermute | solution.py:290
  43.8 5.9 %collective-permute-start.6 = (f32[16,1280]{1,0:T(8,128)S(1)}, f32[16,1280]{1,0:T(8,128)S(1)}, u32[]{:S(2)}, u32[]{:S(2)}) collective-permute-start(f32[16,1280]{1,0:T(8,128)S(1)} %slice.63), channel_id=1, source_target_pairs={{0,8},{2,10},{4,12},{6,14},{8,0},{10,2},{12,4},{14,6},{1,9},{3,11}... | collective-permute-start | bytes 245768 | tf_op jit(solution)/shard_map/ppermute | solution.py:293
  46.8 3.1 %collective-permute-start.10 = (bf16[8,1024]{1,0:T(8,128)(2,1)S(1)}, bf16[8,1024]{1,0:T(8,128)(2,1)S(1)}, u32[]{:S(2)}, u32[]{:S(2)}) collective-permute-start(bf16[8,1024]{1,0:T(8,128)(2,1)S(1)} %get-tuple-element.35), channel_id=1, source_target_pairs={{0,1},{1,0},{2,3},{3,2},{4,5},{5,4},{6,7},{7,6},{8,9},{9,8},{10,11... | collective-permute-start | bytes 49160 | tf_op jit(solution)/shard_map/ppermute | solution.py:290
  49.7 1.3 %collective-permute-start.11 = (bf16[8,1280]{1,0:T(8,128)(2,1)S(1)}, bf16[8,1280]{1,0:T(8,128)(2,1)S(1)}, u32[]{:S(2)}, u32[]{:S(2)}) collective-permute-start(bf16[8,1280]{1,0:T(8,128)(2,1)S(1)} %get-tuple-element.31), channel_id=1, source_target_pairs={{0,1},{1,0},{2,3},{3,2},{4,5},{5,4},{6,7},{7,6},{8,9},{9,8},{10,11... | collective-permute-start | bytes 61448 | tf_op jit(solution)/shard_map/ppermute | solution.py:290
  59.0 1.3 %collective-permute-start.13 = (bf16[8,3072]{1,0:T(8,128)(2,1)S(1)}, bf16[8,3072]{1,0:T(8,128)(2,1)S(1)}, u32[]{:S(2)}, u32[]{:S(2)}) collective-permute-start(bf16[8,3072]{1,0:T(8,128)(2,1)S(1)} %get-tuple-element.24), channel_id=1, source_target_pairs={{0,1},{1,0},{2,3},{3,2},{4,5},{5,4},{6,7},{7,6},{8,9},{9,8},{10,11... | collective-permute-start | bytes 147464 | tf_op jit(solution)/shard_map/ppermute | solution.py:290
  60.3 5.3 %collective-permute-start.17 = (bf16[16,1536]{1,0:T(8,128)(2,1)S(1)}, bf16[16,1536]{1,0:T(8,128)(2,1)S(1)}, u32[]{:S(2)}, u32[]{:S(2)}) collective-permute-start(bf16[16,1536]{1,0:T(8,128)(2,1)S(1)} %get-tuple-element.29), channel_id=1, source_target_pairs={{0,8},{2,10},{4,12},{6,14},{8,0},{10,2},{12,4},{14,6},{1,9},{3,11}... | collective-permute-start | bytes 147464 | tf_op jit(solution)/shard_map/ppermute | solution.py:293
  62.9 4.1 %collective-permute-start.14 = (bf16[16,1536]{1,0:T(8,128)(2,1)S(1)}, bf16[16,1536]{1,0:T(8,128)(2,1)S(1)}, u32[]{:S(2)}, u32[]{:S(2)}) collective-permute-start(bf16[16,1536]{1,0:T(8,128)(2,1)S(1)} %get-tuple-element.30), channel_id=1, source_target_pairs={{0,2},{2,0},{4,6},{6,4},{8,10},{10,8},{12,14},{14,12},{1,3},{3,1},... | collective-permute-start | bytes 147464 | tf_op jit(solution)/shard_map/ppermute | solution.py:293
  65.6 5.7 %collective-permute-start.18 = (bf16[32,1536]{1,0:T(8,128)(2,1)S(1)}, bf16[32,1536]{1,0:T(8,128)(2,1)S(1)}, u32[]{:S(2)}, u32[]{:S(2)}) collective-permute-start(bf16[32,1536]{1,0:T(8,128)(2,1)S(1)} %pad_maximum_fusion.3), channel_id=1, source_target_pairs={{0,4},{2,6},{4,0},{6,2},{8,12},{10,14},{12,8},{14,10},{1,5},{3,7},... | collective-permute-start | bytes 294920 | tf_op jit(solution)/shard_map/ppermute | solution.py:293
  67.0 6.8 %collective-permute-start.15 = (bf16[32,1536]{1,0:T(8,128)(2,1)S(1)}, bf16[32,1536]{1,0:T(8,128)(2,1)S(1)}, u32[]{:S(2)}, u32[]{:S(2)}) collective-permute-start(bf16[32,1536]{1,0:T(8,128)(2,1)S(1)} %pad_maximum_fusion.2), channel_id=1, source_target_pairs={{0,8},{2,10},{4,12},{6,14},{8,0},{10,2},{12,4},{14,6},{1,9},{3,11}... | collective-permute-start | bytes 294920 | tf_op jit(solution)/shard_map/ppermute | solution.py:293
  71.4 5.7 %collective-permute-start.19 = (bf16[64,1536]{1,0:T(8,128)(2,1)S(1)}, bf16[64,1536]{1,0:T(8,128)(2,1)S(1)}, u32[]{:S(2)}, u32[]{:S(2)}) collective-permute-start(bf16[64,1536]{1,0:T(8,128)(2,1)S(1)} %pad_maximum_fusion.1.near_ref), channel_id=1, source_target_pairs={{0,2},{2,0},{4,6},{6,4},{8,10},{10,8},{12,14},{14,12},{1,3},{3,1},... | collective-permute-start | bytes 589832 | tf_op jit(solution)/shard_map/ppermute | solution.py:293
  73.8 9.2 %collective-permute-start.16 = (bf16[64,1536]{1,0:T(8,128)(2,1)S(1)}, bf16[64,1536]{1,0:T(8,128)(2,1)S(1)}, u32[]{:S(2)}, u32[]{:S(2)}) collective-permute-start(bf16[64,1536]{1,0:T(8,128)(2,1)S(1)} %pad_maximum_fusion.near_ref), channel_id=1, source_target_pairs={{0,4},{2,6},{4,0},{6,2},{8,12},{10,14},{12,8},{14,10},{1,5},{3,7},... | collective-permute-start | bytes 589832 | tf_op jit(solution)/shard_map/ppermute | solution.py:293
  88.9 2.1 %collective-permute-start.20 = (f32[64,2304]{1,0:T(8,128)S(1)}, f32[64,2304]{1,0:T(8,128)S(1)}, u32[]{:S(2)}, u32[]{:S(2)}) collective-permute-start(f32[64,2304]{1,0:T(8,128)S(1)} %get-tuple-element.28), channel_id=1, source_target_pairs={{0,1},{1,0},{2,3},{3,2},{4,5},{5,4},{6,7},{7,6},{8,9},{9,8},{10,11... | collective-permute-start | bytes 1769480 | tf_op jit(solution)/shard_map/ppermute | solution.py:290

commit v5 on v4

--- a/solution.py
+++ b/solution.py
@@ -16,10 +16,6 @@
 SMEM = pl.BlockSpec(memory_space=pltpu.SMEM)
 
 
-def slabs_of(depth):
-    return depth // 256 if depth % 256 == 0 else 1
-
-
 class InOrder:
     def __init__(self, copies, ahead):
         self.copies, self.ahead = copies, ahead
@@ -39,82 +35,108 @@
     return order
 
 
-def project_kernel(order, rows, first, kv_width, after, ids_ref, own_ref, other_ref, w_ref, *refs):
+def spans_of(width):
+    return [(at, min(512, width - at)) for at in range(0, width, 512)]
+
+
+def project_kernel(orders, rows, first, widths, kv_width, ids_ref, own_ref, other_ref, w_ref, *refs):
     refs = list(refs)
     kv_ref = refs.pop(0) if kv_width else None
-    send_ref, keep_ref, xs_ref, ws_ref, row_sem, w_sem = refs[after:]
-    n = len(order)
-    slabs, slab, columns = ws_ref.shape
+    outs, (xs_ref, ws_ref, row_sem, w_sem) = refs[:-4], refs[-4:]
+    n = len(orders[0])
+    half = n // 2
     me, core = ids_ref[0], ids_ref[1]
-    half = n // 2
-
-    def row_copy(source_ref, p):
-        block = jnp.bitwise_xor(me, order[p])
+    features = xs_ref.shape[2]
+
+    def row_copy(source_ref, chunk, p):
+        block = jnp.bitwise_xor(me, orders[chunk][p])
         source = pl.ds(pl.multiple_of((block % half) * rows, rows), rows)
         return pltpu.make_async_copy(
-            source_ref.at[source, :], xs_ref.at[pl.ds(p * rows, rows), :], row_sem.at[p]
+            source_ref.at[source, :],
+            xs_ref.at[chunk, pl.ds(p * rows, rows), :],
+            row_sem.at[chunk, p],
         )
 
-    for p in range(n):
-        mine = jnp.bitwise_xor(me, order[p]) // half == core
-
-        @pl.when(mine)
-        def _():
-            row_copy(own_ref, p).start()
-
-        @pl.when(jnp.logical_not(mine))
-        def _():
-            row_copy(other_ref, p).start()
-
-    copies = []
-    per_slab = 1
-    for k in range(slabs):
-        span = pl.ds(k * slab, slab)
-        if kv_width:
-            per_slab = 2
-            own = pl.ds(pl.multiple_of(core * kv_width, kv_width), kv_width)
-            target = ws_ref.at[k, :, pl.ds(0, kv_width)]
-            copies.append(pltpu.make_async_copy(kv_ref.at[span, own], target, w_sem.at[1, k]))
-        width = columns - kv_width
-        target = ws_ref.at[k, :, pl.ds(kv_width, width)]
-        copies.append(pltpu.make_async_copy(w_ref.at[span, pl.ds(first, width)], target, w_sem.at[0, k]))
-    weights = InOrder(copies, 3 * per_slab)
-    for p in range(n):
-        row_copy(own_ref, p).wait()
-    cut = n * rows // 2
-    for k in range(slabs):
-        for at in range(per_slab):
-            weights.wait(k * per_slab + at)
-        part = jnp.dot(
-            xs_ref[:, k * slab : (k + 1) * slab], ws_ref[k], preferred_element_type=jnp.float32
+    for chunk, order in enumerate(orders):
+        for p in range(n):
+            mine = jnp.bitwise_xor(me, order[p]) // half == core
+
+            @pl.when(mine)
+            def _():
+                row_copy(own_ref, chunk, p).start()
+
+            @pl.when(jnp.logical_not(mine))
+            def _():
+                row_copy(other_ref, chunk, p).start()
+
+    tiles, copies, at, source = [], [], 0, first
+    depth = features // 2 if features % 32 == 0 else features
+
+    def fetch(from_ref, column, width):
+        for part in range(features // depth):
+            span = pl.ds(part * depth, depth)
+            copies.append(
+                pltpu.make_async_copy(
+                    from_ref.at[span, pl.ds(column, width)],
+                    ws_ref.at[span, pl.ds(at, width)],
+                    w_sem.at[len(copies)],
+                )
+            )
+
+    for chunk, width in enumerate(widths):
+        column = 0
+        if kv_width and chunk == 0:
+            fetch(kv_ref, pl.multiple_of(core * kv_width, kv_width), kv_width)
+            tiles.append((chunk, 0, at, kv_width))
+            at += kv_width
+            column = kv_width
+        for offset, tile in spans_of(width):
+            fetch(w_ref, source, tile)
+            tiles.append((chunk, column + offset, at, tile))
+            at += tile
+            source += tile
+    per_tile = features // depth
+    weights = InOrder(copies, 3 * per_tile)
+    cut = half * rows
+    ready = set()
+    for t, (chunk, column, at, width) in enumerate(tiles):
+        if chunk not in ready:
+            ready.add(chunk)
+            for p in range(n):
+                row_copy(own_ref, chunk, p).wait()
+        for part in range(per_tile):
+            weights.wait(t * per_tile + part)
+        total = jnp.dot(
+            xs_ref[chunk], ws_ref[:, at : at + width], preferred_element_type=jnp.float32
         )
-        if k == 0:
-            keep_ref[...] = part[:cut]
-            send_ref[...] = part[cut:]
-        else:
-            keep_ref[...] += part[:cut]
-            send_ref[...] += part[cut:]
-
-
-def project(bits, rows, ids, tokens, other, query_weight, kv_weight, first, width, after):
+        span = slice(column, column + width)
+        outs[2 * chunk][:, span] = total[cut:]
+        outs[2 * chunk + 1][:, span] = total[:cut]
+
+
+def project(plan, rows, ids, tokens, other, query_weight, kv_weight, first):
     features = tokens.shape[1]
-    order = order_of(bits)
-    n = len(order)
-    slabs = slabs_of(features)
+    orders = [order_of(bits) for _, bits in plan]
+    widths = [width for width, _ in plan]
+    n = len(orders[0])
     kv_width = kv_weight.shape[1] // 2 if kv_weight is not None else 0
-    columns = width + kv_width
-    out = jax.ShapeDtypeStruct((n * rows // 2, columns), jnp.float32)
+    columns = sum(widths) + kv_width
+    outs = []
+    for chunk, width in enumerate(widths):
+        shape = (n * rows // 2, width + (0 if chunk else kv_width))
+        outs += [jax.ShapeDtypeStruct(shape, jnp.float32)] * 2
     weights = [query_weight] + ([kv_weight] if kv_width else [])
-    return pl.pallas_call(
-        functools.partial(project_kernel, order, rows, first, kv_width, len(after)),
-        out_shape=(out, out),
-        in_specs=[SMEM, ANY, ANY] + [HBM] * len(weights) + [ANY] * len(after),
-        out_specs=(VMEM, VMEM),
+    copies = 2 * (len(weights) - 1 + sum(len(spans_of(width)) for width in widths))
+    outs = pl.pallas_call(
+        functools.partial(project_kernel, orders, rows, first, widths, kv_width),
+        out_shape=outs,
+        in_specs=[SMEM, ANY, ANY] + [HBM] * len(weights),
+        out_specs=[VMEM] * len(outs),
         scratch_shapes=[
-            pltpu.VMEM((n * rows, features), tokens.dtype),
-            pltpu.VMEM((slabs, features // slabs, columns), tokens.dtype),
-            pltpu.SemaphoreType.DMA((n,)),
-            pltpu.SemaphoreType.DMA((2, slabs)),
+            pltpu.VMEM((len(orders), n * rows, features), tokens.dtype),
+            pltpu.VMEM((features, columns), tokens.dtype),
+            pltpu.SemaphoreType.DMA((len(orders), n)),
+            pltpu.SemaphoreType.DMA((copies,)),
         ],
         compiler_params=pltpu.CompilerParams(vmem_limit_bytes=46 * MIB),
         cost_estimate=pl.CostEstimate(
@@ -123,7 +145,8 @@
             transcendentals=0,
         ),
         name="project",
-    )(ids, tokens, other, *weights, *after)
+    )(ids, tokens, other, *weights)
+    return list(zip(outs[::2], outs[1::2]))
 
 
 def attend_kernel(parts, scalars_ref, *refs):
@@ -135,7 +158,7 @@
     for row in range(rows):
         copies.append(pltpu.make_async_copy(k_hbm.at[row], k_ref.at[row], sems.at[0, row]))
         copies.append(pltpu.make_async_copy(v_hbm.at[row], v_ref.at[row], sems.at[1, row]))
-    caches = InOrder(copies, 4)
+    caches = InOrder(copies, 8)
     at = 0
     for side in (own_q, other_q):
         for ref, (heads, skip) in zip(side, parts):
@@ -200,72 +223,65 @@
     )(scalars, *own_q, *other_q, keys, values)
 
 
-def output_kernel(order, rows, first, with_prior, ids_ref, near_ref, far_ref, w_hbm, *refs):
-    if with_prior:
-        send_in, keep_in, send_ref, keep_ref, xs_ref, ws_ref, row_sem, w_sem = refs
-    else:
-        send_ref, keep_ref, xs_ref, ws_ref, row_sem, w_sem = refs
+def output_kernel(order, rows, first, spans, ids_ref, *refs):
+    count = len(refs) - 7
+    block_refs = refs[:count]
+    w_hbm, send_ref, keep_ref, xs_ref, ws_ref, row_sem, w_sem = refs[count:]
+    depth = block_refs[0].shape[1]
+    copies = [
+        pltpu.make_async_copy(
+            w_hbm.at[:, pl.ds(first + at, width)], ws_ref.at[:, pl.ds(at, width)], w_sem.at[k]
+        )
+        for k, (at, width) in enumerate(spans)
+    ]
     me, core = ids_ref[0], ids_ref[1]
-    n = len(order)
+    n = len(order[0])
     half = n // 2
-    slabs, slab, _ = ws_ref.shape
     row_copies = []
-    for p, j in enumerate(order):
-        block = jnp.bitwise_xor(me, j)
-        place = block % half + jnp.where(block // half == core, half, 0)
-        source = near_ref if p < half else far_ref
-        row_copies.append(
-            pltpu.make_async_copy(
-                source.at[pl.ds((p % half) * rows, rows), :],
-                xs_ref.at[pl.ds(pl.multiple_of(place * rows, rows), rows), :],
-                row_sem.at[p],
+    for group, (near_ref, far_ref) in enumerate(zip(block_refs[::2], block_refs[1::2])):
+        for p, j in enumerate(order[group]):
+            block = jnp.bitwise_xor(me, j)
+            place = block % half + jnp.where(block // half == core, half, 0)
+            source = near_ref if p < half else far_ref
+            row_copies.append(
+                pltpu.make_async_copy(
+                    source.at[pl.ds((p % half) * rows, rows), :],
+                    xs_ref.at[
+                        pl.ds(pl.multiple_of(place * rows, rows), rows), pl.ds(group * depth, depth)
+                    ],
+                    row_sem.at[group, p],
+                )
             )
-        )
     for copy in row_copies:
         copy.start()
-    weights = InOrder(
-        [
-            pltpu.make_async_copy(w_hbm.at[pl.ds(first + k * slab, slab)], ws_ref.at[k], w_sem.at[k])
-            for k in range(slabs)
-        ],
-        2,
-    )
+    weights = InOrder(copies, 2)
     for copy in row_copies:
         copy.wait()
     cut = half * rows
-    for k in range(slabs):
+    for k, (at, width) in enumerate(spans):
         weights.wait(k)
-        part = jnp.dot(
-            xs_ref[:, k * slab : (k + 1) * slab], ws_ref[k], preferred_element_type=jnp.float32
-        )
-        if k:
-            send_ref[...] += part[:cut]
-            keep_ref[...] += part[cut:]
-        elif with_prior:
-            send_ref[...] = send_in[...] + part[:cut]
-            keep_ref[...] = keep_in[...] + part[cut:]
-        else:
-            send_ref[...] = part[:cut]
-            keep_ref[...] = part[cut:]
-
-
-def project_out(order, rows, ids, near, far, out_weight, first, prior):
-    depth = near.shape[1]
-    columns = out_weight.shape[1]
-    n = len(order)
-    slabs = slabs_of(depth)
+        span = slice(at, at + width)
+        total = jnp.dot(xs_ref[...], ws_ref[:, span], preferred_element_type=jnp.float32)
+        send_ref[:, span] = total[:cut]
+        keep_ref[:, span] = total[cut:]
+
+
+def project_out(orders, rows, ids, blocks, out_weight, first, columns):
+    depth = out_weight.shape[0]
+    n = len(orders[0])
+    tile = 384 if columns % 384 == 0 else columns
+    spans = [(at, tile) for at in range(0, columns, tile)]
     out = jax.ShapeDtypeStruct((n * rows // 2, columns), jnp.float32)
-    operands = [ids, near, far, out_weight] + ([] if prior is None else list(prior))
     return pl.pallas_call(
-        functools.partial(output_kernel, order, rows, first, prior is not None),
+        functools.partial(output_kernel, orders, rows, first, spans),
         out_shape=(out, out),
-        in_specs=[SMEM, ANY, ANY, HBM] + [VMEM] * (len(operands) - 4),
+        in_specs=[SMEM] + [ANY] * len(blocks) + [HBM],
         out_specs=(VMEM, VMEM),
         scratch_shapes=[
             pltpu.VMEM((n * rows, depth), jnp.bfloat16),
-            pltpu.VMEM((slabs, depth // slabs, columns), jnp.bfloat16),
-            pltpu.SemaphoreType.DMA((n,)),
-            pltpu.SemaphoreType.DMA((slabs,)),
+            pltpu.VMEM((depth, columns), jnp.bfloat16),
+            pltpu.SemaphoreType.DMA((len(orders), n)),
+            pltpu.SemaphoreType.DMA((len(spans),)),
         ],
         compiler_params=pltpu.CompilerParams(vmem_limit_bytes=46 * MIB),
         cost_estimate=pl.CostEstimate(
@@ -274,7 +290,7 @@
             transcendentals=0,
         ),
         name="project_out",
-    )(*operands)
+    )(ids, *blocks, out_weight)
 
 
 def local(tokens, query_weight, kv_weight, out_weight, key_cache, value_cache, lengths):
@@ -298,16 +314,14 @@
 
     y, z = bits[:1], bits[1:]
     unit = query_weight.shape[1] // 12
-    plan = [(3 * unit, y + z), (5 * unit, y + z), (4 * unit, z + y)]
-    state, moving, first, after = [], [], 0, []
-    for i, (columns, order) in enumerate(plan):
-        send, keep = project(
-            order, rows, ids, own_tokens, other_tokens, query_weight, None if i else kv_weight, first, columns, after
-        )
-        state.append((send, keep))
-        moving.append(across(send, order[0]))
-        first += columns
-        after = []
+    plan = [(3 * unit, y + z[::-1]), (5 * unit, z[:1] + y + z[1:]), (4 * unit, z[:1] + y + z[1:])]
+    state, first = [], 0
+    for group in (slice(0, 3),):
+        chunks = plan[group]
+        weight = None if state else kv_weight
+        state += project(chunks, rows, ids, own_tokens, other_tokens, query_weight, weight, first)
+        first += sum(columns for columns, _ in chunks)
+    moving = [across(send, order[0]) for (send, _), (_, order) in zip(state, plan)]
     for step in range(len(bits)):
         for i, (columns, order) in enumerate(plan):
             total = state[i][1] + moving[i]
@@ -337,11 +351,16 @@
             if step:
                 near[i] = jnp.concatenate([near[i], far[i]])
             far[i] = across(near[i], paths[i][step])
-    prior = None
-    for i in range(2):
-        prior = project_out(order_of(paths[i][::-1]), rows, ids, near[i], far[i], out_weight, i * width, prior)
-    send, keep = prior
-    return (keep + swap(send)).astype(jnp.bfloat16)
+    orders = [order_of(path[::-1]) for path in paths]
+    blocks = [b for pair in zip(near, far) for b in pair]
+    total_columns = out_weight.shape[1]
+    cuts = 2 if total_columns % 768 == 0 else 1
+    columns = total_columns // cuts
+    results = []
+    for cut in range(cuts):
+        send, keep = project_out(orders, rows, ids, blocks, out_weight, cut * columns, columns)
+        results.append((keep + swap(send)).astype(jnp.bfloat16))
+    return jnp.concatenate(results, axis=1)
 
 
 def solution(mesh):

time: 92.3 us -> 90.2 us (0.977)
  waiting for transfers between devices: 27.2 us -> 36.8 us
  Pallas kernels: 36.6 us -> 28.3 us
  starting transfers between devices: 25.5 us -> 20.8 us
  local copies, waits for them, and re-layouts: 0.1 us -> 1.76 us
    ppermute x15, waiting for transfers between devices: 22.7 us -> 33.1 us  [across(): return lax.ppermute(array, 'gx', [(g, g ^ mask) for g in range(n)])]
    pallas_call x5 -> x3, Pallas kernels: 28.5 us -> 20.3 us  [the longest x2 10.8 us: project_out(): pl.pallas_call(functools.partial(output_kernel, orders, rows, first, span...]
    ppermute x15, starting transfers between devices: 24.6 us -> 19.3 us  [across(): return lax.ppermute(array, 'gx', [(g, g ^ mask) for g in range(n)])]
    unnamed x4, local copies, waits for them, and re-layouts: 0.01 us -> 1.67 us
    ppermute x6 -> x7, waiting for transfers between devices: 4.5 us -> 3.68 us  [swap(): return lax.ppermute(array, 'gy', [(0, 1), (1, 0)])]
  transfers between devices with their start and end apart: 21 -> 22, of which waited for: 13 -> 15; matrix products, arithmetic and copies ran while one was open for 2% -> 2% of each run, Pallas kernels for 19% -> 6%
where the time goes in v5:
time: 90.2 us; the launch traced here: 90 us
  waiting for transfers between devices  36.8 us (41%)
  Pallas kernels  28.3 us (31%)
  starting transfers between devices  20.8 us (23%)
  other arithmetic  2.18 us (2%)
  local copies, waits for them, and re-layouts  1.76 us (2%)
    ppermute x15, waiting for transfers between devices, across(): return lax.ppermute(array, 'gx', [(g, g ^ mask) for g in range(n)])  33.1 us
    ppermute x15, starting transfers between devices, across(): return lax.ppermute(array, 'gx', [(g, g ^ mask) for g in range(n)])  19.3 us
    pallas_call x2, Pallas kernels, project_out(): pl.pallas_call(functools.partial(output_kernel, orders, rows, first, span...  10.8 us
    pallas_call x1, Pallas kernels, project(): pl.pallas_call(functools.partial(project_kernel, orders, rows, first, wid...  9.48 us
    pallas_call x1, Pallas kernels, attend(): pl.pallas_call(functools.partial(attend_kernel, parts), out_shape=(out, o...  8.04 us
    ppermute x7, waiting for transfers between devices, swap(): return lax.ppermute(array, 'gy', [(0, 1), (1, 0)])  3.68 us
  transfers between devices with their start and end apart: 22, of which 15 were waited for; matrix products, arithmetic and copies ran while one was open for 2% of the time, Pallas kernels for 6%

profile of v5, /device:TPU:0, one launch (start us, length us, event | category | flops | bytes accessed | tf_op | source)
XLA Modules:
  0.0 90.0 jit_solution(1626053851348988549)
XLA Ops:
  0.0 0.5 collective-permute-start
  0.5 1.0 %broadcast_select_fusion.own_ref = bf16[64,2304]{1,0:T(8,128)(2,1)S(1)} fusion(bf16[64,2304]{1,0:T(8,128)(2,1)} %param.7, pred[]{:T(512)S(6)} %lt.6), kind=kLoop, calls=%fused_computation.3 | loop fusion | flops 147456 | bytes 589825 | tf_op jit(solution)/shard_map/jit(_where)/select_n | solution.py:312
  1.9 1.7 %copy-done = bf16[2304,512]{1,0:T(8,128)(2,1)S(1)} copy-done((bf16[2304,512]{1,0:T(8,128)(2,1)S(1)}, bf16[2304,512]{1,0:T(8,128)(2,1)}, u32[]{:S(2)}) %copy-start) | copy-done | bytes 2359320
  3.5 9.5 %project.1 = (f32[64,1024]{1,0:T(8,128)S(1)}, f32[64,1024]{1,0:T(8,128)S(1)}, f32[64,1280]{1,0:T(8,128)S(1)}, f32[64,1280]{1,0:T(8,128)S(1)}, f32[64,1024]{1,0:T(8,128)S(1)}, /*index=5*/f32[64,1024]{1,0:T(8,128)S(1)}) custom-call(s32[2]{0:T(128)S(1)} %pad_add_fusion.ids_ref, bf16[64,2304]{1,0:T(8,128)(2,1)S(1)} %broadcast_select_fusion.own_ref, ...), custom_call_target="tpu_custom_call" | custom-call | flops 1962934272 | bytes 17039360 | tf_op jit(solution)/shard_map/project/pallas_call | solution.py:130
  13.0 3.0 %collective-permute-start.7 = (f32[64,1024]{1,0:T(8,128)S(1)}, f32[64,1024]{1,0:T(8,128)S(1)}, u32[]{:S(2)}, u32[]{:S(2)}) collective-permute-start(f32[64,1024]{1,0:T(8,128)S(1)} %get-tuple-element.22), channel_id=1, source_target_pairs={{0,4},{2,6},{4,0},{6,2},{8,12},{10,14},{12,8},{14,10},{1,5},{3,7},... | collective-permute-start | bytes 786440 | tf_op jit(solution)/shard_map/ppermute | solution.py:309
  16.1 1.9 %collective-permute-start.1 = (f32[64,1024]{1,0:T(8,128)S(1)}, f32[64,1024]{1,0:T(8,128)S(1)}, u32[]{:S(2)}, u32[]{:S(2)}) collective-permute-start(f32[64,1024]{1,0:T(8,128)S(1)} %get-tuple-element.18), channel_id=1, source_target_pairs={{0,2},{2,0},{4,6},{6,4},{8,10},{10,8},{12,14},{14,12},{1,3},{3,1},... | collective-permute-start | bytes 786440 | tf_op jit(solution)/shard_map/ppermute | solution.py:309
  18.0 5.1 %collective-permute-done.7 = f32[64,1024]{1,0:T(8,128)S(1)} collective-permute-done((f32[64,1024]{1,0:T(8,128)S(1)}, f32[64,1024]{1,0:T(8,128)S(1)}, u32[]{:S(2)}, u32[]{:S(2)}) %collective-permute-start.7) | collective-permute-done | bytes 262176 | tf_op jit(solution)/shard_map/ppermute | solution.py:309
  23.2 2.1 %collective-permute-start.8 = (f32[32,1024]{1,0:T(8,128)S(1)}, f32[32,1024]{1,0:T(8,128)S(1)}, u32[]{:S(2)}, u32[]{:S(2)}) collective-permute-start(f32[32,1024]{1,0:T(8,128)S(1)} %slice.65), channel_id=1, source_target_pairs={{0,2},{2,0},{4,6},{6,4},{8,10},{10,8},{12,14},{14,12},{1,3},{3,1},... | collective-permute-start | bytes 393224 | tf_op jit(solution)/shard_map/ppermute | solution.py:309
  25.3 2.7 %collective-permute-start.2 = (f32[32,1024]{1,0:T(8,128)S(1)}, f32[32,1024]{1,0:T(8,128)S(1)}, u32[]{:S(2)}, u32[]{:S(2)}) collective-permute-start(f32[32,1024]{1,0:T(8,128)S(1)} %slice.57), channel_id=1, source_target_pairs={{0,8},{2,10},{4,12},{6,14},{8,0},{10,2},{12,4},{14,6},{1,9},{3,11}... | collective-permute-start | bytes 393224 | tf_op jit(solution)/shard_map/ppermute | solution.py:309
  28.0 4.5 %collective-permute-done.4 = f32[64,1280]{1,0:T(8,128)S(1)} collective-permute-done((f32[64,1280]{1,0:T(8,128)S(1)}, f32[64,1280]{1,0:T(8,128)S(1)}, u32[]{:S(2)}, u32[]{:S(2)}) %collective-permute-start.4) | collective-permute-done | bytes 327712 | tf_op jit(solution)/shard_map/ppermute | solution.py:309
  32.5 1.7 %collective-permute-start.5 = (f32[32,1280]{1,0:T(8,128)S(1)}, f32[32,1280]{1,0:T(8,128)S(1)}, u32[]{:S(2)}, u32[]{:S(2)}) collective-permute-start(f32[32,1280]{1,0:T(8,128)S(1)} %slice.61), channel_id=1, source_target_pairs={{0,2},{2,0},{4,6},{6,4},{8,10},{10,8},{12,14},{14,12},{1,3},{3,1},... | collective-permute-start | bytes 491528 | tf_op jit(solution)/shard_map/ppermute | solution.py:309
  34.3 1.2 %collective-permute-start.9 = (f32[16,1024]{1,0:T(8,128)S(1)}, f32[16,1024]{1,0:T(8,128)S(1)}, u32[]{:S(2)}, u32[]{:S(2)}) collective-permute-start(f32[16,1024]{1,0:T(8,128)S(1)} %slice.67), channel_id=1, source_target_pairs={{0,8},{2,10},{4,12},{6,14},{8,0},{10,2},{12,4},{14,6},{1,9},{3,11}... | collective-permute-start | bytes 196616 | tf_op jit(solution)/shard_map/ppermute | solution.py:309
  35.6 2.5 %collective-permute-start.3 = (f32[16,1024]{1,0:T(8,128)S(1)}, f32[16,1024]{1,0:T(8,128)S(1)}, u32[]{:S(2)}, u32[]{:S(2)}) collective-permute-start(f32[16,1024]{1,0:T(8,128)S(1)} %slice.59), channel_id=1, source_target_pairs={{0,4},{2,6},{4,0},{6,2},{8,12},{10,14},{12,8},{14,10},{1,5},{3,7},... | collective-permute-start | bytes 196616 | tf_op jit(solution)/shard_map/ppermute | solution.py:309
  38.1 2.2 %collective-permute-done.9 = f32[16,1024]{1,0:T(8,128)S(1)} collective-permute-done((f32[16,1024]{1,0:T(8,128)S(1)}, f32[16,1024]{1,0:T(8,128)S(1)}, u32[]{:S(2)}, u32[]{:S(2)}) %collective-permute-start.9) | collective-permute-done | bytes 65568 | tf_op jit(solution)/shard_map/ppermute | solution.py:309
  40.9 0.9 %collective-permute-start.6 = (f32[16,1280]{1,0:T(8,128)S(1)}, f32[16,1280]{1,0:T(8,128)S(1)}, u32[]{:S(2)}, u32[]{:S(2)}) collective-permute-start(f32[16,1280]{1,0:T(8,128)S(1)} %slice.63), channel_id=1, source_target_pairs={{0,8},{2,10},{4,12},{6,14},{8,0},{10,2},{12,4},{14,6},{1,9},{3,11}... | collective-permute-start | bytes 245768 | tf_op jit(solution)/shard_map/ppermute | solution.py:309
  41.8 6.0 %collective-permute-done.6 = f32[16,1280]{1,0:T(8,128)S(1)} collective-permute-done((f32[16,1280]{1,0:T(8,128)S(1)}, f32[16,1280]{1,0:T(8,128)S(1)}, u32[]{:S(2)}, u32[]{:S(2)}) %collective-permute-start.6) | collective-permute-done | bytes 81952 | tf_op jit(solution)/shard_map/ppermute | solution.py:309
  48.0 1.1 %collective-permute-done.11.refs_4_ = bf16[8,1280]{1,0:T(8,128)(2,1)S(1)} collective-permute-done((bf16[8,1280]{1,0:T(8,128)(2,1)S(1)}, bf16[8,1280]{1,0:T(8,128)(2,1)S(1)}, u32[]{:S(2)}, u32[]{:S(2)}) %collective-permute-start.11) | collective-permute-done | bytes 20512 | tf_op jit(solution)/shard_map/ppermute | solution.py:306
  49.1 8.0 %attend.1 = (bf16[8,3072]{1,0:T(8,128)(2,1)S(1)}, bf16[8,3072]{1,0:T(8,128)(2,1)S(1)}) custom-call(s32[9]{0:T(128)S(1)} %pad_add_fusion.1.scalars_ref, bf16[8,1024]{1,0:T(8,128)(2,1)S(1)} %get-tuple-element.36.refs_0_, bf16[8,1280]{1,0:T(8,128)(2,1)S(1)} %get-tuple-element.32.refs_1_, bf16[8,1024]{1,0:T(8,128)(2,1)S(1)} %get-tuple-element.34.refs_2_, ...), custom_call_target="tpu_custom_call" | custom-call | flops 201326592 | bytes 8388608 | tf_op jit(solution)/shard_map/attend/pallas_call | solution.py:208
  57.4 1.1 %collective-permute-done.13 = bf16[8,3072]{1,0:T(8,128)(2,1)S(1)} collective-permute-done((bf16[8,3072]{1,0:T(8,128)(2,1)S(1)}, bf16[8,3072]{1,0:T(8,128)(2,1)S(1)}, u32[]{:S(2)}, u32[]{:S(2)}) %collective-permute-start.13) | collective-permute-done | bytes 49184 | tf_op jit(solution)/shard_map/ppermute | solution.py:306
  58.9 3.8 %collective-permute-done.17 = bf16[16,1536]{1,0:T(8,128)(2,1)S(1)} collective-permute-done((bf16[16,1536]{1,0:T(8,128)(2,1)S(1)}, bf16[16,1536]{1,0:T(8,128)(2,1)S(1)}, u32[]{:S(2)}, u32[]{:S(2)}) %collective-permute-start.17) | collective-permute-done | bytes 49184 | tf_op jit(solution)/shard_map/ppermute | solution.py:309
  62.7 1.3 %collective-permute-done.14 = bf16[16,1536]{1,0:T(8,128)(2,1)S(1)} collective-permute-done((bf16[16,1536]{1,0:T(8,128)(2,1)S(1)}, bf16[16,1536]{1,0:T(8,128)(2,1)S(1)}, u32[]{:S(2)}, u32[]{:S(2)}) %collective-permute-start.14) | collective-permute-done | bytes 49184 | tf_op jit(solution)/shard_map/ppermute | solution.py:309
  64.0 1.3 %collective-permute-start.15 = (bf16[32,1536]{1,0:T(8,128)(2,1)S(1)}, bf16[32,1536]{1,0:T(8,128)(2,1)S(1)}, u32[]{:S(2)}, u32[]{:S(2)}) collective-permute-start(bf16[32,1536]{1,0:T(8,128)(2,1)S(1)} %pad_maximum_fusion.3), channel_id=1, source_target_pairs={{0,4},{2,6},{4,0},{6,2},{8,12},{10,14},{12,8},{14,10},{1,5},{3,7},... | collective-permute-start | bytes 294920 | tf_op jit(solution)/shard_map/ppermute | solution.py:309
  65.4 3.8 %collective-permute-done.18 = bf16[32,1536]{1,0:T(8,128)(2,1)S(1)} collective-permute-done((bf16[32,1536]{1,0:T(8,128)(2,1)S(1)}, bf16[32,1536]{1,0:T(8,128)(2,1)S(1)}, u32[]{:S(2)}, u32[]{:S(2)}) %collective-permute-start.18) | collective-permute-done | bytes 98336 | tf_op jit(solution)/shard_map/ppermute | solution.py:309
  69.4 1.2 %collective-permute-done.15 = bf16[32,1536]{1,0:T(8,128)(2,1)S(1)} collective-permute-done((bf16[32,1536]{1,0:T(8,128)(2,1)S(1)}, bf16[32,1536]{1,0:T(8,128)(2,1)S(1)}, u32[]{:S(2)}, u32[]{:S(2)}) %collective-permute-start.15) | collective-permute-done | bytes 98336 | tf_op jit(solution)/shard_map/ppermute | solution.py:309
  70.6 1.1 %collective-permute-start.16 = (bf16[64,1536]{1,0:T(8,128)(2,1)S(1)}, bf16[64,1536]{1,0:T(8,128)(2,1)S(1)}, u32[]{:S(2)}, u32[]{:S(2)}) collective-permute-start(bf16[64,1536]{1,0:T(8,128)(2,1)S(1)} %pad_maximum_fusion.1.refs_0_), channel_id=1, source_target_pairs={{0,2},{2,0},{4,6},{6,4},{8,10},{10,8},{12,14},{14,12},{1,3},{3,1},... | collective-permute-start | bytes 589832 | tf_op jit(solution)/shard_map/ppermute | solution.py:309
  71.8 3.1 %collective-permute-done.19.refs_3_ = bf16[64,1536]{1,0:T(8,128)(2,1)S(1)} collective-permute-done((bf16[64,1536]{1,0:T(8,128)(2,1)S(1)}, bf16[64,1536]{1,0:T(8,128)(2,1)S(1)}, u32[]{:S(2)}, u32[]{:S(2)}) %collective-permute-start.19) | collective-permute-done | bytes 196640 | tf_op jit(solution)/shard_map/ppermute | solution.py:309
  74.9 1.7 %collective-permute-done.16.refs_1_ = bf16[64,1536]{1,0:T(8,128)(2,1)S(1)} collective-permute-done((bf16[64,1536]{1,0:T(8,128)(2,1)S(1)}, bf16[64,1536]{1,0:T(8,128)(2,1)S(1)}, u32[]{:S(2)}, u32[]{:S(2)}) %collective-permute-start.16) | collective-permute-done | bytes 196640 | tf_op jit(solution)/shard_map/ppermute | solution.py:309
  76.6 5.4 %project_out.2 = (f32[64,1152]{1,0:T(8,128)S(1)}, f32[64,1152]{1,0:T(8,128)S(1)}) custom-call(s32[2]{0:T(128)S(1)} %pad_add_fusion.ids_ref, bf16[64,1536]{1,0:T(8,128)(2,1)S(1)} %pad_maximum_fusion.1.refs_0_, bf16[64,1536]{1,0:T(8,128)(2,1)S(1)} %collective-permute-done.16.refs_1_, bf16[64,1536]{1,0:T(8,128)(2,1)S(1)} %pad_maximum_fusion.2.refs_2_, ...), custom_call_target="tpu_custom_call" | custom-call | flops 905969664 | bytes 7667712 | tf_op jit(solution)/shard_map/project_out/pallas_call | solution.py:275
  82.1 5.4 %project_out.3 = (f32[64,1152]{1,0:T(8,128)S(1)}, f32[64,1152]{1,0:T(8,128)S(1)}) custom-call(s32[2]{0:T(128)S(1)} %pad_add_fusion.ids_ref, bf16[64,1536]{1,0:T(8,128)(2,1)S(1)} %pad_maximum_fusion.1.refs_0_, bf16[64,1536]{1,0:T(8,128)(2,1)S(1)} %collective-permute-done.16.refs_1_, bf16[64,1536]{1,0:T(8,128)(2,1)S(1)} %pad_maximum_fusion.2.refs_2_, ...), custom_call_target="tpu_custom_call" | custom-call | flops 905969664 | bytes 7667712 | tf_op jit(solution)/shard_map/project_out/pallas_call | solution.py:275
  87.5 0.6 collective-permute-start.21
  88.1 1.2 %collective-permute-done.21 = f32[64,1152]{1,0:T(8,128)S(1)} collective-permute-done((f32[64,1152]{1,0:T(8,128)S(1)}, f32[64,1152]{1,0:T(8,128)S(1)}, u32[]{:S(2)}, u32[]{:S(2)}) %collective-permute-start.21) | collective-permute-done | bytes 294944 | tf_op jit(solution)/shard_map/ppermute | solution.py:306
  89.3 0.7 pad_maximum_fusion
  (50 shorter events, 2.5 us)
Async XLA Ops:
  0.0 1.9 %collective-permute-start = (bf16[64,2304]{1,0:T(8,128)(2,1)}, bf16[64,2304]{1,0:T(8,128)(2,1)S(1)}, u32[]{:S(2)}, u32[]{:S(2)}) collective-permute-start(bf16[64,2304]{1,0:T(8,128)(2,1)} %param.7), channel_id=1, source_target_pairs={{0,1},{1,0},{2,3},{3,2},{4,5},{5,4},{6,7},{7,6},{8,9},{9,8},{10,11... | collective-permute-start | bytes 884744 | tf_op jit(solution)/shard_map/ppermute | solution.py:306
  1.9 1.7 %copy-start = (bf16[2304,512]{1,0:T(8,128)(2,1)S(1)}, bf16[2304,512]{1,0:T(8,128)(2,1)}, u32[]{:S(2)}) copy-start(bf16[2304,512]{1,0:T(8,128)(2,1)} %refs_0_.1) | copy-start | bytes 7077892
  13.0 34.9 %copy-start.1 = (s32[8]{0:T(128)S(1)}, s32[8]{0:T(128)}, u32[]{:S(2)}) copy-start(s32[8]{0:T(128)} %param.13) | copy-start | bytes 100
  13.0 10.1 %collective-permute-start.7 = (f32[64,1024]{1,0:T(8,128)S(1)}, f32[64,1024]{1,0:T(8,128)S(1)}, u32[]{:S(2)}, u32[]{:S(2)}) collective-permute-start(f32[64,1024]{1,0:T(8,128)S(1)} %get-tuple-element.22), channel_id=1, source_target_pairs={{0,4},{2,6},{4,0},{6,2},{8,12},{10,14},{12,8},{14,10},{1,5},{3,7},... | collective-permute-start | bytes 786440 | tf_op jit(solution)/shard_map/ppermute | solution.py:309
  16.1 16.4 %collective-permute-start.4 = (f32[64,1280]{1,0:T(8,128)S(1)}, f32[64,1280]{1,0:T(8,128)S(1)}, u32[]{:S(2)}, u32[]{:S(2)}) collective-permute-start(f32[64,1280]{1,0:T(8,128)S(1)} %get-tuple-element.20), channel_id=1, source_target_pairs={{0,4},{2,6},{4,0},{6,2},{8,12},{10,14},{12,8},{14,10},{1,5},{3,7},... | collective-permute-start | bytes 983048 | tf_op jit(solution)/shard_map/ppermute | solution.py:309
  16.1 9.1 %collective-permute-start.1 = (f32[64,1024]{1,0:T(8,128)S(1)}, f32[64,1024]{1,0:T(8,128)S(1)}, u32[]{:S(2)}, u32[]{:S(2)}) collective-permute-start(f32[64,1024]{1,0:T(8,128)S(1)} %get-tuple-element.18), channel_id=1, source_target_pairs={{0,2},{2,0},{4,6},{6,4},{8,10},{10,8},{12,14},{14,12},{1,3},{3,1},... | collective-permute-start | bytes 786440 | tf_op jit(solution)/shard_map/ppermute | solution.py:309
  23.2 11.1 %collective-permute-start.8 = (f32[32,1024]{1,0:T(8,128)S(1)}, f32[32,1024]{1,0:T(8,128)S(1)}, u32[]{:S(2)}, u32[]{:S(2)}) collective-permute-start(f32[32,1024]{1,0:T(8,128)S(1)} %slice.65), channel_id=1, source_target_pairs={{0,2},{2,0},{4,6},{6,4},{8,10},{10,8},{12,14},{14,12},{1,3},{3,1},... | collective-permute-start | bytes 393224 | tf_op jit(solution)/shard_map/ppermute | solution.py:309
  25.3 10.2 %collective-permute-start.2 = (f32[32,1024]{1,0:T(8,128)S(1)}, f32[32,1024]{1,0:T(8,128)S(1)}, u32[]{:S(2)}, u32[]{:S(2)}) collective-permute-start(f32[32,1024]{1,0:T(8,128)S(1)} %slice.57), channel_id=1, source_target_pairs={{0,8},{2,10},{4,12},{6,14},{8,0},{10,2},{12,4},{14,6},{1,9},{3,11}... | collective-permute-start | bytes 393224 | tf_op jit(solution)/shard_map/ppermute | solution.py:309
  32.5 8.3 %collective-permute-start.5 = (f32[32,1280]{1,0:T(8,128)S(1)}, f32[32,1280]{1,0:T(8,128)S(1)}, u32[]{:S(2)}, u32[]{:S(2)}) collective-permute-start(f32[32,1280]{1,0:T(8,128)S(1)} %slice.61), channel_id=1, source_target_pairs={{0,2},{2,0},{4,6},{6,4},{8,10},{10,8},{12,14},{14,12},{1,3},{3,1},... | collective-permute-start | bytes 491528 | tf_op jit(solution)/shard_map/ppermute | solution.py:309
  34.3 6.0 %collective-permute-start.9 = (f32[16,1024]{1,0:T(8,128)S(1)}, f32[16,1024]{1,0:T(8,128)S(1)}, u32[]{:S(2)}, u32[]{:S(2)}) collective-permute-start(f32[16,1024]{1,0:T(8,128)S(1)} %slice.67), channel_id=1, source_target_pairs={{0,8},{2,10},{4,12},{6,14},{8,0},{10,2},{12,4},{14,6},{1,9},{3,11}... | collective-permute-start | bytes 196616 | tf_op jit(solution)/shard_map/ppermute | solution.py:309
  35.6 5.2 %collective-permute-start.3 = (f32[16,1024]{1,0:T(8,128)S(1)}, f32[16,1024]{1,0:T(8,128)S(1)}, u32[]{:S(2)}, u32[]{:S(2)}) collective-permute-start(f32[16,1024]{1,0:T(8,128)S(1)} %slice.59), channel_id=1, source_target_pairs={{0,4},{2,6},{4,0},{6,2},{8,12},{10,14},{12,8},{14,10},{1,5},{3,7},... | collective-permute-start | bytes 196616 | tf_op jit(solution)/shard_map/ppermute | solution.py:309
  40.4 7.6 %collective-permute-start.12 = (bf16[8,1024]{1,0:T(8,128)(2,1)S(1)}, bf16[8,1024]{1,0:T(8,128)(2,1)S(1)}, u32[]{:S(2)}, u32[]{:S(2)}) collective-permute-start(bf16[8,1024]{1,0:T(8,128)(2,1)S(1)} %get-tuple-element.33), channel_id=1, source_target_pairs={{0,1},{1,0},{2,3},{3,2},{4,5},{5,4},{6,7},{7,6},{8,9},{9,8},{10,11... | collective-permute-start | bytes 49160 | tf_op jit(solution)/shard_map/ppermute | solution.py:306
  40.9 6.9 %collective-permute-start.6 = (f32[16,1280]{1,0:T(8,128)S(1)}, f32[16,1280]{1,0:T(8,128)S(1)}, u32[]{:S(2)}, u32[]{:S(2)}) collective-permute-start(f32[16,1280]{1,0:T(8,128)S(1)} %slice.63), channel_id=1, source_target_pairs={{0,8},{2,10},{4,12},{6,14},{8,0},{10,2},{12,4},{14,6},{1,9},{3,11}... | collective-permute-start | bytes 245768 | tf_op jit(solution)/shard_map/ppermute | solution.py:309
  41.8 6.2 %collective-permute-start.10 = (bf16[8,1024]{1,0:T(8,128)(2,1)S(1)}, bf16[8,1024]{1,0:T(8,128)(2,1)S(1)}, u32[]{:S(2)}, u32[]{:S(2)}) collective-permute-start(bf16[8,1024]{1,0:T(8,128)(2,1)S(1)} %get-tuple-element.35), channel_id=1, source_target_pairs={{0,1},{1,0},{2,3},{3,2},{4,5},{5,4},{6,7},{7,6},{8,9},{9,8},{10,11... | collective-permute-start | bytes 49160 | tf_op jit(solution)/shard_map/ppermute | solution.py:306
  47.8 1.3 %collective-permute-start.11 = (bf16[8,1280]{1,0:T(8,128)(2,1)S(1)}, bf16[8,1280]{1,0:T(8,128)(2,1)S(1)}, u32[]{:S(2)}, u32[]{:S(2)}) collective-permute-start(bf16[8,1280]{1,0:T(8,128)(2,1)S(1)} %get-tuple-element.31), channel_id=1, source_target_pairs={{0,1},{1,0},{2,3},{3,2},{4,5},{5,4},{6,7},{7,6},{8,9},{9,8},{10,11... | collective-permute-start | bytes 61448 | tf_op jit(solution)/shard_map/ppermute | solution.py:306
  57.2 1.3 %collective-permute-start.13 = (bf16[8,3072]{1,0:T(8,128)(2,1)S(1)}, bf16[8,3072]{1,0:T(8,128)(2,1)S(1)}, u32[]{:S(2)}, u32[]{:S(2)}) collective-permute-start(bf16[8,3072]{1,0:T(8,128)(2,1)S(1)} %get-tuple-element.24), channel_id=1, source_target_pairs={{0,1},{1,0},{2,3},{3,2},{4,5},{5,4},{6,7},{7,6},{8,9},{9,8},{10,11... | collective-permute-start | bytes 147464 | tf_op jit(solution)/shard_map/ppermute | solution.py:306
  58.5 4.2 %collective-permute-start.17 = (bf16[16,1536]{1,0:T(8,128)(2,1)S(1)}, bf16[16,1536]{1,0:T(8,128)(2,1)S(1)}, u32[]{:S(2)}, u32[]{:S(2)}) collective-permute-start(bf16[16,1536]{1,0:T(8,128)(2,1)S(1)} %get-tuple-element.29), channel_id=1, source_target_pairs={{0,2},{2,0},{4,6},{6,4},{8,10},{10,8},{12,14},{14,12},{1,3},{3,1},... | collective-permute-start | bytes 147464 | tf_op jit(solution)/shard_map/ppermute | solution.py:309
  58.9 5.1 %collective-permute-start.14 = (bf16[16,1536]{1,0:T(8,128)(2,1)S(1)}, bf16[16,1536]{1,0:T(8,128)(2,1)S(1)}, u32[]{:S(2)}, u32[]{:S(2)}) collective-permute-start(bf16[16,1536]{1,0:T(8,128)(2,1)S(1)} %get-tuple-element.30), channel_id=1, source_target_pairs={{0,8},{2,10},{4,12},{6,14},{8,0},{10,2},{12,4},{14,6},{1,9},{3,11}... | collective-permute-start | bytes 147464 | tf_op jit(solution)/shard_map/ppermute | solution.py:309
  62.7 6.5 %collective-permute-start.18 = (bf16[32,1536]{1,0:T(8,128)(2,1)S(1)}, bf16[32,1536]{1,0:T(8,128)(2,1)S(1)}, u32[]{:S(2)}, u32[]{:S(2)}) collective-permute-start(bf16[32,1536]{1,0:T(8,128)(2,1)S(1)} %pad_maximum_fusion.4), channel_id=1, source_target_pairs={{0,8},{2,10},{4,12},{6,14},{8,0},{10,2},{12,4},{14,6},{1,9},{3,11}... | collective-permute-start | bytes 294920 | tf_op jit(solution)/shard_map/ppermute | solution.py:309
  64.0 6.6 %collective-permute-start.15 = (bf16[32,1536]{1,0:T(8,128)(2,1)S(1)}, bf16[32,1536]{1,0:T(8,128)(2,1)S(1)}, u32[]{:S(2)}, u32[]{:S(2)}) collective-permute-start(bf16[32,1536]{1,0:T(8,128)(2,1)S(1)} %pad_maximum_fusion.3), channel_id=1, source_target_pairs={{0,4},{2,6},{4,0},{6,2},{8,12},{10,14},{12,8},{14,10},{1,5},{3,7},... | collective-permute-start | bytes 294920 | tf_op jit(solution)/shard_map/ppermute | solution.py:309
  69.2 5.7 %collective-permute-start.19 = (bf16[64,1536]{1,0:T(8,128)(2,1)S(1)}, bf16[64,1536]{1,0:T(8,128)(2,1)S(1)}, u32[]{:S(2)}, u32[]{:S(2)}) collective-permute-start(bf16[64,1536]{1,0:T(8,128)(2,1)S(1)} %pad_maximum_fusion.2.refs_2_), channel_id=1, source_target_pairs={{0,4},{2,6},{4,0},{6,2},{8,12},{10,14},{12,8},{14,10},{1,5},{3,7},... | collective-permute-start | bytes 589832 | tf_op jit(solution)/shard_map/ppermute | solution.py:309
  70.6 6.0 %collective-permute-start.16 = (bf16[64,1536]{1,0:T(8,128)(2,1)S(1)}, bf16[64,1536]{1,0:T(8,128)(2,1)S(1)}, u32[]{:S(2)}, u32[]{:S(2)}) collective-permute-start(bf16[64,1536]{1,0:T(8,128)(2,1)S(1)} %pad_maximum_fusion.1.refs_0_), channel_id=1, source_target_pairs={{0,2},{2,0},{4,6},{6,4},{8,10},{10,8},{12,14},{14,12},{1,3},{3,1},... | collective-permute-start | bytes 589832 | tf_op jit(solution)/shard_map/ppermute | solution.py:309
  82.0 6.0 %collective-permute-start.20 = (f32[64,1152]{1,0:T(8,128)S(1)}, f32[64,1152]{1,0:T(8,128)S(1)}, u32[]{:S(2)}, u32[]{:S(2)}) collective-permute-start(f32[64,1152]{1,0:T(8,128)S(1)} %get-tuple-element.26), channel_id=1, source_target_pairs={{0,1},{1,0},{2,3},{3,2},{4,5},{5,4},{6,7},{7,6},{8,9},{9,8},{10,11... | collective-permute-start | bytes 884744 | tf_op jit(solution)/shard_map/ppermute | solution.py:306
  87.5 1.8 %collective-permute-start.21 = (f32[64,1152]{1,0:T(8,128)S(1)}, f32[64,1152]{1,0:T(8,128)S(1)}, u32[]{:S(2)}, u32[]{:S(2)}) collective-permute-start(f32[64,1152]{1,0:T(8,128)S(1)} %get-tuple-element.28), channel_id=1, source_target_pairs={{0,1},{1,0},{2,3},{3,2},{4,5},{5,4},{6,7},{7,6},{8,9},{9,8},{10,11... | collective-permute-start | bytes 884744 | tf_op jit(solution)/shard_map/ppermute | solution.py:306

commit v6 on v5

--- a/solution.py
+++ b/solution.py
@@ -35,14 +35,69 @@
     return order
 
 
+def cuts_of(array):
+    if len(array.shape) == 3:
+        return [(at, None) for at in range(array.shape[0])]
+    depth, columns = array.shape
+    tall, wide = 512, (768 if columns % 768 == 0 else columns)
+    return [
+        ((at, tall), (column, wide)) for at in range(0, depth, tall) for column in range(0, columns, wide)
+    ]
+
+
+def piece_of(array, cut):
+    if cut[1] is None:
+        shape = array.shape[1:]
+    else:
+        shape = (cut[0][1], cut[1][1])
+    return jax.ShapeDtypeStruct(shape, array.dtype)
+
+
+def fetches(refs, cuts, targets, sems):
+    copies = []
+    for ref, cut in cuts:
+        source = refs[ref]
+        view = source.at[cut[0]] if cut[1] is None else source.at[pl.ds(*cut[0]), pl.ds(*cut[1])]
+        copies.append(pltpu.make_async_copy(view, targets[len(copies)], sems.at[len(copies)]))
+    return copies
+
+
+def load_kernel(after, cuts, count, *refs):
+    refs = refs[after:]
+    in_refs, out_refs, zero_ref, sems = refs[:count], refs[count:-2], refs[-2], refs[-1]
+    copies = fetches(in_refs, cuts, out_refs, sems)
+    for copy in copies:
+        copy.start()
+    zero_ref[...] = jnp.zeros_like(zero_ref)
+    for copy in copies:
+        copy.wait()
+
+
+def load(arrays, cuts, after, grant):
+    shapes = [piece_of(arrays[at], cut) for at, cut in cuts]
+    *held, zero = pl.pallas_call(
+        functools.partial(load_kernel, len(after), cuts, len(arrays)),
+        out_shape=(*shapes, jax.ShapeDtypeStruct((8, 128), jnp.float32)),
+        in_specs=[ANY] * len(after) + [HBM] * len(arrays),
+        out_specs=[VMEM] * (len(cuts) + 1),
+        scratch_shapes=[pltpu.SemaphoreType.DMA((len(cuts),))],
+        compiler_params=pltpu.CompilerParams(vmem_limit_bytes=grant * MIB),
+        cost_estimate=pl.CostEstimate(
+            flops=0, bytes_accessed=sum(4 * s.shape[0] * s.shape[1] for s in shapes), transcendentals=0
+        ),
+        name="load",
+    )(*after, *arrays)
+    return held, zero[0, 0]
+
+
 def spans_of(width):
     return [(at, min(512, width - at)) for at in range(0, width, 512)]
 
 
-def project_kernel(orders, rows, first, widths, kv_width, ids_ref, own_ref, other_ref, w_ref, *refs):
+def project_kernel(orders, rows, first, widths, kv_width, after, ids_ref, own_ref, other_ref, w_ref, *refs):
     refs = list(refs)
     kv_ref = refs.pop(0) if kv_width else None
-    outs, (xs_ref, ws_ref, row_sem, w_sem) = refs[:-4], refs[-4:]
+    outs, (xs_ref, ws_ref, row_sem, w_sem) = refs[after:-4], refs[-4:]
     n = len(orders[0])
     half = n // 2
     me, core = ids_ref[0], ids_ref[1]
@@ -114,7 +169,7 @@
         outs[2 * chunk + 1][:, span] = total[:cut]
 
 
-def project(plan, rows, ids, tokens, other, query_weight, kv_weight, first):
+def project(plan, rows, ids, tokens, other, query_weight, kv_weight, first, after):
     features = tokens.shape[1]
     orders = [order_of(bits) for _, bits in plan]
     widths = [width for width, _ in plan]
@@ -128,9 +183,9 @@
     weights = [query_weight] + ([kv_weight] if kv_width else [])
     copies = 2 * (len(weights) - 1 + sum(len(spans_of(width)) for width in widths))
     outs = pl.pallas_call(
-        functools.partial(project_kernel, orders, rows, first, widths, kv_width),
+        functools.partial(project_kernel, orders, rows, first, widths, kv_width, len(after)),
         out_shape=outs,
-        in_specs=[SMEM, ANY, ANY] + [HBM] * len(weights),
+        in_specs=[SMEM, ANY, ANY] + [HBM] * len(weights) + [ANY] * len(after),
         out_specs=[VMEM] * len(outs),
         scratch_shapes=[
             pltpu.VMEM((len(orders), n * rows, features), tokens.dtype),
@@ -145,20 +200,19 @@
             transcendentals=0,
         ),
         name="project",
-    )(ids, tokens, other, *weights)
+    )(ids, tokens, other, *weights, *after)
     return list(zip(outs[::2], outs[1::2]))
 
 
-def attend_kernel(parts, scalars_ref, *refs):
+def attend_kernel(parts, rows, cuts, scalars_ref, *refs):
     own_q, other_q = refs[: len(parts)], refs[len(parts) : 2 * len(parts)]
-    k_hbm, v_hbm, own_out, other_out, k_ref, v_ref, q_scr, o_scr, sems = refs[2 * len(parts) :]
+    refs = refs[2 * len(parts) :]
+    k_refs, v_refs, w_hbm, refs = refs[:rows], refs[rows : 2 * rows], refs[2 * rows], refs[2 * rows + 1 :]
+    own_out, other_out, held, (q_scr, o_scr, sems) = refs[0], refs[1], refs[2:-3], refs[-3:]
+    copies = fetches([w_hbm], [(0, cut) for cut in cuts], held, sems)
+    for copy in copies:
+        copy.start()
     core = scalars_ref[0]
-    rows, positions, _ = k_ref.shape
-    copies = []
-    for row in range(rows):
-        copies.append(pltpu.make_async_copy(k_hbm.at[row], k_ref.at[row], sems.at[0, row]))
-        copies.append(pltpu.make_async_copy(v_hbm.at[row], v_ref.at[row], sems.at[1, row]))
-    caches = InOrder(copies, 8)
     at = 0
     for side in (own_q, other_q):
         for ref, (heads, skip) in zip(side, parts):
@@ -167,17 +221,17 @@
                 q_scr[:, at, :] = ref[:, column : column + DH].astype(jnp.float32)
                 at += 1
     total_heads = at
-    first = own_q[0][:, :DH].astype(jnp.float32)
-    second = other_q[0][:, :DH].astype(jnp.float32)
+    kv_at = [skip > 0 for _, skip in parts].index(True)
+    first = own_q[kv_at][:, :DH].astype(jnp.float32)
+    second = other_q[kv_at][:, :DH].astype(jnp.float32)
     new_keys = jnp.where(core == 0, first, second)
     new_values = jnp.where(core == 0, second, first)
     scale = DH**-0.5
     for row in range(rows):
         query = q_scr[row]
-        caches.wait(2 * row)
         scores = scale * lax.dot_general(
             query.astype(jnp.bfloat16),
-            k_ref[row],
+            k_refs[row][...],
             (((1,), (1,)), ((), ())),
             preferred_element_type=jnp.float32,
         )
@@ -190,56 +244,50 @@
         denominator = jnp.sum(raised, axis=1, keepdims=True) + self_raised
         weights = (raised / denominator).astype(jnp.bfloat16)
         self_weight = (self_raised / denominator).astype(jnp.bfloat16).astype(jnp.float32)
-        caches.wait(2 * row + 1)
-        total = jnp.dot(weights, v_ref[row], preferred_element_type=jnp.float32)
+        total = jnp.dot(weights, v_refs[row][...], preferred_element_type=jnp.float32)
         o_scr[row] = total + self_weight * new_values[row : row + 1]
     half = total_heads // 2
     for head in range(total_heads):
         ref = own_out if head < half else other_out
         column = (head % half) * DH
         ref[:, column : column + DH] = o_scr[:, head, :].astype(jnp.bfloat16)
-
-
-def attend(core, lengths, own_q, other_q, parts, keys, values):
-    rows, positions, _ = keys.shape
+    for copy in copies:
+        copy.wait()
+
+
+def attend(core, lengths, own_q, other_q, parts, keys, values, out_weight, cuts):
+    rows, (positions, _) = len(keys), keys[0].shape
     heads = 2 * sum(part[0] for part in parts)
     out = jax.ShapeDtypeStruct((rows, heads * DH // 2), jnp.bfloat16)
     scalars = jnp.concatenate([core[None], lengths])
     return pl.pallas_call(
-        functools.partial(attend_kernel, parts),
-        out_shape=(out, out),
-        in_specs=[SMEM] + [VMEM] * (2 * len(parts)) + [HBM, HBM],
-        out_specs=(VMEM, VMEM),
-        scratch_shapes=[pltpu.VMEM(keys.shape, keys.dtype)] * 2
-        + [pltpu.VMEM((rows, heads, DH), jnp.float32)] * 2
-        + [pltpu.SemaphoreType.DMA((2, rows))],
-        compiler_params=pltpu.CompilerParams(vmem_limit_bytes=52 * MIB),
+        functools.partial(attend_kernel, parts, rows, cuts),
+        out_shape=[out, out] + [piece_of(out_weight, cut) for cut in cuts],
+        in_specs=[SMEM] + [VMEM] * (2 * len(parts) + 2 * rows) + [HBM],
+        out_specs=[VMEM] * (2 + len(cuts)),
+        scratch_shapes=[pltpu.VMEM((rows, heads, DH), jnp.float32)] * 2
+        + [pltpu.SemaphoreType.DMA((max(1, len(cuts)),))],
+        compiler_params=pltpu.CompilerParams(vmem_limit_bytes=28 * MIB),
         cost_estimate=pl.CostEstimate(
             flops=4 * rows * heads * positions * DH,
             bytes_accessed=4 * rows * positions * DH,
             transcendentals=rows * heads * positions,
         ),
         name="attend",
-    )(scalars, *own_q, *other_q, keys, values)
-
-
-def output_kernel(order, rows, first, spans, ids_ref, *refs):
-    count = len(refs) - 7
-    block_refs = refs[:count]
-    w_hbm, send_ref, keep_ref, xs_ref, ws_ref, row_sem, w_sem = refs[count:]
+    )(scalars, *own_q, *other_q, *keys, *values, out_weight)
+
+
+def output_kernel(orders, rows, columns, pieces, ids_ref, *refs):
+    count = 2 * len(orders)
+    block_refs, w_refs = refs[:count], refs[count : count + len(pieces)]
+    send_ref, keep_ref, xs_ref, row_sem = refs[count + len(pieces) :]
     depth = block_refs[0].shape[1]
-    copies = [
-        pltpu.make_async_copy(
-            w_hbm.at[:, pl.ds(first + at, width)], ws_ref.at[:, pl.ds(at, width)], w_sem.at[k]
-        )
-        for k, (at, width) in enumerate(spans)
-    ]
     me, core = ids_ref[0], ids_ref[1]
-    n = len(order[0])
+    n = len(orders[0])
     half = n // 2
     row_copies = []
     for group, (near_ref, far_ref) in enumerate(zip(block_refs[::2], block_refs[1::2])):
-        for p, j in enumerate(order[group]):
+        for p, j in enumerate(orders[group]):
             block = jnp.bitwise_xor(me, j)
             place = block % half + jnp.where(block // half == core, half, 0)
             source = near_ref if p < half else far_ref
@@ -254,43 +302,44 @@
             )
     for copy in row_copies:
         copy.start()
-    weights = InOrder(copies, 2)
     for copy in row_copies:
         copy.wait()
     cut = half * rows
-    for k, (at, width) in enumerate(spans):
-        weights.wait(k)
-        span = slice(at, at + width)
-        total = jnp.dot(xs_ref[...], ws_ref[:, span], preferred_element_type=jnp.float32)
-        send_ref[:, span] = total[:cut]
-        keep_ref[:, span] = total[cut:]
-
-
-def project_out(orders, rows, ids, blocks, out_weight, first, columns):
-    depth = out_weight.shape[0]
+    totals = {}
+    for w_ref, ((first, tall), span) in zip(w_refs, pieces):
+        part = jnp.dot(
+            xs_ref[:, first : first + tall], w_ref[...], preferred_element_type=jnp.float32
+        )
+        totals[span] = totals[span] + part if span in totals else part
+    for (column, width), total in totals.items():
+        send_ref[:, column - columns[0] : column - columns[0] + width] = total[:cut]
+        keep_ref[:, column - columns[0] : column - columns[0] + width] = total[cut:]
+
+
+def project_out(orders, rows, ids, blocks, held, cuts, columns):
+    chosen = [at for at, (_, (column, _)) in enumerate(cuts) if columns[0] <= column < sum(columns)]
+    weights, pieces = [held[at] for at in chosen], [cuts[at] for at in chosen]
+    pieces, weights = zip(*sorted(zip(pieces, weights), key=lambda pair: (pair[0][1], pair[0][0])))
+    depth = len(orders) * blocks[0].shape[1]
     n = len(orders[0])
-    tile = 384 if columns % 384 == 0 else columns
-    spans = [(at, tile) for at in range(0, columns, tile)]
-    out = jax.ShapeDtypeStruct((n * rows // 2, columns), jnp.float32)
+    out = jax.ShapeDtypeStruct((n * rows // 2, columns[1]), jnp.float32)
     return pl.pallas_call(
-        functools.partial(output_kernel, orders, rows, first, spans),
+        functools.partial(output_kernel, orders, rows, columns, pieces),
         out_shape=(out, out),
-        in_specs=[SMEM] + [ANY] * len(blocks) + [HBM],
+        in_specs=[SMEM] + [ANY] * len(blocks) + [VMEM] * len(weights),
         out_specs=(VMEM, VMEM),
         scratch_shapes=[
             pltpu.VMEM((n * rows, depth), jnp.bfloat16),
-            pltpu.VMEM((depth, columns), jnp.bfloat16),
             pltpu.SemaphoreType.DMA((len(orders), n)),
-            pltpu.SemaphoreType.DMA((len(spans),)),
         ],
-        compiler_params=pltpu.CompilerParams(vmem_limit_bytes=46 * MIB),
+        compiler_params=pltpu.CompilerParams(vmem_limit_bytes=12 * MIB),
         cost_estimate=pl.CostEstimate(
-            flops=2 * n * rows * depth * columns,
-            bytes_accessed=2 * depth * columns + 4 * n * rows * columns,
+            flops=2 * n * rows * depth * columns[1],
+            bytes_accessed=2 * depth * columns[1] + 4 * n * rows * columns[1],
             transcendentals=0,
         ),
         name="project_out",
-    )(ids, *blocks, out_weight)
+    )(ids, *blocks, *weights)
 
 
 def local(tokens, query_weight, kv_weight, out_weight, key_cache, value_cache, lengths):
@@ -315,16 +364,31 @@
     y, z = bits[:1], bits[1:]
     unit = query_weight.shape[1] // 12
     plan = [(3 * unit, y + z[::-1]), (5 * unit, z[:1] + y + z[1:]), (4 * unit, z[:1] + y + z[1:])]
-    state, first = [], 0
-    for group in (slice(0, 3),):
-        chunks = plan[group]
-        weight = None if state else kv_weight
-        state += project(chunks, rows, ids, own_tokens, other_tokens, query_weight, weight, first)
+    state, first, after = [None] * len(plan), 0, []
+    for group in ((2,), (0, 1)):
+        chunks = [plan[i] for i in group]
+        weight = kv_weight if 0 in group else None
+        made = project(chunks, rows, ids, own_tokens, other_tokens, query_weight, weight, first, after)
+        for i, pair in zip(group, made):
+            state[i] = pair
+        after = [made[0][0]]
         first += sum(columns for columns, _ in chunks)
     moving = [across(send, order[0]) for (send, _), (_, order) in zip(state, plan)]
+    cache_cuts = [(at, cut) for at in range(2) for cut in cuts_of(key_cache)]
+    out_cuts = cuts_of(out_weight)
+    early = len(out_cuts) * 9 // 18
     for step in range(len(bits)):
-        for i, (columns, order) in enumerate(plan):
+        for turn, i in enumerate((2, 0, 1)):
+            columns, order = plan[i]
             total = state[i][1] + moving[i]
+            if step == 0 and turn:
+                ahead = [state[(2, 0, 1)[turn - 1]][0]]
+                if turn == 1:
+                    caches, zero = load([key_cache, value_cache], cache_cuts, ahead, 41)
+                else:
+                    first_cuts = [(0, cut) for cut in out_cuts[:early]]
+                    out_first, zero = load([out_weight], first_cuts, ahead, 36)
+                total = total + zero
             if step + 1 < len(bits):
                 cut = total.shape[0] // 2
                 state[i] = (total[cut:], total[:cut])
@@ -338,8 +402,14 @@
         theirs.append(swap(give))
 
     kv_width = kv_weight.shape[1] // 2
-    parts = tuple((columns // DH, 0 if i else kv_width) for i, (columns, _) in enumerate(plan))
-    own, other = attend(core, lengths, mine, theirs, parts, key_cache, value_cache)
+    by_column = [i for group in ((2,), (0, 1)) for i in group]
+    parts = tuple((plan[i][0] // DH, 0 if i else kv_width) for i in by_column)
+    mine, theirs = [mine[i] for i in by_column], [theirs[i] for i in by_column]
+    keys, values = caches[:own_rows], caches[own_rows:]
+    own, other, *out_rest = attend(
+        core, lengths, mine, theirs, parts, keys, values, out_weight, out_cuts[early:]
+    )
+    out_held = [*out_first, *out_rest]
     got = swap(other)
     block = jnp.where(core == 0, jnp.concatenate([own, got]), jnp.concatenate([got, own]))
 
@@ -354,12 +424,12 @@
     orders = [order_of(path[::-1]) for path in paths]
     blocks = [b for pair in zip(near, far) for b in pair]
     total_columns = out_weight.shape[1]
-    cuts = 2 if total_columns % 768 == 0 else 1
-    columns = total_columns // cuts
+    last = 768 if total_columns % 768 == 0 and total_columns > 768 else 0
     results = []
-    for cut in range(cuts):
-        send, keep = project_out(orders, rows, ids, blocks, out_weight, cut * columns, columns)
-        results.append((keep + swap(send)).astype(jnp.bfloat16))
+    for columns in ((0, total_columns - last), (total_columns - last, last)):
+        if columns[1]:
+            send, keep = project_out(orders, rows, ids, blocks, out_held, out_cuts, columns)
+            results.append((keep + swap(send)).astype(jnp.bfloat16))
     return jnp.concatenate(results, axis=1)
 
 

time: 90.2 us -> 101 us (1.12)
  local copies, waits for them, and re-layouts: 1.76 us -> 20.1 us
  waiting for transfers between devices: 36.8 us -> 29.9 us
  starting transfers between devices: 20.8 us -> 17.2 us
  other arithmetic: 2.18 us -> 4.4 us
    unnamed x4 -> x62, local copies, waits for them, and re-layouts: 1.67 us -> 18.8 us
    ppermute x15, waiting for transfers between devices: 33.1 us -> 26.2 us  [across(): return lax.ppermute(array, 'gx', [(g, g ^ mask) for g in range(n)])]
    ppermute x15, starting transfers between devices: 19.3 us -> 15.8 us  [across(): return lax.ppermute(array, 'gx', [(g, g ^ mask) for g in range(n)])]
    pallas_call x1 -> x2, Pallas kernels: 9.48 us -> 12.3 us  [project(): pl.pallas_call(functools.partial(project_kernel, orders, rows, first, wid...]
    pallas_call x3 -> x5, Pallas kernels: 18.8 us -> 16.2 us  [the longest x2 5.71 us: load(): pl.pallas_call(functools.partial(load_kernel, len(after), cuts, len(array...]
    add x0 -> x2, other arithmetic: none -> 2.29 us  [local(): total = total + zero]
    slice x0 -> x2, local copies, waits for them, and re-layouts: none -> 1.14 us  [load(): return (held, zero[0, 0])]
  transfers between devices with their start and end apart: 22 -> 22, of which waited for: 15 -> 12; matrix products, arithmetic and copies ran while one was open for 2% -> 5% of each run, Pallas kernels for 6% -> 16%
where the time goes in v6:
time: 101 us
  waiting for transfers between devices  29.9 us (30%)
  Pallas kernels  28.5 us (28%)
  local copies, waits for them, and re-layouts  20.1 us (20%)
  starting transfers between devices  17.2 us (17%)
  other arithmetic  4.4 us (4%)
    ppermute x15, waiting for transfers between devices, across(): return lax.ppermute(array, 'gx', [(g, g ^ mask) for g in range(n)])  26.2 us
    unnamed x62, local copies, waits for them, and re-layouts  18.8 us
    ppermute x15, starting transfers between devices, across(): return lax.ppermute(array, 'gx', [(g, g ^ mask) for g in range(n)])  15.8 us
    pallas_call x2, Pallas kernels, project(): pl.pallas_call(functools.partial(project_kernel, orders, rows, first, wid...  12.3 us
    pallas_call x2, Pallas kernels, load(): pl.pallas_call(functools.partial(load_kernel, len(after), cuts, len(array...  5.71 us
    pallas_call x1, Pallas kernels, attend(): pl.pallas_call(functools.partial(attend_kernel, parts, rows, cuts), out_s...  5.68 us
    pallas_call x2, Pallas kernels, project_out(): pl.pallas_call(functools.partial(output_kernel, orders, rows, columns, pi...  4.83 us
    ppermute x7, waiting for transfers between devices, swap(): return lax.ppermute(array, 'gy', [(0, 1), (1, 0)])  3.76 us
  transfers between devices with their start and end apart: 22, of which 12 were waited for; matrix products, arithmetic and copies ran while one was open for 5% of the time, Pallas kernels for 16%

profile of v6, /device:TPU:0, one launch (start us, length us, event | category | flops | bytes accessed | tf_op | source)
XLA Modules:
  0.0 100.6 jit_solution(2185313051077030097)
XLA Ops:
  1.9 4.4 %project.2 = (f32[64,1024]{1,0:T(8,128)S(1)}, f32[64,1024]{1,0:T(8,128)S(1)}) custom-call(s32[2]{0:T(128)S(1)} %pad_add_fusion.ids_ref, bf16[64,2304]{1,0:T(8,128)(2,1)S(1)} %broadcast_select_fusion.own_ref, bf16[64,2304]{1,0:T(8,128)(2,1)S(1)} %collective-permute-done.other_ref, bf16[2304,3072]{1,0:T(8,128)(2,1)} %w_ref.3), custom_call_target="tpu_custom_call" | custom-call | flops 603979776 | bytes 5242880 | tf_op jit(solution)/shard_map/project/pallas_call | solution.py:185
  6.3 3.0 %collective-permute-start.1 = (f32[64,1024]{1,0:T(8,128)S(1)}, f32[64,1024]{1,0:T(8,128)S(1)}, u32[]{:S(2)}, u32[]{:S(2)}) collective-permute-start(f32[64,1024]{1,0:T(8,128)S(1)} %get-tuple-element.54.refs_1_), channel_id=1, source_target_pairs={{0,4},{2,6},{4,0},{6,2},{8,12},{10,14},{12,8},{14,10},{1,5},{3,7},... | collective-permute-start | bytes 786440 | tf_op jit(solution)/shard_map/ppermute | solution.py:358
  9.3 7.9 %project.3 = (f32[64,1024]{1,0:T(8,128)S(1)}, f32[64,1024]{1,0:T(8,128)S(1)}, f32[64,1280]{1,0:T(8,128)}, f32[64,1280]{1,0:T(8,128)S(1)}) custom-call(s32[2]{0:T(128)S(1)} %pad_add_fusion.ids_ref, bf16[64,2304]{1,0:T(8,128)(2,1)S(1)} %broadcast_select_fusion.own_ref, bf16[64,2304]{1,0:T(8,128)(2,1)S(1)} %collective-permute-done.other_ref, ...), custom_call_target="tpu_custom_call" | custom-call | flops 1358954496 | bytes 11796480 | tf_op jit(solution)/shard_map/project/pallas_call | solution.py:185
  17.2 1.6 %collective-permute-start.4 = (f32[64,1024]{1,0:T(8,128)S(1)}, f32[64,1024]{1,0:T(8,128)S(1)}, u32[]{:S(2)}, u32[]{:S(2)}) collective-permute-start(f32[64,1024]{1,0:T(8,128)S(1)} %get-tuple-element.56), channel_id=1, source_target_pairs={{0,2},{2,0},{4,6},{6,4},{8,10},{10,8},{12,14},{14,12},{1,3},{3,1},... | collective-permute-start | bytes 786440 | tf_op jit(solution)/shard_map/ppermute | solution.py:358
  19.4 2.2 %copy-done = bf16[8,1024,256]{2,1,0:T(8,128)(2,1)S(1)} copy-done((bf16[8,1024,256]{2,1,0:T(8,128)(2,1)S(1)}, bf16[8,1024,256]{2,1,0:T(8,128)(2,1)}, u32[]{:S(2)}) %copy-start) | copy-done | bytes 4194328
  21.6 2.6 %load.2 = (bf16[1024,256]{1,0:T(8,128)(2,1)S(1)}, bf16[1024,256]{1,0:T(8,128)(2,1)S(1)}, bf16[1024,256]{1,0:T(8,128)(2,1)S(1)}, bf16[1024,256]{1,0:T(8,128)(2,1)...) custom-call(f32[32,1024]{1,0:T(8,128)S(1)} %slice.65.refs_0_, ...), custom_call_target="tpu_custom_call" | custom-call | bytes 16777216 | tf_op jit(solution)/shard_map/load/pallas_call | solution.py:78
  24.8 1.6 %collective-permute-done.4 = f32[64,1024]{1,0:T(8,128)S(1)} collective-permute-done((f32[64,1024]{1,0:T(8,128)S(1)}, f32[64,1024]{1,0:T(8,128)S(1)}, u32[]{:S(2)}, u32[]{:S(2)}) %collective-permute-start.4) | collective-permute-done | bytes 262176 | tf_op jit(solution)/shard_map/ppermute | solution.py:358
  27.2 2.7 %collective-permute-start.5 = (f32[32,1024]{1,0:T(8,128)S(1)}, f32[32,1024]{1,0:T(8,128)S(1)}, u32[]{:S(2)}, u32[]{:S(2)}) collective-permute-start(f32[32,1024]{1,0:T(8,128)S(1)} %slice.69.refs_0_), channel_id=1, source_target_pairs={{0,8},{2,10},{4,12},{6,14},{8,0},{10,2},{12,4},{14,6},{1,9},{3,11}... | collective-permute-start | bytes 393224 | tf_op jit(solution)/shard_map/ppermute | solution.py:358
  29.9 3.1 %load.3 = (bf16[512,768]{1,0:T(8,128)(2,1)S(1)}, bf16[512,768]{1,0:T(8,128)(2,1)S(1)}, bf16[512,768]{1,0:T(8,128)(2,1)S(1)}, bf16[512,768]{1,0:T(8,128)(2,1)S(1)...) custom-call(f32[32,1024]{1,0:T(8,128)S(1)} %slice.69.refs_0_, ...), custom_call_target="tpu_custom_call" | custom-call | bytes 14155776 | tf_op jit(solution)/shard_map/load/pallas_call | solution.py:78
  35.4 1.6 %add_add_fusion = f32[64,1280]{1,0:T(8,128)S(1)} fusion(f32[64,1280]{1,0:T(8,128)S(1)} %get-tuple-element.58, f32[64,1280]{1,0:T(8,128)} %collective-permute-done.7, f32[]{:T(128)} %bitcast.3), kind=kLoop, calls=%fused_computation.1 | loop fusion | flops 163840 | bytes 983044 | tf_op jit(solution)/shard_map/add | solution.py:391
  37.0 1.6 %collective-permute-start.8 = (f32[32,1280]{1,0:T(8,128)S(1)}, f32[32,1280]{1,0:T(8,128)S(1)}, u32[]{:S(2)}, u32[]{:S(2)}) collective-permute-start(f32[32,1280]{1,0:T(8,128)S(1)} %slice.73), channel_id=1, source_target_pairs={{0,2},{2,0},{4,6},{6,4},{8,10},{10,8},{12,14},{14,12},{1,3},{3,1},... | collective-permute-start | bytes 491528 | tf_op jit(solution)/shard_map/ppermute | solution.py:358
  39.5 4.9 %collective-permute-done.3 = f32[16,1024]{1,0:T(8,128)S(1)} collective-permute-done((f32[16,1024]{1,0:T(8,128)S(1)}, f32[16,1024]{1,0:T(8,128)S(1)}, u32[]{:S(2)}, u32[]{:S(2)}) %collective-permute-start.3) | collective-permute-done | bytes 65568 | tf_op jit(solution)/shard_map/ppermute | solution.py:358
  44.6 1.5 %collective-permute-start.9 = (f32[16,1280]{1,0:T(8,128)S(1)}, f32[16,1280]{1,0:T(8,128)S(1)}, u32[]{:S(2)}, u32[]{:S(2)}) collective-permute-start(f32[16,1280]{1,0:T(8,128)S(1)} %slice.75), channel_id=1, source_target_pairs={{0,8},{2,10},{4,12},{6,14},{8,0},{10,2},{12,4},{14,6},{1,9},{3,11}... | collective-permute-start | bytes 245768 | tf_op jit(solution)/shard_map/ppermute | solution.py:358
  46.1 5.4 %collective-permute-done.9 = f32[16,1280]{1,0:T(8,128)S(1)} collective-permute-done((f32[16,1280]{1,0:T(8,128)S(1)}, f32[16,1280]{1,0:T(8,128)S(1)}, u32[]{:S(2)}, u32[]{:S(2)}) %collective-permute-start.9) | collective-permute-done | bytes 81952 | tf_op jit(solution)/shard_map/ppermute | solution.py:358
  51.8 1.0 %collective-permute-done.12.refs_5_ = bf16[8,1280]{1,0:T(8,128)(2,1)S(1)} collective-permute-done((bf16[8,1280]{1,0:T(8,128)(2,1)S(1)}, bf16[8,1280]{1,0:T(8,128)(2,1)S(1)}, u32[]{:S(2)}, u32[]{:S(2)}) %collective-permute-start.12) | collective-permute-done | bytes 20512 | tf_op jit(solution)/shard_map/ppermute | solution.py:355
  52.8 5.7 %attend.1 = (bf16[8,3072]{1,0:T(8,128)(2,1)S(1)}, bf16[8,3072]{1,0:T(8,128)(2,1)S(1)}, bf16[512,768]{1,0:T(8,128)(2,1)S(1)}, bf16[512,768]{1,0:T(8,128)(2,1)S(1)...) custom-call(s32[9]{0:T(128)S(1)} %pad_add_fusion.1.scalars_ref, ...), custom_call_target="tpu_custom_call" | custom-call | flops 201326592 | bytes 8388608 | tf_op jit(solution)/shard_map/attend/pallas_call | solution.py:263
  66.7 1.0 %collective-permute-done.13 = bf16[8,3072]{1,0:T(8,128)(2,1)S(1)} collective-permute-done((bf16[8,3072]{1,0:T(8,128)(2,1)S(1)}, bf16[8,3072]{1,0:T(8,128)(2,1)S(1)}, u32[]{:S(2)}, u32[]{:S(2)}) %collective-permute-start.13) | collective-permute-done | bytes 49184 | tf_op jit(solution)/shard_map/ppermute | solution.py:355
  68.5 4.4 %collective-permute-done.14 = bf16[16,1536]{1,0:T(8,128)(2,1)S(1)} collective-permute-done((bf16[16,1536]{1,0:T(8,128)(2,1)S(1)}, bf16[16,1536]{1,0:T(8,128)(2,1)S(1)}, u32[]{:S(2)}, u32[]{:S(2)}) %collective-permute-start.14) | collective-permute-done | bytes 49184 | tf_op jit(solution)/shard_map/ppermute | solution.py:358
  73.0 2.3 %collective-permute-start.18 = (bf16[32,1536]{1,0:T(8,128)(2,1)S(1)}, bf16[32,1536]{1,0:T(8,128)(2,1)S(1)}, u32[]{:S(2)}, u32[]{:S(2)}) collective-permute-start(bf16[32,1536]{1,0:T(8,128)(2,1)S(1)} %pad_maximum_fusion.4), channel_id=1, source_target_pairs={{0,8},{2,10},{4,12},{6,14},{8,0},{10,2},{12,4},{14,6},{1,9},{3,11}... | collective-permute-start | bytes 294920 | tf_op jit(solution)/shard_map/ppermute | solution.py:358
  75.3 2.7 %collective-permute-done.15 = bf16[32,1536]{1,0:T(8,128)(2,1)S(1)} collective-permute-done((bf16[32,1536]{1,0:T(8,128)(2,1)S(1)}, bf16[32,1536]{1,0:T(8,128)(2,1)S(1)}, u32[]{:S(2)}, u32[]{:S(2)}) %collective-permute-start.15) | collective-permute-done | bytes 98336 | tf_op jit(solution)/shard_map/ppermute | solution.py:358
  78.6 1.7 %collective-permute-done.18 = bf16[32,1536]{1,0:T(8,128)(2,1)S(1)} collective-permute-done((bf16[32,1536]{1,0:T(8,128)(2,1)S(1)}, bf16[32,1536]{1,0:T(8,128)(2,1)S(1)}, u32[]{:S(2)}, u32[]{:S(2)}) %collective-permute-start.18) | collective-permute-done | bytes 98336 | tf_op jit(solution)/shard_map/ppermute | solution.py:358
  80.7 3.0 %collective-permute-done.16.refs_1_ = bf16[64,1536]{1,0:T(8,128)(2,1)S(1)} collective-permute-done((bf16[64,1536]{1,0:T(8,128)(2,1)S(1)}, bf16[64,1536]{1,0:T(8,128)(2,1)S(1)}, u32[]{:S(2)}, u32[]{:S(2)}) %collective-permute-start.16) | collective-permute-done | bytes 196640 | tf_op jit(solution)/shard_map/ppermute | solution.py:358
  83.8 2.3 %collective-permute-done.19.refs_3_ = bf16[64,1536]{1,0:T(8,128)(2,1)S(1)} collective-permute-done((bf16[64,1536]{1,0:T(8,128)(2,1)S(1)}, bf16[64,1536]{1,0:T(8,128)(2,1)S(1)}, u32[]{:S(2)}, u32[]{:S(2)}) %collective-permute-start.19) | collective-permute-done | bytes 196640 | tf_op jit(solution)/shard_map/ppermute | solution.py:358
  86.1 1.1 %copy-done.19 = bf16[512,768]{1,0:T(8,128)(2,1)S(1)} copy-done((bf16[512,768]{1,0:T(8,128)(2,1)S(1)}, bf16[512,768]{1,0:T(8,128)(2,1)}, u32[]{:S(2)}) %copy-start.19) | copy-done | bytes 786456
  87.2 1.1 %copy-done.21 = bf16[512,768]{1,0:T(8,128)(2,1)S(1)} copy-done((bf16[512,768]{1,0:T(8,128)(2,1)S(1)}, bf16[512,768]{1,0:T(8,128)(2,1)}, u32[]{:S(2)}) %copy-start.21) | copy-done | bytes 786456
  88.4 1.1 %copy-done.23 = bf16[512,768]{1,0:T(8,128)(2,1)S(1)} copy-done((bf16[512,768]{1,0:T(8,128)(2,1)S(1)}, bf16[512,768]{1,0:T(8,128)(2,1)}, u32[]{:S(2)}) %copy-start.23) | copy-done | bytes 786456
  89.5 1.1 %copy-done.25 = bf16[512,768]{1,0:T(8,128)(2,1)S(1)} copy-done((bf16[512,768]{1,0:T(8,128)(2,1)S(1)}, bf16[512,768]{1,0:T(8,128)(2,1)}, u32[]{:S(2)}) %copy-start.25) | copy-done | bytes 786456
  90.6 1.1 %copy-done.27 = bf16[512,768]{1,0:T(8,128)(2,1)S(1)} copy-done((bf16[512,768]{1,0:T(8,128)(2,1)S(1)}, bf16[512,768]{1,0:T(8,128)(2,1)}, u32[]{:S(2)}) %copy-start.27) | copy-done | bytes 786456
  91.8 1.1 %copy-done.29 = bf16[512,768]{1,0:T(8,128)(2,1)S(1)} copy-done((bf16[512,768]{1,0:T(8,128)(2,1)S(1)}, bf16[512,768]{1,0:T(8,128)(2,1)}, u32[]{:S(2)}) %copy-start.29) | copy-done | bytes 786456
  92.9 2.1 %project_out.3 = (f32[64,768]{1,0:T(8,128)S(1)}, f32[64,768]{1,0:T(8,128)S(1)}) custom-call(s32[2]{0:T(128)S(1)} %pad_add_fusion.ids_ref, bf16[64,1536]{1,0:T(8,128)(2,1)S(1)} %pad_maximum_fusion.1.refs_0_, bf16[64,1536]{1,0:T(8,128)(2,1)S(1)} %collective-permute-done.16.refs_1_, bf16[64,1536]{1,0:T(8,128)(2,1)S(1)} %pad_maximum_fusion.2.refs_2_, ...), custom_call_target="tpu_custom_call" | custom-call | flops 603979776 | bytes 5111808 | tf_op jit(solution)/shard_map/project_out/pallas_call | solution.py:326
  95.1 2.7 %project_out.2 = (f32[64,1536]{1,0:T(8,128)S(1)}, f32[64,1536]{1,0:T(8,128)S(1)}) custom-call(s32[2]{0:T(128)S(1)} %pad_add_fusion.ids_ref, bf16[64,1536]{1,0:T(8,128)(2,1)S(1)} %pad_maximum_fusion.1.refs_0_, bf16[64,1536]{1,0:T(8,128)(2,1)S(1)} %collective-permute-done.16.refs_1_, bf16[64,1536]{1,0:T(8,128)(2,1)S(1)} %pad_maximum_fusion.2.refs_2_, ...), custom_call_target="tpu_custom_call" | custom-call | flops 1207959552 | bytes 10223616 | tf_op jit(solution)/shard_map/project_out/pallas_call | solution.py:326
  98.5 1.3 %collective-permute-done.20 = f32[64,1536]{1,0:T(8,128)S(1)} collective-permute-done((f32[64,1536]{1,0:T(8,128)S(1)}, f32[64,1536]{1,0:T(8,128)S(1)}, u32[]{:S(2)}, u32[]{:S(2)}) %collective-permute-start.20) | collective-permute-done | bytes 393248 | tf_op jit(solution)/shard_map/ppermute | solution.py:355
  (113 shorter events, 18.9 us)
Async XLA Ops:
  0.0 1.9 %collective-permute-start = (bf16[64,2304]{1,0:T(8,128)(2,1)}, bf16[64,2304]{1,0:T(8,128)(2,1)S(1)}, u32[]{:S(2)}, u32[]{:S(2)}) collective-permute-start(bf16[64,2304]{1,0:T(8,128)(2,1)} %param.7), channel_id=1, source_target_pairs={{0,1},{1,0},{2,3},{3,2},{4,5},{5,4},{6,7},{7,6},{8,9},{9,8},{10,11... | collective-permute-start | bytes 884744 | tf_op jit(solution)/shard_map/ppermute | solution.py:355
  6.3 13.0 %collective-permute-start.1 = (f32[64,1024]{1,0:T(8,128)S(1)}, f32[64,1024]{1,0:T(8,128)S(1)}, u32[]{:S(2)}, u32[]{:S(2)}) collective-permute-start(f32[64,1024]{1,0:T(8,128)S(1)} %get-tuple-element.54.refs_1_), channel_id=1, source_target_pairs={{0,4},{2,6},{4,0},{6,2},{8,12},{10,14},{12,8},{14,10},{1,5},{3,7},... | collective-permute-start | bytes 786440 | tf_op jit(solution)/shard_map/ppermute | solution.py:358
  17.2 9.3 %collective-permute-start.4 = (f32[64,1024]{1,0:T(8,128)S(1)}, f32[64,1024]{1,0:T(8,128)S(1)}, u32[]{:S(2)}, u32[]{:S(2)}) collective-permute-start(f32[64,1024]{1,0:T(8,128)S(1)} %get-tuple-element.56), channel_id=1, source_target_pairs={{0,2},{2,0},{4,6},{6,4},{8,10},{10,8},{12,14},{14,12},{1,3},{3,1},... | collective-permute-start | bytes 786440 | tf_op jit(solution)/shard_map/ppermute | solution.py:358
  18.8 16.6 %collective-permute-start.7 = (f32[64,1280]{1,0:T(8,128)}, f32[64,1280]{1,0:T(8,128)}, u32[]{:S(2)}, u32[]{:S(2)}) collective-permute-start(f32[64,1280]{1,0:T(8,128)} %get-tuple-element.59), channel_id=1, source_target_pairs={{0,4},{2,6},{4,0},{6,2},{8,12},{10,14},{12,8},{14,10},{1,5},{3,7},... | collective-permute-start | bytes 983048 | tf_op jit(solution)/shard_map/ppermute | solution.py:358
  19.3 19.3 %collective-permute-start.2 = (f32[32,1024]{1,0:T(8,128)S(1)}, f32[32,1024]{1,0:T(8,128)S(1)}, u32[]{:S(2)}, u32[]{:S(2)}) collective-permute-start(f32[32,1024]{1,0:T(8,128)S(1)} %slice.65.refs_0_), channel_id=1, source_target_pairs={{0,2},{2,0},{4,6},{6,4},{8,10},{10,8},{12,14},{14,12},{1,3},{3,1},... | collective-permute-start | bytes 393224 | tf_op jit(solution)/shard_map/ppermute | solution.py:358
  27.2 24.5 %copy-start.30 = (s32[8]{0:T(128)S(1)}, s32[8]{0:T(128)}, u32[]{:S(2)}) copy-start(s32[8]{0:T(128)} %param.13) | copy-start | bytes 100
  27.2 11.8 %collective-permute-start.5 = (f32[32,1024]{1,0:T(8,128)S(1)}, f32[32,1024]{1,0:T(8,128)S(1)}, u32[]{:S(2)}, u32[]{:S(2)}) collective-permute-start(f32[32,1024]{1,0:T(8,128)S(1)} %slice.69.refs_0_), channel_id=1, source_target_pairs={{0,8},{2,10},{4,12},{6,14},{8,0},{10,2},{12,4},{14,6},{1,9},{3,11}... | collective-permute-start | bytes 393224 | tf_op jit(solution)/shard_map/ppermute | solution.py:358
  34.8 18.0 %copy-start.22 = (bf16[512,768]{1,0:T(8,128)(2,1)}, bf16[512,768]{1,0:T(8,128)(2,1)S(1)}, u32[]{:S(2)}) copy-start(bf16[512,768]{1,0:T(8,128)(2,1)S(1)} %get-tuple-element.95.refs_6_) | copy-start | bytes 2359300
  37.0 7.6 %collective-permute-start.8 = (f32[32,1280]{1,0:T(8,128)S(1)}, f32[32,1280]{1,0:T(8,128)S(1)}, u32[]{:S(2)}, u32[]{:S(2)}) collective-permute-start(f32[32,1280]{1,0:T(8,128)S(1)} %slice.73), channel_id=1, source_target_pairs={{0,2},{2,0},{4,6},{6,4},{8,10},{10,8},{12,14},{14,12},{1,3},{3,1},... | collective-permute-start | bytes 491528 | tf_op jit(solution)/shard_map/ppermute | solution.py:358
  38.6 5.8 %collective-permute-start.3 = (f32[16,1024]{1,0:T(8,128)S(1)}, f32[16,1024]{1,0:T(8,128)S(1)}, u32[]{:S(2)}, u32[]{:S(2)}) collective-permute-start(f32[16,1024]{1,0:T(8,128)S(1)} %slice.67), channel_id=1, source_target_pairs={{0,8},{2,10},{4,12},{6,14},{8,0},{10,2},{12,4},{14,6},{1,9},{3,11}... | collective-permute-start | bytes 196616 | tf_op jit(solution)/shard_map/ppermute | solution.py:358
  39.0 5.5 %collective-permute-start.6 = (f32[16,1024]{1,0:T(8,128)S(1)}, f32[16,1024]{1,0:T(8,128)S(1)}, u32[]{:S(2)}, u32[]{:S(2)}) collective-permute-start(f32[16,1024]{1,0:T(8,128)S(1)} %slice.71), channel_id=1, source_target_pairs={{0,4},{2,6},{4,0},{6,2},{8,12},{10,14},{12,8},{14,10},{1,5},{3,7},... | collective-permute-start | bytes 196616 | tf_op jit(solution)/shard_map/ppermute | solution.py:358
  44.4 7.3 %collective-permute-start.10 = (bf16[8,1024]{1,0:T(8,128)(2,1)S(1)}, bf16[8,1024]{1,0:T(8,128)(2,1)S(1)}, u32[]{:S(2)}, u32[]{:S(2)}) collective-permute-start(bf16[8,1024]{1,0:T(8,128)(2,1)S(1)} %get-tuple-element.107), channel_id=1, source_target_pairs={{0,1},{1,0},{2,3},{3,2},{4,5},{5,4},{6,7},{7,6},{8,9},{9,8},{10,11... | collective-permute-start | bytes 49160 | tf_op jit(solution)/shard_map/ppermute | solution.py:355
  44.6 6.9 %collective-permute-start.9 = (f32[16,1280]{1,0:T(8,128)S(1)}, f32[16,1280]{1,0:T(8,128)S(1)}, u32[]{:S(2)}, u32[]{:S(2)}) collective-permute-start(f32[16,1280]{1,0:T(8,128)S(1)} %slice.75), channel_id=1, source_target_pairs={{0,8},{2,10},{4,12},{6,14},{8,0},{10,2},{12,4},{14,6},{1,9},{3,11}... | collective-permute-start | bytes 245768 | tf_op jit(solution)/shard_map/ppermute | solution.py:358
  46.1 5.7 %collective-permute-start.11 = (bf16[8,1024]{1,0:T(8,128)(2,1)S(1)}, bf16[8,1024]{1,0:T(8,128)(2,1)S(1)}, u32[]{:S(2)}, u32[]{:S(2)}) collective-permute-start(bf16[8,1024]{1,0:T(8,128)(2,1)S(1)} %get-tuple-element.105), channel_id=1, source_target_pairs={{0,1},{1,0},{2,3},{3,2},{4,5},{5,4},{6,7},{7,6},{8,9},{9,8},{10,11... | collective-permute-start | bytes 49160 | tf_op jit(solution)/shard_map/ppermute | solution.py:355
  51.6 1.3 %collective-permute-start.12 = (bf16[8,1280]{1,0:T(8,128)(2,1)S(1)}, bf16[8,1280]{1,0:T(8,128)(2,1)S(1)}, u32[]{:S(2)}, u32[]{:S(2)}) collective-permute-start(bf16[8,1280]{1,0:T(8,128)(2,1)S(1)} %get-tuple-element.103), channel_id=1, source_target_pairs={{0,1},{1,0},{2,3},{3,2},{4,5},{5,4},{6,7},{7,6},{8,9},{9,8},{10,11... | collective-permute-start | bytes 61448 | tf_op jit(solution)/shard_map/ppermute | solution.py:355
  66.5 1.2 %collective-permute-start.13 = (bf16[8,3072]{1,0:T(8,128)(2,1)S(1)}, bf16[8,3072]{1,0:T(8,128)(2,1)S(1)}, u32[]{:S(2)}, u32[]{:S(2)}) collective-permute-start(bf16[8,3072]{1,0:T(8,128)(2,1)S(1)} %get-tuple-element.78), channel_id=1, source_target_pairs={{0,1},{1,0},{2,3},{3,2},{4,5},{5,4},{6,7},{7,6},{8,9},{9,8},{10,11... | collective-permute-start | bytes 147464 | tf_op jit(solution)/shard_map/ppermute | solution.py:355
  66.7 28.4 %copy-start.3 = (bf16[512,768]{1,0:T(8,128)(2,1)S(1)}, bf16[512,768]{1,0:T(8,128)(2,1)}, u32[]{:S(2)}) copy-start(bf16[512,768]{1,0:T(8,128)(2,1)} %copy-done.2) | copy-start | bytes 2359300
  66.7 28.4 %copy-start.5 = (bf16[512,768]{1,0:T(8,128)(2,1)S(1)}, bf16[512,768]{1,0:T(8,128)(2,1)}, u32[]{:S(2)}) copy-start(bf16[512,768]{1,0:T(8,128)(2,1)} %copy-done.4) | copy-start | bytes 2359300
  66.7 28.4 %copy-start.7 = (bf16[512,768]{1,0:T(8,128)(2,1)S(1)}, bf16[512,768]{1,0:T(8,128)(2,1)}, u32[]{:S(2)}) copy-start(bf16[512,768]{1,0:T(8,128)(2,1)} %copy-done.6) | copy-start | bytes 2359300
  66.7 28.4 %copy-start.9 = (bf16[512,768]{1,0:T(8,128)(2,1)S(1)}, bf16[512,768]{1,0:T(8,128)(2,1)}, u32[]{:S(2)}) copy-start(bf16[512,768]{1,0:T(8,128)(2,1)} %copy-done.8) | copy-start | bytes 2359300
  66.7 28.4 %copy-start.11 = (bf16[512,768]{1,0:T(8,128)(2,1)S(1)}, bf16[512,768]{1,0:T(8,128)(2,1)}, u32[]{:S(2)}) copy-start(bf16[512,768]{1,0:T(8,128)(2,1)} %copy-done.10) | copy-start | bytes 2359300
  66.7 28.4 %copy-start.13 = (bf16[512,768]{1,0:T(8,128)(2,1)S(1)}, bf16[512,768]{1,0:T(8,128)(2,1)}, u32[]{:S(2)}) copy-start(bf16[512,768]{1,0:T(8,128)(2,1)} %copy-done.12) | copy-start | bytes 2359300
  66.7 28.4 %copy-start.15 = (bf16[512,768]{1,0:T(8,128)(2,1)S(1)}, bf16[512,768]{1,0:T(8,128)(2,1)}, u32[]{:S(2)}) copy-start(bf16[512,768]{1,0:T(8,128)(2,1)} %copy-done.14) | copy-start | bytes 2359300
  66.7 28.4 %copy-start.17 = (bf16[512,768]{1,0:T(8,128)(2,1)S(1)}, bf16[512,768]{1,0:T(8,128)(2,1)}, u32[]{:S(2)}) copy-start(bf16[512,768]{1,0:T(8,128)(2,1)} %copy-done.16) | copy-start | bytes 2359300
  67.8 5.1 %collective-permute-start.14 = (bf16[16,1536]{1,0:T(8,128)(2,1)S(1)}, bf16[16,1536]{1,0:T(8,128)(2,1)S(1)}, u32[]{:S(2)}, u32[]{:S(2)}) collective-permute-start(bf16[16,1536]{1,0:T(8,128)(2,1)S(1)} %get-tuple-element.102), channel_id=1, source_target_pairs={{0,8},{2,10},{4,12},{6,14},{8,0},{10,2},{12,4},{14,6},{1,9},{3,11}... | collective-permute-start | bytes 147464 | tf_op jit(solution)/shard_map/ppermute | solution.py:358
  67.9 5.1 %collective-permute-start.17 = (bf16[16,1536]{1,0:T(8,128)(2,1)S(1)}, bf16[16,1536]{1,0:T(8,128)(2,1)S(1)}, u32[]{:S(2)}, u32[]{:S(2)}) collective-permute-start(bf16[16,1536]{1,0:T(8,128)(2,1)S(1)} %get-tuple-element.101), channel_id=1, source_target_pairs={{0,2},{2,0},{4,6},{6,4},{8,10},{10,8},{12,14},{14,12},{1,3},{3,1},... | collective-permute-start | bytes 147464 | tf_op jit(solution)/shard_map/ppermute | solution.py:358
  72.9 5.1 %collective-permute-start.15 = (bf16[32,1536]{1,0:T(8,128)(2,1)S(1)}, bf16[32,1536]{1,0:T(8,128)(2,1)S(1)}, u32[]{:S(2)}, u32[]{:S(2)}) collective-permute-start(bf16[32,1536]{1,0:T(8,128)(2,1)S(1)} %pad_maximum_fusion.3), channel_id=1, source_target_pairs={{0,4},{2,6},{4,0},{6,2},{8,12},{10,14},{12,8},{14,10},{1,5},{3,7},... | collective-permute-start | bytes 294920 | tf_op jit(solution)/shard_map/ppermute | solution.py:358
  73.0 7.4 %collective-permute-start.18 = (bf16[32,1536]{1,0:T(8,128)(2,1)S(1)}, bf16[32,1536]{1,0:T(8,128)(2,1)S(1)}, u32[]{:S(2)}, u32[]{:S(2)}) collective-permute-start(bf16[32,1536]{1,0:T(8,128)(2,1)S(1)} %pad_maximum_fusion.4), channel_id=1, source_target_pairs={{0,8},{2,10},{4,12},{6,14},{8,0},{10,2},{12,4},{14,6},{1,9},{3,11}... | collective-permute-start | bytes 294920 | tf_op jit(solution)/shard_map/ppermute | solution.py:358
  78.0 5.7 %collective-permute-start.16 = (bf16[64,1536]{1,0:T(8,128)(2,1)S(1)}, bf16[64,1536]{1,0:T(8,128)(2,1)S(1)}, u32[]{:S(2)}, u32[]{:S(2)}) collective-permute-start(bf16[64,1536]{1,0:T(8,128)(2,1)S(1)} %pad_maximum_fusion.1.refs_0_), channel_id=1, source_target_pairs={{0,2},{2,0},{4,6},{6,4},{8,10},{10,8},{12,14},{14,12},{1,3},{3,1},... | collective-permute-start | bytes 589832 | tf_op jit(solution)/shard_map/ppermute | solution.py:358
  80.4 5.7 %collective-permute-start.19 = (bf16[64,1536]{1,0:T(8,128)(2,1)S(1)}, bf16[64,1536]{1,0:T(8,128)(2,1)S(1)}, u32[]{:S(2)}, u32[]{:S(2)}) collective-permute-start(bf16[64,1536]{1,0:T(8,128)(2,1)S(1)} %pad_maximum_fusion.2.refs_2_), channel_id=1, source_target_pairs={{0,4},{2,6},{4,0},{6,2},{8,12},{10,14},{12,8},{14,10},{1,5},{3,7},... | collective-permute-start | bytes 589832 | tf_op jit(solution)/shard_map/ppermute | solution.py:358
  95.0 3.5 %collective-permute-start.21 = (f32[64,768]{1,0:T(8,128)S(1)}, f32[64,768]{1,0:T(8,128)S(1)}, u32[]{:S(2)}, u32[]{:S(2)}) collective-permute-start(f32[64,768]{1,0:T(8,128)S(1)} %get-tuple-element.100), channel_id=1, source_target_pairs={{0,1},{1,0},{2,3},{3,2},{4,5},{5,4},{6,7},{7,6},{8,9},{9,8},{10,11... | collective-permute-start | bytes 589832 | tf_op jit(solution)/shard_map/ppermute | solution.py:355
  97.9 1.9 %collective-permute-start.20 = (f32[64,1536]{1,0:T(8,128)S(1)}, f32[64,1536]{1,0:T(8,128)S(1)}, u32[]{:S(2)}, u32[]{:S(2)}) collective-permute-start(f32[64,1536]{1,0:T(8,128)S(1)} %get-tuple-element.92), channel_id=1, source_target_pairs={{0,1},{1,0},{2,3},{3,2},{4,5},{5,4},{6,7},{7,6},{8,9},{9,8},{10,11... | collective-permute-start | bytes 1179656 | tf_op jit(solution)/shard_map/ppermute | solution.py:355
  (21 other events, 62.6 us)

commit v7 on v6

--- a/solution.py
+++ b/solution.py
@@ -73,11 +73,11 @@
         copy.wait()
 
 
-def load(arrays, cuts, after, grant):
+def load(arrays, cuts, after, grant, zeros=128):
     shapes = [piece_of(arrays[at], cut) for at, cut in cuts]
     *held, zero = pl.pallas_call(
         functools.partial(load_kernel, len(after), cuts, len(arrays)),
-        out_shape=(*shapes, jax.ShapeDtypeStruct((8, 128), jnp.float32)),
+        out_shape=(*shapes, jax.ShapeDtypeStruct((1, zeros), jnp.float32)),
         in_specs=[ANY] * len(after) + [HBM] * len(arrays),
         out_specs=[VMEM] * (len(cuts) + 1),
         scratch_shapes=[pltpu.SemaphoreType.DMA((len(cuts),))],
@@ -87,7 +87,7 @@
         ),
         name="load",
     )(*after, *arrays)
-    return held, zero[0, 0]
+    return held, zero
 
 
 def spans_of(width):
@@ -204,15 +204,14 @@
     return list(zip(outs[::2], outs[1::2]))
 
 
-def attend_kernel(parts, rows, cuts, scalars_ref, *refs):
+def attend_kernel(parts, scalars_ref, *refs):
     own_q, other_q = refs[: len(parts)], refs[len(parts) : 2 * len(parts)]
-    refs = refs[2 * len(parts) :]
-    k_refs, v_refs, w_hbm, refs = refs[:rows], refs[rows : 2 * rows], refs[2 * rows], refs[2 * rows + 1 :]
-    own_out, other_out, held, (q_scr, o_scr, sems) = refs[0], refs[1], refs[2:-3], refs[-3:]
-    copies = fetches([w_hbm], [(0, cut) for cut in cuts], held, sems)
+    k_ref, v_hbm, own_out, other_out, v_ref, q_scr, o_scr, sems = refs[2 * len(parts) :]
+    core = scalars_ref[0]
+    rows, positions, _ = k_ref.shape
+    copies = [pltpu.make_async_copy(v_hbm.at[row], v_ref.at[row], sems.at[row]) for row in range(rows)]
     for copy in copies:
         copy.start()
-    core = scalars_ref[0]
     at = 0
     for side in (own_q, other_q):
         for ref, (heads, skip) in zip(side, parts):
@@ -227,11 +226,12 @@
     new_keys = jnp.where(core == 0, first, second)
     new_values = jnp.where(core == 0, second, first)
     scale = DH**-0.5
+    shares = []
     for row in range(rows):
         query = q_scr[row]
         scores = scale * lax.dot_general(
             query.astype(jnp.bfloat16),
-            k_refs[row][...],
+            k_ref[row],
             (((1,), (1,)), ((), ())),
             preferred_element_type=jnp.float32,
         )
@@ -244,37 +244,40 @@
         denominator = jnp.sum(raised, axis=1, keepdims=True) + self_raised
         weights = (raised / denominator).astype(jnp.bfloat16)
         self_weight = (self_raised / denominator).astype(jnp.bfloat16).astype(jnp.float32)
-        total = jnp.dot(weights, v_refs[row][...], preferred_element_type=jnp.float32)
+        shares.append((weights, self_weight))
+    for copy in copies:
+        copy.wait()
+    for row, (weights, self_weight) in enumerate(shares):
+        total = jnp.dot(weights, v_ref[row], preferred_element_type=jnp.float32)
         o_scr[row] = total + self_weight * new_values[row : row + 1]
     half = total_heads // 2
     for head in range(total_heads):
         ref = own_out if head < half else other_out
         column = (head % half) * DH
         ref[:, column : column + DH] = o_scr[:, head, :].astype(jnp.bfloat16)
-    for copy in copies:
-        copy.wait()
-
-
-def attend(core, lengths, own_q, other_q, parts, keys, values, out_weight, cuts):
-    rows, (positions, _) = len(keys), keys[0].shape
+
+
+def attend(core, lengths, own_q, other_q, parts, keys, values):
+    rows, positions, _ = keys.shape
     heads = 2 * sum(part[0] for part in parts)
     out = jax.ShapeDtypeStruct((rows, heads * DH // 2), jnp.bfloat16)
     scalars = jnp.concatenate([core[None], lengths])
     return pl.pallas_call(
-        functools.partial(attend_kernel, parts, rows, cuts),
-        out_shape=[out, out] + [piece_of(out_weight, cut) for cut in cuts],
-        in_specs=[SMEM] + [VMEM] * (2 * len(parts) + 2 * rows) + [HBM],
-        out_specs=[VMEM] * (2 + len(cuts)),
-        scratch_shapes=[pltpu.VMEM((rows, heads, DH), jnp.float32)] * 2
-        + [pltpu.SemaphoreType.DMA((max(1, len(cuts)),))],
-        compiler_params=pltpu.CompilerParams(vmem_limit_bytes=28 * MIB),
+        functools.partial(attend_kernel, parts),
+        out_shape=(out, out),
+        in_specs=[SMEM] + [VMEM] * (2 * len(parts) + 1) + [HBM],
+        out_specs=(VMEM, VMEM),
+        scratch_shapes=[pltpu.VMEM(values.shape, values.dtype)]
+        + [pltpu.VMEM((rows, heads, DH), jnp.float32)] * 2
+        + [pltpu.SemaphoreType.DMA((rows,))],
+        compiler_params=pltpu.CompilerParams(vmem_limit_bytes=49 * MIB),
         cost_estimate=pl.CostEstimate(
             flops=4 * rows * heads * positions * DH,
             bytes_accessed=4 * rows * positions * DH,
             transcendentals=rows * heads * positions,
         ),
         name="attend",
-    )(scalars, *own_q, *other_q, *keys, *values, out_weight)
+    )(scalars, *own_q, *other_q, keys, values)
 
 
 def output_kernel(orders, rows, columns, pieces, ids_ref, *refs):
@@ -374,21 +377,10 @@
         after = [made[0][0]]
         first += sum(columns for columns, _ in chunks)
     moving = [across(send, order[0]) for (send, _), (_, order) in zip(state, plan)]
-    cache_cuts = [(at, cut) for at in range(2) for cut in cuts_of(key_cache)]
-    out_cuts = cuts_of(out_weight)
-    early = len(out_cuts) * 9 // 18
     for step in range(len(bits)):
-        for turn, i in enumerate((2, 0, 1)):
+        for i in (2, 0, 1):
             columns, order = plan[i]
             total = state[i][1] + moving[i]
-            if step == 0 and turn:
-                ahead = [state[(2, 0, 1)[turn - 1]][0]]
-                if turn == 1:
-                    caches, zero = load([key_cache, value_cache], cache_cuts, ahead, 41)
-                else:
-                    first_cuts = [(0, cut) for cut in out_cuts[:early]]
-                    out_first, zero = load([out_weight], first_cuts, ahead, 36)
-                total = total + zero
             if step + 1 < len(bits):
                 cut = total.shape[0] // 2
                 state[i] = (total[cut:], total[:cut])
@@ -405,21 +397,25 @@
     by_column = [i for group in ((2,), (0, 1)) for i in group]
     parts = tuple((plan[i][0] // DH, 0 if i else kv_width) for i in by_column)
     mine, theirs = [mine[i] for i in by_column], [theirs[i] for i in by_column]
-    keys, values = caches[:own_rows], caches[own_rows:]
-    own, other, *out_rest = attend(
-        core, lengths, mine, theirs, parts, keys, values, out_weight, out_cuts[early:]
-    )
-    out_held = [*out_first, *out_rest]
+    own, other = attend(core, lengths, mine, theirs, parts, key_cache, value_cache)
     got = swap(other)
     block = jnp.where(core == 0, jnp.concatenate([own, got]), jnp.concatenate([got, own]))
 
     near = [block[:, :width], block[:, width:]]
     far = [None, None]
     paths = [bits[::-1], bits[:1] + bits[:0:-1]]
+    out_cuts, out_held = cuts_of(out_weight), []
+    early = len(out_cuts) * 9 // 18
     for step in range(len(bits)):
         for i in range(2):
             if step:
                 near[i] = jnp.concatenate([near[i], far[i]])
+                if i == 0 and out_held:
+                    near[i] = near[i] + zero.astype(jnp.bfloat16)
+                if i == 1 and step + 2 >= len(bits):
+                    part = out_cuts[early:] if out_held else out_cuts[:early]
+                    held, zero = load([out_weight], [(0, cut) for cut in part], near, 36, width)
+                    out_held += held
             far[i] = across(near[i], paths[i][step])
     orders = [order_of(path[::-1]) for path in paths]
     blocks = [b for pair in zip(near, far) for b in pair]

time: 101 us -> 78.3 us (0.78)
  local copies, waits for them, and re-layouts: 20.1 us -> 0.1 us
  starting transfers between devices: 17.2 us -> 25.5 us
  waiting for transfers between devices: 29.9 us -> 21.7 us
  other arithmetic: 4.4 us -> 2.28 us
    unnamed x62 -> x6, local copies, waits for them, and re-layouts: 18.8 us -> 0.01 us
    ppermute x15, waiting for transfers between devices: 26.2 us -> 17.8 us  [across(): return lax.ppermute(array, 'gx', [(g, g ^ mask) for g in range(n)])]
    ppermute x15, starting transfers between devices: 15.8 us -> 24.1 us  [across(): return lax.ppermute(array, 'gx', [(g, g ^ mask) for g in range(n)])]
    add x2 -> x1, other arithmetic: 2.29 us -> 0.04 us  [local(): near[i] = near[i] + zero.astype(jnp.bfloat16)]
    pallas_call x1, Pallas kernels: 5.68 us -> 4.3 us  [attend(): pl.pallas_call(functools.partial(attend_kernel, parts), out_shape=(out, o...]
    slice x2 -> x0, local copies, waits for them, and re-layouts: 1.14 us -> none  [load(): return (held, zero[0, 0])]
    pallas_call x2, Pallas kernels: 5.71 us -> 6.84 us  [load(): pl.pallas_call(functools.partial(load_kernel, len(after), cuts, len(array...]
  transfers between devices with their start and end apart: 22 -> 22, of which waited for: 12 -> 12; matrix products, arithmetic and copies ran while one was open for 5% -> 2% of each run, Pallas kernels for 16% -> 22%
where the time goes in v7:
time: 78.3 us; the launch traced here: 77.4 us
  Pallas kernels  27.6 us (35%)
  starting transfers between devices  25.5 us (33%)
  waiting for transfers between devices  21.7 us (28%)
  other arithmetic  2.28 us (3%)
    ppermute x15, starting transfers between devices, across(): return lax.ppermute(array, 'gx', [(g, g ^ mask) for g in range(n)])  24.1 us
    ppermute x15, waiting for transfers between devices, across(): return lax.ppermute(array, 'gx', [(g, g ^ mask) for g in range(n)])  17.8 us
    pallas_call x2, Pallas kernels, project(): pl.pallas_call(functools.partial(project_kernel, orders, rows, first, wid...  11.6 us
    pallas_call x2, Pallas kernels, load(): pl.pallas_call(functools.partial(load_kernel, len(after), cuts, len(array...  6.84 us
    pallas_call x2, Pallas kernels, project_out(): pl.pallas_call(functools.partial(output_kernel, orders, rows, columns, pi...  4.86 us
    pallas_call x1, Pallas kernels, attend(): pl.pallas_call(functools.partial(attend_kernel, parts), out_shape=(out, o...  4.3 us
    ppermute x7, waiting for transfers between devices, swap(): return lax.ppermute(array, 'gy', [(0, 1), (1, 0)])  3.83 us
  transfers between devices with their start and end apart: 22, of which 12 were waited for; matrix products, arithmetic and copies ran while one was open for 2% of the time, Pallas kernels for 22%

profile of v7, /device:TPU:0, one launch (start us, length us, event | category | flops | bytes accessed | tf_op | source)
XLA Modules:
  0.0 77.4 jit_solution(10742168091519758941)
XLA Ops:
  0.0 0.5 collective-permute-start
  0.5 1.0 %broadcast_select_fusion.own_ref = bf16[64,2304]{1,0:T(8,128)(2,1)S(1)} fusion(bf16[64,2304]{1,0:T(8,128)(2,1)} %param.7, pred[]{:T(512)S(6)} %lt.6), kind=kLoop, calls=%fused_computation.2 | loop fusion | flops 147456 | bytes 589825 | tf_op jit(solution)/shard_map/jit(_where)/select_n | solution.py:364
  1.5 0.3 collective-permute-done.other_ref
  1.9 4.4 %project.2 = (f32[64,1024]{1,0:T(8,128)S(1)}, f32[64,1024]{1,0:T(8,128)S(1)}) custom-call(s32[2]{0:T(128)S(1)} %pad_add_fusion.ids_ref, bf16[64,2304]{1,0:T(8,128)(2,1)S(1)} %broadcast_select_fusion.own_ref, bf16[64,2304]{1,0:T(8,128)(2,1)S(1)} %collective-permute-done.other_ref, bf16[2304,3072]{1,0:T(8,128)(2,1)} %w_ref.3), custom_call_target="tpu_custom_call" | custom-call | flops 603979776 | bytes 5242880 | tf_op jit(solution)/shard_map/project/pallas_call | solution.py:185
  6.3 3.0 %collective-permute-start.1 = (f32[64,1024]{1,0:T(8,128)S(1)}, f32[64,1024]{1,0:T(8,128)S(1)}, u32[]{:S(2)}, u32[]{:S(2)}) collective-permute-start(f32[64,1024]{1,0:T(8,128)S(1)} %get-tuple-element.37.refs_1_), channel_id=1, source_target_pairs={{0,4},{2,6},{4,0},{6,2},{8,12},{10,14},{12,8},{14,10},{1,5},{3,7},... | collective-permute-start | bytes 786440 | tf_op jit(solution)/shard_map/ppermute | solution.py:361
  9.3 7.2 %project.3 = (f32[64,1024]{1,0:T(8,128)S(1)}, f32[64,1024]{1,0:T(8,128)S(1)}, f32[64,1280]{1,0:T(8,128)S(1)}, f32[64,1280]{1,0:T(8,128)S(1)}) custom-call(s32[2]{0:T(128)S(1)} %pad_add_fusion.ids_ref, bf16[64,2304]{1,0:T(8,128)(2,1)S(1)} %broadcast_select_fusion.own_ref, bf16[64,2304]{1,0:T(8,128)(2,1)S(1)} %collective-permute-done.other_ref, ...), custom_call_target="tpu_custom_call" | custom-call | flops 1358954496 | bytes 11796480 | tf_op jit(solution)/shard_map/project/pallas_call | solution.py:185
  16.6 1.9 %collective-permute-start.4 = (f32[64,1024]{1,0:T(8,128)S(1)}, f32[64,1024]{1,0:T(8,128)S(1)}, u32[]{:S(2)}, u32[]{:S(2)}) collective-permute-start(f32[64,1024]{1,0:T(8,128)S(1)} %get-tuple-element.39), channel_id=1, source_target_pairs={{0,2},{2,0},{4,6},{6,4},{8,10},{10,8},{12,14},{14,12},{1,3},{3,1},... | collective-permute-start | bytes 786440 | tf_op jit(solution)/shard_map/ppermute | solution.py:361
  18.8 7.0 %collective-permute-done.4 = f32[64,1024]{1,0:T(8,128)S(1)} collective-permute-done((f32[64,1024]{1,0:T(8,128)S(1)}, f32[64,1024]{1,0:T(8,128)S(1)}, u32[]{:S(2)}, u32[]{:S(2)}) %collective-permute-start.4) | collective-permute-done | bytes 262176 | tf_op jit(solution)/shard_map/ppermute | solution.py:361
  25.9 3.0 %collective-permute-start.5 = (f32[32,1024]{1,0:T(8,128)S(1)}, f32[32,1024]{1,0:T(8,128)S(1)}, u32[]{:S(2)}, u32[]{:S(2)}) collective-permute-start(f32[32,1024]{1,0:T(8,128)S(1)} %slice.61), channel_id=1, source_target_pairs={{0,8},{2,10},{4,12},{6,14},{8,0},{10,2},{12,4},{14,6},{1,9},{3,11}... | collective-permute-start | bytes 393224 | tf_op jit(solution)/shard_map/ppermute | solution.py:361
  29.0 1.6 %collective-permute-start.8 = (f32[32,1280]{1,0:T(8,128)S(1)}, f32[32,1280]{1,0:T(8,128)S(1)}, u32[]{:S(2)}, u32[]{:S(2)}) collective-permute-start(f32[32,1280]{1,0:T(8,128)S(1)} %slice.65), channel_id=1, source_target_pairs={{0,2},{2,0},{4,6},{6,4},{8,10},{10,8},{12,14},{14,12},{1,3},{3,1},... | collective-permute-start | bytes 491528 | tf_op jit(solution)/shard_map/ppermute | solution.py:361
  30.6 0.4 collective-permute-start.3
  31.0 3.7 %collective-permute-done.5 = f32[32,1024]{1,0:T(8,128)S(1)} collective-permute-done((f32[32,1024]{1,0:T(8,128)S(1)}, f32[32,1024]{1,0:T(8,128)S(1)}, u32[]{:S(2)}, u32[]{:S(2)}) %collective-permute-start.5) | collective-permute-done | bytes 131104 | tf_op jit(solution)/shard_map/ppermute | solution.py:361
  34.7 1.0 %collective-permute-start.6 = (f32[16,1024]{1,0:T(8,128)S(1)}, f32[16,1024]{1,0:T(8,128)S(1)}, u32[]{:S(2)}, u32[]{:S(2)}) collective-permute-start(f32[16,1024]{1,0:T(8,128)S(1)} %slice.63), channel_id=1, source_target_pairs={{0,4},{2,6},{4,0},{6,2},{8,12},{10,14},{12,8},{14,10},{1,5},{3,7},... | collective-permute-start | bytes 196616 | tf_op jit(solution)/shard_map/ppermute | solution.py:361
  36.0 3.1 %collective-permute-done.6 = f32[16,1024]{1,0:T(8,128)S(1)} collective-permute-done((f32[16,1024]{1,0:T(8,128)S(1)}, f32[16,1024]{1,0:T(8,128)S(1)}, u32[]{:S(2)}, u32[]{:S(2)}) %collective-permute-start.6) | collective-permute-done | bytes 65568 | tf_op jit(solution)/shard_map/ppermute | solution.py:361
  39.1 2.3 %collective-permute-start.9 = (f32[16,1280]{1,0:T(8,128)S(1)}, f32[16,1280]{1,0:T(8,128)S(1)}, u32[]{:S(2)}, u32[]{:S(2)}) collective-permute-start(f32[16,1280]{1,0:T(8,128)S(1)} %slice.67), channel_id=1, source_target_pairs={{0,8},{2,10},{4,12},{6,14},{8,0},{10,2},{12,4},{14,6},{1,9},{3,11}... | collective-permute-start | bytes 245768 | tf_op jit(solution)/shard_map/ppermute | solution.py:361
  41.4 3.1 %collective-permute-done.9 = f32[16,1280]{1,0:T(8,128)S(1)} collective-permute-done((f32[16,1280]{1,0:T(8,128)S(1)}, f32[16,1280]{1,0:T(8,128)S(1)}, u32[]{:S(2)}, u32[]{:S(2)}) %collective-permute-start.9) | collective-permute-done | bytes 81952 | tf_op jit(solution)/shard_map/ppermute | solution.py:361
  44.7 1.1 %collective-permute-done.12.refs_5_ = bf16[8,1280]{1,0:T(8,128)(2,1)S(1)} collective-permute-done((bf16[8,1280]{1,0:T(8,128)(2,1)S(1)}, bf16[8,1280]{1,0:T(8,128)(2,1)S(1)}, u32[]{:S(2)}, u32[]{:S(2)}) %collective-permute-start.12) | collective-permute-done | bytes 20512 | tf_op jit(solution)/shard_map/ppermute | solution.py:358
  45.8 4.3 %attend.1 = (bf16[8,3072]{1,0:T(8,128)(2,1)S(1)}, bf16[8,3072]{1,0:T(8,128)(2,1)S(1)}) custom-call(s32[9]{0:T(128)S(1)} %pad_add_fusion.1.scalars_ref, bf16[8,1024]{1,0:T(8,128)(2,1)S(1)} %get-tuple-element.74.refs_0_, bf16[8,1024]{1,0:T(8,128)(2,1)S(1)} %get-tuple-element.72.refs_1_, bf16[8,1280]{1,0:T(8,128)(2,1)S(1)} %get-tuple-element.70.refs_2_, ...), custom_call_target="tpu_custom_call" | custom-call | flops 201326592 | bytes 8388608 | tf_op jit(solution)/shard_map/attend/pallas_call | solution.py:265
  50.4 1.1 %collective-permute-done.13 = bf16[8,3072]{1,0:T(8,128)(2,1)S(1)} collective-permute-done((bf16[8,3072]{1,0:T(8,128)(2,1)S(1)}, bf16[8,3072]{1,0:T(8,128)(2,1)S(1)}, u32[]{:S(2)}, u32[]{:S(2)}) %collective-permute-start.13) | collective-permute-done | bytes 49184 | tf_op jit(solution)/shard_map/ppermute | solution.py:358
  51.5 1.2 %collective-permute-start.16 = (bf16[16,1536]{1,0:T(8,128)(2,1)S(1)}, bf16[16,1536]{1,0:T(8,128)(2,1)S(1)}, u32[]{:S(2)}, u32[]{:S(2)}) collective-permute-start(bf16[16,1536]{1,0:T(8,128)(2,1)S(1)} %get-tuple-element.67), channel_id=1, source_target_pairs={{0,2},{2,0},{4,6},{6,4},{8,10},{10,8},{12,14},{14,12},{1,3},{3,1},... | collective-permute-start | bytes 147464 | tf_op jit(solution)/shard_map/ppermute | solution.py:361
  52.7 2.7 %collective-permute-start.14 = (bf16[16,1536]{1,0:T(8,128)(2,1)S(1)}, bf16[16,1536]{1,0:T(8,128)(2,1)S(1)}, u32[]{:S(2)}, u32[]{:S(2)}) collective-permute-start(bf16[16,1536]{1,0:T(8,128)(2,1)S(1)} %get-tuple-element.68), channel_id=1, source_target_pairs={{0,8},{2,10},{4,12},{6,14},{8,0},{10,2},{12,4},{14,6},{1,9},{3,11}... | collective-permute-start | bytes 147464 | tf_op jit(solution)/shard_map/ppermute | solution.py:361
  55.6 2.3 %collective-permute-start.18 = (bf16[32,1536]{1,0:T(8,128)(2,1)S(1)}, bf16[32,1536]{1,0:T(8,128)(2,1)S(1)}, u32[]{:S(2)}, u32[]{:S(2)}) collective-permute-start(bf16[32,1536]{1,0:T(8,128)(2,1)S(1)} %pad_maximum_fusion.3.refs_1_), channel_id=1, source_target_pairs={{0,8},{2,10},{4,12},{6,14},{8,0},{10,2},{12,4},{14,6},{1,9},{3,11}... | collective-permute-start | bytes 294920 | tf_op jit(solution)/shard_map/ppermute | solution.py:361
  58.0 2.8 %collective-permute-start.15 = (bf16[32,1536]{1,0:T(8,128)(2,1)S(1)}, bf16[32,1536]{1,0:T(8,128)(2,1)S(1)}, u32[]{:S(2)}, u32[]{:S(2)}) collective-permute-start(bf16[32,1536]{1,0:T(8,128)(2,1)S(1)} %pad_maximum_fusion.2.refs_0_), channel_id=1, source_target_pairs={{0,4},{2,6},{4,0},{6,2},{8,12},{10,14},{12,8},{14,10},{1,5},{3,7},... | collective-permute-start | bytes 294920 | tf_op jit(solution)/shard_map/ppermute | solution.py:361
  60.7 3.1 %load.2 = (bf16[512,768]{1,0:T(8,128)(2,1)S(1)}, bf16[512,768]{1,0:T(8,128)(2,1)S(1)}, bf16[512,768]{1,0:T(8,128)(2,1)S(1)}, bf16[512,768]{1,0:T(8,128)(2,1)S(1)...) custom-call(bf16[32,1536]{1,0:T(8,128)(2,1)S(1)} %pad_maximum_fusion, ...), custom_call_target="tpu_custom_call" | custom-call | bytes 14155776 | tf_op jit(solution)/shard_map/load/pallas_call | solution.py:78
  64.1 1.6 %collective-permute-start.17 = (bf16[64,1536]{1,0:T(8,128)(2,1)S(1)}, bf16[64,1536]{1,0:T(8,128)(2,1)S(1)}, u32[]{:S(2)}, u32[]{:S(2)}) collective-permute-start(bf16[64,1536]{1,0:T(8,128)(2,1)S(1)} %maximum_add_fusion.refs_0_), channel_id=1, source_target_pairs={{0,2},{2,0},{4,6},{6,4},{8,10},{10,8},{12,14},{14,12},{1,3},{3,1},... | collective-permute-start | bytes 589832 | tf_op jit(solution)/shard_map/ppermute | solution.py:361
  65.6 3.7 %load.3 = (bf16[512,768]{1,0:T(8,128)(2,1)S(1)}, bf16[512,768]{1,0:T(8,128)(2,1)S(1)}, bf16[512,768]{1,0:T(8,128)(2,1)S(1)}, bf16[512,768]{1,0:T(8,128)(2,1)S(1)...) custom-call(bf16[64,1536]{1,0:T(8,128)(2,1)S(1)} %maximum_add_fusion, ...), custom_call_target="tpu_custom_call" | custom-call | bytes 14155776 | tf_op jit(solution)/shard_map/load/pallas_call | solution.py:78
  69.3 0.3 collective-permute-done.19.refs_3_
  69.8 2.1 %project_out.3 = (f32[64,768]{1,0:T(8,128)S(1)}, f32[64,768]{1,0:T(8,128)S(1)}) custom-call(s32[2]{0:T(128)S(1)} %pad_add_fusion.ids_ref, bf16[64,1536]{1,0:T(8,128)(2,1)S(1)} %maximum_add_fusion.refs_0_, bf16[64,1536]{1,0:T(8,128)(2,1)S(1)} %collective-permute-done.17.refs_1_, bf16[64,1536]{1,0:T(8,128)(2,1)S(1)} %pad_maximum_fusion.1.refs_1_.refs_2_, ...), custom_call_target="tpu_custom_call" | custom-call | flops 603979776 | bytes 5111808 | tf_op jit(solution)/shard_map/project_out/pallas_call | solution.py:329
  72.0 2.8 %project_out.2 = (f32[64,1536]{1,0:T(8,128)S(1)}, f32[64,1536]{1,0:T(8,128)S(1)}) custom-call(s32[2]{0:T(128)S(1)} %pad_add_fusion.ids_ref, bf16[64,1536]{1,0:T(8,128)(2,1)S(1)} %maximum_add_fusion.refs_0_, bf16[64,1536]{1,0:T(8,128)(2,1)S(1)} %collective-permute-done.17.refs_1_, bf16[64,1536]{1,0:T(8,128)(2,1)S(1)} %pad_maximum_fusion.1.refs_1_.refs_2_, ...), custom_call_target="tpu_custom_call" | custom-call | flops 1207959552 | bytes 10223616 | tf_op jit(solution)/shard_map/project_out/pallas_call | solution.py:329
  74.8 0.5 collective-permute-start.20
  75.3 1.3 %collective-permute-done.20 = f32[64,1536]{1,0:T(8,128)S(1)} collective-permute-done((f32[64,1536]{1,0:T(8,128)S(1)}, f32[64,1536]{1,0:T(8,128)S(1)}, u32[]{:S(2)}, u32[]{:S(2)}) %collective-permute-start.20) | collective-permute-done | bytes 393248 | tf_op jit(solution)/shard_map/ppermute | solution.py:358
  76.7 0.7 pad_maximum_fusion
  (56 shorter events, 2.1 us)
Async XLA Ops:
  0.0 1.9 %collective-permute-start = (bf16[64,2304]{1,0:T(8,128)(2,1)}, bf16[64,2304]{1,0:T(8,128)(2,1)S(1)}, u32[]{:S(2)}, u32[]{:S(2)}) collective-permute-start(bf16[64,2304]{1,0:T(8,128)(2,1)} %param.7), channel_id=1, source_target_pairs={{0,1},{1,0},{2,3},{3,2},{4,5},{5,4},{6,7},{7,6},{8,9},{9,8},{10,11... | collective-permute-start | bytes 884744 | tf_op jit(solution)/shard_map/ppermute | solution.py:358
  1.5 7.8 %copy-start.1 = (bf16[2304,512]{1,0:T(8,128)(2,1)S(1)}, bf16[2304,512]{1,0:T(8,128)(2,1)}, u32[]{:S(2)}) copy-start(bf16[2304,512]{1,0:T(8,128)(2,1)} %refs_0_.1) | copy-start | bytes 7077892
  6.3 12.3 %collective-permute-start.1 = (f32[64,1024]{1,0:T(8,128)S(1)}, f32[64,1024]{1,0:T(8,128)S(1)}, u32[]{:S(2)}, u32[]{:S(2)}) collective-permute-start(f32[64,1024]{1,0:T(8,128)S(1)} %get-tuple-element.37.refs_1_), channel_id=1, source_target_pairs={{0,4},{2,6},{4,0},{6,2},{8,12},{10,14},{12,8},{14,10},{1,5},{3,7},... | collective-permute-start | bytes 786440 | tf_op jit(solution)/shard_map/ppermute | solution.py:361
  16.5 28.2 %copy-start.2 = (s32[8]{0:T(128)S(1)}, s32[8]{0:T(128)}, u32[]{:S(2)}) copy-start(s32[8]{0:T(128)} %param.13) | copy-start | bytes 100
  16.5 12.4 %collective-permute-start.7 = (f32[64,1280]{1,0:T(8,128)S(1)}, f32[64,1280]{1,0:T(8,128)S(1)}, u32[]{:S(2)}, u32[]{:S(2)}) collective-permute-start(f32[64,1280]{1,0:T(8,128)S(1)} %get-tuple-element.41), channel_id=1, source_target_pairs={{0,4},{2,6},{4,0},{6,2},{8,12},{10,14},{12,8},{14,10},{1,5},{3,7},... | collective-permute-start | bytes 983048 | tf_op jit(solution)/shard_map/ppermute | solution.py:361
  16.6 9.2 %collective-permute-start.4 = (f32[64,1024]{1,0:T(8,128)S(1)}, f32[64,1024]{1,0:T(8,128)S(1)}, u32[]{:S(2)}, u32[]{:S(2)}) collective-permute-start(f32[64,1024]{1,0:T(8,128)S(1)} %get-tuple-element.39), channel_id=1, source_target_pairs={{0,2},{2,0},{4,6},{6,4},{8,10},{10,8},{12,14},{14,12},{1,3},{3,1},... | collective-permute-start | bytes 786440 | tf_op jit(solution)/shard_map/ppermute | solution.py:361
  18.6 12.0 %collective-permute-start.2 = (f32[32,1024]{1,0:T(8,128)S(1)}, f32[32,1024]{1,0:T(8,128)S(1)}, u32[]{:S(2)}, u32[]{:S(2)}) collective-permute-start(f32[32,1024]{1,0:T(8,128)S(1)} %slice.57), channel_id=1, source_target_pairs={{0,2},{2,0},{4,6},{6,4},{8,10},{10,8},{12,14},{14,12},{1,3},{3,1},... | collective-permute-start | bytes 393224 | tf_op jit(solution)/shard_map/ppermute | solution.py:361
  18.8 27.0 %copy-start = (bf16[8,1024,256]{2,1,0:T(8,128)(2,1)S(1)}, bf16[8,1024,256]{2,1,0:T(8,128)(2,1)}, u32[]{:S(2)}) copy-start(bf16[8,1024,256]{2,1,0:T(8,128)(2,1)} %refs_6_.1) | copy-start | bytes 12582916
  25.9 8.8 %collective-permute-start.5 = (f32[32,1024]{1,0:T(8,128)S(1)}, f32[32,1024]{1,0:T(8,128)S(1)}, u32[]{:S(2)}, u32[]{:S(2)}) collective-permute-start(f32[32,1024]{1,0:T(8,128)S(1)} %slice.61), channel_id=1, source_target_pairs={{0,8},{2,10},{4,12},{6,14},{8,0},{10,2},{12,4},{14,6},{1,9},{3,11}... | collective-permute-start | bytes 393224 | tf_op jit(solution)/shard_map/ppermute | solution.py:361
  29.0 10.1 %collective-permute-start.8 = (f32[32,1280]{1,0:T(8,128)S(1)}, f32[32,1280]{1,0:T(8,128)S(1)}, u32[]{:S(2)}, u32[]{:S(2)}) collective-permute-start(f32[32,1280]{1,0:T(8,128)S(1)} %slice.65), channel_id=1, source_target_pairs={{0,2},{2,0},{4,6},{6,4},{8,10},{10,8},{12,14},{14,12},{1,3},{3,1},... | collective-permute-start | bytes 491528 | tf_op jit(solution)/shard_map/ppermute | solution.py:361
  30.6 5.2 %collective-permute-start.3 = (f32[16,1024]{1,0:T(8,128)S(1)}, f32[16,1024]{1,0:T(8,128)S(1)}, u32[]{:S(2)}, u32[]{:S(2)}) collective-permute-start(f32[16,1024]{1,0:T(8,128)S(1)} %slice.59), channel_id=1, source_target_pairs={{0,8},{2,10},{4,12},{6,14},{8,0},{10,2},{12,4},{14,6},{1,9},{3,11}... | collective-permute-start | bytes 196616 | tf_op jit(solution)/shard_map/ppermute | solution.py:361
  34.7 4.3 %collective-permute-start.6 = (f32[16,1024]{1,0:T(8,128)S(1)}, f32[16,1024]{1,0:T(8,128)S(1)}, u32[]{:S(2)}, u32[]{:S(2)}) collective-permute-start(f32[16,1024]{1,0:T(8,128)S(1)} %slice.63), channel_id=1, source_target_pairs={{0,4},{2,6},{4,0},{6,2},{8,12},{10,14},{12,8},{14,10},{1,5},{3,7},... | collective-permute-start | bytes 196616 | tf_op jit(solution)/shard_map/ppermute | solution.py:361
  35.9 8.9 %collective-permute-start.10 = (bf16[8,1024]{1,0:T(8,128)(2,1)S(1)}, bf16[8,1024]{1,0:T(8,128)(2,1)S(1)}, u32[]{:S(2)}, u32[]{:S(2)}) collective-permute-start(bf16[8,1024]{1,0:T(8,128)(2,1)S(1)} %get-tuple-element.73), channel_id=1, source_target_pairs={{0,1},{1,0},{2,3},{3,2},{4,5},{5,4},{6,7},{7,6},{8,9},{9,8},{10,11... | collective-permute-start | bytes 49160 | tf_op jit(solution)/shard_map/ppermute | solution.py:358
  39.1 5.4 %collective-permute-start.9 = (f32[16,1280]{1,0:T(8,128)S(1)}, f32[16,1280]{1,0:T(8,128)S(1)}, u32[]{:S(2)}, u32[]{:S(2)}) collective-permute-start(f32[16,1280]{1,0:T(8,128)S(1)} %slice.67), channel_id=1, source_target_pairs={{0,8},{2,10},{4,12},{6,14},{8,0},{10,2},{12,4},{14,6},{1,9},{3,11}... | collective-permute-start | bytes 245768 | tf_op jit(solution)/shard_map/ppermute | solution.py:361
  41.4 3.3 %collective-permute-start.11 = (bf16[8,1024]{1,0:T(8,128)(2,1)S(1)}, bf16[8,1024]{1,0:T(8,128)(2,1)S(1)}, u32[]{:S(2)}, u32[]{:S(2)}) collective-permute-start(bf16[8,1024]{1,0:T(8,128)(2,1)S(1)} %get-tuple-element.71), channel_id=1, source_target_pairs={{0,1},{1,0},{2,3},{3,2},{4,5},{5,4},{6,7},{7,6},{8,9},{9,8},{10,11... | collective-permute-start | bytes 49160 | tf_op jit(solution)/shard_map/ppermute | solution.py:358
  44.6 1.3 %collective-permute-start.12 = (bf16[8,1280]{1,0:T(8,128)(2,1)S(1)}, bf16[8,1280]{1,0:T(8,128)(2,1)S(1)}, u32[]{:S(2)}, u32[]{:S(2)}) collective-permute-start(bf16[8,1280]{1,0:T(8,128)(2,1)S(1)} %get-tuple-element.69), channel_id=1, source_target_pairs={{0,1},{1,0},{2,3},{3,2},{4,5},{5,4},{6,7},{7,6},{8,9},{9,8},{10,11... | collective-permute-start | bytes 61448 | tf_op jit(solution)/shard_map/ppermute | solution.py:358
  50.1 1.3 %collective-permute-start.13 = (bf16[8,3072]{1,0:T(8,128)(2,1)S(1)}, bf16[8,3072]{1,0:T(8,128)(2,1)S(1)}, u32[]{:S(2)}, u32[]{:S(2)}) collective-permute-start(bf16[8,3072]{1,0:T(8,128)(2,1)S(1)} %get-tuple-element.43), channel_id=1, source_target_pairs={{0,1},{1,0},{2,3},{3,2},{4,5},{5,4},{6,7},{7,6},{8,9},{9,8},{10,11... | collective-permute-start | bytes 147464 | tf_op jit(solution)/shard_map/ppermute | solution.py:358
  51.5 4.2 %collective-permute-start.16 = (bf16[16,1536]{1,0:T(8,128)(2,1)S(1)}, bf16[16,1536]{1,0:T(8,128)(2,1)S(1)}, u32[]{:S(2)}, u32[]{:S(2)}) collective-permute-start(bf16[16,1536]{1,0:T(8,128)(2,1)S(1)} %get-tuple-element.67), channel_id=1, source_target_pairs={{0,2},{2,0},{4,6},{6,4},{8,10},{10,8},{12,14},{14,12},{1,3},{3,1},... | collective-permute-start | bytes 147464 | tf_op jit(solution)/shard_map/ppermute | solution.py:361
  52.7 5.3 %collective-permute-start.14 = (bf16[16,1536]{1,0:T(8,128)(2,1)S(1)}, bf16[16,1536]{1,0:T(8,128)(2,1)S(1)}, u32[]{:S(2)}, u32[]{:S(2)}) collective-permute-start(bf16[16,1536]{1,0:T(8,128)(2,1)S(1)} %get-tuple-element.68), channel_id=1, source_target_pairs={{0,8},{2,10},{4,12},{6,14},{8,0},{10,2},{12,4},{14,6},{1,9},{3,11}... | collective-permute-start | bytes 147464 | tf_op jit(solution)/shard_map/ppermute | solution.py:361
  55.6 8.3 %collective-permute-start.18 = (bf16[32,1536]{1,0:T(8,128)(2,1)S(1)}, bf16[32,1536]{1,0:T(8,128)(2,1)S(1)}, u32[]{:S(2)}, u32[]{:S(2)}) collective-permute-start(bf16[32,1536]{1,0:T(8,128)(2,1)S(1)} %pad_maximum_fusion.3.refs_1_), channel_id=1, source_target_pairs={{0,8},{2,10},{4,12},{6,14},{8,0},{10,2},{12,4},{14,6},{1,9},{3,11}... | collective-permute-start | bytes 294920 | tf_op jit(solution)/shard_map/ppermute | solution.py:361
  58.0 6.0 %collective-permute-start.15 = (bf16[32,1536]{1,0:T(8,128)(2,1)S(1)}, bf16[32,1536]{1,0:T(8,128)(2,1)S(1)}, u32[]{:S(2)}, u32[]{:S(2)}) collective-permute-start(bf16[32,1536]{1,0:T(8,128)(2,1)S(1)} %pad_maximum_fusion.2.refs_0_), channel_id=1, source_target_pairs={{0,4},{2,6},{4,0},{6,2},{8,12},{10,14},{12,8},{14,10},{1,5},{3,7},... | collective-permute-start | bytes 294920 | tf_op jit(solution)/shard_map/ppermute | solution.py:361
  63.9 5.7 %collective-permute-start.19 = (bf16[64,1536]{1,0:T(8,128)(2,1)S(1)}, bf16[64,1536]{1,0:T(8,128)(2,1)S(1)}, u32[]{:S(2)}, u32[]{:S(2)}) collective-permute-start(bf16[64,1536]{1,0:T(8,128)(2,1)S(1)} %pad_maximum_fusion.1.refs_1_.refs_2_), channel_id=1, source_target_pairs={{0,4},{2,6},{4,0},{6,2},{8,12},{10,14},{12,8},{14,10},{1,5},{3,7},... | collective-permute-start | bytes 589832 | tf_op jit(solution)/shard_map/ppermute | solution.py:361
  64.1 5.7 %collective-permute-start.17 = (bf16[64,1536]{1,0:T(8,128)(2,1)S(1)}, bf16[64,1536]{1,0:T(8,128)(2,1)S(1)}, u32[]{:S(2)}, u32[]{:S(2)}) collective-permute-start(bf16[64,1536]{1,0:T(8,128)(2,1)S(1)} %maximum_add_fusion.refs_0_), channel_id=1, source_target_pairs={{0,2},{2,0},{4,6},{6,4},{8,10},{10,8},{12,14},{14,12},{1,3},{3,1},... | collective-permute-start | bytes 589832 | tf_op jit(solution)/shard_map/ppermute | solution.py:361
  71.9 3.4 %collective-permute-start.21 = (f32[64,768]{1,0:T(8,128)S(1)}, f32[64,768]{1,0:T(8,128)S(1)}, u32[]{:S(2)}, u32[]{:S(2)}) collective-permute-start(f32[64,768]{1,0:T(8,128)S(1)} %get-tuple-element.66), channel_id=1, source_target_pairs={{0,1},{1,0},{2,3},{3,2},{4,5},{5,4},{6,7},{7,6},{8,9},{9,8},{10,11... | collective-permute-start | bytes 589832 | tf_op jit(solution)/shard_map/ppermute | solution.py:358
  74.8 1.9 %collective-permute-start.20 = (f32[64,1536]{1,0:T(8,128)S(1)}, f32[64,1536]{1,0:T(8,128)S(1)}, u32[]{:S(2)}, u32[]{:S(2)}) collective-permute-start(f32[64,1536]{1,0:T(8,128)S(1)} %get-tuple-element.58), channel_id=1, source_target_pairs={{0,1},{1,0},{2,3},{3,2},{4,5},{5,4},{6,7},{7,6},{8,9},{9,8},{10,11... | collective-permute-start | bytes 1179656 | tf_op jit(solution)/shard_map/ppermute | solution.py:358

commit v8 on v7

--- a/solution.py
+++ b/solution.py
@@ -151,7 +151,7 @@
             at += tile
             source += tile
     per_tile = features // depth
-    weights = InOrder(copies, 3 * per_tile)
+    weights = InOrder(copies, 3)
     cut = half * rows
     ready = set()
     for t, (chunk, column, at, width) in enumerate(tiles):
@@ -280,33 +280,23 @@
     )(scalars, *own_q, *other_q, keys, values)
 
 
-def output_kernel(orders, rows, columns, pieces, ids_ref, *refs):
+def output_kernel(orders, rows, columns, pieces, after, ids_ref, *refs):
     count = 2 * len(orders)
     block_refs, w_refs = refs[:count], refs[count : count + len(pieces)]
-    send_ref, keep_ref, xs_ref, row_sem = refs[count + len(pieces) :]
+    send_ref, keep_ref, xs_ref = refs[count + len(pieces) + after :]
     depth = block_refs[0].shape[1]
     me, core = ids_ref[0], ids_ref[1]
     n = len(orders[0])
     half = n // 2
-    row_copies = []
     for group, (near_ref, far_ref) in enumerate(zip(block_refs[::2], block_refs[1::2])):
         for p, j in enumerate(orders[group]):
             block = jnp.bitwise_xor(me, j)
             place = block % half + jnp.where(block // half == core, half, 0)
             source = near_ref if p < half else far_ref
-            row_copies.append(
-                pltpu.make_async_copy(
-                    source.at[pl.ds((p % half) * rows, rows), :],
-                    xs_ref.at[
-                        pl.ds(pl.multiple_of(place * rows, rows), rows), pl.ds(group * depth, depth)
-                    ],
-                    row_sem.at[group, p],
-                )
-            )
-    for copy in row_copies:
-        copy.start()
-    for copy in row_copies:
-        copy.wait()
+            at = (p % half) * rows
+            xs_ref[
+                pl.ds(pl.multiple_of(place * rows, rows), rows), group * depth : (group + 1) * depth
+            ] = source[at : at + rows, :]
     cut = half * rows
     totals = {}
     for w_ref, ((first, tall), span) in zip(w_refs, pieces):
@@ -319,7 +309,7 @@
         keep_ref[:, column - columns[0] : column - columns[0] + width] = total[cut:]
 
 
-def project_out(orders, rows, ids, blocks, held, cuts, columns):
+def project_out(orders, rows, ids, blocks, held, cuts, columns, after):
     chosen = [at for at, (_, (column, _)) in enumerate(cuts) if columns[0] <= column < sum(columns)]
     weights, pieces = [held[at] for at in chosen], [cuts[at] for at in chosen]
     pieces, weights = zip(*sorted(zip(pieces, weights), key=lambda pair: (pair[0][1], pair[0][0])))
@@ -327,14 +317,11 @@
     n = len(orders[0])
     out = jax.ShapeDtypeStruct((n * rows // 2, columns[1]), jnp.float32)
     return pl.pallas_call(
-        functools.partial(output_kernel, orders, rows, columns, pieces),
+        functools.partial(output_kernel, orders, rows, columns, pieces, len(after)),
         out_shape=(out, out),
-        in_specs=[SMEM] + [ANY] * len(blocks) + [VMEM] * len(weights),
+        in_specs=[SMEM] + [VMEM] * (len(blocks) + len(weights)) + [ANY] * len(after),
         out_specs=(VMEM, VMEM),
-        scratch_shapes=[
-            pltpu.VMEM((n * rows, depth), jnp.bfloat16),
-            pltpu.SemaphoreType.DMA((len(orders), n)),
-        ],
+        scratch_shapes=[pltpu.VMEM((n * rows, depth), jnp.bfloat16)],
         compiler_params=pltpu.CompilerParams(vmem_limit_bytes=12 * MIB),
         cost_estimate=pl.CostEstimate(
             flops=2 * n * rows * depth * columns[1],
@@ -342,7 +329,7 @@
             transcendentals=0,
         ),
         name="project_out",
-    )(ids, *blocks, *weights)
+    )(ids, *blocks, *weights, *after)
 
 
 def local(tokens, query_weight, kv_weight, out_weight, key_cache, value_cache, lengths):
@@ -366,7 +353,7 @@
 
     y, z = bits[:1], bits[1:]
     unit = query_weight.shape[1] // 12
-    plan = [(3 * unit, y + z[::-1]), (5 * unit, z[:1] + y + z[1:]), (4 * unit, z[:1] + y + z[1:])]
+    plan = [(3 * unit, z[:1] + y + z[1:]), (5 * unit, y + z), (4 * unit, z + y)]
     state, first, after = [None] * len(plan), 0, []
     for group in ((2,), (0, 1)):
         chunks = [plan[i] for i in group]
@@ -421,10 +408,11 @@
     blocks = [b for pair in zip(near, far) for b in pair]
     total_columns = out_weight.shape[1]
     last = 768 if total_columns % 768 == 0 and total_columns > 768 else 0
-    results = []
+    results, after = [], []
     for columns in ((0, total_columns - last), (total_columns - last, last)):
         if columns[1]:
-            send, keep = project_out(orders, rows, ids, blocks, out_held, out_cuts, columns)
+            send, keep = project_out(orders, rows, ids, blocks, out_held, out_cuts, columns, after)
+            after = [send]
             results.append((keep + swap(send)).astype(jnp.bfloat16))
     return jnp.concatenate(results, axis=1)
 

time: 78.3 us -> 78.3 us (level)
  waiting for transfers between devices: 21.7 us -> 27.4 us
  starting transfers between devices: 25.5 us -> 20.4 us
    ppermute x15, waiting for transfers between devices: 17.8 us -> 23.5 us  [across(): return lax.ppermute(array, 'gx', [(g, g ^ mask) for g in range(n)])]
    ppermute x15, starting transfers between devices: 24.1 us -> 19 us  [across(): return lax.ppermute(array, 'gx', [(g, g ^ mask) for g in range(n)])]
    pallas_call x2, Pallas kernels: 4.86 us -> 3.39 us  [project_out(): pl.pallas_call(functools.partial(output_kernel, orders, rows, columns, pi...]
    pallas_call x2, Pallas kernels: 11.6 us -> 13 us  [project(): pl.pallas_call(functools.partial(project_kernel, orders, rows, first, wid...]
  transfers between devices with their start and end apart: 22 -> 22, of which waited for: 12 -> 13; matrix products, arithmetic and copies ran while one was open for 2% -> 2% of each run, Pallas kernels for 22% -> 19%
where the time goes in v8:
time: 78.3 us; the launch traced here: 78 us
  Pallas kernels  27.5 us (35%)
  waiting for transfers between devices  27.4 us (35%)
  starting transfers between devices  20.4 us (26%)
  other arithmetic  2.26 us (3%)
    ppermute x15, waiting for transfers between devices, across(): return lax.ppermute(array, 'gx', [(g, g ^ mask) for g in range(n)])  23.5 us
    ppermute x15, starting transfers between devices, across(): return lax.ppermute(array, 'gx', [(g, g ^ mask) for g in range(n)])  19 us
    pallas_call x2, Pallas kernels, project(): pl.pallas_call(functools.partial(project_kernel, orders, rows, first, wid...  13 us
    pallas_call x2, Pallas kernels, load(): pl.pallas_call(functools.partial(load_kernel, len(after), cuts, len(array...  6.84 us
    pallas_call x1, Pallas kernels, attend(): pl.pallas_call(functools.partial(attend_kernel, parts), out_shape=(out, o...  4.3 us
    ppermute x7, waiting for transfers between devices, swap(): return lax.ppermute(array, 'gy', [(0, 1), (1, 0)])  3.97 us
    pallas_call x2, Pallas kernels, project_out(): pl.pallas_call(functools.partial(output_kernel, orders, rows, columns, pi...  3.39 us
  transfers between devices with their start and end apart: 22, of which 13 were waited for; matrix products, arithmetic and copies ran while one was open for 2% of the time, Pallas kernels for 19%

profile of v8, /device:TPU:0, one launch (start us, length us, event | category | flops | bytes accessed | tf_op | source)
XLA Modules:
  0.0 78.0 jit_solution(1386034780355233424)
XLA Ops:
  0.5 1.0 %broadcast_select_fusion.own_ref = bf16[64,2304]{1,0:T(8,128)(2,1)S(1)} fusion(bf16[64,2304]{1,0:T(8,128)(2,1)} %param.7, pred[]{:T(512)S(6)} %lt.6), kind=kLoop, calls=%fused_computation.2 | loop fusion | flops 147456 | bytes 589825 | tf_op jit(solution)/shard_map/jit(_where)/select_n | solution.py:351
  1.9 4.8 %project.2 = (f32[64,1024]{1,0:T(8,128)S(1)}, f32[64,1024]{1,0:T(8,128)S(1)}) custom-call(s32[2]{0:T(128)S(1)} %pad_add_fusion.ids_ref, bf16[64,2304]{1,0:T(8,128)(2,1)S(1)} %broadcast_select_fusion.own_ref, bf16[64,2304]{1,0:T(8,128)(2,1)S(1)} %collective-permute-done.other_ref, bf16[2304,3072]{1,0:T(8,128)(2,1)} %w_ref.3), custom_call_target="tpu_custom_call" | custom-call | flops 603979776 | bytes 5242880 | tf_op jit(solution)/shard_map/project/pallas_call | solution.py:185
  6.6 3.0 %collective-permute-start.1 = (f32[64,1024]{1,0:T(8,128)S(1)}, f32[64,1024]{1,0:T(8,128)S(1)}, u32[]{:S(2)}, u32[]{:S(2)}) collective-permute-start(f32[64,1024]{1,0:T(8,128)S(1)} %get-tuple-element.37.refs_1_), channel_id=1, source_target_pairs={{0,4},{2,6},{4,0},{6,2},{8,12},{10,14},{12,8},{14,10},{1,5},{3,7},... | collective-permute-start | bytes 786440 | tf_op jit(solution)/shard_map/ppermute | solution.py:348
  9.7 8.2 %project.3 = (f32[64,1024]{1,0:T(8,128)S(1)}, f32[64,1024]{1,0:T(8,128)S(1)}, f32[64,1280]{1,0:T(8,128)S(1)}, f32[64,1280]{1,0:T(8,128)S(1)}) custom-call(s32[2]{0:T(128)S(1)} %pad_add_fusion.ids_ref, bf16[64,2304]{1,0:T(8,128)(2,1)S(1)} %broadcast_select_fusion.own_ref, bf16[64,2304]{1,0:T(8,128)(2,1)S(1)} %collective-permute-done.other_ref, ...), custom_call_target="tpu_custom_call" | custom-call | flops 1358954496 | bytes 11796480 | tf_op jit(solution)/shard_map/project/pallas_call | solution.py:185
  17.9 1.6 %collective-permute-start.7 = (f32[64,1280]{1,0:T(8,128)S(1)}, f32[64,1280]{1,0:T(8,128)S(1)}, u32[]{:S(2)}, u32[]{:S(2)}) collective-permute-start(f32[64,1280]{1,0:T(8,128)S(1)} %get-tuple-element.41), channel_id=1, source_target_pairs={{0,2},{2,0},{4,6},{6,4},{8,10},{10,8},{12,14},{14,12},{1,3},{3,1},... | collective-permute-start | bytes 983048 | tf_op jit(solution)/shard_map/ppermute | solution.py:348
  20.0 2.7 %collective-permute-start.2 = (f32[32,1024]{1,0:T(8,128)S(1)}, f32[32,1024]{1,0:T(8,128)S(1)}, u32[]{:S(2)}, u32[]{:S(2)}) collective-permute-start(f32[32,1024]{1,0:T(8,128)S(1)} %slice.57), channel_id=1, source_target_pairs={{0,8},{2,10},{4,12},{6,14},{8,0},{10,2},{12,4},{14,6},{1,9},{3,11}... | collective-permute-start | bytes 393224 | tf_op jit(solution)/shard_map/ppermute | solution.py:348
  22.7 7.4 %collective-permute-done.4 = f32[64,1024]{1,0:T(8,128)S(1)} collective-permute-done((f32[64,1024]{1,0:T(8,128)S(1)}, f32[64,1024]{1,0:T(8,128)S(1)}, u32[]{:S(2)}, u32[]{:S(2)}) %collective-permute-start.4) | collective-permute-done | bytes 262176 | tf_op jit(solution)/shard_map/ppermute | solution.py:348
  30.2 0.6 collective-permute-start.5
  30.9 1.6 %collective-permute-start.3 = (f32[16,1024]{1,0:T(8,128)S(1)}, f32[16,1024]{1,0:T(8,128)S(1)}, u32[]{:S(2)}, u32[]{:S(2)}) collective-permute-start(f32[16,1024]{1,0:T(8,128)S(1)} %slice.59), channel_id=1, source_target_pairs={{0,2},{2,0},{4,6},{6,4},{8,10},{10,8},{12,14},{14,12},{1,3},{3,1},... | collective-permute-start | bytes 196616 | tf_op jit(solution)/shard_map/ppermute | solution.py:348
  32.5 2.7 %collective-permute-done.5 = f32[32,1024]{1,0:T(8,128)S(1)} collective-permute-done((f32[32,1024]{1,0:T(8,128)S(1)}, f32[32,1024]{1,0:T(8,128)S(1)}, u32[]{:S(2)}, u32[]{:S(2)}) %collective-permute-start.5) | collective-permute-done | bytes 131104 | tf_op jit(solution)/shard_map/ppermute | solution.py:348
  35.2 1.6 %collective-permute-start.6 = (f32[16,1024]{1,0:T(8,128)S(1)}, f32[16,1024]{1,0:T(8,128)S(1)}, u32[]{:S(2)}, u32[]{:S(2)}) collective-permute-start(f32[16,1024]{1,0:T(8,128)S(1)} %slice.63), channel_id=1, source_target_pairs={{0,8},{2,10},{4,12},{6,14},{8,0},{10,2},{12,4},{14,6},{1,9},{3,11}... | collective-permute-start | bytes 196616 | tf_op jit(solution)/shard_map/ppermute | solution.py:348
  37.0 3.9 %collective-permute-done.6 = f32[16,1024]{1,0:T(8,128)S(1)} collective-permute-done((f32[16,1024]{1,0:T(8,128)S(1)}, f32[16,1024]{1,0:T(8,128)S(1)}, u32[]{:S(2)}, u32[]{:S(2)}) %collective-permute-start.6) | collective-permute-done | bytes 65568 | tf_op jit(solution)/shard_map/ppermute | solution.py:348
  40.9 1.3 %collective-permute-start.9 = (f32[16,1280]{1,0:T(8,128)S(1)}, f32[16,1280]{1,0:T(8,128)S(1)}, u32[]{:S(2)}, u32[]{:S(2)}) collective-permute-start(f32[16,1280]{1,0:T(8,128)S(1)} %slice.67), channel_id=1, source_target_pairs={{0,8},{2,10},{4,12},{6,14},{8,0},{10,2},{12,4},{14,6},{1,9},{3,11}... | collective-permute-start | bytes 245768 | tf_op jit(solution)/shard_map/ppermute | solution.py:348
  42.2 4.1 %collective-permute-done.9 = f32[16,1280]{1,0:T(8,128)S(1)} collective-permute-done((f32[16,1280]{1,0:T(8,128)S(1)}, f32[16,1280]{1,0:T(8,128)S(1)}, u32[]{:S(2)}, u32[]{:S(2)}) %collective-permute-start.9) | collective-permute-done | bytes 81952 | tf_op jit(solution)/shard_map/ppermute | solution.py:348
  46.5 1.1 %collective-permute-done.12.refs_5_ = bf16[8,1280]{1,0:T(8,128)(2,1)S(1)} collective-permute-done((bf16[8,1280]{1,0:T(8,128)(2,1)S(1)}, bf16[8,1280]{1,0:T(8,128)(2,1)S(1)}, u32[]{:S(2)}, u32[]{:S(2)}) %collective-permute-start.12) | collective-permute-done | bytes 20512 | tf_op jit(solution)/shard_map/ppermute | solution.py:345
  47.6 4.3 %attend.1 = (bf16[8,3072]{1,0:T(8,128)(2,1)S(1)}, bf16[8,3072]{1,0:T(8,128)(2,1)S(1)}) custom-call(s32[9]{0:T(128)S(1)} %pad_add_fusion.1.scalars_ref, bf16[8,1024]{1,0:T(8,128)(2,1)S(1)} %get-tuple-element.74.refs_0_, bf16[8,1024]{1,0:T(8,128)(2,1)S(1)} %get-tuple-element.72.refs_1_, bf16[8,1280]{1,0:T(8,128)(2,1)S(1)} %get-tuple-element.70.refs_2_, ...), custom_call_target="tpu_custom_call" | custom-call | flops 201326592 | bytes 8388608 | tf_op jit(solution)/shard_map/attend/pallas_call | solution.py:265
  52.1 1.1 %collective-permute-done.13 = bf16[8,3072]{1,0:T(8,128)(2,1)S(1)} collective-permute-done((bf16[8,3072]{1,0:T(8,128)(2,1)S(1)}, bf16[8,3072]{1,0:T(8,128)(2,1)S(1)}, u32[]{:S(2)}, u32[]{:S(2)}) %collective-permute-start.13) | collective-permute-done | bytes 49184 | tf_op jit(solution)/shard_map/ppermute | solution.py:345
  53.3 1.3 %collective-permute-start.16 = (bf16[16,1536]{1,0:T(8,128)(2,1)S(1)}, bf16[16,1536]{1,0:T(8,128)(2,1)S(1)}, u32[]{:S(2)}, u32[]{:S(2)}) collective-permute-start(bf16[16,1536]{1,0:T(8,128)(2,1)S(1)} %get-tuple-element.67), channel_id=1, source_target_pairs={{0,2},{2,0},{4,6},{6,4},{8,10},{10,8},{12,14},{14,12},{1,3},{3,1},... | collective-permute-start | bytes 147464 | tf_op jit(solution)/shard_map/ppermute | solution.py:348
  54.6 0.9 %collective-permute-start.14 = (bf16[16,1536]{1,0:T(8,128)(2,1)S(1)}, bf16[16,1536]{1,0:T(8,128)(2,1)S(1)}, u32[]{:S(2)}, u32[]{:S(2)}) collective-permute-start(bf16[16,1536]{1,0:T(8,128)(2,1)S(1)} %get-tuple-element.68), channel_id=1, source_target_pairs={{0,8},{2,10},{4,12},{6,14},{8,0},{10,2},{12,4},{14,6},{1,9},{3,11}... | collective-permute-start | bytes 147464 | tf_op jit(solution)/shard_map/ppermute | solution.py:348
  55.5 2.0 %collective-permute-done.16 = bf16[16,1536]{1,0:T(8,128)(2,1)S(1)} collective-permute-done((bf16[16,1536]{1,0:T(8,128)(2,1)S(1)}, bf16[16,1536]{1,0:T(8,128)(2,1)S(1)}, u32[]{:S(2)}, u32[]{:S(2)}) %collective-permute-start.16) | collective-permute-done | bytes 49184 | tf_op jit(solution)/shard_map/ppermute | solution.py:348
  57.4 1.3 %collective-permute-start.18 = (bf16[32,1536]{1,0:T(8,128)(2,1)S(1)}, bf16[32,1536]{1,0:T(8,128)(2,1)S(1)}, u32[]{:S(2)}, u32[]{:S(2)}) collective-permute-start(bf16[32,1536]{1,0:T(8,128)(2,1)S(1)} %pad_maximum_fusion.3.refs_1_), channel_id=1, source_target_pairs={{0,8},{2,10},{4,12},{6,14},{8,0},{10,2},{12,4},{14,6},{1,9},{3,11}... | collective-permute-start | bytes 294920 | tf_op jit(solution)/shard_map/ppermute | solution.py:348
  58.7 1.8 %collective-permute-done.14 = bf16[16,1536]{1,0:T(8,128)(2,1)S(1)} collective-permute-done((bf16[16,1536]{1,0:T(8,128)(2,1)S(1)}, bf16[16,1536]{1,0:T(8,128)(2,1)S(1)}, u32[]{:S(2)}, u32[]{:S(2)}) %collective-permute-start.14) | collective-permute-done | bytes 49184 | tf_op jit(solution)/shard_map/ppermute | solution.py:348
  60.6 1.8 %collective-permute-start.15 = (bf16[32,1536]{1,0:T(8,128)(2,1)S(1)}, bf16[32,1536]{1,0:T(8,128)(2,1)S(1)}, u32[]{:S(2)}, u32[]{:S(2)}) collective-permute-start(bf16[32,1536]{1,0:T(8,128)(2,1)S(1)} %pad_maximum_fusion.2.refs_0_), channel_id=1, source_target_pairs={{0,4},{2,6},{4,0},{6,2},{8,12},{10,14},{12,8},{14,10},{1,5},{3,7},... | collective-permute-start | bytes 294920 | tf_op jit(solution)/shard_map/ppermute | solution.py:348
  62.4 3.1 %load.2 = (bf16[512,768]{1,0:T(8,128)(2,1)S(1)}, bf16[512,768]{1,0:T(8,128)(2,1)S(1)}, bf16[512,768]{1,0:T(8,128)(2,1)S(1)}, bf16[512,768]{1,0:T(8,128)(2,1)S(1)...) custom-call(bf16[32,1536]{1,0:T(8,128)(2,1)S(1)} %pad_maximum_fusion, ...), custom_call_target="tpu_custom_call" | custom-call | bytes 14155776 | tf_op jit(solution)/shard_map/load/pallas_call | solution.py:78
  66.4 3.7 %load.3 = (bf16[512,768]{1,0:T(8,128)(2,1)S(1)}, bf16[512,768]{1,0:T(8,128)(2,1)S(1)}, bf16[512,768]{1,0:T(8,128)(2,1)S(1)}, bf16[512,768]{1,0:T(8,128)(2,1)S(1)...) custom-call(bf16[64,1536]{1,0:T(8,128)(2,1)S(1)} %maximum_add_fusion, ...), custom_call_target="tpu_custom_call" | custom-call | bytes 14155776 | tf_op jit(solution)/shard_map/load/pallas_call | solution.py:78
  70.2 1.2 %collective-permute-done.19.refs_3_ = bf16[64,1536]{1,0:T(8,128)(2,1)S(1)} collective-permute-done((bf16[64,1536]{1,0:T(8,128)(2,1)S(1)}, bf16[64,1536]{1,0:T(8,128)(2,1)S(1)}, u32[]{:S(2)}, u32[]{:S(2)}) %collective-permute-start.19) | collective-permute-done | bytes 196640 | tf_op jit(solution)/shard_map/ppermute | solution.py:348
  71.7 2.0 %project_out.2 = (f32[64,1536]{1,0:T(8,128)S(1)}, f32[64,1536]{1,0:T(8,128)S(1)}) custom-call(s32[2]{0:T(128)S(1)} %pad_add_fusion.ids_ref, bf16[64,1536]{1,0:T(8,128)(2,1)S(1)} %maximum_add_fusion.refs_0_, bf16[64,1536]{1,0:T(8,128)(2,1)S(1)} %collective-permute-done.17.refs_1_, bf16[64,1536]{1,0:T(8,128)(2,1)S(1)} %pad_maximum_fusion.1.refs_1_.refs_2_, ...), custom_call_target="tpu_custom_call" | custom-call | flops 1207959552 | bytes 10223616 | tf_op jit(solution)/shard_map/project_out/pallas_call | solution.py:319
  73.7 1.4 %project_out.3 = (f32[64,768]{1,0:T(8,128)S(1)}, f32[64,768]{1,0:T(8,128)S(1)}) custom-call(s32[2]{0:T(128)S(1)} %pad_add_fusion.ids_ref, bf16[64,1536]{1,0:T(8,128)(2,1)S(1)} %maximum_add_fusion.refs_0_, bf16[64,1536]{1,0:T(8,128)(2,1)S(1)} %collective-permute-done.17.refs_1_, bf16[64,1536]{1,0:T(8,128)(2,1)S(1)} %pad_maximum_fusion.1.refs_1_.refs_2_, ...), custom_call_target="tpu_custom_call" | custom-call | flops 603979776 | bytes 5111808 | tf_op jit(solution)/shard_map/project_out/pallas_call | solution.py:319
  75.2 0.5 collective-permute-start.20
  75.7 0.9 %collective-permute-done.21 = f32[64,768]{1,0:T(8,128)S(1)} collective-permute-done((f32[64,768]{1,0:T(8,128)S(1)}, f32[64,768]{1,0:T(8,128)S(1)}, u32[]{:S(2)}, u32[]{:S(2)}) %collective-permute-start.21) | collective-permute-done | bytes 196640 | tf_op jit(solution)/shard_map/ppermute | solution.py:345
  76.7 0.5 collective-permute-done.20
  77.2 0.7 pad_maximum_fusion
  (56 shorter events, 3.6 us)
Async XLA Ops:
  0.0 1.9 %collective-permute-start = (bf16[64,2304]{1,0:T(8,128)(2,1)}, bf16[64,2304]{1,0:T(8,128)(2,1)S(1)}, u32[]{:S(2)}, u32[]{:S(2)}) collective-permute-start(bf16[64,2304]{1,0:T(8,128)(2,1)} %param.7), channel_id=1, source_target_pairs={{0,1},{1,0},{2,3},{3,2},{4,5},{5,4},{6,7},{7,6},{8,9},{9,8},{10,11... | collective-permute-start | bytes 884744 | tf_op jit(solution)/shard_map/ppermute | solution.py:345
  1.5 8.1 %copy-start.1 = (bf16[2304,512]{1,0:T(8,128)(2,1)S(1)}, bf16[2304,512]{1,0:T(8,128)(2,1)}, u32[]{:S(2)}) copy-start(bf16[2304,512]{1,0:T(8,128)(2,1)} %refs_0_.1) | copy-start | bytes 7077892
  6.6 13.3 %collective-permute-start.1 = (f32[64,1024]{1,0:T(8,128)S(1)}, f32[64,1024]{1,0:T(8,128)S(1)}, u32[]{:S(2)}, u32[]{:S(2)}) collective-permute-start(f32[64,1024]{1,0:T(8,128)S(1)} %get-tuple-element.37.refs_1_), channel_id=1, source_target_pairs={{0,4},{2,6},{4,0},{6,2},{8,12},{10,14},{12,8},{14,10},{1,5},{3,7},... | collective-permute-start | bytes 786440 | tf_op jit(solution)/shard_map/ppermute | solution.py:348
  17.9 28.5 %copy-start.2 = (s32[8]{0:T(128)S(1)}, s32[8]{0:T(128)}, u32[]{:S(2)}) copy-start(s32[8]{0:T(128)} %param.13) | copy-start | bytes 100
  17.9 12.8 %collective-permute-start.7 = (f32[64,1280]{1,0:T(8,128)S(1)}, f32[64,1280]{1,0:T(8,128)S(1)}, u32[]{:S(2)}, u32[]{:S(2)}) collective-permute-start(f32[64,1280]{1,0:T(8,128)S(1)} %get-tuple-element.41), channel_id=1, source_target_pairs={{0,2},{2,0},{4,6},{6,4},{8,10},{10,8},{12,14},{14,12},{1,3},{3,1},... | collective-permute-start | bytes 983048 | tf_op jit(solution)/shard_map/ppermute | solution.py:348
  19.5 10.6 %collective-permute-start.4 = (f32[64,1024]{1,0:T(8,128)S(1)}, f32[64,1024]{1,0:T(8,128)S(1)}, u32[]{:S(2)}, u32[]{:S(2)}) collective-permute-start(f32[64,1024]{1,0:T(8,128)S(1)} %get-tuple-element.39), channel_id=1, source_target_pairs={{0,4},{2,6},{4,0},{6,2},{8,12},{10,14},{12,8},{14,10},{1,5},{3,7},... | collective-permute-start | bytes 786440 | tf_op jit(solution)/shard_map/ppermute | solution.py:348
  20.0 10.9 %collective-permute-start.2 = (f32[32,1024]{1,0:T(8,128)S(1)}, f32[32,1024]{1,0:T(8,128)S(1)}, u32[]{:S(2)}, u32[]{:S(2)}) collective-permute-start(f32[32,1024]{1,0:T(8,128)S(1)} %slice.57), channel_id=1, source_target_pairs={{0,8},{2,10},{4,12},{6,14},{8,0},{10,2},{12,4},{14,6},{1,9},{3,11}... | collective-permute-start | bytes 393224 | tf_op jit(solution)/shard_map/ppermute | solution.py:348
  22.7 24.9 %copy-start = (bf16[8,1024,256]{2,1,0:T(8,128)(2,1)S(1)}, bf16[8,1024,256]{2,1,0:T(8,128)(2,1)}, u32[]{:S(2)}) copy-start(bf16[8,1024,256]{2,1,0:T(8,128)(2,1)} %refs_6_.1) | copy-start | bytes 12582916
  30.2 5.0 %collective-permute-start.5 = (f32[32,1024]{1,0:T(8,128)S(1)}, f32[32,1024]{1,0:T(8,128)S(1)}, u32[]{:S(2)}, u32[]{:S(2)}) collective-permute-start(f32[32,1024]{1,0:T(8,128)S(1)} %slice.61), channel_id=1, source_target_pairs={{0,2},{2,0},{4,6},{6,4},{8,10},{10,8},{12,14},{14,12},{1,3},{3,1},... | collective-permute-start | bytes 393224 | tf_op jit(solution)/shard_map/ppermute | solution.py:348
  30.8 10.1 %collective-permute-start.8 = (f32[32,1280]{1,0:T(8,128)S(1)}, f32[32,1280]{1,0:T(8,128)S(1)}, u32[]{:S(2)}, u32[]{:S(2)}) collective-permute-start(f32[32,1280]{1,0:T(8,128)S(1)} %slice.65), channel_id=1, source_target_pairs={{0,4},{2,6},{4,0},{6,2},{8,12},{10,14},{12,8},{14,10},{1,5},{3,7},... | collective-permute-start | bytes 491528 | tf_op jit(solution)/shard_map/ppermute | solution.py:348
  30.9 5.9 %collective-permute-start.3 = (f32[16,1024]{1,0:T(8,128)S(1)}, f32[16,1024]{1,0:T(8,128)S(1)}, u32[]{:S(2)}, u32[]{:S(2)}) collective-permute-start(f32[16,1024]{1,0:T(8,128)S(1)} %slice.59), channel_id=1, source_target_pairs={{0,2},{2,0},{4,6},{6,4},{8,10},{10,8},{12,14},{14,12},{1,3},{3,1},... | collective-permute-start | bytes 196616 | tf_op jit(solution)/shard_map/ppermute | solution.py:348
  35.2 5.6 %collective-permute-start.6 = (f32[16,1024]{1,0:T(8,128)S(1)}, f32[16,1024]{1,0:T(8,128)S(1)}, u32[]{:S(2)}, u32[]{:S(2)}) collective-permute-start(f32[16,1024]{1,0:T(8,128)S(1)} %slice.63), channel_id=1, source_target_pairs={{0,8},{2,10},{4,12},{6,14},{8,0},{10,2},{12,4},{14,6},{1,9},{3,11}... | collective-permute-start | bytes 196616 | tf_op jit(solution)/shard_map/ppermute | solution.py:348
  36.9 9.6 %collective-permute-start.10 = (bf16[8,1024]{1,0:T(8,128)(2,1)S(1)}, bf16[8,1024]{1,0:T(8,128)(2,1)S(1)}, u32[]{:S(2)}, u32[]{:S(2)}) collective-permute-start(bf16[8,1024]{1,0:T(8,128)(2,1)S(1)} %get-tuple-element.73), channel_id=1, source_target_pairs={{0,1},{1,0},{2,3},{3,2},{4,5},{5,4},{6,7},{7,6},{8,9},{9,8},{10,11... | collective-permute-start | bytes 49160 | tf_op jit(solution)/shard_map/ppermute | solution.py:345
  40.9 5.4 %collective-permute-start.9 = (f32[16,1280]{1,0:T(8,128)S(1)}, f32[16,1280]{1,0:T(8,128)S(1)}, u32[]{:S(2)}, u32[]{:S(2)}) collective-permute-start(f32[16,1280]{1,0:T(8,128)S(1)} %slice.67), channel_id=1, source_target_pairs={{0,8},{2,10},{4,12},{6,14},{8,0},{10,2},{12,4},{14,6},{1,9},{3,11}... | collective-permute-start | bytes 245768 | tf_op jit(solution)/shard_map/ppermute | solution.py:348
  42.2 4.3 %collective-permute-start.11 = (bf16[8,1024]{1,0:T(8,128)(2,1)S(1)}, bf16[8,1024]{1,0:T(8,128)(2,1)S(1)}, u32[]{:S(2)}, u32[]{:S(2)}) collective-permute-start(bf16[8,1024]{1,0:T(8,128)(2,1)S(1)} %get-tuple-element.71), channel_id=1, source_target_pairs={{0,1},{1,0},{2,3},{3,2},{4,5},{5,4},{6,7},{7,6},{8,9},{9,8},{10,11... | collective-permute-start | bytes 49160 | tf_op jit(solution)/shard_map/ppermute | solution.py:345
  46.3 1.3 %collective-permute-start.12 = (bf16[8,1280]{1,0:T(8,128)(2,1)S(1)}, bf16[8,1280]{1,0:T(8,128)(2,1)S(1)}, u32[]{:S(2)}, u32[]{:S(2)}) collective-permute-start(bf16[8,1280]{1,0:T(8,128)(2,1)S(1)} %get-tuple-element.69), channel_id=1, source_target_pairs={{0,1},{1,0},{2,3},{3,2},{4,5},{5,4},{6,7},{7,6},{8,9},{9,8},{10,11... | collective-permute-start | bytes 61448 | tf_op jit(solution)/shard_map/ppermute | solution.py:345
  51.9 1.3 %collective-permute-start.13 = (bf16[8,3072]{1,0:T(8,128)(2,1)S(1)}, bf16[8,3072]{1,0:T(8,128)(2,1)S(1)}, u32[]{:S(2)}, u32[]{:S(2)}) collective-permute-start(bf16[8,3072]{1,0:T(8,128)(2,1)S(1)} %get-tuple-element.43), channel_id=1, source_target_pairs={{0,1},{1,0},{2,3},{3,2},{4,5},{5,4},{6,7},{7,6},{8,9},{9,8},{10,11... | collective-permute-start | bytes 147464 | tf_op jit(solution)/shard_map/ppermute | solution.py:345
  53.3 4.2 %collective-permute-start.16 = (bf16[16,1536]{1,0:T(8,128)(2,1)S(1)}, bf16[16,1536]{1,0:T(8,128)(2,1)S(1)}, u32[]{:S(2)}, u32[]{:S(2)}) collective-permute-start(bf16[16,1536]{1,0:T(8,128)(2,1)S(1)} %get-tuple-element.67), channel_id=1, source_target_pairs={{0,2},{2,0},{4,6},{6,4},{8,10},{10,8},{12,14},{14,12},{1,3},{3,1},... | collective-permute-start | bytes 147464 | tf_op jit(solution)/shard_map/ppermute | solution.py:348
  54.6 6.0 %collective-permute-start.14 = (bf16[16,1536]{1,0:T(8,128)(2,1)S(1)}, bf16[16,1536]{1,0:T(8,128)(2,1)S(1)}, u32[]{:S(2)}, u32[]{:S(2)}) collective-permute-start(bf16[16,1536]{1,0:T(8,128)(2,1)S(1)} %get-tuple-element.68), channel_id=1, source_target_pairs={{0,8},{2,10},{4,12},{6,14},{8,0},{10,2},{12,4},{14,6},{1,9},{3,11}... | collective-permute-start | bytes 147464 | tf_op jit(solution)/shard_map/ppermute | solution.py:348
  57.4 8.2 %collective-permute-start.18 = (bf16[32,1536]{1,0:T(8,128)(2,1)S(1)}, bf16[32,1536]{1,0:T(8,128)(2,1)S(1)}, u32[]{:S(2)}, u32[]{:S(2)}) collective-permute-start(bf16[32,1536]{1,0:T(8,128)(2,1)S(1)} %pad_maximum_fusion.3.refs_1_), channel_id=1, source_target_pairs={{0,8},{2,10},{4,12},{6,14},{8,0},{10,2},{12,4},{14,6},{1,9},{3,11}... | collective-permute-start | bytes 294920 | tf_op jit(solution)/shard_map/ppermute | solution.py:348
  60.6 5.4 %collective-permute-start.15 = (bf16[32,1536]{1,0:T(8,128)(2,1)S(1)}, bf16[32,1536]{1,0:T(8,128)(2,1)S(1)}, u32[]{:S(2)}, u32[]{:S(2)}) collective-permute-start(bf16[32,1536]{1,0:T(8,128)(2,1)S(1)} %pad_maximum_fusion.2.refs_0_), channel_id=1, source_target_pairs={{0,4},{2,6},{4,0},{6,2},{8,12},{10,14},{12,8},{14,10},{1,5},{3,7},... | collective-permute-start | bytes 294920 | tf_op jit(solution)/shard_map/ppermute | solution.py:348
  65.6 5.7 %collective-permute-start.19 = (bf16[64,1536]{1,0:T(8,128)(2,1)S(1)}, bf16[64,1536]{1,0:T(8,128)(2,1)S(1)}, u32[]{:S(2)}, u32[]{:S(2)}) collective-permute-start(bf16[64,1536]{1,0:T(8,128)(2,1)S(1)} %pad_maximum_fusion.1.refs_1_.refs_2_), channel_id=1, source_target_pairs={{0,4},{2,6},{4,0},{6,2},{8,12},{10,14},{12,8},{14,10},{1,5},{3,7},... | collective-permute-start | bytes 589832 | tf_op jit(solution)/shard_map/ppermute | solution.py:348
  66.0 5.7 %collective-permute-start.17 = (bf16[64,1536]{1,0:T(8,128)(2,1)S(1)}, bf16[64,1536]{1,0:T(8,128)(2,1)S(1)}, u32[]{:S(2)}, u32[]{:S(2)}) collective-permute-start(bf16[64,1536]{1,0:T(8,128)(2,1)S(1)} %maximum_add_fusion.refs_0_), channel_id=1, source_target_pairs={{0,2},{2,0},{4,6},{6,4},{8,10},{10,8},{12,14},{14,12},{1,3},{3,1},... | collective-permute-start | bytes 589832 | tf_op jit(solution)/shard_map/ppermute | solution.py:348
  75.1 1.5 %collective-permute-start.21 = (f32[64,768]{1,0:T(8,128)S(1)}, f32[64,768]{1,0:T(8,128)S(1)}, u32[]{:S(2)}, u32[]{:S(2)}) collective-permute-start(f32[64,768]{1,0:T(8,128)S(1)} %get-tuple-element.66), channel_id=1, source_target_pairs={{0,1},{1,0},{2,3},{3,2},{4,5},{5,4},{6,7},{7,6},{8,9},{9,8},{10,11... | collective-permute-start | bytes 589832 | tf_op jit(solution)/shard_map/ppermute | solution.py:345
  75.2 2.0 %collective-permute-start.20 = (f32[64,1536]{1,0:T(8,128)S(1)}, f32[64,1536]{1,0:T(8,128)S(1)}, u32[]{:S(2)}, u32[]{:S(2)}) collective-permute-start(f32[64,1536]{1,0:T(8,128)S(1)} %get-tuple-element.58.refs_10_), channel_id=1, source_target_pairs={{0,1},{1,0},{2,3},{3,2},{4,5},{5,4},{6,7},{7,6},{8,9},{9,8},{10,11... | collective-permute-start | bytes 1179656 | tf_op jit(solution)/shard_map/ppermute | solution.py:345

commit v9 on v8

--- a/solution.py
+++ b/solution.py
@@ -125,7 +125,7 @@
                 row_copy(other_ref, chunk, p).start()
 
     tiles, copies, at, source = [], [], 0, first
-    depth = features // 2 if features % 32 == 0 else features
+    depth = 768 if features % 768 == 0 else features
 
     def fetch(from_ref, column, width):
         for part in range(features // depth):
@@ -151,7 +151,7 @@
             at += tile
             source += tile
     per_tile = features // depth
-    weights = InOrder(copies, 3)
+    weights = InOrder(copies, 9)
     cut = half * rows
     ready = set()
     for t, (chunk, column, at, width) in enumerate(tiles):
@@ -181,7 +181,8 @@
         shape = (n * rows // 2, width + (0 if chunk else kv_width))
         outs += [jax.ShapeDtypeStruct(shape, jnp.float32)] * 2
     weights = [query_weight] + ([kv_weight] if kv_width else [])
-    copies = 2 * (len(weights) - 1 + sum(len(spans_of(width)) for width in widths))
+    parts = features // 768 if features % 768 == 0 else 1
+    copies = parts * (len(weights) - 1 + sum(len(spans_of(width)) for width in widths))
     outs = pl.pallas_call(
         functools.partial(project_kernel, orders, rows, first, widths, kv_width, len(after)),
         out_shape=outs,

time: 78.3 us -> 76.8 us (0.981)
  Pallas kernels: 27.5 us -> 26.2 us
    pallas_call x2, Pallas kernels: 13 us -> 11.6 us  [project(): pl.pallas_call(functools.partial(project_kernel, orders, rows, first, wid...]
  transfers between devices with their start and end apart: 22 -> 22, of which waited for: 13 -> 13; matrix products, arithmetic and copies ran while one was open for 2% -> 2% of each run, Pallas kernels for 19% -> 18%
where the time goes in v9:
time: 76.8 us; the launch traced here: 76.6 us
  waiting for transfers between devices  27.4 us (36%)
  Pallas kernels  26.2 us (34%)
  starting transfers between devices  20.4 us (27%)
  other arithmetic  2.26 us (3%)
    ppermute x15, waiting for transfers between devices, across(): return lax.ppermute(array, 'gx', [(g, g ^ mask) for g in range(n)])  23.5 us
    ppermute x15, starting transfers between devices, across(): return lax.ppermute(array, 'gx', [(g, g ^ mask) for g in range(n)])  19 us
    pallas_call x2, Pallas kernels, project(): pl.pallas_call(functools.partial(project_kernel, orders, rows, first, wid...  11.6 us
    pallas_call x2, Pallas kernels, load(): pl.pallas_call(functools.partial(load_kernel, len(after), cuts, len(array...  6.84 us
    pallas_call x1, Pallas kernels, attend(): pl.pallas_call(functools.partial(attend_kernel, parts), out_shape=(out, o...  4.3 us
    ppermute x7, waiting for transfers between devices, swap(): return lax.ppermute(array, 'gy', [(0, 1), (1, 0)])  3.97 us
    pallas_call x2, Pallas kernels, project_out(): pl.pallas_call(functools.partial(output_kernel, orders, rows, columns, pi...  3.39 us
  transfers between devices with their start and end apart: 22, of which 13 were waited for; matrix products, arithmetic and copies ran while one was open for 2% of the time, Pallas kernels for 18%

profile of v9, /device:TPU:0, one launch (start us, length us, event | category | flops | bytes accessed | tf_op | source)
XLA Modules:
  0.0 76.6 jit_solution(8212693021277583317)
XLA Ops:
  0.5 1.0 %broadcast_select_fusion.own_ref = bf16[64,2304]{1,0:T(8,128)(2,1)S(1)} fusion(bf16[64,2304]{1,0:T(8,128)(2,1)} %param.7, pred[]{:T(512)S(6)} %lt.6), kind=kLoop, calls=%fused_computation.2 | loop fusion | flops 147456 | bytes 589825 | tf_op jit(solution)/shard_map/jit(_where)/select_n | solution.py:352
  1.9 4.4 %project.2 = (f32[64,1024]{1,0:T(8,128)S(1)}, f32[64,1024]{1,0:T(8,128)S(1)}) custom-call(s32[2]{0:T(128)S(1)} %pad_add_fusion.ids_ref, bf16[64,2304]{1,0:T(8,128)(2,1)S(1)} %broadcast_select_fusion.own_ref, bf16[64,2304]{1,0:T(8,128)(2,1)S(1)} %collective-permute-done.other_ref, bf16[2304,3072]{1,0:T(8,128)(2,1)} %w_ref.3), custom_call_target="tpu_custom_call" | custom-call | flops 603979776 | bytes 5242880 | tf_op jit(solution)/shard_map/project/pallas_call | solution.py:186
  6.3 3.0 %collective-permute-start.1 = (f32[64,1024]{1,0:T(8,128)S(1)}, f32[64,1024]{1,0:T(8,128)S(1)}, u32[]{:S(2)}, u32[]{:S(2)}) collective-permute-start(f32[64,1024]{1,0:T(8,128)S(1)} %get-tuple-element.37.refs_1_), channel_id=1, source_target_pairs={{0,4},{2,6},{4,0},{6,2},{8,12},{10,14},{12,8},{14,10},{1,5},{3,7},... | collective-permute-start | bytes 786440 | tf_op jit(solution)/shard_map/ppermute | solution.py:349
  9.3 7.2 %project.3 = (f32[64,1024]{1,0:T(8,128)S(1)}, f32[64,1024]{1,0:T(8,128)S(1)}, f32[64,1280]{1,0:T(8,128)S(1)}, f32[64,1280]{1,0:T(8,128)S(1)}) custom-call(s32[2]{0:T(128)S(1)} %pad_add_fusion.ids_ref, bf16[64,2304]{1,0:T(8,128)(2,1)S(1)} %broadcast_select_fusion.own_ref, bf16[64,2304]{1,0:T(8,128)(2,1)S(1)} %collective-permute-done.other_ref, ...), custom_call_target="tpu_custom_call" | custom-call | flops 1358954496 | bytes 11796480 | tf_op jit(solution)/shard_map/project/pallas_call | solution.py:186
  16.5 1.6 %collective-permute-start.7 = (f32[64,1280]{1,0:T(8,128)S(1)}, f32[64,1280]{1,0:T(8,128)S(1)}, u32[]{:S(2)}, u32[]{:S(2)}) collective-permute-start(f32[64,1280]{1,0:T(8,128)S(1)} %get-tuple-element.41), channel_id=1, source_target_pairs={{0,2},{2,0},{4,6},{6,4},{8,10},{10,8},{12,14},{14,12},{1,3},{3,1},... | collective-permute-start | bytes 983048 | tf_op jit(solution)/shard_map/ppermute | solution.py:349
  18.6 2.7 %collective-permute-start.2 = (f32[32,1024]{1,0:T(8,128)S(1)}, f32[32,1024]{1,0:T(8,128)S(1)}, u32[]{:S(2)}, u32[]{:S(2)}) collective-permute-start(f32[32,1024]{1,0:T(8,128)S(1)} %slice.57), channel_id=1, source_target_pairs={{0,8},{2,10},{4,12},{6,14},{8,0},{10,2},{12,4},{14,6},{1,9},{3,11}... | collective-permute-start | bytes 393224 | tf_op jit(solution)/shard_map/ppermute | solution.py:349
  21.3 7.4 %collective-permute-done.4 = f32[64,1024]{1,0:T(8,128)S(1)} collective-permute-done((f32[64,1024]{1,0:T(8,128)S(1)}, f32[64,1024]{1,0:T(8,128)S(1)}, u32[]{:S(2)}, u32[]{:S(2)}) %collective-permute-start.4) | collective-permute-done | bytes 262176 | tf_op jit(solution)/shard_map/ppermute | solution.py:349
  28.8 0.6 collective-permute-start.5
  29.5 1.6 %collective-permute-start.3 = (f32[16,1024]{1,0:T(8,128)S(1)}, f32[16,1024]{1,0:T(8,128)S(1)}, u32[]{:S(2)}, u32[]{:S(2)}) collective-permute-start(f32[16,1024]{1,0:T(8,128)S(1)} %slice.59), channel_id=1, source_target_pairs={{0,2},{2,0},{4,6},{6,4},{8,10},{10,8},{12,14},{14,12},{1,3},{3,1},... | collective-permute-start | bytes 196616 | tf_op jit(solution)/shard_map/ppermute | solution.py:349
  31.1 2.7 %collective-permute-done.5 = f32[32,1024]{1,0:T(8,128)S(1)} collective-permute-done((f32[32,1024]{1,0:T(8,128)S(1)}, f32[32,1024]{1,0:T(8,128)S(1)}, u32[]{:S(2)}, u32[]{:S(2)}) %collective-permute-start.5) | collective-permute-done | bytes 131104 | tf_op jit(solution)/shard_map/ppermute | solution.py:349
  33.8 1.6 %collective-permute-start.6 = (f32[16,1024]{1,0:T(8,128)S(1)}, f32[16,1024]{1,0:T(8,128)S(1)}, u32[]{:S(2)}, u32[]{:S(2)}) collective-permute-start(f32[16,1024]{1,0:T(8,128)S(1)} %slice.63), channel_id=1, source_target_pairs={{0,8},{2,10},{4,12},{6,14},{8,0},{10,2},{12,4},{14,6},{1,9},{3,11}... | collective-permute-start | bytes 196616 | tf_op jit(solution)/shard_map/ppermute | solution.py:349
  35.6 3.9 %collective-permute-done.6 = f32[16,1024]{1,0:T(8,128)S(1)} collective-permute-done((f32[16,1024]{1,0:T(8,128)S(1)}, f32[16,1024]{1,0:T(8,128)S(1)}, u32[]{:S(2)}, u32[]{:S(2)}) %collective-permute-start.6) | collective-permute-done | bytes 65568 | tf_op jit(solution)/shard_map/ppermute | solution.py:349
  39.5 1.3 %collective-permute-start.9 = (f32[16,1280]{1,0:T(8,128)S(1)}, f32[16,1280]{1,0:T(8,128)S(1)}, u32[]{:S(2)}, u32[]{:S(2)}) collective-permute-start(f32[16,1280]{1,0:T(8,128)S(1)} %slice.67), channel_id=1, source_target_pairs={{0,8},{2,10},{4,12},{6,14},{8,0},{10,2},{12,4},{14,6},{1,9},{3,11}... | collective-permute-start | bytes 245768 | tf_op jit(solution)/shard_map/ppermute | solution.py:349
  40.9 4.1 %collective-permute-done.9 = f32[16,1280]{1,0:T(8,128)S(1)} collective-permute-done((f32[16,1280]{1,0:T(8,128)S(1)}, f32[16,1280]{1,0:T(8,128)S(1)}, u32[]{:S(2)}, u32[]{:S(2)}) %collective-permute-start.9) | collective-permute-done | bytes 81952 | tf_op jit(solution)/shard_map/ppermute | solution.py:349
  45.1 1.1 %collective-permute-done.12.refs_5_ = bf16[8,1280]{1,0:T(8,128)(2,1)S(1)} collective-permute-done((bf16[8,1280]{1,0:T(8,128)(2,1)S(1)}, bf16[8,1280]{1,0:T(8,128)(2,1)S(1)}, u32[]{:S(2)}, u32[]{:S(2)}) %collective-permute-start.12) | collective-permute-done | bytes 20512 | tf_op jit(solution)/shard_map/ppermute | solution.py:346
  46.2 4.3 %attend.1 = (bf16[8,3072]{1,0:T(8,128)(2,1)S(1)}, bf16[8,3072]{1,0:T(8,128)(2,1)S(1)}) custom-call(s32[9]{0:T(128)S(1)} %pad_add_fusion.1.scalars_ref, bf16[8,1024]{1,0:T(8,128)(2,1)S(1)} %get-tuple-element.74.refs_0_, bf16[8,1024]{1,0:T(8,128)(2,1)S(1)} %get-tuple-element.72.refs_1_, bf16[8,1280]{1,0:T(8,128)(2,1)S(1)} %get-tuple-element.70.refs_2_, ...), custom_call_target="tpu_custom_call" | custom-call | flops 201326592 | bytes 8388608 | tf_op jit(solution)/shard_map/attend/pallas_call | solution.py:266
  50.8 1.1 %collective-permute-done.13 = bf16[8,3072]{1,0:T(8,128)(2,1)S(1)} collective-permute-done((bf16[8,3072]{1,0:T(8,128)(2,1)S(1)}, bf16[8,3072]{1,0:T(8,128)(2,1)S(1)}, u32[]{:S(2)}, u32[]{:S(2)}) %collective-permute-start.13) | collective-permute-done | bytes 49184 | tf_op jit(solution)/shard_map/ppermute | solution.py:346
  51.9 1.3 %collective-permute-start.16 = (bf16[16,1536]{1,0:T(8,128)(2,1)S(1)}, bf16[16,1536]{1,0:T(8,128)(2,1)S(1)}, u32[]{:S(2)}, u32[]{:S(2)}) collective-permute-start(bf16[16,1536]{1,0:T(8,128)(2,1)S(1)} %get-tuple-element.67), channel_id=1, source_target_pairs={{0,2},{2,0},{4,6},{6,4},{8,10},{10,8},{12,14},{14,12},{1,3},{3,1},... | collective-permute-start | bytes 147464 | tf_op jit(solution)/shard_map/ppermute | solution.py:349
  53.2 0.9 %collective-permute-start.14 = (bf16[16,1536]{1,0:T(8,128)(2,1)S(1)}, bf16[16,1536]{1,0:T(8,128)(2,1)S(1)}, u32[]{:S(2)}, u32[]{:S(2)}) collective-permute-start(bf16[16,1536]{1,0:T(8,128)(2,1)S(1)} %get-tuple-element.68), channel_id=1, source_target_pairs={{0,8},{2,10},{4,12},{6,14},{8,0},{10,2},{12,4},{14,6},{1,9},{3,11}... | collective-permute-start | bytes 147464 | tf_op jit(solution)/shard_map/ppermute | solution.py:349
  54.1 2.0 %collective-permute-done.16 = bf16[16,1536]{1,0:T(8,128)(2,1)S(1)} collective-permute-done((bf16[16,1536]{1,0:T(8,128)(2,1)S(1)}, bf16[16,1536]{1,0:T(8,128)(2,1)S(1)}, u32[]{:S(2)}, u32[]{:S(2)}) %collective-permute-start.16) | collective-permute-done | bytes 49184 | tf_op jit(solution)/shard_map/ppermute | solution.py:349
  56.0 1.3 %collective-permute-start.18 = (bf16[32,1536]{1,0:T(8,128)(2,1)S(1)}, bf16[32,1536]{1,0:T(8,128)(2,1)S(1)}, u32[]{:S(2)}, u32[]{:S(2)}) collective-permute-start(bf16[32,1536]{1,0:T(8,128)(2,1)S(1)} %pad_maximum_fusion.3.refs_1_), channel_id=1, source_target_pairs={{0,8},{2,10},{4,12},{6,14},{8,0},{10,2},{12,4},{14,6},{1,9},{3,11}... | collective-permute-start | bytes 294920 | tf_op jit(solution)/shard_map/ppermute | solution.py:349
  57.4 1.8 %collective-permute-done.14 = bf16[16,1536]{1,0:T(8,128)(2,1)S(1)} collective-permute-done((bf16[16,1536]{1,0:T(8,128)(2,1)S(1)}, bf16[16,1536]{1,0:T(8,128)(2,1)S(1)}, u32[]{:S(2)}, u32[]{:S(2)}) %collective-permute-start.14) | collective-permute-done | bytes 49184 | tf_op jit(solution)/shard_map/ppermute | solution.py:349
  59.2 1.8 %collective-permute-start.15 = (bf16[32,1536]{1,0:T(8,128)(2,1)S(1)}, bf16[32,1536]{1,0:T(8,128)(2,1)S(1)}, u32[]{:S(2)}, u32[]{:S(2)}) collective-permute-start(bf16[32,1536]{1,0:T(8,128)(2,1)S(1)} %pad_maximum_fusion.2.refs_0_), channel_id=1, source_target_pairs={{0,4},{2,6},{4,0},{6,2},{8,12},{10,14},{12,8},{14,10},{1,5},{3,7},... | collective-permute-start | bytes 294920 | tf_op jit(solution)/shard_map/ppermute | solution.py:349
  61.0 3.1 %load.2 = (bf16[512,768]{1,0:T(8,128)(2,1)S(1)}, bf16[512,768]{1,0:T(8,128)(2,1)S(1)}, bf16[512,768]{1,0:T(8,128)(2,1)S(1)}, bf16[512,768]{1,0:T(8,128)(2,1)S(1)...) custom-call(bf16[32,1536]{1,0:T(8,128)(2,1)S(1)} %pad_maximum_fusion, ...), custom_call_target="tpu_custom_call" | custom-call | bytes 14155776 | tf_op jit(solution)/shard_map/load/pallas_call | solution.py:78
  65.1 3.7 %load.3 = (bf16[512,768]{1,0:T(8,128)(2,1)S(1)}, bf16[512,768]{1,0:T(8,128)(2,1)S(1)}, bf16[512,768]{1,0:T(8,128)(2,1)S(1)}, bf16[512,768]{1,0:T(8,128)(2,1)S(1)...) custom-call(bf16[64,1536]{1,0:T(8,128)(2,1)S(1)} %maximum_add_fusion, ...), custom_call_target="tpu_custom_call" | custom-call | bytes 14155776 | tf_op jit(solution)/shard_map/load/pallas_call | solution.py:78
  68.8 1.2 %collective-permute-done.19.refs_3_ = bf16[64,1536]{1,0:T(8,128)(2,1)S(1)} collective-permute-done((bf16[64,1536]{1,0:T(8,128)(2,1)S(1)}, bf16[64,1536]{1,0:T(8,128)(2,1)S(1)}, u32[]{:S(2)}, u32[]{:S(2)}) %collective-permute-start.19) | collective-permute-done | bytes 196640 | tf_op jit(solution)/shard_map/ppermute | solution.py:349
  70.4 2.0 %project_out.2 = (f32[64,1536]{1,0:T(8,128)S(1)}, f32[64,1536]{1,0:T(8,128)S(1)}) custom-call(s32[2]{0:T(128)S(1)} %pad_add_fusion.ids_ref, bf16[64,1536]{1,0:T(8,128)(2,1)S(1)} %maximum_add_fusion.refs_0_, bf16[64,1536]{1,0:T(8,128)(2,1)S(1)} %collective-permute-done.17.refs_1_, bf16[64,1536]{1,0:T(8,128)(2,1)S(1)} %pad_maximum_fusion.1.refs_1_.refs_2_, ...), custom_call_target="tpu_custom_call" | custom-call | flops 1207959552 | bytes 10223616 | tf_op jit(solution)/shard_map/project_out/pallas_call | solution.py:320
  72.3 1.4 %project_out.3 = (f32[64,768]{1,0:T(8,128)S(1)}, f32[64,768]{1,0:T(8,128)S(1)}) custom-call(s32[2]{0:T(128)S(1)} %pad_add_fusion.ids_ref, bf16[64,1536]{1,0:T(8,128)(2,1)S(1)} %maximum_add_fusion.refs_0_, bf16[64,1536]{1,0:T(8,128)(2,1)S(1)} %collective-permute-done.17.refs_1_, bf16[64,1536]{1,0:T(8,128)(2,1)S(1)} %pad_maximum_fusion.1.refs_1_.refs_2_, ...), custom_call_target="tpu_custom_call" | custom-call | flops 603979776 | bytes 5111808 | tf_op jit(solution)/shard_map/project_out/pallas_call | solution.py:320
  73.8 0.5 collective-permute-start.20
  74.3 0.9 %collective-permute-done.21 = f32[64,768]{1,0:T(8,128)S(1)} collective-permute-done((f32[64,768]{1,0:T(8,128)S(1)}, f32[64,768]{1,0:T(8,128)S(1)}, u32[]{:S(2)}, u32[]{:S(2)}) %collective-permute-start.21) | collective-permute-done | bytes 196640 | tf_op jit(solution)/shard_map/ppermute | solution.py:346
  75.3 0.5 collective-permute-done.20
  75.9 0.7 pad_maximum_fusion
  (56 shorter events, 3.6 us)
Async XLA Ops:
  0.0 1.9 %collective-permute-start = (bf16[64,2304]{1,0:T(8,128)(2,1)}, bf16[64,2304]{1,0:T(8,128)(2,1)S(1)}, u32[]{:S(2)}, u32[]{:S(2)}) collective-permute-start(bf16[64,2304]{1,0:T(8,128)(2,1)} %param.7), channel_id=1, source_target_pairs={{0,1},{1,0},{2,3},{3,2},{4,5},{5,4},{6,7},{7,6},{8,9},{9,8},{10,11... | collective-permute-start | bytes 884744 | tf_op jit(solution)/shard_map/ppermute | solution.py:346
  1.5 7.8 %copy-start.1 = (bf16[2304,512]{1,0:T(8,128)(2,1)S(1)}, bf16[2304,512]{1,0:T(8,128)(2,1)}, u32[]{:S(2)}) copy-start(bf16[2304,512]{1,0:T(8,128)(2,1)} %refs_0_.1) | copy-start | bytes 7077892
  6.3 12.3 %collective-permute-start.1 = (f32[64,1024]{1,0:T(8,128)S(1)}, f32[64,1024]{1,0:T(8,128)S(1)}, u32[]{:S(2)}, u32[]{:S(2)}) collective-permute-start(f32[64,1024]{1,0:T(8,128)S(1)} %get-tuple-element.37.refs_1_), channel_id=1, source_target_pairs={{0,4},{2,6},{4,0},{6,2},{8,12},{10,14},{12,8},{14,10},{1,5},{3,7},... | collective-permute-start | bytes 786440 | tf_op jit(solution)/shard_map/ppermute | solution.py:349
  16.5 28.5 %copy-start.2 = (s32[8]{0:T(128)S(1)}, s32[8]{0:T(128)}, u32[]{:S(2)}) copy-start(s32[8]{0:T(128)} %param.13) | copy-start | bytes 100
  16.5 12.8 %collective-permute-start.7 = (f32[64,1280]{1,0:T(8,128)S(1)}, f32[64,1280]{1,0:T(8,128)S(1)}, u32[]{:S(2)}, u32[]{:S(2)}) collective-permute-start(f32[64,1280]{1,0:T(8,128)S(1)} %get-tuple-element.41), channel_id=1, source_target_pairs={{0,2},{2,0},{4,6},{6,4},{8,10},{10,8},{12,14},{14,12},{1,3},{3,1},... | collective-permute-start | bytes 983048 | tf_op jit(solution)/shard_map/ppermute | solution.py:349
  18.1 10.6 %collective-permute-start.4 = (f32[64,1024]{1,0:T(8,128)S(1)}, f32[64,1024]{1,0:T(8,128)S(1)}, u32[]{:S(2)}, u32[]{:S(2)}) collective-permute-start(f32[64,1024]{1,0:T(8,128)S(1)} %get-tuple-element.39), channel_id=1, source_target_pairs={{0,4},{2,6},{4,0},{6,2},{8,12},{10,14},{12,8},{14,10},{1,5},{3,7},... | collective-permute-start | bytes 786440 | tf_op jit(solution)/shard_map/ppermute | solution.py:349
  18.6 10.9 %collective-permute-start.2 = (f32[32,1024]{1,0:T(8,128)S(1)}, f32[32,1024]{1,0:T(8,128)S(1)}, u32[]{:S(2)}, u32[]{:S(2)}) collective-permute-start(f32[32,1024]{1,0:T(8,128)S(1)} %slice.57), channel_id=1, source_target_pairs={{0,8},{2,10},{4,12},{6,14},{8,0},{10,2},{12,4},{14,6},{1,9},{3,11}... | collective-permute-start | bytes 393224 | tf_op jit(solution)/shard_map/ppermute | solution.py:349
  21.3 24.9 %copy-start = (bf16[8,1024,256]{2,1,0:T(8,128)(2,1)S(1)}, bf16[8,1024,256]{2,1,0:T(8,128)(2,1)}, u32[]{:S(2)}) copy-start(bf16[8,1024,256]{2,1,0:T(8,128)(2,1)} %refs_6_.1) | copy-start | bytes 12582916
  28.8 5.0 %collective-permute-start.5 = (f32[32,1024]{1,0:T(8,128)S(1)}, f32[32,1024]{1,0:T(8,128)S(1)}, u32[]{:S(2)}, u32[]{:S(2)}) collective-permute-start(f32[32,1024]{1,0:T(8,128)S(1)} %slice.61), channel_id=1, source_target_pairs={{0,2},{2,0},{4,6},{6,4},{8,10},{10,8},{12,14},{14,12},{1,3},{3,1},... | collective-permute-start | bytes 393224 | tf_op jit(solution)/shard_map/ppermute | solution.py:349
  29.4 10.1 %collective-permute-start.8 = (f32[32,1280]{1,0:T(8,128)S(1)}, f32[32,1280]{1,0:T(8,128)S(1)}, u32[]{:S(2)}, u32[]{:S(2)}) collective-permute-start(f32[32,1280]{1,0:T(8,128)S(1)} %slice.65), channel_id=1, source_target_pairs={{0,4},{2,6},{4,0},{6,2},{8,12},{10,14},{12,8},{14,10},{1,5},{3,7},... | collective-permute-start | bytes 491528 | tf_op jit(solution)/shard_map/ppermute | solution.py:349
  29.5 5.9 %collective-permute-start.3 = (f32[16,1024]{1,0:T(8,128)S(1)}, f32[16,1024]{1,0:T(8,128)S(1)}, u32[]{:S(2)}, u32[]{:S(2)}) collective-permute-start(f32[16,1024]{1,0:T(8,128)S(1)} %slice.59), channel_id=1, source_target_pairs={{0,2},{2,0},{4,6},{6,4},{8,10},{10,8},{12,14},{14,12},{1,3},{3,1},... | collective-permute-start | bytes 196616 | tf_op jit(solution)/shard_map/ppermute | solution.py:349
  33.8 5.6 %collective-permute-start.6 = (f32[16,1024]{1,0:T(8,128)S(1)}, f32[16,1024]{1,0:T(8,128)S(1)}, u32[]{:S(2)}, u32[]{:S(2)}) collective-permute-start(f32[16,1024]{1,0:T(8,128)S(1)} %slice.63), channel_id=1, source_target_pairs={{0,8},{2,10},{4,12},{6,14},{8,0},{10,2},{12,4},{14,6},{1,9},{3,11}... | collective-permute-start | bytes 196616 | tf_op jit(solution)/shard_map/ppermute | solution.py:349
  35.5 9.6 %collective-permute-start.10 = (bf16[8,1024]{1,0:T(8,128)(2,1)S(1)}, bf16[8,1024]{1,0:T(8,128)(2,1)S(1)}, u32[]{:S(2)}, u32[]{:S(2)}) collective-permute-start(bf16[8,1024]{1,0:T(8,128)(2,1)S(1)} %get-tuple-element.73), channel_id=1, source_target_pairs={{0,1},{1,0},{2,3},{3,2},{4,5},{5,4},{6,7},{7,6},{8,9},{9,8},{10,11... | collective-permute-start | bytes 49160 | tf_op jit(solution)/shard_map/ppermute | solution.py:346
  39.5 5.4 %collective-permute-start.9 = (f32[16,1280]{1,0:T(8,128)S(1)}, f32[16,1280]{1,0:T(8,128)S(1)}, u32[]{:S(2)}, u32[]{:S(2)}) collective-permute-start(f32[16,1280]{1,0:T(8,128)S(1)} %slice.67), channel_id=1, source_target_pairs={{0,8},{2,10},{4,12},{6,14},{8,0},{10,2},{12,4},{14,6},{1,9},{3,11}... | collective-permute-start | bytes 245768 | tf_op jit(solution)/shard_map/ppermute | solution.py:349
  40.8 4.3 %collective-permute-start.11 = (bf16[8,1024]{1,0:T(8,128)(2,1)S(1)}, bf16[8,1024]{1,0:T(8,128)(2,1)S(1)}, u32[]{:S(2)}, u32[]{:S(2)}) collective-permute-start(bf16[8,1024]{1,0:T(8,128)(2,1)S(1)} %get-tuple-element.71), channel_id=1, source_target_pairs={{0,1},{1,0},{2,3},{3,2},{4,5},{5,4},{6,7},{7,6},{8,9},{9,8},{10,11... | collective-permute-start | bytes 49160 | tf_op jit(solution)/shard_map/ppermute | solution.py:346
  45.0 1.3 %collective-permute-start.12 = (bf16[8,1280]{1,0:T(8,128)(2,1)S(1)}, bf16[8,1280]{1,0:T(8,128)(2,1)S(1)}, u32[]{:S(2)}, u32[]{:S(2)}) collective-permute-start(bf16[8,1280]{1,0:T(8,128)(2,1)S(1)} %get-tuple-element.69), channel_id=1, source_target_pairs={{0,1},{1,0},{2,3},{3,2},{4,5},{5,4},{6,7},{7,6},{8,9},{9,8},{10,11... | collective-permute-start | bytes 61448 | tf_op jit(solution)/shard_map/ppermute | solution.py:346
  50.5 1.3 %collective-permute-start.13 = (bf16[8,3072]{1,0:T(8,128)(2,1)S(1)}, bf16[8,3072]{1,0:T(8,128)(2,1)S(1)}, u32[]{:S(2)}, u32[]{:S(2)}) collective-permute-start(bf16[8,3072]{1,0:T(8,128)(2,1)S(1)} %get-tuple-element.43), channel_id=1, source_target_pairs={{0,1},{1,0},{2,3},{3,2},{4,5},{5,4},{6,7},{7,6},{8,9},{9,8},{10,11... | collective-permute-start | bytes 147464 | tf_op jit(solution)/shard_map/ppermute | solution.py:346
  51.9 4.2 %collective-permute-start.16 = (bf16[16,1536]{1,0:T(8,128)(2,1)S(1)}, bf16[16,1536]{1,0:T(8,128)(2,1)S(1)}, u32[]{:S(2)}, u32[]{:S(2)}) collective-permute-start(bf16[16,1536]{1,0:T(8,128)(2,1)S(1)} %get-tuple-element.67), channel_id=1, source_target_pairs={{0,2},{2,0},{4,6},{6,4},{8,10},{10,8},{12,14},{14,12},{1,3},{3,1},... | collective-permute-start | bytes 147464 | tf_op jit(solution)/shard_map/ppermute | solution.py:349
  53.2 6.0 %collective-permute-start.14 = (bf16[16,1536]{1,0:T(8,128)(2,1)S(1)}, bf16[16,1536]{1,0:T(8,128)(2,1)S(1)}, u32[]{:S(2)}, u32[]{:S(2)}) collective-permute-start(bf16[16,1536]{1,0:T(8,128)(2,1)S(1)} %get-tuple-element.68), channel_id=1, source_target_pairs={{0,8},{2,10},{4,12},{6,14},{8,0},{10,2},{12,4},{14,6},{1,9},{3,11}... | collective-permute-start | bytes 147464 | tf_op jit(solution)/shard_map/ppermute | solution.py:349
  56.0 8.2 %collective-permute-start.18 = (bf16[32,1536]{1,0:T(8,128)(2,1)S(1)}, bf16[32,1536]{1,0:T(8,128)(2,1)S(1)}, u32[]{:S(2)}, u32[]{:S(2)}) collective-permute-start(bf16[32,1536]{1,0:T(8,128)(2,1)S(1)} %pad_maximum_fusion.3.refs_1_), channel_id=1, source_target_pairs={{0,8},{2,10},{4,12},{6,14},{8,0},{10,2},{12,4},{14,6},{1,9},{3,11}... | collective-permute-start | bytes 294920 | tf_op jit(solution)/shard_map/ppermute | solution.py:349
  59.2 5.4 %collective-permute-start.15 = (bf16[32,1536]{1,0:T(8,128)(2,1)S(1)}, bf16[32,1536]{1,0:T(8,128)(2,1)S(1)}, u32[]{:S(2)}, u32[]{:S(2)}) collective-permute-start(bf16[32,1536]{1,0:T(8,128)(2,1)S(1)} %pad_maximum_fusion.2.refs_0_), channel_id=1, source_target_pairs={{0,4},{2,6},{4,0},{6,2},{8,12},{10,14},{12,8},{14,10},{1,5},{3,7},... | collective-permute-start | bytes 294920 | tf_op jit(solution)/shard_map/ppermute | solution.py:349
  64.2 5.7 %collective-permute-start.19 = (bf16[64,1536]{1,0:T(8,128)(2,1)S(1)}, bf16[64,1536]{1,0:T(8,128)(2,1)S(1)}, u32[]{:S(2)}, u32[]{:S(2)}) collective-permute-start(bf16[64,1536]{1,0:T(8,128)(2,1)S(1)} %pad_maximum_fusion.1.refs_1_.refs_2_), channel_id=1, source_target_pairs={{0,4},{2,6},{4,0},{6,2},{8,12},{10,14},{12,8},{14,10},{1,5},{3,7},... | collective-permute-start | bytes 589832 | tf_op jit(solution)/shard_map/ppermute | solution.py:349
  64.6 5.7 %collective-permute-start.17 = (bf16[64,1536]{1,0:T(8,128)(2,1)S(1)}, bf16[64,1536]{1,0:T(8,128)(2,1)S(1)}, u32[]{:S(2)}, u32[]{:S(2)}) collective-permute-start(bf16[64,1536]{1,0:T(8,128)(2,1)S(1)} %maximum_add_fusion.refs_0_), channel_id=1, source_target_pairs={{0,2},{2,0},{4,6},{6,4},{8,10},{10,8},{12,14},{14,12},{1,3},{3,1},... | collective-permute-start | bytes 589832 | tf_op jit(solution)/shard_map/ppermute | solution.py:349
  73.8 1.5 %collective-permute-start.21 = (f32[64,768]{1,0:T(8,128)S(1)}, f32[64,768]{1,0:T(8,128)S(1)}, u32[]{:S(2)}, u32[]{:S(2)}) collective-permute-start(f32[64,768]{1,0:T(8,128)S(1)} %get-tuple-element.66), channel_id=1, source_target_pairs={{0,1},{1,0},{2,3},{3,2},{4,5},{5,4},{6,7},{7,6},{8,9},{9,8},{10,11... | collective-permute-start | bytes 589832 | tf_op jit(solution)/shard_map/ppermute | solution.py:346
  73.8 2.0 %collective-permute-start.20 = (f32[64,1536]{1,0:T(8,128)S(1)}, f32[64,1536]{1,0:T(8,128)S(1)}, u32[]{:S(2)}, u32[]{:S(2)}) collective-permute-start(f32[64,1536]{1,0:T(8,128)S(1)} %get-tuple-element.58.refs_10_), channel_id=1, source_target_pairs={{0,1},{1,0},{2,3},{3,2},{4,5},{5,4},{6,7},{7,6},{8,9},{9,8},{10,11... | collective-permute-start | bytes 1179656 | tf_op jit(solution)/shard_map/ppermute | solution.py:346

commit v10 on v9

--- a/solution.py
+++ b/solution.py
@@ -97,32 +97,11 @@
 def project_kernel(orders, rows, first, widths, kv_width, after, ids_ref, own_ref, other_ref, w_ref, *refs):
     refs = list(refs)
     kv_ref = refs.pop(0) if kv_width else None
-    outs, (xs_ref, ws_ref, row_sem, w_sem) = refs[after:-4], refs[-4:]
+    outs, (xs_ref, ws_ref, w_sem) = refs[after:-3], refs[-3:]
     n = len(orders[0])
     half = n // 2
     me, core = ids_ref[0], ids_ref[1]
-    features = xs_ref.shape[2]
-
-    def row_copy(source_ref, chunk, p):
-        block = jnp.bitwise_xor(me, orders[chunk][p])
-        source = pl.ds(pl.multiple_of((block % half) * rows, rows), rows)
-        return pltpu.make_async_copy(
-            source_ref.at[source, :],
-            xs_ref.at[chunk, pl.ds(p * rows, rows), :],
-            row_sem.at[chunk, p],
-        )
-
-    for chunk, order in enumerate(orders):
-        for p in range(n):
-            mine = jnp.bitwise_xor(me, order[p]) // half == core
-
-            @pl.when(mine)
-            def _():
-                row_copy(own_ref, chunk, p).start()
-
-            @pl.when(jnp.logical_not(mine))
-            def _():
-                row_copy(other_ref, chunk, p).start()
+    features = xs_ref.shape[1]
 
     tiles, copies, at, source = [], [], 0, first
     depth = 768 if features % 768 == 0 else features
@@ -152,21 +131,32 @@
             source += tile
     per_tile = features // depth
     weights = InOrder(copies, 9)
-    cut = half * rows
-    ready = set()
+    def place_rows(low_ref, high_ref):
+        for j in range(n):
+            block = jnp.bitwise_xor(me, j) % half
+            source = low_ref if j < half else high_ref
+            xs_ref[j * rows : (j + 1) * rows, :] = source[
+                pl.ds(pl.multiple_of(block * rows, rows), rows), :
+            ]
+
+    low_mine = me // half == core
+
+    @pl.when(low_mine)
+    def _():
+        place_rows(own_ref, other_ref)
+
+    @pl.when(jnp.logical_not(low_mine))
+    def _():
+        place_rows(other_ref, own_ref)
+
     for t, (chunk, column, at, width) in enumerate(tiles):
-        if chunk not in ready:
-            ready.add(chunk)
-            for p in range(n):
-                row_copy(own_ref, chunk, p).wait()
         for part in range(per_tile):
             weights.wait(t * per_tile + part)
-        total = jnp.dot(
-            xs_ref[chunk], ws_ref[:, at : at + width], preferred_element_type=jnp.float32
-        )
+        total = jnp.dot(xs_ref[...], ws_ref[:, at : at + width], preferred_element_type=jnp.float32)
         span = slice(column, column + width)
-        outs[2 * chunk][:, span] = total[cut:]
-        outs[2 * chunk + 1][:, span] = total[:cut]
+        for p, j in enumerate(orders[chunk]):
+            out = outs[2 * chunk + 1] if p < half else outs[2 * chunk]
+            out[(p % half) * rows : (p % half + 1) * rows, span] = total[j * rows : (j + 1) * rows]
 
 
 def project(plan, rows, ids, tokens, other, query_weight, kv_weight, first, after):
@@ -186,12 +176,11 @@
     outs = pl.pallas_call(
         functools.partial(project_kernel, orders, rows, first, widths, kv_width, len(after)),
         out_shape=outs,
-        in_specs=[SMEM, ANY, ANY] + [HBM] * len(weights) + [ANY] * len(after),
+        in_specs=[SMEM, VMEM, VMEM] + [HBM] * len(weights) + [ANY] * len(after),
         out_specs=[VMEM] * len(outs),
         scratch_shapes=[
-            pltpu.VMEM((len(orders), n * rows, features), tokens.dtype),
+            pltpu.VMEM((n * rows, features), tokens.dtype),
             pltpu.VMEM((features, columns), tokens.dtype),
-            pltpu.SemaphoreType.DMA((len(orders), n)),
             pltpu.SemaphoreType.DMA((copies,)),
         ],
         compiler_params=pltpu.CompilerParams(vmem_limit_bytes=46 * MIB),

time: 76.8 us -> 73.4 us (0.956)
  Pallas kernels: 26.2 us -> 23.3 us
    pallas_call x2, Pallas kernels: 11.6 us -> 8.76 us  [project(): pl.pallas_call(functools.partial(project_kernel, orders, rows, first, wid...]
  transfers between devices with their start and end apart: 22 -> 22, of which waited for: 13 -> 13; matrix products, arithmetic and copies ran while one was open for 2% -> 2% of each run, Pallas kernels for 18% -> 17%
where the time goes in v10:
time: 73.4 us; the launch traced here: 73.3 us
  waiting for transfers between devices  27 us (37%)
  Pallas kernels  23.3 us (32%)
  starting transfers between devices  20.4 us (28%)
  other arithmetic  2.26 us (3%)
    ppermute x15, waiting for transfers between devices, across(): return lax.ppermute(array, 'gx', [(g, g ^ mask) for g in range(n)])  23 us
    ppermute x15, starting transfers between devices, across(): return lax.ppermute(array, 'gx', [(g, g ^ mask) for g in range(n)])  19 us
    pallas_call x2, Pallas kernels, project(): pl.pallas_call(functools.partial(project_kernel, orders, rows, first, wid...  8.76 us
    pallas_call x2, Pallas kernels, load(): pl.pallas_call(functools.partial(load_kernel, len(after), cuts, len(array...  6.84 us
    pallas_call x1, Pallas kernels, attend(): pl.pallas_call(functools.partial(attend_kernel, parts), out_shape=(out, o...  4.3 us
    ppermute x7, waiting for transfers between devices, swap(): return lax.ppermute(array, 'gy', [(0, 1), (1, 0)])  3.97 us
    pallas_call x2, Pallas kernels, project_out(): pl.pallas_call(functools.partial(output_kernel, orders, rows, columns, pi...  3.4 us
  transfers between devices with their start and end apart: 22, of which 13 were waited for; matrix products, arithmetic and copies ran while one was open for 2% of the time, Pallas kernels for 17%

profile of v10, /device:TPU:0, one launch (start us, length us, event | category | flops | bytes accessed | tf_op | source)
XLA Modules:
  0.0 73.3 jit_solution(16895127784863075440)
XLA Ops:
  0.5 1.0 %broadcast_select_fusion.own_ref = bf16[64,2304]{1,0:T(8,128)(2,1)S(1)} fusion(bf16[64,2304]{1,0:T(8,128)(2,1)} %param.7, pred[]{:T(512)S(6)} %lt.6), kind=kLoop, calls=%fused_computation.2 | loop fusion | flops 147456 | bytes 589825 | tf_op jit(solution)/shard_map/jit(_where)/select_n | solution.py:341
  1.9 3.4 %project.2 = (f32[64,1024]{1,0:T(8,128)S(1)}, f32[64,1024]{1,0:T(8,128)S(1)}) custom-call(s32[2]{0:T(128)S(1)} %pad_add_fusion.ids_ref, bf16[64,2304]{1,0:T(8,128)(2,1)S(1)} %broadcast_select_fusion.own_ref, bf16[64,2304]{1,0:T(8,128)(2,1)S(1)} %collective-permute-done.other_ref, bf16[2304,3072]{1,0:T(8,128)(2,1)} %w_ref.3), custom_call_target="tpu_custom_call" | custom-call | flops 603979776 | bytes 5242880 | tf_op jit(solution)/shard_map/project/pallas_call | solution.py:176
  5.3 3.0 %collective-permute-start.1 = (f32[64,1024]{1,0:T(8,128)S(1)}, f32[64,1024]{1,0:T(8,128)S(1)}, u32[]{:S(2)}, u32[]{:S(2)}) collective-permute-start(f32[64,1024]{1,0:T(8,128)S(1)} %get-tuple-element.37.refs_1_), channel_id=1, source_target_pairs={{0,4},{2,6},{4,0},{6,2},{8,12},{10,14},{12,8},{14,10},{1,5},{3,7},... | collective-permute-start | bytes 786440 | tf_op jit(solution)/shard_map/ppermute | solution.py:338
  8.3 5.3 %project.3 = (f32[64,1024]{1,0:T(8,128)S(1)}, f32[64,1024]{1,0:T(8,128)S(1)}, f32[64,1280]{1,0:T(8,128)S(1)}, f32[64,1280]{1,0:T(8,128)S(1)}) custom-call(s32[2]{0:T(128)S(1)} %pad_add_fusion.ids_ref, bf16[64,2304]{1,0:T(8,128)(2,1)S(1)} %broadcast_select_fusion.own_ref, bf16[64,2304]{1,0:T(8,128)(2,1)S(1)} %collective-permute-done.other_ref, ...), custom_call_target="tpu_custom_call" | custom-call | flops 1358954496 | bytes 11796480 | tf_op jit(solution)/shard_map/project/pallas_call | solution.py:176
  13.7 1.6 %collective-permute-start.7 = (f32[64,1280]{1,0:T(8,128)S(1)}, f32[64,1280]{1,0:T(8,128)S(1)}, u32[]{:S(2)}, u32[]{:S(2)}) collective-permute-start(f32[64,1280]{1,0:T(8,128)S(1)} %get-tuple-element.41), channel_id=1, source_target_pairs={{0,2},{2,0},{4,6},{6,4},{8,10},{10,8},{12,14},{14,12},{1,3},{3,1},... | collective-permute-start | bytes 983048 | tf_op jit(solution)/shard_map/ppermute | solution.py:338
  15.8 2.6 %collective-permute-start.2 = (f32[32,1024]{1,0:T(8,128)S(1)}, f32[32,1024]{1,0:T(8,128)S(1)}, u32[]{:S(2)}, u32[]{:S(2)}) collective-permute-start(f32[32,1024]{1,0:T(8,128)S(1)} %slice.57), channel_id=1, source_target_pairs={{0,8},{2,10},{4,12},{6,14},{8,0},{10,2},{12,4},{14,6},{1,9},{3,11}... | collective-permute-start | bytes 393224 | tf_op jit(solution)/shard_map/ppermute | solution.py:338
  18.4 7.4 %collective-permute-done.4 = f32[64,1024]{1,0:T(8,128)S(1)} collective-permute-done((f32[64,1024]{1,0:T(8,128)S(1)}, f32[64,1024]{1,0:T(8,128)S(1)}, u32[]{:S(2)}, u32[]{:S(2)}) %collective-permute-start.4) | collective-permute-done | bytes 262176 | tf_op jit(solution)/shard_map/ppermute | solution.py:338
  25.9 0.6 collective-permute-start.5
  26.7 1.6 %collective-permute-start.3 = (f32[16,1024]{1,0:T(8,128)S(1)}, f32[16,1024]{1,0:T(8,128)S(1)}, u32[]{:S(2)}, u32[]{:S(2)}) collective-permute-start(f32[16,1024]{1,0:T(8,128)S(1)} %slice.59), channel_id=1, source_target_pairs={{0,2},{2,0},{4,6},{6,4},{8,10},{10,8},{12,14},{14,12},{1,3},{3,1},... | collective-permute-start | bytes 196616 | tf_op jit(solution)/shard_map/ppermute | solution.py:338
  28.3 2.7 %collective-permute-done.5 = f32[32,1024]{1,0:T(8,128)S(1)} collective-permute-done((f32[32,1024]{1,0:T(8,128)S(1)}, f32[32,1024]{1,0:T(8,128)S(1)}, u32[]{:S(2)}, u32[]{:S(2)}) %collective-permute-start.5) | collective-permute-done | bytes 131104 | tf_op jit(solution)/shard_map/ppermute | solution.py:338
  31.0 1.5 %collective-permute-start.6 = (f32[16,1024]{1,0:T(8,128)S(1)}, f32[16,1024]{1,0:T(8,128)S(1)}, u32[]{:S(2)}, u32[]{:S(2)}) collective-permute-start(f32[16,1024]{1,0:T(8,128)S(1)} %slice.63), channel_id=1, source_target_pairs={{0,8},{2,10},{4,12},{6,14},{8,0},{10,2},{12,4},{14,6},{1,9},{3,11}... | collective-permute-start | bytes 196616 | tf_op jit(solution)/shard_map/ppermute | solution.py:338
  32.6 4.0 %collective-permute-done.6 = f32[16,1024]{1,0:T(8,128)S(1)} collective-permute-done((f32[16,1024]{1,0:T(8,128)S(1)}, f32[16,1024]{1,0:T(8,128)S(1)}, u32[]{:S(2)}, u32[]{:S(2)}) %collective-permute-start.6) | collective-permute-done | bytes 65568 | tf_op jit(solution)/shard_map/ppermute | solution.py:338
  36.7 1.1 %collective-permute-start.9 = (f32[16,1280]{1,0:T(8,128)S(1)}, f32[16,1280]{1,0:T(8,128)S(1)}, u32[]{:S(2)}, u32[]{:S(2)}) collective-permute-start(f32[16,1280]{1,0:T(8,128)S(1)} %slice.67), channel_id=1, source_target_pairs={{0,8},{2,10},{4,12},{6,14},{8,0},{10,2},{12,4},{14,6},{1,9},{3,11}... | collective-permute-start | bytes 245768 | tf_op jit(solution)/shard_map/ppermute | solution.py:338
  37.8 4.3 %collective-permute-done.9 = f32[16,1280]{1,0:T(8,128)S(1)} collective-permute-done((f32[16,1280]{1,0:T(8,128)S(1)}, f32[16,1280]{1,0:T(8,128)S(1)}, u32[]{:S(2)}, u32[]{:S(2)}) %collective-permute-start.9) | collective-permute-done | bytes 81952 | tf_op jit(solution)/shard_map/ppermute | solution.py:338
  42.3 1.1 %collective-permute-done.12.refs_5_ = bf16[8,1280]{1,0:T(8,128)(2,1)S(1)} collective-permute-done((bf16[8,1280]{1,0:T(8,128)(2,1)S(1)}, bf16[8,1280]{1,0:T(8,128)(2,1)S(1)}, u32[]{:S(2)}, u32[]{:S(2)}) %collective-permute-start.12) | collective-permute-done | bytes 20512 | tf_op jit(solution)/shard_map/ppermute | solution.py:335
  43.4 4.3 %attend.1 = (bf16[8,3072]{1,0:T(8,128)(2,1)S(1)}, bf16[8,3072]{1,0:T(8,128)(2,1)S(1)}) custom-call(s32[9]{0:T(128)S(1)} %pad_add_fusion.1.scalars_ref, bf16[8,1024]{1,0:T(8,128)(2,1)S(1)} %get-tuple-element.74.refs_0_, bf16[8,1024]{1,0:T(8,128)(2,1)S(1)} %get-tuple-element.72.refs_1_, bf16[8,1280]{1,0:T(8,128)(2,1)S(1)} %get-tuple-element.70.refs_2_, ...), custom_call_target="tpu_custom_call" | custom-call | flops 201326592 | bytes 8388608 | tf_op jit(solution)/shard_map/attend/pallas_call | solution.py:255
  47.9 1.1 %collective-permute-done.13 = bf16[8,3072]{1,0:T(8,128)(2,1)S(1)} collective-permute-done((bf16[8,3072]{1,0:T(8,128)(2,1)S(1)}, bf16[8,3072]{1,0:T(8,128)(2,1)S(1)}, u32[]{:S(2)}, u32[]{:S(2)}) %collective-permute-start.13) | collective-permute-done | bytes 49184 | tf_op jit(solution)/shard_map/ppermute | solution.py:335
  49.0 1.2 %collective-permute-start.16 = (bf16[16,1536]{1,0:T(8,128)(2,1)S(1)}, bf16[16,1536]{1,0:T(8,128)(2,1)S(1)}, u32[]{:S(2)}, u32[]{:S(2)}) collective-permute-start(bf16[16,1536]{1,0:T(8,128)(2,1)S(1)} %get-tuple-element.67), channel_id=1, source_target_pairs={{0,2},{2,0},{4,6},{6,4},{8,10},{10,8},{12,14},{14,12},{1,3},{3,1},... | collective-permute-start | bytes 147464 | tf_op jit(solution)/shard_map/ppermute | solution.py:338
  50.2 1.0 %collective-permute-start.14 = (bf16[16,1536]{1,0:T(8,128)(2,1)S(1)}, bf16[16,1536]{1,0:T(8,128)(2,1)S(1)}, u32[]{:S(2)}, u32[]{:S(2)}) collective-permute-start(bf16[16,1536]{1,0:T(8,128)(2,1)S(1)} %get-tuple-element.68), channel_id=1, source_target_pairs={{0,8},{2,10},{4,12},{6,14},{8,0},{10,2},{12,4},{14,6},{1,9},{3,11}... | collective-permute-start | bytes 147464 | tf_op jit(solution)/shard_map/ppermute | solution.py:338
  51.2 1.9 %collective-permute-done.16 = bf16[16,1536]{1,0:T(8,128)(2,1)S(1)} collective-permute-done((bf16[16,1536]{1,0:T(8,128)(2,1)S(1)}, bf16[16,1536]{1,0:T(8,128)(2,1)S(1)}, u32[]{:S(2)}, u32[]{:S(2)}) %collective-permute-start.16) | collective-permute-done | bytes 49184 | tf_op jit(solution)/shard_map/ppermute | solution.py:338
  53.2 1.1 %collective-permute-start.18 = (bf16[32,1536]{1,0:T(8,128)(2,1)S(1)}, bf16[32,1536]{1,0:T(8,128)(2,1)S(1)}, u32[]{:S(2)}, u32[]{:S(2)}) collective-permute-start(bf16[32,1536]{1,0:T(8,128)(2,1)S(1)} %pad_maximum_fusion.3.refs_1_), channel_id=1, source_target_pairs={{0,8},{2,10},{4,12},{6,14},{8,0},{10,2},{12,4},{14,6},{1,9},{3,11}... | collective-permute-start | bytes 294920 | tf_op jit(solution)/shard_map/ppermute | solution.py:338
  54.3 1.5 %collective-permute-done.14 = bf16[16,1536]{1,0:T(8,128)(2,1)S(1)} collective-permute-done((bf16[16,1536]{1,0:T(8,128)(2,1)S(1)}, bf16[16,1536]{1,0:T(8,128)(2,1)S(1)}, u32[]{:S(2)}, u32[]{:S(2)}) %collective-permute-start.14) | collective-permute-done | bytes 49184 | tf_op jit(solution)/shard_map/ppermute | solution.py:338
  55.9 2.1 %collective-permute-start.15 = (bf16[32,1536]{1,0:T(8,128)(2,1)S(1)}, bf16[32,1536]{1,0:T(8,128)(2,1)S(1)}, u32[]{:S(2)}, u32[]{:S(2)}) collective-permute-start(bf16[32,1536]{1,0:T(8,128)(2,1)S(1)} %pad_maximum_fusion.2.refs_0_), channel_id=1, source_target_pairs={{0,4},{2,6},{4,0},{6,2},{8,12},{10,14},{12,8},{14,10},{1,5},{3,7},... | collective-permute-start | bytes 294920 | tf_op jit(solution)/shard_map/ppermute | solution.py:338
  57.9 3.1 %load.2 = (bf16[512,768]{1,0:T(8,128)(2,1)S(1)}, bf16[512,768]{1,0:T(8,128)(2,1)S(1)}, bf16[512,768]{1,0:T(8,128)(2,1)S(1)}, bf16[512,768]{1,0:T(8,128)(2,1)S(1)...) custom-call(bf16[32,1536]{1,0:T(8,128)(2,1)S(1)} %pad_maximum_fusion, ...), custom_call_target="tpu_custom_call" | custom-call | bytes 14155776 | tf_op jit(solution)/shard_map/load/pallas_call | solution.py:78
  61.3 0.9 %collective-permute-start.17 = (bf16[64,1536]{1,0:T(8,128)(2,1)S(1)}, bf16[64,1536]{1,0:T(8,128)(2,1)S(1)}, u32[]{:S(2)}, u32[]{:S(2)}) collective-permute-start(bf16[64,1536]{1,0:T(8,128)(2,1)S(1)} %maximum_add_fusion.refs_0_), channel_id=1, source_target_pairs={{0,2},{2,0},{4,6},{6,4},{8,10},{10,8},{12,14},{14,12},{1,3},{3,1},... | collective-permute-start | bytes 589832 | tf_op jit(solution)/shard_map/ppermute | solution.py:338
  62.2 3.7 %load.3 = (bf16[512,768]{1,0:T(8,128)(2,1)S(1)}, bf16[512,768]{1,0:T(8,128)(2,1)S(1)}, bf16[512,768]{1,0:T(8,128)(2,1)S(1)}, bf16[512,768]{1,0:T(8,128)(2,1)S(1)...) custom-call(bf16[64,1536]{1,0:T(8,128)(2,1)S(1)} %maximum_add_fusion, ...), custom_call_target="tpu_custom_call" | custom-call | bytes 14155776 | tf_op jit(solution)/shard_map/load/pallas_call | solution.py:78
  65.9 1.0 %collective-permute-done.19.refs_3_ = bf16[64,1536]{1,0:T(8,128)(2,1)S(1)} collective-permute-done((bf16[64,1536]{1,0:T(8,128)(2,1)S(1)}, bf16[64,1536]{1,0:T(8,128)(2,1)S(1)}, u32[]{:S(2)}, u32[]{:S(2)}) %collective-permute-start.19) | collective-permute-done | bytes 196640 | tf_op jit(solution)/shard_map/ppermute | solution.py:338
  67.0 2.0 %project_out.2 = (f32[64,1536]{1,0:T(8,128)S(1)}, f32[64,1536]{1,0:T(8,128)S(1)}) custom-call(s32[2]{0:T(128)S(1)} %pad_add_fusion.ids_ref, bf16[64,1536]{1,0:T(8,128)(2,1)S(1)} %maximum_add_fusion.refs_0_, bf16[64,1536]{1,0:T(8,128)(2,1)S(1)} %collective-permute-done.17.refs_1_, bf16[64,1536]{1,0:T(8,128)(2,1)S(1)} %pad_maximum_fusion.1.refs_1_.refs_2_, ...), custom_call_target="tpu_custom_call" | custom-call | flops 1207959552 | bytes 10223616 | tf_op jit(solution)/shard_map/project_out/pallas_call | solution.py:309
  69.0 1.4 %project_out.3 = (f32[64,768]{1,0:T(8,128)S(1)}, f32[64,768]{1,0:T(8,128)S(1)}) custom-call(s32[2]{0:T(128)S(1)} %pad_add_fusion.ids_ref, bf16[64,1536]{1,0:T(8,128)(2,1)S(1)} %maximum_add_fusion.refs_0_, bf16[64,1536]{1,0:T(8,128)(2,1)S(1)} %collective-permute-done.17.refs_1_, bf16[64,1536]{1,0:T(8,128)(2,1)S(1)} %pad_maximum_fusion.1.refs_1_.refs_2_, ...), custom_call_target="tpu_custom_call" | custom-call | flops 603979776 | bytes 5111808 | tf_op jit(solution)/shard_map/project_out/pallas_call | solution.py:309
  71.0 0.9 %collective-permute-done.21 = f32[64,768]{1,0:T(8,128)S(1)} collective-permute-done((f32[64,768]{1,0:T(8,128)S(1)}, f32[64,768]{1,0:T(8,128)S(1)}, u32[]{:S(2)}, u32[]{:S(2)}) %collective-permute-start.21) | collective-permute-done | bytes 196640 | tf_op jit(solution)/shard_map/ppermute | solution.py:335
  72.0 0.5 collective-permute-done.20
  72.5 0.7 %pad_maximum_fusion = bf16[64,2304]{1,0:T(8,128)(2,1)} fusion(bf16[64,768]{1,0:T(8,128)(2,1)S(1)} %add_convert_fusion.1, bf16[64,1536]{1,0:T(8,128)(2,1)S(1)} %add_convert_fusion), kind=kLoop, calls=%fused_computation.1 | loop fusion | flops 589824 | bytes 589824 | tf_op jit(solution)/shard_map/concatenate | solution.py:407
  (56 shorter events, 3.2 us)
Async XLA Ops:
  0.0 1.9 %collective-permute-start = (bf16[64,2304]{1,0:T(8,128)(2,1)}, bf16[64,2304]{1,0:T(8,128)(2,1)S(1)}, u32[]{:S(2)}, u32[]{:S(2)}) collective-permute-start(bf16[64,2304]{1,0:T(8,128)(2,1)} %param.7), channel_id=1, source_target_pairs={{0,1},{1,0},{2,3},{3,2},{4,5},{5,4},{6,7},{7,6},{8,9},{9,8},{10,11... | collective-permute-start | bytes 884744 | tf_op jit(solution)/shard_map/ppermute | solution.py:335
  1.5 6.8 %copy-start.1 = (bf16[2304,512]{1,0:T(8,128)(2,1)S(1)}, bf16[2304,512]{1,0:T(8,128)(2,1)}, u32[]{:S(2)}) copy-start(bf16[2304,512]{1,0:T(8,128)(2,1)} %refs_0_.1) | copy-start | bytes 7077892
  5.3 10.4 %collective-permute-start.1 = (f32[64,1024]{1,0:T(8,128)S(1)}, f32[64,1024]{1,0:T(8,128)S(1)}, u32[]{:S(2)}, u32[]{:S(2)}) collective-permute-start(f32[64,1024]{1,0:T(8,128)S(1)} %get-tuple-element.37.refs_1_), channel_id=1, source_target_pairs={{0,4},{2,6},{4,0},{6,2},{8,12},{10,14},{12,8},{14,10},{1,5},{3,7},... | collective-permute-start | bytes 786440 | tf_op jit(solution)/shard_map/ppermute | solution.py:338
  13.7 28.5 %copy-start.2 = (s32[8]{0:T(128)S(1)}, s32[8]{0:T(128)}, u32[]{:S(2)}) copy-start(s32[8]{0:T(128)} %param.13) | copy-start | bytes 100
  13.7 12.8 %collective-permute-start.7 = (f32[64,1280]{1,0:T(8,128)S(1)}, f32[64,1280]{1,0:T(8,128)S(1)}, u32[]{:S(2)}, u32[]{:S(2)}) collective-permute-start(f32[64,1280]{1,0:T(8,128)S(1)} %get-tuple-element.41), channel_id=1, source_target_pairs={{0,2},{2,0},{4,6},{6,4},{8,10},{10,8},{12,14},{14,12},{1,3},{3,1},... | collective-permute-start | bytes 983048 | tf_op jit(solution)/shard_map/ppermute | solution.py:338
  15.3 10.6 %collective-permute-start.4 = (f32[64,1024]{1,0:T(8,128)S(1)}, f32[64,1024]{1,0:T(8,128)S(1)}, u32[]{:S(2)}, u32[]{:S(2)}) collective-permute-start(f32[64,1024]{1,0:T(8,128)S(1)} %get-tuple-element.39), channel_id=1, source_target_pairs={{0,4},{2,6},{4,0},{6,2},{8,12},{10,14},{12,8},{14,10},{1,5},{3,7},... | collective-permute-start | bytes 786440 | tf_op jit(solution)/shard_map/ppermute | solution.py:338
  15.8 10.9 %collective-permute-start.2 = (f32[32,1024]{1,0:T(8,128)S(1)}, f32[32,1024]{1,0:T(8,128)S(1)}, u32[]{:S(2)}, u32[]{:S(2)}) collective-permute-start(f32[32,1024]{1,0:T(8,128)S(1)} %slice.57), channel_id=1, source_target_pairs={{0,8},{2,10},{4,12},{6,14},{8,0},{10,2},{12,4},{14,6},{1,9},{3,11}... | collective-permute-start | bytes 393224 | tf_op jit(solution)/shard_map/ppermute | solution.py:338
  18.4 24.9 %copy-start = (bf16[8,1024,256]{2,1,0:T(8,128)(2,1)S(1)}, bf16[8,1024,256]{2,1,0:T(8,128)(2,1)}, u32[]{:S(2)}) copy-start(bf16[8,1024,256]{2,1,0:T(8,128)(2,1)} %refs_6_.1) | copy-start | bytes 12582916
  25.9 5.0 %collective-permute-start.5 = (f32[32,1024]{1,0:T(8,128)S(1)}, f32[32,1024]{1,0:T(8,128)S(1)}, u32[]{:S(2)}, u32[]{:S(2)}) collective-permute-start(f32[32,1024]{1,0:T(8,128)S(1)} %slice.61), channel_id=1, source_target_pairs={{0,2},{2,0},{4,6},{6,4},{8,10},{10,8},{12,14},{14,12},{1,3},{3,1},... | collective-permute-start | bytes 393224 | tf_op jit(solution)/shard_map/ppermute | solution.py:338
  26.6 10.1 %collective-permute-start.8 = (f32[32,1280]{1,0:T(8,128)S(1)}, f32[32,1280]{1,0:T(8,128)S(1)}, u32[]{:S(2)}, u32[]{:S(2)}) collective-permute-start(f32[32,1280]{1,0:T(8,128)S(1)} %slice.65), channel_id=1, source_target_pairs={{0,4},{2,6},{4,0},{6,2},{8,12},{10,14},{12,8},{14,10},{1,5},{3,7},... | collective-permute-start | bytes 491528 | tf_op jit(solution)/shard_map/ppermute | solution.py:338
  26.7 5.8 %collective-permute-start.3 = (f32[16,1024]{1,0:T(8,128)S(1)}, f32[16,1024]{1,0:T(8,128)S(1)}, u32[]{:S(2)}, u32[]{:S(2)}) collective-permute-start(f32[16,1024]{1,0:T(8,128)S(1)} %slice.59), channel_id=1, source_target_pairs={{0,2},{2,0},{4,6},{6,4},{8,10},{10,8},{12,14},{14,12},{1,3},{3,1},... | collective-permute-start | bytes 196616 | tf_op jit(solution)/shard_map/ppermute | solution.py:338
  31.0 5.6 %collective-permute-start.6 = (f32[16,1024]{1,0:T(8,128)S(1)}, f32[16,1024]{1,0:T(8,128)S(1)}, u32[]{:S(2)}, u32[]{:S(2)}) collective-permute-start(f32[16,1024]{1,0:T(8,128)S(1)} %slice.63), channel_id=1, source_target_pairs={{0,8},{2,10},{4,12},{6,14},{8,0},{10,2},{12,4},{14,6},{1,9},{3,11}... | collective-permute-start | bytes 196616 | tf_op jit(solution)/shard_map/ppermute | solution.py:338
  32.5 9.8 %collective-permute-start.10 = (bf16[8,1024]{1,0:T(8,128)(2,1)S(1)}, bf16[8,1024]{1,0:T(8,128)(2,1)S(1)}, u32[]{:S(2)}, u32[]{:S(2)}) collective-permute-start(bf16[8,1024]{1,0:T(8,128)(2,1)S(1)} %get-tuple-element.73), channel_id=1, source_target_pairs={{0,1},{1,0},{2,3},{3,2},{4,5},{5,4},{6,7},{7,6},{8,9},{9,8},{10,11... | collective-permute-start | bytes 49160 | tf_op jit(solution)/shard_map/ppermute | solution.py:335
  36.7 5.4 %collective-permute-start.9 = (f32[16,1280]{1,0:T(8,128)S(1)}, f32[16,1280]{1,0:T(8,128)S(1)}, u32[]{:S(2)}, u32[]{:S(2)}) collective-permute-start(f32[16,1280]{1,0:T(8,128)S(1)} %slice.67), channel_id=1, source_target_pairs={{0,8},{2,10},{4,12},{6,14},{8,0},{10,2},{12,4},{14,6},{1,9},{3,11}... | collective-permute-start | bytes 245768 | tf_op jit(solution)/shard_map/ppermute | solution.py:338
  37.8 4.5 %collective-permute-start.11 = (bf16[8,1024]{1,0:T(8,128)(2,1)S(1)}, bf16[8,1024]{1,0:T(8,128)(2,1)S(1)}, u32[]{:S(2)}, u32[]{:S(2)}) collective-permute-start(bf16[8,1024]{1,0:T(8,128)(2,1)S(1)} %get-tuple-element.71), channel_id=1, source_target_pairs={{0,1},{1,0},{2,3},{3,2},{4,5},{5,4},{6,7},{7,6},{8,9},{9,8},{10,11... | collective-permute-start | bytes 49160 | tf_op jit(solution)/shard_map/ppermute | solution.py:335
  42.1 1.3 %collective-permute-start.12 = (bf16[8,1280]{1,0:T(8,128)(2,1)S(1)}, bf16[8,1280]{1,0:T(8,128)(2,1)S(1)}, u32[]{:S(2)}, u32[]{:S(2)}) collective-permute-start(bf16[8,1280]{1,0:T(8,128)(2,1)S(1)} %get-tuple-element.69), channel_id=1, source_target_pairs={{0,1},{1,0},{2,3},{3,2},{4,5},{5,4},{6,7},{7,6},{8,9},{9,8},{10,11... | collective-permute-start | bytes 61448 | tf_op jit(solution)/shard_map/ppermute | solution.py:335
  47.7 1.3 %collective-permute-start.13 = (bf16[8,3072]{1,0:T(8,128)(2,1)S(1)}, bf16[8,3072]{1,0:T(8,128)(2,1)S(1)}, u32[]{:S(2)}, u32[]{:S(2)}) collective-permute-start(bf16[8,3072]{1,0:T(8,128)(2,1)S(1)} %get-tuple-element.43), channel_id=1, source_target_pairs={{0,1},{1,0},{2,3},{3,2},{4,5},{5,4},{6,7},{7,6},{8,9},{9,8},{10,11... | collective-permute-start | bytes 147464 | tf_op jit(solution)/shard_map/ppermute | solution.py:335
  49.0 4.2 %collective-permute-start.16 = (bf16[16,1536]{1,0:T(8,128)(2,1)S(1)}, bf16[16,1536]{1,0:T(8,128)(2,1)S(1)}, u32[]{:S(2)}, u32[]{:S(2)}) collective-permute-start(bf16[16,1536]{1,0:T(8,128)(2,1)S(1)} %get-tuple-element.67), channel_id=1, source_target_pairs={{0,2},{2,0},{4,6},{6,4},{8,10},{10,8},{12,14},{14,12},{1,3},{3,1},... | collective-permute-start | bytes 147464 | tf_op jit(solution)/shard_map/ppermute | solution.py:338
  50.2 5.6 %collective-permute-start.14 = (bf16[16,1536]{1,0:T(8,128)(2,1)S(1)}, bf16[16,1536]{1,0:T(8,128)(2,1)S(1)}, u32[]{:S(2)}, u32[]{:S(2)}) collective-permute-start(bf16[16,1536]{1,0:T(8,128)(2,1)S(1)} %get-tuple-element.68), channel_id=1, source_target_pairs={{0,8},{2,10},{4,12},{6,14},{8,0},{10,2},{12,4},{14,6},{1,9},{3,11}... | collective-permute-start | bytes 147464 | tf_op jit(solution)/shard_map/ppermute | solution.py:338
  53.2 7.9 %collective-permute-start.18 = (bf16[32,1536]{1,0:T(8,128)(2,1)S(1)}, bf16[32,1536]{1,0:T(8,128)(2,1)S(1)}, u32[]{:S(2)}, u32[]{:S(2)}) collective-permute-start(bf16[32,1536]{1,0:T(8,128)(2,1)S(1)} %pad_maximum_fusion.3.refs_1_), channel_id=1, source_target_pairs={{0,8},{2,10},{4,12},{6,14},{8,0},{10,2},{12,4},{14,6},{1,9},{3,11}... | collective-permute-start | bytes 294920 | tf_op jit(solution)/shard_map/ppermute | solution.py:338
  55.9 5.4 %collective-permute-start.15 = (bf16[32,1536]{1,0:T(8,128)(2,1)S(1)}, bf16[32,1536]{1,0:T(8,128)(2,1)S(1)}, u32[]{:S(2)}, u32[]{:S(2)}) collective-permute-start(bf16[32,1536]{1,0:T(8,128)(2,1)S(1)} %pad_maximum_fusion.2.refs_0_), channel_id=1, source_target_pairs={{0,4},{2,6},{4,0},{6,2},{8,12},{10,14},{12,8},{14,10},{1,5},{3,7},... | collective-permute-start | bytes 294920 | tf_op jit(solution)/shard_map/ppermute | solution.py:338
  61.1 5.7 %collective-permute-start.19 = (bf16[64,1536]{1,0:T(8,128)(2,1)S(1)}, bf16[64,1536]{1,0:T(8,128)(2,1)S(1)}, u32[]{:S(2)}, u32[]{:S(2)}) collective-permute-start(bf16[64,1536]{1,0:T(8,128)(2,1)S(1)} %pad_maximum_fusion.1.refs_1_.refs_2_), channel_id=1, source_target_pairs={{0,4},{2,6},{4,0},{6,2},{8,12},{10,14},{12,8},{14,10},{1,5},{3,7},... | collective-permute-start | bytes 589832 | tf_op jit(solution)/shard_map/ppermute | solution.py:338
  61.3 5.7 %collective-permute-start.17 = (bf16[64,1536]{1,0:T(8,128)(2,1)S(1)}, bf16[64,1536]{1,0:T(8,128)(2,1)S(1)}, u32[]{:S(2)}, u32[]{:S(2)}) collective-permute-start(bf16[64,1536]{1,0:T(8,128)(2,1)S(1)} %maximum_add_fusion.refs_0_), channel_id=1, source_target_pairs={{0,2},{2,0},{4,6},{6,4},{8,10},{10,8},{12,14},{14,12},{1,3},{3,1},... | collective-permute-start | bytes 589832 | tf_op jit(solution)/shard_map/ppermute | solution.py:338
  70.4 1.5 %collective-permute-start.21 = (f32[64,768]{1,0:T(8,128)S(1)}, f32[64,768]{1,0:T(8,128)S(1)}, u32[]{:S(2)}, u32[]{:S(2)}) collective-permute-start(f32[64,768]{1,0:T(8,128)S(1)} %get-tuple-element.66), channel_id=1, source_target_pairs={{0,1},{1,0},{2,3},{3,2},{4,5},{5,4},{6,7},{7,6},{8,9},{9,8},{10,11... | collective-permute-start | bytes 589832 | tf_op jit(solution)/shard_map/ppermute | solution.py:335
  70.5 2.0 %collective-permute-start.20 = (f32[64,1536]{1,0:T(8,128)S(1)}, f32[64,1536]{1,0:T(8,128)S(1)}, u32[]{:S(2)}, u32[]{:S(2)}) collective-permute-start(f32[64,1536]{1,0:T(8,128)S(1)} %get-tuple-element.58.refs_10_), channel_id=1, source_target_pairs={{0,1},{1,0},{2,3},{3,2},{4,5},{5,4},{6,7},{7,6},{8,9},{9,8},{10,11... | collective-permute-start | bytes 1179656 | tf_op jit(solution)/shard_map/ppermute | solution.py:335

commit v11 on v10

--- a/solution.py
+++ b/solution.py
@@ -270,23 +270,24 @@
     )(scalars, *own_q, *other_q, keys, values)
 
 
-def output_kernel(orders, rows, columns, pieces, after, ids_ref, *refs):
-    count = 2 * len(orders)
-    block_refs, w_refs = refs[:count], refs[count : count + len(pieces)]
-    send_ref, keep_ref, xs_ref = refs[count + len(pieces) + after :]
+def output_kernel(layout, rows, pieces, ahead, ids_ref, *refs):
+    block_refs, refs = refs[: len(layout)], refs[len(layout) :]
+    w_refs, refs = refs[: len(pieces)], refs[len(pieces) :]
+    w_hbm, refs = refs[: bool(ahead)], refs[bool(ahead) :]
+    send_ref, keep_ref, next_refs, (xs_ref, sems) = refs[0], refs[1], refs[2:-2], refs[-2:]
+    copies = fetches(w_hbm, [(0, cut) for cut in ahead], next_refs, sems)
+    for copy in copies:
+        copy.start()
+    me, core = ids_ref[0], ids_ref[1]
     depth = block_refs[0].shape[1]
-    me, core = ids_ref[0], ids_ref[1]
-    n = len(orders[0])
-    half = n // 2
-    for group, (near_ref, far_ref) in enumerate(zip(block_refs[::2], block_refs[1::2])):
-        for p, j in enumerate(orders[group]):
+    half = xs_ref.shape[0] // rows // 2
+    for ref, (group, places) in zip(block_refs, layout):
+        for at, j in enumerate(places):
             block = jnp.bitwise_xor(me, j)
             place = block % half + jnp.where(block // half == core, half, 0)
-            source = near_ref if p < half else far_ref
-            at = (p % half) * rows
             xs_ref[
                 pl.ds(pl.multiple_of(place * rows, rows), rows), group * depth : (group + 1) * depth
-            ] = source[at : at + rows, :]
+            ] = ref[at * rows : (at + 1) * rows, :]
     cut = half * rows
     totals = {}
     for w_ref, ((first, tall), span) in zip(w_refs, pieces):
@@ -294,32 +295,40 @@
             xs_ref[:, first : first + tall], w_ref[...], preferred_element_type=jnp.float32
         )
         totals[span] = totals[span] + part if span in totals else part
+    base = min(column for column, _ in totals)
     for (column, width), total in totals.items():
-        send_ref[:, column - columns[0] : column - columns[0] + width] = total[:cut]
-        keep_ref[:, column - columns[0] : column - columns[0] + width] = total[cut:]
-
-
-def project_out(orders, rows, ids, blocks, held, cuts, columns, after):
-    chosen = [at for at, (_, (column, _)) in enumerate(cuts) if columns[0] <= column < sum(columns)]
-    weights, pieces = [held[at] for at in chosen], [cuts[at] for at in chosen]
-    pieces, weights = zip(*sorted(zip(pieces, weights), key=lambda pair: (pair[0][1], pair[0][0])))
-    depth = len(orders) * blocks[0].shape[1]
-    n = len(orders[0])
-    out = jax.ShapeDtypeStruct((n * rows // 2, columns[1]), jnp.float32)
+        send_ref[:, column - base : column - base + width] = total[:cut]
+        keep_ref[:, column - base : column - base + width] = total[cut:]
+    for copy in copies:
+        copy.wait()
+
+
+def project_out(rows, ids, blocks, held, cuts, out_weight, ahead):
+    chosen = sorted(range(len(cuts)), key=lambda at: (cuts[at][1], cuts[at][0]))
+    pieces, weights = [cuts[at] for at in chosen], [held[at] for at in chosen]
+    layout = [(group, tuple(places)) for group, arrays in enumerate(blocks) for _, places in arrays]
+    arrays = [array for group in blocks for array, _ in group]
+    depth = out_weight.shape[0]
+    columns = sum(dict.fromkeys(span for _, span in pieces), ())[1::2]
+    total_rows = rows * sum(len(places) for _, places in layout) // len(blocks)
+    out = jax.ShapeDtypeStruct((total_rows // 2, sum(columns)), jnp.float32)
     return pl.pallas_call(
-        functools.partial(output_kernel, orders, rows, columns, pieces, len(after)),
-        out_shape=(out, out),
-        in_specs=[SMEM] + [VMEM] * (len(blocks) + len(weights)) + [ANY] * len(after),
-        out_specs=(VMEM, VMEM),
-        scratch_shapes=[pltpu.VMEM((n * rows, depth), jnp.bfloat16)],
-        compiler_params=pltpu.CompilerParams(vmem_limit_bytes=12 * MIB),
+        functools.partial(output_kernel, layout, rows, pieces, ahead),
+        out_shape=[out, out] + [piece_of(out_weight, cut) for cut in ahead],
+        in_specs=[SMEM] + [VMEM] * (len(arrays) + len(weights)) + [HBM] * bool(ahead),
+        out_specs=[VMEM] * (2 + len(ahead)),
+        scratch_shapes=[
+            pltpu.VMEM((total_rows, depth), jnp.bfloat16),
+            pltpu.SemaphoreType.DMA((max(1, len(ahead)),)),
+        ],
+        compiler_params=pltpu.CompilerParams(vmem_limit_bytes=34 * MIB),
         cost_estimate=pl.CostEstimate(
-            flops=2 * n * rows * depth * columns[1],
-            bytes_accessed=2 * depth * columns[1] + 4 * n * rows * columns[1],
+            flops=2 * total_rows * depth * sum(columns),
+            bytes_accessed=2 * depth * sum(columns) + 4 * total_rows * sum(columns),
             transcendentals=0,
         ),
         name="project_out",
-    )(ids, *blocks, *weights, *after)
+    )(ids, *arrays, *weights, *([out_weight] if ahead else []))
 
 
 def local(tokens, query_weight, kv_weight, out_weight, key_cache, value_cache, lengths):
@@ -354,10 +363,15 @@
         after = [made[0][0]]
         first += sum(columns for columns, _ in chunks)
     moving = [across(send, order[0]) for (send, _), (_, order) in zip(state, plan)]
+    second = None
     for step in range(len(bits)):
         for i in (2, 0, 1):
             columns, order = plan[i]
             total = state[i][1] + moving[i]
+            if i == 0 and step == 2 and len(bits) == 3:
+                total = total + 0.0 * second[:1, : total.shape[1]]
+            if i == 1 and step == 1:
+                second = total
             if step + 1 < len(bits):
                 cut = total.shape[0] // 2
                 state[i] = (total[cut:], total[:cut])
@@ -378,33 +392,27 @@
     got = swap(other)
     block = jnp.where(core == 0, jnp.concatenate([own, got]), jnp.concatenate([got, own]))
 
-    near = [block[:, :width], block[:, width:]]
-    far = [None, None]
-    paths = [bits[::-1], bits[:1] + bits[:0:-1]]
-    out_cuts, out_held = cuts_of(out_weight), []
-    early = len(out_cuts) * 9 // 18
-    for step in range(len(bits)):
-        for i in range(2):
-            if step:
-                near[i] = jnp.concatenate([near[i], far[i]])
-                if i == 0 and out_held:
-                    near[i] = near[i] + zero.astype(jnp.bfloat16)
-                if i == 1 and step + 2 >= len(bits):
-                    part = out_cuts[early:] if out_held else out_cuts[:early]
-                    held, zero = load([out_weight], [(0, cut) for cut in part], near, 36, width)
-                    out_held += held
-            far[i] = across(near[i], paths[i][step])
-    orders = [order_of(path[::-1]) for path in paths]
-    blocks = [b for pair in zip(near, far) for b in pair]
+    def along_z(array):
+        return [array] + [across(array, 2 * m) for m in range(1, n // 2)]
+
+    first, second = block[:, :width], block[:, width:]
+    pair = jnp.concatenate([second, across(second, 1)])
+    near = jnp.concatenate(along_z(first)) + jnp.bfloat16(0) * pair[-1:]
+    blocks = [[(near, range(0, n, 2)), (across(near, 1), range(1, n, 2))]]
+    blocks.append([(array, (2 * m, 2 * m + 1)) for m, array in enumerate(along_z(pair))])
+
     total_columns = out_weight.shape[1]
     last = 768 if total_columns % 768 == 0 and total_columns > 768 else 0
-    results, after = [], []
-    for columns in ((0, total_columns - last), (total_columns - last, last)):
-        if columns[1]:
-            send, keep = project_out(orders, rows, ids, blocks, out_held, out_cuts, columns, after)
-            after = [send]
-            results.append((keep + swap(send)).astype(jnp.bfloat16))
-    return jnp.concatenate(results, axis=1)
+    out_cuts = cuts_of(out_weight)
+    early = [cut for cut in out_cuts if cut[1][0] < total_columns - last]
+    late = [cut for cut in out_cuts if cut[1][0] >= total_columns - last]
+    held, _ = load([out_weight], [(0, cut) for cut in early], [near], 40)
+    send, keep, *held = project_out(rows, ids, blocks, held, early, out_weight, late)
+    results = [(keep, swap(send))]
+    if late:
+        send, keep = project_out(rows, ids, blocks, held, late, out_weight, [])
+        results.append((keep, swap(send)))
+    return jnp.concatenate([(keep + got).astype(jnp.bfloat16) for keep, got in results], axis=1)
 
 
 def solution(mesh):

time: 73.4 us -> 76.3 us (1.040)
  starting transfers between devices: 20.4 us -> 25.6 us
  waiting for transfers between devices: 27 us -> 24.9 us
    ppermute x15 -> x17, starting transfers between devices: 19 us -> 24.2 us  [across(): return lax.ppermute(array, 'gx', [(g, g ^ mask) for g in range(n)])]
    pallas_call x2 -> x1, Pallas kernels: 6.84 us -> 4.35 us  [load(): pl.pallas_call(functools.partial(load_kernel, len(after), cuts, len(array...]
    pallas_call x2, Pallas kernels: 3.4 us -> 5.45 us  [project_out(): pl.pallas_call(functools.partial(output_kernel, layout, rows, pieces, ahe...]
    ppermute x15 -> x17, waiting for transfers between devices: 23 us -> 21 us  [across(): return lax.ppermute(array, 'gx', [(g, g ^ mask) for g in range(n)])]
  transfers between devices with their start and end apart: 22 -> 24, of which waited for: 13 -> 12; matrix products, arithmetic and copies ran while one was open for 2% -> 2% of each run, Pallas kernels for 17% -> 13%
where the time goes in v11:
time: 76.3 us; the launch traced here: 76.1 us
  starting transfers between devices  25.6 us (34%)
  waiting for transfers between devices  24.9 us (33%)
  Pallas kernels  22.8 us (30%)
  other arithmetic  2.25 us (3%)
    ppermute x17, starting transfers between devices, across(): return lax.ppermute(array, 'gx', [(g, g ^ mask) for g in range(n)])  24.2 us
    ppermute x17, waiting for transfers between devices, across(): return lax.ppermute(array, 'gx', [(g, g ^ mask) for g in range(n)])  21 us
    pallas_call x2, Pallas kernels, project(): pl.pallas_call(functools.partial(project_kernel, orders, rows, first, wid...  8.76 us
    pallas_call x2, Pallas kernels, project_out(): pl.pallas_call(functools.partial(output_kernel, layout, rows, pieces, ahe...  5.45 us
    pallas_call x1, Pallas kernels, load(): pl.pallas_call(functools.partial(load_kernel, len(after), cuts, len(array...  4.35 us
    pallas_call x1, Pallas kernels, attend(): pl.pallas_call(functools.partial(attend_kernel, parts), out_shape=(out, o...  4.3 us
    ppermute x7, waiting for transfers between devices, swap(): return lax.ppermute(array, 'gy', [(0, 1), (1, 0)])  3.97 us
  transfers between devices with their start and end apart: 24, of which 12 were waited for; matrix products, arithmetic and copies ran while one was open for 2% of the time, Pallas kernels for 13%

profile of v11, /device:TPU:0, one launch (start us, length us, event | category | flops | bytes accessed | tf_op | source)
XLA Modules:
  0.0 76.1 jit_solution(13665850585796613100)
XLA Ops:
  0.5 1.0 %broadcast_select_fusion.own_ref = bf16[64,2304]{1,0:T(8,128)(2,1)S(1)} fusion(bf16[64,2304]{1,0:T(8,128)(2,1)} %param.7, pred[]{:T(512)S(6)} %lt.6), kind=kLoop, calls=%fused_computation.2 | loop fusion | flops 147456 | bytes 589825 | tf_op jit(solution)/shard_map/jit(_where)/select_n | solution.py:350
  1.9 3.4 %project.2 = (f32[64,1024]{1,0:T(8,128)S(1)}, f32[64,1024]{1,0:T(8,128)S(1)}) custom-call(s32[2]{0:T(128)S(1)} %pad_add_fusion.ids_ref, bf16[64,2304]{1,0:T(8,128)(2,1)S(1)} %broadcast_select_fusion.own_ref, bf16[64,2304]{1,0:T(8,128)(2,1)S(1)} %collective-permute-done.other_ref, bf16[2304,3072]{1,0:T(8,128)(2,1)} %w_ref.3), custom_call_target="tpu_custom_call" | custom-call | flops 603979776 | bytes 5242880 | tf_op jit(solution)/shard_map/project/pallas_call | solution.py:176
  5.3 3.0 %collective-permute-start.1 = (f32[64,1024]{1,0:T(8,128)S(1)}, f32[64,1024]{1,0:T(8,128)S(1)}, u32[]{:S(2)}, u32[]{:S(2)}) collective-permute-start(f32[64,1024]{1,0:T(8,128)S(1)} %get-tuple-element.36.refs_1_), channel_id=1, source_target_pairs={{0,4},{2,6},{4,0},{6,2},{8,12},{10,14},{12,8},{14,10},{1,5},{3,7},... | collective-permute-start | bytes 786440 | tf_op jit(solution)/shard_map/ppermute | solution.py:347
  8.3 5.3 %project.3 = (f32[64,1024]{1,0:T(8,128)S(1)}, f32[64,1024]{1,0:T(8,128)S(1)}, f32[64,1280]{1,0:T(8,128)S(1)}, f32[64,1280]{1,0:T(8,128)S(1)}) custom-call(s32[2]{0:T(128)S(1)} %pad_add_fusion.ids_ref, bf16[64,2304]{1,0:T(8,128)(2,1)S(1)} %broadcast_select_fusion.own_ref, bf16[64,2304]{1,0:T(8,128)(2,1)S(1)} %collective-permute-done.other_ref, ...), custom_call_target="tpu_custom_call" | custom-call | flops 1358954496 | bytes 11796480 | tf_op jit(solution)/shard_map/project/pallas_call | solution.py:176
  13.7 1.6 %collective-permute-start.7 = (f32[64,1280]{1,0:T(8,128)S(1)}, f32[64,1280]{1,0:T(8,128)S(1)}, u32[]{:S(2)}, u32[]{:S(2)}) collective-permute-start(f32[64,1280]{1,0:T(8,128)S(1)} %get-tuple-element.40), channel_id=1, source_target_pairs={{0,2},{2,0},{4,6},{6,4},{8,10},{10,8},{12,14},{14,12},{1,3},{3,1},... | collective-permute-start | bytes 983048 | tf_op jit(solution)/shard_map/ppermute | solution.py:347
  15.8 2.6 %collective-permute-start.2 = (f32[32,1024]{1,0:T(8,128)S(1)}, f32[32,1024]{1,0:T(8,128)S(1)}, u32[]{:S(2)}, u32[]{:S(2)}) collective-permute-start(f32[32,1024]{1,0:T(8,128)S(1)} %slice.65), channel_id=1, source_target_pairs={{0,8},{2,10},{4,12},{6,14},{8,0},{10,2},{12,4},{14,6},{1,9},{3,11}... | collective-permute-start | bytes 393224 | tf_op jit(solution)/shard_map/ppermute | solution.py:347
  18.4 7.4 %collective-permute-done.4 = f32[64,1024]{1,0:T(8,128)S(1)} collective-permute-done((f32[64,1024]{1,0:T(8,128)S(1)}, f32[64,1024]{1,0:T(8,128)S(1)}, u32[]{:S(2)}, u32[]{:S(2)}) %collective-permute-start.4) | collective-permute-done | bytes 262176 | tf_op jit(solution)/shard_map/ppermute | solution.py:347
  25.9 0.6 collective-permute-start.5
  26.7 1.6 %collective-permute-start.3 = (f32[16,1024]{1,0:T(8,128)S(1)}, f32[16,1024]{1,0:T(8,128)S(1)}, u32[]{:S(2)}, u32[]{:S(2)}) collective-permute-start(f32[16,1024]{1,0:T(8,128)S(1)} %slice.67), channel_id=1, source_target_pairs={{0,2},{2,0},{4,6},{6,4},{8,10},{10,8},{12,14},{14,12},{1,3},{3,1},... | collective-permute-start | bytes 196616 | tf_op jit(solution)/shard_map/ppermute | solution.py:347
  28.3 2.7 %collective-permute-done.5 = f32[32,1024]{1,0:T(8,128)S(1)} collective-permute-done((f32[32,1024]{1,0:T(8,128)S(1)}, f32[32,1024]{1,0:T(8,128)S(1)}, u32[]{:S(2)}, u32[]{:S(2)}) %collective-permute-start.5) | collective-permute-done | bytes 131104 | tf_op jit(solution)/shard_map/ppermute | solution.py:347
  31.0 1.5 %collective-permute-start.6 = (f32[16,1024]{1,0:T(8,128)S(1)}, f32[16,1024]{1,0:T(8,128)S(1)}, u32[]{:S(2)}, u32[]{:S(2)}) collective-permute-start(f32[16,1024]{1,0:T(8,128)S(1)} %slice.71), channel_id=1, source_target_pairs={{0,8},{2,10},{4,12},{6,14},{8,0},{10,2},{12,4},{14,6},{1,9},{3,11}... | collective-permute-start | bytes 196616 | tf_op jit(solution)/shard_map/ppermute | solution.py:347
  32.6 1.6 %collective-permute-start.9 = (f32[16,1280]{1,0:T(8,128)S(1)}, f32[16,1280]{1,0:T(8,128)S(1)}, u32[]{:S(2)}, u32[]{:S(2)}) collective-permute-start(f32[16,1280]{1,0:T(8,128)S(1)} %slice.76), channel_id=1, source_target_pairs={{0,8},{2,10},{4,12},{6,14},{8,0},{10,2},{12,4},{14,6},{1,9},{3,11}... | collective-permute-start | bytes 245768 | tf_op jit(solution)/shard_map/ppermute | solution.py:347
  34.2 2.4 %collective-permute-done.6 = f32[16,1024]{1,0:T(8,128)S(1)} collective-permute-done((f32[16,1024]{1,0:T(8,128)S(1)}, f32[16,1024]{1,0:T(8,128)S(1)}, u32[]{:S(2)}, u32[]{:S(2)}) %collective-permute-start.6) | collective-permute-done | bytes 65568 | tf_op jit(solution)/shard_map/ppermute | solution.py:347
  36.7 3.5 %collective-permute-done.9 = f32[16,1280]{1,0:T(8,128)S(1)} collective-permute-done((f32[16,1280]{1,0:T(8,128)S(1)}, f32[16,1280]{1,0:T(8,128)S(1)}, u32[]{:S(2)}, u32[]{:S(2)}) %collective-permute-start.9) | collective-permute-done | bytes 81952 | tf_op jit(solution)/shard_map/ppermute | solution.py:347
  40.4 1.1 %collective-permute-done.12.refs_5_ = bf16[8,1280]{1,0:T(8,128)(2,1)S(1)} collective-permute-done((bf16[8,1280]{1,0:T(8,128)(2,1)S(1)}, bf16[8,1280]{1,0:T(8,128)(2,1)S(1)}, u32[]{:S(2)}, u32[]{:S(2)}) %collective-permute-start.12) | collective-permute-done | bytes 20512 | tf_op jit(solution)/shard_map/ppermute | solution.py:344
  41.5 4.3 %attend.1 = (bf16[8,3072]{1,0:T(8,128)(2,1)S(1)}, bf16[8,3072]{1,0:T(8,128)(2,1)S(1)}) custom-call(s32[9]{0:T(128)S(1)} %pad_add_fusion.1.scalars_ref, bf16[8,1024]{1,0:T(8,128)(2,1)S(1)} %get-tuple-element.72.refs_0_, bf16[8,1024]{1,0:T(8,128)(2,1)S(1)} %get-tuple-element.70.refs_1_, bf16[8,1280]{1,0:T(8,128)(2,1)S(1)} %get-tuple-element.68.refs_2_, ...), custom_call_target="tpu_custom_call" | custom-call | flops 201326592 | bytes 8388608 | tf_op jit(solution)/shard_map/attend/pallas_call | solution.py:255
  46.0 1.1 %collective-permute-done.13 = bf16[8,3072]{1,0:T(8,128)(2,1)S(1)} collective-permute-done((bf16[8,3072]{1,0:T(8,128)(2,1)S(1)}, bf16[8,3072]{1,0:T(8,128)(2,1)S(1)}, u32[]{:S(2)}, u32[]{:S(2)}) %collective-permute-start.13) | collective-permute-done | bytes 49184 | tf_op jit(solution)/shard_map/ppermute | solution.py:344
  47.1 1.0 %collective-permute-start.17 = (bf16[16,1536]{1,0:T(8,128)(2,1)S(1)}, bf16[16,1536]{1,0:T(8,128)(2,1)S(1)}, u32[]{:S(2)}, u32[]{:S(2)}) collective-permute-start(bf16[16,1536]{1,0:T(8,128)(2,1)S(1)} %get-tuple-element.65), channel_id=1, source_target_pairs={{0,2},{2,0},{4,6},{6,4},{8,10},{10,8},{12,14},{14,12},{1,3},{3,1},... | collective-permute-start | bytes 147464 | tf_op jit(solution)/shard_map/ppermute | solution.py:347
  48.2 2.1 %collective-permute-start.16 = (bf16[16,1536]{1,0:T(8,128)(2,1)S(1)}, bf16[16,1536]{1,0:T(8,128)(2,1)S(1)}, u32[]{:S(2)}, u32[]{:S(2)}) collective-permute-start(bf16[16,1536]{1,0:T(8,128)(2,1)S(1)} %get-tuple-element.66), channel_id=1, source_target_pairs={{0,12},{2,14},{4,8},{6,10},{8,4},{10,6},{12,0},{14,2},{1,13},{3,15... | collective-permute-start | bytes 147464 | tf_op jit(solution)/shard_map/ppermute | solution.py:347
  50.3 2.3 %collective-permute-start.14 = (bf16[16,1536]{1,0:T(8,128)(2,1)S(1)}, bf16[16,1536]{1,0:T(8,128)(2,1)S(1)}, u32[]{:S(2)}, u32[]{:S(2)}) collective-permute-start(bf16[16,1536]{1,0:T(8,128)(2,1)S(1)} %get-tuple-element.66), channel_id=1, source_target_pairs={{0,4},{2,6},{4,0},{6,2},{8,12},{10,14},{12,8},{14,10},{1,5},{3,7},... | collective-permute-start | bytes 147464 | tf_op jit(solution)/shard_map/ppermute | solution.py:347
  52.6 1.5 %collective-permute-done.16 = bf16[16,1536]{1,0:T(8,128)(2,1)S(1)} collective-permute-done((bf16[16,1536]{1,0:T(8,128)(2,1)S(1)}, bf16[16,1536]{1,0:T(8,128)(2,1)S(1)}, u32[]{:S(2)}, u32[]{:S(2)}) %collective-permute-start.16) | collective-permute-done | bytes 49184 | tf_op jit(solution)/shard_map/ppermute | solution.py:347
  54.1 1.5 %collective-permute-done.15 = bf16[16,1536]{1,0:T(8,128)(2,1)S(1)} collective-permute-done((bf16[16,1536]{1,0:T(8,128)(2,1)S(1)}, bf16[16,1536]{1,0:T(8,128)(2,1)S(1)}, u32[]{:S(2)}, u32[]{:S(2)}) %collective-permute-start.15) | collective-permute-done | bytes 49184 | tf_op jit(solution)/shard_map/ppermute | solution.py:347
  55.7 1.3 %collective-permute-start.18 = (bf16[64,1536]{1,0:T(8,128)(2,1)S(1)}, bf16[64,1536]{1,0:T(8,128)(2,1)S(1)}, u32[]{:S(2)}, u32[]{:S(2)}) collective-permute-start(bf16[64,1536]{1,0:T(8,128)(2,1)S(1)} %maximum_add_fusion.refs_0_), channel_id=1, source_target_pairs={{0,2},{2,0},{4,6},{6,4},{8,10},{10,8},{12,14},{14,12},{1,3},{3,1},... | collective-permute-start | bytes 589832 | tf_op jit(solution)/shard_map/ppermute | solution.py:347
  57.0 2.4 %collective-permute-start.21 = (bf16[32,1536]{1,0:T(8,128)(2,1)S(1)}, bf16[32,1536]{1,0:T(8,128)(2,1)S(1)}, u32[]{:S(2)}, u32[]{:S(2)}) collective-permute-start(bf16[32,1536]{1,0:T(8,128)(2,1)S(1)} %pad_maximum_fusion.1.refs_2_), channel_id=1, source_target_pairs={{0,12},{2,14},{4,8},{6,10},{8,4},{10,6},{12,0},{14,2},{1,13},{3,15... | collective-permute-start | bytes 294920 | tf_op jit(solution)/shard_map/ppermute | solution.py:347
  59.4 2.0 %collective-permute-start.19 = (bf16[32,1536]{1,0:T(8,128)(2,1)S(1)}, bf16[32,1536]{1,0:T(8,128)(2,1)S(1)}, u32[]{:S(2)}, u32[]{:S(2)}) collective-permute-start(bf16[32,1536]{1,0:T(8,128)(2,1)S(1)} %pad_maximum_fusion.1.refs_2_), channel_id=1, source_target_pairs={{0,4},{2,6},{4,0},{6,2},{8,12},{10,14},{12,8},{14,10},{1,5},{3,7},... | collective-permute-start | bytes 294920 | tf_op jit(solution)/shard_map/ppermute | solution.py:347
  61.4 4.3 %load.1 = (bf16[512,768]{1,0:T(8,128)(2,1)S(1)}, bf16[512,768]{1,0:T(8,128)(2,1)S(1)}, bf16[512,768]{1,0:T(8,128)(2,1)S(1)}, bf16[512,768]{1,0:T(8,128)(2,1)S(1)...) custom-call(bf16[64,1536]{1,0:T(8,128)(2,1)S(1)} %maximum_add_fusion, ...), custom_call_target="tpu_custom_call" | custom-call | bytes 18874368 | tf_op jit(solution)/shard_map/load/pallas_call | solution.py:78
  65.8 2.0 %collective-permute-done.20.refs_4_ = bf16[32,1536]{1,0:T(8,128)(2,1)S(1)} collective-permute-done((bf16[32,1536]{1,0:T(8,128)(2,1)S(1)}, bf16[32,1536]{1,0:T(8,128)(2,1)S(1)}, u32[]{:S(2)}, u32[]{:S(2)}) %collective-permute-start.20) | collective-permute-done | bytes 98336 | tf_op jit(solution)/shard_map/ppermute | solution.py:347
  67.8 4.0 %project_out.2 = (f32[64,1536]{1,0:T(8,128)S(1)}, f32[64,1536]{1,0:T(8,128)S(1)}, bf16[512,768]{1,0:T(8,128)(2,1)S(1)}, bf16[512,768]{1,0:T(8,128)(2,1)S(1)}, bf...) custom-call(s32[2]{0:T(128)S(1)} %pad_add_fusion.ids_ref, ...), custom_call_target="tpu_custom_call" | custom-call | flops 1207959552 | bytes 10223616 | tf_op jit(solution)/shard_map/project_out/pallas_call | solution.py:315
  71.8 1.4 %project_out.3 = (f32[64,768]{1,0:T(8,128)S(1)}, f32[64,768]{1,0:T(8,128)S(1)}) custom-call(s32[2]{0:T(128)S(1)} %pad_add_fusion.ids_ref, bf16[64,1536]{1,0:T(8,128)(2,1)S(1)} %maximum_add_fusion.refs_0_, bf16[64,1536]{1,0:T(8,128)(2,1)S(1)} %collective-permute-done.18.refs_1_, bf16[32,1536]{1,0:T(8,128)(2,1)S(1)} %pad_maximum_fusion.1.refs_2_, ...), custom_call_target="tpu_custom_call" | custom-call | flops 603979776 | bytes 5111808 | tf_op jit(solution)/shard_map/project_out/pallas_call | solution.py:315
  73.8 0.9 %collective-permute-done.23 = f32[64,768]{1,0:T(8,128)S(1)} collective-permute-done((f32[64,768]{1,0:T(8,128)S(1)}, f32[64,768]{1,0:T(8,128)S(1)}, u32[]{:S(2)}, u32[]{:S(2)}) %collective-permute-start.23) | collective-permute-done | bytes 196640 | tf_op jit(solution)/shard_map/ppermute | solution.py:344
  74.8 0.5 collective-permute-done.22
  75.3 0.7 pad_maximum_fusion
  (58 shorter events, 3.0 us)
Async XLA Ops:
  0.0 1.9 %collective-permute-start = (bf16[64,2304]{1,0:T(8,128)(2,1)}, bf16[64,2304]{1,0:T(8,128)(2,1)S(1)}, u32[]{:S(2)}, u32[]{:S(2)}) collective-permute-start(bf16[64,2304]{1,0:T(8,128)(2,1)} %param.7), channel_id=1, source_target_pairs={{0,1},{1,0},{2,3},{3,2},{4,5},{5,4},{6,7},{7,6},{8,9},{9,8},{10,11... | collective-permute-start | bytes 884744 | tf_op jit(solution)/shard_map/ppermute | solution.py:344
  1.5 6.8 %copy-start.1 = (bf16[2304,512]{1,0:T(8,128)(2,1)S(1)}, bf16[2304,512]{1,0:T(8,128)(2,1)}, u32[]{:S(2)}) copy-start(bf16[2304,512]{1,0:T(8,128)(2,1)} %refs_0_.1) | copy-start | bytes 7077892
  5.3 10.4 %collective-permute-start.1 = (f32[64,1024]{1,0:T(8,128)S(1)}, f32[64,1024]{1,0:T(8,128)S(1)}, u32[]{:S(2)}, u32[]{:S(2)}) collective-permute-start(f32[64,1024]{1,0:T(8,128)S(1)} %get-tuple-element.36.refs_1_), channel_id=1, source_target_pairs={{0,4},{2,6},{4,0},{6,2},{8,12},{10,14},{12,8},{14,10},{1,5},{3,7},... | collective-permute-start | bytes 786440 | tf_op jit(solution)/shard_map/ppermute | solution.py:347
  13.7 26.7 %copy-start.2 = (s32[8]{0:T(128)S(1)}, s32[8]{0:T(128)}, u32[]{:S(2)}) copy-start(s32[8]{0:T(128)} %param.13) | copy-start | bytes 100
  13.7 12.8 %collective-permute-start.7 = (f32[64,1280]{1,0:T(8,128)S(1)}, f32[64,1280]{1,0:T(8,128)S(1)}, u32[]{:S(2)}, u32[]{:S(2)}) collective-permute-start(f32[64,1280]{1,0:T(8,128)S(1)} %get-tuple-element.40), channel_id=1, source_target_pairs={{0,2},{2,0},{4,6},{6,4},{8,10},{10,8},{12,14},{14,12},{1,3},{3,1},... | collective-permute-start | bytes 983048 | tf_op jit(solution)/shard_map/ppermute | solution.py:347
  15.3 10.6 %collective-permute-start.4 = (f32[64,1024]{1,0:T(8,128)S(1)}, f32[64,1024]{1,0:T(8,128)S(1)}, u32[]{:S(2)}, u32[]{:S(2)}) collective-permute-start(f32[64,1024]{1,0:T(8,128)S(1)} %get-tuple-element.38), channel_id=1, source_target_pairs={{0,4},{2,6},{4,0},{6,2},{8,12},{10,14},{12,8},{14,10},{1,5},{3,7},... | collective-permute-start | bytes 786440 | tf_op jit(solution)/shard_map/ppermute | solution.py:347
  15.8 10.9 %collective-permute-start.2 = (f32[32,1024]{1,0:T(8,128)S(1)}, f32[32,1024]{1,0:T(8,128)S(1)}, u32[]{:S(2)}, u32[]{:S(2)}) collective-permute-start(f32[32,1024]{1,0:T(8,128)S(1)} %slice.65), channel_id=1, source_target_pairs={{0,8},{2,10},{4,12},{6,14},{8,0},{10,2},{12,4},{14,6},{1,9},{3,11}... | collective-permute-start | bytes 393224 | tf_op jit(solution)/shard_map/ppermute | solution.py:347
  18.4 23.1 %copy-start = (bf16[8,1024,256]{2,1,0:T(8,128)(2,1)S(1)}, bf16[8,1024,256]{2,1,0:T(8,128)(2,1)}, u32[]{:S(2)}) copy-start(bf16[8,1024,256]{2,1,0:T(8,128)(2,1)} %refs_6_.1) | copy-start | bytes 12582916
  25.9 5.0 %collective-permute-start.5 = (f32[32,1024]{1,0:T(8,128)S(1)}, f32[32,1024]{1,0:T(8,128)S(1)}, u32[]{:S(2)}, u32[]{:S(2)}) collective-permute-start(f32[32,1024]{1,0:T(8,128)S(1)} %slice.69), channel_id=1, source_target_pairs={{0,2},{2,0},{4,6},{6,4},{8,10},{10,8},{12,14},{14,12},{1,3},{3,1},... | collective-permute-start | bytes 393224 | tf_op jit(solution)/shard_map/ppermute | solution.py:347
  26.6 6.0 %collective-permute-start.8 = (f32[32,1280]{1,0:T(8,128)S(1)}, f32[32,1280]{1,0:T(8,128)S(1)}, u32[]{:S(2)}, u32[]{:S(2)}) collective-permute-start(f32[32,1280]{1,0:T(8,128)S(1)} %slice.73), channel_id=1, source_target_pairs={{0,4},{2,6},{4,0},{6,2},{8,12},{10,14},{12,8},{14,10},{1,5},{3,7},... | collective-permute-start | bytes 491528 | tf_op jit(solution)/shard_map/ppermute | solution.py:347
  26.7 5.8 %collective-permute-start.3 = (f32[16,1024]{1,0:T(8,128)S(1)}, f32[16,1024]{1,0:T(8,128)S(1)}, u32[]{:S(2)}, u32[]{:S(2)}) collective-permute-start(f32[16,1024]{1,0:T(8,128)S(1)} %slice.67), channel_id=1, source_target_pairs={{0,2},{2,0},{4,6},{6,4},{8,10},{10,8},{12,14},{14,12},{1,3},{3,1},... | collective-permute-start | bytes 196616 | tf_op jit(solution)/shard_map/ppermute | solution.py:347
  31.0 5.6 %collective-permute-start.6 = (f32[16,1024]{1,0:T(8,128)S(1)}, f32[16,1024]{1,0:T(8,128)S(1)}, u32[]{:S(2)}, u32[]{:S(2)}) collective-permute-start(f32[16,1024]{1,0:T(8,128)S(1)} %slice.71), channel_id=1, source_target_pairs={{0,8},{2,10},{4,12},{6,14},{8,0},{10,2},{12,4},{14,6},{1,9},{3,11}... | collective-permute-start | bytes 196616 | tf_op jit(solution)/shard_map/ppermute | solution.py:347
  32.5 7.9 %collective-permute-start.10 = (bf16[8,1024]{1,0:T(8,128)(2,1)S(1)}, bf16[8,1024]{1,0:T(8,128)(2,1)S(1)}, u32[]{:S(2)}, u32[]{:S(2)}) collective-permute-start(bf16[8,1024]{1,0:T(8,128)(2,1)S(1)} %get-tuple-element.71), channel_id=1, source_target_pairs={{0,1},{1,0},{2,3},{3,2},{4,5},{5,4},{6,7},{7,6},{8,9},{9,8},{10,11... | collective-permute-start | bytes 49160 | tf_op jit(solution)/shard_map/ppermute | solution.py:344
  32.6 7.6 %collective-permute-start.9 = (f32[16,1280]{1,0:T(8,128)S(1)}, f32[16,1280]{1,0:T(8,128)S(1)}, u32[]{:S(2)}, u32[]{:S(2)}) collective-permute-start(f32[16,1280]{1,0:T(8,128)S(1)} %slice.76), channel_id=1, source_target_pairs={{0,8},{2,10},{4,12},{6,14},{8,0},{10,2},{12,4},{14,6},{1,9},{3,11}... | collective-permute-start | bytes 245768 | tf_op jit(solution)/shard_map/ppermute | solution.py:347
  36.6 3.8 %collective-permute-start.11 = (bf16[8,1024]{1,0:T(8,128)(2,1)S(1)}, bf16[8,1024]{1,0:T(8,128)(2,1)S(1)}, u32[]{:S(2)}, u32[]{:S(2)}) collective-permute-start(bf16[8,1024]{1,0:T(8,128)(2,1)S(1)} %get-tuple-element.69), channel_id=1, source_target_pairs={{0,1},{1,0},{2,3},{3,2},{4,5},{5,4},{6,7},{7,6},{8,9},{9,8},{10,11... | collective-permute-start | bytes 49160 | tf_op jit(solution)/shard_map/ppermute | solution.py:344
  40.2 1.3 %collective-permute-start.12 = (bf16[8,1280]{1,0:T(8,128)(2,1)S(1)}, bf16[8,1280]{1,0:T(8,128)(2,1)S(1)}, u32[]{:S(2)}, u32[]{:S(2)}) collective-permute-start(bf16[8,1280]{1,0:T(8,128)(2,1)S(1)} %get-tuple-element.67), channel_id=1, source_target_pairs={{0,1},{1,0},{2,3},{3,2},{4,5},{5,4},{6,7},{7,6},{8,9},{9,8},{10,11... | collective-permute-start | bytes 61448 | tf_op jit(solution)/shard_map/ppermute | solution.py:344
  45.8 1.3 %collective-permute-start.13 = (bf16[8,3072]{1,0:T(8,128)(2,1)S(1)}, bf16[8,3072]{1,0:T(8,128)(2,1)S(1)}, u32[]{:S(2)}, u32[]{:S(2)}) collective-permute-start(bf16[8,3072]{1,0:T(8,128)(2,1)S(1)} %get-tuple-element.42), channel_id=1, source_target_pairs={{0,1},{1,0},{2,3},{3,2},{4,5},{5,4},{6,7},{7,6},{8,9},{9,8},{10,11... | collective-permute-start | bytes 147464 | tf_op jit(solution)/shard_map/ppermute | solution.py:344
  47.1 5.4 %collective-permute-start.17 = (bf16[16,1536]{1,0:T(8,128)(2,1)S(1)}, bf16[16,1536]{1,0:T(8,128)(2,1)S(1)}, u32[]{:S(2)}, u32[]{:S(2)}) collective-permute-start(bf16[16,1536]{1,0:T(8,128)(2,1)S(1)} %get-tuple-element.65), channel_id=1, source_target_pairs={{0,2},{2,0},{4,6},{6,4},{8,10},{10,8},{12,14},{14,12},{1,3},{3,1},... | collective-permute-start | bytes 147464 | tf_op jit(solution)/shard_map/ppermute | solution.py:347
  48.2 5.9 %collective-permute-start.16 = (bf16[16,1536]{1,0:T(8,128)(2,1)S(1)}, bf16[16,1536]{1,0:T(8,128)(2,1)S(1)}, u32[]{:S(2)}, u32[]{:S(2)}) collective-permute-start(bf16[16,1536]{1,0:T(8,128)(2,1)S(1)} %get-tuple-element.66), channel_id=1, source_target_pairs={{0,12},{2,14},{4,8},{6,10},{8,4},{10,6},{12,0},{14,2},{1,13},{3,15... | collective-permute-start | bytes 147464 | tf_op jit(solution)/shard_map/ppermute | solution.py:347
  50.3 5.3 %collective-permute-start.15 = (bf16[16,1536]{1,0:T(8,128)(2,1)S(1)}, bf16[16,1536]{1,0:T(8,128)(2,1)S(1)}, u32[]{:S(2)}, u32[]{:S(2)}) collective-permute-start(bf16[16,1536]{1,0:T(8,128)(2,1)S(1)} %get-tuple-element.66), channel_id=1, source_target_pairs={{0,8},{2,10},{4,12},{6,14},{8,0},{10,2},{12,4},{14,6},{1,9},{3,11}... | collective-permute-start | bytes 147464 | tf_op jit(solution)/shard_map/ppermute | solution.py:347
  50.3 5.3 %collective-permute-start.14 = (bf16[16,1536]{1,0:T(8,128)(2,1)S(1)}, bf16[16,1536]{1,0:T(8,128)(2,1)S(1)}, u32[]{:S(2)}, u32[]{:S(2)}) collective-permute-start(bf16[16,1536]{1,0:T(8,128)(2,1)S(1)} %get-tuple-element.66), channel_id=1, source_target_pairs={{0,4},{2,6},{4,0},{6,2},{8,12},{10,14},{12,8},{14,10},{1,5},{3,7},... | collective-permute-start | bytes 147464 | tf_op jit(solution)/shard_map/ppermute | solution.py:347
  55.7 12.1 %collective-permute-start.18 = (bf16[64,1536]{1,0:T(8,128)(2,1)S(1)}, bf16[64,1536]{1,0:T(8,128)(2,1)S(1)}, u32[]{:S(2)}, u32[]{:S(2)}) collective-permute-start(bf16[64,1536]{1,0:T(8,128)(2,1)S(1)} %maximum_add_fusion.refs_0_), channel_id=1, source_target_pairs={{0,2},{2,0},{4,6},{6,4},{8,10},{10,8},{12,14},{14,12},{1,3},{3,1},... | collective-permute-start | bytes 589832 | tf_op jit(solution)/shard_map/ppermute | solution.py:347
  57.0 8.8 %collective-permute-start.21 = (bf16[32,1536]{1,0:T(8,128)(2,1)S(1)}, bf16[32,1536]{1,0:T(8,128)(2,1)S(1)}, u32[]{:S(2)}, u32[]{:S(2)}) collective-permute-start(bf16[32,1536]{1,0:T(8,128)(2,1)S(1)} %pad_maximum_fusion.1.refs_2_), channel_id=1, source_target_pairs={{0,12},{2,14},{4,8},{6,10},{8,4},{10,6},{12,0},{14,2},{1,13},{3,15... | collective-permute-start | bytes 294920 | tf_op jit(solution)/shard_map/ppermute | solution.py:347
  59.4 8.4 %collective-permute-start.20 = (bf16[32,1536]{1,0:T(8,128)(2,1)S(1)}, bf16[32,1536]{1,0:T(8,128)(2,1)S(1)}, u32[]{:S(2)}, u32[]{:S(2)}) collective-permute-start(bf16[32,1536]{1,0:T(8,128)(2,1)S(1)} %pad_maximum_fusion.1.refs_2_), channel_id=1, source_target_pairs={{0,8},{2,10},{4,12},{6,14},{8,0},{10,2},{12,4},{14,6},{1,9},{3,11}... | collective-permute-start | bytes 294920 | tf_op jit(solution)/shard_map/ppermute | solution.py:347
  59.4 8.4 %collective-permute-start.19 = (bf16[32,1536]{1,0:T(8,128)(2,1)S(1)}, bf16[32,1536]{1,0:T(8,128)(2,1)S(1)}, u32[]{:S(2)}, u32[]{:S(2)}) collective-permute-start(bf16[32,1536]{1,0:T(8,128)(2,1)S(1)} %pad_maximum_fusion.1.refs_2_), channel_id=1, source_target_pairs={{0,4},{2,6},{4,0},{6,2},{8,12},{10,14},{12,8},{14,10},{1,5},{3,7},... | collective-permute-start | bytes 294920 | tf_op jit(solution)/shard_map/ppermute | solution.py:347
  73.2 1.5 %collective-permute-start.23 = (f32[64,768]{1,0:T(8,128)S(1)}, f32[64,768]{1,0:T(8,128)S(1)}, u32[]{:S(2)}, u32[]{:S(2)}) collective-permute-start(f32[64,768]{1,0:T(8,128)S(1)} %get-tuple-element.64), channel_id=1, source_target_pairs={{0,1},{1,0},{2,3},{3,2},{4,5},{5,4},{6,7},{7,6},{8,9},{9,8},{10,11... | collective-permute-start | bytes 589832 | tf_op jit(solution)/shard_map/ppermute | solution.py:344
  73.3 2.0 %collective-permute-start.22 = (f32[64,1536]{1,0:T(8,128)S(1)}, f32[64,1536]{1,0:T(8,128)S(1)}, u32[]{:S(2)}, u32[]{:S(2)}) collective-permute-start(f32[64,1536]{1,0:T(8,128)S(1)} %get-tuple-element.56), channel_id=1, source_target_pairs={{0,1},{1,0},{2,3},{3,2},{4,5},{5,4},{6,7},{7,6},{8,9},{9,8},{10,11... | collective-permute-start | bytes 1179656 | tf_op jit(solution)/shard_map/ppermute | solution.py:344

commit v12 on v10

--- a/solution.py
+++ b/solution.py
@@ -354,10 +354,15 @@
         after = [made[0][0]]
         first += sum(columns for columns, _ in chunks)
     moving = [across(send, order[0]) for (send, _), (_, order) in zip(state, plan)]
+    second = None
     for step in range(len(bits)):
         for i in (2, 0, 1):
             columns, order = plan[i]
             total = state[i][1] + moving[i]
+            if i == 0 and step == 2 and len(bits) == 3:
+                total = total + 0.0 * second[:1, : total.shape[1]]
+            if i == 1 and step == 1:
+                second = total
             if step + 1 < len(bits):
                 cut = total.shape[0] // 2
                 state[i] = (total[cut:], total[:cut])

time: 73.4 us -> 71.7 us (0.977)
  starting transfers between devices: 20.4 us -> 19.5 us
  waiting for transfers between devices: 27 us -> 26.1 us
    ppermute x15, starting transfers between devices: 19 us -> 18 us  [across(): return lax.ppermute(array, 'gx', [(g, g ^ mask) for g in range(n)])]
    ppermute x15, waiting for transfers between devices: 23 us -> 22.1 us  [across(): return lax.ppermute(array, 'gx', [(g, g ^ mask) for g in range(n)])]
  transfers between devices with their start and end apart: 22 -> 22, of which waited for: 13 -> 14; matrix products, arithmetic and copies ran while one was open for 2% -> 2% of each run, Pallas kernels for 17% -> 17%
where the time goes in v12:
time: 71.7 us; the launch traced here: 71.6 us
  waiting for transfers between devices  26.1 us (36%)
  Pallas kernels  23.3 us (32%)
  starting transfers between devices  19.5 us (27%)
  other arithmetic  2.27 us (3%)
    ppermute x15, waiting for transfers between devices, across(): return lax.ppermute(array, 'gx', [(g, g ^ mask) for g in range(n)])  22.1 us
    ppermute x15, starting transfers between devices, across(): return lax.ppermute(array, 'gx', [(g, g ^ mask) for g in range(n)])  18 us
    pallas_call x2, Pallas kernels, project(): pl.pallas_call(functools.partial(project_kernel, orders, rows, first, wid...  8.76 us
    pallas_call x2, Pallas kernels, load(): pl.pallas_call(functools.partial(load_kernel, len(after), cuts, len(array...  6.84 us
    pallas_call x1, Pallas kernels, attend(): pl.pallas_call(functools.partial(attend_kernel, parts), out_shape=(out, o...  4.3 us
    ppermute x7, waiting for transfers between devices, swap(): return lax.ppermute(array, 'gy', [(0, 1), (1, 0)])  3.97 us
    pallas_call x2, Pallas kernels, project_out(): pl.pallas_call(functools.partial(output_kernel, orders, rows, columns, pi...  3.39 us
    ppermute x7, starting transfers between devices, swap(): return lax.ppermute(array, 'gy', [(0, 1), (1, 0)])  1.46 us
  transfers between devices with their start and end apart: 22, of which 14 were waited for; matrix products, arithmetic and copies ran while one was open for 2% of the time, Pallas kernels for 17%

profile of v12, /device:TPU:0, one launch (start us, length us, event | category | flops | bytes accessed | tf_op | source)
XLA Modules:
  0.0 71.6 jit_solution(9869010003372979009)
XLA Ops:
  0.5 1.0 %broadcast_select_fusion.own_ref = bf16[64,2304]{1,0:T(8,128)(2,1)S(1)} fusion(bf16[64,2304]{1,0:T(8,128)(2,1)} %param.7, pred[]{:T(512)S(6)} %lt.6), kind=kLoop, calls=%fused_computation.2 | loop fusion | flops 147456 | bytes 589825 | tf_op jit(solution)/shard_map/jit(_where)/select_n | solution.py:341
  1.9 3.4 %project.2 = (f32[64,1024]{1,0:T(8,128)S(1)}, f32[64,1024]{1,0:T(8,128)S(1)}) custom-call(s32[2]{0:T(128)S(1)} %pad_add_fusion.ids_ref, bf16[64,2304]{1,0:T(8,128)(2,1)S(1)} %broadcast_select_fusion.own_ref, bf16[64,2304]{1,0:T(8,128)(2,1)S(1)} %collective-permute-done.other_ref, bf16[2304,3072]{1,0:T(8,128)(2,1)} %w_ref.3), custom_call_target="tpu_custom_call" | custom-call | flops 603979776 | bytes 5242880 | tf_op jit(solution)/shard_map/project/pallas_call | solution.py:176
  5.3 3.0 %collective-permute-start.1 = (f32[64,1024]{1,0:T(8,128)S(1)}, f32[64,1024]{1,0:T(8,128)S(1)}, u32[]{:S(2)}, u32[]{:S(2)}) collective-permute-start(f32[64,1024]{1,0:T(8,128)S(1)} %get-tuple-element.37.refs_1_), channel_id=1, source_target_pairs={{0,4},{2,6},{4,0},{6,2},{8,12},{10,14},{12,8},{14,10},{1,5},{3,7},... | collective-permute-start | bytes 786440 | tf_op jit(solution)/shard_map/ppermute | solution.py:338
  8.3 5.3 %project.3 = (f32[64,1024]{1,0:T(8,128)S(1)}, f32[64,1024]{1,0:T(8,128)S(1)}, f32[64,1280]{1,0:T(8,128)S(1)}, f32[64,1280]{1,0:T(8,128)S(1)}) custom-call(s32[2]{0:T(128)S(1)} %pad_add_fusion.ids_ref, bf16[64,2304]{1,0:T(8,128)(2,1)S(1)} %broadcast_select_fusion.own_ref, bf16[64,2304]{1,0:T(8,128)(2,1)S(1)} %collective-permute-done.other_ref, ...), custom_call_target="tpu_custom_call" | custom-call | flops 1358954496 | bytes 11796480 | tf_op jit(solution)/shard_map/project/pallas_call | solution.py:176
  13.7 1.6 %collective-permute-start.7 = (f32[64,1280]{1,0:T(8,128)S(1)}, f32[64,1280]{1,0:T(8,128)S(1)}, u32[]{:S(2)}, u32[]{:S(2)}) collective-permute-start(f32[64,1280]{1,0:T(8,128)S(1)} %get-tuple-element.41), channel_id=1, source_target_pairs={{0,2},{2,0},{4,6},{6,4},{8,10},{10,8},{12,14},{14,12},{1,3},{3,1},... | collective-permute-start | bytes 983048 | tf_op jit(solution)/shard_map/ppermute | solution.py:338
  15.8 2.6 %collective-permute-start.2 = (f32[32,1024]{1,0:T(8,128)S(1)}, f32[32,1024]{1,0:T(8,128)S(1)}, u32[]{:S(2)}, u32[]{:S(2)}) collective-permute-start(f32[32,1024]{1,0:T(8,128)S(1)} %slice.61), channel_id=1, source_target_pairs={{0,8},{2,10},{4,12},{6,14},{8,0},{10,2},{12,4},{14,6},{1,9},{3,11}... | collective-permute-start | bytes 393224 | tf_op jit(solution)/shard_map/ppermute | solution.py:338
  18.4 7.4 %collective-permute-done.4 = f32[64,1024]{1,0:T(8,128)S(1)} collective-permute-done((f32[64,1024]{1,0:T(8,128)S(1)}, f32[64,1024]{1,0:T(8,128)S(1)}, u32[]{:S(2)}, u32[]{:S(2)}) %collective-permute-start.4) | collective-permute-done | bytes 262176 | tf_op jit(solution)/shard_map/ppermute | solution.py:338
  25.9 0.6 collective-permute-start.5
  26.7 1.6 %collective-permute-start.3 = (f32[16,1024]{1,0:T(8,128)S(1)}, f32[16,1024]{1,0:T(8,128)S(1)}, u32[]{:S(2)}, u32[]{:S(2)}) collective-permute-start(f32[16,1024]{1,0:T(8,128)S(1)} %slice.63), channel_id=1, source_target_pairs={{0,2},{2,0},{4,6},{6,4},{8,10},{10,8},{12,14},{14,12},{1,3},{3,1},... | collective-permute-start | bytes 196616 | tf_op jit(solution)/shard_map/ppermute | solution.py:338
  28.3 2.7 %collective-permute-done.5 = f32[32,1024]{1,0:T(8,128)S(1)} collective-permute-done((f32[32,1024]{1,0:T(8,128)S(1)}, f32[32,1024]{1,0:T(8,128)S(1)}, u32[]{:S(2)}, u32[]{:S(2)}) %collective-permute-start.5) | collective-permute-done | bytes 131104 | tf_op jit(solution)/shard_map/ppermute | solution.py:338
  31.0 1.5 %collective-permute-start.6 = (f32[16,1024]{1,0:T(8,128)S(1)}, f32[16,1024]{1,0:T(8,128)S(1)}, u32[]{:S(2)}, u32[]{:S(2)}) collective-permute-start(f32[16,1024]{1,0:T(8,128)S(1)} %slice.67), channel_id=1, source_target_pairs={{0,8},{2,10},{4,12},{6,14},{8,0},{10,2},{12,4},{14,6},{1,9},{3,11}... | collective-permute-start | bytes 196616 | tf_op jit(solution)/shard_map/ppermute | solution.py:338
  32.6 1.6 %collective-permute-start.9 = (f32[16,1280]{1,0:T(8,128)S(1)}, f32[16,1280]{1,0:T(8,128)S(1)}, u32[]{:S(2)}, u32[]{:S(2)}) collective-permute-start(f32[16,1280]{1,0:T(8,128)S(1)} %slice.72), channel_id=1, source_target_pairs={{0,8},{2,10},{4,12},{6,14},{8,0},{10,2},{12,4},{14,6},{1,9},{3,11}... | collective-permute-start | bytes 245768 | tf_op jit(solution)/shard_map/ppermute | solution.py:338
  34.2 2.4 %collective-permute-done.6 = f32[16,1024]{1,0:T(8,128)S(1)} collective-permute-done((f32[16,1024]{1,0:T(8,128)S(1)}, f32[16,1024]{1,0:T(8,128)S(1)}, u32[]{:S(2)}, u32[]{:S(2)}) %collective-permute-start.6) | collective-permute-done | bytes 65568 | tf_op jit(solution)/shard_map/ppermute | solution.py:338
  36.7 3.5 %collective-permute-done.9 = f32[16,1280]{1,0:T(8,128)S(1)} collective-permute-done((f32[16,1280]{1,0:T(8,128)S(1)}, f32[16,1280]{1,0:T(8,128)S(1)}, u32[]{:S(2)}, u32[]{:S(2)}) %collective-permute-start.9) | collective-permute-done | bytes 81952 | tf_op jit(solution)/shard_map/ppermute | solution.py:338
  40.4 1.1 %collective-permute-done.12.refs_5_ = bf16[8,1280]{1,0:T(8,128)(2,1)S(1)} collective-permute-done((bf16[8,1280]{1,0:T(8,128)(2,1)S(1)}, bf16[8,1280]{1,0:T(8,128)(2,1)S(1)}, u32[]{:S(2)}, u32[]{:S(2)}) %collective-permute-start.12) | collective-permute-done | bytes 20512 | tf_op jit(solution)/shard_map/ppermute | solution.py:335
  41.5 4.3 %attend.1 = (bf16[8,3072]{1,0:T(8,128)(2,1)S(1)}, bf16[8,3072]{1,0:T(8,128)(2,1)S(1)}) custom-call(s32[9]{0:T(128)S(1)} %pad_add_fusion.1.scalars_ref, bf16[8,1024]{1,0:T(8,128)(2,1)S(1)} %get-tuple-element.74.refs_0_, bf16[8,1024]{1,0:T(8,128)(2,1)S(1)} %get-tuple-element.72.refs_1_, bf16[8,1280]{1,0:T(8,128)(2,1)S(1)} %get-tuple-element.70.refs_2_, ...), custom_call_target="tpu_custom_call" | custom-call | flops 201326592 | bytes 8388608 | tf_op jit(solution)/shard_map/attend/pallas_call | solution.py:255
  46.0 1.1 %collective-permute-done.13 = bf16[8,3072]{1,0:T(8,128)(2,1)S(1)} collective-permute-done((bf16[8,3072]{1,0:T(8,128)(2,1)S(1)}, bf16[8,3072]{1,0:T(8,128)(2,1)S(1)}, u32[]{:S(2)}, u32[]{:S(2)}) %collective-permute-start.13) | collective-permute-done | bytes 49184 | tf_op jit(solution)/shard_map/ppermute | solution.py:335
  47.1 1.0 %collective-permute-start.16 = (bf16[16,1536]{1,0:T(8,128)(2,1)S(1)}, bf16[16,1536]{1,0:T(8,128)(2,1)S(1)}, u32[]{:S(2)}, u32[]{:S(2)}) collective-permute-start(bf16[16,1536]{1,0:T(8,128)(2,1)S(1)} %get-tuple-element.67), channel_id=1, source_target_pairs={{0,2},{2,0},{4,6},{6,4},{8,10},{10,8},{12,14},{14,12},{1,3},{3,1},... | collective-permute-start | bytes 147464 | tf_op jit(solution)/shard_map/ppermute | solution.py:338
  48.6 2.7 %collective-permute-done.16 = bf16[16,1536]{1,0:T(8,128)(2,1)S(1)} collective-permute-done((bf16[16,1536]{1,0:T(8,128)(2,1)S(1)}, bf16[16,1536]{1,0:T(8,128)(2,1)S(1)}, u32[]{:S(2)}, u32[]{:S(2)}) %collective-permute-start.16) | collective-permute-done | bytes 49184 | tf_op jit(solution)/shard_map/ppermute | solution.py:338
  51.4 1.8 %collective-permute-done.14 = bf16[16,1536]{1,0:T(8,128)(2,1)S(1)} collective-permute-done((bf16[16,1536]{1,0:T(8,128)(2,1)S(1)}, bf16[16,1536]{1,0:T(8,128)(2,1)S(1)}, u32[]{:S(2)}, u32[]{:S(2)}) %collective-permute-start.14) | collective-permute-done | bytes 49184 | tf_op jit(solution)/shard_map/ppermute | solution.py:338
  53.2 1.4 %collective-permute-start.15 = (bf16[32,1536]{1,0:T(8,128)(2,1)S(1)}, bf16[32,1536]{1,0:T(8,128)(2,1)S(1)}, u32[]{:S(2)}, u32[]{:S(2)}) collective-permute-start(bf16[32,1536]{1,0:T(8,128)(2,1)S(1)} %pad_maximum_fusion.2.refs_0_), channel_id=1, source_target_pairs={{0,4},{2,6},{4,0},{6,2},{8,12},{10,14},{12,8},{14,10},{1,5},{3,7},... | collective-permute-start | bytes 294920 | tf_op jit(solution)/shard_map/ppermute | solution.py:338
  54.6 3.1 %load.2 = (bf16[512,768]{1,0:T(8,128)(2,1)S(1)}, bf16[512,768]{1,0:T(8,128)(2,1)S(1)}, bf16[512,768]{1,0:T(8,128)(2,1)S(1)}, bf16[512,768]{1,0:T(8,128)(2,1)S(1)...) custom-call(bf16[32,1536]{1,0:T(8,128)(2,1)S(1)} %pad_maximum_fusion, ...), custom_call_target="tpu_custom_call" | custom-call | bytes 14155776 | tf_op jit(solution)/shard_map/load/pallas_call | solution.py:78
  58.5 0.5 collective-permute-done.15
  59.1 1.6 %collective-permute-start.17 = (bf16[64,1536]{1,0:T(8,128)(2,1)S(1)}, bf16[64,1536]{1,0:T(8,128)(2,1)S(1)}, u32[]{:S(2)}, u32[]{:S(2)}) collective-permute-start(bf16[64,1536]{1,0:T(8,128)(2,1)S(1)} %maximum_add_fusion.refs_0_), channel_id=1, source_target_pairs={{0,2},{2,0},{4,6},{6,4},{8,10},{10,8},{12,14},{14,12},{1,3},{3,1},... | collective-permute-start | bytes 589832 | tf_op jit(solution)/shard_map/ppermute | solution.py:338
  60.7 3.7 %load.3 = (bf16[512,768]{1,0:T(8,128)(2,1)S(1)}, bf16[512,768]{1,0:T(8,128)(2,1)S(1)}, bf16[512,768]{1,0:T(8,128)(2,1)S(1)}, bf16[512,768]{1,0:T(8,128)(2,1)S(1)...) custom-call(bf16[64,1536]{1,0:T(8,128)(2,1)S(1)} %maximum_add_fusion, ...), custom_call_target="tpu_custom_call" | custom-call | bytes 14155776 | tf_op jit(solution)/shard_map/load/pallas_call | solution.py:78
  64.4 0.9 %collective-permute-done.17.refs_1_ = bf16[64,1536]{1,0:T(8,128)(2,1)S(1)} collective-permute-done((bf16[64,1536]{1,0:T(8,128)(2,1)S(1)}, bf16[64,1536]{1,0:T(8,128)(2,1)S(1)}, u32[]{:S(2)}, u32[]{:S(2)}) %collective-permute-start.17) | collective-permute-done | bytes 196640 | tf_op jit(solution)/shard_map/ppermute | solution.py:338
  65.3 2.0 %project_out.2 = (f32[64,1536]{1,0:T(8,128)S(1)}, f32[64,1536]{1,0:T(8,128)S(1)}) custom-call(s32[2]{0:T(128)S(1)} %pad_add_fusion.ids_ref, bf16[64,1536]{1,0:T(8,128)(2,1)S(1)} %maximum_add_fusion.refs_0_, bf16[64,1536]{1,0:T(8,128)(2,1)S(1)} %collective-permute-done.17.refs_1_, bf16[64,1536]{1,0:T(8,128)(2,1)S(1)} %pad_maximum_fusion.1.refs_1_.refs_2_, ...), custom_call_target="tpu_custom_call" | custom-call | flops 1207959552 | bytes 10223616 | tf_op jit(solution)/shard_map/project_out/pallas_call | solution.py:309
  67.3 1.4 %project_out.3 = (f32[64,768]{1,0:T(8,128)S(1)}, f32[64,768]{1,0:T(8,128)S(1)}) custom-call(s32[2]{0:T(128)S(1)} %pad_add_fusion.ids_ref, bf16[64,1536]{1,0:T(8,128)(2,1)S(1)} %maximum_add_fusion.refs_0_, bf16[64,1536]{1,0:T(8,128)(2,1)S(1)} %collective-permute-done.17.refs_1_, bf16[64,1536]{1,0:T(8,128)(2,1)S(1)} %pad_maximum_fusion.1.refs_1_.refs_2_, ...), custom_call_target="tpu_custom_call" | custom-call | flops 603979776 | bytes 5111808 | tf_op jit(solution)/shard_map/project_out/pallas_call | solution.py:309
  68.8 0.5 collective-permute-start.20
  69.3 0.9 %collective-permute-done.21 = f32[64,768]{1,0:T(8,128)S(1)} collective-permute-done((f32[64,768]{1,0:T(8,128)S(1)}, f32[64,768]{1,0:T(8,128)S(1)}, u32[]{:S(2)}, u32[]{:S(2)}) %collective-permute-start.21) | collective-permute-done | bytes 196640 | tf_op jit(solution)/shard_map/ppermute | solution.py:335
  70.2 0.5 collective-permute-done.20
  70.8 0.7 %pad_maximum_fusion = bf16[64,2304]{1,0:T(8,128)(2,1)} fusion(bf16[64,768]{1,0:T(8,128)(2,1)S(1)} %add_convert_fusion.1, bf16[64,1536]{1,0:T(8,128)(2,1)S(1)} %add_convert_fusion), kind=kLoop, calls=%fused_computation.1 | loop fusion | flops 589824 | bytes 589824 | tf_op jit(solution)/shard_map/concatenate | solution.py:412
  (57 shorter events, 3.8 us)
Async XLA Ops:
  0.0 1.9 %collective-permute-start = (bf16[64,2304]{1,0:T(8,128)(2,1)}, bf16[64,2304]{1,0:T(8,128)(2,1)S(1)}, u32[]{:S(2)}, u32[]{:S(2)}) collective-permute-start(bf16[64,2304]{1,0:T(8,128)(2,1)} %param.7), channel_id=1, source_target_pairs={{0,1},{1,0},{2,3},{3,2},{4,5},{5,4},{6,7},{7,6},{8,9},{9,8},{10,11... | collective-permute-start | bytes 884744 | tf_op jit(solution)/shard_map/ppermute | solution.py:335
  1.5 6.8 %copy-start.1 = (bf16[2304,512]{1,0:T(8,128)(2,1)S(1)}, bf16[2304,512]{1,0:T(8,128)(2,1)}, u32[]{:S(2)}) copy-start(bf16[2304,512]{1,0:T(8,128)(2,1)} %refs_0_.1) | copy-start | bytes 7077892
  5.3 10.4 %collective-permute-start.1 = (f32[64,1024]{1,0:T(8,128)S(1)}, f32[64,1024]{1,0:T(8,128)S(1)}, u32[]{:S(2)}, u32[]{:S(2)}) collective-permute-start(f32[64,1024]{1,0:T(8,128)S(1)} %get-tuple-element.37.refs_1_), channel_id=1, source_target_pairs={{0,4},{2,6},{4,0},{6,2},{8,12},{10,14},{12,8},{14,10},{1,5},{3,7},... | collective-permute-start | bytes 786440 | tf_op jit(solution)/shard_map/ppermute | solution.py:338
  13.7 26.7 %copy-start.2 = (s32[8]{0:T(128)S(1)}, s32[8]{0:T(128)}, u32[]{:S(2)}) copy-start(s32[8]{0:T(128)} %param.13) | copy-start | bytes 100
  13.7 12.8 %collective-permute-start.7 = (f32[64,1280]{1,0:T(8,128)S(1)}, f32[64,1280]{1,0:T(8,128)S(1)}, u32[]{:S(2)}, u32[]{:S(2)}) collective-permute-start(f32[64,1280]{1,0:T(8,128)S(1)} %get-tuple-element.41), channel_id=1, source_target_pairs={{0,2},{2,0},{4,6},{6,4},{8,10},{10,8},{12,14},{14,12},{1,3},{3,1},... | collective-permute-start | bytes 983048 | tf_op jit(solution)/shard_map/ppermute | solution.py:338
  15.3 10.6 %collective-permute-start.4 = (f32[64,1024]{1,0:T(8,128)S(1)}, f32[64,1024]{1,0:T(8,128)S(1)}, u32[]{:S(2)}, u32[]{:S(2)}) collective-permute-start(f32[64,1024]{1,0:T(8,128)S(1)} %get-tuple-element.39), channel_id=1, source_target_pairs={{0,4},{2,6},{4,0},{6,2},{8,12},{10,14},{12,8},{14,10},{1,5},{3,7},... | collective-permute-start | bytes 786440 | tf_op jit(solution)/shard_map/ppermute | solution.py:338
  15.8 10.9 %collective-permute-start.2 = (f32[32,1024]{1,0:T(8,128)S(1)}, f32[32,1024]{1,0:T(8,128)S(1)}, u32[]{:S(2)}, u32[]{:S(2)}) collective-permute-start(f32[32,1024]{1,0:T(8,128)S(1)} %slice.61), channel_id=1, source_target_pairs={{0,8},{2,10},{4,12},{6,14},{8,0},{10,2},{12,4},{14,6},{1,9},{3,11}... | collective-permute-start | bytes 393224 | tf_op jit(solution)/shard_map/ppermute | solution.py:338
  18.4 23.1 %copy-start = (bf16[8,1024,256]{2,1,0:T(8,128)(2,1)S(1)}, bf16[8,1024,256]{2,1,0:T(8,128)(2,1)}, u32[]{:S(2)}) copy-start(bf16[8,1024,256]{2,1,0:T(8,128)(2,1)} %refs_6_.1) | copy-start | bytes 12582916
  25.9 5.0 %collective-permute-start.5 = (f32[32,1024]{1,0:T(8,128)S(1)}, f32[32,1024]{1,0:T(8,128)S(1)}, u32[]{:S(2)}, u32[]{:S(2)}) collective-permute-start(f32[32,1024]{1,0:T(8,128)S(1)} %slice.65), channel_id=1, source_target_pairs={{0,2},{2,0},{4,6},{6,4},{8,10},{10,8},{12,14},{14,12},{1,3},{3,1},... | collective-permute-start | bytes 393224 | tf_op jit(solution)/shard_map/ppermute | solution.py:338
  26.6 6.0 %collective-permute-start.8 = (f32[32,1280]{1,0:T(8,128)S(1)}, f32[32,1280]{1,0:T(8,128)S(1)}, u32[]{:S(2)}, u32[]{:S(2)}) collective-permute-start(f32[32,1280]{1,0:T(8,128)S(1)} %slice.69), channel_id=1, source_target_pairs={{0,4},{2,6},{4,0},{6,2},{8,12},{10,14},{12,8},{14,10},{1,5},{3,7},... | collective-permute-start | bytes 491528 | tf_op jit(solution)/shard_map/ppermute | solution.py:338
  26.7 5.8 %collective-permute-start.3 = (f32[16,1024]{1,0:T(8,128)S(1)}, f32[16,1024]{1,0:T(8,128)S(1)}, u32[]{:S(2)}, u32[]{:S(2)}) collective-permute-start(f32[16,1024]{1,0:T(8,128)S(1)} %slice.63), channel_id=1, source_target_pairs={{0,2},{2,0},{4,6},{6,4},{8,10},{10,8},{12,14},{14,12},{1,3},{3,1},... | collective-permute-start | bytes 196616 | tf_op jit(solution)/shard_map/ppermute | solution.py:338
  31.0 5.6 %collective-permute-start.6 = (f32[16,1024]{1,0:T(8,128)S(1)}, f32[16,1024]{1,0:T(8,128)S(1)}, u32[]{:S(2)}, u32[]{:S(2)}) collective-permute-start(f32[16,1024]{1,0:T(8,128)S(1)} %slice.67), channel_id=1, source_target_pairs={{0,8},{2,10},{4,12},{6,14},{8,0},{10,2},{12,4},{14,6},{1,9},{3,11}... | collective-permute-start | bytes 196616 | tf_op jit(solution)/shard_map/ppermute | solution.py:338
  32.5 7.9 %collective-permute-start.10 = (bf16[8,1024]{1,0:T(8,128)(2,1)S(1)}, bf16[8,1024]{1,0:T(8,128)(2,1)S(1)}, u32[]{:S(2)}, u32[]{:S(2)}) collective-permute-start(bf16[8,1024]{1,0:T(8,128)(2,1)S(1)} %get-tuple-element.73), channel_id=1, source_target_pairs={{0,1},{1,0},{2,3},{3,2},{4,5},{5,4},{6,7},{7,6},{8,9},{9,8},{10,11... | collective-permute-start | bytes 49160 | tf_op jit(solution)/shard_map/ppermute | solution.py:335
  32.6 7.6 %collective-permute-start.9 = (f32[16,1280]{1,0:T(8,128)S(1)}, f32[16,1280]{1,0:T(8,128)S(1)}, u32[]{:S(2)}, u32[]{:S(2)}) collective-permute-start(f32[16,1280]{1,0:T(8,128)S(1)} %slice.72), channel_id=1, source_target_pairs={{0,8},{2,10},{4,12},{6,14},{8,0},{10,2},{12,4},{14,6},{1,9},{3,11}... | collective-permute-start | bytes 245768 | tf_op jit(solution)/shard_map/ppermute | solution.py:338
  36.6 3.8 %collective-permute-start.11 = (bf16[8,1024]{1,0:T(8,128)(2,1)S(1)}, bf16[8,1024]{1,0:T(8,128)(2,1)S(1)}, u32[]{:S(2)}, u32[]{:S(2)}) collective-permute-start(bf16[8,1024]{1,0:T(8,128)(2,1)S(1)} %get-tuple-element.71), channel_id=1, source_target_pairs={{0,1},{1,0},{2,3},{3,2},{4,5},{5,4},{6,7},{7,6},{8,9},{9,8},{10,11... | collective-permute-start | bytes 49160 | tf_op jit(solution)/shard_map/ppermute | solution.py:335
  40.2 1.3 %collective-permute-start.12 = (bf16[8,1280]{1,0:T(8,128)(2,1)S(1)}, bf16[8,1280]{1,0:T(8,128)(2,1)S(1)}, u32[]{:S(2)}, u32[]{:S(2)}) collective-permute-start(bf16[8,1280]{1,0:T(8,128)(2,1)S(1)} %get-tuple-element.69), channel_id=1, source_target_pairs={{0,1},{1,0},{2,3},{3,2},{4,5},{5,4},{6,7},{7,6},{8,9},{9,8},{10,11... | collective-permute-start | bytes 61448 | tf_op jit(solution)/shard_map/ppermute | solution.py:335
  45.8 1.3 %collective-permute-start.13 = (bf16[8,3072]{1,0:T(8,128)(2,1)S(1)}, bf16[8,3072]{1,0:T(8,128)(2,1)S(1)}, u32[]{:S(2)}, u32[]{:S(2)}) collective-permute-start(bf16[8,3072]{1,0:T(8,128)(2,1)S(1)} %get-tuple-element.43), channel_id=1, source_target_pairs={{0,1},{1,0},{2,3},{3,2},{4,5},{5,4},{6,7},{7,6},{8,9},{9,8},{10,11... | collective-permute-start | bytes 147464 | tf_op jit(solution)/shard_map/ppermute | solution.py:335
  47.1 4.2 %collective-permute-start.16 = (bf16[16,1536]{1,0:T(8,128)(2,1)S(1)}, bf16[16,1536]{1,0:T(8,128)(2,1)S(1)}, u32[]{:S(2)}, u32[]{:S(2)}) collective-permute-start(bf16[16,1536]{1,0:T(8,128)(2,1)S(1)} %get-tuple-element.67), channel_id=1, source_target_pairs={{0,2},{2,0},{4,6},{6,4},{8,10},{10,8},{12,14},{14,12},{1,3},{3,1},... | collective-permute-start | bytes 147464 | tf_op jit(solution)/shard_map/ppermute | solution.py:338
  48.2 5.0 %collective-permute-start.14 = (bf16[16,1536]{1,0:T(8,128)(2,1)S(1)}, bf16[16,1536]{1,0:T(8,128)(2,1)S(1)}, u32[]{:S(2)}, u32[]{:S(2)}) collective-permute-start(bf16[16,1536]{1,0:T(8,128)(2,1)S(1)} %get-tuple-element.68), channel_id=1, source_target_pairs={{0,8},{2,10},{4,12},{6,14},{8,0},{10,2},{12,4},{14,6},{1,9},{3,11}... | collective-permute-start | bytes 147464 | tf_op jit(solution)/shard_map/ppermute | solution.py:338
  51.3 6.7 %collective-permute-start.18 = (bf16[32,1536]{1,0:T(8,128)(2,1)S(1)}, bf16[32,1536]{1,0:T(8,128)(2,1)S(1)}, u32[]{:S(2)}, u32[]{:S(2)}) collective-permute-start(bf16[32,1536]{1,0:T(8,128)(2,1)S(1)} %pad_maximum_fusion.3.refs_1_), channel_id=1, source_target_pairs={{0,8},{2,10},{4,12},{6,14},{8,0},{10,2},{12,4},{14,6},{1,9},{3,11}... | collective-permute-start | bytes 294920 | tf_op jit(solution)/shard_map/ppermute | solution.py:338
  53.2 5.9 %collective-permute-start.15 = (bf16[32,1536]{1,0:T(8,128)(2,1)S(1)}, bf16[32,1536]{1,0:T(8,128)(2,1)S(1)}, u32[]{:S(2)}, u32[]{:S(2)}) collective-permute-start(bf16[32,1536]{1,0:T(8,128)(2,1)S(1)} %pad_maximum_fusion.2.refs_0_), channel_id=1, source_target_pairs={{0,4},{2,6},{4,0},{6,2},{8,12},{10,14},{12,8},{14,10},{1,5},{3,7},... | collective-permute-start | bytes 294920 | tf_op jit(solution)/shard_map/ppermute | solution.py:338
  58.1 6.4 %collective-permute-start.19 = (bf16[64,1536]{1,0:T(8,128)(2,1)S(1)}, bf16[64,1536]{1,0:T(8,128)(2,1)S(1)}, u32[]{:S(2)}, u32[]{:S(2)}) collective-permute-start(bf16[64,1536]{1,0:T(8,128)(2,1)S(1)} %pad_maximum_fusion.1.refs_1_.refs_2_), channel_id=1, source_target_pairs={{0,4},{2,6},{4,0},{6,2},{8,12},{10,14},{12,8},{14,10},{1,5},{3,7},... | collective-permute-start | bytes 589832 | tf_op jit(solution)/shard_map/ppermute | solution.py:338
  59.1 6.2 %collective-permute-start.17 = (bf16[64,1536]{1,0:T(8,128)(2,1)S(1)}, bf16[64,1536]{1,0:T(8,128)(2,1)S(1)}, u32[]{:S(2)}, u32[]{:S(2)}) collective-permute-start(bf16[64,1536]{1,0:T(8,128)(2,1)S(1)} %maximum_add_fusion.refs_0_), channel_id=1, source_target_pairs={{0,2},{2,0},{4,6},{6,4},{8,10},{10,8},{12,14},{14,12},{1,3},{3,1},... | collective-permute-start | bytes 589832 | tf_op jit(solution)/shard_map/ppermute | solution.py:338
  68.7 1.5 %collective-permute-start.21 = (f32[64,768]{1,0:T(8,128)S(1)}, f32[64,768]{1,0:T(8,128)S(1)}, u32[]{:S(2)}, u32[]{:S(2)}) collective-permute-start(f32[64,768]{1,0:T(8,128)S(1)} %get-tuple-element.66), channel_id=1, source_target_pairs={{0,1},{1,0},{2,3},{3,2},{4,5},{5,4},{6,7},{7,6},{8,9},{9,8},{10,11... | collective-permute-start | bytes 589832 | tf_op jit(solution)/shard_map/ppermute | solution.py:335
  68.8 2.0 %collective-permute-start.20 = (f32[64,1536]{1,0:T(8,128)S(1)}, f32[64,1536]{1,0:T(8,128)S(1)}, u32[]{:S(2)}, u32[]{:S(2)}) collective-permute-start(f32[64,1536]{1,0:T(8,128)S(1)} %get-tuple-element.58.refs_10_), channel_id=1, source_target_pairs={{0,1},{1,0},{2,3},{3,2},{4,5},{5,4},{6,7},{7,6},{8,9},{9,8},{10,11... | collective-permute-start | bytes 1179656 | tf_op jit(solution)/shard_map/ppermute | solution.py:335

commit v13 on v10

--- a/solution.py
+++ b/solution.py
@@ -194,25 +194,22 @@
     return list(zip(outs[::2], outs[1::2]))
 
 
-def attend_kernel(parts, scalars_ref, *refs):
-    own_q, other_q = refs[: len(parts)], refs[len(parts) : 2 * len(parts)]
-    k_ref, v_hbm, own_out, other_out, v_ref, q_scr, o_scr, sems = refs[2 * len(parts) :]
+def attend_kernel(kv_column, scalars_ref, own_q, other_q, *refs):
+    k_ref, v_hbm, own_out, other_out, v_ref, q_scr, o_scr, sems = refs
     core = scalars_ref[0]
     rows, positions, _ = k_ref.shape
     copies = [pltpu.make_async_copy(v_hbm.at[row], v_ref.at[row], sems.at[row]) for row in range(rows)]
     for copy in copies:
         copy.start()
     at = 0
-    for side in (own_q, other_q):
-        for ref, (heads, skip) in zip(side, parts):
-            for head in range(heads):
-                column = skip + head * DH
+    for ref in (own_q, other_q):
+        for column in range(0, ref.shape[1], DH):
+            if column != kv_column:
                 q_scr[:, at, :] = ref[:, column : column + DH].astype(jnp.float32)
                 at += 1
     total_heads = at
-    kv_at = [skip > 0 for _, skip in parts].index(True)
-    first = own_q[kv_at][:, :DH].astype(jnp.float32)
-    second = other_q[kv_at][:, :DH].astype(jnp.float32)
+    first = own_q[:, kv_column : kv_column + DH].astype(jnp.float32)
+    second = other_q[:, kv_column : kv_column + DH].astype(jnp.float32)
     new_keys = jnp.where(core == 0, first, second)
     new_values = jnp.where(core == 0, second, first)
     scale = DH**-0.5
@@ -247,15 +244,15 @@
         ref[:, column : column + DH] = o_scr[:, head, :].astype(jnp.bfloat16)
 
 
-def attend(core, lengths, own_q, other_q, parts, keys, values):
+def attend(core, lengths, own_q, other_q, kv_column, keys, values):
     rows, positions, _ = keys.shape
-    heads = 2 * sum(part[0] for part in parts)
+    heads = 2 * (own_q.shape[1] // DH - 1)
     out = jax.ShapeDtypeStruct((rows, heads * DH // 2), jnp.bfloat16)
     scalars = jnp.concatenate([core[None], lengths])
     return pl.pallas_call(
-        functools.partial(attend_kernel, parts),
+        functools.partial(attend_kernel, kv_column),
         out_shape=(out, out),
-        in_specs=[SMEM] + [VMEM] * (2 * len(parts) + 1) + [HBM],
+        in_specs=[SMEM] + [VMEM] * 3 + [HBM],
         out_specs=(VMEM, VMEM),
         scratch_shapes=[pltpu.VMEM(values.shape, values.dtype)]
         + [pltpu.VMEM((rows, heads, DH), jnp.float32)] * 2
@@ -267,7 +264,7 @@
             transcendentals=rows * heads * positions,
         ),
         name="attend",
-    )(scalars, *own_q, *other_q, keys, values)
+    )(scalars, own_q, other_q, keys, values)
 
 
 def output_kernel(orders, rows, columns, pieces, after, ids_ref, *refs):
@@ -364,17 +361,13 @@
                 moving[i] = across(state[i][0], order[step + 1])
             else:
                 state[i] = total
-    mine, theirs = [], []
-    for total in state:
-        mine.append(lax.dynamic_slice_in_dim(total, core * own_rows, own_rows, 0).astype(jnp.bfloat16))
-        give = lax.dynamic_slice_in_dim(total, (1 - core) * own_rows, own_rows, 0).astype(jnp.bfloat16)
-        theirs.append(swap(give))
-
     kv_width = kv_weight.shape[1] // 2
     by_column = [i for group in ((2,), (0, 1)) for i in group]
-    parts = tuple((plan[i][0] // DH, 0 if i else kv_width) for i in by_column)
-    mine, theirs = [mine[i] for i in by_column], [theirs[i] for i in by_column]
-    own, other = attend(core, lengths, mine, theirs, parts, key_cache, value_cache)
+    total = jnp.concatenate([state[i] for i in by_column], axis=1)
+    mine = lax.dynamic_slice_in_dim(total, core * own_rows, own_rows, 0).astype(jnp.bfloat16)
+    give = lax.dynamic_slice_in_dim(total, (1 - core) * own_rows, own_rows, 0).astype(jnp.bfloat16)
+    kv_column = sum(plan[i][0] for i in by_column[: by_column.index(0)])
+    own, other = attend(core, lengths, mine, swap(give), kv_column, key_cache, value_cache)
     got = swap(other)
     block = jnp.where(core == 0, jnp.concatenate([own, got]), jnp.concatenate([got, own]))
 

time: 73.4 us -> 71 us (0.967)
  waiting for transfers between devices: 27 us -> 23.4 us
  starting transfers between devices: 20.4 us -> 21.6 us
    ppermute x15, waiting for transfers between devices: 23 us -> 19.3 us  [across(): return lax.ppermute(array, 'gx', [(g, g ^ mask) for g in range(n)])]
    ppermute x15, starting transfers between devices: 19 us -> 20.3 us  [across(): return lax.ppermute(array, 'gx', [(g, g ^ mask) for g in range(n)])]
    ppermute x7 -> x5, waiting for transfers between devices: 3.97 us -> 4.03 us  [swap(): return lax.ppermute(array, 'gy', [(0, 1), (1, 0)])]
  transfers between devices with their start and end apart: 22 -> 20, of which waited for: 13 -> 14; matrix products, arithmetic and copies ran while one was open for 2% -> 2% of each run, Pallas kernels for 17% -> 17%
where the time goes in v13:
time: 71 us; the launch traced here: 70.8 us
  waiting for transfers between devices  23.4 us (33%)
  Pallas kernels  23.3 us (33%)
  starting transfers between devices  21.6 us (30%)
  other arithmetic  2.26 us (3%)
    ppermute x15, starting transfers between devices, across(): return lax.ppermute(array, 'gx', [(g, g ^ mask) for g in range(n)])  20.3 us
    ppermute x15, waiting for transfers between devices, across(): return lax.ppermute(array, 'gx', [(g, g ^ mask) for g in range(n)])  19.3 us
    pallas_call x2, Pallas kernels, project(): pl.pallas_call(functools.partial(project_kernel, orders, rows, first, wid...  8.76 us
    pallas_call x2, Pallas kernels, load(): pl.pallas_call(functools.partial(load_kernel, len(after), cuts, len(array...  6.84 us
    pallas_call x1, Pallas kernels, attend(): pl.pallas_call(functools.partial(attend_kernel, kv_column), out_shape=(ou...  4.3 us
    ppermute x5, waiting for transfers between devices, swap(): return lax.ppermute(array, 'gy', [(0, 1), (1, 0)])  4.03 us
    pallas_call x2, Pallas kernels, project_out(): pl.pallas_call(functools.partial(output_kernel, orders, rows, columns, pi...  3.39 us
  transfers between devices with their start and end apart: 20, of which 14 were waited for; matrix products, arithmetic and copies ran while one was open for 2% of the time, Pallas kernels for 17%

profile of v13, /device:TPU:0, one launch (start us, length us, event | category | flops | bytes accessed | tf_op | source)
XLA Modules:
  0.0 70.8 jit_solution(8339002792078054255)
XLA Ops:
  0.5 1.0 %broadcast_select_fusion.own_ref = bf16[64,2304]{1,0:T(8,128)(2,1)S(1)} fusion(bf16[64,2304]{1,0:T(8,128)(2,1)} %param.7, pred[]{:T(512)S(6)} %lt.9), kind=kLoop, calls=%fused_computation.2 | loop fusion | flops 147456 | bytes 589825 | tf_op jit(solution)/shard_map/jit(_where)/select_n | solution.py:338
  1.9 3.4 %project.2 = (f32[64,1024]{1,0:T(8,128)S(1)}, f32[64,1024]{1,0:T(8,128)S(1)}) custom-call(s32[2]{0:T(128)S(1)} %pad_add_fusion.ids_ref, bf16[64,2304]{1,0:T(8,128)(2,1)S(1)} %broadcast_select_fusion.own_ref, bf16[64,2304]{1,0:T(8,128)(2,1)S(1)} %collective-permute-done.other_ref, bf16[2304,3072]{1,0:T(8,128)(2,1)} %w_ref.3), custom_call_target="tpu_custom_call" | custom-call | flops 603979776 | bytes 5242880 | tf_op jit(solution)/shard_map/project/pallas_call | solution.py:176
  5.3 3.0 %collective-permute-start.1 = (f32[64,1024]{1,0:T(8,128)S(1)}, f32[64,1024]{1,0:T(8,128)S(1)}, u32[]{:S(2)}, u32[]{:S(2)}) collective-permute-start(f32[64,1024]{1,0:T(8,128)S(1)} %get-tuple-element.37.refs_1_), channel_id=1, source_target_pairs={{0,4},{2,6},{4,0},{6,2},{8,12},{10,14},{12,8},{14,10},{1,5},{3,7},... | collective-permute-start | bytes 786440 | tf_op jit(solution)/shard_map/ppermute | solution.py:335
  8.3 5.3 %project.3 = (f32[64,1024]{1,0:T(8,128)S(1)}, f32[64,1024]{1,0:T(8,128)S(1)}, f32[64,1280]{1,0:T(8,128)S(1)}, f32[64,1280]{1,0:T(8,128)S(1)}) custom-call(s32[2]{0:T(128)S(1)} %pad_add_fusion.ids_ref, bf16[64,2304]{1,0:T(8,128)(2,1)S(1)} %broadcast_select_fusion.own_ref, bf16[64,2304]{1,0:T(8,128)(2,1)S(1)} %collective-permute-done.other_ref, ...), custom_call_target="tpu_custom_call" | custom-call | flops 1358954496 | bytes 11796480 | tf_op jit(solution)/shard_map/project/pallas_call | solution.py:176
  13.7 1.6 %collective-permute-start.7 = (f32[64,1280]{1,0:T(8,128)S(1)}, f32[64,1280]{1,0:T(8,128)S(1)}, u32[]{:S(2)}, u32[]{:S(2)}) collective-permute-start(f32[64,1280]{1,0:T(8,128)S(1)} %get-tuple-element.41), channel_id=1, source_target_pairs={{0,2},{2,0},{4,6},{6,4},{8,10},{10,8},{12,14},{14,12},{1,3},{3,1},... | collective-permute-start | bytes 983048 | tf_op jit(solution)/shard_map/ppermute | solution.py:335
  15.8 2.6 %collective-permute-start.2 = (f32[32,1024]{1,0:T(8,128)S(1)}, f32[32,1024]{1,0:T(8,128)S(1)}, u32[]{:S(2)}, u32[]{:S(2)}) collective-permute-start(f32[32,1024]{1,0:T(8,128)S(1)} %slice.57), channel_id=1, source_target_pairs={{0,8},{2,10},{4,12},{6,14},{8,0},{10,2},{12,4},{14,6},{1,9},{3,11}... | collective-permute-start | bytes 393224 | tf_op jit(solution)/shard_map/ppermute | solution.py:335
  18.4 7.4 %collective-permute-done.4 = f32[64,1024]{1,0:T(8,128)S(1)} collective-permute-done((f32[64,1024]{1,0:T(8,128)S(1)}, f32[64,1024]{1,0:T(8,128)S(1)}, u32[]{:S(2)}, u32[]{:S(2)}) %collective-permute-start.4) | collective-permute-done | bytes 262176 | tf_op jit(solution)/shard_map/ppermute | solution.py:335
  25.9 0.6 collective-permute-start.5
  26.7 1.6 %collective-permute-start.3 = (f32[16,1024]{1,0:T(8,128)S(1)}, f32[16,1024]{1,0:T(8,128)S(1)}, u32[]{:S(2)}, u32[]{:S(2)}) collective-permute-start(f32[16,1024]{1,0:T(8,128)S(1)} %slice.59), channel_id=1, source_target_pairs={{0,2},{2,0},{4,6},{6,4},{8,10},{10,8},{12,14},{14,12},{1,3},{3,1},... | collective-permute-start | bytes 196616 | tf_op jit(solution)/shard_map/ppermute | solution.py:335
  28.3 2.7 %collective-permute-done.5 = f32[32,1024]{1,0:T(8,128)S(1)} collective-permute-done((f32[32,1024]{1,0:T(8,128)S(1)}, f32[32,1024]{1,0:T(8,128)S(1)}, u32[]{:S(2)}, u32[]{:S(2)}) %collective-permute-start.5) | collective-permute-done | bytes 131104 | tf_op jit(solution)/shard_map/ppermute | solution.py:335
  31.0 1.5 %collective-permute-start.6 = (f32[16,1024]{1,0:T(8,128)S(1)}, f32[16,1024]{1,0:T(8,128)S(1)}, u32[]{:S(2)}, u32[]{:S(2)}) collective-permute-start(f32[16,1024]{1,0:T(8,128)S(1)} %slice.63), channel_id=1, source_target_pairs={{0,8},{2,10},{4,12},{6,14},{8,0},{10,2},{12,4},{14,6},{1,9},{3,11}... | collective-permute-start | bytes 196616 | tf_op jit(solution)/shard_map/ppermute | solution.py:335
  32.5 1.6 %collective-permute-start.9 = (f32[16,1280]{1,0:T(8,128)S(1)}, f32[16,1280]{1,0:T(8,128)S(1)}, u32[]{:S(2)}, u32[]{:S(2)}) collective-permute-start(f32[16,1280]{1,0:T(8,128)S(1)} %slice.67), channel_id=1, source_target_pairs={{0,8},{2,10},{4,12},{6,14},{8,0},{10,2},{12,4},{14,6},{1,9},{3,11}... | collective-permute-start | bytes 245768 | tf_op jit(solution)/shard_map/ppermute | solution.py:335
  34.1 2.6 %collective-permute-done.6 = f32[16,1024]{1,0:T(8,128)S(1)} collective-permute-done((f32[16,1024]{1,0:T(8,128)S(1)}, f32[16,1024]{1,0:T(8,128)S(1)}, u32[]{:S(2)}, u32[]{:S(2)}) %collective-permute-start.6) | collective-permute-done | bytes 65568 | tf_op jit(solution)/shard_map/ppermute | solution.py:335
  36.7 1.3 %collective-permute-done.9 = f32[16,1280]{1,0:T(8,128)S(1)} collective-permute-done((f32[16,1280]{1,0:T(8,128)S(1)}, f32[16,1280]{1,0:T(8,128)S(1)}, u32[]{:S(2)}, u32[]{:S(2)}) %collective-permute-start.9) | collective-permute-done | bytes 81952 | tf_op jit(solution)/shard_map/ppermute | solution.py:335
  38.2 1.1 %collective-permute-done.10.other_q = bf16[8,3328]{1,0:T(8,128)(2,1)S(1)} collective-permute-done((bf16[8,3328]{1,0:T(8,128)(2,1)S(1)}, bf16[8,3328]{1,0:T(8,128)(2,1)S(1)}, u32[]{:S(2)}, u32[]{:S(2)}) %collective-permute-start.10) | collective-permute-done | bytes 53280 | tf_op jit(solution)/shard_map/ppermute | solution.py:332
  39.3 4.3 %attend.1 = (bf16[8,3072]{1,0:T(8,128)(2,1)S(1)}, bf16[8,3072]{1,0:T(8,128)(2,1)S(1)}) custom-call(s32[9]{0:T(128)S(1)} %pad_add_fusion.1.scalars_ref, bf16[8,3328]{1,0:T(8,128)(2,1)S(1)} %get-tuple-element.68.own_q, bf16[8,3328]{1,0:T(8,128)(2,1)S(1)} %collective-permute-done.10.other_q, bf16[8,1024,256]{2,1,0:T(8,128)(2,1)S(1)} %copy-done, ...), custom_call_target="tpu_custom_call" | custom-call | flops 201326592 | bytes 8388608 | tf_op jit(solution)/shard_map/attend/pallas_call | solution.py:252
  43.8 1.1 %collective-permute-done.11 = bf16[8,3072]{1,0:T(8,128)(2,1)S(1)} collective-permute-done((bf16[8,3072]{1,0:T(8,128)(2,1)S(1)}, bf16[8,3072]{1,0:T(8,128)(2,1)S(1)}, u32[]{:S(2)}, u32[]{:S(2)}) %collective-permute-start.11) | collective-permute-done | bytes 49184 | tf_op jit(solution)/shard_map/ppermute | solution.py:332
  44.9 2.4 %collective-permute-start.14 = (bf16[16,1536]{1,0:T(8,128)(2,1)S(1)}, bf16[16,1536]{1,0:T(8,128)(2,1)S(1)}, u32[]{:S(2)}, u32[]{:S(2)}) collective-permute-start(bf16[16,1536]{1,0:T(8,128)(2,1)S(1)} %get-tuple-element.69), channel_id=1, source_target_pairs={{0,2},{2,0},{4,6},{6,4},{8,10},{10,8},{12,14},{14,12},{1,3},{3,1},... | collective-permute-start | bytes 147464 | tf_op jit(solution)/shard_map/ppermute | solution.py:335
  47.4 0.8 %collective-permute-start.12 = (bf16[16,1536]{1,0:T(8,128)(2,1)S(1)}, bf16[16,1536]{1,0:T(8,128)(2,1)S(1)}, u32[]{:S(2)}, u32[]{:S(2)}) collective-permute-start(bf16[16,1536]{1,0:T(8,128)(2,1)S(1)} %get-tuple-element.70), channel_id=1, source_target_pairs={{0,8},{2,10},{4,12},{6,14},{8,0},{10,2},{12,4},{14,6},{1,9},{3,11}... | collective-permute-start | bytes 147464 | tf_op jit(solution)/shard_map/ppermute | solution.py:335
  48.2 1.3 %collective-permute-done.14 = bf16[16,1536]{1,0:T(8,128)(2,1)S(1)} collective-permute-done((bf16[16,1536]{1,0:T(8,128)(2,1)S(1)}, bf16[16,1536]{1,0:T(8,128)(2,1)S(1)}, u32[]{:S(2)}, u32[]{:S(2)}) %collective-permute-start.14) | collective-permute-done | bytes 49184 | tf_op jit(solution)/shard_map/ppermute | solution.py:335
  49.5 1.3 %collective-permute-start.16 = (bf16[32,1536]{1,0:T(8,128)(2,1)S(1)}, bf16[32,1536]{1,0:T(8,128)(2,1)S(1)}, u32[]{:S(2)}, u32[]{:S(2)}) collective-permute-start(bf16[32,1536]{1,0:T(8,128)(2,1)S(1)} %pad_maximum_fusion.4.refs_1_), channel_id=1, source_target_pairs={{0,8},{2,10},{4,12},{6,14},{8,0},{10,2},{12,4},{14,6},{1,9},{3,11}... | collective-permute-start | bytes 294920 | tf_op jit(solution)/shard_map/ppermute | solution.py:335
  50.8 2.2 %collective-permute-done.12 = bf16[16,1536]{1,0:T(8,128)(2,1)S(1)} collective-permute-done((bf16[16,1536]{1,0:T(8,128)(2,1)S(1)}, bf16[16,1536]{1,0:T(8,128)(2,1)S(1)}, u32[]{:S(2)}, u32[]{:S(2)}) %collective-permute-start.12) | collective-permute-done | bytes 49184 | tf_op jit(solution)/shard_map/ppermute | solution.py:335
  53.0 0.6 collective-permute-start.13
  53.6 3.1 %load.2 = (bf16[512,768]{1,0:T(8,128)(2,1)S(1)}, bf16[512,768]{1,0:T(8,128)(2,1)S(1)}, bf16[512,768]{1,0:T(8,128)(2,1)S(1)}, bf16[512,768]{1,0:T(8,128)(2,1)S(1)...) custom-call(bf16[32,1536]{1,0:T(8,128)(2,1)S(1)} %pad_maximum_fusion, ...), custom_call_target="tpu_custom_call" | custom-call | bytes 14155776 | tf_op jit(solution)/shard_map/load/pallas_call | solution.py:78
  57.0 1.3 %collective-permute-start.17 = (bf16[64,1536]{1,0:T(8,128)(2,1)S(1)}, bf16[64,1536]{1,0:T(8,128)(2,1)S(1)}, u32[]{:S(2)}, u32[]{:S(2)}) collective-permute-start(bf16[64,1536]{1,0:T(8,128)(2,1)S(1)} %pad_maximum_fusion.2.refs_1_.refs_2_), channel_id=1, source_target_pairs={{0,4},{2,6},{4,0},{6,2},{8,12},{10,14},{12,8},{14,10},{1,5},{3,7},... | collective-permute-start | bytes 589832 | tf_op jit(solution)/shard_map/ppermute | solution.py:335
  58.4 0.9 %collective-permute-start.15 = (bf16[64,1536]{1,0:T(8,128)(2,1)S(1)}, bf16[64,1536]{1,0:T(8,128)(2,1)S(1)}, u32[]{:S(2)}, u32[]{:S(2)}) collective-permute-start(bf16[64,1536]{1,0:T(8,128)(2,1)S(1)} %maximum_add_fusion.refs_0_), channel_id=1, source_target_pairs={{0,2},{2,0},{4,6},{6,4},{8,10},{10,8},{12,14},{14,12},{1,3},{3,1},... | collective-permute-start | bytes 589832 | tf_op jit(solution)/shard_map/ppermute | solution.py:335
  59.3 3.7 %load.3 = (bf16[512,768]{1,0:T(8,128)(2,1)S(1)}, bf16[512,768]{1,0:T(8,128)(2,1)S(1)}, bf16[512,768]{1,0:T(8,128)(2,1)S(1)}, bf16[512,768]{1,0:T(8,128)(2,1)S(1)...) custom-call(bf16[64,1536]{1,0:T(8,128)(2,1)S(1)} %maximum_add_fusion, ...), custom_call_target="tpu_custom_call" | custom-call | bytes 14155776 | tf_op jit(solution)/shard_map/load/pallas_call | solution.py:78
  63.4 1.2 %collective-permute-done.15.refs_1_ = bf16[64,1536]{1,0:T(8,128)(2,1)S(1)} collective-permute-done((bf16[64,1536]{1,0:T(8,128)(2,1)S(1)}, bf16[64,1536]{1,0:T(8,128)(2,1)S(1)}, u32[]{:S(2)}, u32[]{:S(2)}) %collective-permute-start.15) | collective-permute-done | bytes 196640 | tf_op jit(solution)/shard_map/ppermute | solution.py:335
  64.6 2.0 %project_out.2 = (f32[64,1536]{1,0:T(8,128)S(1)}, f32[64,1536]{1,0:T(8,128)S(1)}) custom-call(s32[2]{0:T(128)S(1)} %pad_add_fusion.ids_ref, bf16[64,1536]{1,0:T(8,128)(2,1)S(1)} %maximum_add_fusion.refs_0_, bf16[64,1536]{1,0:T(8,128)(2,1)S(1)} %collective-permute-done.15.refs_1_, bf16[64,1536]{1,0:T(8,128)(2,1)S(1)} %pad_maximum_fusion.2.refs_1_.refs_2_, ...), custom_call_target="tpu_custom_call" | custom-call | flops 1207959552 | bytes 10223616 | tf_op jit(solution)/shard_map/project_out/pallas_call | solution.py:306
  66.6 1.4 %project_out.3 = (f32[64,768]{1,0:T(8,128)S(1)}, f32[64,768]{1,0:T(8,128)S(1)}) custom-call(s32[2]{0:T(128)S(1)} %pad_add_fusion.ids_ref, bf16[64,1536]{1,0:T(8,128)(2,1)S(1)} %maximum_add_fusion.refs_0_, bf16[64,1536]{1,0:T(8,128)(2,1)S(1)} %collective-permute-done.15.refs_1_, bf16[64,1536]{1,0:T(8,128)(2,1)S(1)} %pad_maximum_fusion.2.refs_1_.refs_2_, ...), custom_call_target="tpu_custom_call" | custom-call | flops 603979776 | bytes 5111808 | tf_op jit(solution)/shard_map/project_out/pallas_call | solution.py:306
  68.6 0.9 %collective-permute-done.19 = f32[64,768]{1,0:T(8,128)S(1)} collective-permute-done((f32[64,768]{1,0:T(8,128)S(1)}, f32[64,768]{1,0:T(8,128)S(1)}, u32[]{:S(2)}, u32[]{:S(2)}) %collective-permute-start.19) | collective-permute-done | bytes 196640 | tf_op jit(solution)/shard_map/ppermute | solution.py:332
  70.1 0.7 %pad_maximum_fusion = bf16[64,2304]{1,0:T(8,128)(2,1)} fusion(bf16[64,768]{1,0:T(8,128)(2,1)S(1)} %add_convert_fusion.1, bf16[64,1536]{1,0:T(8,128)(2,1)S(1)} %add_convert_fusion), kind=kLoop, calls=%fused_computation.1 | loop fusion | flops 589824 | bytes 589824 | tf_op jit(solution)/shard_map/concatenate | solution.py:400
  (51 shorter events, 4.1 us)
Async XLA Ops:
  0.0 1.9 %collective-permute-start = (bf16[64,2304]{1,0:T(8,128)(2,1)}, bf16[64,2304]{1,0:T(8,128)(2,1)S(1)}, u32[]{:S(2)}, u32[]{:S(2)}) collective-permute-start(bf16[64,2304]{1,0:T(8,128)(2,1)} %param.7), channel_id=1, source_target_pairs={{0,1},{1,0},{2,3},{3,2},{4,5},{5,4},{6,7},{7,6},{8,9},{9,8},{10,11... | collective-permute-start | bytes 884744 | tf_op jit(solution)/shard_map/ppermute | solution.py:332
  1.5 6.8 %copy-start.1 = (bf16[2304,512]{1,0:T(8,128)(2,1)S(1)}, bf16[2304,512]{1,0:T(8,128)(2,1)}, u32[]{:S(2)}) copy-start(bf16[2304,512]{1,0:T(8,128)(2,1)} %refs_0_.2) | copy-start | bytes 7077892
  5.3 10.4 %collective-permute-start.1 = (f32[64,1024]{1,0:T(8,128)S(1)}, f32[64,1024]{1,0:T(8,128)S(1)}, u32[]{:S(2)}, u32[]{:S(2)}) collective-permute-start(f32[64,1024]{1,0:T(8,128)S(1)} %get-tuple-element.37.refs_1_), channel_id=1, source_target_pairs={{0,4},{2,6},{4,0},{6,2},{8,12},{10,14},{12,8},{14,10},{1,5},{3,7},... | collective-permute-start | bytes 786440 | tf_op jit(solution)/shard_map/ppermute | solution.py:335
  13.7 24.4 %copy-start.2 = (s32[8]{0:T(128)S(1)}, s32[8]{0:T(128)}, u32[]{:S(2)}) copy-start(s32[8]{0:T(128)} %param.13) | copy-start | bytes 100
  13.7 12.8 %collective-permute-start.7 = (f32[64,1280]{1,0:T(8,128)S(1)}, f32[64,1280]{1,0:T(8,128)S(1)}, u32[]{:S(2)}, u32[]{:S(2)}) collective-permute-start(f32[64,1280]{1,0:T(8,128)S(1)} %get-tuple-element.41), channel_id=1, source_target_pairs={{0,2},{2,0},{4,6},{6,4},{8,10},{10,8},{12,14},{14,12},{1,3},{3,1},... | collective-permute-start | bytes 983048 | tf_op jit(solution)/shard_map/ppermute | solution.py:335
  15.3 10.6 %collective-permute-start.4 = (f32[64,1024]{1,0:T(8,128)S(1)}, f32[64,1024]{1,0:T(8,128)S(1)}, u32[]{:S(2)}, u32[]{:S(2)}) collective-permute-start(f32[64,1024]{1,0:T(8,128)S(1)} %get-tuple-element.39), channel_id=1, source_target_pairs={{0,4},{2,6},{4,0},{6,2},{8,12},{10,14},{12,8},{14,10},{1,5},{3,7},... | collective-permute-start | bytes 786440 | tf_op jit(solution)/shard_map/ppermute | solution.py:335
  15.8 10.9 %collective-permute-start.2 = (f32[32,1024]{1,0:T(8,128)S(1)}, f32[32,1024]{1,0:T(8,128)S(1)}, u32[]{:S(2)}, u32[]{:S(2)}) collective-permute-start(f32[32,1024]{1,0:T(8,128)S(1)} %slice.57), channel_id=1, source_target_pairs={{0,8},{2,10},{4,12},{6,14},{8,0},{10,2},{12,4},{14,6},{1,9},{3,11}... | collective-permute-start | bytes 393224 | tf_op jit(solution)/shard_map/ppermute | solution.py:335
  18.4 20.9 %copy-start = (bf16[8,1024,256]{2,1,0:T(8,128)(2,1)S(1)}, bf16[8,1024,256]{2,1,0:T(8,128)(2,1)}, u32[]{:S(2)}) copy-start(bf16[8,1024,256]{2,1,0:T(8,128)(2,1)} %refs_0_.3) | copy-start | bytes 12582916
  25.9 5.0 %collective-permute-start.5 = (f32[32,1024]{1,0:T(8,128)S(1)}, f32[32,1024]{1,0:T(8,128)S(1)}, u32[]{:S(2)}, u32[]{:S(2)}) collective-permute-start(f32[32,1024]{1,0:T(8,128)S(1)} %slice.61), channel_id=1, source_target_pairs={{0,2},{2,0},{4,6},{6,4},{8,10},{10,8},{12,14},{14,12},{1,3},{3,1},... | collective-permute-start | bytes 393224 | tf_op jit(solution)/shard_map/ppermute | solution.py:335
  26.6 5.9 %collective-permute-start.8 = (f32[32,1280]{1,0:T(8,128)S(1)}, f32[32,1280]{1,0:T(8,128)S(1)}, u32[]{:S(2)}, u32[]{:S(2)}) collective-permute-start(f32[32,1280]{1,0:T(8,128)S(1)} %slice.65), channel_id=1, source_target_pairs={{0,4},{2,6},{4,0},{6,2},{8,12},{10,14},{12,8},{14,10},{1,5},{3,7},... | collective-permute-start | bytes 491528 | tf_op jit(solution)/shard_map/ppermute | solution.py:335
  26.7 5.8 %collective-permute-start.3 = (f32[16,1024]{1,0:T(8,128)S(1)}, f32[16,1024]{1,0:T(8,128)S(1)}, u32[]{:S(2)}, u32[]{:S(2)}) collective-permute-start(f32[16,1024]{1,0:T(8,128)S(1)} %slice.59), channel_id=1, source_target_pairs={{0,2},{2,0},{4,6},{6,4},{8,10},{10,8},{12,14},{14,12},{1,3},{3,1},... | collective-permute-start | bytes 196616 | tf_op jit(solution)/shard_map/ppermute | solution.py:335
  31.0 5.7 %collective-permute-start.6 = (f32[16,1024]{1,0:T(8,128)S(1)}, f32[16,1024]{1,0:T(8,128)S(1)}, u32[]{:S(2)}, u32[]{:S(2)}) collective-permute-start(f32[16,1024]{1,0:T(8,128)S(1)} %slice.63), channel_id=1, source_target_pairs={{0,8},{2,10},{4,12},{6,14},{8,0},{10,2},{12,4},{14,6},{1,9},{3,11}... | collective-permute-start | bytes 196616 | tf_op jit(solution)/shard_map/ppermute | solution.py:335
  32.5 5.4 %collective-permute-start.9 = (f32[16,1280]{1,0:T(8,128)S(1)}, f32[16,1280]{1,0:T(8,128)S(1)}, u32[]{:S(2)}, u32[]{:S(2)}) collective-permute-start(f32[16,1280]{1,0:T(8,128)S(1)} %slice.67), channel_id=1, source_target_pairs={{0,8},{2,10},{4,12},{6,14},{8,0},{10,2},{12,4},{14,6},{1,9},{3,11}... | collective-permute-start | bytes 245768 | tf_op jit(solution)/shard_map/ppermute | solution.py:335
  38.0 1.3 %collective-permute-start.10 = (bf16[8,3328]{1,0:T(8,128)(2,1)S(1)}, bf16[8,3328]{1,0:T(8,128)(2,1)S(1)}, u32[]{:S(2)}, u32[]{:S(2)}) collective-permute-start(bf16[8,3328]{1,0:T(8,128)(2,1)S(1)} %get-tuple-element.67), channel_id=1, source_target_pairs={{0,1},{1,0},{2,3},{3,2},{4,5},{5,4},{6,7},{7,6},{8,9},{9,8},{10,11... | collective-permute-start | bytes 159752 | tf_op jit(solution)/shard_map/ppermute | solution.py:332
  43.6 1.3 %collective-permute-start.11 = (bf16[8,3072]{1,0:T(8,128)(2,1)S(1)}, bf16[8,3072]{1,0:T(8,128)(2,1)S(1)}, u32[]{:S(2)}, u32[]{:S(2)}) collective-permute-start(bf16[8,3072]{1,0:T(8,128)(2,1)S(1)} %get-tuple-element.43), channel_id=1, source_target_pairs={{0,1},{1,0},{2,3},{3,2},{4,5},{5,4},{6,7},{7,6},{8,9},{9,8},{10,11... | collective-permute-start | bytes 147464 | tf_op jit(solution)/shard_map/ppermute | solution.py:332
  44.9 4.5 %collective-permute-start.14 = (bf16[16,1536]{1,0:T(8,128)(2,1)S(1)}, bf16[16,1536]{1,0:T(8,128)(2,1)S(1)}, u32[]{:S(2)}, u32[]{:S(2)}) collective-permute-start(bf16[16,1536]{1,0:T(8,128)(2,1)S(1)} %get-tuple-element.69), channel_id=1, source_target_pairs={{0,2},{2,0},{4,6},{6,4},{8,10},{10,8},{12,14},{14,12},{1,3},{3,1},... | collective-permute-start | bytes 147464 | tf_op jit(solution)/shard_map/ppermute | solution.py:335
  47.4 5.6 %collective-permute-start.12 = (bf16[16,1536]{1,0:T(8,128)(2,1)S(1)}, bf16[16,1536]{1,0:T(8,128)(2,1)S(1)}, u32[]{:S(2)}, u32[]{:S(2)}) collective-permute-start(bf16[16,1536]{1,0:T(8,128)(2,1)S(1)} %get-tuple-element.70), channel_id=1, source_target_pairs={{0,8},{2,10},{4,12},{6,14},{8,0},{10,2},{12,4},{14,6},{1,9},{3,11}... | collective-permute-start | bytes 147464 | tf_op jit(solution)/shard_map/ppermute | solution.py:335
  49.5 7.6 %collective-permute-start.16 = (bf16[32,1536]{1,0:T(8,128)(2,1)S(1)}, bf16[32,1536]{1,0:T(8,128)(2,1)S(1)}, u32[]{:S(2)}, u32[]{:S(2)}) collective-permute-start(bf16[32,1536]{1,0:T(8,128)(2,1)S(1)} %pad_maximum_fusion.4.refs_1_), channel_id=1, source_target_pairs={{0,8},{2,10},{4,12},{6,14},{8,0},{10,2},{12,4},{14,6},{1,9},{3,11}... | collective-permute-start | bytes 294920 | tf_op jit(solution)/shard_map/ppermute | solution.py:335
  53.0 5.4 %collective-permute-start.13 = (bf16[32,1536]{1,0:T(8,128)(2,1)S(1)}, bf16[32,1536]{1,0:T(8,128)(2,1)S(1)}, u32[]{:S(2)}, u32[]{:S(2)}) collective-permute-start(bf16[32,1536]{1,0:T(8,128)(2,1)S(1)} %pad_maximum_fusion.3.refs_0_), channel_id=1, source_target_pairs={{0,4},{2,6},{4,0},{6,2},{8,12},{10,14},{12,8},{14,10},{1,5},{3,7},... | collective-permute-start | bytes 294920 | tf_op jit(solution)/shard_map/ppermute | solution.py:335
  57.0 6.3 %collective-permute-start.17 = (bf16[64,1536]{1,0:T(8,128)(2,1)S(1)}, bf16[64,1536]{1,0:T(8,128)(2,1)S(1)}, u32[]{:S(2)}, u32[]{:S(2)}) collective-permute-start(bf16[64,1536]{1,0:T(8,128)(2,1)S(1)} %pad_maximum_fusion.2.refs_1_.refs_2_), channel_id=1, source_target_pairs={{0,4},{2,6},{4,0},{6,2},{8,12},{10,14},{12,8},{14,10},{1,5},{3,7},... | collective-permute-start | bytes 589832 | tf_op jit(solution)/shard_map/ppermute | solution.py:335
  58.4 6.2 %collective-permute-start.15 = (bf16[64,1536]{1,0:T(8,128)(2,1)S(1)}, bf16[64,1536]{1,0:T(8,128)(2,1)S(1)}, u32[]{:S(2)}, u32[]{:S(2)}) collective-permute-start(bf16[64,1536]{1,0:T(8,128)(2,1)S(1)} %maximum_add_fusion.refs_0_), channel_id=1, source_target_pairs={{0,2},{2,0},{4,6},{6,4},{8,10},{10,8},{12,14},{14,12},{1,3},{3,1},... | collective-permute-start | bytes 589832 | tf_op jit(solution)/shard_map/ppermute | solution.py:335
  68.0 1.5 %collective-permute-start.19 = (f32[64,768]{1,0:T(8,128)S(1)}, f32[64,768]{1,0:T(8,128)S(1)}, u32[]{:S(2)}, u32[]{:S(2)}) collective-permute-start(f32[64,768]{1,0:T(8,128)S(1)} %get-tuple-element.66), channel_id=1, source_target_pairs={{0,1},{1,0},{2,3},{3,2},{4,5},{5,4},{6,7},{7,6},{8,9},{9,8},{10,11... | collective-permute-start | bytes 589832 | tf_op jit(solution)/shard_map/ppermute | solution.py:332
  68.1 2.0 %collective-permute-start.18 = (f32[64,1536]{1,0:T(8,128)S(1)}, f32[64,1536]{1,0:T(8,128)S(1)}, u32[]{:S(2)}, u32[]{:S(2)}) collective-permute-start(f32[64,1536]{1,0:T(8,128)S(1)} %get-tuple-element.58.refs_10_), channel_id=1, source_target_pairs={{0,1},{1,0},{2,3},{3,2},{4,5},{5,4},{6,7},{7,6},{8,9},{9,8},{10,11... | collective-permute-start | bytes 1179656 | tf_op jit(solution)/shard_map/ppermute | solution.py:332

commit v14 on v13

--- a/solution.py
+++ b/solution.py
@@ -205,32 +205,31 @@
     for ref in (own_q, other_q):
         for column in range(0, ref.shape[1], DH):
             if column != kv_column:
-                q_scr[:, at, :] = ref[:, column : column + DH].astype(jnp.float32)
+                q_scr[:, at, :] = DH**-0.5 * ref[:, column : column + DH].astype(jnp.float32)
                 at += 1
     total_heads = at
     first = own_q[:, kv_column : kv_column + DH].astype(jnp.float32)
     second = other_q[:, kv_column : kv_column + DH].astype(jnp.float32)
     new_keys = jnp.where(core == 0, first, second)
     new_values = jnp.where(core == 0, second, first)
-    scale = DH**-0.5
     shares = []
     for row in range(rows):
         query = q_scr[row]
-        scores = scale * lax.dot_general(
+        scores = lax.dot_general(
             query.astype(jnp.bfloat16),
             k_ref[row],
             (((1,), (1,)), ((), ())),
             preferred_element_type=jnp.float32,
         )
-        self_score = scale * jnp.sum(query * new_keys[row : row + 1], axis=1, keepdims=True)
+        self_score = jnp.sum(query * new_keys[row : row + 1], axis=1, keepdims=True)
         visible = lax.broadcasted_iota(jnp.int32, scores.shape, 1) < scalars_ref[1 + row]
         masked = jnp.where(visible, scores, jnp.float32(-1e30))
         peak = jnp.maximum(jnp.max(masked, axis=1, keepdims=True), self_score)
-        raised = jnp.where(visible, jnp.exp(masked - peak), jnp.float32(0.0))
+        raised = jnp.exp(masked - peak)
         self_raised = jnp.exp(self_score - peak)
-        denominator = jnp.sum(raised, axis=1, keepdims=True) + self_raised
-        weights = (raised / denominator).astype(jnp.bfloat16)
-        self_weight = (self_raised / denominator).astype(jnp.bfloat16).astype(jnp.float32)
+        inverse = 1.0 / (jnp.sum(raised, axis=1, keepdims=True) + self_raised)
+        weights = (raised * inverse).astype(jnp.bfloat16)
+        self_weight = (self_raised * inverse).astype(jnp.bfloat16).astype(jnp.float32)
         shares.append((weights, self_weight))
     for copy in copies:
         copy.wait()
@@ -389,15 +388,8 @@
             far[i] = across(near[i], paths[i][step])
     orders = [order_of(path[::-1]) for path in paths]
     blocks = [b for pair in zip(near, far) for b in pair]
-    total_columns = out_weight.shape[1]
-    last = 768 if total_columns % 768 == 0 and total_columns > 768 else 0
-    results, after = [], []
-    for columns in ((0, total_columns - last), (total_columns - last, last)):
-        if columns[1]:
-            send, keep = project_out(orders, rows, ids, blocks, out_held, out_cuts, columns, after)
-            after = [send]
-            results.append((keep + swap(send)).astype(jnp.bfloat16))
-    return jnp.concatenate(results, axis=1)
+    send, keep = project_out(orders, rows, ids, blocks, out_held, out_cuts, (0, out_weight.shape[1]), [])
+    return (keep + swap(send)).astype(jnp.bfloat16)
 
 
 def solution(mesh):

time: 71 us -> 70.3 us (level)
  Pallas kernels: 23.3 us -> 22.5 us
    pallas_call x2 -> x1, Pallas kernels: 3.39 us -> 2.64 us  [project_out(): pl.pallas_call(functools.partial(output_kernel, orders, rows, columns, pi...]
    concatenate x1 -> x0, other arithmetic: 0.73 us -> none  [local(): return jnp.concatenate(results, axis=1)]
    convert_element_type x2 -> x1, other arithmetic: 0.06 us -> 0.79 us  [local(): return (keep + swap(send)).astype(jnp.bfloat16)]
    ppermute x5 -> x4, waiting for transfers between devices: 4.03 us -> 4.55 us  [swap(): return lax.ppermute(array, 'gy', [(0, 1), (1, 0)])]
  transfers between devices with their start and end apart: 20 -> 19, of which waited for: 14 -> 13; matrix products, arithmetic and copies ran while one was open for 2% -> 2% of each run, Pallas kernels for 17% -> 17%
where the time goes in v14:
time: 70.3 us; the launch traced here: 70.1 us
  waiting for transfers between devices  23.9 us (34%)
  Pallas kernels  22.5 us (32%)
  starting transfers between devices  21.1 us (30%)
  other arithmetic  2.26 us (3%)
    ppermute x15, starting transfers between devices, across(): return lax.ppermute(array, 'gx', [(g, g ^ mask) for g in range(n)])  20.3 us
    ppermute x15, waiting for transfers between devices, across(): return lax.ppermute(array, 'gx', [(g, g ^ mask) for g in range(n)])  19.3 us
    pallas_call x2, Pallas kernels, project(): pl.pallas_call(functools.partial(project_kernel, orders, rows, first, wid...  8.76 us
    pallas_call x2, Pallas kernels, load(): pl.pallas_call(functools.partial(load_kernel, len(after), cuts, len(array...  6.84 us
    ppermute x4, waiting for transfers between devices, swap(): return lax.ppermute(array, 'gy', [(0, 1), (1, 0)])  4.55 us
    pallas_call x1, Pallas kernels, attend(): pl.pallas_call(functools.partial(attend_kernel, kv_column), out_shape=(ou...  4.28 us
    pallas_call x1, Pallas kernels, project_out(): pl.pallas_call(functools.partial(output_kernel, orders, rows, columns, pi...  2.64 us
  transfers between devices with their start and end apart: 19, of which 13 were waited for; matrix products, arithmetic and copies ran while one was open for 2% of the time, Pallas kernels for 17%

profile of v14, /device:TPU:0, one launch (start us, length us, event | category | flops | bytes accessed | tf_op | source)
XLA Modules:
  0.0 70.1 jit_solution(17895989057950489561)
XLA Ops:
  0.5 1.0 %broadcast_select_fusion.own_ref = bf16[64,2304]{1,0:T(8,128)(2,1)S(1)} fusion(bf16[64,2304]{1,0:T(8,128)(2,1)} %param.7, pred[]{:T(512)S(6)} %lt.9), kind=kLoop, calls=%fused_computation.1 | loop fusion | flops 147456 | bytes 589825 | tf_op jit(solution)/shard_map/jit(_where)/select_n | solution.py:337
  1.9 3.4 %project.2 = (f32[64,1024]{1,0:T(8,128)S(1)}, f32[64,1024]{1,0:T(8,128)S(1)}) custom-call(s32[2]{0:T(128)S(1)} %pad_add_fusion.ids_ref, bf16[64,2304]{1,0:T(8,128)(2,1)S(1)} %broadcast_select_fusion.own_ref, bf16[64,2304]{1,0:T(8,128)(2,1)S(1)} %collective-permute-done.other_ref, bf16[2304,3072]{1,0:T(8,128)(2,1)} %w_ref.3), custom_call_target="tpu_custom_call" | custom-call | flops 603979776 | bytes 5242880 | tf_op jit(solution)/shard_map/project/pallas_call | solution.py:176
  5.3 3.0 %collective-permute-start.1 = (f32[64,1024]{1,0:T(8,128)S(1)}, f32[64,1024]{1,0:T(8,128)S(1)}, u32[]{:S(2)}, u32[]{:S(2)}) collective-permute-start(f32[64,1024]{1,0:T(8,128)S(1)} %get-tuple-element.35.refs_1_), channel_id=1, source_target_pairs={{0,4},{2,6},{4,0},{6,2},{8,12},{10,14},{12,8},{14,10},{1,5},{3,7},... | collective-permute-start | bytes 786440 | tf_op jit(solution)/shard_map/ppermute | solution.py:334
  8.3 5.3 %project.3 = (f32[64,1024]{1,0:T(8,128)S(1)}, f32[64,1024]{1,0:T(8,128)S(1)}, f32[64,1280]{1,0:T(8,128)S(1)}, f32[64,1280]{1,0:T(8,128)S(1)}) custom-call(s32[2]{0:T(128)S(1)} %pad_add_fusion.ids_ref, bf16[64,2304]{1,0:T(8,128)(2,1)S(1)} %broadcast_select_fusion.own_ref, bf16[64,2304]{1,0:T(8,128)(2,1)S(1)} %collective-permute-done.other_ref, ...), custom_call_target="tpu_custom_call" | custom-call | flops 1358954496 | bytes 11796480 | tf_op jit(solution)/shard_map/project/pallas_call | solution.py:176
  13.7 1.6 %collective-permute-start.7 = (f32[64,1280]{1,0:T(8,128)S(1)}, f32[64,1280]{1,0:T(8,128)S(1)}, u32[]{:S(2)}, u32[]{:S(2)}) collective-permute-start(f32[64,1280]{1,0:T(8,128)S(1)} %get-tuple-element.39), channel_id=1, source_target_pairs={{0,2},{2,0},{4,6},{6,4},{8,10},{10,8},{12,14},{14,12},{1,3},{3,1},... | collective-permute-start | bytes 983048 | tf_op jit(solution)/shard_map/ppermute | solution.py:334
  15.3 0.5 collective-permute-start.4
  15.8 2.6 %collective-permute-start.2 = (f32[32,1024]{1,0:T(8,128)S(1)}, f32[32,1024]{1,0:T(8,128)S(1)}, u32[]{:S(2)}, u32[]{:S(2)}) collective-permute-start(f32[32,1024]{1,0:T(8,128)S(1)} %slice.57), channel_id=1, source_target_pairs={{0,8},{2,10},{4,12},{6,14},{8,0},{10,2},{12,4},{14,6},{1,9},{3,11}... | collective-permute-start | bytes 393224 | tf_op jit(solution)/shard_map/ppermute | solution.py:334
  18.4 7.4 %collective-permute-done.4 = f32[64,1024]{1,0:T(8,128)S(1)} collective-permute-done((f32[64,1024]{1,0:T(8,128)S(1)}, f32[64,1024]{1,0:T(8,128)S(1)}, u32[]{:S(2)}, u32[]{:S(2)}) %collective-permute-start.4) | collective-permute-done | bytes 262176 | tf_op jit(solution)/shard_map/ppermute | solution.py:334
  25.9 0.6 collective-permute-start.5
  26.7 1.6 %collective-permute-start.3 = (f32[16,1024]{1,0:T(8,128)S(1)}, f32[16,1024]{1,0:T(8,128)S(1)}, u32[]{:S(2)}, u32[]{:S(2)}) collective-permute-start(f32[16,1024]{1,0:T(8,128)S(1)} %slice.59), channel_id=1, source_target_pairs={{0,2},{2,0},{4,6},{6,4},{8,10},{10,8},{12,14},{14,12},{1,3},{3,1},... | collective-permute-start | bytes 196616 | tf_op jit(solution)/shard_map/ppermute | solution.py:334
  28.3 2.7 %collective-permute-done.5 = f32[32,1024]{1,0:T(8,128)S(1)} collective-permute-done((f32[32,1024]{1,0:T(8,128)S(1)}, f32[32,1024]{1,0:T(8,128)S(1)}, u32[]{:S(2)}, u32[]{:S(2)}) %collective-permute-start.5) | collective-permute-done | bytes 131104 | tf_op jit(solution)/shard_map/ppermute | solution.py:334
  31.0 1.5 %collective-permute-start.6 = (f32[16,1024]{1,0:T(8,128)S(1)}, f32[16,1024]{1,0:T(8,128)S(1)}, u32[]{:S(2)}, u32[]{:S(2)}) collective-permute-start(f32[16,1024]{1,0:T(8,128)S(1)} %slice.63), channel_id=1, source_target_pairs={{0,8},{2,10},{4,12},{6,14},{8,0},{10,2},{12,4},{14,6},{1,9},{3,11}... | collective-permute-start | bytes 196616 | tf_op jit(solution)/shard_map/ppermute | solution.py:334
  32.5 1.6 %collective-permute-start.9 = (f32[16,1280]{1,0:T(8,128)S(1)}, f32[16,1280]{1,0:T(8,128)S(1)}, u32[]{:S(2)}, u32[]{:S(2)}) collective-permute-start(f32[16,1280]{1,0:T(8,128)S(1)} %slice.67), channel_id=1, source_target_pairs={{0,8},{2,10},{4,12},{6,14},{8,0},{10,2},{12,4},{14,6},{1,9},{3,11}... | collective-permute-start | bytes 245768 | tf_op jit(solution)/shard_map/ppermute | solution.py:334
  34.1 2.6 %collective-permute-done.6 = f32[16,1024]{1,0:T(8,128)S(1)} collective-permute-done((f32[16,1024]{1,0:T(8,128)S(1)}, f32[16,1024]{1,0:T(8,128)S(1)}, u32[]{:S(2)}, u32[]{:S(2)}) %collective-permute-start.6) | collective-permute-done | bytes 65568 | tf_op jit(solution)/shard_map/ppermute | solution.py:334
  36.7 1.3 %collective-permute-done.9 = f32[16,1280]{1,0:T(8,128)S(1)} collective-permute-done((f32[16,1280]{1,0:T(8,128)S(1)}, f32[16,1280]{1,0:T(8,128)S(1)}, u32[]{:S(2)}, u32[]{:S(2)}) %collective-permute-start.9) | collective-permute-done | bytes 81952 | tf_op jit(solution)/shard_map/ppermute | solution.py:334
  38.2 1.1 %collective-permute-done.10.other_q = bf16[8,3328]{1,0:T(8,128)(2,1)S(1)} collective-permute-done((bf16[8,3328]{1,0:T(8,128)(2,1)S(1)}, bf16[8,3328]{1,0:T(8,128)(2,1)S(1)}, u32[]{:S(2)}, u32[]{:S(2)}) %collective-permute-start.10) | collective-permute-done | bytes 53280 | tf_op jit(solution)/shard_map/ppermute | solution.py:331
  39.3 4.3 %attend.1 = (bf16[8,3072]{1,0:T(8,128)(2,1)S(1)}, bf16[8,3072]{1,0:T(8,128)(2,1)S(1)}) custom-call(s32[9]{0:T(128)S(1)} %pad_add_fusion.1.scalars_ref, bf16[8,3328]{1,0:T(8,128)(2,1)S(1)} %get-tuple-element.64.own_q, bf16[8,3328]{1,0:T(8,128)(2,1)S(1)} %collective-permute-done.10.other_q, bf16[8,1024,256]{2,1,0:T(8,128)(2,1)S(1)} %copy-done, ...), custom_call_target="tpu_custom_call" | custom-call | flops 201326592 | bytes 8388608 | tf_op jit(solution)/shard_map/attend/pallas_call | solution.py:251
  43.8 1.1 %collective-permute-done.11 = bf16[8,3072]{1,0:T(8,128)(2,1)S(1)} collective-permute-done((bf16[8,3072]{1,0:T(8,128)(2,1)S(1)}, bf16[8,3072]{1,0:T(8,128)(2,1)S(1)}, u32[]{:S(2)}, u32[]{:S(2)}) %collective-permute-start.11) | collective-permute-done | bytes 49184 | tf_op jit(solution)/shard_map/ppermute | solution.py:331
  44.9 2.4 %collective-permute-start.14 = (bf16[16,1536]{1,0:T(8,128)(2,1)S(1)}, bf16[16,1536]{1,0:T(8,128)(2,1)S(1)}, u32[]{:S(2)}, u32[]{:S(2)}) collective-permute-start(bf16[16,1536]{1,0:T(8,128)(2,1)S(1)} %get-tuple-element.65), channel_id=1, source_target_pairs={{0,2},{2,0},{4,6},{6,4},{8,10},{10,8},{12,14},{14,12},{1,3},{3,1},... | collective-permute-start | bytes 147464 | tf_op jit(solution)/shard_map/ppermute | solution.py:334
  47.4 0.8 %collective-permute-start.12 = (bf16[16,1536]{1,0:T(8,128)(2,1)S(1)}, bf16[16,1536]{1,0:T(8,128)(2,1)S(1)}, u32[]{:S(2)}, u32[]{:S(2)}) collective-permute-start(bf16[16,1536]{1,0:T(8,128)(2,1)S(1)} %get-tuple-element.66), channel_id=1, source_target_pairs={{0,8},{2,10},{4,12},{6,14},{8,0},{10,2},{12,4},{14,6},{1,9},{3,11}... | collective-permute-start | bytes 147464 | tf_op jit(solution)/shard_map/ppermute | solution.py:334
  48.2 1.3 %collective-permute-done.14 = bf16[16,1536]{1,0:T(8,128)(2,1)S(1)} collective-permute-done((bf16[16,1536]{1,0:T(8,128)(2,1)S(1)}, bf16[16,1536]{1,0:T(8,128)(2,1)S(1)}, u32[]{:S(2)}, u32[]{:S(2)}) %collective-permute-start.14) | collective-permute-done | bytes 49184 | tf_op jit(solution)/shard_map/ppermute | solution.py:334
  49.5 1.3 %collective-permute-start.16 = (bf16[32,1536]{1,0:T(8,128)(2,1)S(1)}, bf16[32,1536]{1,0:T(8,128)(2,1)S(1)}, u32[]{:S(2)}, u32[]{:S(2)}) collective-permute-start(bf16[32,1536]{1,0:T(8,128)(2,1)S(1)} %pad_maximum_fusion.3.refs_1_), channel_id=1, source_target_pairs={{0,8},{2,10},{4,12},{6,14},{8,0},{10,2},{12,4},{14,6},{1,9},{3,11}... | collective-permute-start | bytes 294920 | tf_op jit(solution)/shard_map/ppermute | solution.py:334
  50.8 2.2 %collective-permute-done.12 = bf16[16,1536]{1,0:T(8,128)(2,1)S(1)} collective-permute-done((bf16[16,1536]{1,0:T(8,128)(2,1)S(1)}, bf16[16,1536]{1,0:T(8,128)(2,1)S(1)}, u32[]{:S(2)}, u32[]{:S(2)}) %collective-permute-start.12) | collective-permute-done | bytes 49184 | tf_op jit(solution)/shard_map/ppermute | solution.py:334
  53.0 0.6 collective-permute-start.13
  53.5 3.1 %load.2 = (bf16[512,768]{1,0:T(8,128)(2,1)S(1)}, bf16[512,768]{1,0:T(8,128)(2,1)S(1)}, bf16[512,768]{1,0:T(8,128)(2,1)S(1)}, bf16[512,768]{1,0:T(8,128)(2,1)S(1)...) custom-call(bf16[32,1536]{1,0:T(8,128)(2,1)S(1)} %pad_maximum_fusion, ...), custom_call_target="tpu_custom_call" | custom-call | bytes 14155776 | tf_op jit(solution)/shard_map/load/pallas_call | solution.py:78
  57.0 1.3 %collective-permute-start.17 = (bf16[64,1536]{1,0:T(8,128)(2,1)S(1)}, bf16[64,1536]{1,0:T(8,128)(2,1)S(1)}, u32[]{:S(2)}, u32[]{:S(2)}) collective-permute-start(bf16[64,1536]{1,0:T(8,128)(2,1)S(1)} %pad_maximum_fusion.1.refs_1_.refs_2_), channel_id=1, source_target_pairs={{0,4},{2,6},{4,0},{6,2},{8,12},{10,14},{12,8},{14,10},{1,5},{3,7},... | collective-permute-start | bytes 589832 | tf_op jit(solution)/shard_map/ppermute | solution.py:334
  58.4 0.9 %collective-permute-start.15 = (bf16[64,1536]{1,0:T(8,128)(2,1)S(1)}, bf16[64,1536]{1,0:T(8,128)(2,1)S(1)}, u32[]{:S(2)}, u32[]{:S(2)}) collective-permute-start(bf16[64,1536]{1,0:T(8,128)(2,1)S(1)} %maximum_add_fusion.refs_0_), channel_id=1, source_target_pairs={{0,2},{2,0},{4,6},{6,4},{8,10},{10,8},{12,14},{14,12},{1,3},{3,1},... | collective-permute-start | bytes 589832 | tf_op jit(solution)/shard_map/ppermute | solution.py:334
  59.3 3.7 %load.3 = (bf16[512,768]{1,0:T(8,128)(2,1)S(1)}, bf16[512,768]{1,0:T(8,128)(2,1)S(1)}, bf16[512,768]{1,0:T(8,128)(2,1)S(1)}, bf16[512,768]{1,0:T(8,128)(2,1)S(1)...) custom-call(bf16[64,1536]{1,0:T(8,128)(2,1)S(1)} %maximum_add_fusion, ...), custom_call_target="tpu_custom_call" | custom-call | bytes 14155776 | tf_op jit(solution)/shard_map/load/pallas_call | solution.py:78
  63.3 1.2 %collective-permute-done.15.refs_1_ = bf16[64,1536]{1,0:T(8,128)(2,1)S(1)} collective-permute-done((bf16[64,1536]{1,0:T(8,128)(2,1)S(1)}, bf16[64,1536]{1,0:T(8,128)(2,1)S(1)}, u32[]{:S(2)}, u32[]{:S(2)}) %collective-permute-start.15) | collective-permute-done | bytes 196640 | tf_op jit(solution)/shard_map/ppermute | solution.py:334
  64.6 2.6 %project_out.1 = (f32[64,2304]{1,0:T(8,128)S(1)}, f32[64,2304]{1,0:T(8,128)S(1)}) custom-call(s32[2]{0:T(128)S(1)} %pad_add_fusion.ids_ref, bf16[64,1536]{1,0:T(8,128)(2,1)S(1)} %maximum_add_fusion.refs_0_, bf16[64,1536]{1,0:T(8,128)(2,1)S(1)} %collective-permute-done.15.refs_1_, bf16[64,1536]{1,0:T(8,128)(2,1)S(1)} %pad_maximum_fusion.1.refs_1_.refs_2_, ...), custom_call_target="tpu_custom_call" | custom-call | flops 1811939328 | bytes 15335424 | tf_op jit(solution)/shard_map/project_out/pallas_call | solution.py:305
  67.3 2.0 %collective-permute-done.18 = f32[64,2304]{1,0:T(8,128)S(1)} collective-permute-done((f32[64,2304]{1,0:T(8,128)S(1)}, f32[64,2304]{1,0:T(8,128)S(1)}, u32[]{:S(2)}, u32[]{:S(2)}) %collective-permute-start.18) | collective-permute-done | bytes 589856 | tf_op jit(solution)/shard_map/ppermute | solution.py:331
  69.3 0.8 %add_convert_fusion = bf16[64,2304]{1,0:T(8,128)(2,1)} fusion(f32[64,2304]{1,0:T(8,128)S(1)} %get-tuple-element.61, f32[64,2304]{1,0:T(8,128)S(1)} %collective-permute-done.18), kind=kLoop, calls=%fused_computation | loop fusion | flops 294912 | bytes 1474560 | tf_op jit(solution)/shard_map/convert_element_type | solution.py:392
  (46 shorter events, 2.5 us)
Async XLA Ops:
  0.0 1.9 %collective-permute-start = (bf16[64,2304]{1,0:T(8,128)(2,1)}, bf16[64,2304]{1,0:T(8,128)(2,1)S(1)}, u32[]{:S(2)}, u32[]{:S(2)}) collective-permute-start(bf16[64,2304]{1,0:T(8,128)(2,1)} %param.7), channel_id=1, source_target_pairs={{0,1},{1,0},{2,3},{3,2},{4,5},{5,4},{6,7},{7,6},{8,9},{9,8},{10,11... | collective-permute-start | bytes 884744 | tf_op jit(solution)/shard_map/ppermute | solution.py:331
  1.5 6.8 %copy-start.1 = (bf16[2304,512]{1,0:T(8,128)(2,1)S(1)}, bf16[2304,512]{1,0:T(8,128)(2,1)}, u32[]{:S(2)}) copy-start(bf16[2304,512]{1,0:T(8,128)(2,1)} %refs_0_.2) | copy-start | bytes 7077892
  5.3 10.4 %collective-permute-start.1 = (f32[64,1024]{1,0:T(8,128)S(1)}, f32[64,1024]{1,0:T(8,128)S(1)}, u32[]{:S(2)}, u32[]{:S(2)}) collective-permute-start(f32[64,1024]{1,0:T(8,128)S(1)} %get-tuple-element.35.refs_1_), channel_id=1, source_target_pairs={{0,4},{2,6},{4,0},{6,2},{8,12},{10,14},{12,8},{14,10},{1,5},{3,7},... | collective-permute-start | bytes 786440 | tf_op jit(solution)/shard_map/ppermute | solution.py:334
  13.7 24.4 %copy-start.2 = (s32[8]{0:T(128)S(1)}, s32[8]{0:T(128)}, u32[]{:S(2)}) copy-start(s32[8]{0:T(128)} %param.13) | copy-start | bytes 100
  13.7 12.8 %collective-permute-start.7 = (f32[64,1280]{1,0:T(8,128)S(1)}, f32[64,1280]{1,0:T(8,128)S(1)}, u32[]{:S(2)}, u32[]{:S(2)}) collective-permute-start(f32[64,1280]{1,0:T(8,128)S(1)} %get-tuple-element.39), channel_id=1, source_target_pairs={{0,2},{2,0},{4,6},{6,4},{8,10},{10,8},{12,14},{14,12},{1,3},{3,1},... | collective-permute-start | bytes 983048 | tf_op jit(solution)/shard_map/ppermute | solution.py:334
  15.3 10.6 %collective-permute-start.4 = (f32[64,1024]{1,0:T(8,128)S(1)}, f32[64,1024]{1,0:T(8,128)S(1)}, u32[]{:S(2)}, u32[]{:S(2)}) collective-permute-start(f32[64,1024]{1,0:T(8,128)S(1)} %get-tuple-element.37), channel_id=1, source_target_pairs={{0,4},{2,6},{4,0},{6,2},{8,12},{10,14},{12,8},{14,10},{1,5},{3,7},... | collective-permute-start | bytes 786440 | tf_op jit(solution)/shard_map/ppermute | solution.py:334
  15.8 10.9 %collective-permute-start.2 = (f32[32,1024]{1,0:T(8,128)S(1)}, f32[32,1024]{1,0:T(8,128)S(1)}, u32[]{:S(2)}, u32[]{:S(2)}) collective-permute-start(f32[32,1024]{1,0:T(8,128)S(1)} %slice.57), channel_id=1, source_target_pairs={{0,8},{2,10},{4,12},{6,14},{8,0},{10,2},{12,4},{14,6},{1,9},{3,11}... | collective-permute-start | bytes 393224 | tf_op jit(solution)/shard_map/ppermute | solution.py:334
  18.4 20.9 %copy-start = (bf16[8,1024,256]{2,1,0:T(8,128)(2,1)S(1)}, bf16[8,1024,256]{2,1,0:T(8,128)(2,1)}, u32[]{:S(2)}) copy-start(bf16[8,1024,256]{2,1,0:T(8,128)(2,1)} %refs_0_.3) | copy-start | bytes 12582916
  25.9 5.0 %collective-permute-start.5 = (f32[32,1024]{1,0:T(8,128)S(1)}, f32[32,1024]{1,0:T(8,128)S(1)}, u32[]{:S(2)}, u32[]{:S(2)}) collective-permute-start(f32[32,1024]{1,0:T(8,128)S(1)} %slice.61), channel_id=1, source_target_pairs={{0,2},{2,0},{4,6},{6,4},{8,10},{10,8},{12,14},{14,12},{1,3},{3,1},... | collective-permute-start | bytes 393224 | tf_op jit(solution)/shard_map/ppermute | solution.py:334
  26.6 5.9 %collective-permute-start.8 = (f32[32,1280]{1,0:T(8,128)S(1)}, f32[32,1280]{1,0:T(8,128)S(1)}, u32[]{:S(2)}, u32[]{:S(2)}) collective-permute-start(f32[32,1280]{1,0:T(8,128)S(1)} %slice.65), channel_id=1, source_target_pairs={{0,4},{2,6},{4,0},{6,2},{8,12},{10,14},{12,8},{14,10},{1,5},{3,7},... | collective-permute-start | bytes 491528 | tf_op jit(solution)/shard_map/ppermute | solution.py:334
  26.7 5.8 %collective-permute-start.3 = (f32[16,1024]{1,0:T(8,128)S(1)}, f32[16,1024]{1,0:T(8,128)S(1)}, u32[]{:S(2)}, u32[]{:S(2)}) collective-permute-start(f32[16,1024]{1,0:T(8,128)S(1)} %slice.59), channel_id=1, source_target_pairs={{0,2},{2,0},{4,6},{6,4},{8,10},{10,8},{12,14},{14,12},{1,3},{3,1},... | collective-permute-start | bytes 196616 | tf_op jit(solution)/shard_map/ppermute | solution.py:334
  31.0 5.7 %collective-permute-start.6 = (f32[16,1024]{1,0:T(8,128)S(1)}, f32[16,1024]{1,0:T(8,128)S(1)}, u32[]{:S(2)}, u32[]{:S(2)}) collective-permute-start(f32[16,1024]{1,0:T(8,128)S(1)} %slice.63), channel_id=1, source_target_pairs={{0,8},{2,10},{4,12},{6,14},{8,0},{10,2},{12,4},{14,6},{1,9},{3,11}... | collective-permute-start | bytes 196616 | tf_op jit(solution)/shard_map/ppermute | solution.py:334
  32.5 5.4 %collective-permute-start.9 = (f32[16,1280]{1,0:T(8,128)S(1)}, f32[16,1280]{1,0:T(8,128)S(1)}, u32[]{:S(2)}, u32[]{:S(2)}) collective-permute-start(f32[16,1280]{1,0:T(8,128)S(1)} %slice.67), channel_id=1, source_target_pairs={{0,8},{2,10},{4,12},{6,14},{8,0},{10,2},{12,4},{14,6},{1,9},{3,11}... | collective-permute-start | bytes 245768 | tf_op jit(solution)/shard_map/ppermute | solution.py:334
  38.0 1.3 %collective-permute-start.10 = (bf16[8,3328]{1,0:T(8,128)(2,1)S(1)}, bf16[8,3328]{1,0:T(8,128)(2,1)S(1)}, u32[]{:S(2)}, u32[]{:S(2)}) collective-permute-start(bf16[8,3328]{1,0:T(8,128)(2,1)S(1)} %get-tuple-element.63), channel_id=1, source_target_pairs={{0,1},{1,0},{2,3},{3,2},{4,5},{5,4},{6,7},{7,6},{8,9},{9,8},{10,11... | collective-permute-start | bytes 159752 | tf_op jit(solution)/shard_map/ppermute | solution.py:331
  43.6 1.3 %collective-permute-start.11 = (bf16[8,3072]{1,0:T(8,128)(2,1)S(1)}, bf16[8,3072]{1,0:T(8,128)(2,1)S(1)}, u32[]{:S(2)}, u32[]{:S(2)}) collective-permute-start(bf16[8,3072]{1,0:T(8,128)(2,1)S(1)} %get-tuple-element.41), channel_id=1, source_target_pairs={{0,1},{1,0},{2,3},{3,2},{4,5},{5,4},{6,7},{7,6},{8,9},{9,8},{10,11... | collective-permute-start | bytes 147464 | tf_op jit(solution)/shard_map/ppermute | solution.py:331
  44.9 4.5 %collective-permute-start.14 = (bf16[16,1536]{1,0:T(8,128)(2,1)S(1)}, bf16[16,1536]{1,0:T(8,128)(2,1)S(1)}, u32[]{:S(2)}, u32[]{:S(2)}) collective-permute-start(bf16[16,1536]{1,0:T(8,128)(2,1)S(1)} %get-tuple-element.65), channel_id=1, source_target_pairs={{0,2},{2,0},{4,6},{6,4},{8,10},{10,8},{12,14},{14,12},{1,3},{3,1},... | collective-permute-start | bytes 147464 | tf_op jit(solution)/shard_map/ppermute | solution.py:334
  47.4 5.6 %collective-permute-start.12 = (bf16[16,1536]{1,0:T(8,128)(2,1)S(1)}, bf16[16,1536]{1,0:T(8,128)(2,1)S(1)}, u32[]{:S(2)}, u32[]{:S(2)}) collective-permute-start(bf16[16,1536]{1,0:T(8,128)(2,1)S(1)} %get-tuple-element.66), channel_id=1, source_target_pairs={{0,8},{2,10},{4,12},{6,14},{8,0},{10,2},{12,4},{14,6},{1,9},{3,11}... | collective-permute-start | bytes 147464 | tf_op jit(solution)/shard_map/ppermute | solution.py:334
  49.5 7.6 %collective-permute-start.16 = (bf16[32,1536]{1,0:T(8,128)(2,1)S(1)}, bf16[32,1536]{1,0:T(8,128)(2,1)S(1)}, u32[]{:S(2)}, u32[]{:S(2)}) collective-permute-start(bf16[32,1536]{1,0:T(8,128)(2,1)S(1)} %pad_maximum_fusion.3.refs_1_), channel_id=1, source_target_pairs={{0,8},{2,10},{4,12},{6,14},{8,0},{10,2},{12,4},{14,6},{1,9},{3,11}... | collective-permute-start | bytes 294920 | tf_op jit(solution)/shard_map/ppermute | solution.py:334
  53.0 5.4 %collective-permute-start.13 = (bf16[32,1536]{1,0:T(8,128)(2,1)S(1)}, bf16[32,1536]{1,0:T(8,128)(2,1)S(1)}, u32[]{:S(2)}, u32[]{:S(2)}) collective-permute-start(bf16[32,1536]{1,0:T(8,128)(2,1)S(1)} %pad_maximum_fusion.2.refs_0_), channel_id=1, source_target_pairs={{0,4},{2,6},{4,0},{6,2},{8,12},{10,14},{12,8},{14,10},{1,5},{3,7},... | collective-permute-start | bytes 294920 | tf_op jit(solution)/shard_map/ppermute | solution.py:334
  57.0 6.3 %collective-permute-start.17 = (bf16[64,1536]{1,0:T(8,128)(2,1)S(1)}, bf16[64,1536]{1,0:T(8,128)(2,1)S(1)}, u32[]{:S(2)}, u32[]{:S(2)}) collective-permute-start(bf16[64,1536]{1,0:T(8,128)(2,1)S(1)} %pad_maximum_fusion.1.refs_1_.refs_2_), channel_id=1, source_target_pairs={{0,4},{2,6},{4,0},{6,2},{8,12},{10,14},{12,8},{14,10},{1,5},{3,7},... | collective-permute-start | bytes 589832 | tf_op jit(solution)/shard_map/ppermute | solution.py:334
  58.4 6.2 %collective-permute-start.15 = (bf16[64,1536]{1,0:T(8,128)(2,1)S(1)}, bf16[64,1536]{1,0:T(8,128)(2,1)S(1)}, u32[]{:S(2)}, u32[]{:S(2)}) collective-permute-start(bf16[64,1536]{1,0:T(8,128)(2,1)S(1)} %maximum_add_fusion.refs_0_), channel_id=1, source_target_pairs={{0,2},{2,0},{4,6},{6,4},{8,10},{10,8},{12,14},{14,12},{1,3},{3,1},... | collective-permute-start | bytes 589832 | tf_op jit(solution)/shard_map/ppermute | solution.py:334
  67.2 2.1 %collective-permute-start.18 = (f32[64,2304]{1,0:T(8,128)S(1)}, f32[64,2304]{1,0:T(8,128)S(1)}, u32[]{:S(2)}, u32[]{:S(2)}) collective-permute-start(f32[64,2304]{1,0:T(8,128)S(1)} %get-tuple-element.62), channel_id=1, source_target_pairs={{0,1},{1,0},{2,3},{3,2},{4,5},{5,4},{6,7},{7,6},{8,9},{9,8},{10,11... | collective-permute-start | bytes 1769480 | tf_op jit(solution)/shard_map/ppermute | solution.py:331

commit v15 on v14

--- a/solution.py
+++ b/solution.py
@@ -195,7 +195,7 @@
 
 
 def attend_kernel(kv_column, scalars_ref, own_q, other_q, *refs):
-    k_ref, v_hbm, own_out, other_out, v_ref, q_scr, o_scr, sems = refs
+    k_ref, v_hbm, own_out, other_out, v_ref, q_scr, o_scr, s_scr, sems = refs
     core = scalars_ref[0]
     rows, positions, _ = k_ref.shape
     copies = [pltpu.make_async_copy(v_hbm.at[row], v_ref.at[row], sems.at[row]) for row in range(rows)]
@@ -212,7 +212,7 @@
     second = other_q[:, kv_column : kv_column + DH].astype(jnp.float32)
     new_keys = jnp.where(core == 0, first, second)
     new_values = jnp.where(core == 0, second, first)
-    shares = []
+    own_scores = []
     for row in range(rows):
         query = q_scr[row]
         scores = lax.dot_general(
@@ -221,21 +221,23 @@
             (((1,), (1,)), ((), ())),
             preferred_element_type=jnp.float32,
         )
-        self_score = jnp.sum(query * new_keys[row : row + 1], axis=1, keepdims=True)
         visible = lax.broadcasted_iota(jnp.int32, scores.shape, 1) < scalars_ref[1 + row]
-        masked = jnp.where(visible, scores, jnp.float32(-1e30))
-        peak = jnp.maximum(jnp.max(masked, axis=1, keepdims=True), self_score)
-        raised = jnp.exp(masked - peak)
-        self_raised = jnp.exp(self_score - peak)
-        inverse = 1.0 / (jnp.sum(raised, axis=1, keepdims=True) + self_raised)
-        weights = (raised * inverse).astype(jnp.bfloat16)
-        self_weight = (self_raised * inverse).astype(jnp.bfloat16).astype(jnp.float32)
-        shares.append((weights, self_weight))
+        s_scr[row] = jnp.where(visible, scores, jnp.float32(-1e30))
+        own_scores.append(jnp.sum(query * new_keys[row : row + 1], axis=1, keepdims=True))
+    self_score = jnp.stack(own_scores)
+    masked = s_scr[...]
+    peak = jnp.maximum(jnp.max(masked, axis=2, keepdims=True), self_score)
+    raised = jnp.exp(masked - peak)
+    self_raised = jnp.exp(self_score - peak)
+    inverse = 1.0 / (jnp.sum(raised, axis=2, keepdims=True) + self_raised)
+    s_scr[...] = raised * inverse
+    self_weight = (self_raised * inverse).astype(jnp.bfloat16).astype(jnp.float32)
     for copy in copies:
         copy.wait()
-    for row, (weights, self_weight) in enumerate(shares):
+    for row in range(rows):
+        weights = s_scr[row].astype(jnp.bfloat16)
         total = jnp.dot(weights, v_ref[row], preferred_element_type=jnp.float32)
-        o_scr[row] = total + self_weight * new_values[row : row + 1]
+        o_scr[row] = total + self_weight[row] * new_values[row : row + 1]
     half = total_heads // 2
     for head in range(total_heads):
         ref = own_out if head < half else other_out
@@ -255,6 +257,7 @@
         out_specs=(VMEM, VMEM),
         scratch_shapes=[pltpu.VMEM(values.shape, values.dtype)]
         + [pltpu.VMEM((rows, heads, DH), jnp.float32)] * 2
+        + [pltpu.VMEM((rows, heads, positions), jnp.float32)]
         + [pltpu.SemaphoreType.DMA((rows,))],
         compiler_params=pltpu.CompilerParams(vmem_limit_bytes=49 * MIB),
         cost_estimate=pl.CostEstimate(

time: 70.3 us -> 70.3 us (level)
  no operation moved by 1% of the time
where the time goes in v15:
time: 70.3 us; the launch traced here: 70.1 us
  waiting for transfers between devices  23.9 us (34%)
  Pallas kernels  22.6 us (32%)
  starting transfers between devices  21.1 us (30%)
  other arithmetic  2.26 us (3%)
    ppermute x15, starting transfers between devices, across(): return lax.ppermute(array, 'gx', [(g, g ^ mask) for g in range(n)])  20.3 us
    ppermute x15, waiting for transfers between devices, across(): return lax.ppermute(array, 'gx', [(g, g ^ mask) for g in range(n)])  19.3 us
    pallas_call x2, Pallas kernels, project(): pl.pallas_call(functools.partial(project_kernel, orders, rows, first, wid...  8.76 us
    pallas_call x2, Pallas kernels, load(): pl.pallas_call(functools.partial(load_kernel, len(after), cuts, len(array...  6.84 us
    ppermute x4, waiting for transfers between devices, swap(): return lax.ppermute(array, 'gy', [(0, 1), (1, 0)])  4.55 us
    pallas_call x1, Pallas kernels, attend(): pl.pallas_call(functools.partial(attend_kernel, kv_column), out_shape=(ou...  4.32 us
    pallas_call x1, Pallas kernels, project_out(): pl.pallas_call(functools.partial(output_kernel, orders, rows, columns, pi...  2.65 us
  transfers between devices with their start and end apart: 19, of which 13 were waited for; matrix products, arithmetic and copies ran while one was open for 2% of the time, Pallas kernels for 17%

profile of v15, /device:TPU:0, one launch (start us, length us, event | category | flops | bytes accessed | tf_op | source)
XLA Modules:
  0.0 70.1 jit_solution(8340847731249839354)
XLA Ops:
  0.5 1.0 %broadcast_select_fusion.own_ref = bf16[64,2304]{1,0:T(8,128)(2,1)S(1)} fusion(bf16[64,2304]{1,0:T(8,128)(2,1)} %param.7, pred[]{:T(512)S(6)} %lt.9), kind=kLoop, calls=%fused_computation.1 | loop fusion | flops 147456 | bytes 589825 | tf_op jit(solution)/shard_map/jit(_where)/select_n | solution.py:340
  1.9 3.4 %project.2 = (f32[64,1024]{1,0:T(8,128)S(1)}, f32[64,1024]{1,0:T(8,128)S(1)}) custom-call(s32[2]{0:T(128)S(1)} %pad_add_fusion.ids_ref, bf16[64,2304]{1,0:T(8,128)(2,1)S(1)} %broadcast_select_fusion.own_ref, bf16[64,2304]{1,0:T(8,128)(2,1)S(1)} %collective-permute-done.other_ref, bf16[2304,3072]{1,0:T(8,128)(2,1)} %w_ref.3), custom_call_target="tpu_custom_call" | custom-call | flops 603979776 | bytes 5242880 | tf_op jit(solution)/shard_map/project/pallas_call | solution.py:176
  5.3 3.0 %collective-permute-start.1 = (f32[64,1024]{1,0:T(8,128)S(1)}, f32[64,1024]{1,0:T(8,128)S(1)}, u32[]{:S(2)}, u32[]{:S(2)}) collective-permute-start(f32[64,1024]{1,0:T(8,128)S(1)} %get-tuple-element.35.refs_1_), channel_id=1, source_target_pairs={{0,4},{2,6},{4,0},{6,2},{8,12},{10,14},{12,8},{14,10},{1,5},{3,7},... | collective-permute-start | bytes 786440 | tf_op jit(solution)/shard_map/ppermute | solution.py:337
  8.3 5.3 %project.3 = (f32[64,1024]{1,0:T(8,128)S(1)}, f32[64,1024]{1,0:T(8,128)S(1)}, f32[64,1280]{1,0:T(8,128)S(1)}, f32[64,1280]{1,0:T(8,128)S(1)}) custom-call(s32[2]{0:T(128)S(1)} %pad_add_fusion.ids_ref, bf16[64,2304]{1,0:T(8,128)(2,1)S(1)} %broadcast_select_fusion.own_ref, bf16[64,2304]{1,0:T(8,128)(2,1)S(1)} %collective-permute-done.other_ref, ...), custom_call_target="tpu_custom_call" | custom-call | flops 1358954496 | bytes 11796480 | tf_op jit(solution)/shard_map/project/pallas_call | solution.py:176
  13.7 1.6 %collective-permute-start.7 = (f32[64,1280]{1,0:T(8,128)S(1)}, f32[64,1280]{1,0:T(8,128)S(1)}, u32[]{:S(2)}, u32[]{:S(2)}) collective-permute-start(f32[64,1280]{1,0:T(8,128)S(1)} %get-tuple-element.39), channel_id=1, source_target_pairs={{0,2},{2,0},{4,6},{6,4},{8,10},{10,8},{12,14},{14,12},{1,3},{3,1},... | collective-permute-start | bytes 983048 | tf_op jit(solution)/shard_map/ppermute | solution.py:337
  15.3 0.5 collective-permute-start.4
  15.8 2.6 %collective-permute-start.2 = (f32[32,1024]{1,0:T(8,128)S(1)}, f32[32,1024]{1,0:T(8,128)S(1)}, u32[]{:S(2)}, u32[]{:S(2)}) collective-permute-start(f32[32,1024]{1,0:T(8,128)S(1)} %slice.57), channel_id=1, source_target_pairs={{0,8},{2,10},{4,12},{6,14},{8,0},{10,2},{12,4},{14,6},{1,9},{3,11}... | collective-permute-start | bytes 393224 | tf_op jit(solution)/shard_map/ppermute | solution.py:337
  18.4 7.4 %collective-permute-done.4 = f32[64,1024]{1,0:T(8,128)S(1)} collective-permute-done((f32[64,1024]{1,0:T(8,128)S(1)}, f32[64,1024]{1,0:T(8,128)S(1)}, u32[]{:S(2)}, u32[]{:S(2)}) %collective-permute-start.4) | collective-permute-done | bytes 262176 | tf_op jit(solution)/shard_map/ppermute | solution.py:337
  25.9 0.6 collective-permute-start.5
  26.7 1.6 %collective-permute-start.3 = (f32[16,1024]{1,0:T(8,128)S(1)}, f32[16,1024]{1,0:T(8,128)S(1)}, u32[]{:S(2)}, u32[]{:S(2)}) collective-permute-start(f32[16,1024]{1,0:T(8,128)S(1)} %slice.59), channel_id=1, source_target_pairs={{0,2},{2,0},{4,6},{6,4},{8,10},{10,8},{12,14},{14,12},{1,3},{3,1},... | collective-permute-start | bytes 196616 | tf_op jit(solution)/shard_map/ppermute | solution.py:337
  28.3 2.7 %collective-permute-done.5 = f32[32,1024]{1,0:T(8,128)S(1)} collective-permute-done((f32[32,1024]{1,0:T(8,128)S(1)}, f32[32,1024]{1,0:T(8,128)S(1)}, u32[]{:S(2)}, u32[]{:S(2)}) %collective-permute-start.5) | collective-permute-done | bytes 131104 | tf_op jit(solution)/shard_map/ppermute | solution.py:337
  31.0 1.5 %collective-permute-start.6 = (f32[16,1024]{1,0:T(8,128)S(1)}, f32[16,1024]{1,0:T(8,128)S(1)}, u32[]{:S(2)}, u32[]{:S(2)}) collective-permute-start(f32[16,1024]{1,0:T(8,128)S(1)} %slice.63), channel_id=1, source_target_pairs={{0,8},{2,10},{4,12},{6,14},{8,0},{10,2},{12,4},{14,6},{1,9},{3,11}... | collective-permute-start | bytes 196616 | tf_op jit(solution)/shard_map/ppermute | solution.py:337
  32.5 1.6 %collective-permute-start.9 = (f32[16,1280]{1,0:T(8,128)S(1)}, f32[16,1280]{1,0:T(8,128)S(1)}, u32[]{:S(2)}, u32[]{:S(2)}) collective-permute-start(f32[16,1280]{1,0:T(8,128)S(1)} %slice.67), channel_id=1, source_target_pairs={{0,8},{2,10},{4,12},{6,14},{8,0},{10,2},{12,4},{14,6},{1,9},{3,11}... | collective-permute-start | bytes 245768 | tf_op jit(solution)/shard_map/ppermute | solution.py:337
  34.1 2.6 %collective-permute-done.6 = f32[16,1024]{1,0:T(8,128)S(1)} collective-permute-done((f32[16,1024]{1,0:T(8,128)S(1)}, f32[16,1024]{1,0:T(8,128)S(1)}, u32[]{:S(2)}, u32[]{:S(2)}) %collective-permute-start.6) | collective-permute-done | bytes 65568 | tf_op jit(solution)/shard_map/ppermute | solution.py:337
  36.7 1.3 %collective-permute-done.9 = f32[16,1280]{1,0:T(8,128)S(1)} collective-permute-done((f32[16,1280]{1,0:T(8,128)S(1)}, f32[16,1280]{1,0:T(8,128)S(1)}, u32[]{:S(2)}, u32[]{:S(2)}) %collective-permute-start.9) | collective-permute-done | bytes 81952 | tf_op jit(solution)/shard_map/ppermute | solution.py:337
  38.2 1.1 %collective-permute-done.10.other_q = bf16[8,3328]{1,0:T(8,128)(2,1)S(1)} collective-permute-done((bf16[8,3328]{1,0:T(8,128)(2,1)S(1)}, bf16[8,3328]{1,0:T(8,128)(2,1)S(1)}, u32[]{:S(2)}, u32[]{:S(2)}) %collective-permute-start.10) | collective-permute-done | bytes 53280 | tf_op jit(solution)/shard_map/ppermute | solution.py:334
  39.3 4.3 %attend.1 = (bf16[8,3072]{1,0:T(8,128)(2,1)S(1)}, bf16[8,3072]{1,0:T(8,128)(2,1)S(1)}) custom-call(s32[9]{0:T(128)S(1)} %pad_add_fusion.1.scalars_ref, bf16[8,3328]{1,0:T(8,128)(2,1)S(1)} %get-tuple-element.64.own_q, bf16[8,3328]{1,0:T(8,128)(2,1)S(1)} %collective-permute-done.10.other_q, bf16[8,1024,256]{2,1,0:T(8,128)(2,1)S(1)} %copy-done, ...), custom_call_target="tpu_custom_call" | custom-call | flops 201326592 | bytes 8388608 | tf_op jit(solution)/shard_map/attend/pallas_call | solution.py:253
  43.9 1.1 %collective-permute-done.11 = bf16[8,3072]{1,0:T(8,128)(2,1)S(1)} collective-permute-done((bf16[8,3072]{1,0:T(8,128)(2,1)S(1)}, bf16[8,3072]{1,0:T(8,128)(2,1)S(1)}, u32[]{:S(2)}, u32[]{:S(2)}) %collective-permute-start.11) | collective-permute-done | bytes 49184 | tf_op jit(solution)/shard_map/ppermute | solution.py:334
  45.0 2.4 %collective-permute-start.14 = (bf16[16,1536]{1,0:T(8,128)(2,1)S(1)}, bf16[16,1536]{1,0:T(8,128)(2,1)S(1)}, u32[]{:S(2)}, u32[]{:S(2)}) collective-permute-start(bf16[16,1536]{1,0:T(8,128)(2,1)S(1)} %get-tuple-element.65), channel_id=1, source_target_pairs={{0,2},{2,0},{4,6},{6,4},{8,10},{10,8},{12,14},{14,12},{1,3},{3,1},... | collective-permute-start | bytes 147464 | tf_op jit(solution)/shard_map/ppermute | solution.py:337
  47.4 0.8 %collective-permute-start.12 = (bf16[16,1536]{1,0:T(8,128)(2,1)S(1)}, bf16[16,1536]{1,0:T(8,128)(2,1)S(1)}, u32[]{:S(2)}, u32[]{:S(2)}) collective-permute-start(bf16[16,1536]{1,0:T(8,128)(2,1)S(1)} %get-tuple-element.66), channel_id=1, source_target_pairs={{0,8},{2,10},{4,12},{6,14},{8,0},{10,2},{12,4},{14,6},{1,9},{3,11}... | collective-permute-start | bytes 147464 | tf_op jit(solution)/shard_map/ppermute | solution.py:337
  48.2 1.3 %collective-permute-done.14 = bf16[16,1536]{1,0:T(8,128)(2,1)S(1)} collective-permute-done((bf16[16,1536]{1,0:T(8,128)(2,1)S(1)}, bf16[16,1536]{1,0:T(8,128)(2,1)S(1)}, u32[]{:S(2)}, u32[]{:S(2)}) %collective-permute-start.14) | collective-permute-done | bytes 49184 | tf_op jit(solution)/shard_map/ppermute | solution.py:337
  49.5 1.3 %collective-permute-start.16 = (bf16[32,1536]{1,0:T(8,128)(2,1)S(1)}, bf16[32,1536]{1,0:T(8,128)(2,1)S(1)}, u32[]{:S(2)}, u32[]{:S(2)}) collective-permute-start(bf16[32,1536]{1,0:T(8,128)(2,1)S(1)} %pad_maximum_fusion.3.refs_1_), channel_id=1, source_target_pairs={{0,8},{2,10},{4,12},{6,14},{8,0},{10,2},{12,4},{14,6},{1,9},{3,11}... | collective-permute-start | bytes 294920 | tf_op jit(solution)/shard_map/ppermute | solution.py:337
  50.8 2.2 %collective-permute-done.12 = bf16[16,1536]{1,0:T(8,128)(2,1)S(1)} collective-permute-done((bf16[16,1536]{1,0:T(8,128)(2,1)S(1)}, bf16[16,1536]{1,0:T(8,128)(2,1)S(1)}, u32[]{:S(2)}, u32[]{:S(2)}) %collective-permute-start.12) | collective-permute-done | bytes 49184 | tf_op jit(solution)/shard_map/ppermute | solution.py:337
  53.0 0.6 collective-permute-start.13
  53.6 3.1 %load.2 = (bf16[512,768]{1,0:T(8,128)(2,1)S(1)}, bf16[512,768]{1,0:T(8,128)(2,1)S(1)}, bf16[512,768]{1,0:T(8,128)(2,1)S(1)}, bf16[512,768]{1,0:T(8,128)(2,1)S(1)...) custom-call(bf16[32,1536]{1,0:T(8,128)(2,1)S(1)} %pad_maximum_fusion, ...), custom_call_target="tpu_custom_call" | custom-call | bytes 14155776 | tf_op jit(solution)/shard_map/load/pallas_call | solution.py:78
  57.1 1.3 %collective-permute-start.17 = (bf16[64,1536]{1,0:T(8,128)(2,1)S(1)}, bf16[64,1536]{1,0:T(8,128)(2,1)S(1)}, u32[]{:S(2)}, u32[]{:S(2)}) collective-permute-start(bf16[64,1536]{1,0:T(8,128)(2,1)S(1)} %pad_maximum_fusion.1.refs_1_.refs_2_), channel_id=1, source_target_pairs={{0,4},{2,6},{4,0},{6,2},{8,12},{10,14},{12,8},{14,10},{1,5},{3,7},... | collective-permute-start | bytes 589832 | tf_op jit(solution)/shard_map/ppermute | solution.py:337
  58.4 0.9 %collective-permute-start.15 = (bf16[64,1536]{1,0:T(8,128)(2,1)S(1)}, bf16[64,1536]{1,0:T(8,128)(2,1)S(1)}, u32[]{:S(2)}, u32[]{:S(2)}) collective-permute-start(bf16[64,1536]{1,0:T(8,128)(2,1)S(1)} %maximum_add_fusion.refs_0_), channel_id=1, source_target_pairs={{0,2},{2,0},{4,6},{6,4},{8,10},{10,8},{12,14},{14,12},{1,3},{3,1},... | collective-permute-start | bytes 589832 | tf_op jit(solution)/shard_map/ppermute | solution.py:337
  59.3 3.7 %load.3 = (bf16[512,768]{1,0:T(8,128)(2,1)S(1)}, bf16[512,768]{1,0:T(8,128)(2,1)S(1)}, bf16[512,768]{1,0:T(8,128)(2,1)S(1)}, bf16[512,768]{1,0:T(8,128)(2,1)S(1)...) custom-call(bf16[64,1536]{1,0:T(8,128)(2,1)S(1)} %maximum_add_fusion, ...), custom_call_target="tpu_custom_call" | custom-call | bytes 14155776 | tf_op jit(solution)/shard_map/load/pallas_call | solution.py:78
  63.4 1.2 %collective-permute-done.15.refs_1_ = bf16[64,1536]{1,0:T(8,128)(2,1)S(1)} collective-permute-done((bf16[64,1536]{1,0:T(8,128)(2,1)S(1)}, bf16[64,1536]{1,0:T(8,128)(2,1)S(1)}, u32[]{:S(2)}, u32[]{:S(2)}) %collective-permute-start.15) | collective-permute-done | bytes 196640 | tf_op jit(solution)/shard_map/ppermute | solution.py:337
  64.6 2.6 %project_out.1 = (f32[64,2304]{1,0:T(8,128)S(1)}, f32[64,2304]{1,0:T(8,128)S(1)}) custom-call(s32[2]{0:T(128)S(1)} %pad_add_fusion.ids_ref, bf16[64,1536]{1,0:T(8,128)(2,1)S(1)} %maximum_add_fusion.refs_0_, bf16[64,1536]{1,0:T(8,128)(2,1)S(1)} %collective-permute-done.15.refs_1_, bf16[64,1536]{1,0:T(8,128)(2,1)S(1)} %pad_maximum_fusion.1.refs_1_.refs_2_, ...), custom_call_target="tpu_custom_call" | custom-call | flops 1811939328 | bytes 15335424 | tf_op jit(solution)/shard_map/project_out/pallas_call | solution.py:308
  67.3 2.0 %collective-permute-done.18 = f32[64,2304]{1,0:T(8,128)S(1)} collective-permute-done((f32[64,2304]{1,0:T(8,128)S(1)}, f32[64,2304]{1,0:T(8,128)S(1)}, u32[]{:S(2)}, u32[]{:S(2)}) %collective-permute-start.18) | collective-permute-done | bytes 589856 | tf_op jit(solution)/shard_map/ppermute | solution.py:334
  69.3 0.8 %add_convert_fusion = bf16[64,2304]{1,0:T(8,128)(2,1)} fusion(f32[64,2304]{1,0:T(8,128)S(1)} %get-tuple-element.61, f32[64,2304]{1,0:T(8,128)S(1)} %collective-permute-done.18), kind=kLoop, calls=%fused_computation | loop fusion | flops 294912 | bytes 1474560 | tf_op jit(solution)/shard_map/convert_element_type | solution.py:395
  (46 shorter events, 2.5 us)
Async XLA Ops:
  0.0 1.9 %collective-permute-start = (bf16[64,2304]{1,0:T(8,128)(2,1)}, bf16[64,2304]{1,0:T(8,128)(2,1)S(1)}, u32[]{:S(2)}, u32[]{:S(2)}) collective-permute-start(bf16[64,2304]{1,0:T(8,128)(2,1)} %param.7), channel_id=1, source_target_pairs={{0,1},{1,0},{2,3},{3,2},{4,5},{5,4},{6,7},{7,6},{8,9},{9,8},{10,11... | collective-permute-start | bytes 884744 | tf_op jit(solution)/shard_map/ppermute | solution.py:334
  1.5 6.8 %copy-start.1 = (bf16[2304,512]{1,0:T(8,128)(2,1)S(1)}, bf16[2304,512]{1,0:T(8,128)(2,1)}, u32[]{:S(2)}) copy-start(bf16[2304,512]{1,0:T(8,128)(2,1)} %refs_0_.2) | copy-start | bytes 7077892
  5.3 10.4 %collective-permute-start.1 = (f32[64,1024]{1,0:T(8,128)S(1)}, f32[64,1024]{1,0:T(8,128)S(1)}, u32[]{:S(2)}, u32[]{:S(2)}) collective-permute-start(f32[64,1024]{1,0:T(8,128)S(1)} %get-tuple-element.35.refs_1_), channel_id=1, source_target_pairs={{0,4},{2,6},{4,0},{6,2},{8,12},{10,14},{12,8},{14,10},{1,5},{3,7},... | collective-permute-start | bytes 786440 | tf_op jit(solution)/shard_map/ppermute | solution.py:337
  13.7 24.4 %copy-start.2 = (s32[8]{0:T(128)S(1)}, s32[8]{0:T(128)}, u32[]{:S(2)}) copy-start(s32[8]{0:T(128)} %param.13) | copy-start | bytes 100
  13.7 12.8 %collective-permute-start.7 = (f32[64,1280]{1,0:T(8,128)S(1)}, f32[64,1280]{1,0:T(8,128)S(1)}, u32[]{:S(2)}, u32[]{:S(2)}) collective-permute-start(f32[64,1280]{1,0:T(8,128)S(1)} %get-tuple-element.39), channel_id=1, source_target_pairs={{0,2},{2,0},{4,6},{6,4},{8,10},{10,8},{12,14},{14,12},{1,3},{3,1},... | collective-permute-start | bytes 983048 | tf_op jit(solution)/shard_map/ppermute | solution.py:337
  15.3 10.6 %collective-permute-start.4 = (f32[64,1024]{1,0:T(8,128)S(1)}, f32[64,1024]{1,0:T(8,128)S(1)}, u32[]{:S(2)}, u32[]{:S(2)}) collective-permute-start(f32[64,1024]{1,0:T(8,128)S(1)} %get-tuple-element.37), channel_id=1, source_target_pairs={{0,4},{2,6},{4,0},{6,2},{8,12},{10,14},{12,8},{14,10},{1,5},{3,7},... | collective-permute-start | bytes 786440 | tf_op jit(solution)/shard_map/ppermute | solution.py:337
  15.8 10.9 %collective-permute-start.2 = (f32[32,1024]{1,0:T(8,128)S(1)}, f32[32,1024]{1,0:T(8,128)S(1)}, u32[]{:S(2)}, u32[]{:S(2)}) collective-permute-start(f32[32,1024]{1,0:T(8,128)S(1)} %slice.57), channel_id=1, source_target_pairs={{0,8},{2,10},{4,12},{6,14},{8,0},{10,2},{12,4},{14,6},{1,9},{3,11}... | collective-permute-start | bytes 393224 | tf_op jit(solution)/shard_map/ppermute | solution.py:337
  18.4 20.9 %copy-start = (bf16[8,1024,256]{2,1,0:T(8,128)(2,1)S(1)}, bf16[8,1024,256]{2,1,0:T(8,128)(2,1)}, u32[]{:S(2)}) copy-start(bf16[8,1024,256]{2,1,0:T(8,128)(2,1)} %refs_0_.3) | copy-start | bytes 12582916
  25.9 5.0 %collective-permute-start.5 = (f32[32,1024]{1,0:T(8,128)S(1)}, f32[32,1024]{1,0:T(8,128)S(1)}, u32[]{:S(2)}, u32[]{:S(2)}) collective-permute-start(f32[32,1024]{1,0:T(8,128)S(1)} %slice.61), channel_id=1, source_target_pairs={{0,2},{2,0},{4,6},{6,4},{8,10},{10,8},{12,14},{14,12},{1,3},{3,1},... | collective-permute-start | bytes 393224 | tf_op jit(solution)/shard_map/ppermute | solution.py:337
  26.6 5.9 %collective-permute-start.8 = (f32[32,1280]{1,0:T(8,128)S(1)}, f32[32,1280]{1,0:T(8,128)S(1)}, u32[]{:S(2)}, u32[]{:S(2)}) collective-permute-start(f32[32,1280]{1,0:T(8,128)S(1)} %slice.65), channel_id=1, source_target_pairs={{0,4},{2,6},{4,0},{6,2},{8,12},{10,14},{12,8},{14,10},{1,5},{3,7},... | collective-permute-start | bytes 491528 | tf_op jit(solution)/shard_map/ppermute | solution.py:337
  26.7 5.8 %collective-permute-start.3 = (f32[16,1024]{1,0:T(8,128)S(1)}, f32[16,1024]{1,0:T(8,128)S(1)}, u32[]{:S(2)}, u32[]{:S(2)}) collective-permute-start(f32[16,1024]{1,0:T(8,128)S(1)} %slice.59), channel_id=1, source_target_pairs={{0,2},{2,0},{4,6},{6,4},{8,10},{10,8},{12,14},{14,12},{1,3},{3,1},... | collective-permute-start | bytes 196616 | tf_op jit(solution)/shard_map/ppermute | solution.py:337
  31.0 5.7 %collective-permute-start.6 = (f32[16,1024]{1,0:T(8,128)S(1)}, f32[16,1024]{1,0:T(8,128)S(1)}, u32[]{:S(2)}, u32[]{:S(2)}) collective-permute-start(f32[16,1024]{1,0:T(8,128)S(1)} %slice.63), channel_id=1, source_target_pairs={{0,8},{2,10},{4,12},{6,14},{8,0},{10,2},{12,4},{14,6},{1,9},{3,11}... | collective-permute-start | bytes 196616 | tf_op jit(solution)/shard_map/ppermute | solution.py:337
  32.5 5.4 %collective-permute-start.9 = (f32[16,1280]{1,0:T(8,128)S(1)}, f32[16,1280]{1,0:T(8,128)S(1)}, u32[]{:S(2)}, u32[]{:S(2)}) collective-permute-start(f32[16,1280]{1,0:T(8,128)S(1)} %slice.67), channel_id=1, source_target_pairs={{0,8},{2,10},{4,12},{6,14},{8,0},{10,2},{12,4},{14,6},{1,9},{3,11}... | collective-permute-start | bytes 245768 | tf_op jit(solution)/shard_map/ppermute | solution.py:337
  38.0 1.3 %collective-permute-start.10 = (bf16[8,3328]{1,0:T(8,128)(2,1)S(1)}, bf16[8,3328]{1,0:T(8,128)(2,1)S(1)}, u32[]{:S(2)}, u32[]{:S(2)}) collective-permute-start(bf16[8,3328]{1,0:T(8,128)(2,1)S(1)} %get-tuple-element.63), channel_id=1, source_target_pairs={{0,1},{1,0},{2,3},{3,2},{4,5},{5,4},{6,7},{7,6},{8,9},{9,8},{10,11... | collective-permute-start | bytes 159752 | tf_op jit(solution)/shard_map/ppermute | solution.py:334
  43.6 1.3 %collective-permute-start.11 = (bf16[8,3072]{1,0:T(8,128)(2,1)S(1)}, bf16[8,3072]{1,0:T(8,128)(2,1)S(1)}, u32[]{:S(2)}, u32[]{:S(2)}) collective-permute-start(bf16[8,3072]{1,0:T(8,128)(2,1)S(1)} %get-tuple-element.41), channel_id=1, source_target_pairs={{0,1},{1,0},{2,3},{3,2},{4,5},{5,4},{6,7},{7,6},{8,9},{9,8},{10,11... | collective-permute-start | bytes 147464 | tf_op jit(solution)/shard_map/ppermute | solution.py:334
  45.0 4.5 %collective-permute-start.14 = (bf16[16,1536]{1,0:T(8,128)(2,1)S(1)}, bf16[16,1536]{1,0:T(8,128)(2,1)S(1)}, u32[]{:S(2)}, u32[]{:S(2)}) collective-permute-start(bf16[16,1536]{1,0:T(8,128)(2,1)S(1)} %get-tuple-element.65), channel_id=1, source_target_pairs={{0,2},{2,0},{4,6},{6,4},{8,10},{10,8},{12,14},{14,12},{1,3},{3,1},... | collective-permute-start | bytes 147464 | tf_op jit(solution)/shard_map/ppermute | solution.py:337
  47.4 5.6 %collective-permute-start.12 = (bf16[16,1536]{1,0:T(8,128)(2,1)S(1)}, bf16[16,1536]{1,0:T(8,128)(2,1)S(1)}, u32[]{:S(2)}, u32[]{:S(2)}) collective-permute-start(bf16[16,1536]{1,0:T(8,128)(2,1)S(1)} %get-tuple-element.66), channel_id=1, source_target_pairs={{0,8},{2,10},{4,12},{6,14},{8,0},{10,2},{12,4},{14,6},{1,9},{3,11}... | collective-permute-start | bytes 147464 | tf_op jit(solution)/shard_map/ppermute | solution.py:337
  49.5 7.6 %collective-permute-start.16 = (bf16[32,1536]{1,0:T(8,128)(2,1)S(1)}, bf16[32,1536]{1,0:T(8,128)(2,1)S(1)}, u32[]{:S(2)}, u32[]{:S(2)}) collective-permute-start(bf16[32,1536]{1,0:T(8,128)(2,1)S(1)} %pad_maximum_fusion.3.refs_1_), channel_id=1, source_target_pairs={{0,8},{2,10},{4,12},{6,14},{8,0},{10,2},{12,4},{14,6},{1,9},{3,11}... | collective-permute-start | bytes 294920 | tf_op jit(solution)/shard_map/ppermute | solution.py:337
  53.0 5.4 %collective-permute-start.13 = (bf16[32,1536]{1,0:T(8,128)(2,1)S(1)}, bf16[32,1536]{1,0:T(8,128)(2,1)S(1)}, u32[]{:S(2)}, u32[]{:S(2)}) collective-permute-start(bf16[32,1536]{1,0:T(8,128)(2,1)S(1)} %pad_maximum_fusion.2.refs_0_), channel_id=1, source_target_pairs={{0,4},{2,6},{4,0},{6,2},{8,12},{10,14},{12,8},{14,10},{1,5},{3,7},... | collective-permute-start | bytes 294920 | tf_op jit(solution)/shard_map/ppermute | solution.py:337
  57.1 6.3 %collective-permute-start.17 = (bf16[64,1536]{1,0:T(8,128)(2,1)S(1)}, bf16[64,1536]{1,0:T(8,128)(2,1)S(1)}, u32[]{:S(2)}, u32[]{:S(2)}) collective-permute-start(bf16[64,1536]{1,0:T(8,128)(2,1)S(1)} %pad_maximum_fusion.1.refs_1_.refs_2_), channel_id=1, source_target_pairs={{0,4},{2,6},{4,0},{6,2},{8,12},{10,14},{12,8},{14,10},{1,5},{3,7},... | collective-permute-start | bytes 589832 | tf_op jit(solution)/shard_map/ppermute | solution.py:337
  58.4 6.2 %collective-permute-start.15 = (bf16[64,1536]{1,0:T(8,128)(2,1)S(1)}, bf16[64,1536]{1,0:T(8,128)(2,1)S(1)}, u32[]{:S(2)}, u32[]{:S(2)}) collective-permute-start(bf16[64,1536]{1,0:T(8,128)(2,1)S(1)} %maximum_add_fusion.refs_0_), channel_id=1, source_target_pairs={{0,2},{2,0},{4,6},{6,4},{8,10},{10,8},{12,14},{14,12},{1,3},{3,1},... | collective-permute-start | bytes 589832 | tf_op jit(solution)/shard_map/ppermute | solution.py:337
  67.3 2.1 %collective-permute-start.18 = (f32[64,2304]{1,0:T(8,128)S(1)}, f32[64,2304]{1,0:T(8,128)S(1)}, u32[]{:S(2)}, u32[]{:S(2)}) collective-permute-start(f32[64,2304]{1,0:T(8,128)S(1)} %get-tuple-element.62), channel_id=1, source_target_pairs={{0,1},{1,0},{2,3},{3,2},{4,5},{5,4},{6,7},{7,6},{8,9},{9,8},{10,11... | collective-permute-start | bytes 1769480 | tf_op jit(solution)/shard_map/ppermute | solution.py:334

commit v16 on v14

--- a/solution.py
+++ b/solution.py
@@ -212,25 +212,39 @@
     second = other_q[:, kv_column : kv_column + DH].astype(jnp.float32)
     new_keys = jnp.where(core == 0, first, second)
     new_values = jnp.where(core == 0, second, first)
+    group = max(g for g in range(1, rows + 1) if rows % g == 0 and g * total_heads <= 128)
+    lane = lax.broadcasted_iota(jnp.int32, (1, 128), 1)
+    place = lax.broadcasted_iota(jnp.int32, (positions, 128), 0)
     shares = []
-    for row in range(rows):
-        query = q_scr[row]
-        scores = lax.dot_general(
-            query.astype(jnp.bfloat16),
-            k_ref[row],
-            (((1,), (1,)), ((), ())),
-            preferred_element_type=jnp.float32,
-        )
-        self_score = jnp.sum(query * new_keys[row : row + 1], axis=1, keepdims=True)
-        visible = lax.broadcasted_iota(jnp.int32, scores.shape, 1) < scalars_ref[1 + row]
-        masked = jnp.where(visible, scores, jnp.float32(-1e30))
-        peak = jnp.maximum(jnp.max(masked, axis=1, keepdims=True), self_score)
+    for base in range(0, rows, group):
+        members = range(base, base + group)
+        queries = jnp.concatenate(
+            [q_scr[row] for row in members]
+            + [jnp.zeros((128 - group * total_heads, DH), jnp.float32)] * (group * total_heads < 128)
+        ).T
+        columns, lengths = [], jnp.zeros((1, 128), jnp.int32)
+        for at, row in enumerate(members):
+            own = (lane >= at * total_heads) & (lane < (at + 1) * total_heads)
+            columns.append(jnp.where(own, queries, 0.0).astype(jnp.bfloat16))
+            lengths = jnp.where(own, scalars_ref[1 + row], lengths)
+        columns = jnp.concatenate(columns)
+        keys = jnp.concatenate([k_ref[row] for row in members], axis=1)
+        scores = jnp.dot(keys, columns, preferred_element_type=jnp.float32)
+        fresh = jnp.concatenate([new_keys[row : row + 1] for row in members], axis=1).astype(jnp.bfloat16)
+        self_score = jnp.dot(
+            jnp.broadcast_to(fresh, (16, group * DH)), columns, preferred_element_type=jnp.float32
+        )[:1]
+        masked = jnp.where(place < lengths, scores, jnp.float32(-1e30))
+        peak = jnp.maximum(jnp.max(masked, axis=0, keepdims=True), self_score)
         raised = jnp.exp(masked - peak)
         self_raised = jnp.exp(self_score - peak)
-        inverse = 1.0 / (jnp.sum(raised, axis=1, keepdims=True) + self_raised)
-        weights = (raised * inverse).astype(jnp.bfloat16)
-        self_weight = (self_raised * inverse).astype(jnp.bfloat16).astype(jnp.float32)
-        shares.append((weights, self_weight))
+        inverse = 1.0 / (jnp.sum(raised, axis=0, keepdims=True) + self_raised)
+        weights = (raised * inverse).T
+        self_weights = jnp.broadcast_to(self_raised * inverse, (128, 128)).T
+        for at, row in enumerate(members):
+            span = slice(at * total_heads, (at + 1) * total_heads)
+            self_weight = self_weights[span, :1].astype(jnp.bfloat16).astype(jnp.float32)
+            shares.append((weights[span].astype(jnp.bfloat16), self_weight))
     for copy in copies:
         copy.wait()
     for row, (weights, self_weight) in enumerate(shares):

time: 70.3 us -> 70.3 us (level)
  no operation moved by 1% of the time
where the time goes in v16:
time: 70.3 us; the launch traced here: 70.1 us
  waiting for transfers between devices  23.9 us (34%)
  Pallas kernels  22.5 us (32%)
  starting transfers between devices  21.1 us (30%)
  other arithmetic  2.26 us (3%)
    ppermute x15, starting transfers between devices, across(): return lax.ppermute(array, 'gx', [(g, g ^ mask) for g in range(n)])  20.3 us
    ppermute x15, waiting for transfers between devices, across(): return lax.ppermute(array, 'gx', [(g, g ^ mask) for g in range(n)])  19.3 us
    pallas_call x2, Pallas kernels, project(): pl.pallas_call(functools.partial(project_kernel, orders, rows, first, wid...  8.76 us
    pallas_call x2, Pallas kernels, load(): pl.pallas_call(functools.partial(load_kernel, len(after), cuts, len(array...  6.84 us
    ppermute x4, waiting for transfers between devices, swap(): return lax.ppermute(array, 'gy', [(0, 1), (1, 0)])  4.55 us
    pallas_call x1, Pallas kernels, attend(): pl.pallas_call(functools.partial(attend_kernel, kv_column), out_shape=(ou...  4.29 us
    pallas_call x1, Pallas kernels, project_out(): pl.pallas_call(functools.partial(output_kernel, orders, rows, columns, pi...  2.65 us
  transfers between devices with their start and end apart: 19, of which 13 were waited for; matrix products, arithmetic and copies ran while one was open for 2% of the time, Pallas kernels for 17%

profile of v16, /device:TPU:0, one launch (start us, length us, event | category | flops | bytes accessed | tf_op | source)
XLA Modules:
  0.0 70.1 jit_solution(15900236909155944154)
XLA Ops:
  0.5 1.0 %broadcast_select_fusion.own_ref = bf16[64,2304]{1,0:T(8,128)(2,1)S(1)} fusion(bf16[64,2304]{1,0:T(8,128)(2,1)} %param.7, pred[]{:T(512)S(6)} %lt.9), kind=kLoop, calls=%fused_computation.1 | loop fusion | flops 147456 | bytes 589825 | tf_op jit(solution)/shard_map/jit(_where)/select_n | solution.py:351
  1.9 3.4 %project.2 = (f32[64,1024]{1,0:T(8,128)S(1)}, f32[64,1024]{1,0:T(8,128)S(1)}) custom-call(s32[2]{0:T(128)S(1)} %pad_add_fusion.ids_ref, bf16[64,2304]{1,0:T(8,128)(2,1)S(1)} %broadcast_select_fusion.own_ref, bf16[64,2304]{1,0:T(8,128)(2,1)S(1)} %collective-permute-done.other_ref, bf16[2304,3072]{1,0:T(8,128)(2,1)} %w_ref.3), custom_call_target="tpu_custom_call" | custom-call | flops 603979776 | bytes 5242880 | tf_op jit(solution)/shard_map/project/pallas_call | solution.py:176
  5.3 3.0 %collective-permute-start.1 = (f32[64,1024]{1,0:T(8,128)S(1)}, f32[64,1024]{1,0:T(8,128)S(1)}, u32[]{:S(2)}, u32[]{:S(2)}) collective-permute-start(f32[64,1024]{1,0:T(8,128)S(1)} %get-tuple-element.35.refs_1_), channel_id=1, source_target_pairs={{0,4},{2,6},{4,0},{6,2},{8,12},{10,14},{12,8},{14,10},{1,5},{3,7},... | collective-permute-start | bytes 786440 | tf_op jit(solution)/shard_map/ppermute | solution.py:348
  8.3 5.3 %project.3 = (f32[64,1024]{1,0:T(8,128)S(1)}, f32[64,1024]{1,0:T(8,128)S(1)}, f32[64,1280]{1,0:T(8,128)S(1)}, f32[64,1280]{1,0:T(8,128)S(1)}) custom-call(s32[2]{0:T(128)S(1)} %pad_add_fusion.ids_ref, bf16[64,2304]{1,0:T(8,128)(2,1)S(1)} %broadcast_select_fusion.own_ref, bf16[64,2304]{1,0:T(8,128)(2,1)S(1)} %collective-permute-done.other_ref, ...), custom_call_target="tpu_custom_call" | custom-call | flops 1358954496 | bytes 11796480 | tf_op jit(solution)/shard_map/project/pallas_call | solution.py:176
  13.7 1.6 %collective-permute-start.7 = (f32[64,1280]{1,0:T(8,128)S(1)}, f32[64,1280]{1,0:T(8,128)S(1)}, u32[]{:S(2)}, u32[]{:S(2)}) collective-permute-start(f32[64,1280]{1,0:T(8,128)S(1)} %get-tuple-element.39), channel_id=1, source_target_pairs={{0,2},{2,0},{4,6},{6,4},{8,10},{10,8},{12,14},{14,12},{1,3},{3,1},... | collective-permute-start | bytes 983048 | tf_op jit(solution)/shard_map/ppermute | solution.py:348
  15.3 0.5 collective-permute-start.4
  15.8 2.6 %collective-permute-start.2 = (f32[32,1024]{1,0:T(8,128)S(1)}, f32[32,1024]{1,0:T(8,128)S(1)}, u32[]{:S(2)}, u32[]{:S(2)}) collective-permute-start(f32[32,1024]{1,0:T(8,128)S(1)} %slice.57), channel_id=1, source_target_pairs={{0,8},{2,10},{4,12},{6,14},{8,0},{10,2},{12,4},{14,6},{1,9},{3,11}... | collective-permute-start | bytes 393224 | tf_op jit(solution)/shard_map/ppermute | solution.py:348
  18.4 7.4 %collective-permute-done.4 = f32[64,1024]{1,0:T(8,128)S(1)} collective-permute-done((f32[64,1024]{1,0:T(8,128)S(1)}, f32[64,1024]{1,0:T(8,128)S(1)}, u32[]{:S(2)}, u32[]{:S(2)}) %collective-permute-start.4) | collective-permute-done | bytes 262176 | tf_op jit(solution)/shard_map/ppermute | solution.py:348
  25.9 0.6 collective-permute-start.5
  26.7 1.6 %collective-permute-start.3 = (f32[16,1024]{1,0:T(8,128)S(1)}, f32[16,1024]{1,0:T(8,128)S(1)}, u32[]{:S(2)}, u32[]{:S(2)}) collective-permute-start(f32[16,1024]{1,0:T(8,128)S(1)} %slice.59), channel_id=1, source_target_pairs={{0,2},{2,0},{4,6},{6,4},{8,10},{10,8},{12,14},{14,12},{1,3},{3,1},... | collective-permute-start | bytes 196616 | tf_op jit(solution)/shard_map/ppermute | solution.py:348
  28.3 2.7 %collective-permute-done.5 = f32[32,1024]{1,0:T(8,128)S(1)} collective-permute-done((f32[32,1024]{1,0:T(8,128)S(1)}, f32[32,1024]{1,0:T(8,128)S(1)}, u32[]{:S(2)}, u32[]{:S(2)}) %collective-permute-start.5) | collective-permute-done | bytes 131104 | tf_op jit(solution)/shard_map/ppermute | solution.py:348
  31.0 1.5 %collective-permute-start.6 = (f32[16,1024]{1,0:T(8,128)S(1)}, f32[16,1024]{1,0:T(8,128)S(1)}, u32[]{:S(2)}, u32[]{:S(2)}) collective-permute-start(f32[16,1024]{1,0:T(8,128)S(1)} %slice.63), channel_id=1, source_target_pairs={{0,8},{2,10},{4,12},{6,14},{8,0},{10,2},{12,4},{14,6},{1,9},{3,11}... | collective-permute-start | bytes 196616 | tf_op jit(solution)/shard_map/ppermute | solution.py:348
  32.5 1.6 %collective-permute-start.9 = (f32[16,1280]{1,0:T(8,128)S(1)}, f32[16,1280]{1,0:T(8,128)S(1)}, u32[]{:S(2)}, u32[]{:S(2)}) collective-permute-start(f32[16,1280]{1,0:T(8,128)S(1)} %slice.67), channel_id=1, source_target_pairs={{0,8},{2,10},{4,12},{6,14},{8,0},{10,2},{12,4},{14,6},{1,9},{3,11}... | collective-permute-start | bytes 245768 | tf_op jit(solution)/shard_map/ppermute | solution.py:348
  34.1 2.6 %collective-permute-done.6 = f32[16,1024]{1,0:T(8,128)S(1)} collective-permute-done((f32[16,1024]{1,0:T(8,128)S(1)}, f32[16,1024]{1,0:T(8,128)S(1)}, u32[]{:S(2)}, u32[]{:S(2)}) %collective-permute-start.6) | collective-permute-done | bytes 65568 | tf_op jit(solution)/shard_map/ppermute | solution.py:348
  36.7 1.3 %collective-permute-done.9 = f32[16,1280]{1,0:T(8,128)S(1)} collective-permute-done((f32[16,1280]{1,0:T(8,128)S(1)}, f32[16,1280]{1,0:T(8,128)S(1)}, u32[]{:S(2)}, u32[]{:S(2)}) %collective-permute-start.9) | collective-permute-done | bytes 81952 | tf_op jit(solution)/shard_map/ppermute | solution.py:348
  38.2 1.1 %collective-permute-done.10.other_q = bf16[8,3328]{1,0:T(8,128)(2,1)S(1)} collective-permute-done((bf16[8,3328]{1,0:T(8,128)(2,1)S(1)}, bf16[8,3328]{1,0:T(8,128)(2,1)S(1)}, u32[]{:S(2)}, u32[]{:S(2)}) %collective-permute-start.10) | collective-permute-done | bytes 53280 | tf_op jit(solution)/shard_map/ppermute | solution.py:345
  39.3 4.3 %attend.1 = (bf16[8,3072]{1,0:T(8,128)(2,1)S(1)}, bf16[8,3072]{1,0:T(8,128)(2,1)S(1)}) custom-call(s32[9]{0:T(128)S(1)} %pad_add_fusion.1.scalars_ref, bf16[8,3328]{1,0:T(8,128)(2,1)S(1)} %get-tuple-element.64.own_q, bf16[8,3328]{1,0:T(8,128)(2,1)S(1)} %collective-permute-done.10.other_q, bf16[8,1024,256]{2,1,0:T(8,128)(2,1)S(1)} %copy-done, ...), custom_call_target="tpu_custom_call" | custom-call | flops 201326592 | bytes 8388608 | tf_op jit(solution)/shard_map/attend/pallas_call | solution.py:265
  43.8 1.1 %collective-permute-done.11 = bf16[8,3072]{1,0:T(8,128)(2,1)S(1)} collective-permute-done((bf16[8,3072]{1,0:T(8,128)(2,1)S(1)}, bf16[8,3072]{1,0:T(8,128)(2,1)S(1)}, u32[]{:S(2)}, u32[]{:S(2)}) %collective-permute-start.11) | collective-permute-done | bytes 49184 | tf_op jit(solution)/shard_map/ppermute | solution.py:345
  44.9 2.4 %collective-permute-start.14 = (bf16[16,1536]{1,0:T(8,128)(2,1)S(1)}, bf16[16,1536]{1,0:T(8,128)(2,1)S(1)}, u32[]{:S(2)}, u32[]{:S(2)}) collective-permute-start(bf16[16,1536]{1,0:T(8,128)(2,1)S(1)} %get-tuple-element.65), channel_id=1, source_target_pairs={{0,2},{2,0},{4,6},{6,4},{8,10},{10,8},{12,14},{14,12},{1,3},{3,1},... | collective-permute-start | bytes 147464 | tf_op jit(solution)/shard_map/ppermute | solution.py:348
  47.4 0.8 %collective-permute-start.12 = (bf16[16,1536]{1,0:T(8,128)(2,1)S(1)}, bf16[16,1536]{1,0:T(8,128)(2,1)S(1)}, u32[]{:S(2)}, u32[]{:S(2)}) collective-permute-start(bf16[16,1536]{1,0:T(8,128)(2,1)S(1)} %get-tuple-element.66), channel_id=1, source_target_pairs={{0,8},{2,10},{4,12},{6,14},{8,0},{10,2},{12,4},{14,6},{1,9},{3,11}... | collective-permute-start | bytes 147464 | tf_op jit(solution)/shard_map/ppermute | solution.py:348
  48.2 1.3 %collective-permute-done.14 = bf16[16,1536]{1,0:T(8,128)(2,1)S(1)} collective-permute-done((bf16[16,1536]{1,0:T(8,128)(2,1)S(1)}, bf16[16,1536]{1,0:T(8,128)(2,1)S(1)}, u32[]{:S(2)}, u32[]{:S(2)}) %collective-permute-start.14) | collective-permute-done | bytes 49184 | tf_op jit(solution)/shard_map/ppermute | solution.py:348
  49.5 1.3 %collective-permute-start.16 = (bf16[32,1536]{1,0:T(8,128)(2,1)S(1)}, bf16[32,1536]{1,0:T(8,128)(2,1)S(1)}, u32[]{:S(2)}, u32[]{:S(2)}) collective-permute-start(bf16[32,1536]{1,0:T(8,128)(2,1)S(1)} %pad_maximum_fusion.3.refs_1_), channel_id=1, source_target_pairs={{0,8},{2,10},{4,12},{6,14},{8,0},{10,2},{12,4},{14,6},{1,9},{3,11}... | collective-permute-start | bytes 294920 | tf_op jit(solution)/shard_map/ppermute | solution.py:348
  50.8 2.2 %collective-permute-done.12 = bf16[16,1536]{1,0:T(8,128)(2,1)S(1)} collective-permute-done((bf16[16,1536]{1,0:T(8,128)(2,1)S(1)}, bf16[16,1536]{1,0:T(8,128)(2,1)S(1)}, u32[]{:S(2)}, u32[]{:S(2)}) %collective-permute-start.12) | collective-permute-done | bytes 49184 | tf_op jit(solution)/shard_map/ppermute | solution.py:348
  53.0 0.6 collective-permute-start.13
  53.5 3.1 %load.2 = (bf16[512,768]{1,0:T(8,128)(2,1)S(1)}, bf16[512,768]{1,0:T(8,128)(2,1)S(1)}, bf16[512,768]{1,0:T(8,128)(2,1)S(1)}, bf16[512,768]{1,0:T(8,128)(2,1)S(1)...) custom-call(bf16[32,1536]{1,0:T(8,128)(2,1)S(1)} %pad_maximum_fusion, ...), custom_call_target="tpu_custom_call" | custom-call | bytes 14155776 | tf_op jit(solution)/shard_map/load/pallas_call | solution.py:78
  57.0 1.3 %collective-permute-start.17 = (bf16[64,1536]{1,0:T(8,128)(2,1)S(1)}, bf16[64,1536]{1,0:T(8,128)(2,1)S(1)}, u32[]{:S(2)}, u32[]{:S(2)}) collective-permute-start(bf16[64,1536]{1,0:T(8,128)(2,1)S(1)} %pad_maximum_fusion.1.refs_1_.refs_2_), channel_id=1, source_target_pairs={{0,4},{2,6},{4,0},{6,2},{8,12},{10,14},{12,8},{14,10},{1,5},{3,7},... | collective-permute-start | bytes 589832 | tf_op jit(solution)/shard_map/ppermute | solution.py:348
  58.4 0.9 %collective-permute-start.15 = (bf16[64,1536]{1,0:T(8,128)(2,1)S(1)}, bf16[64,1536]{1,0:T(8,128)(2,1)S(1)}, u32[]{:S(2)}, u32[]{:S(2)}) collective-permute-start(bf16[64,1536]{1,0:T(8,128)(2,1)S(1)} %maximum_add_fusion.refs_0_), channel_id=1, source_target_pairs={{0,2},{2,0},{4,6},{6,4},{8,10},{10,8},{12,14},{14,12},{1,3},{3,1},... | collective-permute-start | bytes 589832 | tf_op jit(solution)/shard_map/ppermute | solution.py:348
  59.3 3.7 %load.3 = (bf16[512,768]{1,0:T(8,128)(2,1)S(1)}, bf16[512,768]{1,0:T(8,128)(2,1)S(1)}, bf16[512,768]{1,0:T(8,128)(2,1)S(1)}, bf16[512,768]{1,0:T(8,128)(2,1)S(1)...) custom-call(bf16[64,1536]{1,0:T(8,128)(2,1)S(1)} %maximum_add_fusion, ...), custom_call_target="tpu_custom_call" | custom-call | bytes 14155776 | tf_op jit(solution)/shard_map/load/pallas_call | solution.py:78
  63.3 1.2 %collective-permute-done.15.refs_1_ = bf16[64,1536]{1,0:T(8,128)(2,1)S(1)} collective-permute-done((bf16[64,1536]{1,0:T(8,128)(2,1)S(1)}, bf16[64,1536]{1,0:T(8,128)(2,1)S(1)}, u32[]{:S(2)}, u32[]{:S(2)}) %collective-permute-start.15) | collective-permute-done | bytes 196640 | tf_op jit(solution)/shard_map/ppermute | solution.py:348
  64.6 2.6 %project_out.1 = (f32[64,2304]{1,0:T(8,128)S(1)}, f32[64,2304]{1,0:T(8,128)S(1)}) custom-call(s32[2]{0:T(128)S(1)} %pad_add_fusion.ids_ref, bf16[64,1536]{1,0:T(8,128)(2,1)S(1)} %maximum_add_fusion.refs_0_, bf16[64,1536]{1,0:T(8,128)(2,1)S(1)} %collective-permute-done.15.refs_1_, bf16[64,1536]{1,0:T(8,128)(2,1)S(1)} %pad_maximum_fusion.1.refs_1_.refs_2_, ...), custom_call_target="tpu_custom_call" | custom-call | flops 1811939328 | bytes 15335424 | tf_op jit(solution)/shard_map/project_out/pallas_call | solution.py:319
  67.3 2.0 %collective-permute-done.18 = f32[64,2304]{1,0:T(8,128)S(1)} collective-permute-done((f32[64,2304]{1,0:T(8,128)S(1)}, f32[64,2304]{1,0:T(8,128)S(1)}, u32[]{:S(2)}, u32[]{:S(2)}) %collective-permute-start.18) | collective-permute-done | bytes 589856 | tf_op jit(solution)/shard_map/ppermute | solution.py:345
  69.3 0.8 %add_convert_fusion = bf16[64,2304]{1,0:T(8,128)(2,1)} fusion(f32[64,2304]{1,0:T(8,128)S(1)} %get-tuple-element.61, f32[64,2304]{1,0:T(8,128)S(1)} %collective-permute-done.18), kind=kLoop, calls=%fused_computation | loop fusion | flops 294912 | bytes 1474560 | tf_op jit(solution)/shard_map/convert_element_type | solution.py:406
  (46 shorter events, 2.5 us)
Async XLA Ops:
  0.0 1.9 %collective-permute-start = (bf16[64,2304]{1,0:T(8,128)(2,1)}, bf16[64,2304]{1,0:T(8,128)(2,1)S(1)}, u32[]{:S(2)}, u32[]{:S(2)}) collective-permute-start(bf16[64,2304]{1,0:T(8,128)(2,1)} %param.7), channel_id=1, source_target_pairs={{0,1},{1,0},{2,3},{3,2},{4,5},{5,4},{6,7},{7,6},{8,9},{9,8},{10,11... | collective-permute-start | bytes 884744 | tf_op jit(solution)/shard_map/ppermute | solution.py:345
  1.5 6.8 %copy-start.1 = (bf16[2304,512]{1,0:T(8,128)(2,1)S(1)}, bf16[2304,512]{1,0:T(8,128)(2,1)}, u32[]{:S(2)}) copy-start(bf16[2304,512]{1,0:T(8,128)(2,1)} %refs_0_.2) | copy-start | bytes 7077892
  5.3 10.4 %collective-permute-start.1 = (f32[64,1024]{1,0:T(8,128)S(1)}, f32[64,1024]{1,0:T(8,128)S(1)}, u32[]{:S(2)}, u32[]{:S(2)}) collective-permute-start(f32[64,1024]{1,0:T(8,128)S(1)} %get-tuple-element.35.refs_1_), channel_id=1, source_target_pairs={{0,4},{2,6},{4,0},{6,2},{8,12},{10,14},{12,8},{14,10},{1,5},{3,7},... | collective-permute-start | bytes 786440 | tf_op jit(solution)/shard_map/ppermute | solution.py:348
  13.7 24.4 %copy-start.2 = (s32[8]{0:T(128)S(1)}, s32[8]{0:T(128)}, u32[]{:S(2)}) copy-start(s32[8]{0:T(128)} %param.13) | copy-start | bytes 100
  13.7 12.8 %collective-permute-start.7 = (f32[64,1280]{1,0:T(8,128)S(1)}, f32[64,1280]{1,0:T(8,128)S(1)}, u32[]{:S(2)}, u32[]{:S(2)}) collective-permute-start(f32[64,1280]{1,0:T(8,128)S(1)} %get-tuple-element.39), channel_id=1, source_target_pairs={{0,2},{2,0},{4,6},{6,4},{8,10},{10,8},{12,14},{14,12},{1,3},{3,1},... | collective-permute-start | bytes 983048 | tf_op jit(solution)/shard_map/ppermute | solution.py:348
  15.3 10.6 %collective-permute-start.4 = (f32[64,1024]{1,0:T(8,128)S(1)}, f32[64,1024]{1,0:T(8,128)S(1)}, u32[]{:S(2)}, u32[]{:S(2)}) collective-permute-start(f32[64,1024]{1,0:T(8,128)S(1)} %get-tuple-element.37), channel_id=1, source_target_pairs={{0,4},{2,6},{4,0},{6,2},{8,12},{10,14},{12,8},{14,10},{1,5},{3,7},... | collective-permute-start | bytes 786440 | tf_op jit(solution)/shard_map/ppermute | solution.py:348
  15.8 10.9 %collective-permute-start.2 = (f32[32,1024]{1,0:T(8,128)S(1)}, f32[32,1024]{1,0:T(8,128)S(1)}, u32[]{:S(2)}, u32[]{:S(2)}) collective-permute-start(f32[32,1024]{1,0:T(8,128)S(1)} %slice.57), channel_id=1, source_target_pairs={{0,8},{2,10},{4,12},{6,14},{8,0},{10,2},{12,4},{14,6},{1,9},{3,11}... | collective-permute-start | bytes 393224 | tf_op jit(solution)/shard_map/ppermute | solution.py:348
  18.4 20.9 %copy-start = (bf16[8,1024,256]{2,1,0:T(8,128)(2,1)S(1)}, bf16[8,1024,256]{2,1,0:T(8,128)(2,1)}, u32[]{:S(2)}) copy-start(bf16[8,1024,256]{2,1,0:T(8,128)(2,1)} %refs_0_.3) | copy-start | bytes 12582916
  25.9 5.0 %collective-permute-start.5 = (f32[32,1024]{1,0:T(8,128)S(1)}, f32[32,1024]{1,0:T(8,128)S(1)}, u32[]{:S(2)}, u32[]{:S(2)}) collective-permute-start(f32[32,1024]{1,0:T(8,128)S(1)} %slice.61), channel_id=1, source_target_pairs={{0,2},{2,0},{4,6},{6,4},{8,10},{10,8},{12,14},{14,12},{1,3},{3,1},... | collective-permute-start | bytes 393224 | tf_op jit(solution)/shard_map/ppermute | solution.py:348
  26.6 5.9 %collective-permute-start.8 = (f32[32,1280]{1,0:T(8,128)S(1)}, f32[32,1280]{1,0:T(8,128)S(1)}, u32[]{:S(2)}, u32[]{:S(2)}) collective-permute-start(f32[32,1280]{1,0:T(8,128)S(1)} %slice.65), channel_id=1, source_target_pairs={{0,4},{2,6},{4,0},{6,2},{8,12},{10,14},{12,8},{14,10},{1,5},{3,7},... | collective-permute-start | bytes 491528 | tf_op jit(solution)/shard_map/ppermute | solution.py:348
  26.7 5.8 %collective-permute-start.3 = (f32[16,1024]{1,0:T(8,128)S(1)}, f32[16,1024]{1,0:T(8,128)S(1)}, u32[]{:S(2)}, u32[]{:S(2)}) collective-permute-start(f32[16,1024]{1,0:T(8,128)S(1)} %slice.59), channel_id=1, source_target_pairs={{0,2},{2,0},{4,6},{6,4},{8,10},{10,8},{12,14},{14,12},{1,3},{3,1},... | collective-permute-start | bytes 196616 | tf_op jit(solution)/shard_map/ppermute | solution.py:348
  31.0 5.7 %collective-permute-start.6 = (f32[16,1024]{1,0:T(8,128)S(1)}, f32[16,1024]{1,0:T(8,128)S(1)}, u32[]{:S(2)}, u32[]{:S(2)}) collective-permute-start(f32[16,1024]{1,0:T(8,128)S(1)} %slice.63), channel_id=1, source_target_pairs={{0,8},{2,10},{4,12},{6,14},{8,0},{10,2},{12,4},{14,6},{1,9},{3,11}... | collective-permute-start | bytes 196616 | tf_op jit(solution)/shard_map/ppermute | solution.py:348
  32.5 5.4 %collective-permute-start.9 = (f32[16,1280]{1,0:T(8,128)S(1)}, f32[16,1280]{1,0:T(8,128)S(1)}, u32[]{:S(2)}, u32[]{:S(2)}) collective-permute-start(f32[16,1280]{1,0:T(8,128)S(1)} %slice.67), channel_id=1, source_target_pairs={{0,8},{2,10},{4,12},{6,14},{8,0},{10,2},{12,4},{14,6},{1,9},{3,11}... | collective-permute-start | bytes 245768 | tf_op jit(solution)/shard_map/ppermute | solution.py:348
  38.0 1.3 %collective-permute-start.10 = (bf16[8,3328]{1,0:T(8,128)(2,1)S(1)}, bf16[8,3328]{1,0:T(8,128)(2,1)S(1)}, u32[]{:S(2)}, u32[]{:S(2)}) collective-permute-start(bf16[8,3328]{1,0:T(8,128)(2,1)S(1)} %get-tuple-element.63), channel_id=1, source_target_pairs={{0,1},{1,0},{2,3},{3,2},{4,5},{5,4},{6,7},{7,6},{8,9},{9,8},{10,11... | collective-permute-start | bytes 159752 | tf_op jit(solution)/shard_map/ppermute | solution.py:345
  43.6 1.3 %collective-permute-start.11 = (bf16[8,3072]{1,0:T(8,128)(2,1)S(1)}, bf16[8,3072]{1,0:T(8,128)(2,1)S(1)}, u32[]{:S(2)}, u32[]{:S(2)}) collective-permute-start(bf16[8,3072]{1,0:T(8,128)(2,1)S(1)} %get-tuple-element.41), channel_id=1, source_target_pairs={{0,1},{1,0},{2,3},{3,2},{4,5},{5,4},{6,7},{7,6},{8,9},{9,8},{10,11... | collective-permute-start | bytes 147464 | tf_op jit(solution)/shard_map/ppermute | solution.py:345
  44.9 4.5 %collective-permute-start.14 = (bf16[16,1536]{1,0:T(8,128)(2,1)S(1)}, bf16[16,1536]{1,0:T(8,128)(2,1)S(1)}, u32[]{:S(2)}, u32[]{:S(2)}) collective-permute-start(bf16[16,1536]{1,0:T(8,128)(2,1)S(1)} %get-tuple-element.65), channel_id=1, source_target_pairs={{0,2},{2,0},{4,6},{6,4},{8,10},{10,8},{12,14},{14,12},{1,3},{3,1},... | collective-permute-start | bytes 147464 | tf_op jit(solution)/shard_map/ppermute | solution.py:348
  47.4 5.6 %collective-permute-start.12 = (bf16[16,1536]{1,0:T(8,128)(2,1)S(1)}, bf16[16,1536]{1,0:T(8,128)(2,1)S(1)}, u32[]{:S(2)}, u32[]{:S(2)}) collective-permute-start(bf16[16,1536]{1,0:T(8,128)(2,1)S(1)} %get-tuple-element.66), channel_id=1, source_target_pairs={{0,8},{2,10},{4,12},{6,14},{8,0},{10,2},{12,4},{14,6},{1,9},{3,11}... | collective-permute-start | bytes 147464 | tf_op jit(solution)/shard_map/ppermute | solution.py:348
  49.5 7.6 %collective-permute-start.16 = (bf16[32,1536]{1,0:T(8,128)(2,1)S(1)}, bf16[32,1536]{1,0:T(8,128)(2,1)S(1)}, u32[]{:S(2)}, u32[]{:S(2)}) collective-permute-start(bf16[32,1536]{1,0:T(8,128)(2,1)S(1)} %pad_maximum_fusion.3.refs_1_), channel_id=1, source_target_pairs={{0,8},{2,10},{4,12},{6,14},{8,0},{10,2},{12,4},{14,6},{1,9},{3,11}... | collective-permute-start | bytes 294920 | tf_op jit(solution)/shard_map/ppermute | solution.py:348
  53.0 5.4 %collective-permute-start.13 = (bf16[32,1536]{1,0:T(8,128)(2,1)S(1)}, bf16[32,1536]{1,0:T(8,128)(2,1)S(1)}, u32[]{:S(2)}, u32[]{:S(2)}) collective-permute-start(bf16[32,1536]{1,0:T(8,128)(2,1)S(1)} %pad_maximum_fusion.2.refs_0_), channel_id=1, source_target_pairs={{0,4},{2,6},{4,0},{6,2},{8,12},{10,14},{12,8},{14,10},{1,5},{3,7},... | collective-permute-start | bytes 294920 | tf_op jit(solution)/shard_map/ppermute | solution.py:348
  57.0 6.3 %collective-permute-start.17 = (bf16[64,1536]{1,0:T(8,128)(2,1)S(1)}, bf16[64,1536]{1,0:T(8,128)(2,1)S(1)}, u32[]{:S(2)}, u32[]{:S(2)}) collective-permute-start(bf16[64,1536]{1,0:T(8,128)(2,1)S(1)} %pad_maximum_fusion.1.refs_1_.refs_2_), channel_id=1, source_target_pairs={{0,4},{2,6},{4,0},{6,2},{8,12},{10,14},{12,8},{14,10},{1,5},{3,7},... | collective-permute-start | bytes 589832 | tf_op jit(solution)/shard_map/ppermute | solution.py:348
  58.4 6.2 %collective-permute-start.15 = (bf16[64,1536]{1,0:T(8,128)(2,1)S(1)}, bf16[64,1536]{1,0:T(8,128)(2,1)S(1)}, u32[]{:S(2)}, u32[]{:S(2)}) collective-permute-start(bf16[64,1536]{1,0:T(8,128)(2,1)S(1)} %maximum_add_fusion.refs_0_), channel_id=1, source_target_pairs={{0,2},{2,0},{4,6},{6,4},{8,10},{10,8},{12,14},{14,12},{1,3},{3,1},... | collective-permute-start | bytes 589832 | tf_op jit(solution)/shard_map/ppermute | solution.py:348
  67.2 2.1 %collective-permute-start.18 = (f32[64,2304]{1,0:T(8,128)S(1)}, f32[64,2304]{1,0:T(8,128)S(1)}, u32[]{:S(2)}, u32[]{:S(2)}) collective-permute-start(f32[64,2304]{1,0:T(8,128)S(1)} %get-tuple-element.62), channel_id=1, source_target_pairs={{0,1},{1,0},{2,3},{3,2},{4,5},{5,4},{6,7},{7,6},{8,9},{9,8},{10,11... | collective-permute-start | bytes 1769480 | tf_op jit(solution)/shard_map/ppermute | solution.py:345

commit v17 on v16

--- a/solution.py
+++ b/solution.py
@@ -195,12 +195,10 @@
 
 
 def attend_kernel(kv_column, scalars_ref, own_q, other_q, *refs):
-    k_ref, v_hbm, own_out, other_out, v_ref, q_scr, o_scr, sems = refs
+    k_ref, refs = refs[0], refs[1:]
+    v_refs, (own_out, other_out, q_scr, o_scr) = refs[:-4], refs[-4:]
     core = scalars_ref[0]
     rows, positions, _ = k_ref.shape
-    copies = [pltpu.make_async_copy(v_hbm.at[row], v_ref.at[row], sems.at[row]) for row in range(rows)]
-    for copy in copies:
-        copy.start()
     at = 0
     for ref in (own_q, other_q):
         for column in range(0, ref.shape[1], DH):
@@ -245,10 +243,8 @@
             span = slice(at * total_heads, (at + 1) * total_heads)
             self_weight = self_weights[span, :1].astype(jnp.bfloat16).astype(jnp.float32)
             shares.append((weights[span].astype(jnp.bfloat16), self_weight))
-    for copy in copies:
-        copy.wait()
     for row, (weights, self_weight) in enumerate(shares):
-        total = jnp.dot(weights, v_ref[row], preferred_element_type=jnp.float32)
+        total = jnp.dot(weights, v_refs[row][...], preferred_element_type=jnp.float32)
         o_scr[row] = total + self_weight * new_values[row : row + 1]
     half = total_heads // 2
     for head in range(total_heads):
@@ -265,19 +261,17 @@
     return pl.pallas_call(
         functools.partial(attend_kernel, kv_column),
         out_shape=(out, out),
-        in_specs=[SMEM] + [VMEM] * 3 + [HBM],
+        in_specs=[SMEM] + [VMEM] * (3 + rows),
         out_specs=(VMEM, VMEM),
-        scratch_shapes=[pltpu.VMEM(values.shape, values.dtype)]
-        + [pltpu.VMEM((rows, heads, DH), jnp.float32)] * 2
-        + [pltpu.SemaphoreType.DMA((rows,))],
-        compiler_params=pltpu.CompilerParams(vmem_limit_bytes=49 * MIB),
+        scratch_shapes=[pltpu.VMEM((rows, heads, DH), jnp.float32)] * 2,
+        compiler_params=pltpu.CompilerParams(vmem_limit_bytes=44 * MIB),
         cost_estimate=pl.CostEstimate(
             flops=4 * rows * heads * positions * DH,
             bytes_accessed=4 * rows * positions * DH,
             transcendentals=rows * heads * positions,
         ),
         name="attend",
-    )(scalars, own_q, other_q, keys, values)
+    )(scalars, own_q, other_q, keys, *values)
 
 
 def output_kernel(orders, rows, columns, pieces, after, ids_ref, *refs):
@@ -368,6 +362,10 @@
         for i in (2, 0, 1):
             columns, order = plan[i]
             total = state[i][1] + moving[i]
+            if i == 0 and step == 0:
+                cuts = [(0, cut) for cut in cuts_of(value_cache)]
+                values, zero = load([value_cache], cuts, [state[2][0]], 46, total.shape[1])
+                total = total + zero
             if step + 1 < len(bits):
                 cut = total.shape[0] // 2
                 state[i] = (total[cut:], total[:cut])
@@ -380,7 +378,7 @@
     mine = lax.dynamic_slice_in_dim(total, core * own_rows, own_rows, 0).astype(jnp.bfloat16)
     give = lax.dynamic_slice_in_dim(total, (1 - core) * own_rows, own_rows, 0).astype(jnp.bfloat16)
     kv_column = sum(plan[i][0] for i in by_column[: by_column.index(0)])
-    own, other = attend(core, lengths, mine, swap(give), kv_column, key_cache, value_cache)
+    own, other = attend(core, lengths, mine, swap(give), kv_column, key_cache, values)
     got = swap(other)
     block = jnp.where(core == 0, jnp.concatenate([own, got]), jnp.concatenate([got, own]))
 

time: 70.3 us -> 67.5 us (0.960)
  starting transfers between devices: 21.1 us -> 17.9 us
  Pallas kernels: 22.5 us -> 23.4 us
    ppermute x15, starting transfers between devices: 20.3 us -> 17.1 us  [across(): return lax.ppermute(array, 'gx', [(g, g ^ mask) for g in range(n)])]
    pallas_call x2 -> x3, Pallas kernels: 6.84 us -> 9.06 us  [load(): pl.pallas_call(functools.partial(load_kernel, len(after), cuts, len(array...]
    pallas_call x1, Pallas kernels: 4.29 us -> 2.95 us  [attend(): pl.pallas_call(functools.partial(attend_kernel, kv_column), out_shape=(ou...]
  transfers between devices with their start and end apart: 19 -> 19, of which waited for: 13 -> 14; matrix products, arithmetic and copies ran while one was open for 2% -> 2% of each run, Pallas kernels for 17% -> 21%
where the time goes in v17:
time: 67.5 us; the launch traced here: 67.4 us
  waiting for transfers between devices  23.4 us (35%)
  Pallas kernels  23.4 us (35%)
  starting transfers between devices  17.9 us (27%)
  other arithmetic  2.26 us (3%)
    ppermute x15, waiting for transfers between devices, across(): return lax.ppermute(array, 'gx', [(g, g ^ mask) for g in range(n)])  18.8 us
    ppermute x15, starting transfers between devices, across(): return lax.ppermute(array, 'gx', [(g, g ^ mask) for g in range(n)])  17.1 us
    pallas_call x3, Pallas kernels, load(): pl.pallas_call(functools.partial(load_kernel, len(after), cuts, len(array...  9.06 us
    pallas_call x2, Pallas kernels, project(): pl.pallas_call(functools.partial(project_kernel, orders, rows, first, wid...  8.76 us
    ppermute x4, waiting for transfers between devices, swap(): return lax.ppermute(array, 'gy', [(0, 1), (1, 0)])  4.55 us
    pallas_call x1, Pallas kernels, attend(): pl.pallas_call(functools.partial(attend_kernel, kv_column), out_shape=(ou...  2.95 us
    pallas_call x1, Pallas kernels, project_out(): pl.pallas_call(functools.partial(output_kernel, orders, rows, columns, pi...  2.65 us
  transfers between devices with their start and end apart: 19, of which 14 were waited for; matrix products, arithmetic and copies ran while one was open for 2% of the time, Pallas kernels for 21%

profile of v17, /device:TPU:0, one launch (start us, length us, event | category | flops | bytes accessed | tf_op | source)
XLA Modules:
  0.0 67.4 jit_solution(7236162154670082020)
XLA Ops:
  0.5 1.0 %broadcast_select_fusion.own_ref = bf16[64,2304]{1,0:T(8,128)(2,1)S(1)} fusion(bf16[64,2304]{1,0:T(8,128)(2,1)} %param.7, pred[]{:T(512)S(6)} %lt.9), kind=kLoop, calls=%fused_computation.1 | loop fusion | flops 147456 | bytes 589825 | tf_op jit(solution)/shard_map/jit(_where)/select_n | solution.py:345
  1.9 3.4 %project.2 = (f32[64,1024]{1,0:T(8,128)S(1)}, f32[64,1024]{1,0:T(8,128)S(1)}) custom-call(s32[2]{0:T(128)S(1)} %pad_add_fusion.ids_ref, bf16[64,2304]{1,0:T(8,128)(2,1)S(1)} %broadcast_select_fusion.own_ref, bf16[64,2304]{1,0:T(8,128)(2,1)S(1)} %collective-permute-done.other_ref, bf16[2304,3072]{1,0:T(8,128)(2,1)} %w_ref.3), custom_call_target="tpu_custom_call" | custom-call | flops 603979776 | bytes 5242880 | tf_op jit(solution)/shard_map/project/pallas_call | solution.py:176
  5.3 3.0 %collective-permute-start.1 = (f32[64,1024]{1,0:T(8,128)S(1)}, f32[64,1024]{1,0:T(8,128)S(1)}, u32[]{:S(2)}, u32[]{:S(2)}) collective-permute-start(f32[64,1024]{1,0:T(8,128)S(1)} %get-tuple-element.44.refs_1_), channel_id=1, source_target_pairs={{0,4},{2,6},{4,0},{6,2},{8,12},{10,14},{12,8},{14,10},{1,5},{3,7},... | collective-permute-start | bytes 786440 | tf_op jit(solution)/shard_map/ppermute | solution.py:342
  8.3 5.3 %project.3 = (f32[64,1024]{1,0:T(8,128)S(1)}, f32[64,1024]{1,0:T(8,128)S(1)}, f32[64,1280]{1,0:T(8,128)S(1)}, f32[64,1280]{1,0:T(8,128)S(1)}) custom-call(s32[2]{0:T(128)S(1)} %pad_add_fusion.ids_ref, bf16[64,2304]{1,0:T(8,128)(2,1)S(1)} %broadcast_select_fusion.own_ref, bf16[64,2304]{1,0:T(8,128)(2,1)S(1)} %collective-permute-done.other_ref, ...), custom_call_target="tpu_custom_call" | custom-call | flops 1358954496 | bytes 11796480 | tf_op jit(solution)/shard_map/project/pallas_call | solution.py:176
  13.8 2.0 %collective-permute-start.7 = (f32[64,1280]{1,0:T(8,128)S(1)}, f32[64,1280]{1,0:T(8,128)S(1)}, u32[]{:S(2)}, u32[]{:S(2)}) collective-permute-start(f32[64,1280]{1,0:T(8,128)S(1)} %get-tuple-element.49), channel_id=1, source_target_pairs={{0,2},{2,0},{4,6},{6,4},{8,10},{10,8},{12,14},{14,12},{1,3},{3,1},... | collective-permute-start | bytes 983048 | tf_op jit(solution)/shard_map/ppermute | solution.py:342
  15.8 2.6 %collective-permute-start.2 = (f32[32,1024]{1,0:T(8,128)S(1)}, f32[32,1024]{1,0:T(8,128)S(1)}, u32[]{:S(2)}, u32[]{:S(2)}) collective-permute-start(f32[32,1024]{1,0:T(8,128)S(1)} %slice.57.refs_0_), channel_id=1, source_target_pairs={{0,8},{2,10},{4,12},{6,14},{8,0},{10,2},{12,4},{14,6},{1,9},{3,11}... | collective-permute-start | bytes 393224 | tf_op jit(solution)/shard_map/ppermute | solution.py:342
  18.4 2.2 %load.3 = (bf16[1024,256]{1,0:T(8,128)(2,1)S(1)}, bf16[1024,256]{1,0:T(8,128)(2,1)S(1)}, bf16[1024,256]{1,0:T(8,128)(2,1)S(1)}, bf16[1024,256]{1,0:T(8,128)(2,1)...) custom-call(f32[32,1024]{1,0:T(8,128)S(1)} %slice.57.refs_0_, ...), custom_call_target="tpu_custom_call" | custom-call | bytes 8388608 | tf_op jit(solution)/shard_map/load/pallas_call | solution.py:78
  20.7 3.9 %collective-permute-done.4 = f32[64,1024]{1,0:T(8,128)S(1)} collective-permute-done((f32[64,1024]{1,0:T(8,128)S(1)}, f32[64,1024]{1,0:T(8,128)S(1)}, u32[]{:S(2)}, u32[]{:S(2)}) %collective-permute-start.4) | collective-permute-done | bytes 262176 | tf_op jit(solution)/shard_map/ppermute | solution.py:342
  24.7 1.6 %collective-permute-start.5 = (f32[32,1024]{1,0:T(8,128)S(1)}, f32[32,1024]{1,0:T(8,128)S(1)}, u32[]{:S(2)}, u32[]{:S(2)}) collective-permute-start(f32[32,1024]{1,0:T(8,128)S(1)} %slice.61), channel_id=1, source_target_pairs={{0,2},{2,0},{4,6},{6,4},{8,10},{10,8},{12,14},{14,12},{1,3},{3,1},... | collective-permute-start | bytes 393224 | tf_op jit(solution)/shard_map/ppermute | solution.py:342
  26.4 0.6 collective-permute-start.3
  27.0 2.9 %collective-permute-done.5 = f32[32,1024]{1,0:T(8,128)S(1)} collective-permute-done((f32[32,1024]{1,0:T(8,128)S(1)}, f32[32,1024]{1,0:T(8,128)S(1)}, u32[]{:S(2)}, u32[]{:S(2)}) %collective-permute-start.5) | collective-permute-done | bytes 131104 | tf_op jit(solution)/shard_map/ppermute | solution.py:342
  29.9 1.1 %collective-permute-start.6 = (f32[16,1024]{1,0:T(8,128)S(1)}, f32[16,1024]{1,0:T(8,128)S(1)}, u32[]{:S(2)}, u32[]{:S(2)}) collective-permute-start(f32[16,1024]{1,0:T(8,128)S(1)} %slice.63), channel_id=1, source_target_pairs={{0,8},{2,10},{4,12},{6,14},{8,0},{10,2},{12,4},{14,6},{1,9},{3,11}... | collective-permute-start | bytes 196616 | tf_op jit(solution)/shard_map/ppermute | solution.py:342
  31.1 1.3 %collective-permute-done.8 = f32[32,1280]{1,0:T(8,128)S(1)} collective-permute-done((f32[32,1280]{1,0:T(8,128)S(1)}, f32[32,1280]{1,0:T(8,128)S(1)}, u32[]{:S(2)}, u32[]{:S(2)}) %collective-permute-start.8) | collective-permute-done | bytes 163872 | tf_op jit(solution)/shard_map/ppermute | solution.py:342
  32.4 1.2 %collective-permute-start.9 = (f32[16,1280]{1,0:T(8,128)S(1)}, f32[16,1280]{1,0:T(8,128)S(1)}, u32[]{:S(2)}, u32[]{:S(2)}) collective-permute-start(f32[16,1280]{1,0:T(8,128)S(1)} %slice.67), channel_id=1, source_target_pairs={{0,8},{2,10},{4,12},{6,14},{8,0},{10,2},{12,4},{14,6},{1,9},{3,11}... | collective-permute-start | bytes 245768 | tf_op jit(solution)/shard_map/ppermute | solution.py:342
  33.6 2.7 %collective-permute-done.6 = f32[16,1024]{1,0:T(8,128)S(1)} collective-permute-done((f32[16,1024]{1,0:T(8,128)S(1)}, f32[16,1024]{1,0:T(8,128)S(1)}, u32[]{:S(2)}, u32[]{:S(2)}) %collective-permute-start.6) | collective-permute-done | bytes 65568 | tf_op jit(solution)/shard_map/ppermute | solution.py:342
  36.3 2.2 %collective-permute-done.9 = f32[16,1280]{1,0:T(8,128)S(1)} collective-permute-done((f32[16,1280]{1,0:T(8,128)S(1)}, f32[16,1280]{1,0:T(8,128)S(1)}, u32[]{:S(2)}, u32[]{:S(2)}) %collective-permute-start.9) | collective-permute-done | bytes 81952 | tf_op jit(solution)/shard_map/ppermute | solution.py:342
  38.8 1.1 %collective-permute-done.10.other_q = bf16[8,3328]{1,0:T(8,128)(2,1)S(1)} collective-permute-done((bf16[8,3328]{1,0:T(8,128)(2,1)S(1)}, bf16[8,3328]{1,0:T(8,128)(2,1)S(1)}, u32[]{:S(2)}, u32[]{:S(2)}) %collective-permute-start.10) | collective-permute-done | bytes 53280 | tf_op jit(solution)/shard_map/ppermute | solution.py:339
  39.9 3.0 %attend.1 = (bf16[8,3072]{1,0:T(8,128)(2,1)S(1)}, bf16[8,3072]{1,0:T(8,128)(2,1)S(1)}) custom-call(s32[9]{0:T(128)S(1)} %pad_add_fusion.1.scalars_ref, bf16[8,3328]{1,0:T(8,128)(2,1)S(1)} %get-tuple-element.82.own_q, bf16[8,3328]{1,0:T(8,128)(2,1)S(1)} %collective-permute-done.10.other_q, bf16[8,1024,256]{2,1,0:T(8,128)(2,1)S(1)} %copy-done, ...), custom_call_target="tpu_custom_call" | custom-call | flops 201326592 | bytes 8388608 | tf_op jit(solution)/shard_map/attend/pallas_call | solution.py:261
  43.1 1.1 %collective-permute-done.11 = bf16[8,3072]{1,0:T(8,128)(2,1)S(1)} collective-permute-done((bf16[8,3072]{1,0:T(8,128)(2,1)S(1)}, bf16[8,3072]{1,0:T(8,128)(2,1)S(1)}, u32[]{:S(2)}, u32[]{:S(2)}) %collective-permute-start.11) | collective-permute-done | bytes 49184 | tf_op jit(solution)/shard_map/ppermute | solution.py:339
  44.3 1.4 %collective-permute-start.12 = (bf16[16,1536]{1,0:T(8,128)(2,1)S(1)}, bf16[16,1536]{1,0:T(8,128)(2,1)S(1)}, u32[]{:S(2)}, u32[]{:S(2)}) collective-permute-start(bf16[16,1536]{1,0:T(8,128)(2,1)S(1)} %get-tuple-element.84), channel_id=1, source_target_pairs={{0,8},{2,10},{4,12},{6,14},{8,0},{10,2},{12,4},{14,6},{1,9},{3,11}... | collective-permute-start | bytes 147464 | tf_op jit(solution)/shard_map/ppermute | solution.py:342
  45.7 2.7 %collective-permute-done.14 = bf16[16,1536]{1,0:T(8,128)(2,1)S(1)} collective-permute-done((bf16[16,1536]{1,0:T(8,128)(2,1)S(1)}, bf16[16,1536]{1,0:T(8,128)(2,1)S(1)}, u32[]{:S(2)}, u32[]{:S(2)}) %collective-permute-start.14) | collective-permute-done | bytes 49184 | tf_op jit(solution)/shard_map/ppermute | solution.py:342
  48.4 0.5 collective-permute-start.16
  48.9 1.2 %collective-permute-done.12 = bf16[16,1536]{1,0:T(8,128)(2,1)S(1)} collective-permute-done((bf16[16,1536]{1,0:T(8,128)(2,1)S(1)}, bf16[16,1536]{1,0:T(8,128)(2,1)S(1)}, u32[]{:S(2)}, u32[]{:S(2)}) %collective-permute-start.12) | collective-permute-done | bytes 49184 | tf_op jit(solution)/shard_map/ppermute | solution.py:342
  50.1 1.1 %collective-permute-start.13 = (bf16[32,1536]{1,0:T(8,128)(2,1)S(1)}, bf16[32,1536]{1,0:T(8,128)(2,1)S(1)}, u32[]{:S(2)}, u32[]{:S(2)}) collective-permute-start(bf16[32,1536]{1,0:T(8,128)(2,1)S(1)} %pad_maximum_fusion.2.refs_0_), channel_id=1, source_target_pairs={{0,4},{2,6},{4,0},{6,2},{8,12},{10,14},{12,8},{14,10},{1,5},{3,7},... | collective-permute-start | bytes 294920 | tf_op jit(solution)/shard_map/ppermute | solution.py:342
  51.2 3.1 %load.4 = (bf16[512,768]{1,0:T(8,128)(2,1)S(1)}, bf16[512,768]{1,0:T(8,128)(2,1)S(1)}, bf16[512,768]{1,0:T(8,128)(2,1)S(1)}, bf16[512,768]{1,0:T(8,128)(2,1)S(1)...) custom-call(bf16[32,1536]{1,0:T(8,128)(2,1)S(1)} %pad_maximum_fusion, ...), custom_call_target="tpu_custom_call" | custom-call | bytes 14155776 | tf_op jit(solution)/shard_map/load/pallas_call | solution.py:78
  54.7 0.7 %collective-permute-start.17 = (bf16[64,1536]{1,0:T(8,128)(2,1)S(1)}, bf16[64,1536]{1,0:T(8,128)(2,1)S(1)}, u32[]{:S(2)}, u32[]{:S(2)}) collective-permute-start(bf16[64,1536]{1,0:T(8,128)(2,1)S(1)} %pad_maximum_fusion.1.refs_1_.refs_2_), channel_id=1, source_target_pairs={{0,4},{2,6},{4,0},{6,2},{8,12},{10,14},{12,8},{14,10},{1,5},{3,7},... | collective-permute-start | bytes 589832 | tf_op jit(solution)/shard_map/ppermute | solution.py:342
  55.8 1.1 %collective-permute-start.15 = (bf16[64,1536]{1,0:T(8,128)(2,1)S(1)}, bf16[64,1536]{1,0:T(8,128)(2,1)S(1)}, u32[]{:S(2)}, u32[]{:S(2)}) collective-permute-start(bf16[64,1536]{1,0:T(8,128)(2,1)S(1)} %maximum_add_fusion.refs_0_), channel_id=1, source_target_pairs={{0,2},{2,0},{4,6},{6,4},{8,10},{10,8},{12,14},{14,12},{1,3},{3,1},... | collective-permute-start | bytes 589832 | tf_op jit(solution)/shard_map/ppermute | solution.py:342
  56.9 3.7 %load.5 = (bf16[512,768]{1,0:T(8,128)(2,1)S(1)}, bf16[512,768]{1,0:T(8,128)(2,1)S(1)}, bf16[512,768]{1,0:T(8,128)(2,1)S(1)}, bf16[512,768]{1,0:T(8,128)(2,1)S(1)...) custom-call(bf16[64,1536]{1,0:T(8,128)(2,1)S(1)} %maximum_add_fusion, ...), custom_call_target="tpu_custom_call" | custom-call | bytes 14155776 | tf_op jit(solution)/shard_map/load/pallas_call | solution.py:78
  60.6 1.2 %collective-permute-done.15.refs_1_ = bf16[64,1536]{1,0:T(8,128)(2,1)S(1)} collective-permute-done((bf16[64,1536]{1,0:T(8,128)(2,1)S(1)}, bf16[64,1536]{1,0:T(8,128)(2,1)S(1)}, u32[]{:S(2)}, u32[]{:S(2)}) %collective-permute-start.15) | collective-permute-done | bytes 196640 | tf_op jit(solution)/shard_map/ppermute | solution.py:342
  61.8 2.6 %project_out.1 = (f32[64,2304]{1,0:T(8,128)S(1)}, f32[64,2304]{1,0:T(8,128)S(1)}) custom-call(s32[2]{0:T(128)S(1)} %pad_add_fusion.ids_ref, bf16[64,1536]{1,0:T(8,128)(2,1)S(1)} %maximum_add_fusion.refs_0_, bf16[64,1536]{1,0:T(8,128)(2,1)S(1)} %collective-permute-done.15.refs_1_, bf16[64,1536]{1,0:T(8,128)(2,1)S(1)} %pad_maximum_fusion.1.refs_1_.refs_2_, ...), custom_call_target="tpu_custom_call" | custom-call | flops 1811939328 | bytes 15335424 | tf_op jit(solution)/shard_map/project_out/pallas_call | solution.py:313
  64.6 2.0 %collective-permute-done.18 = f32[64,2304]{1,0:T(8,128)S(1)} collective-permute-done((f32[64,2304]{1,0:T(8,128)S(1)}, f32[64,2304]{1,0:T(8,128)S(1)}, u32[]{:S(2)}, u32[]{:S(2)}) %collective-permute-start.18) | collective-permute-done | bytes 589856 | tf_op jit(solution)/shard_map/ppermute | solution.py:339
  66.6 0.8 %add_convert_fusion = bf16[64,2304]{1,0:T(8,128)(2,1)} fusion(f32[64,2304]{1,0:T(8,128)S(1)} %get-tuple-element.79, f32[64,2304]{1,0:T(8,128)S(1)} %collective-permute-done.18), kind=kLoop, calls=%fused_computation | loop fusion | flops 294912 | bytes 1474560 | tf_op jit(solution)/shard_map/convert_element_type | solution.py:404
  (47 shorter events, 2.6 us)
Async XLA Ops:
  0.0 1.9 %collective-permute-start = (bf16[64,2304]{1,0:T(8,128)(2,1)}, bf16[64,2304]{1,0:T(8,128)(2,1)S(1)}, u32[]{:S(2)}, u32[]{:S(2)}) collective-permute-start(bf16[64,2304]{1,0:T(8,128)(2,1)} %param.7), channel_id=1, source_target_pairs={{0,1},{1,0},{2,3},{3,2},{4,5},{5,4},{6,7},{7,6},{8,9},{9,8},{10,11... | collective-permute-start | bytes 884744 | tf_op jit(solution)/shard_map/ppermute | solution.py:339
  1.5 6.8 %copy-start.1 = (bf16[2304,512]{1,0:T(8,128)(2,1)S(1)}, bf16[2304,512]{1,0:T(8,128)(2,1)}, u32[]{:S(2)}) copy-start(bf16[2304,512]{1,0:T(8,128)(2,1)} %refs_0_.2) | copy-start | bytes 7077892
  5.3 10.4 %collective-permute-start.1 = (f32[64,1024]{1,0:T(8,128)S(1)}, f32[64,1024]{1,0:T(8,128)S(1)}, u32[]{:S(2)}, u32[]{:S(2)}) collective-permute-start(f32[64,1024]{1,0:T(8,128)S(1)} %get-tuple-element.44.refs_1_), channel_id=1, source_target_pairs={{0,4},{2,6},{4,0},{6,2},{8,12},{10,14},{12,8},{14,10},{1,5},{3,7},... | collective-permute-start | bytes 786440 | tf_op jit(solution)/shard_map/ppermute | solution.py:342
  13.7 10.9 %collective-permute-start.4 = (f32[64,1024]{1,0:T(8,128)S(1)}, f32[64,1024]{1,0:T(8,128)S(1)}, u32[]{:S(2)}, u32[]{:S(2)}) collective-permute-start(f32[64,1024]{1,0:T(8,128)S(1)} %get-tuple-element.46), channel_id=1, source_target_pairs={{0,4},{2,6},{4,0},{6,2},{8,12},{10,14},{12,8},{14,10},{1,5},{3,7},... | collective-permute-start | bytes 786440 | tf_op jit(solution)/shard_map/ppermute | solution.py:342
  13.8 12.5 %collective-permute-start.7 = (f32[64,1280]{1,0:T(8,128)S(1)}, f32[64,1280]{1,0:T(8,128)S(1)}, u32[]{:S(2)}, u32[]{:S(2)}) collective-permute-start(f32[64,1280]{1,0:T(8,128)S(1)} %get-tuple-element.49), channel_id=1, source_target_pairs={{0,2},{2,0},{4,6},{6,4},{8,10},{10,8},{12,14},{14,12},{1,3},{3,1},... | collective-permute-start | bytes 983048 | tf_op jit(solution)/shard_map/ppermute | solution.py:342
  15.8 22.9 %copy-start.2 = (s32[8]{0:T(128)S(1)}, s32[8]{0:T(128)}, u32[]{:S(2)}) copy-start(s32[8]{0:T(128)} %param.13) | copy-start | bytes 100
  15.8 24.1 %copy-start = (bf16[8,1024,256]{2,1,0:T(8,128)(2,1)S(1)}, bf16[8,1024,256]{2,1,0:T(8,128)(2,1)}, u32[]{:S(2)}) copy-start(bf16[8,1024,256]{2,1,0:T(8,128)(2,1)} %refs_0_.3) | copy-start | bytes 12582916
  15.8 10.6 %collective-permute-start.2 = (f32[32,1024]{1,0:T(8,128)S(1)}, f32[32,1024]{1,0:T(8,128)S(1)}, u32[]{:S(2)}, u32[]{:S(2)}) collective-permute-start(f32[32,1024]{1,0:T(8,128)S(1)} %slice.57.refs_0_), channel_id=1, source_target_pairs={{0,8},{2,10},{4,12},{6,14},{8,0},{10,2},{12,4},{14,6},{1,9},{3,11}... | collective-permute-start | bytes 393224 | tf_op jit(solution)/shard_map/ppermute | solution.py:342
  24.7 5.2 %collective-permute-start.5 = (f32[32,1024]{1,0:T(8,128)S(1)}, f32[32,1024]{1,0:T(8,128)S(1)}, u32[]{:S(2)}, u32[]{:S(2)}) collective-permute-start(f32[32,1024]{1,0:T(8,128)S(1)} %slice.61), channel_id=1, source_target_pairs={{0,2},{2,0},{4,6},{6,4},{8,10},{10,8},{12,14},{14,12},{1,3},{3,1},... | collective-permute-start | bytes 393224 | tf_op jit(solution)/shard_map/ppermute | solution.py:342
  26.3 6.1 %collective-permute-start.8 = (f32[32,1280]{1,0:T(8,128)S(1)}, f32[32,1280]{1,0:T(8,128)S(1)}, u32[]{:S(2)}, u32[]{:S(2)}) collective-permute-start(f32[32,1280]{1,0:T(8,128)S(1)} %slice.65), channel_id=1, source_target_pairs={{0,4},{2,6},{4,0},{6,2},{8,12},{10,14},{12,8},{14,10},{1,5},{3,7},... | collective-permute-start | bytes 491528 | tf_op jit(solution)/shard_map/ppermute | solution.py:342
  26.4 4.6 %collective-permute-start.3 = (f32[16,1024]{1,0:T(8,128)S(1)}, f32[16,1024]{1,0:T(8,128)S(1)}, u32[]{:S(2)}, u32[]{:S(2)}) collective-permute-start(f32[16,1024]{1,0:T(8,128)S(1)} %slice.59), channel_id=1, source_target_pairs={{0,2},{2,0},{4,6},{6,4},{8,10},{10,8},{12,14},{14,12},{1,3},{3,1},... | collective-permute-start | bytes 196616 | tf_op jit(solution)/shard_map/ppermute | solution.py:342
  29.9 6.4 %collective-permute-start.6 = (f32[16,1024]{1,0:T(8,128)S(1)}, f32[16,1024]{1,0:T(8,128)S(1)}, u32[]{:S(2)}, u32[]{:S(2)}) collective-permute-start(f32[16,1024]{1,0:T(8,128)S(1)} %slice.63), channel_id=1, source_target_pairs={{0,8},{2,10},{4,12},{6,14},{8,0},{10,2},{12,4},{14,6},{1,9},{3,11}... | collective-permute-start | bytes 196616 | tf_op jit(solution)/shard_map/ppermute | solution.py:342
  32.4 6.1 %collective-permute-start.9 = (f32[16,1280]{1,0:T(8,128)S(1)}, f32[16,1280]{1,0:T(8,128)S(1)}, u32[]{:S(2)}, u32[]{:S(2)}) collective-permute-start(f32[16,1280]{1,0:T(8,128)S(1)} %slice.67), channel_id=1, source_target_pairs={{0,8},{2,10},{4,12},{6,14},{8,0},{10,2},{12,4},{14,6},{1,9},{3,11}... | collective-permute-start | bytes 245768 | tf_op jit(solution)/shard_map/ppermute | solution.py:342
  38.6 1.3 %collective-permute-start.10 = (bf16[8,3328]{1,0:T(8,128)(2,1)S(1)}, bf16[8,3328]{1,0:T(8,128)(2,1)S(1)}, u32[]{:S(2)}, u32[]{:S(2)}) collective-permute-start(bf16[8,3328]{1,0:T(8,128)(2,1)S(1)} %get-tuple-element.81), channel_id=1, source_target_pairs={{0,1},{1,0},{2,3},{3,2},{4,5},{5,4},{6,7},{7,6},{8,9},{9,8},{10,11... | collective-permute-start | bytes 159752 | tf_op jit(solution)/shard_map/ppermute | solution.py:339
  42.9 1.3 %collective-permute-start.11 = (bf16[8,3072]{1,0:T(8,128)(2,1)S(1)}, bf16[8,3072]{1,0:T(8,128)(2,1)S(1)}, u32[]{:S(2)}, u32[]{:S(2)}) collective-permute-start(bf16[8,3072]{1,0:T(8,128)(2,1)S(1)} %get-tuple-element.59), channel_id=1, source_target_pairs={{0,1},{1,0},{2,3},{3,2},{4,5},{5,4},{6,7},{7,6},{8,9},{9,8},{10,11... | collective-permute-start | bytes 147464 | tf_op jit(solution)/shard_map/ppermute | solution.py:339
  44.2 4.2 %collective-permute-start.14 = (bf16[16,1536]{1,0:T(8,128)(2,1)S(1)}, bf16[16,1536]{1,0:T(8,128)(2,1)S(1)}, u32[]{:S(2)}, u32[]{:S(2)}) collective-permute-start(bf16[16,1536]{1,0:T(8,128)(2,1)S(1)} %get-tuple-element.83), channel_id=1, source_target_pairs={{0,2},{2,0},{4,6},{6,4},{8,10},{10,8},{12,14},{14,12},{1,3},{3,1},... | collective-permute-start | bytes 147464 | tf_op jit(solution)/shard_map/ppermute | solution.py:342
  44.3 5.8 %collective-permute-start.12 = (bf16[16,1536]{1,0:T(8,128)(2,1)S(1)}, bf16[16,1536]{1,0:T(8,128)(2,1)S(1)}, u32[]{:S(2)}, u32[]{:S(2)}) collective-permute-start(bf16[16,1536]{1,0:T(8,128)(2,1)S(1)} %get-tuple-element.84), channel_id=1, source_target_pairs={{0,8},{2,10},{4,12},{6,14},{8,0},{10,2},{12,4},{14,6},{1,9},{3,11}... | collective-permute-start | bytes 147464 | tf_op jit(solution)/shard_map/ppermute | solution.py:342
  48.4 6.3 %collective-permute-start.16 = (bf16[32,1536]{1,0:T(8,128)(2,1)S(1)}, bf16[32,1536]{1,0:T(8,128)(2,1)S(1)}, u32[]{:S(2)}, u32[]{:S(2)}) collective-permute-start(bf16[32,1536]{1,0:T(8,128)(2,1)S(1)} %pad_maximum_fusion.3.refs_1_), channel_id=1, source_target_pairs={{0,8},{2,10},{4,12},{6,14},{8,0},{10,2},{12,4},{14,6},{1,9},{3,11}... | collective-permute-start | bytes 294920 | tf_op jit(solution)/shard_map/ppermute | solution.py:342
  50.1 5.6 %collective-permute-start.13 = (bf16[32,1536]{1,0:T(8,128)(2,1)S(1)}, bf16[32,1536]{1,0:T(8,128)(2,1)S(1)}, u32[]{:S(2)}, u32[]{:S(2)}) collective-permute-start(bf16[32,1536]{1,0:T(8,128)(2,1)S(1)} %pad_maximum_fusion.2.refs_0_), channel_id=1, source_target_pairs={{0,4},{2,6},{4,0},{6,2},{8,12},{10,14},{12,8},{14,10},{1,5},{3,7},... | collective-permute-start | bytes 294920 | tf_op jit(solution)/shard_map/ppermute | solution.py:342
  54.7 5.9 %collective-permute-start.17 = (bf16[64,1536]{1,0:T(8,128)(2,1)S(1)}, bf16[64,1536]{1,0:T(8,128)(2,1)S(1)}, u32[]{:S(2)}, u32[]{:S(2)}) collective-permute-start(bf16[64,1536]{1,0:T(8,128)(2,1)S(1)} %pad_maximum_fusion.1.refs_1_.refs_2_), channel_id=1, source_target_pairs={{0,4},{2,6},{4,0},{6,2},{8,12},{10,14},{12,8},{14,10},{1,5},{3,7},... | collective-permute-start | bytes 589832 | tf_op jit(solution)/shard_map/ppermute | solution.py:342
  55.8 6.1 %collective-permute-start.15 = (bf16[64,1536]{1,0:T(8,128)(2,1)S(1)}, bf16[64,1536]{1,0:T(8,128)(2,1)S(1)}, u32[]{:S(2)}, u32[]{:S(2)}) collective-permute-start(bf16[64,1536]{1,0:T(8,128)(2,1)S(1)} %maximum_add_fusion.refs_0_), channel_id=1, source_target_pairs={{0,2},{2,0},{4,6},{6,4},{8,10},{10,8},{12,14},{14,12},{1,3},{3,1},... | collective-permute-start | bytes 589832 | tf_op jit(solution)/shard_map/ppermute | solution.py:342
  64.5 2.1 %collective-permute-start.18 = (f32[64,2304]{1,0:T(8,128)S(1)}, f32[64,2304]{1,0:T(8,128)S(1)}, u32[]{:S(2)}, u32[]{:S(2)}) collective-permute-start(f32[64,2304]{1,0:T(8,128)S(1)} %get-tuple-element.80), channel_id=1, source_target_pairs={{0,1},{1,0},{2,3},{3,2},{4,5},{5,4},{6,7},{7,6},{8,9},{9,8},{10,11... | collective-permute-start | bytes 1769480 | tf_op jit(solution)/shard_map/ppermute | solution.py:339

commit v18 on v15

--- a/solution.py
+++ b/solution.py
@@ -195,12 +195,10 @@
 
 
 def attend_kernel(kv_column, scalars_ref, own_q, other_q, *refs):
-    k_ref, v_hbm, own_out, other_out, v_ref, q_scr, o_scr, s_scr, sems = refs
+    k_ref, refs = refs[0], refs[1:]
+    v_refs, (own_out, other_out, q_scr, o_scr, s_scr) = refs[:-5], refs[-5:]
     core = scalars_ref[0]
     rows, positions, _ = k_ref.shape
-    copies = [pltpu.make_async_copy(v_hbm.at[row], v_ref.at[row], sems.at[row]) for row in range(rows)]
-    for copy in copies:
-        copy.start()
     at = 0
     for ref in (own_q, other_q):
         for column in range(0, ref.shape[1], DH):
@@ -232,11 +230,9 @@
     inverse = 1.0 / (jnp.sum(raised, axis=2, keepdims=True) + self_raised)
     s_scr[...] = raised * inverse
     self_weight = (self_raised * inverse).astype(jnp.bfloat16).astype(jnp.float32)
-    for copy in copies:
-        copy.wait()
     for row in range(rows):
         weights = s_scr[row].astype(jnp.bfloat16)
-        total = jnp.dot(weights, v_ref[row], preferred_element_type=jnp.float32)
+        total = jnp.dot(weights, v_refs[row][...], preferred_element_type=jnp.float32)
         o_scr[row] = total + self_weight[row] * new_values[row : row + 1]
     half = total_heads // 2
     for head in range(total_heads):
@@ -253,20 +249,18 @@
     return pl.pallas_call(
         functools.partial(attend_kernel, kv_column),
         out_shape=(out, out),
-        in_specs=[SMEM] + [VMEM] * 3 + [HBM],
+        in_specs=[SMEM] + [VMEM] * (3 + rows),
         out_specs=(VMEM, VMEM),
-        scratch_shapes=[pltpu.VMEM(values.shape, values.dtype)]
-        + [pltpu.VMEM((rows, heads, DH), jnp.float32)] * 2
-        + [pltpu.VMEM((rows, heads, positions), jnp.float32)]
-        + [pltpu.SemaphoreType.DMA((rows,))],
-        compiler_params=pltpu.CompilerParams(vmem_limit_bytes=49 * MIB),
+        scratch_shapes=[pltpu.VMEM((rows, heads, DH), jnp.float32)] * 2
+        + [pltpu.VMEM((rows, heads, positions), jnp.float32)],
+        compiler_params=pltpu.CompilerParams(vmem_limit_bytes=44 * MIB),
         cost_estimate=pl.CostEstimate(
             flops=4 * rows * heads * positions * DH,
             bytes_accessed=4 * rows * positions * DH,
             transcendentals=rows * heads * positions,
         ),
         name="attend",
-    )(scalars, own_q, other_q, keys, values)
+    )(scalars, own_q, other_q, keys, *values)
 
 
 def output_kernel(orders, rows, columns, pieces, after, ids_ref, *refs):
@@ -357,6 +351,10 @@
         for i in (2, 0, 1):
             columns, order = plan[i]
             total = state[i][1] + moving[i]
+            if i == 0 and step == 0:
+                cuts = [(0, cut) for cut in cuts_of(value_cache)]
+                values, zero = load([value_cache], cuts, [state[2][0]], 46, total.shape[1])
+                total = total + zero
             if step + 1 < len(bits):
                 cut = total.shape[0] // 2
                 state[i] = (total[cut:], total[:cut])
@@ -369,7 +367,7 @@
     mine = lax.dynamic_slice_in_dim(total, core * own_rows, own_rows, 0).astype(jnp.bfloat16)
     give = lax.dynamic_slice_in_dim(total, (1 - core) * own_rows, own_rows, 0).astype(jnp.bfloat16)
     kv_column = sum(plan[i][0] for i in by_column[: by_column.index(0)])
-    own, other = attend(core, lengths, mine, swap(give), kv_column, key_cache, value_cache)
+    own, other = attend(core, lengths, mine, swap(give), kv_column, key_cache, values)
     got = swap(other)
     block = jnp.where(core == 0, jnp.concatenate([own, got]), jnp.concatenate([got, own]))
 

time: 70.3 us -> 67.4 us (0.959)
  starting transfers between devices: 21.1 us -> 17.9 us
    ppermute x15, starting transfers between devices: 20.3 us -> 17.1 us  [across(): return lax.ppermute(array, 'gx', [(g, g ^ mask) for g in range(n)])]
    pallas_call x2 -> x3, Pallas kernels: 6.84 us -> 9.06 us  [load(): pl.pallas_call(functools.partial(load_kernel, len(after), cuts, len(array...]
    pallas_call x1, Pallas kernels: 4.32 us -> 2.87 us  [attend(): pl.pallas_call(functools.partial(attend_kernel, kv_column), out_shape=(ou...]
  transfers between devices with their start and end apart: 19 -> 19, of which waited for: 13 -> 14; matrix products, arithmetic and copies ran while one was open for 2% -> 2% of each run, Pallas kernels for 17% -> 21%
where the time goes in v18:
time: 67.4 us; the launch traced here: 67.3 us
  waiting for transfers between devices  23.4 us (35%)
  Pallas kernels  23.3 us (35%)
  starting transfers between devices  17.9 us (27%)
  other arithmetic  2.26 us (3%)
    ppermute x15, waiting for transfers between devices, across(): return lax.ppermute(array, 'gx', [(g, g ^ mask) for g in range(n)])  18.8 us
    ppermute x15, starting transfers between devices, across(): return lax.ppermute(array, 'gx', [(g, g ^ mask) for g in range(n)])  17.1 us
    pallas_call x3, Pallas kernels, load(): pl.pallas_call(functools.partial(load_kernel, len(after), cuts, len(array...  9.06 us
    pallas_call x2, Pallas kernels, project(): pl.pallas_call(functools.partial(project_kernel, orders, rows, first, wid...  8.76 us
    ppermute x4, waiting for transfers between devices, swap(): return lax.ppermute(array, 'gy', [(0, 1), (1, 0)])  4.55 us
    pallas_call x1, Pallas kernels, attend(): pl.pallas_call(functools.partial(attend_kernel, kv_column), out_shape=(ou...  2.87 us
    pallas_call x1, Pallas kernels, project_out(): pl.pallas_call(functools.partial(output_kernel, orders, rows, columns, pi...  2.65 us
  transfers between devices with their start and end apart: 19, of which 14 were waited for; matrix products, arithmetic and copies ran while one was open for 2% of the time, Pallas kernels for 21%

profile of v18, /device:TPU:0, one launch (start us, length us, event | category | flops | bytes accessed | tf_op | source)
XLA Modules:
  0.0 67.3 jit_solution(6384511977482645035)
XLA Ops:
  0.5 1.0 %broadcast_select_fusion.own_ref = bf16[64,2304]{1,0:T(8,128)(2,1)S(1)} fusion(bf16[64,2304]{1,0:T(8,128)(2,1)} %param.7, pred[]{:T(512)S(6)} %lt.9), kind=kLoop, calls=%fused_computation.1 | loop fusion | flops 147456 | bytes 589825 | tf_op jit(solution)/shard_map/jit(_where)/select_n | solution.py:334
  1.9 3.4 %project.2 = (f32[64,1024]{1,0:T(8,128)S(1)}, f32[64,1024]{1,0:T(8,128)S(1)}) custom-call(s32[2]{0:T(128)S(1)} %pad_add_fusion.ids_ref, bf16[64,2304]{1,0:T(8,128)(2,1)S(1)} %broadcast_select_fusion.own_ref, bf16[64,2304]{1,0:T(8,128)(2,1)S(1)} %collective-permute-done.other_ref, bf16[2304,3072]{1,0:T(8,128)(2,1)} %w_ref.3), custom_call_target="tpu_custom_call" | custom-call | flops 603979776 | bytes 5242880 | tf_op jit(solution)/shard_map/project/pallas_call | solution.py:176
  5.3 3.0 %collective-permute-start.1 = (f32[64,1024]{1,0:T(8,128)S(1)}, f32[64,1024]{1,0:T(8,128)S(1)}, u32[]{:S(2)}, u32[]{:S(2)}) collective-permute-start(f32[64,1024]{1,0:T(8,128)S(1)} %get-tuple-element.44.refs_1_), channel_id=1, source_target_pairs={{0,4},{2,6},{4,0},{6,2},{8,12},{10,14},{12,8},{14,10},{1,5},{3,7},... | collective-permute-start | bytes 786440 | tf_op jit(solution)/shard_map/ppermute | solution.py:331
  8.3 5.3 %project.3 = (f32[64,1024]{1,0:T(8,128)S(1)}, f32[64,1024]{1,0:T(8,128)S(1)}, f32[64,1280]{1,0:T(8,128)S(1)}, f32[64,1280]{1,0:T(8,128)S(1)}) custom-call(s32[2]{0:T(128)S(1)} %pad_add_fusion.ids_ref, bf16[64,2304]{1,0:T(8,128)(2,1)S(1)} %broadcast_select_fusion.own_ref, bf16[64,2304]{1,0:T(8,128)(2,1)S(1)} %collective-permute-done.other_ref, ...), custom_call_target="tpu_custom_call" | custom-call | flops 1358954496 | bytes 11796480 | tf_op jit(solution)/shard_map/project/pallas_call | solution.py:176
  13.8 2.0 %collective-permute-start.7 = (f32[64,1280]{1,0:T(8,128)S(1)}, f32[64,1280]{1,0:T(8,128)S(1)}, u32[]{:S(2)}, u32[]{:S(2)}) collective-permute-start(f32[64,1280]{1,0:T(8,128)S(1)} %get-tuple-element.49), channel_id=1, source_target_pairs={{0,2},{2,0},{4,6},{6,4},{8,10},{10,8},{12,14},{14,12},{1,3},{3,1},... | collective-permute-start | bytes 983048 | tf_op jit(solution)/shard_map/ppermute | solution.py:331
  15.8 2.6 %collective-permute-start.2 = (f32[32,1024]{1,0:T(8,128)S(1)}, f32[32,1024]{1,0:T(8,128)S(1)}, u32[]{:S(2)}, u32[]{:S(2)}) collective-permute-start(f32[32,1024]{1,0:T(8,128)S(1)} %slice.57.refs_0_), channel_id=1, source_target_pairs={{0,8},{2,10},{4,12},{6,14},{8,0},{10,2},{12,4},{14,6},{1,9},{3,11}... | collective-permute-start | bytes 393224 | tf_op jit(solution)/shard_map/ppermute | solution.py:331
  18.4 2.2 %load.3 = (bf16[1024,256]{1,0:T(8,128)(2,1)S(1)}, bf16[1024,256]{1,0:T(8,128)(2,1)S(1)}, bf16[1024,256]{1,0:T(8,128)(2,1)S(1)}, bf16[1024,256]{1,0:T(8,128)(2,1)...) custom-call(f32[32,1024]{1,0:T(8,128)S(1)} %slice.57.refs_0_, ...), custom_call_target="tpu_custom_call" | custom-call | bytes 8388608 | tf_op jit(solution)/shard_map/load/pallas_call | solution.py:78
  20.7 3.9 %collective-permute-done.4 = f32[64,1024]{1,0:T(8,128)S(1)} collective-permute-done((f32[64,1024]{1,0:T(8,128)S(1)}, f32[64,1024]{1,0:T(8,128)S(1)}, u32[]{:S(2)}, u32[]{:S(2)}) %collective-permute-start.4) | collective-permute-done | bytes 262176 | tf_op jit(solution)/shard_map/ppermute | solution.py:331
  24.7 1.6 %collective-permute-start.5 = (f32[32,1024]{1,0:T(8,128)S(1)}, f32[32,1024]{1,0:T(8,128)S(1)}, u32[]{:S(2)}, u32[]{:S(2)}) collective-permute-start(f32[32,1024]{1,0:T(8,128)S(1)} %slice.61), channel_id=1, source_target_pairs={{0,2},{2,0},{4,6},{6,4},{8,10},{10,8},{12,14},{14,12},{1,3},{3,1},... | collective-permute-start | bytes 393224 | tf_op jit(solution)/shard_map/ppermute | solution.py:331
  26.4 0.6 collective-permute-start.3
  27.0 2.9 %collective-permute-done.5 = f32[32,1024]{1,0:T(8,128)S(1)} collective-permute-done((f32[32,1024]{1,0:T(8,128)S(1)}, f32[32,1024]{1,0:T(8,128)S(1)}, u32[]{:S(2)}, u32[]{:S(2)}) %collective-permute-start.5) | collective-permute-done | bytes 131104 | tf_op jit(solution)/shard_map/ppermute | solution.py:331
  29.9 1.1 %collective-permute-start.6 = (f32[16,1024]{1,0:T(8,128)S(1)}, f32[16,1024]{1,0:T(8,128)S(1)}, u32[]{:S(2)}, u32[]{:S(2)}) collective-permute-start(f32[16,1024]{1,0:T(8,128)S(1)} %slice.63), channel_id=1, source_target_pairs={{0,8},{2,10},{4,12},{6,14},{8,0},{10,2},{12,4},{14,6},{1,9},{3,11}... | collective-permute-start | bytes 196616 | tf_op jit(solution)/shard_map/ppermute | solution.py:331
  31.1 1.3 %collective-permute-done.8 = f32[32,1280]{1,0:T(8,128)S(1)} collective-permute-done((f32[32,1280]{1,0:T(8,128)S(1)}, f32[32,1280]{1,0:T(8,128)S(1)}, u32[]{:S(2)}, u32[]{:S(2)}) %collective-permute-start.8) | collective-permute-done | bytes 163872 | tf_op jit(solution)/shard_map/ppermute | solution.py:331
  32.4 1.2 %collective-permute-start.9 = (f32[16,1280]{1,0:T(8,128)S(1)}, f32[16,1280]{1,0:T(8,128)S(1)}, u32[]{:S(2)}, u32[]{:S(2)}) collective-permute-start(f32[16,1280]{1,0:T(8,128)S(1)} %slice.67), channel_id=1, source_target_pairs={{0,8},{2,10},{4,12},{6,14},{8,0},{10,2},{12,4},{14,6},{1,9},{3,11}... | collective-permute-start | bytes 245768 | tf_op jit(solution)/shard_map/ppermute | solution.py:331
  33.6 2.7 %collective-permute-done.6 = f32[16,1024]{1,0:T(8,128)S(1)} collective-permute-done((f32[16,1024]{1,0:T(8,128)S(1)}, f32[16,1024]{1,0:T(8,128)S(1)}, u32[]{:S(2)}, u32[]{:S(2)}) %collective-permute-start.6) | collective-permute-done | bytes 65568 | tf_op jit(solution)/shard_map/ppermute | solution.py:331
  36.3 2.2 %collective-permute-done.9 = f32[16,1280]{1,0:T(8,128)S(1)} collective-permute-done((f32[16,1280]{1,0:T(8,128)S(1)}, f32[16,1280]{1,0:T(8,128)S(1)}, u32[]{:S(2)}, u32[]{:S(2)}) %collective-permute-start.9) | collective-permute-done | bytes 81952 | tf_op jit(solution)/shard_map/ppermute | solution.py:331
  38.8 1.1 %collective-permute-done.10.other_q = bf16[8,3328]{1,0:T(8,128)(2,1)S(1)} collective-permute-done((bf16[8,3328]{1,0:T(8,128)(2,1)S(1)}, bf16[8,3328]{1,0:T(8,128)(2,1)S(1)}, u32[]{:S(2)}, u32[]{:S(2)}) %collective-permute-start.10) | collective-permute-done | bytes 53280 | tf_op jit(solution)/shard_map/ppermute | solution.py:328
  39.9 2.9 %attend.1 = (bf16[8,3072]{1,0:T(8,128)(2,1)S(1)}, bf16[8,3072]{1,0:T(8,128)(2,1)S(1)}) custom-call(s32[9]{0:T(128)S(1)} %pad_add_fusion.1.scalars_ref, bf16[8,3328]{1,0:T(8,128)(2,1)S(1)} %get-tuple-element.82.own_q, bf16[8,3328]{1,0:T(8,128)(2,1)S(1)} %collective-permute-done.10.other_q, bf16[8,1024,256]{2,1,0:T(8,128)(2,1)S(1)} %copy-done, ...), custom_call_target="tpu_custom_call" | custom-call | flops 201326592 | bytes 8388608 | tf_op jit(solution)/shard_map/attend/pallas_call | solution.py:249
  43.0 1.1 %collective-permute-done.11 = bf16[8,3072]{1,0:T(8,128)(2,1)S(1)} collective-permute-done((bf16[8,3072]{1,0:T(8,128)(2,1)S(1)}, bf16[8,3072]{1,0:T(8,128)(2,1)S(1)}, u32[]{:S(2)}, u32[]{:S(2)}) %collective-permute-start.11) | collective-permute-done | bytes 49184 | tf_op jit(solution)/shard_map/ppermute | solution.py:328
  44.2 1.4 %collective-permute-start.12 = (bf16[16,1536]{1,0:T(8,128)(2,1)S(1)}, bf16[16,1536]{1,0:T(8,128)(2,1)S(1)}, u32[]{:S(2)}, u32[]{:S(2)}) collective-permute-start(bf16[16,1536]{1,0:T(8,128)(2,1)S(1)} %get-tuple-element.84), channel_id=1, source_target_pairs={{0,8},{2,10},{4,12},{6,14},{8,0},{10,2},{12,4},{14,6},{1,9},{3,11}... | collective-permute-start | bytes 147464 | tf_op jit(solution)/shard_map/ppermute | solution.py:331
  45.6 2.7 %collective-permute-done.14 = bf16[16,1536]{1,0:T(8,128)(2,1)S(1)} collective-permute-done((bf16[16,1536]{1,0:T(8,128)(2,1)S(1)}, bf16[16,1536]{1,0:T(8,128)(2,1)S(1)}, u32[]{:S(2)}, u32[]{:S(2)}) %collective-permute-start.14) | collective-permute-done | bytes 49184 | tf_op jit(solution)/shard_map/ppermute | solution.py:331
  48.3 0.5 collective-permute-start.16
  48.8 1.2 %collective-permute-done.12 = bf16[16,1536]{1,0:T(8,128)(2,1)S(1)} collective-permute-done((bf16[16,1536]{1,0:T(8,128)(2,1)S(1)}, bf16[16,1536]{1,0:T(8,128)(2,1)S(1)}, u32[]{:S(2)}, u32[]{:S(2)}) %collective-permute-start.12) | collective-permute-done | bytes 49184 | tf_op jit(solution)/shard_map/ppermute | solution.py:331
  50.0 1.1 %collective-permute-start.13 = (bf16[32,1536]{1,0:T(8,128)(2,1)S(1)}, bf16[32,1536]{1,0:T(8,128)(2,1)S(1)}, u32[]{:S(2)}, u32[]{:S(2)}) collective-permute-start(bf16[32,1536]{1,0:T(8,128)(2,1)S(1)} %pad_maximum_fusion.2.refs_0_), channel_id=1, source_target_pairs={{0,4},{2,6},{4,0},{6,2},{8,12},{10,14},{12,8},{14,10},{1,5},{3,7},... | collective-permute-start | bytes 294920 | tf_op jit(solution)/shard_map/ppermute | solution.py:331
  51.1 3.1 %load.4 = (bf16[512,768]{1,0:T(8,128)(2,1)S(1)}, bf16[512,768]{1,0:T(8,128)(2,1)S(1)}, bf16[512,768]{1,0:T(8,128)(2,1)S(1)}, bf16[512,768]{1,0:T(8,128)(2,1)S(1)...) custom-call(bf16[32,1536]{1,0:T(8,128)(2,1)S(1)} %pad_maximum_fusion, ...), custom_call_target="tpu_custom_call" | custom-call | bytes 14155776 | tf_op jit(solution)/shard_map/load/pallas_call | solution.py:78
  54.7 0.7 %collective-permute-start.17 = (bf16[64,1536]{1,0:T(8,128)(2,1)S(1)}, bf16[64,1536]{1,0:T(8,128)(2,1)S(1)}, u32[]{:S(2)}, u32[]{:S(2)}) collective-permute-start(bf16[64,1536]{1,0:T(8,128)(2,1)S(1)} %pad_maximum_fusion.1.refs_1_.refs_2_), channel_id=1, source_target_pairs={{0,4},{2,6},{4,0},{6,2},{8,12},{10,14},{12,8},{14,10},{1,5},{3,7},... | collective-permute-start | bytes 589832 | tf_op jit(solution)/shard_map/ppermute | solution.py:331
  55.7 1.1 %collective-permute-start.15 = (bf16[64,1536]{1,0:T(8,128)(2,1)S(1)}, bf16[64,1536]{1,0:T(8,128)(2,1)S(1)}, u32[]{:S(2)}, u32[]{:S(2)}) collective-permute-start(bf16[64,1536]{1,0:T(8,128)(2,1)S(1)} %maximum_add_fusion.refs_0_), channel_id=1, source_target_pairs={{0,2},{2,0},{4,6},{6,4},{8,10},{10,8},{12,14},{14,12},{1,3},{3,1},... | collective-permute-start | bytes 589832 | tf_op jit(solution)/shard_map/ppermute | solution.py:331
  56.8 3.7 %load.5 = (bf16[512,768]{1,0:T(8,128)(2,1)S(1)}, bf16[512,768]{1,0:T(8,128)(2,1)S(1)}, bf16[512,768]{1,0:T(8,128)(2,1)S(1)}, bf16[512,768]{1,0:T(8,128)(2,1)S(1)...) custom-call(bf16[64,1536]{1,0:T(8,128)(2,1)S(1)} %maximum_add_fusion, ...), custom_call_target="tpu_custom_call" | custom-call | bytes 14155776 | tf_op jit(solution)/shard_map/load/pallas_call | solution.py:78
  60.5 1.2 %collective-permute-done.15.refs_1_ = bf16[64,1536]{1,0:T(8,128)(2,1)S(1)} collective-permute-done((bf16[64,1536]{1,0:T(8,128)(2,1)S(1)}, bf16[64,1536]{1,0:T(8,128)(2,1)S(1)}, u32[]{:S(2)}, u32[]{:S(2)}) %collective-permute-start.15) | collective-permute-done | bytes 196640 | tf_op jit(solution)/shard_map/ppermute | solution.py:331
  61.8 2.6 %project_out.1 = (f32[64,2304]{1,0:T(8,128)S(1)}, f32[64,2304]{1,0:T(8,128)S(1)}) custom-call(s32[2]{0:T(128)S(1)} %pad_add_fusion.ids_ref, bf16[64,1536]{1,0:T(8,128)(2,1)S(1)} %maximum_add_fusion.refs_0_, bf16[64,1536]{1,0:T(8,128)(2,1)S(1)} %collective-permute-done.15.refs_1_, bf16[64,1536]{1,0:T(8,128)(2,1)S(1)} %pad_maximum_fusion.1.refs_1_.refs_2_, ...), custom_call_target="tpu_custom_call" | custom-call | flops 1811939328 | bytes 15335424 | tf_op jit(solution)/shard_map/project_out/pallas_call | solution.py:302
  64.5 2.0 %collective-permute-done.18 = f32[64,2304]{1,0:T(8,128)S(1)} collective-permute-done((f32[64,2304]{1,0:T(8,128)S(1)}, f32[64,2304]{1,0:T(8,128)S(1)}, u32[]{:S(2)}, u32[]{:S(2)}) %collective-permute-start.18) | collective-permute-done | bytes 589856 | tf_op jit(solution)/shard_map/ppermute | solution.py:328
  66.5 0.8 %add_convert_fusion = bf16[64,2304]{1,0:T(8,128)(2,1)} fusion(f32[64,2304]{1,0:T(8,128)S(1)} %get-tuple-element.79, f32[64,2304]{1,0:T(8,128)S(1)} %collective-permute-done.18), kind=kLoop, calls=%fused_computation | loop fusion | flops 294912 | bytes 1474560 | tf_op jit(solution)/shard_map/convert_element_type | solution.py:393
  (47 shorter events, 2.6 us)
Async XLA Ops:
  0.0 1.9 %collective-permute-start = (bf16[64,2304]{1,0:T(8,128)(2,1)}, bf16[64,2304]{1,0:T(8,128)(2,1)S(1)}, u32[]{:S(2)}, u32[]{:S(2)}) collective-permute-start(bf16[64,2304]{1,0:T(8,128)(2,1)} %param.7), channel_id=1, source_target_pairs={{0,1},{1,0},{2,3},{3,2},{4,5},{5,4},{6,7},{7,6},{8,9},{9,8},{10,11... | collective-permute-start | bytes 884744 | tf_op jit(solution)/shard_map/ppermute | solution.py:328
  1.5 6.8 %copy-start.1 = (bf16[2304,512]{1,0:T(8,128)(2,1)S(1)}, bf16[2304,512]{1,0:T(8,128)(2,1)}, u32[]{:S(2)}) copy-start(bf16[2304,512]{1,0:T(8,128)(2,1)} %refs_0_.2) | copy-start | bytes 7077892
  5.3 10.4 %collective-permute-start.1 = (f32[64,1024]{1,0:T(8,128)S(1)}, f32[64,1024]{1,0:T(8,128)S(1)}, u32[]{:S(2)}, u32[]{:S(2)}) collective-permute-start(f32[64,1024]{1,0:T(8,128)S(1)} %get-tuple-element.44.refs_1_), channel_id=1, source_target_pairs={{0,4},{2,6},{4,0},{6,2},{8,12},{10,14},{12,8},{14,10},{1,5},{3,7},... | collective-permute-start | bytes 786440 | tf_op jit(solution)/shard_map/ppermute | solution.py:331
  13.7 10.9 %collective-permute-start.4 = (f32[64,1024]{1,0:T(8,128)S(1)}, f32[64,1024]{1,0:T(8,128)S(1)}, u32[]{:S(2)}, u32[]{:S(2)}) collective-permute-start(f32[64,1024]{1,0:T(8,128)S(1)} %get-tuple-element.46), channel_id=1, source_target_pairs={{0,4},{2,6},{4,0},{6,2},{8,12},{10,14},{12,8},{14,10},{1,5},{3,7},... | collective-permute-start | bytes 786440 | tf_op jit(solution)/shard_map/ppermute | solution.py:331
  13.8 12.5 %collective-permute-start.7 = (f32[64,1280]{1,0:T(8,128)S(1)}, f32[64,1280]{1,0:T(8,128)S(1)}, u32[]{:S(2)}, u32[]{:S(2)}) collective-permute-start(f32[64,1280]{1,0:T(8,128)S(1)} %get-tuple-element.49), channel_id=1, source_target_pairs={{0,2},{2,0},{4,6},{6,4},{8,10},{10,8},{12,14},{14,12},{1,3},{3,1},... | collective-permute-start | bytes 983048 | tf_op jit(solution)/shard_map/ppermute | solution.py:331
  15.8 22.9 %copy-start.2 = (s32[8]{0:T(128)S(1)}, s32[8]{0:T(128)}, u32[]{:S(2)}) copy-start(s32[8]{0:T(128)} %param.13) | copy-start | bytes 100
  15.8 24.1 %copy-start = (bf16[8,1024,256]{2,1,0:T(8,128)(2,1)S(1)}, bf16[8,1024,256]{2,1,0:T(8,128)(2,1)}, u32[]{:S(2)}) copy-start(bf16[8,1024,256]{2,1,0:T(8,128)(2,1)} %refs_0_.3) | copy-start | bytes 12582916
  15.8 10.6 %collective-permute-start.2 = (f32[32,1024]{1,0:T(8,128)S(1)}, f32[32,1024]{1,0:T(8,128)S(1)}, u32[]{:S(2)}, u32[]{:S(2)}) collective-permute-start(f32[32,1024]{1,0:T(8,128)S(1)} %slice.57.refs_0_), channel_id=1, source_target_pairs={{0,8},{2,10},{4,12},{6,14},{8,0},{10,2},{12,4},{14,6},{1,9},{3,11}... | collective-permute-start | bytes 393224 | tf_op jit(solution)/shard_map/ppermute | solution.py:331
  24.7 5.2 %collective-permute-start.5 = (f32[32,1024]{1,0:T(8,128)S(1)}, f32[32,1024]{1,0:T(8,128)S(1)}, u32[]{:S(2)}, u32[]{:S(2)}) collective-permute-start(f32[32,1024]{1,0:T(8,128)S(1)} %slice.61), channel_id=1, source_target_pairs={{0,2},{2,0},{4,6},{6,4},{8,10},{10,8},{12,14},{14,12},{1,3},{3,1},... | collective-permute-start | bytes 393224 | tf_op jit(solution)/shard_map/ppermute | solution.py:331
  26.3 6.1 %collective-permute-start.8 = (f32[32,1280]{1,0:T(8,128)S(1)}, f32[32,1280]{1,0:T(8,128)S(1)}, u32[]{:S(2)}, u32[]{:S(2)}) collective-permute-start(f32[32,1280]{1,0:T(8,128)S(1)} %slice.65), channel_id=1, source_target_pairs={{0,4},{2,6},{4,0},{6,2},{8,12},{10,14},{12,8},{14,10},{1,5},{3,7},... | collective-permute-start | bytes 491528 | tf_op jit(solution)/shard_map/ppermute | solution.py:331
  26.4 4.6 %collective-permute-start.3 = (f32[16,1024]{1,0:T(8,128)S(1)}, f32[16,1024]{1,0:T(8,128)S(1)}, u32[]{:S(2)}, u32[]{:S(2)}) collective-permute-start(f32[16,1024]{1,0:T(8,128)S(1)} %slice.59), channel_id=1, source_target_pairs={{0,2},{2,0},{4,6},{6,4},{8,10},{10,8},{12,14},{14,12},{1,3},{3,1},... | collective-permute-start | bytes 196616 | tf_op jit(solution)/shard_map/ppermute | solution.py:331
  29.9 6.4 %collective-permute-start.6 = (f32[16,1024]{1,0:T(8,128)S(1)}, f32[16,1024]{1,0:T(8,128)S(1)}, u32[]{:S(2)}, u32[]{:S(2)}) collective-permute-start(f32[16,1024]{1,0:T(8,128)S(1)} %slice.63), channel_id=1, source_target_pairs={{0,8},{2,10},{4,12},{6,14},{8,0},{10,2},{12,4},{14,6},{1,9},{3,11}... | collective-permute-start | bytes 196616 | tf_op jit(solution)/shard_map/ppermute | solution.py:331
  32.4 6.1 %collective-permute-start.9 = (f32[16,1280]{1,0:T(8,128)S(1)}, f32[16,1280]{1,0:T(8,128)S(1)}, u32[]{:S(2)}, u32[]{:S(2)}) collective-permute-start(f32[16,1280]{1,0:T(8,128)S(1)} %slice.67), channel_id=1, source_target_pairs={{0,8},{2,10},{4,12},{6,14},{8,0},{10,2},{12,4},{14,6},{1,9},{3,11}... | collective-permute-start | bytes 245768 | tf_op jit(solution)/shard_map/ppermute | solution.py:331
  38.6 1.3 %collective-permute-start.10 = (bf16[8,3328]{1,0:T(8,128)(2,1)S(1)}, bf16[8,3328]{1,0:T(8,128)(2,1)S(1)}, u32[]{:S(2)}, u32[]{:S(2)}) collective-permute-start(bf16[8,3328]{1,0:T(8,128)(2,1)S(1)} %get-tuple-element.81), channel_id=1, source_target_pairs={{0,1},{1,0},{2,3},{3,2},{4,5},{5,4},{6,7},{7,6},{8,9},{9,8},{10,11... | collective-permute-start | bytes 159752 | tf_op jit(solution)/shard_map/ppermute | solution.py:328
  42.8 1.3 %collective-permute-start.11 = (bf16[8,3072]{1,0:T(8,128)(2,1)S(1)}, bf16[8,3072]{1,0:T(8,128)(2,1)S(1)}, u32[]{:S(2)}, u32[]{:S(2)}) collective-permute-start(bf16[8,3072]{1,0:T(8,128)(2,1)S(1)} %get-tuple-element.59), channel_id=1, source_target_pairs={{0,1},{1,0},{2,3},{3,2},{4,5},{5,4},{6,7},{7,6},{8,9},{9,8},{10,11... | collective-permute-start | bytes 147464 | tf_op jit(solution)/shard_map/ppermute | solution.py:328
  44.1 4.2 %collective-permute-start.14 = (bf16[16,1536]{1,0:T(8,128)(2,1)S(1)}, bf16[16,1536]{1,0:T(8,128)(2,1)S(1)}, u32[]{:S(2)}, u32[]{:S(2)}) collective-permute-start(bf16[16,1536]{1,0:T(8,128)(2,1)S(1)} %get-tuple-element.83), channel_id=1, source_target_pairs={{0,2},{2,0},{4,6},{6,4},{8,10},{10,8},{12,14},{14,12},{1,3},{3,1},... | collective-permute-start | bytes 147464 | tf_op jit(solution)/shard_map/ppermute | solution.py:331
  44.2 5.8 %collective-permute-start.12 = (bf16[16,1536]{1,0:T(8,128)(2,1)S(1)}, bf16[16,1536]{1,0:T(8,128)(2,1)S(1)}, u32[]{:S(2)}, u32[]{:S(2)}) collective-permute-start(bf16[16,1536]{1,0:T(8,128)(2,1)S(1)} %get-tuple-element.84), channel_id=1, source_target_pairs={{0,8},{2,10},{4,12},{6,14},{8,0},{10,2},{12,4},{14,6},{1,9},{3,11}... | collective-permute-start | bytes 147464 | tf_op jit(solution)/shard_map/ppermute | solution.py:331
  48.3 6.3 %collective-permute-start.16 = (bf16[32,1536]{1,0:T(8,128)(2,1)S(1)}, bf16[32,1536]{1,0:T(8,128)(2,1)S(1)}, u32[]{:S(2)}, u32[]{:S(2)}) collective-permute-start(bf16[32,1536]{1,0:T(8,128)(2,1)S(1)} %pad_maximum_fusion.3.refs_1_), channel_id=1, source_target_pairs={{0,8},{2,10},{4,12},{6,14},{8,0},{10,2},{12,4},{14,6},{1,9},{3,11}... | collective-permute-start | bytes 294920 | tf_op jit(solution)/shard_map/ppermute | solution.py:331
  50.0 5.6 %collective-permute-start.13 = (bf16[32,1536]{1,0:T(8,128)(2,1)S(1)}, bf16[32,1536]{1,0:T(8,128)(2,1)S(1)}, u32[]{:S(2)}, u32[]{:S(2)}) collective-permute-start(bf16[32,1536]{1,0:T(8,128)(2,1)S(1)} %pad_maximum_fusion.2.refs_0_), channel_id=1, source_target_pairs={{0,4},{2,6},{4,0},{6,2},{8,12},{10,14},{12,8},{14,10},{1,5},{3,7},... | collective-permute-start | bytes 294920 | tf_op jit(solution)/shard_map/ppermute | solution.py:331
  54.7 5.9 %collective-permute-start.17 = (bf16[64,1536]{1,0:T(8,128)(2,1)S(1)}, bf16[64,1536]{1,0:T(8,128)(2,1)S(1)}, u32[]{:S(2)}, u32[]{:S(2)}) collective-permute-start(bf16[64,1536]{1,0:T(8,128)(2,1)S(1)} %pad_maximum_fusion.1.refs_1_.refs_2_), channel_id=1, source_target_pairs={{0,4},{2,6},{4,0},{6,2},{8,12},{10,14},{12,8},{14,10},{1,5},{3,7},... | collective-permute-start | bytes 589832 | tf_op jit(solution)/shard_map/ppermute | solution.py:331
  55.7 6.1 %collective-permute-start.15 = (bf16[64,1536]{1,0:T(8,128)(2,1)S(1)}, bf16[64,1536]{1,0:T(8,128)(2,1)S(1)}, u32[]{:S(2)}, u32[]{:S(2)}) collective-permute-start(bf16[64,1536]{1,0:T(8,128)(2,1)S(1)} %maximum_add_fusion.refs_0_), channel_id=1, source_target_pairs={{0,2},{2,0},{4,6},{6,4},{8,10},{10,8},{12,14},{14,12},{1,3},{3,1},... | collective-permute-start | bytes 589832 | tf_op jit(solution)/shard_map/ppermute | solution.py:331
  64.4 2.1 %collective-permute-start.18 = (f32[64,2304]{1,0:T(8,128)S(1)}, f32[64,2304]{1,0:T(8,128)S(1)}, u32[]{:S(2)}, u32[]{:S(2)}) collective-permute-start(f32[64,2304]{1,0:T(8,128)S(1)} %get-tuple-element.80), channel_id=1, source_target_pairs={{0,1},{1,0},{2,3},{3,2},{4,5},{5,4},{6,7},{7,6},{8,9},{9,8},{10,11... | collective-permute-start | bytes 1769480 | tf_op jit(solution)/shard_map/ppermute | solution.py:328

commit v19 on v18

--- a/solution.py
+++ b/solution.py
@@ -91,7 +91,7 @@
 
 
 def spans_of(width):
-    return [(at, min(512, width - at)) for at in range(0, width, 512)]
+    return [(at, min(768, width - at)) for at in range(0, width, 768)]
 
 
 def project_kernel(orders, rows, first, widths, kv_width, after, ids_ref, own_ref, other_ref, w_ref, *refs):

time: 67.4 us -> 67.4 us (level)
  no operation moved by 1% of the time
where the time goes in v19:
time: 67.4 us; the launch traced here: 67.2 us
  waiting for transfers between devices  23.8 us (35%)
  Pallas kernels  23.5 us (35%)
  starting transfers between devices  17.3 us (26%)
  other arithmetic  2.26 us (3%)
    ppermute x15, waiting for transfers between devices, across(): return lax.ppermute(array, 'gx', [(g, g ^ mask) for g in range(n)])  19.2 us
    ppermute x15, starting transfers between devices, across(): return lax.ppermute(array, 'gx', [(g, g ^ mask) for g in range(n)])  16.5 us
    pallas_call x3, Pallas kernels, load(): pl.pallas_call(functools.partial(load_kernel, len(after), cuts, len(array...  9.06 us
    pallas_call x2, Pallas kernels, project(): pl.pallas_call(functools.partial(project_kernel, orders, rows, first, wid...  8.92 us
    ppermute x4, waiting for transfers between devices, swap(): return lax.ppermute(array, 'gy', [(0, 1), (1, 0)])  4.55 us
    pallas_call x1, Pallas kernels, attend(): pl.pallas_call(functools.partial(attend_kernel, kv_column), out_shape=(ou...  2.87 us
    pallas_call x1, Pallas kernels, project_out(): pl.pallas_call(functools.partial(output_kernel, orders, rows, columns, pi...  2.65 us
  transfers between devices with their start and end apart: 19, of which 14 were waited for; matrix products, arithmetic and copies ran while one was open for 2% of the time, Pallas kernels for 21%

profile of v19, /device:TPU:0, one launch (start us, length us, event | category | flops | bytes accessed | tf_op | source)
XLA Modules:
  0.0 67.2 jit_solution(14174127464671417274)
XLA Ops:
  0.0 0.5 collective-permute-start
  0.5 1.0 %broadcast_select_fusion.own_ref = bf16[64,2304]{1,0:T(8,128)(2,1)S(1)} fusion(bf16[64,2304]{1,0:T(8,128)(2,1)} %param.7, pred[]{:T(512)S(6)} %lt.9), kind=kLoop, calls=%fused_computation.1 | loop fusion | flops 147456 | bytes 589825 | tf_op jit(solution)/shard_map/jit(_where)/select_n | solution.py:334
  1.9 3.8 %project.2 = (f32[64,1024]{1,0:T(8,128)S(1)}, f32[64,1024]{1,0:T(8,128)S(1)}) custom-call(s32[2]{0:T(128)S(1)} %pad_add_fusion.ids_ref, bf16[64,2304]{1,0:T(8,128)(2,1)S(1)} %broadcast_select_fusion.own_ref, bf16[64,2304]{1,0:T(8,128)(2,1)S(1)} %collective-permute-done.other_ref, bf16[2304,3072]{1,0:T(8,128)(2,1)} %w_ref.3), custom_call_target="tpu_custom_call" | custom-call | flops 603979776 | bytes 5242880 | tf_op jit(solution)/shard_map/project/pallas_call | solution.py:176
  5.7 3.0 %collective-permute-start.1 = (f32[64,1024]{1,0:T(8,128)S(1)}, f32[64,1024]{1,0:T(8,128)S(1)}, u32[]{:S(2)}, u32[]{:S(2)}) collective-permute-start(f32[64,1024]{1,0:T(8,128)S(1)} %get-tuple-element.44.refs_1_), channel_id=1, source_target_pairs={{0,4},{2,6},{4,0},{6,2},{8,12},{10,14},{12,8},{14,10},{1,5},{3,7},... | collective-permute-start | bytes 786440 | tf_op jit(solution)/shard_map/ppermute | solution.py:331
  8.7 5.1 %project.3 = (f32[64,1024]{1,0:T(8,128)S(1)}, f32[64,1024]{1,0:T(8,128)S(1)}, f32[64,1280]{1,0:T(8,128)S(1)}, f32[64,1280]{1,0:T(8,128)S(1)}) custom-call(s32[2]{0:T(128)S(1)} %pad_add_fusion.ids_ref, bf16[64,2304]{1,0:T(8,128)(2,1)S(1)} %broadcast_select_fusion.own_ref, bf16[64,2304]{1,0:T(8,128)(2,1)S(1)} %collective-permute-done.other_ref, ...), custom_call_target="tpu_custom_call" | custom-call | flops 1358954496 | bytes 11796480 | tf_op jit(solution)/shard_map/project/pallas_call | solution.py:176
  13.9 1.9 %collective-permute-start.7 = (f32[64,1280]{1,0:T(8,128)S(1)}, f32[64,1280]{1,0:T(8,128)S(1)}, u32[]{:S(2)}, u32[]{:S(2)}) collective-permute-start(f32[64,1280]{1,0:T(8,128)S(1)} %get-tuple-element.49), channel_id=1, source_target_pairs={{0,2},{2,0},{4,6},{6,4},{8,10},{10,8},{12,14},{14,12},{1,3},{3,1},... | collective-permute-start | bytes 983048 | tf_op jit(solution)/shard_map/ppermute | solution.py:331
  15.9 2.7 %collective-permute-start.2 = (f32[32,1024]{1,0:T(8,128)S(1)}, f32[32,1024]{1,0:T(8,128)S(1)}, u32[]{:S(2)}, u32[]{:S(2)}) collective-permute-start(f32[32,1024]{1,0:T(8,128)S(1)} %slice.57.refs_0_), channel_id=1, source_target_pairs={{0,8},{2,10},{4,12},{6,14},{8,0},{10,2},{12,4},{14,6},{1,9},{3,11}... | collective-permute-start | bytes 393224 | tf_op jit(solution)/shard_map/ppermute | solution.py:331
  18.6 2.2 %load.3 = (bf16[1024,256]{1,0:T(8,128)(2,1)S(1)}, bf16[1024,256]{1,0:T(8,128)(2,1)S(1)}, bf16[1024,256]{1,0:T(8,128)(2,1)S(1)}, bf16[1024,256]{1,0:T(8,128)(2,1)...) custom-call(f32[32,1024]{1,0:T(8,128)S(1)} %slice.57.refs_0_, ...), custom_call_target="tpu_custom_call" | custom-call | bytes 8388608 | tf_op jit(solution)/shard_map/load/pallas_call | solution.py:78
  20.8 3.9 %collective-permute-done.4 = f32[64,1024]{1,0:T(8,128)S(1)} collective-permute-done((f32[64,1024]{1,0:T(8,128)S(1)}, f32[64,1024]{1,0:T(8,128)S(1)}, u32[]{:S(2)}, u32[]{:S(2)}) %collective-permute-start.4) | collective-permute-done | bytes 262176 | tf_op jit(solution)/shard_map/ppermute | solution.py:331
  24.8 1.6 %collective-permute-start.5 = (f32[32,1024]{1,0:T(8,128)S(1)}, f32[32,1024]{1,0:T(8,128)S(1)}, u32[]{:S(2)}, u32[]{:S(2)}) collective-permute-start(f32[32,1024]{1,0:T(8,128)S(1)} %slice.61), channel_id=1, source_target_pairs={{0,2},{2,0},{4,6},{6,4},{8,10},{10,8},{12,14},{14,12},{1,3},{3,1},... | collective-permute-start | bytes 393224 | tf_op jit(solution)/shard_map/ppermute | solution.py:331
  26.6 0.6 collective-permute-start.3
  27.2 2.9 %collective-permute-done.5 = f32[32,1024]{1,0:T(8,128)S(1)} collective-permute-done((f32[32,1024]{1,0:T(8,128)S(1)}, f32[32,1024]{1,0:T(8,128)S(1)}, u32[]{:S(2)}, u32[]{:S(2)}) %collective-permute-start.5) | collective-permute-done | bytes 131104 | tf_op jit(solution)/shard_map/ppermute | solution.py:331
  30.1 0.8 %collective-permute-start.6 = (f32[16,1024]{1,0:T(8,128)S(1)}, f32[16,1024]{1,0:T(8,128)S(1)}, u32[]{:S(2)}, u32[]{:S(2)}) collective-permute-start(f32[16,1024]{1,0:T(8,128)S(1)} %slice.63), channel_id=1, source_target_pairs={{0,8},{2,10},{4,12},{6,14},{8,0},{10,2},{12,4},{14,6},{1,9},{3,11}... | collective-permute-start | bytes 196616 | tf_op jit(solution)/shard_map/ppermute | solution.py:331
  30.9 1.6 %collective-permute-done.8 = f32[32,1280]{1,0:T(8,128)S(1)} collective-permute-done((f32[32,1280]{1,0:T(8,128)S(1)}, f32[32,1280]{1,0:T(8,128)S(1)}, u32[]{:S(2)}, u32[]{:S(2)}) %collective-permute-start.8) | collective-permute-done | bytes 163872 | tf_op jit(solution)/shard_map/ppermute | solution.py:331
  32.6 1.2 %collective-permute-start.9 = (f32[16,1280]{1,0:T(8,128)S(1)}, f32[16,1280]{1,0:T(8,128)S(1)}, u32[]{:S(2)}, u32[]{:S(2)}) collective-permute-start(f32[16,1280]{1,0:T(8,128)S(1)} %slice.67), channel_id=1, source_target_pairs={{0,8},{2,10},{4,12},{6,14},{8,0},{10,2},{12,4},{14,6},{1,9},{3,11}... | collective-permute-start | bytes 245768 | tf_op jit(solution)/shard_map/ppermute | solution.py:331
  33.8 2.7 %collective-permute-done.6 = f32[16,1024]{1,0:T(8,128)S(1)} collective-permute-done((f32[16,1024]{1,0:T(8,128)S(1)}, f32[16,1024]{1,0:T(8,128)S(1)}, u32[]{:S(2)}, u32[]{:S(2)}) %collective-permute-start.6) | collective-permute-done | bytes 65568 | tf_op jit(solution)/shard_map/ppermute | solution.py:331
  36.5 2.4 %collective-permute-done.9 = f32[16,1280]{1,0:T(8,128)S(1)} collective-permute-done((f32[16,1280]{1,0:T(8,128)S(1)}, f32[16,1280]{1,0:T(8,128)S(1)}, u32[]{:S(2)}, u32[]{:S(2)}) %collective-permute-start.9) | collective-permute-done | bytes 81952 | tf_op jit(solution)/shard_map/ppermute | solution.py:331
  39.1 1.1 %collective-permute-done.10.other_q = bf16[8,3328]{1,0:T(8,128)(2,1)S(1)} collective-permute-done((bf16[8,3328]{1,0:T(8,128)(2,1)S(1)}, bf16[8,3328]{1,0:T(8,128)(2,1)S(1)}, u32[]{:S(2)}, u32[]{:S(2)}) %collective-permute-start.10) | collective-permute-done | bytes 53280 | tf_op jit(solution)/shard_map/ppermute | solution.py:328
  40.2 2.9 %attend.1 = (bf16[8,3072]{1,0:T(8,128)(2,1)S(1)}, bf16[8,3072]{1,0:T(8,128)(2,1)S(1)}) custom-call(s32[9]{0:T(128)S(1)} %pad_add_fusion.1.scalars_ref, bf16[8,3328]{1,0:T(8,128)(2,1)S(1)} %get-tuple-element.82.own_q, bf16[8,3328]{1,0:T(8,128)(2,1)S(1)} %collective-permute-done.10.other_q, bf16[8,1024,256]{2,1,0:T(8,128)(2,1)S(1)} %copy-done, ...), custom_call_target="tpu_custom_call" | custom-call | flops 201326592 | bytes 8388608 | tf_op jit(solution)/shard_map/attend/pallas_call | solution.py:249
  43.3 1.1 %collective-permute-done.11 = bf16[8,3072]{1,0:T(8,128)(2,1)S(1)} collective-permute-done((bf16[8,3072]{1,0:T(8,128)(2,1)S(1)}, bf16[8,3072]{1,0:T(8,128)(2,1)S(1)}, u32[]{:S(2)}, u32[]{:S(2)}) %collective-permute-start.11) | collective-permute-done | bytes 49184 | tf_op jit(solution)/shard_map/ppermute | solution.py:328
  44.5 1.2 %collective-permute-start.12 = (bf16[16,1536]{1,0:T(8,128)(2,1)S(1)}, bf16[16,1536]{1,0:T(8,128)(2,1)S(1)}, u32[]{:S(2)}, u32[]{:S(2)}) collective-permute-start(bf16[16,1536]{1,0:T(8,128)(2,1)S(1)} %get-tuple-element.84), channel_id=1, source_target_pairs={{0,8},{2,10},{4,12},{6,14},{8,0},{10,2},{12,4},{14,6},{1,9},{3,11}... | collective-permute-start | bytes 147464 | tf_op jit(solution)/shard_map/ppermute | solution.py:331
  45.7 2.9 %collective-permute-done.14 = bf16[16,1536]{1,0:T(8,128)(2,1)S(1)} collective-permute-done((bf16[16,1536]{1,0:T(8,128)(2,1)S(1)}, bf16[16,1536]{1,0:T(8,128)(2,1)S(1)}, u32[]{:S(2)}, u32[]{:S(2)}) %collective-permute-start.14) | collective-permute-done | bytes 49184 | tf_op jit(solution)/shard_map/ppermute | solution.py:331
  49.0 1.4 %collective-permute-done.12 = bf16[16,1536]{1,0:T(8,128)(2,1)S(1)} collective-permute-done((bf16[16,1536]{1,0:T(8,128)(2,1)S(1)}, bf16[16,1536]{1,0:T(8,128)(2,1)S(1)}, u32[]{:S(2)}, u32[]{:S(2)}) %collective-permute-start.12) | collective-permute-done | bytes 49184 | tf_op jit(solution)/shard_map/ppermute | solution.py:331
  50.4 1.0 %collective-permute-start.13 = (bf16[32,1536]{1,0:T(8,128)(2,1)S(1)}, bf16[32,1536]{1,0:T(8,128)(2,1)S(1)}, u32[]{:S(2)}, u32[]{:S(2)}) collective-permute-start(bf16[32,1536]{1,0:T(8,128)(2,1)S(1)} %pad_maximum_fusion.2.refs_0_), channel_id=1, source_target_pairs={{0,4},{2,6},{4,0},{6,2},{8,12},{10,14},{12,8},{14,10},{1,5},{3,7},... | collective-permute-start | bytes 294920 | tf_op jit(solution)/shard_map/ppermute | solution.py:331
  51.3 3.1 %load.4 = (bf16[512,768]{1,0:T(8,128)(2,1)S(1)}, bf16[512,768]{1,0:T(8,128)(2,1)S(1)}, bf16[512,768]{1,0:T(8,128)(2,1)S(1)}, bf16[512,768]{1,0:T(8,128)(2,1)S(1)...) custom-call(bf16[32,1536]{1,0:T(8,128)(2,1)S(1)} %pad_maximum_fusion, ...), custom_call_target="tpu_custom_call" | custom-call | bytes 14155776 | tf_op jit(solution)/shard_map/load/pallas_call | solution.py:78
  54.9 0.8 %collective-permute-start.17 = (bf16[64,1536]{1,0:T(8,128)(2,1)S(1)}, bf16[64,1536]{1,0:T(8,128)(2,1)S(1)}, u32[]{:S(2)}, u32[]{:S(2)}) collective-permute-start(bf16[64,1536]{1,0:T(8,128)(2,1)S(1)} %pad_maximum_fusion.1.refs_1_.refs_2_), channel_id=1, source_target_pairs={{0,4},{2,6},{4,0},{6,2},{8,12},{10,14},{12,8},{14,10},{1,5},{3,7},... | collective-permute-start | bytes 589832 | tf_op jit(solution)/shard_map/ppermute | solution.py:331
  56.0 1.2 %collective-permute-start.15 = (bf16[64,1536]{1,0:T(8,128)(2,1)S(1)}, bf16[64,1536]{1,0:T(8,128)(2,1)S(1)}, u32[]{:S(2)}, u32[]{:S(2)}) collective-permute-start(bf16[64,1536]{1,0:T(8,128)(2,1)S(1)} %maximum_add_fusion.refs_0_), channel_id=1, source_target_pairs={{0,2},{2,0},{4,6},{6,4},{8,10},{10,8},{12,14},{14,12},{1,3},{3,1},... | collective-permute-start | bytes 589832 | tf_op jit(solution)/shard_map/ppermute | solution.py:331
  57.1 3.7 %load.5 = (bf16[512,768]{1,0:T(8,128)(2,1)S(1)}, bf16[512,768]{1,0:T(8,128)(2,1)S(1)}, bf16[512,768]{1,0:T(8,128)(2,1)S(1)}, bf16[512,768]{1,0:T(8,128)(2,1)S(1)...) custom-call(bf16[64,1536]{1,0:T(8,128)(2,1)S(1)} %maximum_add_fusion, ...), custom_call_target="tpu_custom_call" | custom-call | bytes 14155776 | tf_op jit(solution)/shard_map/load/pallas_call | solution.py:78
  60.9 0.8 %collective-permute-done.15.refs_1_ = bf16[64,1536]{1,0:T(8,128)(2,1)S(1)} collective-permute-done((bf16[64,1536]{1,0:T(8,128)(2,1)S(1)}, bf16[64,1536]{1,0:T(8,128)(2,1)S(1)}, u32[]{:S(2)}, u32[]{:S(2)}) %collective-permute-start.15) | collective-permute-done | bytes 196640 | tf_op jit(solution)/shard_map/ppermute | solution.py:331
  61.7 2.6 %project_out.1 = (f32[64,2304]{1,0:T(8,128)S(1)}, f32[64,2304]{1,0:T(8,128)S(1)}) custom-call(s32[2]{0:T(128)S(1)} %pad_add_fusion.ids_ref, bf16[64,1536]{1,0:T(8,128)(2,1)S(1)} %maximum_add_fusion.refs_0_, bf16[64,1536]{1,0:T(8,128)(2,1)S(1)} %collective-permute-done.15.refs_1_, bf16[64,1536]{1,0:T(8,128)(2,1)S(1)} %pad_maximum_fusion.1.refs_1_.refs_2_, ...), custom_call_target="tpu_custom_call" | custom-call | flops 1811939328 | bytes 15335424 | tf_op jit(solution)/shard_map/project_out/pallas_call | solution.py:302
  64.4 2.0 %collective-permute-done.18 = f32[64,2304]{1,0:T(8,128)S(1)} collective-permute-done((f32[64,2304]{1,0:T(8,128)S(1)}, f32[64,2304]{1,0:T(8,128)S(1)}, u32[]{:S(2)}, u32[]{:S(2)}) %collective-permute-start.18) | collective-permute-done | bytes 589856 | tf_op jit(solution)/shard_map/ppermute | solution.py:328
  66.4 0.8 %add_convert_fusion = bf16[64,2304]{1,0:T(8,128)(2,1)} fusion(f32[64,2304]{1,0:T(8,128)S(1)} %get-tuple-element.79, f32[64,2304]{1,0:T(8,128)S(1)} %collective-permute-done.18), kind=kLoop, calls=%fused_computation | loop fusion | flops 294912 | bytes 1474560 | tf_op jit(solution)/shard_map/convert_element_type | solution.py:393
  (47 shorter events, 2.5 us)
Async XLA Ops:
  0.0 1.9 %collective-permute-start = (bf16[64,2304]{1,0:T(8,128)(2,1)}, bf16[64,2304]{1,0:T(8,128)(2,1)S(1)}, u32[]{:S(2)}, u32[]{:S(2)}) collective-permute-start(bf16[64,2304]{1,0:T(8,128)(2,1)} %param.7), channel_id=1, source_target_pairs={{0,1},{1,0},{2,3},{3,2},{4,5},{5,4},{6,7},{7,6},{8,9},{9,8},{10,11... | collective-permute-start | bytes 884744 | tf_op jit(solution)/shard_map/ppermute | solution.py:328
  1.5 7.2 %copy-start.1 = (bf16[2304,512]{1,0:T(8,128)(2,1)S(1)}, bf16[2304,512]{1,0:T(8,128)(2,1)}, u32[]{:S(2)}) copy-start(bf16[2304,512]{1,0:T(8,128)(2,1)} %refs_0_.2) | copy-start | bytes 7077892
  5.7 10.1 %collective-permute-start.1 = (f32[64,1024]{1,0:T(8,128)S(1)}, f32[64,1024]{1,0:T(8,128)S(1)}, u32[]{:S(2)}, u32[]{:S(2)}) collective-permute-start(f32[64,1024]{1,0:T(8,128)S(1)} %get-tuple-element.44.refs_1_), channel_id=1, source_target_pairs={{0,4},{2,6},{4,0},{6,2},{8,12},{10,14},{12,8},{14,10},{1,5},{3,7},... | collective-permute-start | bytes 786440 | tf_op jit(solution)/shard_map/ppermute | solution.py:331
  13.8 10.9 %collective-permute-start.4 = (f32[64,1024]{1,0:T(8,128)S(1)}, f32[64,1024]{1,0:T(8,128)S(1)}, u32[]{:S(2)}, u32[]{:S(2)}) collective-permute-start(f32[64,1024]{1,0:T(8,128)S(1)} %get-tuple-element.46), channel_id=1, source_target_pairs={{0,4},{2,6},{4,0},{6,2},{8,12},{10,14},{12,8},{14,10},{1,5},{3,7},... | collective-permute-start | bytes 786440 | tf_op jit(solution)/shard_map/ppermute | solution.py:331
  13.9 12.5 %collective-permute-start.7 = (f32[64,1280]{1,0:T(8,128)S(1)}, f32[64,1280]{1,0:T(8,128)S(1)}, u32[]{:S(2)}, u32[]{:S(2)}) collective-permute-start(f32[64,1280]{1,0:T(8,128)S(1)} %get-tuple-element.49), channel_id=1, source_target_pairs={{0,2},{2,0},{4,6},{6,4},{8,10},{10,8},{12,14},{14,12},{1,3},{3,1},... | collective-permute-start | bytes 983048 | tf_op jit(solution)/shard_map/ppermute | solution.py:331
  15.9 23.1 %copy-start.2 = (s32[8]{0:T(128)S(1)}, s32[8]{0:T(128)}, u32[]{:S(2)}) copy-start(s32[8]{0:T(128)} %param.13) | copy-start | bytes 100
  15.9 24.3 %copy-start = (bf16[8,1024,256]{2,1,0:T(8,128)(2,1)S(1)}, bf16[8,1024,256]{2,1,0:T(8,128)(2,1)}, u32[]{:S(2)}) copy-start(bf16[8,1024,256]{2,1,0:T(8,128)(2,1)} %refs_0_.3) | copy-start | bytes 12582916
  15.9 10.6 %collective-permute-start.2 = (f32[32,1024]{1,0:T(8,128)S(1)}, f32[32,1024]{1,0:T(8,128)S(1)}, u32[]{:S(2)}, u32[]{:S(2)}) collective-permute-start(f32[32,1024]{1,0:T(8,128)S(1)} %slice.57.refs_0_), channel_id=1, source_target_pairs={{0,8},{2,10},{4,12},{6,14},{8,0},{10,2},{12,4},{14,6},{1,9},{3,11}... | collective-permute-start | bytes 393224 | tf_op jit(solution)/shard_map/ppermute | solution.py:331
  24.8 5.2 %collective-permute-start.5 = (f32[32,1024]{1,0:T(8,128)S(1)}, f32[32,1024]{1,0:T(8,128)S(1)}, u32[]{:S(2)}, u32[]{:S(2)}) collective-permute-start(f32[32,1024]{1,0:T(8,128)S(1)} %slice.61), channel_id=1, source_target_pairs={{0,2},{2,0},{4,6},{6,4},{8,10},{10,8},{12,14},{14,12},{1,3},{3,1},... | collective-permute-start | bytes 393224 | tf_op jit(solution)/shard_map/ppermute | solution.py:331
  26.5 6.1 %collective-permute-start.8 = (f32[32,1280]{1,0:T(8,128)S(1)}, f32[32,1280]{1,0:T(8,128)S(1)}, u32[]{:S(2)}, u32[]{:S(2)}) collective-permute-start(f32[32,1280]{1,0:T(8,128)S(1)} %slice.65), channel_id=1, source_target_pairs={{0,4},{2,6},{4,0},{6,2},{8,12},{10,14},{12,8},{14,10},{1,5},{3,7},... | collective-permute-start | bytes 491528 | tf_op jit(solution)/shard_map/ppermute | solution.py:331
  26.6 4.3 %collective-permute-start.3 = (f32[16,1024]{1,0:T(8,128)S(1)}, f32[16,1024]{1,0:T(8,128)S(1)}, u32[]{:S(2)}, u32[]{:S(2)}) collective-permute-start(f32[16,1024]{1,0:T(8,128)S(1)} %slice.59), channel_id=1, source_target_pairs={{0,2},{2,0},{4,6},{6,4},{8,10},{10,8},{12,14},{14,12},{1,3},{3,1},... | collective-permute-start | bytes 196616 | tf_op jit(solution)/shard_map/ppermute | solution.py:331
  30.1 6.4 %collective-permute-start.6 = (f32[16,1024]{1,0:T(8,128)S(1)}, f32[16,1024]{1,0:T(8,128)S(1)}, u32[]{:S(2)}, u32[]{:S(2)}) collective-permute-start(f32[16,1024]{1,0:T(8,128)S(1)} %slice.63), channel_id=1, source_target_pairs={{0,8},{2,10},{4,12},{6,14},{8,0},{10,2},{12,4},{14,6},{1,9},{3,11}... | collective-permute-start | bytes 196616 | tf_op jit(solution)/shard_map/ppermute | solution.py:331
  32.6 6.3 %collective-permute-start.9 = (f32[16,1280]{1,0:T(8,128)S(1)}, f32[16,1280]{1,0:T(8,128)S(1)}, u32[]{:S(2)}, u32[]{:S(2)}) collective-permute-start(f32[16,1280]{1,0:T(8,128)S(1)} %slice.67), channel_id=1, source_target_pairs={{0,8},{2,10},{4,12},{6,14},{8,0},{10,2},{12,4},{14,6},{1,9},{3,11}... | collective-permute-start | bytes 245768 | tf_op jit(solution)/shard_map/ppermute | solution.py:331
  38.9 1.3 %collective-permute-start.10 = (bf16[8,3328]{1,0:T(8,128)(2,1)S(1)}, bf16[8,3328]{1,0:T(8,128)(2,1)S(1)}, u32[]{:S(2)}, u32[]{:S(2)}) collective-permute-start(bf16[8,3328]{1,0:T(8,128)(2,1)S(1)} %get-tuple-element.81), channel_id=1, source_target_pairs={{0,1},{1,0},{2,3},{3,2},{4,5},{5,4},{6,7},{7,6},{8,9},{9,8},{10,11... | collective-permute-start | bytes 159752 | tf_op jit(solution)/shard_map/ppermute | solution.py:328
  43.1 1.3 %collective-permute-start.11 = (bf16[8,3072]{1,0:T(8,128)(2,1)S(1)}, bf16[8,3072]{1,0:T(8,128)(2,1)S(1)}, u32[]{:S(2)}, u32[]{:S(2)}) collective-permute-start(bf16[8,3072]{1,0:T(8,128)(2,1)S(1)} %get-tuple-element.59), channel_id=1, source_target_pairs={{0,1},{1,0},{2,3},{3,2},{4,5},{5,4},{6,7},{7,6},{8,9},{9,8},{10,11... | collective-permute-start | bytes 147464 | tf_op jit(solution)/shard_map/ppermute | solution.py:328
  44.4 4.2 %collective-permute-start.14 = (bf16[16,1536]{1,0:T(8,128)(2,1)S(1)}, bf16[16,1536]{1,0:T(8,128)(2,1)S(1)}, u32[]{:S(2)}, u32[]{:S(2)}) collective-permute-start(bf16[16,1536]{1,0:T(8,128)(2,1)S(1)} %get-tuple-element.83), channel_id=1, source_target_pairs={{0,2},{2,0},{4,6},{6,4},{8,10},{10,8},{12,14},{14,12},{1,3},{3,1},... | collective-permute-start | bytes 147464 | tf_op jit(solution)/shard_map/ppermute | solution.py:331
  44.5 5.8 %collective-permute-start.12 = (bf16[16,1536]{1,0:T(8,128)(2,1)S(1)}, bf16[16,1536]{1,0:T(8,128)(2,1)S(1)}, u32[]{:S(2)}, u32[]{:S(2)}) collective-permute-start(bf16[16,1536]{1,0:T(8,128)(2,1)S(1)} %get-tuple-element.84), channel_id=1, source_target_pairs={{0,8},{2,10},{4,12},{6,14},{8,0},{10,2},{12,4},{14,6},{1,9},{3,11}... | collective-permute-start | bytes 147464 | tf_op jit(solution)/shard_map/ppermute | solution.py:331
  48.6 6.2 %collective-permute-start.16 = (bf16[32,1536]{1,0:T(8,128)(2,1)S(1)}, bf16[32,1536]{1,0:T(8,128)(2,1)S(1)}, u32[]{:S(2)}, u32[]{:S(2)}) collective-permute-start(bf16[32,1536]{1,0:T(8,128)(2,1)S(1)} %pad_maximum_fusion.3.refs_1_), channel_id=1, source_target_pairs={{0,8},{2,10},{4,12},{6,14},{8,0},{10,2},{12,4},{14,6},{1,9},{3,11}... | collective-permute-start | bytes 294920 | tf_op jit(solution)/shard_map/ppermute | solution.py:331
  50.4 5.6 %collective-permute-start.13 = (bf16[32,1536]{1,0:T(8,128)(2,1)S(1)}, bf16[32,1536]{1,0:T(8,128)(2,1)S(1)}, u32[]{:S(2)}, u32[]{:S(2)}) collective-permute-start(bf16[32,1536]{1,0:T(8,128)(2,1)S(1)} %pad_maximum_fusion.2.refs_0_), channel_id=1, source_target_pairs={{0,4},{2,6},{4,0},{6,2},{8,12},{10,14},{12,8},{14,10},{1,5},{3,7},... | collective-permute-start | bytes 294920 | tf_op jit(solution)/shard_map/ppermute | solution.py:331
  54.9 6.0 %collective-permute-start.17 = (bf16[64,1536]{1,0:T(8,128)(2,1)S(1)}, bf16[64,1536]{1,0:T(8,128)(2,1)S(1)}, u32[]{:S(2)}, u32[]{:S(2)}) collective-permute-start(bf16[64,1536]{1,0:T(8,128)(2,1)S(1)} %pad_maximum_fusion.1.refs_1_.refs_2_), channel_id=1, source_target_pairs={{0,4},{2,6},{4,0},{6,2},{8,12},{10,14},{12,8},{14,10},{1,5},{3,7},... | collective-permute-start | bytes 589832 | tf_op jit(solution)/shard_map/ppermute | solution.py:331
  56.0 5.7 %collective-permute-start.15 = (bf16[64,1536]{1,0:T(8,128)(2,1)S(1)}, bf16[64,1536]{1,0:T(8,128)(2,1)S(1)}, u32[]{:S(2)}, u32[]{:S(2)}) collective-permute-start(bf16[64,1536]{1,0:T(8,128)(2,1)S(1)} %maximum_add_fusion.refs_0_), channel_id=1, source_target_pairs={{0,2},{2,0},{4,6},{6,4},{8,10},{10,8},{12,14},{14,12},{1,3},{3,1},... | collective-permute-start | bytes 589832 | tf_op jit(solution)/shard_map/ppermute | solution.py:331
  64.3 2.1 %collective-permute-start.18 = (f32[64,2304]{1,0:T(8,128)S(1)}, f32[64,2304]{1,0:T(8,128)S(1)}, u32[]{:S(2)}, u32[]{:S(2)}) collective-permute-start(f32[64,2304]{1,0:T(8,128)S(1)} %get-tuple-element.80), channel_id=1, source_target_pairs={{0,1},{1,0},{2,3},{3,2},{4,5},{5,4},{6,7},{7,6},{8,9},{9,8},{10,11... | collective-permute-start | bytes 1769480 | tf_op jit(solution)/shard_map/ppermute | solution.py:328

commit v20 on v19

--- a/solution.py
+++ b/solution.py
@@ -90,8 +90,8 @@
     return held, zero
 
 
-def spans_of(width):
-    return [(at, min(768, width - at)) for at in range(0, width, 768)]
+def spans_of(width, tile):
+    return [(at, min(tile, width - at)) for at in range(0, width, tile)]
 
 
 def project_kernel(orders, rows, first, widths, kv_width, after, ids_ref, own_ref, other_ref, w_ref, *refs):
@@ -104,6 +104,7 @@
     features = xs_ref.shape[1]
 
     tiles, copies, at, source = [], [], 0, first
+    wide = 512 if len(widths) == 1 else 768
     depth = 768 if features % 768 == 0 else features
 
     def fetch(from_ref, column, width):
@@ -124,7 +125,7 @@
             tiles.append((chunk, 0, at, kv_width))
             at += kv_width
             column = kv_width
-        for offset, tile in spans_of(width):
+        for offset, tile in spans_of(width, wide):
             fetch(w_ref, source, tile)
             tiles.append((chunk, column + offset, at, tile))
             at += tile
@@ -172,7 +173,7 @@
         outs += [jax.ShapeDtypeStruct(shape, jnp.float32)] * 2
     weights = [query_weight] + ([kv_weight] if kv_width else [])
     parts = features // 768 if features % 768 == 0 else 1
-    copies = parts * (len(weights) - 1 + sum(len(spans_of(width)) for width in widths))
+    copies = parts * (len(weights) - 1 + sum(len(spans_of(width, 512)) for width in widths))
     outs = pl.pallas_call(
         functools.partial(project_kernel, orders, rows, first, widths, kv_width, len(after)),
         out_shape=outs,

time: 67.4 us -> 67.2 us (level)
  no operation moved by 1% of the time
where the time goes in v20:
time: 67.2 us; the launch traced here: 67.1 us
  waiting for transfers between devices  23.8 us (35%)
  Pallas kernels  23.1 us (34%)
  starting transfers between devices  17.5 us (26%)
  other arithmetic  2.26 us (3%)
    ppermute x15, waiting for transfers between devices, across(): return lax.ppermute(array, 'gx', [(g, g ^ mask) for g in range(n)])  19.3 us
    ppermute x15, starting transfers between devices, across(): return lax.ppermute(array, 'gx', [(g, g ^ mask) for g in range(n)])  16.7 us
    pallas_call x3, Pallas kernels, load(): pl.pallas_call(functools.partial(load_kernel, len(after), cuts, len(array...  9.06 us
    pallas_call x2, Pallas kernels, project(): pl.pallas_call(functools.partial(project_kernel, orders, rows, first, wid...  8.56 us
    ppermute x4, waiting for transfers between devices, swap(): return lax.ppermute(array, 'gy', [(0, 1), (1, 0)])  4.55 us
    pallas_call x1, Pallas kernels, attend(): pl.pallas_call(functools.partial(attend_kernel, kv_column), out_shape=(ou...  2.87 us
    pallas_call x1, Pallas kernels, project_out(): pl.pallas_call(functools.partial(output_kernel, orders, rows, columns, pi...  2.65 us
  transfers between devices with their start and end apart: 19, of which 14 were waited for; matrix products, arithmetic and copies ran while one was open for 2% of the time, Pallas kernels for 21%

profile of v20, /device:TPU:0, one launch (start us, length us, event | category | flops | bytes accessed | tf_op | source)
XLA Modules:
  0.0 67.1 jit_solution(15253815983745462920)
XLA Ops:
  0.0 0.5 collective-permute-start
  0.5 1.0 %broadcast_select_fusion.own_ref = bf16[64,2304]{1,0:T(8,128)(2,1)S(1)} fusion(bf16[64,2304]{1,0:T(8,128)(2,1)} %param.7, pred[]{:T(512)S(6)} %lt.9), kind=kLoop, calls=%fused_computation.1 | loop fusion | flops 147456 | bytes 589825 | tf_op jit(solution)/shard_map/jit(_where)/select_n | solution.py:335
  1.9 3.4 %project.2 = (f32[64,1024]{1,0:T(8,128)S(1)}, f32[64,1024]{1,0:T(8,128)S(1)}) custom-call(s32[2]{0:T(128)S(1)} %pad_add_fusion.ids_ref, bf16[64,2304]{1,0:T(8,128)(2,1)S(1)} %broadcast_select_fusion.own_ref, bf16[64,2304]{1,0:T(8,128)(2,1)S(1)} %collective-permute-done.other_ref, bf16[2304,3072]{1,0:T(8,128)(2,1)} %w_ref.3), custom_call_target="tpu_custom_call" | custom-call | flops 603979776 | bytes 5242880 | tf_op jit(solution)/shard_map/project/pallas_call | solution.py:177
  5.3 3.0 %collective-permute-start.1 = (f32[64,1024]{1,0:T(8,128)S(1)}, f32[64,1024]{1,0:T(8,128)S(1)}, u32[]{:S(2)}, u32[]{:S(2)}) collective-permute-start(f32[64,1024]{1,0:T(8,128)S(1)} %get-tuple-element.44.refs_1_), channel_id=1, source_target_pairs={{0,4},{2,6},{4,0},{6,2},{8,12},{10,14},{12,8},{14,10},{1,5},{3,7},... | collective-permute-start | bytes 786440 | tf_op jit(solution)/shard_map/ppermute | solution.py:332
  8.3 5.1 %project.3 = (f32[64,1024]{1,0:T(8,128)S(1)}, f32[64,1024]{1,0:T(8,128)S(1)}, f32[64,1280]{1,0:T(8,128)S(1)}, f32[64,1280]{1,0:T(8,128)S(1)}) custom-call(s32[2]{0:T(128)S(1)} %pad_add_fusion.ids_ref, bf16[64,2304]{1,0:T(8,128)(2,1)S(1)} %broadcast_select_fusion.own_ref, bf16[64,2304]{1,0:T(8,128)(2,1)S(1)} %collective-permute-done.other_ref, ...), custom_call_target="tpu_custom_call" | custom-call | flops 1358954496 | bytes 11796480 | tf_op jit(solution)/shard_map/project/pallas_call | solution.py:177
  13.6 1.9 %collective-permute-start.7 = (f32[64,1280]{1,0:T(8,128)S(1)}, f32[64,1280]{1,0:T(8,128)S(1)}, u32[]{:S(2)}, u32[]{:S(2)}) collective-permute-start(f32[64,1280]{1,0:T(8,128)S(1)} %get-tuple-element.49), channel_id=1, source_target_pairs={{0,2},{2,0},{4,6},{6,4},{8,10},{10,8},{12,14},{14,12},{1,3},{3,1},... | collective-permute-start | bytes 983048 | tf_op jit(solution)/shard_map/ppermute | solution.py:332
  15.6 2.6 %collective-permute-start.2 = (f32[32,1024]{1,0:T(8,128)S(1)}, f32[32,1024]{1,0:T(8,128)S(1)}, u32[]{:S(2)}, u32[]{:S(2)}) collective-permute-start(f32[32,1024]{1,0:T(8,128)S(1)} %slice.57.refs_0_), channel_id=1, source_target_pairs={{0,8},{2,10},{4,12},{6,14},{8,0},{10,2},{12,4},{14,6},{1,9},{3,11}... | collective-permute-start | bytes 393224 | tf_op jit(solution)/shard_map/ppermute | solution.py:332
  18.3 2.2 %load.3 = (bf16[1024,256]{1,0:T(8,128)(2,1)S(1)}, bf16[1024,256]{1,0:T(8,128)(2,1)S(1)}, bf16[1024,256]{1,0:T(8,128)(2,1)S(1)}, bf16[1024,256]{1,0:T(8,128)(2,1)...) custom-call(f32[32,1024]{1,0:T(8,128)S(1)} %slice.57.refs_0_, ...), custom_call_target="tpu_custom_call" | custom-call | bytes 8388608 | tf_op jit(solution)/shard_map/load/pallas_call | solution.py:78
  20.5 3.9 %collective-permute-done.4 = f32[64,1024]{1,0:T(8,128)S(1)} collective-permute-done((f32[64,1024]{1,0:T(8,128)S(1)}, f32[64,1024]{1,0:T(8,128)S(1)}, u32[]{:S(2)}, u32[]{:S(2)}) %collective-permute-start.4) | collective-permute-done | bytes 262176 | tf_op jit(solution)/shard_map/ppermute | solution.py:332
  24.5 1.6 %collective-permute-start.5 = (f32[32,1024]{1,0:T(8,128)S(1)}, f32[32,1024]{1,0:T(8,128)S(1)}, u32[]{:S(2)}, u32[]{:S(2)}) collective-permute-start(f32[32,1024]{1,0:T(8,128)S(1)} %slice.61), channel_id=1, source_target_pairs={{0,2},{2,0},{4,6},{6,4},{8,10},{10,8},{12,14},{14,12},{1,3},{3,1},... | collective-permute-start | bytes 393224 | tf_op jit(solution)/shard_map/ppermute | solution.py:332
  26.2 0.6 collective-permute-start.3
  26.8 2.9 %collective-permute-done.5 = f32[32,1024]{1,0:T(8,128)S(1)} collective-permute-done((f32[32,1024]{1,0:T(8,128)S(1)}, f32[32,1024]{1,0:T(8,128)S(1)}, u32[]{:S(2)}, u32[]{:S(2)}) %collective-permute-start.5) | collective-permute-done | bytes 131104 | tf_op jit(solution)/shard_map/ppermute | solution.py:332
  29.7 0.9 %collective-permute-start.6 = (f32[16,1024]{1,0:T(8,128)S(1)}, f32[16,1024]{1,0:T(8,128)S(1)}, u32[]{:S(2)}, u32[]{:S(2)}) collective-permute-start(f32[16,1024]{1,0:T(8,128)S(1)} %slice.63), channel_id=1, source_target_pairs={{0,8},{2,10},{4,12},{6,14},{8,0},{10,2},{12,4},{14,6},{1,9},{3,11}... | collective-permute-start | bytes 196616 | tf_op jit(solution)/shard_map/ppermute | solution.py:332
  30.6 1.6 %collective-permute-done.8 = f32[32,1280]{1,0:T(8,128)S(1)} collective-permute-done((f32[32,1280]{1,0:T(8,128)S(1)}, f32[32,1280]{1,0:T(8,128)S(1)}, u32[]{:S(2)}, u32[]{:S(2)}) %collective-permute-start.8) | collective-permute-done | bytes 163872 | tf_op jit(solution)/shard_map/ppermute | solution.py:332
  32.2 1.2 %collective-permute-start.9 = (f32[16,1280]{1,0:T(8,128)S(1)}, f32[16,1280]{1,0:T(8,128)S(1)}, u32[]{:S(2)}, u32[]{:S(2)}) collective-permute-start(f32[16,1280]{1,0:T(8,128)S(1)} %slice.67), channel_id=1, source_target_pairs={{0,8},{2,10},{4,12},{6,14},{8,0},{10,2},{12,4},{14,6},{1,9},{3,11}... | collective-permute-start | bytes 245768 | tf_op jit(solution)/shard_map/ppermute | solution.py:332
  33.4 2.7 %collective-permute-done.6 = f32[16,1024]{1,0:T(8,128)S(1)} collective-permute-done((f32[16,1024]{1,0:T(8,128)S(1)}, f32[16,1024]{1,0:T(8,128)S(1)}, u32[]{:S(2)}, u32[]{:S(2)}) %collective-permute-start.6) | collective-permute-done | bytes 65568 | tf_op jit(solution)/shard_map/ppermute | solution.py:332
  36.1 2.3 %collective-permute-done.9 = f32[16,1280]{1,0:T(8,128)S(1)} collective-permute-done((f32[16,1280]{1,0:T(8,128)S(1)}, f32[16,1280]{1,0:T(8,128)S(1)}, u32[]{:S(2)}, u32[]{:S(2)}) %collective-permute-start.9) | collective-permute-done | bytes 81952 | tf_op jit(solution)/shard_map/ppermute | solution.py:332
  38.7 1.1 %collective-permute-done.10.other_q = bf16[8,3328]{1,0:T(8,128)(2,1)S(1)} collective-permute-done((bf16[8,3328]{1,0:T(8,128)(2,1)S(1)}, bf16[8,3328]{1,0:T(8,128)(2,1)S(1)}, u32[]{:S(2)}, u32[]{:S(2)}) %collective-permute-start.10) | collective-permute-done | bytes 53280 | tf_op jit(solution)/shard_map/ppermute | solution.py:329
  39.8 2.9 %attend.1 = (bf16[8,3072]{1,0:T(8,128)(2,1)S(1)}, bf16[8,3072]{1,0:T(8,128)(2,1)S(1)}) custom-call(s32[9]{0:T(128)S(1)} %pad_add_fusion.1.scalars_ref, bf16[8,3328]{1,0:T(8,128)(2,1)S(1)} %get-tuple-element.82.own_q, bf16[8,3328]{1,0:T(8,128)(2,1)S(1)} %collective-permute-done.10.other_q, bf16[8,1024,256]{2,1,0:T(8,128)(2,1)S(1)} %copy-done, ...), custom_call_target="tpu_custom_call" | custom-call | flops 201326592 | bytes 8388608 | tf_op jit(solution)/shard_map/attend/pallas_call | solution.py:250
  42.9 1.1 %collective-permute-done.11 = bf16[8,3072]{1,0:T(8,128)(2,1)S(1)} collective-permute-done((bf16[8,3072]{1,0:T(8,128)(2,1)S(1)}, bf16[8,3072]{1,0:T(8,128)(2,1)S(1)}, u32[]{:S(2)}, u32[]{:S(2)}) %collective-permute-start.11) | collective-permute-done | bytes 49184 | tf_op jit(solution)/shard_map/ppermute | solution.py:329
  44.1 1.3 %collective-permute-start.12 = (bf16[16,1536]{1,0:T(8,128)(2,1)S(1)}, bf16[16,1536]{1,0:T(8,128)(2,1)S(1)}, u32[]{:S(2)}, u32[]{:S(2)}) collective-permute-start(bf16[16,1536]{1,0:T(8,128)(2,1)S(1)} %get-tuple-element.84), channel_id=1, source_target_pairs={{0,8},{2,10},{4,12},{6,14},{8,0},{10,2},{12,4},{14,6},{1,9},{3,11}... | collective-permute-start | bytes 147464 | tf_op jit(solution)/shard_map/ppermute | solution.py:332
  45.4 2.8 %collective-permute-done.14 = bf16[16,1536]{1,0:T(8,128)(2,1)S(1)} collective-permute-done((bf16[16,1536]{1,0:T(8,128)(2,1)S(1)}, bf16[16,1536]{1,0:T(8,128)(2,1)S(1)}, u32[]{:S(2)}, u32[]{:S(2)}) %collective-permute-start.14) | collective-permute-done | bytes 49184 | tf_op jit(solution)/shard_map/ppermute | solution.py:332
  48.6 1.3 %collective-permute-done.12 = bf16[16,1536]{1,0:T(8,128)(2,1)S(1)} collective-permute-done((bf16[16,1536]{1,0:T(8,128)(2,1)S(1)}, bf16[16,1536]{1,0:T(8,128)(2,1)S(1)}, u32[]{:S(2)}, u32[]{:S(2)}) %collective-permute-start.12) | collective-permute-done | bytes 49184 | tf_op jit(solution)/shard_map/ppermute | solution.py:332
  49.9 1.0 %collective-permute-start.13 = (bf16[32,1536]{1,0:T(8,128)(2,1)S(1)}, bf16[32,1536]{1,0:T(8,128)(2,1)S(1)}, u32[]{:S(2)}, u32[]{:S(2)}) collective-permute-start(bf16[32,1536]{1,0:T(8,128)(2,1)S(1)} %pad_maximum_fusion.2.refs_0_), channel_id=1, source_target_pairs={{0,4},{2,6},{4,0},{6,2},{8,12},{10,14},{12,8},{14,10},{1,5},{3,7},... | collective-permute-start | bytes 294920 | tf_op jit(solution)/shard_map/ppermute | solution.py:332
  51.0 3.1 %load.4 = (bf16[512,768]{1,0:T(8,128)(2,1)S(1)}, bf16[512,768]{1,0:T(8,128)(2,1)S(1)}, bf16[512,768]{1,0:T(8,128)(2,1)S(1)}, bf16[512,768]{1,0:T(8,128)(2,1)S(1)...) custom-call(bf16[32,1536]{1,0:T(8,128)(2,1)S(1)} %pad_maximum_fusion, ...), custom_call_target="tpu_custom_call" | custom-call | bytes 14155776 | tf_op jit(solution)/shard_map/load/pallas_call | solution.py:78
  54.5 0.8 %collective-permute-start.17 = (bf16[64,1536]{1,0:T(8,128)(2,1)S(1)}, bf16[64,1536]{1,0:T(8,128)(2,1)S(1)}, u32[]{:S(2)}, u32[]{:S(2)}) collective-permute-start(bf16[64,1536]{1,0:T(8,128)(2,1)S(1)} %pad_maximum_fusion.1.refs_1_.refs_2_), channel_id=1, source_target_pairs={{0,4},{2,6},{4,0},{6,2},{8,12},{10,14},{12,8},{14,10},{1,5},{3,7},... | collective-permute-start | bytes 589832 | tf_op jit(solution)/shard_map/ppermute | solution.py:332
  55.6 1.1 %collective-permute-start.15 = (bf16[64,1536]{1,0:T(8,128)(2,1)S(1)}, bf16[64,1536]{1,0:T(8,128)(2,1)S(1)}, u32[]{:S(2)}, u32[]{:S(2)}) collective-permute-start(bf16[64,1536]{1,0:T(8,128)(2,1)S(1)} %maximum_add_fusion.refs_0_), channel_id=1, source_target_pairs={{0,2},{2,0},{4,6},{6,4},{8,10},{10,8},{12,14},{14,12},{1,3},{3,1},... | collective-permute-start | bytes 589832 | tf_op jit(solution)/shard_map/ppermute | solution.py:332
  56.7 3.7 %load.5 = (bf16[512,768]{1,0:T(8,128)(2,1)S(1)}, bf16[512,768]{1,0:T(8,128)(2,1)S(1)}, bf16[512,768]{1,0:T(8,128)(2,1)S(1)}, bf16[512,768]{1,0:T(8,128)(2,1)S(1)...) custom-call(bf16[64,1536]{1,0:T(8,128)(2,1)S(1)} %maximum_add_fusion, ...), custom_call_target="tpu_custom_call" | custom-call | bytes 14155776 | tf_op jit(solution)/shard_map/load/pallas_call | solution.py:78
  60.4 1.1 %collective-permute-done.15.refs_1_ = bf16[64,1536]{1,0:T(8,128)(2,1)S(1)} collective-permute-done((bf16[64,1536]{1,0:T(8,128)(2,1)S(1)}, bf16[64,1536]{1,0:T(8,128)(2,1)S(1)}, u32[]{:S(2)}, u32[]{:S(2)}) %collective-permute-start.15) | collective-permute-done | bytes 196640 | tf_op jit(solution)/shard_map/ppermute | solution.py:332
  61.6 2.6 %project_out.1 = (f32[64,2304]{1,0:T(8,128)S(1)}, f32[64,2304]{1,0:T(8,128)S(1)}) custom-call(s32[2]{0:T(128)S(1)} %pad_add_fusion.ids_ref, bf16[64,1536]{1,0:T(8,128)(2,1)S(1)} %maximum_add_fusion.refs_0_, bf16[64,1536]{1,0:T(8,128)(2,1)S(1)} %collective-permute-done.15.refs_1_, bf16[64,1536]{1,0:T(8,128)(2,1)S(1)} %pad_maximum_fusion.1.refs_1_.refs_2_, ...), custom_call_target="tpu_custom_call" | custom-call | flops 1811939328 | bytes 15335424 | tf_op jit(solution)/shard_map/project_out/pallas_call | solution.py:303
  64.3 2.0 %collective-permute-done.18 = f32[64,2304]{1,0:T(8,128)S(1)} collective-permute-done((f32[64,2304]{1,0:T(8,128)S(1)}, f32[64,2304]{1,0:T(8,128)S(1)}, u32[]{:S(2)}, u32[]{:S(2)}) %collective-permute-start.18) | collective-permute-done | bytes 589856 | tf_op jit(solution)/shard_map/ppermute | solution.py:329
  66.3 0.8 %add_convert_fusion = bf16[64,2304]{1,0:T(8,128)(2,1)} fusion(f32[64,2304]{1,0:T(8,128)S(1)} %get-tuple-element.79, f32[64,2304]{1,0:T(8,128)S(1)} %collective-permute-done.18), kind=kLoop, calls=%fused_computation | loop fusion | flops 294912 | bytes 1474560 | tf_op jit(solution)/shard_map/convert_element_type | solution.py:394
  (47 shorter events, 2.6 us)
Async XLA Ops:
  0.0 1.9 %collective-permute-start = (bf16[64,2304]{1,0:T(8,128)(2,1)}, bf16[64,2304]{1,0:T(8,128)(2,1)S(1)}, u32[]{:S(2)}, u32[]{:S(2)}) collective-permute-start(bf16[64,2304]{1,0:T(8,128)(2,1)} %param.7), channel_id=1, source_target_pairs={{0,1},{1,0},{2,3},{3,2},{4,5},{5,4},{6,7},{7,6},{8,9},{9,8},{10,11... | collective-permute-start | bytes 884744 | tf_op jit(solution)/shard_map/ppermute | solution.py:329
  1.5 6.8 %copy-start.1 = (bf16[2304,512]{1,0:T(8,128)(2,1)S(1)}, bf16[2304,512]{1,0:T(8,128)(2,1)}, u32[]{:S(2)}) copy-start(bf16[2304,512]{1,0:T(8,128)(2,1)} %refs_0_.2) | copy-start | bytes 7077892
  5.3 10.2 %collective-permute-start.1 = (f32[64,1024]{1,0:T(8,128)S(1)}, f32[64,1024]{1,0:T(8,128)S(1)}, u32[]{:S(2)}, u32[]{:S(2)}) collective-permute-start(f32[64,1024]{1,0:T(8,128)S(1)} %get-tuple-element.44.refs_1_), channel_id=1, source_target_pairs={{0,4},{2,6},{4,0},{6,2},{8,12},{10,14},{12,8},{14,10},{1,5},{3,7},... | collective-permute-start | bytes 786440 | tf_op jit(solution)/shard_map/ppermute | solution.py:332
  13.5 10.9 %collective-permute-start.4 = (f32[64,1024]{1,0:T(8,128)S(1)}, f32[64,1024]{1,0:T(8,128)S(1)}, u32[]{:S(2)}, u32[]{:S(2)}) collective-permute-start(f32[64,1024]{1,0:T(8,128)S(1)} %get-tuple-element.46), channel_id=1, source_target_pairs={{0,4},{2,6},{4,0},{6,2},{8,12},{10,14},{12,8},{14,10},{1,5},{3,7},... | collective-permute-start | bytes 786440 | tf_op jit(solution)/shard_map/ppermute | solution.py:332
  13.6 12.5 %collective-permute-start.7 = (f32[64,1280]{1,0:T(8,128)S(1)}, f32[64,1280]{1,0:T(8,128)S(1)}, u32[]{:S(2)}, u32[]{:S(2)}) collective-permute-start(f32[64,1280]{1,0:T(8,128)S(1)} %get-tuple-element.49), channel_id=1, source_target_pairs={{0,2},{2,0},{4,6},{6,4},{8,10},{10,8},{12,14},{14,12},{1,3},{3,1},... | collective-permute-start | bytes 983048 | tf_op jit(solution)/shard_map/ppermute | solution.py:332
  15.6 23.0 %copy-start.2 = (s32[8]{0:T(128)S(1)}, s32[8]{0:T(128)}, u32[]{:S(2)}) copy-start(s32[8]{0:T(128)} %param.13) | copy-start | bytes 100
  15.6 24.2 %copy-start = (bf16[8,1024,256]{2,1,0:T(8,128)(2,1)S(1)}, bf16[8,1024,256]{2,1,0:T(8,128)(2,1)}, u32[]{:S(2)}) copy-start(bf16[8,1024,256]{2,1,0:T(8,128)(2,1)} %refs_0_.3) | copy-start | bytes 12582916
  15.6 10.6 %collective-permute-start.2 = (f32[32,1024]{1,0:T(8,128)S(1)}, f32[32,1024]{1,0:T(8,128)S(1)}, u32[]{:S(2)}, u32[]{:S(2)}) collective-permute-start(f32[32,1024]{1,0:T(8,128)S(1)} %slice.57.refs_0_), channel_id=1, source_target_pairs={{0,8},{2,10},{4,12},{6,14},{8,0},{10,2},{12,4},{14,6},{1,9},{3,11}... | collective-permute-start | bytes 393224 | tf_op jit(solution)/shard_map/ppermute | solution.py:332
  24.5 5.2 %collective-permute-start.5 = (f32[32,1024]{1,0:T(8,128)S(1)}, f32[32,1024]{1,0:T(8,128)S(1)}, u32[]{:S(2)}, u32[]{:S(2)}) collective-permute-start(f32[32,1024]{1,0:T(8,128)S(1)} %slice.61), channel_id=1, source_target_pairs={{0,2},{2,0},{4,6},{6,4},{8,10},{10,8},{12,14},{14,12},{1,3},{3,1},... | collective-permute-start | bytes 393224 | tf_op jit(solution)/shard_map/ppermute | solution.py:332
  26.1 6.1 %collective-permute-start.8 = (f32[32,1280]{1,0:T(8,128)S(1)}, f32[32,1280]{1,0:T(8,128)S(1)}, u32[]{:S(2)}, u32[]{:S(2)}) collective-permute-start(f32[32,1280]{1,0:T(8,128)S(1)} %slice.65), channel_id=1, source_target_pairs={{0,4},{2,6},{4,0},{6,2},{8,12},{10,14},{12,8},{14,10},{1,5},{3,7},... | collective-permute-start | bytes 491528 | tf_op jit(solution)/shard_map/ppermute | solution.py:332
  26.2 4.4 %collective-permute-start.3 = (f32[16,1024]{1,0:T(8,128)S(1)}, f32[16,1024]{1,0:T(8,128)S(1)}, u32[]{:S(2)}, u32[]{:S(2)}) collective-permute-start(f32[16,1024]{1,0:T(8,128)S(1)} %slice.59), channel_id=1, source_target_pairs={{0,2},{2,0},{4,6},{6,4},{8,10},{10,8},{12,14},{14,12},{1,3},{3,1},... | collective-permute-start | bytes 196616 | tf_op jit(solution)/shard_map/ppermute | solution.py:332
  29.7 6.4 %collective-permute-start.6 = (f32[16,1024]{1,0:T(8,128)S(1)}, f32[16,1024]{1,0:T(8,128)S(1)}, u32[]{:S(2)}, u32[]{:S(2)}) collective-permute-start(f32[16,1024]{1,0:T(8,128)S(1)} %slice.63), channel_id=1, source_target_pairs={{0,8},{2,10},{4,12},{6,14},{8,0},{10,2},{12,4},{14,6},{1,9},{3,11}... | collective-permute-start | bytes 196616 | tf_op jit(solution)/shard_map/ppermute | solution.py:332
  32.2 6.2 %collective-permute-start.9 = (f32[16,1280]{1,0:T(8,128)S(1)}, f32[16,1280]{1,0:T(8,128)S(1)}, u32[]{:S(2)}, u32[]{:S(2)}) collective-permute-start(f32[16,1280]{1,0:T(8,128)S(1)} %slice.67), channel_id=1, source_target_pairs={{0,8},{2,10},{4,12},{6,14},{8,0},{10,2},{12,4},{14,6},{1,9},{3,11}... | collective-permute-start | bytes 245768 | tf_op jit(solution)/shard_map/ppermute | solution.py:332
  38.5 1.3 %collective-permute-start.10 = (bf16[8,3328]{1,0:T(8,128)(2,1)S(1)}, bf16[8,3328]{1,0:T(8,128)(2,1)S(1)}, u32[]{:S(2)}, u32[]{:S(2)}) collective-permute-start(bf16[8,3328]{1,0:T(8,128)(2,1)S(1)} %get-tuple-element.81), channel_id=1, source_target_pairs={{0,1},{1,0},{2,3},{3,2},{4,5},{5,4},{6,7},{7,6},{8,9},{9,8},{10,11... | collective-permute-start | bytes 159752 | tf_op jit(solution)/shard_map/ppermute | solution.py:329
  42.7 1.3 %collective-permute-start.11 = (bf16[8,3072]{1,0:T(8,128)(2,1)S(1)}, bf16[8,3072]{1,0:T(8,128)(2,1)S(1)}, u32[]{:S(2)}, u32[]{:S(2)}) collective-permute-start(bf16[8,3072]{1,0:T(8,128)(2,1)S(1)} %get-tuple-element.59), channel_id=1, source_target_pairs={{0,1},{1,0},{2,3},{3,2},{4,5},{5,4},{6,7},{7,6},{8,9},{9,8},{10,11... | collective-permute-start | bytes 147464 | tf_op jit(solution)/shard_map/ppermute | solution.py:329
  44.0 4.2 %collective-permute-start.14 = (bf16[16,1536]{1,0:T(8,128)(2,1)S(1)}, bf16[16,1536]{1,0:T(8,128)(2,1)S(1)}, u32[]{:S(2)}, u32[]{:S(2)}) collective-permute-start(bf16[16,1536]{1,0:T(8,128)(2,1)S(1)} %get-tuple-element.83), channel_id=1, source_target_pairs={{0,2},{2,0},{4,6},{6,4},{8,10},{10,8},{12,14},{14,12},{1,3},{3,1},... | collective-permute-start | bytes 147464 | tf_op jit(solution)/shard_map/ppermute | solution.py:332
  44.1 5.8 %collective-permute-start.12 = (bf16[16,1536]{1,0:T(8,128)(2,1)S(1)}, bf16[16,1536]{1,0:T(8,128)(2,1)S(1)}, u32[]{:S(2)}, u32[]{:S(2)}) collective-permute-start(bf16[16,1536]{1,0:T(8,128)(2,1)S(1)} %get-tuple-element.84), channel_id=1, source_target_pairs={{0,8},{2,10},{4,12},{6,14},{8,0},{10,2},{12,4},{14,6},{1,9},{3,11}... | collective-permute-start | bytes 147464 | tf_op jit(solution)/shard_map/ppermute | solution.py:332
  48.2 6.3 %collective-permute-start.16 = (bf16[32,1536]{1,0:T(8,128)(2,1)S(1)}, bf16[32,1536]{1,0:T(8,128)(2,1)S(1)}, u32[]{:S(2)}, u32[]{:S(2)}) collective-permute-start(bf16[32,1536]{1,0:T(8,128)(2,1)S(1)} %pad_maximum_fusion.3.refs_1_), channel_id=1, source_target_pairs={{0,8},{2,10},{4,12},{6,14},{8,0},{10,2},{12,4},{14,6},{1,9},{3,11}... | collective-permute-start | bytes 294920 | tf_op jit(solution)/shard_map/ppermute | solution.py:332
  49.9 5.6 %collective-permute-start.13 = (bf16[32,1536]{1,0:T(8,128)(2,1)S(1)}, bf16[32,1536]{1,0:T(8,128)(2,1)S(1)}, u32[]{:S(2)}, u32[]{:S(2)}) collective-permute-start(bf16[32,1536]{1,0:T(8,128)(2,1)S(1)} %pad_maximum_fusion.2.refs_0_), channel_id=1, source_target_pairs={{0,4},{2,6},{4,0},{6,2},{8,12},{10,14},{12,8},{14,10},{1,5},{3,7},... | collective-permute-start | bytes 294920 | tf_op jit(solution)/shard_map/ppermute | solution.py:332
  54.5 6.0 %collective-permute-start.17 = (bf16[64,1536]{1,0:T(8,128)(2,1)S(1)}, bf16[64,1536]{1,0:T(8,128)(2,1)S(1)}, u32[]{:S(2)}, u32[]{:S(2)}) collective-permute-start(bf16[64,1536]{1,0:T(8,128)(2,1)S(1)} %pad_maximum_fusion.1.refs_1_.refs_2_), channel_id=1, source_target_pairs={{0,4},{2,6},{4,0},{6,2},{8,12},{10,14},{12,8},{14,10},{1,5},{3,7},... | collective-permute-start | bytes 589832 | tf_op jit(solution)/shard_map/ppermute | solution.py:332
  55.6 5.9 %collective-permute-start.15 = (bf16[64,1536]{1,0:T(8,128)(2,1)S(1)}, bf16[64,1536]{1,0:T(8,128)(2,1)S(1)}, u32[]{:S(2)}, u32[]{:S(2)}) collective-permute-start(bf16[64,1536]{1,0:T(8,128)(2,1)S(1)} %maximum_add_fusion.refs_0_), channel_id=1, source_target_pairs={{0,2},{2,0},{4,6},{6,4},{8,10},{10,8},{12,14},{14,12},{1,3},{3,1},... | collective-permute-start | bytes 589832 | tf_op jit(solution)/shard_map/ppermute | solution.py:332
  64.2 2.1 %collective-permute-start.18 = (f32[64,2304]{1,0:T(8,128)S(1)}, f32[64,2304]{1,0:T(8,128)S(1)}, u32[]{:S(2)}, u32[]{:S(2)}) collective-permute-start(f32[64,2304]{1,0:T(8,128)S(1)} %get-tuple-element.80), channel_id=1, source_target_pairs={{0,1},{1,0},{2,3},{3,2},{4,5},{5,4},{6,7},{7,6},{8,9},{9,8},{10,11... | collective-permute-start | bytes 1769480 | tf_op jit(solution)/shard_map/ppermute | solution.py:329

commit v21 on v19

--- a/solution.py
+++ b/solution.py
@@ -196,7 +196,7 @@
 
 def attend_kernel(kv_column, scalars_ref, own_q, other_q, *refs):
     k_ref, refs = refs[0], refs[1:]
-    v_refs, (own_out, other_out, q_scr, o_scr, s_scr) = refs[:-5], refs[-5:]
+    v_refs, (own_out, other_out, q_scr, o_scr) = refs[:-4], refs[-4:]
     core = scalars_ref[0]
     rows, positions, _ = k_ref.shape
     at = 0
@@ -210,7 +210,6 @@
     second = other_q[:, kv_column : kv_column + DH].astype(jnp.float32)
     new_keys = jnp.where(core == 0, first, second)
     new_values = jnp.where(core == 0, second, first)
-    own_scores = []
     for row in range(rows):
         query = q_scr[row]
         scores = lax.dot_general(
@@ -219,21 +218,17 @@
             (((1,), (1,)), ((), ())),
             preferred_element_type=jnp.float32,
         )
+        self_score = jnp.sum(query * new_keys[row : row + 1], axis=1, keepdims=True)
         visible = lax.broadcasted_iota(jnp.int32, scores.shape, 1) < scalars_ref[1 + row]
-        s_scr[row] = jnp.where(visible, scores, jnp.float32(-1e30))
-        own_scores.append(jnp.sum(query * new_keys[row : row + 1], axis=1, keepdims=True))
-    self_score = jnp.stack(own_scores)
-    masked = s_scr[...]
-    peak = jnp.maximum(jnp.max(masked, axis=2, keepdims=True), self_score)
-    raised = jnp.exp(masked - peak)
-    self_raised = jnp.exp(self_score - peak)
-    inverse = 1.0 / (jnp.sum(raised, axis=2, keepdims=True) + self_raised)
-    s_scr[...] = raised * inverse
-    self_weight = (self_raised * inverse).astype(jnp.bfloat16).astype(jnp.float32)
-    for row in range(rows):
-        weights = s_scr[row].astype(jnp.bfloat16)
+        masked = jnp.where(visible, scores, jnp.float32(-1e30))
+        peak = jnp.maximum(jnp.max(masked, axis=1, keepdims=True), self_score)
+        raised = jnp.exp(masked - peak)
+        self_raised = jnp.exp(self_score - peak)
+        inverse = 1.0 / (jnp.sum(raised, axis=1, keepdims=True) + self_raised)
+        weights = (raised * inverse).astype(jnp.bfloat16)
+        self_weight = (self_raised * inverse).astype(jnp.bfloat16).astype(jnp.float32)
         total = jnp.dot(weights, v_refs[row][...], preferred_element_type=jnp.float32)
-        o_scr[row] = total + self_weight[row] * new_values[row : row + 1]
+        o_scr[row] = total + self_weight * new_values[row : row + 1]
     half = total_heads // 2
     for head in range(total_heads):
         ref = own_out if head < half else other_out
@@ -251,8 +246,7 @@
         out_shape=(out, out),
         in_specs=[SMEM] + [VMEM] * (3 + rows),
         out_specs=(VMEM, VMEM),
-        scratch_shapes=[pltpu.VMEM((rows, heads, DH), jnp.float32)] * 2
-        + [pltpu.VMEM((rows, heads, positions), jnp.float32)],
+        scratch_shapes=[pltpu.VMEM((rows, heads, DH), jnp.float32)] * 2,
         compiler_params=pltpu.CompilerParams(vmem_limit_bytes=44 * MIB),
         cost_estimate=pl.CostEstimate(
             flops=4 * rows * heads * positions * DH,

time: 67.4 us -> 69.1 us (1.025)
  Pallas kernels: 23.5 us -> 25.3 us
    pallas_call x1, Pallas kernels: 2.87 us -> 4.64 us  [attend(): pl.pallas_call(functools.partial(attend_kernel, kv_column), out_shape=(ou...]
where the time goes in v21:
time: 69.1 us; the launch traced here: 69 us
  Pallas kernels  25.3 us (37%)
  waiting for transfers between devices  23.8 us (34%)
  starting transfers between devices  17.3 us (25%)
  other arithmetic  2.26 us (3%)
    ppermute x15, waiting for transfers between devices, across(): return lax.ppermute(array, 'gx', [(g, g ^ mask) for g in range(n)])  19.2 us
    ppermute x15, starting transfers between devices, across(): return lax.ppermute(array, 'gx', [(g, g ^ mask) for g in range(n)])  16.5 us
    pallas_call x3, Pallas kernels, load(): pl.pallas_call(functools.partial(load_kernel, len(after), cuts, len(array...  9.06 us
    pallas_call x2, Pallas kernels, project(): pl.pallas_call(functools.partial(project_kernel, orders, rows, first, wid...  8.92 us
    pallas_call x1, Pallas kernels, attend(): pl.pallas_call(functools.partial(attend_kernel, kv_column), out_shape=(ou...  4.64 us
    ppermute x4, waiting for transfers between devices, swap(): return lax.ppermute(array, 'gy', [(0, 1), (1, 0)])  4.55 us
    pallas_call x1, Pallas kernels, project_out(): pl.pallas_call(functools.partial(output_kernel, orders, rows, columns, pi...  2.64 us
  transfers between devices with their start and end apart: 19, of which 14 were waited for; matrix products, arithmetic and copies ran while one was open for 2% of the time, Pallas kernels for 21%

profile of v21, /device:TPU:0, one launch (start us, length us, event | category | flops | bytes accessed | tf_op | source)
XLA Modules:
  0.0 69.0 jit_solution(8176535356689207035)
XLA Ops:
  0.0 0.5 collective-permute-start
  0.5 1.0 %broadcast_select_fusion.own_ref = bf16[64,2304]{1,0:T(8,128)(2,1)S(1)} fusion(bf16[64,2304]{1,0:T(8,128)(2,1)} %param.7, pred[]{:T(512)S(6)} %lt.9), kind=kLoop, calls=%fused_computation.1 | loop fusion | flops 147456 | bytes 589825 | tf_op jit(solution)/shard_map/jit(_where)/select_n | solution.py:328
  1.9 3.8 %project.2 = (f32[64,1024]{1,0:T(8,128)S(1)}, f32[64,1024]{1,0:T(8,128)S(1)}) custom-call(s32[2]{0:T(128)S(1)} %pad_add_fusion.ids_ref, bf16[64,2304]{1,0:T(8,128)(2,1)S(1)} %broadcast_select_fusion.own_ref, bf16[64,2304]{1,0:T(8,128)(2,1)S(1)} %collective-permute-done.other_ref, bf16[2304,3072]{1,0:T(8,128)(2,1)} %w_ref.3), custom_call_target="tpu_custom_call" | custom-call | flops 603979776 | bytes 5242880 | tf_op jit(solution)/shard_map/project/pallas_call | solution.py:176
  5.7 3.0 %collective-permute-start.1 = (f32[64,1024]{1,0:T(8,128)S(1)}, f32[64,1024]{1,0:T(8,128)S(1)}, u32[]{:S(2)}, u32[]{:S(2)}) collective-permute-start(f32[64,1024]{1,0:T(8,128)S(1)} %get-tuple-element.44.refs_1_), channel_id=1, source_target_pairs={{0,4},{2,6},{4,0},{6,2},{8,12},{10,14},{12,8},{14,10},{1,5},{3,7},... | collective-permute-start | bytes 786440 | tf_op jit(solution)/shard_map/ppermute | solution.py:325
  8.7 5.1 %project.3 = (f32[64,1024]{1,0:T(8,128)S(1)}, f32[64,1024]{1,0:T(8,128)S(1)}, f32[64,1280]{1,0:T(8,128)S(1)}, f32[64,1280]{1,0:T(8,128)S(1)}) custom-call(s32[2]{0:T(128)S(1)} %pad_add_fusion.ids_ref, bf16[64,2304]{1,0:T(8,128)(2,1)S(1)} %broadcast_select_fusion.own_ref, bf16[64,2304]{1,0:T(8,128)(2,1)S(1)} %collective-permute-done.other_ref, ...), custom_call_target="tpu_custom_call" | custom-call | flops 1358954496 | bytes 11796480 | tf_op jit(solution)/shard_map/project/pallas_call | solution.py:176
  13.9 1.9 %collective-permute-start.7 = (f32[64,1280]{1,0:T(8,128)S(1)}, f32[64,1280]{1,0:T(8,128)S(1)}, u32[]{:S(2)}, u32[]{:S(2)}) collective-permute-start(f32[64,1280]{1,0:T(8,128)S(1)} %get-tuple-element.49), channel_id=1, source_target_pairs={{0,2},{2,0},{4,6},{6,4},{8,10},{10,8},{12,14},{14,12},{1,3},{3,1},... | collective-permute-start | bytes 983048 | tf_op jit(solution)/shard_map/ppermute | solution.py:325
  15.9 2.7 %collective-permute-start.2 = (f32[32,1024]{1,0:T(8,128)S(1)}, f32[32,1024]{1,0:T(8,128)S(1)}, u32[]{:S(2)}, u32[]{:S(2)}) collective-permute-start(f32[32,1024]{1,0:T(8,128)S(1)} %slice.57.refs_0_), channel_id=1, source_target_pairs={{0,8},{2,10},{4,12},{6,14},{8,0},{10,2},{12,4},{14,6},{1,9},{3,11}... | collective-permute-start | bytes 393224 | tf_op jit(solution)/shard_map/ppermute | solution.py:325
  18.6 2.2 %load.3 = (bf16[1024,256]{1,0:T(8,128)(2,1)S(1)}, bf16[1024,256]{1,0:T(8,128)(2,1)S(1)}, bf16[1024,256]{1,0:T(8,128)(2,1)S(1)}, bf16[1024,256]{1,0:T(8,128)(2,1)...) custom-call(f32[32,1024]{1,0:T(8,128)S(1)} %slice.57.refs_0_, ...), custom_call_target="tpu_custom_call" | custom-call | bytes 8388608 | tf_op jit(solution)/shard_map/load/pallas_call | solution.py:78
  20.8 3.9 %collective-permute-done.4 = f32[64,1024]{1,0:T(8,128)S(1)} collective-permute-done((f32[64,1024]{1,0:T(8,128)S(1)}, f32[64,1024]{1,0:T(8,128)S(1)}, u32[]{:S(2)}, u32[]{:S(2)}) %collective-permute-start.4) | collective-permute-done | bytes 262176 | tf_op jit(solution)/shard_map/ppermute | solution.py:325
  24.8 1.6 %collective-permute-start.5 = (f32[32,1024]{1,0:T(8,128)S(1)}, f32[32,1024]{1,0:T(8,128)S(1)}, u32[]{:S(2)}, u32[]{:S(2)}) collective-permute-start(f32[32,1024]{1,0:T(8,128)S(1)} %slice.61), channel_id=1, source_target_pairs={{0,2},{2,0},{4,6},{6,4},{8,10},{10,8},{12,14},{14,12},{1,3},{3,1},... | collective-permute-start | bytes 393224 | tf_op jit(solution)/shard_map/ppermute | solution.py:325
  26.6 0.6 collective-permute-start.3
  27.2 2.9 %collective-permute-done.5 = f32[32,1024]{1,0:T(8,128)S(1)} collective-permute-done((f32[32,1024]{1,0:T(8,128)S(1)}, f32[32,1024]{1,0:T(8,128)S(1)}, u32[]{:S(2)}, u32[]{:S(2)}) %collective-permute-start.5) | collective-permute-done | bytes 131104 | tf_op jit(solution)/shard_map/ppermute | solution.py:325
  30.1 0.8 %collective-permute-start.6 = (f32[16,1024]{1,0:T(8,128)S(1)}, f32[16,1024]{1,0:T(8,128)S(1)}, u32[]{:S(2)}, u32[]{:S(2)}) collective-permute-start(f32[16,1024]{1,0:T(8,128)S(1)} %slice.63), channel_id=1, source_target_pairs={{0,8},{2,10},{4,12},{6,14},{8,0},{10,2},{12,4},{14,6},{1,9},{3,11}... | collective-permute-start | bytes 196616 | tf_op jit(solution)/shard_map/ppermute | solution.py:325
  30.9 1.6 %collective-permute-done.8 = f32[32,1280]{1,0:T(8,128)S(1)} collective-permute-done((f32[32,1280]{1,0:T(8,128)S(1)}, f32[32,1280]{1,0:T(8,128)S(1)}, u32[]{:S(2)}, u32[]{:S(2)}) %collective-permute-start.8) | collective-permute-done | bytes 163872 | tf_op jit(solution)/shard_map/ppermute | solution.py:325
  32.6 1.2 %collective-permute-start.9 = (f32[16,1280]{1,0:T(8,128)S(1)}, f32[16,1280]{1,0:T(8,128)S(1)}, u32[]{:S(2)}, u32[]{:S(2)}) collective-permute-start(f32[16,1280]{1,0:T(8,128)S(1)} %slice.67), channel_id=1, source_target_pairs={{0,8},{2,10},{4,12},{6,14},{8,0},{10,2},{12,4},{14,6},{1,9},{3,11}... | collective-permute-start | bytes 245768 | tf_op jit(solution)/shard_map/ppermute | solution.py:325
  33.8 2.7 %collective-permute-done.6 = f32[16,1024]{1,0:T(8,128)S(1)} collective-permute-done((f32[16,1024]{1,0:T(8,128)S(1)}, f32[16,1024]{1,0:T(8,128)S(1)}, u32[]{:S(2)}, u32[]{:S(2)}) %collective-permute-start.6) | collective-permute-done | bytes 65568 | tf_op jit(solution)/shard_map/ppermute | solution.py:325
  36.5 2.4 %collective-permute-done.9 = f32[16,1280]{1,0:T(8,128)S(1)} collective-permute-done((f32[16,1280]{1,0:T(8,128)S(1)}, f32[16,1280]{1,0:T(8,128)S(1)}, u32[]{:S(2)}, u32[]{:S(2)}) %collective-permute-start.9) | collective-permute-done | bytes 81952 | tf_op jit(solution)/shard_map/ppermute | solution.py:325
  39.1 1.1 %collective-permute-done.10.other_q = bf16[8,3328]{1,0:T(8,128)(2,1)S(1)} collective-permute-done((bf16[8,3328]{1,0:T(8,128)(2,1)S(1)}, bf16[8,3328]{1,0:T(8,128)(2,1)S(1)}, u32[]{:S(2)}, u32[]{:S(2)}) %collective-permute-start.10) | collective-permute-done | bytes 53280 | tf_op jit(solution)/shard_map/ppermute | solution.py:322
  40.2 4.6 %attend.1 = (bf16[8,3072]{1,0:T(8,128)(2,1)S(1)}, bf16[8,3072]{1,0:T(8,128)(2,1)S(1)}) custom-call(s32[9]{0:T(128)S(1)} %pad_add_fusion.1.scalars_ref, bf16[8,3328]{1,0:T(8,128)(2,1)S(1)} %get-tuple-element.82.own_q, bf16[8,3328]{1,0:T(8,128)(2,1)S(1)} %collective-permute-done.10.other_q, bf16[8,1024,256]{2,1,0:T(8,128)(2,1)S(1)} %copy-done, ...), custom_call_target="tpu_custom_call" | custom-call | flops 201326592 | bytes 8388608 | tf_op jit(solution)/shard_map/attend/pallas_call | solution.py:244
  45.1 1.1 %collective-permute-done.11 = bf16[8,3072]{1,0:T(8,128)(2,1)S(1)} collective-permute-done((bf16[8,3072]{1,0:T(8,128)(2,1)S(1)}, bf16[8,3072]{1,0:T(8,128)(2,1)S(1)}, u32[]{:S(2)}, u32[]{:S(2)}) %collective-permute-start.11) | collective-permute-done | bytes 49184 | tf_op jit(solution)/shard_map/ppermute | solution.py:322
  46.3 1.2 %collective-permute-start.12 = (bf16[16,1536]{1,0:T(8,128)(2,1)S(1)}, bf16[16,1536]{1,0:T(8,128)(2,1)S(1)}, u32[]{:S(2)}, u32[]{:S(2)}) collective-permute-start(bf16[16,1536]{1,0:T(8,128)(2,1)S(1)} %get-tuple-element.84), channel_id=1, source_target_pairs={{0,8},{2,10},{4,12},{6,14},{8,0},{10,2},{12,4},{14,6},{1,9},{3,11}... | collective-permute-start | bytes 147464 | tf_op jit(solution)/shard_map/ppermute | solution.py:325
  47.5 2.9 %collective-permute-done.14 = bf16[16,1536]{1,0:T(8,128)(2,1)S(1)} collective-permute-done((bf16[16,1536]{1,0:T(8,128)(2,1)S(1)}, bf16[16,1536]{1,0:T(8,128)(2,1)S(1)}, u32[]{:S(2)}, u32[]{:S(2)}) %collective-permute-start.14) | collective-permute-done | bytes 49184 | tf_op jit(solution)/shard_map/ppermute | solution.py:325
  50.7 1.4 %collective-permute-done.12 = bf16[16,1536]{1,0:T(8,128)(2,1)S(1)} collective-permute-done((bf16[16,1536]{1,0:T(8,128)(2,1)S(1)}, bf16[16,1536]{1,0:T(8,128)(2,1)S(1)}, u32[]{:S(2)}, u32[]{:S(2)}) %collective-permute-start.12) | collective-permute-done | bytes 49184 | tf_op jit(solution)/shard_map/ppermute | solution.py:325
  52.1 1.0 %collective-permute-start.13 = (bf16[32,1536]{1,0:T(8,128)(2,1)S(1)}, bf16[32,1536]{1,0:T(8,128)(2,1)S(1)}, u32[]{:S(2)}, u32[]{:S(2)}) collective-permute-start(bf16[32,1536]{1,0:T(8,128)(2,1)S(1)} %pad_maximum_fusion.2.refs_0_), channel_id=1, source_target_pairs={{0,4},{2,6},{4,0},{6,2},{8,12},{10,14},{12,8},{14,10},{1,5},{3,7},... | collective-permute-start | bytes 294920 | tf_op jit(solution)/shard_map/ppermute | solution.py:325
  53.1 3.1 %load.4 = (bf16[512,768]{1,0:T(8,128)(2,1)S(1)}, bf16[512,768]{1,0:T(8,128)(2,1)S(1)}, bf16[512,768]{1,0:T(8,128)(2,1)S(1)}, bf16[512,768]{1,0:T(8,128)(2,1)S(1)...) custom-call(bf16[32,1536]{1,0:T(8,128)(2,1)S(1)} %pad_maximum_fusion, ...), custom_call_target="tpu_custom_call" | custom-call | bytes 14155776 | tf_op jit(solution)/shard_map/load/pallas_call | solution.py:78
  56.6 0.8 %collective-permute-start.17 = (bf16[64,1536]{1,0:T(8,128)(2,1)S(1)}, bf16[64,1536]{1,0:T(8,128)(2,1)S(1)}, u32[]{:S(2)}, u32[]{:S(2)}) collective-permute-start(bf16[64,1536]{1,0:T(8,128)(2,1)S(1)} %pad_maximum_fusion.1.refs_1_.refs_2_), channel_id=1, source_target_pairs={{0,4},{2,6},{4,0},{6,2},{8,12},{10,14},{12,8},{14,10},{1,5},{3,7},... | collective-permute-start | bytes 589832 | tf_op jit(solution)/shard_map/ppermute | solution.py:325
  57.7 1.2 %collective-permute-start.15 = (bf16[64,1536]{1,0:T(8,128)(2,1)S(1)}, bf16[64,1536]{1,0:T(8,128)(2,1)S(1)}, u32[]{:S(2)}, u32[]{:S(2)}) collective-permute-start(bf16[64,1536]{1,0:T(8,128)(2,1)S(1)} %maximum_add_fusion.refs_0_), channel_id=1, source_target_pairs={{0,2},{2,0},{4,6},{6,4},{8,10},{10,8},{12,14},{14,12},{1,3},{3,1},... | collective-permute-start | bytes 589832 | tf_op jit(solution)/shard_map/ppermute | solution.py:325
  58.9 3.7 %load.5 = (bf16[512,768]{1,0:T(8,128)(2,1)S(1)}, bf16[512,768]{1,0:T(8,128)(2,1)S(1)}, bf16[512,768]{1,0:T(8,128)(2,1)S(1)}, bf16[512,768]{1,0:T(8,128)(2,1)S(1)...) custom-call(bf16[64,1536]{1,0:T(8,128)(2,1)S(1)} %maximum_add_fusion, ...), custom_call_target="tpu_custom_call" | custom-call | bytes 14155776 | tf_op jit(solution)/shard_map/load/pallas_call | solution.py:78
  62.6 0.8 %collective-permute-done.15.refs_1_ = bf16[64,1536]{1,0:T(8,128)(2,1)S(1)} collective-permute-done((bf16[64,1536]{1,0:T(8,128)(2,1)S(1)}, bf16[64,1536]{1,0:T(8,128)(2,1)S(1)}, u32[]{:S(2)}, u32[]{:S(2)}) %collective-permute-start.15) | collective-permute-done | bytes 196640 | tf_op jit(solution)/shard_map/ppermute | solution.py:325
  63.5 2.6 %project_out.1 = (f32[64,2304]{1,0:T(8,128)S(1)}, f32[64,2304]{1,0:T(8,128)S(1)}) custom-call(s32[2]{0:T(128)S(1)} %pad_add_fusion.ids_ref, bf16[64,1536]{1,0:T(8,128)(2,1)S(1)} %maximum_add_fusion.refs_0_, bf16[64,1536]{1,0:T(8,128)(2,1)S(1)} %collective-permute-done.15.refs_1_, bf16[64,1536]{1,0:T(8,128)(2,1)S(1)} %pad_maximum_fusion.1.refs_1_.refs_2_, ...), custom_call_target="tpu_custom_call" | custom-call | flops 1811939328 | bytes 15335424 | tf_op jit(solution)/shard_map/project_out/pallas_call | solution.py:296
  66.2 2.0 %collective-permute-done.18 = f32[64,2304]{1,0:T(8,128)S(1)} collective-permute-done((f32[64,2304]{1,0:T(8,128)S(1)}, f32[64,2304]{1,0:T(8,128)S(1)}, u32[]{:S(2)}, u32[]{:S(2)}) %collective-permute-start.18) | collective-permute-done | bytes 589856 | tf_op jit(solution)/shard_map/ppermute | solution.py:322
  68.2 0.8 %add_convert_fusion = bf16[64,2304]{1,0:T(8,128)(2,1)} fusion(f32[64,2304]{1,0:T(8,128)S(1)} %get-tuple-element.79, f32[64,2304]{1,0:T(8,128)S(1)} %collective-permute-done.18), kind=kLoop, calls=%fused_computation | loop fusion | flops 294912 | bytes 1474560 | tf_op jit(solution)/shard_map/convert_element_type | solution.py:387
  (47 shorter events, 2.5 us)
Async XLA Ops:
  0.0 1.9 %collective-permute-start = (bf16[64,2304]{1,0:T(8,128)(2,1)}, bf16[64,2304]{1,0:T(8,128)(2,1)S(1)}, u32[]{:S(2)}, u32[]{:S(2)}) collective-permute-start(bf16[64,2304]{1,0:T(8,128)(2,1)} %param.7), channel_id=1, source_target_pairs={{0,1},{1,0},{2,3},{3,2},{4,5},{5,4},{6,7},{7,6},{8,9},{9,8},{10,11... | collective-permute-start | bytes 884744 | tf_op jit(solution)/shard_map/ppermute | solution.py:322
  1.5 7.2 %copy-start.1 = (bf16[2304,512]{1,0:T(8,128)(2,1)S(1)}, bf16[2304,512]{1,0:T(8,128)(2,1)}, u32[]{:S(2)}) copy-start(bf16[2304,512]{1,0:T(8,128)(2,1)} %refs_0_.2) | copy-start | bytes 7077892
  5.7 10.1 %collective-permute-start.1 = (f32[64,1024]{1,0:T(8,128)S(1)}, f32[64,1024]{1,0:T(8,128)S(1)}, u32[]{:S(2)}, u32[]{:S(2)}) collective-permute-start(f32[64,1024]{1,0:T(8,128)S(1)} %get-tuple-element.44.refs_1_), channel_id=1, source_target_pairs={{0,4},{2,6},{4,0},{6,2},{8,12},{10,14},{12,8},{14,10},{1,5},{3,7},... | collective-permute-start | bytes 786440 | tf_op jit(solution)/shard_map/ppermute | solution.py:325
  13.8 10.9 %collective-permute-start.4 = (f32[64,1024]{1,0:T(8,128)S(1)}, f32[64,1024]{1,0:T(8,128)S(1)}, u32[]{:S(2)}, u32[]{:S(2)}) collective-permute-start(f32[64,1024]{1,0:T(8,128)S(1)} %get-tuple-element.46), channel_id=1, source_target_pairs={{0,4},{2,6},{4,0},{6,2},{8,12},{10,14},{12,8},{14,10},{1,5},{3,7},... | collective-permute-start | bytes 786440 | tf_op jit(solution)/shard_map/ppermute | solution.py:325
  13.9 12.5 %collective-permute-start.7 = (f32[64,1280]{1,0:T(8,128)S(1)}, f32[64,1280]{1,0:T(8,128)S(1)}, u32[]{:S(2)}, u32[]{:S(2)}) collective-permute-start(f32[64,1280]{1,0:T(8,128)S(1)} %get-tuple-element.49), channel_id=1, source_target_pairs={{0,2},{2,0},{4,6},{6,4},{8,10},{10,8},{12,14},{14,12},{1,3},{3,1},... | collective-permute-start | bytes 983048 | tf_op jit(solution)/shard_map/ppermute | solution.py:325
  15.9 23.1 %copy-start.2 = (s32[8]{0:T(128)S(1)}, s32[8]{0:T(128)}, u32[]{:S(2)}) copy-start(s32[8]{0:T(128)} %param.13) | copy-start | bytes 100
  15.9 24.3 %copy-start = (bf16[8,1024,256]{2,1,0:T(8,128)(2,1)S(1)}, bf16[8,1024,256]{2,1,0:T(8,128)(2,1)}, u32[]{:S(2)}) copy-start(bf16[8,1024,256]{2,1,0:T(8,128)(2,1)} %refs_0_.3) | copy-start | bytes 12582916
  15.9 10.6 %collective-permute-start.2 = (f32[32,1024]{1,0:T(8,128)S(1)}, f32[32,1024]{1,0:T(8,128)S(1)}, u32[]{:S(2)}, u32[]{:S(2)}) collective-permute-start(f32[32,1024]{1,0:T(8,128)S(1)} %slice.57.refs_0_), channel_id=1, source_target_pairs={{0,8},{2,10},{4,12},{6,14},{8,0},{10,2},{12,4},{14,6},{1,9},{3,11}... | collective-permute-start | bytes 393224 | tf_op jit(solution)/shard_map/ppermute | solution.py:325
  24.8 5.2 %collective-permute-start.5 = (f32[32,1024]{1,0:T(8,128)S(1)}, f32[32,1024]{1,0:T(8,128)S(1)}, u32[]{:S(2)}, u32[]{:S(2)}) collective-permute-start(f32[32,1024]{1,0:T(8,128)S(1)} %slice.61), channel_id=1, source_target_pairs={{0,2},{2,0},{4,6},{6,4},{8,10},{10,8},{12,14},{14,12},{1,3},{3,1},... | collective-permute-start | bytes 393224 | tf_op jit(solution)/shard_map/ppermute | solution.py:325
  26.5 6.1 %collective-permute-start.8 = (f32[32,1280]{1,0:T(8,128)S(1)}, f32[32,1280]{1,0:T(8,128)S(1)}, u32[]{:S(2)}, u32[]{:S(2)}) collective-permute-start(f32[32,1280]{1,0:T(8,128)S(1)} %slice.65), channel_id=1, source_target_pairs={{0,4},{2,6},{4,0},{6,2},{8,12},{10,14},{12,8},{14,10},{1,5},{3,7},... | collective-permute-start | bytes 491528 | tf_op jit(solution)/shard_map/ppermute | solution.py:325
  26.6 4.3 %collective-permute-start.3 = (f32[16,1024]{1,0:T(8,128)S(1)}, f32[16,1024]{1,0:T(8,128)S(1)}, u32[]{:S(2)}, u32[]{:S(2)}) collective-permute-start(f32[16,1024]{1,0:T(8,128)S(1)} %slice.59), channel_id=1, source_target_pairs={{0,2},{2,0},{4,6},{6,4},{8,10},{10,8},{12,14},{14,12},{1,3},{3,1},... | collective-permute-start | bytes 196616 | tf_op jit(solution)/shard_map/ppermute | solution.py:325
  30.1 6.4 %collective-permute-start.6 = (f32[16,1024]{1,0:T(8,128)S(1)}, f32[16,1024]{1,0:T(8,128)S(1)}, u32[]{:S(2)}, u32[]{:S(2)}) collective-permute-start(f32[16,1024]{1,0:T(8,128)S(1)} %slice.63), channel_id=1, source_target_pairs={{0,8},{2,10},{4,12},{6,14},{8,0},{10,2},{12,4},{14,6},{1,9},{3,11}... | collective-permute-start | bytes 196616 | tf_op jit(solution)/shard_map/ppermute | solution.py:325
  32.6 6.3 %collective-permute-start.9 = (f32[16,1280]{1,0:T(8,128)S(1)}, f32[16,1280]{1,0:T(8,128)S(1)}, u32[]{:S(2)}, u32[]{:S(2)}) collective-permute-start(f32[16,1280]{1,0:T(8,128)S(1)} %slice.67), channel_id=1, source_target_pairs={{0,8},{2,10},{4,12},{6,14},{8,0},{10,2},{12,4},{14,6},{1,9},{3,11}... | collective-permute-start | bytes 245768 | tf_op jit(solution)/shard_map/ppermute | solution.py:325
  38.9 1.3 %collective-permute-start.10 = (bf16[8,3328]{1,0:T(8,128)(2,1)S(1)}, bf16[8,3328]{1,0:T(8,128)(2,1)S(1)}, u32[]{:S(2)}, u32[]{:S(2)}) collective-permute-start(bf16[8,3328]{1,0:T(8,128)(2,1)S(1)} %get-tuple-element.81), channel_id=1, source_target_pairs={{0,1},{1,0},{2,3},{3,2},{4,5},{5,4},{6,7},{7,6},{8,9},{9,8},{10,11... | collective-permute-start | bytes 159752 | tf_op jit(solution)/shard_map/ppermute | solution.py:322
  44.9 1.3 %collective-permute-start.11 = (bf16[8,3072]{1,0:T(8,128)(2,1)S(1)}, bf16[8,3072]{1,0:T(8,128)(2,1)S(1)}, u32[]{:S(2)}, u32[]{:S(2)}) collective-permute-start(bf16[8,3072]{1,0:T(8,128)(2,1)S(1)} %get-tuple-element.59), channel_id=1, source_target_pairs={{0,1},{1,0},{2,3},{3,2},{4,5},{5,4},{6,7},{7,6},{8,9},{9,8},{10,11... | collective-permute-start | bytes 147464 | tf_op jit(solution)/shard_map/ppermute | solution.py:322
  46.2 4.2 %collective-permute-start.14 = (bf16[16,1536]{1,0:T(8,128)(2,1)S(1)}, bf16[16,1536]{1,0:T(8,128)(2,1)S(1)}, u32[]{:S(2)}, u32[]{:S(2)}) collective-permute-start(bf16[16,1536]{1,0:T(8,128)(2,1)S(1)} %get-tuple-element.83), channel_id=1, source_target_pairs={{0,2},{2,0},{4,6},{6,4},{8,10},{10,8},{12,14},{14,12},{1,3},{3,1},... | collective-permute-start | bytes 147464 | tf_op jit(solution)/shard_map/ppermute | solution.py:325
  46.3 5.8 %collective-permute-start.12 = (bf16[16,1536]{1,0:T(8,128)(2,1)S(1)}, bf16[16,1536]{1,0:T(8,128)(2,1)S(1)}, u32[]{:S(2)}, u32[]{:S(2)}) collective-permute-start(bf16[16,1536]{1,0:T(8,128)(2,1)S(1)} %get-tuple-element.84), channel_id=1, source_target_pairs={{0,8},{2,10},{4,12},{6,14},{8,0},{10,2},{12,4},{14,6},{1,9},{3,11}... | collective-permute-start | bytes 147464 | tf_op jit(solution)/shard_map/ppermute | solution.py:325
  50.4 6.2 %collective-permute-start.16 = (bf16[32,1536]{1,0:T(8,128)(2,1)S(1)}, bf16[32,1536]{1,0:T(8,128)(2,1)S(1)}, u32[]{:S(2)}, u32[]{:S(2)}) collective-permute-start(bf16[32,1536]{1,0:T(8,128)(2,1)S(1)} %pad_maximum_fusion.3.refs_1_), channel_id=1, source_target_pairs={{0,8},{2,10},{4,12},{6,14},{8,0},{10,2},{12,4},{14,6},{1,9},{3,11}... | collective-permute-start | bytes 294920 | tf_op jit(solution)/shard_map/ppermute | solution.py:325
  52.1 5.6 %collective-permute-start.13 = (bf16[32,1536]{1,0:T(8,128)(2,1)S(1)}, bf16[32,1536]{1,0:T(8,128)(2,1)S(1)}, u32[]{:S(2)}, u32[]{:S(2)}) collective-permute-start(bf16[32,1536]{1,0:T(8,128)(2,1)S(1)} %pad_maximum_fusion.2.refs_0_), channel_id=1, source_target_pairs={{0,4},{2,6},{4,0},{6,2},{8,12},{10,14},{12,8},{14,10},{1,5},{3,7},... | collective-permute-start | bytes 294920 | tf_op jit(solution)/shard_map/ppermute | solution.py:325
  56.6 6.0 %collective-permute-start.17 = (bf16[64,1536]{1,0:T(8,128)(2,1)S(1)}, bf16[64,1536]{1,0:T(8,128)(2,1)S(1)}, u32[]{:S(2)}, u32[]{:S(2)}) collective-permute-start(bf16[64,1536]{1,0:T(8,128)(2,1)S(1)} %pad_maximum_fusion.1.refs_1_.refs_2_), channel_id=1, source_target_pairs={{0,4},{2,6},{4,0},{6,2},{8,12},{10,14},{12,8},{14,10},{1,5},{3,7},... | collective-permute-start | bytes 589832 | tf_op jit(solution)/shard_map/ppermute | solution.py:325
  57.7 5.7 %collective-permute-start.15 = (bf16[64,1536]{1,0:T(8,128)(2,1)S(1)}, bf16[64,1536]{1,0:T(8,128)(2,1)S(1)}, u32[]{:S(2)}, u32[]{:S(2)}) collective-permute-start(bf16[64,1536]{1,0:T(8,128)(2,1)S(1)} %maximum_add_fusion.refs_0_), channel_id=1, source_target_pairs={{0,2},{2,0},{4,6},{6,4},{8,10},{10,8},{12,14},{14,12},{1,3},{3,1},... | collective-permute-start | bytes 589832 | tf_op jit(solution)/shard_map/ppermute | solution.py:325
  66.1 2.1 %collective-permute-start.18 = (f32[64,2304]{1,0:T(8,128)S(1)}, f32[64,2304]{1,0:T(8,128)S(1)}, u32[]{:S(2)}, u32[]{:S(2)}) collective-permute-start(f32[64,2304]{1,0:T(8,128)S(1)} %get-tuple-element.80), channel_id=1, source_target_pairs={{0,1},{1,0},{2,3},{3,2},{4,5},{5,4},{6,7},{7,6},{8,9},{9,8},{10,11... | collective-permute-start | bytes 1769480 | tf_op jit(solution)/shard_map/ppermute | solution.py:322
